TPU v7x, 32 devices: a whole 2x2x4 slice. The times are simulated.
32 devices in a mesh: ctx: 4 (over z), chan: 8 (over y, x, core).
Axes of the slice: x: 2, y: 2, z: 4, core: 2. Of those that a mesh axis runs over, the one named last changes fastest.
Arguments:
- conv_input: bfloat16 [512, 16384], P('ctx', 'chan'), may hold values from -6 to 6
- gate_input: bfloat16 [512, 16384], P('ctx', 'chan'), may hold values from -6 to 6
- out_grad: bfloat16 [512, 16384], P('ctx', 'chan'), may hold values from -6 to 6
- conv_weight: float32 [4, 16384], P(None, 'chan'), may hold values from -3 to 3
- conv_bias: float32 [16384], P('chan'), may hold values from -3 to 3
- proj_weight: bfloat16 [544, 16384], P(None, 'chan'), may hold values from -0.046875 to 0.046875
- step_weight: bfloat16 [512, 16384], P(None, 'chan'), may hold values from -0.25 to 0.25
- step_bias: float32 [16384], P('chan'), may hold values from -12 to -3
- decay_log: float32 [16, 16384], P(None, 'chan'), may hold values from -0.7 to 1.4
- skip_gain: float32 [16384], P('chan'), may hold values from 0.1 to 1.9
Outputs:
- grad_input: bfloat16 [512, 16384], P('ctx', 'chan')
- grad_gate: bfloat16 [512, 16384], P('ctx', 'chan')
- grad_proj: float32 [512, 16384], P('ctx', 'chan')
- grad_coef: float32 [32, 16384], P('ctx', 'chan')
- grad_step: float32 [512, 16384], P('ctx', 'chan')
- grad_conv_weight: float32 [4, 16384], P(None, 'chan')
- grad_conv_bias: float32 [16384], P('chan')
- grad_step_bias: float32 [16384], P('chan')
- grad_decay_log: float32 [16, 16384], P(None, 'chan')
- grad_skip: float32 [16384], P('chan')
All inputs are finite; a program needn't handle non-finite values.
Results may differ from a plain program's by a relative error of at most 0.023.
Values may be sent and summed in bfloat16 or wider, within the bound.
No kernel may reach another device: no remote copies, remote signals or barrier semaphores. Data moves between devices by JAX's collectives and lax.ppermute only.
A program may use at most 128 MiB of HBM per device.

v0:
```python
import jax
import jax.numpy as jnp
from jax import lax
from jax.sharding import PartitionSpec as P

BLOCK = 64


def from_behind(block, axis, distance):
    devices = range(lax.axis_size(axis))
    route = [(i - distance, i) for i in devices if i - distance in devices]
    return lax.ppermute(block, axis, route)


def prefix(shard, axis, combine, identity):
    peers, place = (lax.axis_size(axis), lax.axis_index(axis))
    everything = jax.tree.map(
        lambda part, kind: lax.all_gather(part.astype(kind), axis),
        shard,
        (jnp.bfloat16, jnp.bfloat16),
    )
    start = jax.tree.map(
        lambda part, zero: jnp.broadcast_to(jnp.asarray(zero, part.dtype), part.shape),
        shard,
        identity,
    )

    def hop(k, before):
        reached = k < place
        new = combine(
            before, jax.tree.map(lambda part, own: part[k].astype(own.dtype), everything, shard)
        )
        return jax.tree.map(lambda a, b: jnp.where(reached, a, b), new, before)

    return lax.fori_loop(0, peers, hop, start)


def entering(part, axis, combine, identity):
    count = lax.axis_size(axis)
    place = lax.axis_index(axis)
    ahead = count - 1 - place
    gathered = jax.tree.map(lambda a: lax.all_gather(a, axis), part)
    state = jax.tree.map(lambda a, e: jnp.zeros_like(a) + jnp.asarray(e, a.dtype), part, identity)

    def one(hop, state):
        source = count - 1 - hop
        return combine(
            state, jax.tree.map(lambda a: lax.dynamic_index_in_dim(a, source, 0, False), gathered)
        )

    return lax.fori_loop(0, ahead, one, state)


def silu_slope(values):
    sigma = jax.nn.sigmoid(values)
    return sigma * (1.0 + values * (1.0 - sigma))


def linear_combine(earlier, later):
    return (earlier[0] * later[0], later[0] * earlier[1] + later[1])


def block_scan(factor, source):
    return lax.associative_scan(linear_combine, (factor, source), axis=0)[1]


def reverse_scan(factor, source):
    return jnp.flip(block_scan(jnp.flip(factor, 0), jnp.flip(source, 0)), 0)


def body(
    conv_input,
    gate_input,
    out_grad,
    conv_weight,
    conv_bias,
    proj_weight,
    step_weight,
    step_bias,
    decay_log,
    skip_gain,
):
    rows_here = conv_input.shape[0]
    chans_here = conv_input.shape[1]
    conv_taps = conv_weight.shape[0]
    low_rank = step_weight.shape[0]
    state_count = decay_log.shape[0]
    block_count = rows_here // BLOCK

    def blocked(array):
        return array.reshape((block_count, BLOCK) + array.shape[1:])

    rim_rows = from_behind(conv_input[rows_here - (conv_taps - 1) :], "ctx", 1)
    extended = jnp.concatenate([rim_rows, conv_input], axis=0).astype(jnp.float32)
    conv_pre = jnp.zeros((rows_here, chans_here), jnp.float32) + conv_bias[None, :]
    for tap in range(conv_taps):
        conv_pre = conv_pre + conv_weight[tap][None, :] * extended[tap : tap + rows_here]
    conv_out = jax.nn.silu(conv_pre).astype(jnp.bfloat16)
    conv_val = lax.optimization_barrier(conv_out).astype(jnp.float32)
    proj_terms = lax.dot_general(
        conv_out, proj_weight, (((1,), (1,)), ((), ())), preferred_element_type=jnp.float32
    )
    projected = lax.psum(proj_terms, "chan").astype(jnp.bfloat16)
    step_low = projected[:, :low_rank]
    input_coef = projected[:, low_rank : low_rank + state_count].astype(jnp.float32)
    output_coef = projected[:, low_rank + state_count :].astype(jnp.float32)
    step_pre = (
        jnp.dot(step_low, step_weight, preferred_element_type=jnp.float32) + step_bias[None, :]
    )
    step_size = jax.nn.softplus(step_pre)
    decay_rate = -jnp.exp(decay_log)
    scan_grad = out_grad.astype(jnp.float32) * jax.nn.silu(gate_input.astype(jnp.float32))
    drive_term = step_size * conv_val
    zero_state = jnp.zeros((state_count, chans_here), jnp.float32)
    size_blocks = blocked(step_size)
    drive_blocks = blocked(drive_term)
    conv_blocks = blocked(conv_val)
    input_blocks = blocked(input_coef)
    output_blocks = blocked(output_coef)
    grad_blocks = blocked(scan_grad)

    def forward_local(carried, packed):
        step_part, drive_part, in_part = packed
        running_size = jnp.cumsum(step_part, axis=0)
        block_total = running_size[-1]
        weights = jnp.exp(decay_rate[None] * (block_total[None, :] - running_size)[:, None, :])
        reached = jnp.sum(weights * drive_part[:, None, :] * in_part[:, :, None], axis=0)
        return (jnp.exp(decay_rate * block_total[None, :]) * carried + reached, carried)

    state_end, start_local = lax.scan(
        forward_local, zero_state, (size_blocks, drive_blocks, input_blocks)
    )

    def adjoint_local(carried, packed):
        step_part, out_part, grad_part = packed
        running_size = jnp.cumsum(step_part, axis=0)
        block_total = running_size[-1]
        weights = jnp.exp(decay_rate[None] * running_size[:, None, :])
        reached = jnp.sum(weights * out_part[:, :, None] * grad_part[:, None, :], axis=0)
        return (jnp.exp(decay_rate * block_total[None, :]) * carried + reached, carried)

    head_local, end_local = lax.scan(
        adjoint_local, zero_state, (size_blocks, output_blocks, grad_blocks), reverse=True
    )
    block_sums = jnp.sum(size_blocks, axis=1)
    size_total = jnp.sum(block_sums, axis=0)
    decay_all = jnp.exp(decay_rate * size_total[None, :])
    running = jnp.cumsum(block_sums, axis=0)
    before_sum = running - block_sums
    later_sum = size_total[None, :] - running
    unit_state = jnp.ones((state_count, chans_here), jnp.float32)
    state_in = prefix((decay_all, state_end), "ctx", linear_combine, (unit_state, zero_state))[1]
    adjoint_in = entering((decay_all, head_local), "ctx", linear_combine, (unit_state, zero_state))[
        1
    ]
    start_true = start_local + jnp.exp(decay_rate[None] * before_sum[:, None, :]) * state_in[None]
    end_true = end_local + jnp.exp(decay_rate[None] * later_sum[:, None, :]) * adjoint_in[None]

    def gradient_block(total_grad, packed):
        step_part, drive_part, conv_part, in_part, out_part, grad_part, start_state, end_carry = (
            packed
        )
        factor = jnp.exp(step_part[:, None, :] * decay_rate[None])
        source = drive_part[:, None, :] * in_part[:, :, None]
        source = source.at[0].add(factor[0] * start_state)
        history = block_scan(factor, source)
        prior = jnp.concatenate([start_state[None], history[:-1]], axis=0)
        back_src = out_part[:, :, None] * grad_part[:, None, :]
        back_src = back_src.at[-1].add(end_carry)
        shifted = jnp.concatenate([factor[1:], jnp.zeros_like(factor[:1])], axis=0)
        adjoint = reverse_scan(shifted, back_src)
        decayed = factor * prior
        scan_out = jnp.sum(out_part[:, :, None] * history, axis=1) + skip_gain[None, :] * conv_part
        d_delta = jnp.sum(
            adjoint * (decay_rate[None] * decayed + in_part[:, :, None] * conv_part[:, None, :]),
            axis=1,
        )
        total_grad = total_grad + jnp.sum(adjoint * decayed * step_part[:, None, :], axis=0)
        coef_in_grad = jnp.sum(adjoint * drive_part[:, None, :], axis=2)
        coef_out_grad = jnp.sum(history * grad_part[:, None, :], axis=2)
        conv_grad_scan = (
            jnp.sum(adjoint * in_part[:, :, None], axis=1) * step_part
            + skip_gain[None, :] * grad_part
        )
        return (total_grad, (scan_out, d_delta, conv_grad_scan, coef_in_grad, coef_out_grad))

    decay_grad, outputs = lax.scan(
        gradient_block,
        zero_state,
        (
            size_blocks,
            drive_blocks,
            conv_blocks,
            input_blocks,
            output_blocks,
            grad_blocks,
            start_true,
            end_true,
        ),
    )
    scan_out = outputs[0].reshape(rows_here, chans_here)
    d_delta = outputs[1].reshape(rows_here, chans_here)
    conv_grad_scan = outputs[2].reshape(rows_here, chans_here)
    coef_in_grad = outputs[3].reshape(rows_here, state_count)
    coef_out_grad = outputs[4].reshape(rows_here, state_count)
    grad_gate = (
        out_grad.astype(jnp.float32) * scan_out * silu_slope(gate_input.astype(jnp.float32))
    ).astype(jnp.bfloat16)
    skip_grad = jnp.sum(scan_grad * conv_val, axis=0)
    d_pre = d_delta * jax.nn.sigmoid(step_pre)
    bias_grad = jnp.sum(d_pre, axis=0)
    pre_bf = d_pre.astype(jnp.bfloat16)
    d_low = lax.dot_general(
        pre_bf, step_weight, (((1,), (1,)), ((), ())), preferred_element_type=jnp.float32
    )
    back_part = jnp.concatenate([d_low, coef_in_grad, coef_out_grad], axis=1)
    back_proj = lax.psum(back_part, "chan").astype(jnp.bfloat16)
    ctx_count = lax.axis_size("ctx")
    rank_rows = low_rank // ctx_count
    coef_rows = 2 * state_count // ctx_count
    token_rows = back_proj.shape[0]
    rank_cols = back_proj[:, :low_rank].reshape(token_rows, ctx_count, rank_rows)
    coef_cols = back_proj[:, low_rank:].reshape(token_rows, ctx_count, coef_rows)
    ordered = jnp.concatenate([rank_cols, coef_cols], axis=2).reshape(
        token_rows, ctx_count * (rank_rows + coef_rows)
    )
    columns = ordered
    proj_rows = lax.psum_scatter(
        lax.dot_general(
            columns, conv_out, (((0,), (0,)), ((), ())), preferred_element_type=jnp.float32
        ).astype(jnp.bfloat16),
        "ctx",
        scatter_dimension=0,
        tiled=True,
    ).astype(jnp.float32)
    grad_proj = proj_rows[:rank_rows]
    grad_coef = proj_rows[rank_rows:]
    columns = step_low
    grad_step = lax.psum_scatter(
        lax.dot_general(
            columns, pre_bf, (((0,), (0,)), ((), ())), preferred_element_type=jnp.float32
        ).astype(jnp.bfloat16),
        "ctx",
        scatter_dimension=0,
        tiled=True,
    ).astype(jnp.float32)
    d_xc = conv_grad_scan + jnp.dot(back_proj, proj_weight, preferred_element_type=jnp.float32)
    d_conv = d_xc * silu_slope(conv_pre)
    next_rows = from_behind(d_conv[: conv_taps - 1], "ctx", -1)
    padded_grad = jnp.concatenate([d_conv, next_rows], axis=0)
    input_grad = jnp.zeros((rows_here, chans_here), jnp.float32)
    for tap in range(conv_taps):
        lead = conv_taps - 1 - tap
        input_grad = input_grad + conv_weight[tap][None, :] * padded_grad[lead : lead + rows_here]
    conv_w_grad = jnp.stack(
        [jnp.sum(d_conv * extended[tap : tap + rows_here], axis=0) for tap in range(conv_taps)]
    )
    conv_b_grad = jnp.sum(d_conv, axis=0)
    decay_log_grad = decay_grad * decay_rate
    reduced = lax.psum((conv_w_grad, conv_b_grad, bias_grad, decay_log_grad, skip_grad), "ctx")
    return (
        input_grad.astype(jnp.bfloat16),
        grad_gate,
        grad_proj,
        grad_coef,
        grad_step,
        reduced[0],
        reduced[1],
        reduced[2],
        reduced[3],
        reduced[4],
    )


def solution(mesh):
    in_specs = (
        P("ctx", "chan"),
        P("ctx", "chan"),
        P("ctx", "chan"),
        P(None, "chan"),
        P("chan"),
        P(None, "chan"),
        P(None, "chan"),
        P("chan"),
        P(None, "chan"),
        P("chan"),
    )
    out_specs = (
        P("ctx", "chan"),
        P("ctx", "chan"),
        P("ctx", "chan"),
        P("ctx", "chan"),
        P("ctx", "chan"),
        P(None, "chan"),
        P("chan"),
        P("chan"),
        P(None, "chan"),
        P("chan"),
    )
    return jax.shard_map(body, mesh=mesh, in_specs=in_specs, out_specs=out_specs, check_vma=False)
```

profile of v0, /device:TPU:0, one launch (start us, length us, event | category | flops | bytes accessed | tf_op | source)
XLA Modules:
  0.0 1046.5 jit_solution(5332680126715362525)
XLA Ops:
  8.2 4.9 collective-permute-start
  19.9 26.6 %all-reduce.31 = bf16[128,544]{0,1:T(8,128)(2,1)S(1)} all-reduce(f32[128,544]{0,1:T(8,128)S(1)} %fusion.56), channel_id=1, replica_groups=mesh['ctx'=4,'chan'=8] {'chan'}, use_global_device_ids=true, to_apply=%region_0.1 | all-reduce | flops 69632 | bytes 417792 | tf_op jit(solution)/shard_map/psum | solution.py:103
  49.0 5.3 convert_multiply_fusion.5
  58.9 25.2 %while.85 = (s32[]{:T(128)}, f32[16,2048]{1,0:T(8,128)}, f32[2,16,2048]{2,1,0:T(8,128)}, f32[2,64,2048]{2,1,0:T(8,128)S(1)}, f32[16,2048]{1,0:T(8,128)S(1)}, /*i...) while((s32[]{:T(128)}, f32[16,2048]{1,0:T(8,128)}, ...), condition=%wide.region_4.5_spmd.clone, body=%wide.region_1.4_spmd.clone.sunk | while | flops 16908292 | bytes 7393472 | solution.py:130
  84.9 20.7 %while.84 = (s32[]{:T(128)}, f32[16,2048]{1,0:T(8,128)S(1)}, f32[2,16,2048]{2,1,0:T(8,128)}, f32[2,64,2048]{2,1,0:T(8,128)S(1)}, f32[16,2048]{1,0:T(8,128)S(1)},...) while((s32[]{:T(128)}, f32[16,2048]{1,0:T(8,128)S(1)}, ...), condition=%wide.region_13.14_spmd.clone, body=%wide.region_10.13_spmd.clone.sunk | while | flops 16777220 | bytes 5288084 | solution.py:142
  106.5 15.7 %all-gather.3 = bf16[64,2048]{1,0:T(8,128)(2,1)} all-gather(bf16[16,2048]{1,0:T(8,128)(2,1)S(1)} %convert_element_type.79), channel_id=5, replica_groups=mesh['ctx'=4,'chan'=8] {'ctx'}, dimensions={0}, use_global_device_ids=true | all-gather | bytes 327680 | tf_op jit(solution)/shard_map/all_gather | solution.py:18
  122.2 15.4 %all-gather.2 = bf16[64,2048]{1,0:T(8,128)(2,1)} all-gather(bf16[16,2048]{1,0:T(8,128)(2,1)} %get-tuple-element.970), channel_id=4, replica_groups=mesh['ctx'=4,'chan'=8] {'ctx'}, dimensions={0}, use_global_device_ids=true | all-gather | bytes 327680 | tf_op jit(solution)/shard_map/all_gather | solution.py:18
  137.6 6.4 while.86
  144.0 16.3 %all-gather.1 = f32[64,2048]{1,0:T(8,128)} all-gather(f32[16,2048]{1,0:T(8,128)S(1)} %get-tuple-element.609), channel_id=3, replica_groups=mesh['ctx'=4,'chan'=8] {'ctx'}, dimensions={0}, use_global_device_ids=true | all-gather | bytes 655360 | tf_op jit(solution)/shard_map/all_gather | solution.py:42
  160.3 16.5 %all-gather = f32[64,2048]{1,0:T(8,128)} all-gather(f32[16,2048]{1,0:T(8,128)} %get-tuple-element.971), channel_id=2, replica_groups=mesh['ctx'=4,'chan'=8] {'ctx'}, dimensions={0}, use_global_device_ids=true | all-gather | bytes 655360 | tf_op jit(solution)/shard_map/all_gather | solution.py:42
  182.0 723.8 %while.87 = (s32[]{:T(128)}, f32[16,2048]{1,0:T(8,128)}, f32[2,64,2048]{2,1,0:T(8,128)}, f32[2,64,2048]{2,1,0:T(8,128)}, f32[2,64,2048]{2,1,0:T(8,128)}, /*index...) while((s32[]{:T(128)}, f32[16,2048]{1,0:T(8,128)}, ...), condition=%wide.region_23.24_spmd.clone, body=%wide.region_16.23_spmd.clone.sunk | while | flops 84375552 | bytes 869651328 | solution.py:187
  215.8 4.3 pad_slice_fusion.13
  225.0 10.1 slice_multiply_fusion.17
  255.8 4.1 pad.388
  264.1 6.5 pad.390
  274.7 4.2 fusion.89
  282.4 11.4 %pad.393 = f32[32,16,2048]{2,1,0:T(8,128)} pad(f32[16,16,2048]{2,1,0:T(8,128)} %pad_maximum_fusion.27, f32[]{:T(128)} %constant.243.clone.1..sunk.2), padding=0_1_1x0_0_0x0_0_0 | pad | bytes 6291460 | tf_op jit(solution)/shard_map/while/body/eval_jaxpr/pad | solution.py:64
  293.8 11.5 %pad.392 = f32[32,16,2048]{2,1,0:T(8,128)} pad(f32[16,16,2048]{2,1,0:T(8,128)} %add.769, f32[]{:T(128)} %constant.243.clone.1..sunk.2), padding=1_0_1x0_0_0x0_0_0 | pad | bytes 6291460 | tf_op jit(solution)/shard_map/while/body/eval_jaxpr/pad | solution.py:64
  305.3 7.8 fusion.90
  318.8 21.1 %pad.394 = f32[64,16,2048]{2,1,0:T(8,128)} pad(f32[32,16,2048]{2,1,0:T(8,128)} %pad_maximum_fusion.28, f32[]{:T(128)} %constant.243.clone.1..sunk.2), padding=0_1_1x0_0_0x0_0_0 | pad | bytes 12582916 | tf_op jit(solution)/shard_map/while/body/eval_jaxpr/pad | solution.py:64
  339.9 21.0 %pad.395 = f32[64,16,2048]{2,1,0:T(8,128)} pad(f32[32,16,2048]{2,1,0:T(8,128)} %add.770, f32[]{:T(128)} %constant.243.clone.1..sunk.2), padding=1_0_1x0_0_0x0_0_0 | pad | bytes 12582916 | tf_op jit(solution)/shard_map/while/body/eval_jaxpr/pad | solution.py:64
  360.9 11.7 %slice_add_fusion.17 = f32[63,16,2048]{2,1,0:T(8,128)} fusion(f32[64,16,2048]{2,1,0:T(8,128)} %pad.395, f32[64,16,2048]{2,1,0:T(8,128)} %pad.394), kind=kLoop, calls=%fused_computation.26.clone.1 | loop fusion | flops 2064384 | bytes 24772608 | tf_op jit(solution)/shard_map/while/body/eval_jaxpr/add | solution.py:64
  372.6 8.1 multiply_reduce_fusion.19
  388.7 10.1 reverse_multiply_fusion.2
  419.4 4.1 pad.398
  427.8 6.5 pad.400
  434.3 4.1 pad.401
  438.4 4.2 fusion.97
  446.1 11.4 %pad.403 = f32[32,16,2048]{2,1,0:T(8,128)} pad(f32[16,16,2048]{2,1,0:T(8,128)} %pad_maximum_fusion.32, f32[]{:T(128)} %constant.243.clone.1..sunk.2), padding=0_1_1x0_0_0x0_0_0 | pad | bytes 6291460 | tf_op jit(solution)/shard_map/while/body/eval_jaxpr/pad | solution.py:64
  457.5 11.4 %pad.402 = f32[32,16,2048]{2,1,0:T(8,128)} pad(f32[16,16,2048]{2,1,0:T(8,128)} %add.773, f32[]{:T(128)} %constant.243.clone.1..sunk.2), padding=1_0_1x0_0_0x0_0_0 | pad | bytes 6291460 | tf_op jit(solution)/shard_map/while/body/eval_jaxpr/pad | solution.py:64
  469.0 7.7 fusion.98
  482.6 21.1 %pad.404 = f32[64,16,2048]{2,1,0:T(8,128)} pad(f32[32,16,2048]{2,1,0:T(8,128)} %pad_maximum_fusion.33, f32[]{:T(128)} %constant.243.clone.1..sunk.2), padding=0_1_1x0_0_0x0_0_0 | pad | bytes 12582916 | tf_op jit(solution)/shard_map/while/body/eval_jaxpr/pad | solution.py:64
  503.6 21.0 %pad.405 = f32[64,16,2048]{2,1,0:T(8,128)} pad(f32[32,16,2048]{2,1,0:T(8,128)} %add.774, f32[]{:T(128)} %constant.243.clone.1..sunk.2), padding=1_0_1x0_0_0x0_0_0 | pad | bytes 12582916 | tf_op jit(solution)/shard_map/while/body/eval_jaxpr/pad | solution.py:64
  524.7 11.9 %add.775 = f32[64,16,2048]{2,1,0:T(8,128)} add(f32[64,16,2048]{2,1,0:T(8,128)} %pad.404, f32[64,16,2048]{2,1,0:T(8,128)} %pad.405) | non-fusion elementwise | flops 2097152 | bytes 25165824 | tf_op jit(solution)/shard_map/while/body/eval_jaxpr/add | solution.py:64
  536.7 14.2 %multiply_reduce_fusion.20 = (f32[64,2048]{1,0:T(8,128)S(1)}, f32[16,2048]{1,0:T(8,128)S(1)}, f32[64,2048]{1,0:T(8,128)S(1)}, f32[64,16]{1,0:T(8,128)S(1)}) fusion(f32[64,16,2048]{2,1,0:T(8,128)} %add.775, f32[64,2048]{1,0:T(8,128)S(1)} %copy-done.32, f32[64,16]{1,0:T(8,128)} %bitcast.146, f32[16,2048]{1,0:T(8,128)S(1)} %get-tuple-element.1562, ...), kind=kLoop, calls=%fused_computation.22.clone.1 | loop fusion | flops 31161344 | bytes 19668992 | tf_op jit(solution)/shard_map/while/body/eval_jaxpr/reduce_sum | solution.py:174
  564.3 4.3 pad_slice_fusion.13
  573.5 10.1 slice_multiply_fusion.17
  604.3 4.1 pad.388
  612.7 6.5 pad.390
  623.3 4.2 fusion.89
  630.9 11.4 %pad.393 = f32[32,16,2048]{2,1,0:T(8,128)} pad(f32[16,16,2048]{2,1,0:T(8,128)} %pad_maximum_fusion.27, f32[]{:T(128)} %constant.243.clone.1..sunk.2), padding=0_1_1x0_0_0x0_0_0 | pad | bytes 6291460 | tf_op jit(solution)/shard_map/while/body/eval_jaxpr/pad | solution.py:64
  642.4 11.5 %pad.392 = f32[32,16,2048]{2,1,0:T(8,128)} pad(f32[16,16,2048]{2,1,0:T(8,128)} %add.769, f32[]{:T(128)} %constant.243.clone.1..sunk.2), padding=1_0_1x0_0_0x0_0_0 | pad | bytes 6291460 | tf_op jit(solution)/shard_map/while/body/eval_jaxpr/pad | solution.py:64
  653.9 7.8 fusion.90
  667.4 21.1 %pad.394 = f32[64,16,2048]{2,1,0:T(8,128)} pad(f32[32,16,2048]{2,1,0:T(8,128)} %pad_maximum_fusion.28, f32[]{:T(128)} %constant.243.clone.1..sunk.2), padding=0_1_1x0_0_0x0_0_0 | pad | bytes 12582916 | tf_op jit(solution)/shard_map/while/body/eval_jaxpr/pad | solution.py:64
  688.5 21.0 %pad.395 = f32[64,16,2048]{2,1,0:T(8,128)} pad(f32[32,16,2048]{2,1,0:T(8,128)} %add.770, f32[]{:T(128)} %constant.243.clone.1..sunk.2), padding=1_0_1x0_0_0x0_0_0 | pad | bytes 12582916 | tf_op jit(solution)/shard_map/while/body/eval_jaxpr/pad | solution.py:64
  709.5 11.7 %slice_add_fusion.17 = f32[63,16,2048]{2,1,0:T(8,128)} fusion(f32[64,16,2048]{2,1,0:T(8,128)} %pad.395, f32[64,16,2048]{2,1,0:T(8,128)} %pad.394), kind=kLoop, calls=%fused_computation.26.clone.1 | loop fusion | flops 2064384 | bytes 24772608 | tf_op jit(solution)/shard_map/while/body/eval_jaxpr/add | solution.py:64
  721.2 8.1 multiply_reduce_fusion.19
  737.3 10.1 reverse_multiply_fusion.2
  767.9 4.1 pad.398
  776.4 6.5 pad.400
  782.8 4.1 pad.401
  787.0 4.2 fusion.97
  794.6 11.4 %pad.403 = f32[32,16,2048]{2,1,0:T(8,128)} pad(f32[16,16,2048]{2,1,0:T(8,128)} %pad_maximum_fusion.32, f32[]{:T(128)} %constant.243.clone.1..sunk.2), padding=0_1_1x0_0_0x0_0_0 | pad | bytes 6291460 | tf_op jit(solution)/shard_map/while/body/eval_jaxpr/pad | solution.py:64
  806.1 11.4 %pad.402 = f32[32,16,2048]{2,1,0:T(8,128)} pad(f32[16,16,2048]{2,1,0:T(8,128)} %add.773, f32[]{:T(128)} %constant.243.clone.1..sunk.2), padding=1_0_1x0_0_0x0_0_0 | pad | bytes 6291460 | tf_op jit(solution)/shard_map/while/body/eval_jaxpr/pad | solution.py:64
  817.5 7.7 fusion.98
  831.1 21.1 %pad.404 = f32[64,16,2048]{2,1,0:T(8,128)} pad(f32[32,16,2048]{2,1,0:T(8,128)} %pad_maximum_fusion.33, f32[]{:T(128)} %constant.243.clone.1..sunk.2), padding=0_1_1x0_0_0x0_0_0 | pad | bytes 12582916 | tf_op jit(solution)/shard_map/while/body/eval_jaxpr/pad | solution.py:64
  852.2 21.0 %pad.405 = f32[64,16,2048]{2,1,0:T(8,128)} pad(f32[32,16,2048]{2,1,0:T(8,128)} %add.774, f32[]{:T(128)} %constant.243.clone.1..sunk.2), padding=1_0_1x0_0_0x0_0_0 | pad | bytes 12582916 | tf_op jit(solution)/shard_map/while/body/eval_jaxpr/pad | solution.py:64
  873.2 11.9 %add.775 = f32[64,16,2048]{2,1,0:T(8,128)} add(f32[64,16,2048]{2,1,0:T(8,128)} %pad.404, f32[64,16,2048]{2,1,0:T(8,128)} %pad.405) | non-fusion elementwise | flops 2097152 | bytes 25165824 | tf_op jit(solution)/shard_map/while/body/eval_jaxpr/add | solution.py:64
  885.2 14.2 %multiply_reduce_fusion.20 = (f32[64,2048]{1,0:T(8,128)S(1)}, f32[16,2048]{1,0:T(8,128)S(1)}, f32[64,2048]{1,0:T(8,128)S(1)}, f32[64,16]{1,0:T(8,128)S(1)}) fusion(f32[64,16,2048]{2,1,0:T(8,128)} %add.775, f32[64,2048]{1,0:T(8,128)S(1)} %copy-done.32, f32[64,16]{1,0:T(8,128)} %bitcast.146, f32[16,2048]{1,0:T(8,128)S(1)} %get-tuple-element.1562, ...), kind=kLoop, calls=%fused_computation.22.clone.1 | loop fusion | flops 31161344 | bytes 19668992 | tf_op jit(solution)/shard_map/while/body/eval_jaxpr/reduce_sum | solution.py:174
  913.4 26.7 %all-reduce.32 = bf16[128,544]{1,0:T(8,128)(2,1)S(1)} all-reduce(f32[128,544]{1,0:T(8,128)S(1)} %pad_maximum_fusion.11), channel_id=1, replica_groups=mesh['ctx'=4,'chan'=8] {'chan'}, use_global_device_ids=true, to_apply=%region_24.25 | all-reduce | flops 69632 | bytes 417792 | tf_op jit(solution)/shard_map/psum | solution.py:217
  951.9 4.6 multiply_reduce_fusion.12
  956.6 18.3 %all-reduce.25 = (f32[4,2048]{1,0:T(4,128)}, f32[2048]{0:T(1024)}, f32[2048]{0:T(1024)}, f32[2048]{0:T(1024)}) all-reduce(f32[4,2048]{1,0:T(4,128)S(1)} %pad_maximum_fusion.13, f32[2048]{0:T(1024)S(1)} %get-tuple-element.874, f32[2048]{0:T(1024)S(1)} %get-tuple-element.968, ...), channel_id=1, replica_groups=mesh['ctx'=4,'chan'=8] {'ctx'}, use_global_device_ids=true, to_apply=%region_31.32 | all-reduce | flops 14336 | bytes 114688 | tf_op jit(solution)/shard_map/psum | solution.py:260
  977.0 24.1 %reduce-scatter.3.cloned.1.call-done = bf16[136,2048]{1,0:T(8,128)(2,1)} async-done(((bf16[544,2048]{1,0:T(8,128)(2,1)}), bf16[136,2048]{1,0:T(8,128)(2,1)}) %reduce-scatter.3.cloned.1.call-update) | async-done | bytes 557072 | tf_op jit(solution)/shard_map/reduce_scatter | solution.py:228
  1004.6 33.7 %all-reduce.30.cloned.1.call-done = f32[16,2048]{1,0:T(8,128)} async-done(((f32[16,2048]{1,0:T(8,128)}), f32[16,2048]{1,0:T(8,128)}) %all-reduce.30.cloned.1.call-update) | async-done | bytes 131088 | tf_op jit(solution)/shard_map/psum | solution.py:260
  (511 shorter events, 299.7 us)
Async XLA Ops:
  7.2 11.9 %copy-start = (bf16[544,2048]{1,0:T(8,128)(2,1)S(1)}, bf16[544,2048]{1,0:T(8,128)(2,1)}, u32[]{:S(2)}) copy-start(bf16[544,2048]{1,0:T(8,128)(2,1)} %param.29) | copy-start | bytes 6684676
  7.2 967.7 %reduce-scatter.5.cloned.1.call-start = ((), (), s32[]{:S(2)}) async-start(), calls=%async_computation.3 | async-start | bytes 2621440 | tf_op jit(solution)/shard_map/reduce_scatter | solution.py:239
  8.2 6.4 collective-permute-start
  16.7 32.3 %copy-start.81 = (f32[2048]{0:T(1024)S(1)}, f32[2048]{0:T(1024)}, u32[]{:S(2)}) copy-start(f32[2048]{0:T(1024)} %param.31) | copy-start | bytes 24580
  19.1 28.8 %copy-start.42 = (bf16[128,2048]{1,0:T(8,128)(2,1)}, bf16[128,2048]{1,0:T(8,128)(2,1)S(1)}, u32[]{:S(2)}) copy-start(bf16[128,2048]{1,0:T(8,128)(2,1)S(1)} %get-tuple-element.972) | copy-start | bytes 1572868
  122.2 59.8 %copy-start.59 = (f32[2048]{0:T(1024)S(1)}, f32[2048]{0:T(1024)}, u32[]{:S(2)}) copy-start(f32[2048]{0:T(1024)} %param.33) | copy-start | bytes 24580
  203.9 7.8 copy-start.27
  206.2 13.8 %copy-start.44 = (f32[1,64,16]{2,1,0:T(8,128)}, f32[1,64,16]{2,1,0:T(8,128)S(1)}, u32[]{:S(2)}) copy-start(f32[1,64,16]{2,1,0:T(8,128)S(1)} %copy.64) | copy-start | bytes 12292 | tf_op jit(solution)/shard_map/while
  207.3 12.7 %copy-start.21 = (f32[64,2048]{1,0:T(8,128)}, f32[64,2048]{1,0:T(8,128)S(1)}, u32[]{:S(2)}) copy-start(f32[64,2048]{1,0:T(8,128)S(1)} %dynamic-slice_bitcast_fusion.22) | copy-start | bytes 1572868 | tf_op jit(solution)/shard_map/while
  211.8 8.9 copy-start.1
  305.3 7.8 copy-start.3
  305.3 8.2 copy-start.5
  360.9 11.7 %copy-start.33 = (f32[64,2048]{1,0:T(8,128)S(1)}, f32[64,2048]{1,0:T(8,128)}, u32[]{:S(2)}) copy-start(f32[64,2048]{1,0:T(8,128)} %dynamic-slice_bitcast_fusion.21) | copy-start | bytes 1572868 | tf_op jit(solution)/shard_map/while
  360.9 11.7 %copy-start.49 = (f32[64,16]{1,0:T(8,128)S(1)}, f32[64,16]{1,0:T(8,128)}, u32[]{:S(2)}) copy-start(f32[64,16]{1,0:T(8,128)} %copy.65) | copy-start | bytes 12292 | tf_op jit(solution)/shard_map/while
  372.6 8.1 copy-start.51
  372.6 8.1 copy-start.41
  372.6 8.1 copy-start.56
  469.0 8.2 copy-start.6
  524.6 11.9 %copy-start.22 = (f32[64,2048]{1,0:T(8,128)S(1)}, f32[64,2048]{1,0:T(8,128)}, u32[]{:S(2)}) copy-start(f32[64,2048]{1,0:T(8,128)} %copy-done.21) | copy-start | bytes 1572868 | tf_op jit(solution)/shard_map/while
  524.6 11.9 %copy-start.24 = (f32[64,2048]{1,0:T(8,128)S(1)}, f32[64,2048]{1,0:T(8,128)}, u32[]{:S(2)}) copy-start(f32[64,2048]{1,0:T(8,128)} %copy-done.23) | copy-start | bytes 1572868 | tf_op jit(solution)/shard_map/while
  524.7 11.9 %copy-start.32 = (f32[64,2048]{1,0:T(8,128)S(1)}, f32[64,2048]{1,0:T(8,128)}, u32[]{:S(2)}) copy-start(f32[64,2048]{1,0:T(8,128)} %get-tuple-element.1391) | copy-start | bytes 1572868 | tf_op jit(solution)/shard_map/while
  524.7 11.9 %copy-start.36 = (f32[1,16,2048]{2,1,0:T(8,128)S(1)}, f32[1,16,2048]{2,1,0:T(8,128)}, u32[]{:S(2)}) copy-start(f32[1,16,2048]{2,1,0:T(8,128)} %get-tuple-element.1392) | copy-start | bytes 393220 | tf_op jit(solution)/shard_map/while
  536.6 14.3 %copy-start.45 = (f32[16,2048]{1,0:T(8,128)S(1)}, f32[16,2048]{1,0:T(8,128)}, u32[]{:S(2)}) copy-start(f32[16,2048]{1,0:T(8,128)} %get-tuple-element.1532) | copy-start | bytes 393220 | tf_op jit(solution)/shard_map/while
  536.6 14.3 %copy-start.50 = (f32[64,16]{1,0:T(8,128)S(1)}, f32[64,16]{1,0:T(8,128)}, u32[]{:S(2)}) copy-start(f32[64,16]{1,0:T(8,128)} %get-tuple-element.1399) | copy-start | bytes 12292 | tf_op jit(solution)/shard_map/while
  536.6 14.3 %copy-start.72 = (f32[2,64,16]{2,1,0:T(8,128)S(1)}, f32[2,64,16]{2,1,0:T(8,128)}, u32[]{:S(2)}) copy-start(f32[2,64,16]{2,1,0:T(8,128)} %get-tuple-element.1537) | copy-start | bytes 24580 | tf_op jit(solution)/shard_map/while
  536.6 14.3 %copy-start.75 = (f32[2,64,16]{2,1,0:T(8,128)S(1)}, f32[2,64,16]{2,1,0:T(8,128)}, u32[]{:S(2)}) copy-start(f32[2,64,16]{2,1,0:T(8,128)} %get-tuple-element.1536) | copy-start | bytes 24580 | tf_op jit(solution)/shard_map/while
  536.6 14.4 %copy-start.28 = (f32[2,64,2048]{2,1,0:T(8,128)S(1)}, f32[2,64,2048]{2,1,0:T(8,128)}, u32[]{:S(2)}) copy-start(f32[2,64,2048]{2,1,0:T(8,128)} %copy-done.27) | copy-start | bytes 3145732 | tf_op jit(solution)/shard_map/while
  536.6 14.4 %copy-start.31 = (f32[2,64,2048]{2,1,0:T(8,128)S(1)}, f32[2,64,2048]{2,1,0:T(8,128)}, u32[]{:S(2)}) copy-start(f32[2,64,2048]{2,1,0:T(8,128)} %get-tuple-element.1559) | copy-start | bytes 3145732 | tf_op jit(solution)/shard_map/while
  536.7 14.4 %copy-start.54 = (f32[2,64,2048]{2,1,0:T(8,128)S(1)}, f32[2,64,2048]{2,1,0:T(8,128)}, u32[]{:S(2)}) copy-start(f32[2,64,2048]{2,1,0:T(8,128)} %get-tuple-element.1534) | copy-start | bytes 3145732 | tf_op jit(solution)/shard_map/while
  536.7 14.4 %copy-start.79 = (f32[2,64,2048]{2,1,0:T(8,128)S(1)}, f32[2,64,2048]{2,1,0:T(8,128)}, u32[]{:S(2)}) copy-start(f32[2,64,2048]{2,1,0:T(8,128)} %get-tuple-element.1535) | copy-start | bytes 3145732 | tf_op jit(solution)/shard_map/while
  552.6 7.8 copy-start.27
  554.8 13.8 %copy-start.44 = (f32[1,64,16]{2,1,0:T(8,128)}, f32[1,64,16]{2,1,0:T(8,128)S(1)}, u32[]{:S(2)}) copy-start(f32[1,64,16]{2,1,0:T(8,128)S(1)} %copy.64) | copy-start | bytes 12292 | tf_op jit(solution)/shard_map/while
  555.9 12.7 %copy-start.21 = (f32[64,2048]{1,0:T(8,128)}, f32[64,2048]{1,0:T(8,128)S(1)}, u32[]{:S(2)}) copy-start(f32[64,2048]{1,0:T(8,128)S(1)} %dynamic-slice_bitcast_fusion.22) | copy-start | bytes 1572868 | tf_op jit(solution)/shard_map/while
  560.3 8.9 copy-start.1
  653.9 7.8 copy-start.3
  653.9 8.2 copy-start.5
  709.5 11.7 %copy-start.33 = (f32[64,2048]{1,0:T(8,128)S(1)}, f32[64,2048]{1,0:T(8,128)}, u32[]{:S(2)}) copy-start(f32[64,2048]{1,0:T(8,128)} %dynamic-slice_bitcast_fusion.21) | copy-start | bytes 1572868 | tf_op jit(solution)/shard_map/while
  709.5 11.7 %copy-start.49 = (f32[64,16]{1,0:T(8,128)S(1)}, f32[64,16]{1,0:T(8,128)}, u32[]{:S(2)}) copy-start(f32[64,16]{1,0:T(8,128)} %copy.65) | copy-start | bytes 12292 | tf_op jit(solution)/shard_map/while
  721.2 8.1 copy-start.51
  721.2 8.1 copy-start.41
  721.2 8.1 copy-start.56
  817.5 8.2 copy-start.6
  873.2 11.9 %copy-start.22 = (f32[64,2048]{1,0:T(8,128)S(1)}, f32[64,2048]{1,0:T(8,128)}, u32[]{:S(2)}) copy-start(f32[64,2048]{1,0:T(8,128)} %copy-done.21) | copy-start | bytes 1572868 | tf_op jit(solution)/shard_map/while
  873.2 11.9 %copy-start.24 = (f32[64,2048]{1,0:T(8,128)S(1)}, f32[64,2048]{1,0:T(8,128)}, u32[]{:S(2)}) copy-start(f32[64,2048]{1,0:T(8,128)} %copy-done.23) | copy-start | bytes 1572868 | tf_op jit(solution)/shard_map/while
  873.2 11.9 %copy-start.32 = (f32[64,2048]{1,0:T(8,128)S(1)}, f32[64,2048]{1,0:T(8,128)}, u32[]{:S(2)}) copy-start(f32[64,2048]{1,0:T(8,128)} %get-tuple-element.1391) | copy-start | bytes 1572868 | tf_op jit(solution)/shard_map/while
  873.2 11.9 %copy-start.36 = (f32[1,16,2048]{2,1,0:T(8,128)S(1)}, f32[1,16,2048]{2,1,0:T(8,128)}, u32[]{:S(2)}) copy-start(f32[1,16,2048]{2,1,0:T(8,128)} %get-tuple-element.1392) | copy-start | bytes 393220 | tf_op jit(solution)/shard_map/while
  885.2 14.3 %copy-start.45 = (f32[16,2048]{1,0:T(8,128)S(1)}, f32[16,2048]{1,0:T(8,128)}, u32[]{:S(2)}) copy-start(f32[16,2048]{1,0:T(8,128)} %get-tuple-element.1532) | copy-start | bytes 393220 | tf_op jit(solution)/shard_map/while
  885.2 14.3 %copy-start.50 = (f32[64,16]{1,0:T(8,128)S(1)}, f32[64,16]{1,0:T(8,128)}, u32[]{:S(2)}) copy-start(f32[64,16]{1,0:T(8,128)} %get-tuple-element.1399) | copy-start | bytes 12292 | tf_op jit(solution)/shard_map/while
  885.2 14.3 %copy-start.72 = (f32[2,64,16]{2,1,0:T(8,128)S(1)}, f32[2,64,16]{2,1,0:T(8,128)}, u32[]{:S(2)}) copy-start(f32[2,64,16]{2,1,0:T(8,128)} %get-tuple-element.1537) | copy-start | bytes 24580 | tf_op jit(solution)/shard_map/while
  885.2 14.3 %copy-start.75 = (f32[2,64,16]{2,1,0:T(8,128)S(1)}, f32[2,64,16]{2,1,0:T(8,128)}, u32[]{:S(2)}) copy-start(f32[2,64,16]{2,1,0:T(8,128)} %get-tuple-element.1536) | copy-start | bytes 24580 | tf_op jit(solution)/shard_map/while
  885.2 14.4 %copy-start.28 = (f32[2,64,2048]{2,1,0:T(8,128)S(1)}, f32[2,64,2048]{2,1,0:T(8,128)}, u32[]{:S(2)}) copy-start(f32[2,64,2048]{2,1,0:T(8,128)} %copy-done.27) | copy-start | bytes 3145732 | tf_op jit(solution)/shard_map/while
  885.2 14.4 %copy-start.31 = (f32[2,64,2048]{2,1,0:T(8,128)S(1)}, f32[2,64,2048]{2,1,0:T(8,128)}, u32[]{:S(2)}) copy-start(f32[2,64,2048]{2,1,0:T(8,128)} %get-tuple-element.1559) | copy-start | bytes 3145732 | tf_op jit(solution)/shard_map/while
  885.2 14.4 %copy-start.54 = (f32[2,64,2048]{2,1,0:T(8,128)S(1)}, f32[2,64,2048]{2,1,0:T(8,128)}, u32[]{:S(2)}) copy-start(f32[2,64,2048]{2,1,0:T(8,128)} %get-tuple-element.1534) | copy-start | bytes 3145732 | tf_op jit(solution)/shard_map/while
  885.2 14.4 %copy-start.79 = (f32[2,64,2048]{2,1,0:T(8,128)S(1)}, f32[2,64,2048]{2,1,0:T(8,128)}, u32[]{:S(2)}) copy-start(f32[2,64,2048]{2,1,0:T(8,128)} %get-tuple-element.1535) | copy-start | bytes 3145732 | tf_op jit(solution)/shard_map/while
  910.7 29.7 %copy-start.43 = (bf16[128,2048]{1,0:T(8,128)(2,1)S(1)}, bf16[128,2048]{1,0:T(8,128)(2,1)}, u32[]{:S(2)}) copy-start(bf16[128,2048]{1,0:T(8,128)(2,1)} %copy-done.42) | copy-start | bytes 1572868
  910.7 90.3 %reduce-scatter.3.cloned.1.call-start = ((), (), s32[]{:S(2)}) async-start(), calls=%async_computation.2 | async-start | bytes 2785280 | tf_op jit(solution)/shard_map/reduce_scatter | solution.py:228
  942.5 95.7 %all-reduce.30.cloned.1.call-start = ((), (), s32[]{:S(2)}) async-start(), calls=%async_computation.4 | async-start | bytes 262144 | tf_op jit(solution)/shard_map/psum | solution.py:260
  942.6 9.3 copy-start.30
  942.6 9.3 copy-start.65
  942.6 9.2 copy-start.67
  942.7 9.2 copy-start.69
  942.7 9.2 copy-start.71
  946.1 5.8 collective-permute-start.1
  947.4 9.2 copy-start.78
  (79 other events, 247.2 us)
Sparse Core Ops, SparseCore 0:
  910.9 41.5 reduce-scatter.4
  954.9 46.0 reduce-scatter.2
  1004.0 34.1 all-reduce.29
where the time goes:
time: 1060 us; the launch traced here: 1050 us
  local copies, waits for them, and re-layouts  444 us (42%)
  other arithmetic  342 us (32%)
  blocking collectives  136 us (13%)
  waiting for transfers between devices  60.7 us (6%)
  loops' own time  28.1 us (3%)
  matrix products  16.1 us (2%)
  between operations  14.5 us (1%)
    pad x40, local copies, waits for them, and re-layouts, block_scan(): return lax.associative_scan(linear_combine, (factor, source), axis=0)[1]  346 us
    add x24, other arithmetic, block_scan(): return lax.associative_scan(linear_combine, (factor, source), axis=0)[1]  80.5 us
    add x21, other arithmetic, linear_combine(): return (earlier[0] * later[0], later[0] * earlier[1] + later[1])  64.4 us
    mul x16, other arithmetic, linear_combine(): return (earlier[0] * later[0], later[0] * earlier[1] + later[1])  57.4 us
    slice x20, local copies, waits for them, and re-layouts, block_scan(): return lax.associative_scan(linear_combine, (factor, source), axis=0)[1]  36.9 us
    psum x1, waiting for transfers between devices, body(): lax.psum((conv_w_grad, conv_b_grad, bias_grad, decay_log_grad, skip_grad)...  33.7 us
    all_gather x2, blocking collectives, entering(): gathered = jax.tree.map(lambda a: lax.all_gather(a, axis), part)  32.8 us
    all_gather x2, blocking collectives, prefix(): lax.all_gather(part.astype(kind), axis)  31.1 us
  transfers between devices with their start and end apart: 5, of which 4 were waited for; matrix products, arithmetic and copies ran while one was open for 2% of the time, Pallas kernels for 0%

commit v1 on v0

v1 whole, which is shorter than its diff:
```python
import functools

import jax
import jax.numpy as jnp
from jax import lax
from jax.experimental import pallas as pl
from jax.experimental.pallas import tpu as pltpu
from jax.sharding import PartitionSpec as P

BF = jnp.bfloat16
F32 = jnp.float32
LOG2E = 1.4426950408889634
LN2 = 0.6931471805599453
VMEM_BYTES = 56 * 1024 * 1024
NT = (((1,), (1,)), ((), ()))
TN = (((0,), (0,)), ((), ()))


def group_rows(chans):
    for rows in (8, 4, 2, 1):
        if chans % (rows * 128) == 0:
            return rows
    return 1


def dot(a, b, dims=(((1,), (0,)), ((), ()))):
    return lax.dot_general(a, b, dims, preferred_element_type=F32)


def params(**more):
    return pltpu.CompilerParams(vmem_limit_bytes=VMEM_BYTES, **more)


def sds(shape, dtype):
    return jax.ShapeDtypeStruct(shape, dtype)


def whole(shape):
    return pl.BlockSpec(shape, lambda i: (0,) * len(shape))


def columns(rows, width):
    return pl.BlockSpec((rows, width), lambda i: (0, i))


def sigmoid(v):
    return 1.0 / (1.0 + jnp.exp(-v))


def piece_start(peers, mask, size):
    return 0 if peers == 1 else (lax.axis_index("chan") ^ mask) * size


def swap(block, axis, mask):
    count = lax.axis_size(axis)
    return lax.ppermute(block, axis, [(i, i ^ mask) for i in range(count)])


def rotate(block, axis, distance):
    count = lax.axis_size(axis)
    return lax.ppermute(block, axis, [(i, (i + distance) % count) for i in range(count)])


def shift(block, axis, distance):
    count = lax.axis_size(axis)
    route = [(i, i + distance) for i in range(count) if 0 <= i + distance < count]
    return lax.ppermute(block, axis, route)


def fill_extended(ext, rim_ref, input_ref, taps):
    rows = input_ref.shape[0]
    ext[8 - (taps - 1) : 8, :] = rim_ref[...].astype(F32)
    ext[8 : 8 + rows, :] = input_ref[...].astype(F32)


def conv_block(ext, weight, bias, taps, start, rows):
    total = bias + jnp.zeros((rows, ext.shape[1]), F32)
    for tap in range(taps):
        first = 8 - (taps - 1) + tap + start
        total = total + weight[tap : tap + 1, :] * ext[first : first + rows, :]
    return total


def conv_kernel(peers, input_ref, rim_ref, weight_ref, bias_ref, proj_ref, out_ref, *rest):
    pieces, (ext, acc) = rest[:peers], rest[peers:]
    step = pl.program_id(0)
    taps = weight_ref.shape[0]
    rows = input_ref.shape[0]
    fill_extended(ext, rim_ref, input_ref, taps)
    for start in range(0, rows, 16):
        pre = conv_block(ext, weight_ref, bias_ref[...], taps, start, 16)
        out_ref[start : start + 16, :] = (pre * sigmoid(pre)).astype(BF)
    part = dot(out_ref[...], proj_ref[...], NT)

    @pl.when(step == 0)
    def _():
        acc[...] = part

    @pl.when(step > 0)
    def _():
        acc[...] += part

    @pl.when(step == pl.num_programs(0) - 1)
    def _():
        size = rows // peers
        for mask in range(peers):
            first = piece_start(peers, mask, size)
            pieces[mask][...] = acc[pl.ds(first, size), :].astype(BF)


def conv_call(peers, conv_input, rim, weight, bias, proj_weight):
    rows, chans = conv_input.shape
    taps = weight.shape[0]
    wide = proj_weight.shape[0]
    width = min(512, chans)
    return pl.pallas_call(
        functools.partial(conv_kernel, peers),
        grid=(chans // width,),
        in_specs=[
            columns(rows, width),
            columns(taps - 1, width),
            columns(taps, width),
            columns(1, width),
            columns(wide, width),
        ],
        out_specs=[columns(rows, width)] + [whole((rows // peers, wide))] * peers,
        out_shape=[sds((rows, chans), BF)] + [sds((rows // peers, wide), BF)] * peers,
        scratch_shapes=[pltpu.VMEM((rows + 8, width), F32), pltpu.VMEM((rows, wide), F32)],
        compiler_params=params(),
        name="conv_project",
    )(conv_input, rim, weight, bias, proj_weight)


def tile_rows(value, target, lead, groups):
    rows = value.shape[0]
    for block in range(rows // 8):
        for group in range(groups):
            first = (block * groups + group) * 8
            target[lead, first : first + 8, :] = value[
                block * 8 : block * 8 + 8, group * 128 : group * 128 + 128
            ]


def local_kernel(
    peers, low_rank, states, *refs
):
    parts, refs = refs[:peers], refs[peers:]
    (weight_ref, bias_ref, decay_ref, conv_ref, gate_ref, grad_ref) = refs[:6]
    (dt_ref, fwd_ref, bwd_ref, coef_ref, low) = refs[6:11]
    (proj, coef_v, coef, dts, dxs, gs, fwd, bwd, sem) = refs[11:]
    step = pl.program_id(0)
    chunks = dts.shape[0]
    rows = conv_ref.shape[0]
    groups = decay_ref.shape[2]

    @pl.when(step == 0)
    def _():
        size = rows // peers
        for mask in range(peers):
            proj[pl.ds(piece_start(peers, mask, size), size), :] = parts[mask][...].astype(F32)
        low[...] = proj[:, :low_rank].astype(BF)
        coef_v[...] = jnp.zeros_like(coef_v)
        coef_v[:, : 2 * states] = proj[:, low_rank:]
        coef_ref[...] = coef_v[...]
        copy = pltpu.make_async_copy(coef_v, coef, sem)
        copy.start()
        copy.wait()

    pre = dot(low[...], weight_ref[...]) + bias_ref[...]
    for start in range(0, rows, 16):
        here = slice(start, start + 16)
        p = pre[here, :]
        size = jnp.maximum(p, 0.0) + jnp.log1p(jnp.exp(-jnp.abs(p)))
        gate = gate_ref[here, :].astype(F32)
        grad = grad_ref[here, :].astype(F32) * gate * sigmoid(gate)
        drive = size * conv_ref[here, :].astype(F32)
        for half in range(2):
            for group in range(groups):
                first = ((start // 8 + half) * groups + group) * 8
                lanes = slice(group * 128, group * 128 + 128)
                subs = slice(half * 8, half * 8 + 8)
                dts[step, first : first + 8, :] = size[subs, lanes]
                dt_ref[0, first : first + 8, :] = size[subs, lanes]
                dxs[step, first : first + 8, :] = drive[subs, lanes]
                gs[step, first : first + 8, :] = grad[subs, lanes]

    @pl.when(step == chunks - 1)
    def _():
        batch = 4
        span = groups * 8
        zero = jnp.zeros((groups, 128), F32)
        for lead in range(0, states, batch):
            pairs = [(n, v) for n in range(lead, lead + batch) for v in range(chunks)]
            rates = [-LOG2E * jnp.exp(decay_ref[v, n]) for n, v in pairs]

            def block(index, carry):
                state, run, head, total = (list(part) for part in carry)
                for sub in range(8):
                    token = index * 8 + sub
                    at = pl.ds(index * span + sub, groups, stride=8)
                    size = [dts[v, at, :] for v in range(chunks)]
                    drive = [dxs[v, at, :] for v in range(chunks)]
                    grad = [gs[v, at, :] for v in range(chunks)]
                    if lead == 0:
                        total = [a + b for a, b in zip(total, size)]
                    for k, (n, v) in enumerate(pairs):
                        factor = jnp.exp2(size[v] * rates[k])
                        state[k] = factor * state[k] + drive[v] * coef[token, n]
                        run[k] = run[k] * factor
                        head[k] = head[k] + run[k] * (grad[v] * coef[token, states + n])
                return state, run, head, total

            many = [zero] * len(pairs)
            state, run, head, total = lax.fori_loop(
                0,
                rows // 8,
                block,
                (many, [zero + 1.0] * len(pairs), many, [zero] * chunks),
            )
            for k, (n, v) in enumerate(pairs):
                fwd[v, n] = state[k]
                bwd[v, n] = head[k]
            if lead == 0:
                for v in range(chunks):
                    coarse = total[v].astype(BF).astype(F32)
                    for target in (fwd, bwd):
                        target[v, states] = coarse
                        target[v, states + 1] = total[v] - coarse
        fwd_ref[...] = fwd[...].astype(BF)
        bwd_ref[...] = bwd[...].astype(BF)


def local_call(parts, step_weight, step_bias, decay, conv_out, gate, grad, states):
    peers = len(parts)
    rows, chans = conv_out.shape
    wide = parts[0].shape[1]
    low_rank = step_weight.shape[0]
    chunks, _, groups, _ = decay.shape
    width = groups * 128
    message = (chunks, states + 2, groups, 128)
    big = pltpu.VMEM((chunks, rows * groups, 128), F32)
    return pl.pallas_call(
        functools.partial(local_kernel, peers, low_rank, states),
        grid=(chunks,),
        in_specs=[whole((rows // peers, wide))] * peers
        + [
            columns(low_rank, width),
            columns(1, width),
            whole(decay.shape),
            columns(rows, width),
            columns(rows, width),
            columns(rows, width),
        ],
        out_specs=[
            pl.BlockSpec((1, rows * groups, 128), lambda i: (i, 0, 0)),
            whole(message),
            whole(message),
            whole((rows, 128)),
            whole((rows, low_rank)),
        ],
        out_shape=[
            sds((chunks, rows * groups, 128), F32),
            sds(message, BF),
            sds(message, BF),
            sds((rows, 128), F32),
            sds((rows, low_rank), BF),
        ],
        scratch_shapes=[
            pltpu.VMEM((rows, wide), F32),
            pltpu.VMEM((rows, 128), F32),
            pltpu.SMEM((rows, 128), F32),
            big,
            big,
            big,
            pltpu.VMEM(message, F32),
            pltpu.VMEM(message, F32),
            pltpu.SemaphoreType.DMA,
        ],
        compiler_params=params(),
        name="local_ends",
    )(*parts, step_weight, step_bias, decay, conv_out, gate, grad)


def fold_sublanes(values):
    rows = lax.broadcasted_iota(jnp.int32, (8, 128), 0)
    if values[0].shape[0] != 8:
        result = jnp.zeros((8, 128), F32)
        for i, value in enumerate(values):
            result = jnp.where(rows == i, jnp.sum(value, axis=0, keepdims=True), result)
        return result
    distance = 4
    while len(values) > 1:
        half = len(values) // 2
        low = (rows & distance) == 0
        values = [
            jnp.where(low, a, b) + pltpu.roll(jnp.where(low, b, a), distance, 0)
            if distance == 4
            else jnp.where(low, a, pltpu.roll(b, distance, 0))
            + jnp.where(low, pltpu.roll(a, 8 - distance, 0), b)
            for a, b in zip(values[:half], values[half:])
        ]
        distance //= 2
    return values[0]


def scan_kernel(peers, hops, states, *refs):
    (coef, low_ref, dt_ref, decay_ref, conv_ref, gate_ref, grad_ref, weight_ref, skip_ref) = refs[:9]
    befores, refs = refs[9 : 9 + hops], refs[9 + hops :]
    afters, refs = refs[:hops], refs[hops:]
    (pre_ref, gate_out, scan_out, small_ref, prod_ref) = refs[:5]
    pieces, refs = refs[5 : 5 + peers], refs[5 + peers :]
    (xs, dxs, gs, ys, dds, qs, decayed, coef_out, coef_in, rate, decay_acc, acc, small) = refs
    step = pl.program_id(0)
    rows = conv_ref.shape[0]
    groups = decay_ref.shape[2]
    low_rank = weight_ref.shape[0]
    span = groups * 8

    for start in range(0, rows, 16):
        here = slice(start, start + 16)
        conv = conv_ref[here, :].astype(F32)
        gate = gate_ref[here, :].astype(F32)
        grad = grad_ref[here, :].astype(F32) * gate * sigmoid(gate)
        for half in range(2):
            for group in range(groups):
                first = ((start // 8 + half) * groups + group) * 8
                lanes = slice(group * 128, group * 128 + 128)
                subs = slice(half * 8, half * 8 + 8)
                xs[first : first + 8, :] = conv[subs, lanes]
                dxs[first : first + 8, :] = conv[subs, lanes] * dt_ref[0, first : first + 8, :]
                gs[first : first + 8, :] = grad[subs, lanes]

    state, carry = [], []
    for n in range(states):
        rate[n] = -LOG2E * jnp.exp(decay_ref[0, n])
    for n in range(states):
        now = jnp.zeros((groups, 128), F32)
        for message in befores[::-1]:
            total = message[0, states].astype(F32) + message[0, states + 1].astype(F32)
            now = jnp.exp2(rate[n] * total) * now + message[0, n].astype(F32)
        state.append(now)
        now = jnp.zeros((groups, 128), F32)
        for message in afters[::-1]:
            total = message[0, states].astype(F32) + message[0, states + 1].astype(F32)
            now = jnp.exp2(rate[n] * total) * now + message[0, n].astype(F32)
        carry.append(now)

    def forward(index, state):
        state = list(state)
        for sub in range(8):
            token = index * 8 + sub
            at = pl.ds(index * span + sub, groups, stride=8)
            size, drive, grad = dt_ref[0, at, :], dxs[at, :], gs[at, :]
            result = jnp.zeros((groups, 128), F32)
            for lead in range(0, states, 8):
                products = []
                for n in range(lead, lead + 8):
                    kept = jnp.exp2(size * rate[n]) * state[n]
                    decayed[token, n] = kept
                    state[n] = kept + drive * coef[token, n]
                    result = result + state[n] * coef[token, states + n]
                    products.append(state[n] * grad)
                coef_out[pl.ds(pl.multiple_of(token * states + lead, 8), 8), :] = fold_sublanes(
                    products
                )
            ys[at, :] = result
        return state

    lax.fori_loop(0, rows // 8, forward, state)

    def backward(hop, both):
        carry, gathered = list(both[0]), list(both[1])
        index = rows // 8 - 1 - hop
        for sub in range(7, -1, -1):
            token = index * 8 + sub
            at = pl.ds(index * span + sub, groups, stride=8)
            size, drive, grad = dt_ref[0, at, :], dxs[at, :], gs[at, :]
            slope = jnp.zeros((groups, 128), F32)
            inner = jnp.zeros((groups, 128), F32)
            for lead in range(0, states, 8):
                products = []
                for n in range(lead, lead + 8):
                    adjoint = carry[n] + grad * coef[token, states + n]
                    carry[n] = jnp.exp2(size * rate[n]) * adjoint
                    weighted = adjoint * decayed[token, n]
                    slope = slope + weighted * rate[n]
                    gathered[n] = gathered[n] + weighted * size
                    inner = inner + adjoint * coef[token, n]
                    products.append(adjoint * drive)
                coef_in[pl.ds(pl.multiple_of(token * states + lead, 8), 8), :] = fold_sublanes(
                    products
                )
            dds[at, :] = slope
            qs[at, :] = inner
        return carry, gathered

    zeros = [jnp.zeros((groups, 128), F32)] * states
    _, gathered = lax.fori_loop(0, rows // 8, backward, (carry, zeros))
    for n in range(states):
        decay_acc[n * groups : n * groups + groups, :] = gathered[n] * (rate[n] * LN2)

    small[...] = jnp.zeros_like(small)
    for group in range(groups):
        small[:states, group * 128 : group * 128 + 128] = decay_acc[
            pl.ds(group, states, stride=groups), :
        ]
    skip = skip_ref[...]
    bias_sum = jnp.zeros((1, conv_ref.shape[1]), F32)
    skip_sum = jnp.zeros((1, conv_ref.shape[1]), F32)
    for start in range(0, rows, 16):
        here = slice(start, start + 16)

        def natural(read):
            return jnp.concatenate(
                [
                    jnp.concatenate(
                        [
                            read(((start // 8 + half) * groups + group) * 8)
                            for group in range(groups)
                        ],
                        axis=1,
                    )
                    for half in range(2)
                ],
                axis=0,
            )

        size = natural(lambda first: dt_ref[0, first : first + 8, :])
        inner = natural(lambda first: qs[first : first + 8, :])
        slope = natural(lambda first: dds[first : first + 8, :])
        out = natural(lambda first: ys[first : first + 8, :])
        conv = conv_ref[here, :].astype(F32)
        gate = gate_ref[here, :].astype(F32)
        grad = grad_ref[here, :].astype(F32)
        sig = sigmoid(gate)
        scan_grad = grad * gate * sig
        tiny = size * (1.0 - 0.5 * size * (1.0 - size * (1.0 / 3.0) * (1.0 - 0.25 * size)))
        step_slope = jnp.where(size < 0.03, tiny, 1.0 - jnp.exp(-size))
        d_pre = (LN2 * slope + conv * inner) * step_slope
        pre_ref[here, :] = d_pre.astype(BF)
        bias_sum = bias_sum + jnp.sum(d_pre, axis=0, keepdims=True)
        skip_sum = skip_sum + jnp.sum(scan_grad * conv, axis=0, keepdims=True)
        scan_out[here, :] = (size * inner + skip * scan_grad).astype(BF)
        gate_out[here, :] = (
            grad * (out + skip * conv) * (sig * (1.0 + gate * (1.0 - sig)))
        ).astype(BF)
    small[states : states + 1, :] = bias_sum
    small[states + 1 : states + 2, :] = skip_sum
    small_ref[...] = small[...].astype(BF)

    pre_bf = pre_ref[...]
    prod_ref[...] = dot(low_ref[...], pre_bf, TN).astype(BF)
    lanes = lax.broadcasted_iota(jnp.int32, (2 * states, 128), 0)
    coefs = jnp.zeros((2 * states, rows), F32)
    for n in range(states):
        at = pl.ds(n, rows, stride=states)
        for kind, source in enumerate((coef_in, coef_out)):
            pick = jnp.where(lanes == kind * states + n, 1.0, 0.0).astype(BF)
            coefs = coefs + dot(pick, source[at, :].astype(BF), NT)
    wide = dot(weight_ref[...], pre_bf, NT)

    @pl.when(step == 0)
    def _():
        acc[:low_rank, :] = wide
        acc[low_rank:, :] = coefs

    @pl.when(step > 0)
    def _():
        acc[:low_rank, :] += wide
        acc[low_rank:, :] += coefs

    @pl.when(step == pl.num_programs(0) - 1)
    def _():
        size = acc.shape[0] // peers
        for mask in range(peers):
            first = piece_start(peers, mask, size)
            pieces[mask][...] = acc[pl.ds(first, size), :].astype(BF)


def scan_call(
    peers, coef, low, dt, decay, conv_out, gate, grad, step_weight, skip, befores, afters
):
    rows, chans = conv_out.shape
    low_rank = step_weight.shape[0]
    chunks, states, groups, _ = decay.shape
    width = groups * 128
    hops = len(befores)
    wide = low_rank + 2 * states
    lead = lambda *shape: pl.BlockSpec((1,) + shape, lambda i: (i,) + (0,) * len(shape))
    tall = pltpu.VMEM((rows * groups, 128), F32)
    return pl.pallas_call(
        functools.partial(scan_kernel, peers, hops, states),
        grid=(chunks,),
        in_specs=[
            pl.BlockSpec(memory_space=pltpu.SMEM),
            whole((rows, low_rank)),
            lead(rows * groups, 128),
            lead(states, groups, 128),
            columns(rows, width),
            columns(rows, width),
            columns(rows, width),
            columns(low_rank, width),
            columns(1, width),
        ]
        + [lead(states + 2, groups, 128)] * (2 * hops),
        out_specs=[
            columns(rows, width),
            columns(rows, width),
            columns(rows, width),
            columns(32, width),
            columns(low_rank, width),
        ]
        + [whole((wide // peers, rows))] * peers,
        out_shape=[
            sds((rows, chans), BF),
            sds((rows, chans), BF),
            sds((rows, chans), BF),
            sds((32, chans), BF),
            sds((low_rank, chans), BF),
        ]
        + [sds((wide // peers, rows), BF)] * peers,
        scratch_shapes=[
            tall,
            tall,
            tall,
            tall,
            tall,
            tall,
            pltpu.VMEM((rows, states, groups, 128), F32),
            pltpu.VMEM((rows * states, 128), F32),
            pltpu.VMEM((rows * states, 128), F32),
            pltpu.VMEM((states, groups, 128), F32),
            pltpu.VMEM((states * groups, 128), F32),
            pltpu.VMEM((wide, rows), F32),
            pltpu.VMEM((32, width), F32),
        ],
        compiler_params=params(),
        name="scan_gradients",
    )(coef, low, dt, decay, conv_out, gate, grad, step_weight, skip, *befores, *afters)


def gather_kernel(peers, places, low_rank, *refs):
    parts, refs = refs[:peers], refs[peers:]
    whole_ref, cuts, full = refs[0], refs[1 : 1 + places], refs[1 + places]
    place = lax.axis_index("ctx")
    size = full.shape[0] // peers
    for mask in range(peers):
        full[pl.ds(piece_start(peers, mask, size), size), :] = parts[mask][...].astype(F32)
    whole_ref[...] = full[...].astype(BF)
    rank_rows = low_rank // places
    coef_rows = (full.shape[0] - low_rank) // places
    for hop in range(places):
        target = lax.rem(place + hop, places)
        cuts[hop][...] = jnp.concatenate(
            [
                full[pl.ds(target * rank_rows, rank_rows), :],
                full[pl.ds(low_rank + target * coef_rows, coef_rows), :],
            ],
            axis=0,
        ).astype(BF)


def gather_call(parts, places, low_rank):
    size, rows = parts[0].shape
    peers = len(parts)
    cut = (size * peers // places, rows)
    return pl.pallas_call(
        functools.partial(gather_kernel, peers, places, low_rank),
        out_shape=[sds((size * peers, rows), BF)] + [sds(cut, BF)] * places,
        scratch_shapes=[pltpu.VMEM((size * peers, rows), F32)],
        compiler_params=params(),
        name="gather_back",
    )(*parts)


def conv_grad_kernel(back_ref, proj_ref, scan_ref, input_ref, rim_ref, weight_ref, bias_ref,
                     out_ref, tail_ref, head_ref, small_ref, ext, grad):
    taps = weight_ref.shape[0]
    rows = input_ref.shape[0]
    fill_extended(ext, rim_ref, input_ref, taps)
    d_xc = dot(back_ref[...], proj_ref[...], TN)
    sums = [jnp.zeros((1, input_ref.shape[1]), F32) for _ in range(taps + 1)]
    for start in range(0, rows, 16):
        here = slice(start, start + 16)
        pre = conv_block(ext, weight_ref, bias_ref[...], taps, start, 16)
        sig = sigmoid(pre)
        value = (d_xc[here, :] + scan_ref[here, :].astype(F32)) * (sig * (1.0 + pre * (1.0 - sig)))
        grad[here, :] = value
        for tap in range(taps):
            first = 8 - (taps - 1) + tap + start
            sums[tap] = sums[tap] + jnp.sum(value * ext[first : first + 16, :], axis=0, keepdims=True)
        sums[taps] = sums[taps] + jnp.sum(value, axis=0, keepdims=True)
    grad[rows : rows + 8, :] = jnp.zeros((8, grad.shape[1]), F32)
    for start in range(0, rows, 16):
        total = jnp.zeros((16, grad.shape[1]), F32)
        for tap in range(taps):
            first = start + taps - 1 - tap
            total = total + weight_ref[tap : tap + 1, :] * grad[first : first + 16, :]
        out_ref[start : start + 16, :] = total.astype(BF)
    tail_ref[...] = total
    head_ref[...] = grad[0:8, :]
    small_ref[...] = jnp.concatenate(
        sums + [jnp.zeros((small_ref.shape[0] - taps - 1, small_ref.shape[1]), F32)], axis=0
    )


def conv_grad_call(back, proj_weight, scan_part, conv_input, rim, weight, bias):
    rows, chans = conv_input.shape
    taps = weight.shape[0]
    wide = proj_weight.shape[0]
    width = min(512, chans)
    return pl.pallas_call(
        conv_grad_kernel,
        grid=(chans // width,),
        in_specs=[
            whole((wide, rows)),
            columns(wide, width),
            columns(rows, width),
            columns(rows, width),
            columns(taps - 1, width),
            columns(taps, width),
            columns(1, width),
        ],
        out_specs=[columns(rows, width), columns(16, width), columns(8, width), columns(8, width)],
        out_shape=[
            sds((rows, chans), BF),
            sds((16, chans), F32),
            sds((8, chans), F32),
            sds((8, chans), F32),
        ],
        scratch_shapes=[pltpu.VMEM((rows + 8, width), F32), pltpu.VMEM((rows + 8, width), F32)],
        compiler_params=params(),
        name="conv_gradients",
    )(back, proj_weight, scan_part, conv_input, rim, weight, bias)


def rows_kernel(places, rank_rows, *refs):
    cuts, conv_ref, out_ref, coef_ref = refs[:places], refs[places], refs[places + 1], refs[places + 2]
    place = lax.axis_index("ctx")
    total = None
    for hop in range(places):
        source = lax.rem(place + places - hop, places)
        part = dot(cuts[hop][...], conv_ref[source])
        total = part if total is None else total + part
    out_ref[...] = total[:rank_rows, :]
    coef_ref[...] = total[rank_rows:, :]


def rows_call(cuts, conv_all, rank_rows):
    places, rows, chans = conv_all.shape
    cut = cuts[0].shape
    width = min(512, chans)
    return pl.pallas_call(
        functools.partial(rows_kernel, places, rank_rows),
        grid=(chans // width,),
        in_specs=[whole(cut)] * places
        + [pl.BlockSpec((places, rows, width), lambda i: (0, 0, i))],
        out_specs=[columns(rank_rows, width), columns(cut[0] - rank_rows, width)],
        out_shape=[sds((rank_rows, chans), F32), sds((cut[0] - rank_rows, chans), F32)],
        compiler_params=params(),
        name="row_gradients",
    )(*cuts, conv_all)


def last_kernel(places, states, taps, *refs):
    (main_ref, tail_ref, next_ref, weight_ref) = refs[:4]
    early, refs = refs[4 : 4 + places], refs[4 + places :]
    late, refs = refs[:places], refs[places:]
    (out_ref, conv_w, conv_b, step_b, decay, skip, fix) = refs
    fix[...] = tail_ref[...]
    for row in range(taps - 1):
        extra = jnp.zeros((1, fix.shape[1]), F32)
        for tap in range(row + 1):
            extra = extra + weight_ref[tap : tap + 1, :] * next_ref[row - tap : row - tap + 1, :]
        at = 16 - (taps - 1) + row
        fix[at : at + 1, :] += extra
    out_ref[...] = fix[...].astype(BF)
    total = early[0][...].astype(F32)
    for part in early[1:]:
        total = total + part[...].astype(F32)
    decay[...] = total[:states, :]
    step_b[...] = total[states : states + 1, :]
    skip[...] = total[states + 1 : states + 2, :]
    total = late[0][...]
    for part in late[1:]:
        total = total + part[...]
    conv_w[...] = total[:taps, :]
    conv_b[...] = total[taps : taps + 1, :]


def last_call(main, tail, following, weight, early, late, states):
    rows, chans = main.shape
    taps = weight.shape[0]
    places = len(early)
    width = chans
    return pl.pallas_call(
        functools.partial(last_kernel, places, states, taps),
        grid=(1,),
        in_specs=[pl.BlockSpec(memory_space=pl.ANY), columns(16, width), columns(8, width), columns(taps, width)]
        + [columns(32, width)] * places
        + [columns(8, width)] * places,
        out_specs=[
            pl.BlockSpec((16, width), lambda i: (rows // 16 - 1, i)),
            columns(taps, width),
            columns(1, width),
            columns(1, width),
            columns(states, width),
            columns(1, width),
        ],
        out_shape=[
            sds((rows, chans), BF),
            sds((taps, chans), F32),
            sds((1, chans), F32),
            sds((1, chans), F32),
            sds((states, chans), F32),
            sds((1, chans), F32),
        ],
        scratch_shapes=[pltpu.VMEM((16, width), F32)],
        input_output_aliases={0: 0},
        compiler_params=params(),
        name="last_rows",
    )(main, tail, following, weight, *early, *late)


def chan_sum(pieces):
    if len(pieces) == 1:
        return [lax.psum(pieces[0], "chan")]
    total = pieces[0].astype(F32)
    for mask in range(1, len(pieces)):
        total = total + swap(pieces[mask], "chan", mask).astype(F32)
    total = total.astype(BF)
    return [total] + [swap(total, "chan", mask) for mask in range(1, len(pieces))]


def body(
    conv_input,
    gate_input,
    out_grad,
    conv_weight,
    conv_bias,
    proj_weight,
    step_weight,
    step_bias,
    decay_log,
    skip_gain,
):
    rows, chans = conv_input.shape
    taps = conv_weight.shape[0]
    low_rank = step_weight.shape[0]
    states = decay_log.shape[0]
    peers = lax.axis_size("chan")
    if rows % (16 * peers) or peers & (peers - 1):
        peers = 1
    places = lax.axis_size("ctx")
    groups = group_rows(chans)
    decay = decay_log.reshape(states, -1, groups, 128).transpose(1, 0, 2, 3)
    conv_bias = conv_bias[None, :]
    step_bias = step_bias[None, :]
    skip_gain = skip_gain[None, :]

    rim = shift(conv_input[rows - (taps - 1) :], "ctx", 1)
    conv_out, *pieces = conv_call(peers, conv_input, rim, conv_weight, conv_bias, proj_weight)
    conv_all = lax.all_gather(conv_out, "ctx")
    parts = chan_sum(pieces)
    dt, fwd, bwd, coef, low = local_call(
        parts, step_weight, step_bias, decay, conv_out, gate_input, out_grad, states
    )
    befores = [shift(fwd, "ctx", hop) for hop in range(1, places)]
    afters = [shift(bwd, "ctx", -hop) for hop in range(1, places)]
    pre_bf, grad_gate, scan_part, small, products, *pieces = scan_call(
        peers, coef, low, dt, decay, conv_out, gate_input, out_grad, step_weight, skip_gain,
        befores, afters,
    )
    grad_step = lax.psum_scatter(products, "ctx", scatter_dimension=0, tiled=True).astype(F32)
    early = [small] + [rotate(small, "ctx", hop) for hop in range(1, places)]
    back, *cuts = gather_call(chan_sum(pieces), places, low_rank)
    cuts = [cuts[0]] + [rotate(cuts[hop], "ctx", hop) for hop in range(1, places)]
    main, tail, head, sums = conv_grad_call(
        back, proj_weight, scan_part, conv_input, rim, conv_weight, conv_bias
    )
    following = shift(head, "ctx", -1)
    late = [sums] + [rotate(sums, "ctx", hop) for hop in range(1, places)]
    grad_proj, grad_coef = rows_call(cuts, conv_all, low_rank // places)
    grad_input, conv_w, conv_b, step_b, decay_grad, skip = last_call(
        main, tail, following, conv_weight, early, late, states
    )
    return (
        grad_input,
        grad_gate,
        grad_proj,
        grad_coef,
        grad_step,
        conv_w,
        conv_b[0],
        step_b[0],
        decay_grad,
        skip[0],
    )


def solution(mesh):
    tokens, columns_, chan = P("ctx", "chan"), P(None, "chan"), P("chan")
    in_specs = (
        tokens, tokens, tokens, columns_, chan, columns_, columns_, chan, columns_, chan,
    )
    out_specs = (
        tokens, tokens, tokens, tokens, tokens, columns_, chan, chan, columns_, chan,
    )
    return jax.shard_map(body, mesh=mesh, in_specs=in_specs, out_specs=out_specs, check_vma=False)
```

time: 1060 us -> 181 us (0.17); the launches traced: 1050 us -> 180 us
  local copies, waits for them, and re-layouts: 444 us -> 5.81 us
  other arithmetic: 342 us -> 2.9 us
  blocking collectives: 136 us -> 0 us
  Pallas kernels: 0 us -> 58.9 us
  starting transfers between devices: 6.33 us -> 56.3 us
  loops' own time: 28.1 us -> 0 us
  waiting for transfers between devices: 60.7 us -> 41.7 us
  matrix products: 16.1 us -> 0 us
    pad x40 -> x0, local copies, waits for them, and re-layouts: 346 us -> none  [block_scan(): return lax.associative_scan(linear_combine, (factor, source), axis=0)[1]]
    add x52 -> x0, other arithmetic: 147 us -> none  [the longest x24 80.5 us: block_scan(): return lax.associative_scan(linear_combine, (factor, source), axis=0)[1]]
    psum x3 -> x0, blocking collectives: 71.6 us -> none  [the longest x1 26.7 us: body(): back_proj = lax.psum(back_part, 'chan').astype(jnp.bfloat16)]
    all_gather x4 -> x0, blocking collectives: 63.9 us -> none  [the longest x2 32.8 us: entering(): gathered = jax.tree.map(lambda a: lax.all_gather(a, axis), part)]
    reduce_sum x11 -> x0, other arithmetic: 63.4 us -> none  [the longest x2 28.4 us: gradient_block(): jnp.sum(adjoint * (decay_rate[None] * decayed + in_part[:, :, None] * con...]
    mul x19 -> x0, other arithmetic: 59.4 us -> none  [the longest x16 57.4 us: linear_combine(): return (earlier[0] * later[0], later[0] * earlier[1] + later[1])]
    pallas_call x0 -> x7, Pallas kernels: none -> 58.9 us  [the longest x1 27 us: scan_call(): pl.pallas_call(functools.partial(scan_kernel, peers, hops, states), grid=...]
    ppermute x2 -> x45, starting transfers between devices: 6.21 us -> 56.3 us  [the longest x28 25.3 us: swap(): return lax.ppermute(block, axis, [(i, i ^ mask) for i in range(count)])]
  transfers between devices with their start and end apart: 5 -> 47, of which waited for: 4 -> 16; matrix products, arithmetic and copies ran while one was open for 2% -> 1% of each run, Pallas kernels for 0% -> 30%
where the time goes in v1:
time: 181 us; the launch traced here: 180 us
  Pallas kernels  58.9 us (33%)
  starting transfers between devices  56.3 us (31%)
  waiting for transfers between devices  41.7 us (23%)
  between operations  14.6 us (8%)
  local copies, waits for them, and re-layouts  5.81 us (3%)
  other arithmetic  2.9 us (2%)
    pallas_call x1, Pallas kernels, scan_call(): pl.pallas_call(functools.partial(scan_kernel, peers, hops, states), grid=...  27 us
    ppermute x28, starting transfers between devices, swap(): return lax.ppermute(block, axis, [(i, i ^ mask) for i in range(count)])  25.3 us
    ppermute x8, starting transfers between devices, shift(): return lax.ppermute(block, axis, route)  20.1 us
    ppermute x8, waiting for transfers between devices, shift(): return lax.ppermute(block, axis, route)  17.5 us
    ppermute x9, waiting for transfers between devices, rotate(): lax.ppermute(block, axis, [(i, (i + distance) % count) for i in range(cou...  14.3 us
    pallas_call x1, Pallas kernels, local_call(): pl.pallas_call(functools.partial(local_kernel, peers, low_rank, states),...  12.7 us
    ppermute x9, starting transfers between devices, rotate(): lax.ppermute(block, axis, [(i, (i + distance) % count) for i in range(cou...  10.9 us
    ppermute x28, waiting for transfers between devices, swap(): return lax.ppermute(block, axis, [(i, i ^ mask) for i in range(count)])  9.87 us
  transfers between devices with their start and end apart: 47, of which 16 were waited for; matrix products, arithmetic and copies ran while one was open for 1% of the time, Pallas kernels for 30%

profile of v1, /device:TPU:0, one launch (start us, length us, event | category | flops | bytes accessed | tf_op | source)
XLA Modules:
  0.0 180.4 jit_solution(6604146180084368407)
XLA Ops:
  7.2 0.8 slice.3
  8.0 4.9 %collective-permute-start = (bf16[3,2048]{1,0:T(4,128)(2,1)S(1)}, bf16[3,2048]{1,0:T(4,128)(2,1)S(1)}, u32[]{:S(2)}, u32[]{:S(2)}) collective-permute-start(bf16[3,2048]{1,0:T(4,128)(2,1)S(1)} %slice.3), channel_id=1, source_target_pairs={{0,8},{8,16},{16,24},{1,9},{9,17},{17,25},{2,10},{10,18},{18,26},{... | collective-permute-start | bytes 36872 | tf_op jit(solution)/shard_map/ppermute | solution.py:67
  13.0 1.4 collective-permute-done.rim_ref
  14.4 0.6 copy-done.13
  15.0 4.9 %conv_project.1 = (bf16[128,2048]{1,0:T(8,128)(2,1)}, bf16[16,544]{1,0:T(8,128)(2,1)}, bf16[16,544]{1,0:T(8,128)(2,1)}, bf16[16,544]{1,0:T(8,128)(2,1)}, bf16[16...) custom-call(bf16[128,2048]{1,0:T(8,128)(2,1)} %input_ref.3, ...), custom_call_target="tpu_custom_call" | custom-call | tf_op jit(solution)/shard_map/conv_project/pallas_call | solution.py:116
  19.9 1.1 collective-permute-start.7
  21.0 1.5 collective-permute-start.6
  22.5 1.4 collective-permute-start.5
  24.4 0.7 collective-permute-start.3
  25.1 0.9 collective-permute-start.2
  26.3 1.5 collective-permute-done.4
  27.9 1.4 collective-permute-done.2
  29.2 0.8 add_convert_fusion.refs_0_
  30.1 0.8 collective-permute-start.9
  30.9 1.0 collective-permute-start.10
  32.0 0.7 collective-permute-start.11
  32.7 1.0 collective-permute-start.12
  33.7 1.6 collective-permute-start.13
  35.3 1.1 collective-permute-start.14
  36.4 0.7 copy.24
  37.1 1.2 collective-permute-done.13.refs_6_
  38.3 1.0 collective-permute-done.14.refs_7_
  40.0 12.7 %local_ends.1 = (f32[2,1024,128]{2,1,0:T(8,128)}, bf16[2,18,8,128]{3,2,1,0:T(8,128)(2,1)}, bf16[2,18,8,128]{3,2,1,0:T(8,128)(2,1)}, f32[128,128]{1,0:T(8,128)}, bf16[128,512]{1,0:T(8,128)(2,1)}) custom-call(bf16[16,544]{1,0:T(8,128)(2,1)} %copy-done.5, bf16[16,544]{1,0:T(8,128)(2,1)} %copy-done.21, bf16[16,544]{1,0:T(8,128)(2,1)} %copy-done.22, ...), custom_call_target="tpu_custom_call" | custom-call | tf_op jit(solution)/shard_map/local_ends/pallas_call | solution.py:242
  52.7 4.2 %collective-permute-start.15 = (bf16[2,18,8,128]{3,2,1,0:T(8,128)(2,1)}, bf16[2,18,8,128]{3,2,1,0:T(8,128)(2,1)S(1)}, u32[]{:S(2)}, u32[]{:S(2)}) collective-permute-start(bf16[2,18,8,128]{3,2,1,0:T(8,128)(2,1)} %get-tuple-element.65), channel_id=1, source_target_pairs={{0,8},{8,16},{16,24},{1,9},{9,17},{17,25},{2,10},{10,18},{18,26},{... | collective-permute-start | bytes 221192 | tf_op jit(solution)/shard_map/ppermute | solution.py:67
  57.0 4.5 %collective-permute-start.16 = (bf16[2,18,8,128]{3,2,1,0:T(8,128)(2,1)}, bf16[2,18,8,128]{3,2,1,0:T(8,128)(2,1)S(1)}, u32[]{:S(2)}, u32[]{:S(2)}) collective-permute-start(bf16[2,18,8,128]{3,2,1,0:T(8,128)(2,1)} %get-tuple-element.65), channel_id=1, source_target_pairs={{0,16},{8,24},{1,17},{9,25},{2,18},{10,26},{3,19},{11,27},{4,20},{... | collective-permute-start | bytes 221192 | tf_op jit(solution)/shard_map/ppermute | solution.py:67
  61.5 1.3 collective-permute-start.17
  62.8 1.3 collective-permute-start.18
  64.1 1.3 collective-permute-start.19
  65.4 1.3 collective-permute-start.20
  66.7 2.2 %collective-permute-done.17.refs_11_ = bf16[2,18,8,128]{3,2,1,0:T(8,128)(2,1)S(1)} collective-permute-done((bf16[2,18,8,128]{3,2,1,0:T(8,128)(2,1)}, bf16[2,18,8,128]{3,2,1,0:T(8,128)(2,1)S(1)}, u32[]{:S(2)}, u32[]{:S(2)}) %collective-permute-start.17) | collective-permute-done | bytes 73760 | tf_op jit(solution)/shard_map/ppermute | solution.py:67
  68.9 0.6 collective-permute-done.18.refs_12_
  69.5 1.9 %collective-permute-done.19.refs_13_ = bf16[2,18,8,128]{3,2,1,0:T(8,128)(2,1)S(1)} collective-permute-done((bf16[2,18,8,128]{3,2,1,0:T(8,128)(2,1)}, bf16[2,18,8,128]{3,2,1,0:T(8,128)(2,1)S(1)}, u32[]{:S(2)}, u32[]{:S(2)}) %collective-permute-start.19) | collective-permute-done | bytes 73760 | tf_op jit(solution)/shard_map/ppermute | solution.py:67
  71.4 3.7 %collective-permute-done.20.refs_14_ = bf16[2,18,8,128]{3,2,1,0:T(8,128)(2,1)S(1)} collective-permute-done((bf16[2,18,8,128]{3,2,1,0:T(8,128)(2,1)}, bf16[2,18,8,128]{3,2,1,0:T(8,128)(2,1)S(1)}, u32[]{:S(2)}, u32[]{:S(2)}) %collective-permute-start.20) | collective-permute-done | bytes 73760 | tf_op jit(solution)/shard_map/ppermute | solution.py:67
  75.1 0.6 copy-done.12
  75.7 27.0 %scan_gradients.1 = (bf16[128,2048]{1,0:T(8,128)(2,1)}, bf16[128,2048]{1,0:T(8,128)(2,1)}, bf16[128,2048]{1,0:T(8,128)(2,1)}, bf16[32,2048]{1,0:T(8,128)(2,1)}, ...) custom-call(f32[128,128]{1,0:T(8,128)} %get-tuple-element.62.refs_0_, ...), custom_call_target="tpu_custom_call" | custom-call | tf_op jit(solution)/shard_map/scan_gradients/pallas_call | solution.py:491
  102.8 0.6 copy-done.45
  103.7 1.6 collective-permute-start.26
  105.3 1.0 collective-permute-start.25
  106.4 1.4 collective-permute-start.24
  107.8 1.0 collective-permute-start.22
  108.9 0.8 collective-permute-start.21
  110.2 0.8 collective-permute-done.23
  111.0 0.8 collective-permute-done.22
  112.0 1.2 collective-permute-start.29
  113.1 0.6 collective-permute-start.30
  113.8 0.7 collective-permute-start.31
  114.5 1.0 collective-permute-start.32
  115.5 1.2 collective-permute-start.33
  116.7 1.5 collective-permute-start.34
  118.2 1.9 %collective-permute-done.33.refs_6_ = bf16[68,128]{1,0:T(8,128)(2,1)S(1)} collective-permute-done((bf16[68,128]{1,0:T(8,128)(2,1)S(1)}, bf16[68,128]{1,0:T(8,128)(2,1)S(1)}, u32[]{:S(2)}, u32[]{:S(2)}) %collective-permute-start.33) | collective-permute-done | bytes 17440 | tf_op jit(solution)/shard_map/ppermute | solution.py:56
  120.1 0.6 collective-permute-done.34.refs_7_
  121.4 1.6 gather_back.1
  123.0 6.6 %conv_gradients.1 = (bf16[128,2048]{1,0:T(8,128)(2,1)}, f32[16,2048]{1,0:T(8,128)}, f32[8,2048]{1,0:T(8,128)}, f32[8,2048]{1,0:T(8,128)}) custom-call(bf16[544,128]{1,0:T(8,128)(2,1)} %get-tuple-element.75.back_ref, bf16[544,2048]{1,0:T(8,128)(2,1)} %proj_ref.3, bf16[128,2048]{1,0:T(8,128)(2,1)} %get-tuple-element.76.scan_ref, bf16[128,2048]{1,0:T(8,128)(2,1)} %input_ref.3, ...), custom_call_target="tpu_custom_call" | custom-call | tf_op jit(solution)/shard_map/conv_gradients/pallas_call | solution.py:612
  129.6 1.3 collective-permute-start.35
  130.9 2.7 %collective-permute-start.39 = (f32[8,2048]{1,0:T(8,128)}, f32[8,2048]{1,0:T(8,128)S(1)}, u32[]{:S(2)}, u32[]{:S(2)}) collective-permute-start(f32[8,2048]{1,0:T(8,128)} %get-tuple-element.81.refs_8_), channel_id=1, source_target_pairs={{0,8},{8,16},{16,24},{24,0},{1,9},{9,17},{17,25},{25,1},{2,10},{10... | collective-permute-start | bytes 196616 | tf_op jit(solution)/shard_map/ppermute | solution.py:61
  133.7 1.7 collective-permute-start.37
  135.4 2.1 %collective-permute-start.38 = (bf16[32,2048]{1,0:T(8,128)(2,1)S(1)}, bf16[32,2048]{1,0:T(8,128)(2,1)S(1)}, u32[]{:S(2)}, u32[]{:S(2)}) collective-permute-start(bf16[32,2048]{1,0:T(8,128)(2,1)S(1)} %copy-done), channel_id=1, source_target_pairs={{0,24},{8,0},{16,8},{24,16},{1,25},{9,1},{17,9},{25,17},{2,26},{10... | collective-permute-start | bytes 393224 | tf_op jit(solution)/shard_map/ppermute | solution.py:61
  137.5 7.7 %collective-permute-done.35.refs_2_ = f32[8,2048]{1,0:T(8,128)S(1)} collective-permute-done((f32[8,2048]{1,0:T(8,128)}, f32[8,2048]{1,0:T(8,128)S(1)}, u32[]{:S(2)}, u32[]{:S(2)}) %collective-permute-start.35) | collective-permute-done | bytes 65568 | tf_op jit(solution)/shard_map/ppermute | solution.py:67
  145.3 14.2 %collective-permute-done.40.refs_10_ = f32[8,2048]{1,0:T(8,128)S(1)} collective-permute-done((f32[8,2048]{1,0:T(8,128)}, f32[8,2048]{1,0:T(8,128)S(1)}, u32[]{:S(2)}, u32[]{:S(2)}) %collective-permute-start.40) | collective-permute-done | bytes 65568 | tf_op jit(solution)/shard_map/ppermute | solution.py:61
  159.6 2.0 %collective-permute-start.43 = (bf16[136,128]{1,0:T(8,128)(2,1)S(1)}, bf16[136,128]{1,0:T(8,128)(2,1)S(1)}, u32[]{:S(2)}, u32[]{:S(2)}) collective-permute-start(bf16[136,128]{1,0:T(8,128)(2,1)S(1)} %copy-done.37), channel_id=1, source_target_pairs={{0,16},{8,24},{16,0},{24,8},{1,17},{9,25},{17,1},{25,9},{2,18},{10... | collective-permute-start | bytes 104456 | tf_op jit(solution)/shard_map/ppermute | solution.py:61
  161.5 2.3 %collective-permute-start.44 = (bf16[136,128]{1,0:T(8,128)(2,1)S(1)}, bf16[136,128]{1,0:T(8,128)(2,1)S(1)}, u32[]{:S(2)}, u32[]{:S(2)}) collective-permute-start(bf16[136,128]{1,0:T(8,128)(2,1)S(1)} %copy-done.36), channel_id=1, source_target_pairs={{0,24},{8,0},{16,8},{24,16},{1,25},{9,1},{17,9},{25,17},{2,26},{10... | collective-permute-start | bytes 104456 | tf_op jit(solution)/shard_map/ppermute | solution.py:61
  164.6 2.0 %last_rows.1 = (bf16[128,2048]{1,0:T(8,128)(2,1)}, f32[4,2048]{1,0:T(4,128)}, f32[1,2048]{1,0:T(1,128)}, f32[1,2048]{1,0:T(1,128)}, f32[16,2048]{1,0:T(8,128)}, /*index=5*/f32[1,2048]{1,0:T(1,128)}) custom-call(bf16[128,2048]{1,0:T(8,128)(2,1)} %get-tuple-element.77.refs_0_, f32[16,2048]{1,0:T(8,128)} %get-tuple-element.78.refs_1_, ...), custom_call_target="tpu_custom_call", output_to_operand_aliasing={{0}: (0, {})} | custom-call | tf_op jit(solution)/shard_map/last_rows/pallas_call | solution.py:696
  167.2 4.2 %row_gradients.1 = (f32[128,2048]{1,0:T(8,128)}, f32[8,2048]{1,0:T(8,128)}) custom-call(bf16[136,128]{1,0:T(8,128)(2,1)} %get-tuple-element.84.refs_0_, bf16[136,128]{1,0:T(8,128)(2,1)} %copy-done.18, bf16[136,128]{1,0:T(8,128)(2,1)} %copy-done.19, bf16[136,128]{1,0:T(8,128)(2,1)} %copy-done.20, bf16[4,128,2048]{2,1,0:T(8,128)(2,1)} %bitcast.13), custom_call_target="tpu_custom_call" | custom-call | tf_op jit(solution)/shard_map/row_gradients/pallas_call | solution.py:653
  171.4 2.1 %convert_element_type.75 = f32[128,2048]{1,0:T(8,128)} convert(bf16[128,2048]{1,0:T(8,128)(2,1)} %reduce-scatter.2.cloned.1.call-done) | non-fusion elementwise | flops 262144 | bytes 1572864 | tf_op jit(solution)/shard_map/convert_element_type | solution.py:774
  (137 shorter events, 4.7 us)
Async XLA Ops:
  7.2 29.2 %copy-start.4 = (f32[16,2048]{1,0:T(8,128)S(1)}, f32[16,2048]{1,0:T(8,128)}, u32[]{:S(2)}) copy-start(f32[16,2048]{1,0:T(8,128)} %param.18) | copy-start | bytes 393220
  7.2 159.5 %all-gather.3.cloned.1.call-start = ((), (), s32[]{:S(2)}) async-start(), calls=%async_computation.2 | async-start | bytes 2621440 | tf_op jit(solution)/shard_map/all_gather | solution.py:763
  8.0 6.4 %collective-permute-start = (bf16[3,2048]{1,0:T(4,128)(2,1)S(1)}, bf16[3,2048]{1,0:T(4,128)(2,1)S(1)}, u32[]{:S(2)}, u32[]{:S(2)}) collective-permute-start(bf16[3,2048]{1,0:T(4,128)(2,1)S(1)} %slice.3), channel_id=1, source_target_pairs={{0,8},{8,16},{16,24},{1,9},{9,17},{17,25},{2,10},{10,18},{18,26},{... | collective-permute-start | bytes 36872 | tf_op jit(solution)/shard_map/ppermute | solution.py:67
  19.9 151.5 %reduce-scatter.2.cloned.1.call-start = ((), (), s32[]{:S(2)}) async-start(), calls=%async_computation.1 | async-start | bytes 2621440 | tf_op jit(solution)/shard_map/reduce_scatter | solution.py:774
  19.9 5.2 %collective-permute-start.7 = (bf16[16,544]{1,0:T(8,128)(2,1)}, bf16[16,544]{1,0:T(8,128)(2,1)S(1)}, u32[]{:S(2)}, u32[]{:S(2)}) collective-permute-start(bf16[16,544]{1,0:T(8,128)(2,1)} %get-tuple-element.60), channel_id=1, source_target_pairs={{0,7},{1,6},{2,5},{3,4},{4,3},{5,2},{6,1},{7,0},{8,15},{9,14},{10,... | collective-permute-start | bytes 52232 | tf_op jit(solution)/shard_map/ppermute | solution.py:56
  21.0 5.0 %collective-permute-start.6 = (bf16[16,544]{1,0:T(8,128)(2,1)}, bf16[16,544]{1,0:T(8,128)(2,1)S(1)}, u32[]{:S(2)}, u32[]{:S(2)}) collective-permute-start(bf16[16,544]{1,0:T(8,128)(2,1)} %get-tuple-element.59), channel_id=1, source_target_pairs={{0,6},{1,7},{2,4},{3,5},{4,2},{5,3},{6,0},{7,1},{8,14},{9,15},{10,... | collective-permute-start | bytes 52232 | tf_op jit(solution)/shard_map/ppermute | solution.py:56
  22.5 3.8 %collective-permute-start.5 = (bf16[16,544]{1,0:T(8,128)(2,1)}, bf16[16,544]{1,0:T(8,128)(2,1)S(1)}, u32[]{:S(2)}, u32[]{:S(2)}) collective-permute-start(bf16[16,544]{1,0:T(8,128)(2,1)} %get-tuple-element.58), channel_id=1, source_target_pairs={{0,5},{1,4},{2,7},{3,6},{4,1},{5,0},{6,3},{7,2},{8,13},{9,12},{10,... | collective-permute-start | bytes 52232 | tf_op jit(solution)/shard_map/ppermute | solution.py:56
  23.9 4.0 %collective-permute-start.4 = (bf16[16,544]{1,0:T(8,128)(2,1)}, bf16[16,544]{1,0:T(8,128)(2,1)S(1)}, u32[]{:S(2)}, u32[]{:S(2)}) collective-permute-start(bf16[16,544]{1,0:T(8,128)(2,1)} %get-tuple-element.57), channel_id=1, source_target_pairs={{0,4},{1,5},{2,6},{3,7},{4,0},{5,1},{6,2},{7,3},{8,12},{9,13},{10,... | collective-permute-start | bytes 52232 | tf_op jit(solution)/shard_map/ppermute | solution.py:56
  24.4 3.5 %collective-permute-start.3 = (bf16[16,544]{1,0:T(8,128)(2,1)}, bf16[16,544]{1,0:T(8,128)(2,1)S(1)}, u32[]{:S(2)}, u32[]{:S(2)}) collective-permute-start(bf16[16,544]{1,0:T(8,128)(2,1)} %get-tuple-element.56), channel_id=1, source_target_pairs={{0,3},{1,2},{2,1},{3,0},{4,7},{5,6},{6,5},{7,4},{8,11},{9,10},{10,... | collective-permute-start | bytes 52232 | tf_op jit(solution)/shard_map/ppermute | solution.py:56
  25.1 4.1 %collective-permute-start.2 = (bf16[16,544]{1,0:T(8,128)(2,1)}, bf16[16,544]{1,0:T(8,128)(2,1)S(1)}, u32[]{:S(2)}, u32[]{:S(2)}) collective-permute-start(bf16[16,544]{1,0:T(8,128)(2,1)} %get-tuple-element.55), channel_id=1, source_target_pairs={{0,2},{1,3},{2,0},{3,1},{4,6},{5,7},{6,4},{7,5},{8,10},{9,11},{10,... | collective-permute-start | bytes 52232 | tf_op jit(solution)/shard_map/ppermute | solution.py:56
  26.0 3.2 %collective-permute-start.1 = (bf16[16,544]{1,0:T(8,128)(2,1)}, bf16[16,544]{1,0:T(8,128)(2,1)S(1)}, u32[]{:S(2)}, u32[]{:S(2)}) collective-permute-start(bf16[16,544]{1,0:T(8,128)(2,1)} %get-tuple-element.54), channel_id=1, source_target_pairs={{0,1},{1,0},{2,3},{3,2},{4,5},{5,4},{6,7},{7,6},{8,9},{9,8},{10,11... | collective-permute-start | bytes 52232 | tf_op jit(solution)/shard_map/ppermute | solution.py:56
  30.0 9.4 %copy-start.5 = (bf16[16,544]{1,0:T(8,128)(2,1)}, bf16[16,544]{1,0:T(8,128)(2,1)S(1)}, u32[]{:S(2)}) copy-start(bf16[16,544]{1,0:T(8,128)(2,1)S(1)} %add_convert_fusion.refs_0_) | copy-start | bytes 52228
  30.0 3.6 %collective-permute-start.8 = (bf16[16,544]{1,0:T(8,128)(2,1)S(1)}, bf16[16,544]{1,0:T(8,128)(2,1)S(1)}, u32[]{:S(2)}, u32[]{:S(2)}) collective-permute-start(bf16[16,544]{1,0:T(8,128)(2,1)S(1)} %add_convert_fusion.refs_0_), channel_id=1, source_target_pairs={{0,1},{1,0},{2,3},{3,2},{4,5},{5,4},{6,7},{7,6},{8,9},{9,8},{10,11... | collective-permute-start | bytes 52232 | tf_op jit(solution)/shard_map/ppermute | solution.py:56
  30.1 5.2 %collective-permute-start.9 = (bf16[16,544]{1,0:T(8,128)(2,1)S(1)}, bf16[16,544]{1,0:T(8,128)(2,1)S(1)}, u32[]{:S(2)}, u32[]{:S(2)}) collective-permute-start(bf16[16,544]{1,0:T(8,128)(2,1)S(1)} %add_convert_fusion.refs_0_), channel_id=1, source_target_pairs={{0,2},{1,3},{2,0},{3,1},{4,6},{5,7},{6,4},{7,5},{8,10},{9,11},{10,... | collective-permute-start | bytes 52232 | tf_op jit(solution)/shard_map/ppermute | solution.py:56
  30.9 6.1 %collective-permute-start.10 = (bf16[16,544]{1,0:T(8,128)(2,1)S(1)}, bf16[16,544]{1,0:T(8,128)(2,1)S(1)}, u32[]{:S(2)}, u32[]{:S(2)}) collective-permute-start(bf16[16,544]{1,0:T(8,128)(2,1)S(1)} %add_convert_fusion.refs_0_), channel_id=1, source_target_pairs={{0,3},{1,2},{2,1},{3,0},{4,7},{5,6},{6,5},{7,4},{8,11},{9,10},{10,... | collective-permute-start | bytes 52232 | tf_op jit(solution)/shard_map/ppermute | solution.py:56
  32.0 5.1 %collective-permute-start.11 = (bf16[16,544]{1,0:T(8,128)(2,1)S(1)}, bf16[16,544]{1,0:T(8,128)(2,1)S(1)}, u32[]{:S(2)}, u32[]{:S(2)}) collective-permute-start(bf16[16,544]{1,0:T(8,128)(2,1)S(1)} %add_convert_fusion.refs_0_), channel_id=1, source_target_pairs={{0,4},{1,5},{2,6},{3,7},{4,0},{5,1},{6,2},{7,3},{8,12},{9,13},{10,... | collective-permute-start | bytes 52232 | tf_op jit(solution)/shard_map/ppermute | solution.py:56
  32.7 4.4 %collective-permute-start.12 = (bf16[16,544]{1,0:T(8,128)(2,1)S(1)}, bf16[16,544]{1,0:T(8,128)(2,1)S(1)}, u32[]{:S(2)}, u32[]{:S(2)}) collective-permute-start(bf16[16,544]{1,0:T(8,128)(2,1)S(1)} %add_convert_fusion.refs_0_), channel_id=1, source_target_pairs={{0,5},{1,4},{2,7},{3,6},{4,1},{5,0},{6,3},{7,2},{8,13},{9,12},{10,... | collective-permute-start | bytes 52232 | tf_op jit(solution)/shard_map/ppermute | solution.py:56
  33.7 5.7 %copy-start.21 = (bf16[16,544]{1,0:T(8,128)(2,1)}, bf16[16,544]{1,0:T(8,128)(2,1)S(1)}, u32[]{:S(2)}) copy-start(bf16[16,544]{1,0:T(8,128)(2,1)S(1)} %collective-permute-done.8.refs_1_) | copy-start | bytes 52228
  33.7 4.7 %collective-permute-start.13 = (bf16[16,544]{1,0:T(8,128)(2,1)S(1)}, bf16[16,544]{1,0:T(8,128)(2,1)S(1)}, u32[]{:S(2)}, u32[]{:S(2)}) collective-permute-start(bf16[16,544]{1,0:T(8,128)(2,1)S(1)} %add_convert_fusion.refs_0_), channel_id=1, source_target_pairs={{0,6},{1,7},{2,4},{3,5},{4,2},{5,3},{6,0},{7,1},{8,14},{9,15},{10,... | collective-permute-start | bytes 52232 | tf_op jit(solution)/shard_map/ppermute | solution.py:56
  35.3 4.1 %collective-permute-start.14 = (bf16[16,544]{1,0:T(8,128)(2,1)S(1)}, bf16[16,544]{1,0:T(8,128)(2,1)S(1)}, u32[]{:S(2)}, u32[]{:S(2)}) collective-permute-start(bf16[16,544]{1,0:T(8,128)(2,1)S(1)} %add_convert_fusion.refs_0_), channel_id=1, source_target_pairs={{0,7},{1,6},{2,5},{3,4},{4,3},{5,2},{6,1},{7,0},{8,15},{9,14},{10,... | collective-permute-start | bytes 52232 | tf_op jit(solution)/shard_map/ppermute | solution.py:56
  52.7 12.6 %collective-permute-start.15 = (bf16[2,18,8,128]{3,2,1,0:T(8,128)(2,1)}, bf16[2,18,8,128]{3,2,1,0:T(8,128)(2,1)S(1)}, u32[]{:S(2)}, u32[]{:S(2)}) collective-permute-start(bf16[2,18,8,128]{3,2,1,0:T(8,128)(2,1)} %get-tuple-element.65), channel_id=1, source_target_pairs={{0,8},{8,16},{16,24},{1,9},{9,17},{17,25},{2,10},{10,18},{18,26},{... | collective-permute-start | bytes 221192 | tf_op jit(solution)/shard_map/ppermute | solution.py:67
  57.0 9.7 %collective-permute-start.16 = (bf16[2,18,8,128]{3,2,1,0:T(8,128)(2,1)}, bf16[2,18,8,128]{3,2,1,0:T(8,128)(2,1)S(1)}, u32[]{:S(2)}, u32[]{:S(2)}) collective-permute-start(bf16[2,18,8,128]{3,2,1,0:T(8,128)(2,1)} %get-tuple-element.65), channel_id=1, source_target_pairs={{0,16},{8,24},{1,17},{9,25},{2,18},{10,26},{3,19},{11,27},{4,20},{... | collective-permute-start | bytes 221192 | tf_op jit(solution)/shard_map/ppermute | solution.py:67
  61.5 7.4 %collective-permute-start.17 = (bf16[2,18,8,128]{3,2,1,0:T(8,128)(2,1)}, bf16[2,18,8,128]{3,2,1,0:T(8,128)(2,1)S(1)}, u32[]{:S(2)}, u32[]{:S(2)}) collective-permute-start(bf16[2,18,8,128]{3,2,1,0:T(8,128)(2,1)} %get-tuple-element.65), channel_id=1, source_target_pairs={{0,24},{1,25},{2,26},{3,27},{4,28},{5,29},{6,30},{7,31}} | collective-permute-start | bytes 221192 | tf_op jit(solution)/shard_map/ppermute | solution.py:67
  62.8 6.8 %collective-permute-start.18 = (bf16[2,18,8,128]{3,2,1,0:T(8,128)(2,1)}, bf16[2,18,8,128]{3,2,1,0:T(8,128)(2,1)S(1)}, u32[]{:S(2)}, u32[]{:S(2)}) collective-permute-start(bf16[2,18,8,128]{3,2,1,0:T(8,128)(2,1)} %get-tuple-element.66), channel_id=1, source_target_pairs={{8,0},{16,8},{24,16},{9,1},{17,9},{25,17},{10,2},{18,10},{26,18},{... | collective-permute-start | bytes 221192 | tf_op jit(solution)/shard_map/ppermute | solution.py:67
  64.1 7.4 %collective-permute-start.19 = (bf16[2,18,8,128]{3,2,1,0:T(8,128)(2,1)}, bf16[2,18,8,128]{3,2,1,0:T(8,128)(2,1)S(1)}, u32[]{:S(2)}, u32[]{:S(2)}) collective-permute-start(bf16[2,18,8,128]{3,2,1,0:T(8,128)(2,1)} %get-tuple-element.66), channel_id=1, source_target_pairs={{16,0},{24,8},{17,1},{25,9},{18,2},{26,10},{19,3},{27,11},{20,4},{... | collective-permute-start | bytes 221192 | tf_op jit(solution)/shard_map/ppermute | solution.py:67
  65.4 9.7 %copy-start.7 = (bf16[2,18,8,128]{3,2,1,0:T(8,128)(2,1)}, bf16[2,18,8,128]{3,2,1,0:T(8,128)(2,1)S(1)}, u32[]{:S(2)}) copy-start(bf16[2,18,8,128]{3,2,1,0:T(8,128)(2,1)S(1)} %collective-permute-done.15.refs_9_) | copy-start | bytes 221188
  65.4 9.7 %collective-permute-start.20 = (bf16[2,18,8,128]{3,2,1,0:T(8,128)(2,1)}, bf16[2,18,8,128]{3,2,1,0:T(8,128)(2,1)S(1)}, u32[]{:S(2)}, u32[]{:S(2)}) collective-permute-start(bf16[2,18,8,128]{3,2,1,0:T(8,128)(2,1)} %get-tuple-element.66), channel_id=1, source_target_pairs={{24,0},{25,1},{26,2},{27,3},{28,4},{29,5},{30,6},{31,7}} | collective-permute-start | bytes 221192 | tf_op jit(solution)/shard_map/ppermute | solution.py:67
  66.7 8.4 %copy-start.8 = (bf16[2,18,8,128]{3,2,1,0:T(8,128)(2,1)}, bf16[2,18,8,128]{3,2,1,0:T(8,128)(2,1)S(1)}, u32[]{:S(2)}) copy-start(bf16[2,18,8,128]{3,2,1,0:T(8,128)(2,1)S(1)} %collective-permute-done.16.refs_10_) | copy-start | bytes 221188
  68.9 6.2 %copy-start.9 = (bf16[2,18,8,128]{3,2,1,0:T(8,128)(2,1)}, bf16[2,18,8,128]{3,2,1,0:T(8,128)(2,1)S(1)}, u32[]{:S(2)}) copy-start(bf16[2,18,8,128]{3,2,1,0:T(8,128)(2,1)S(1)} %collective-permute-done.17.refs_11_) | copy-start | bytes 221188
  69.5 5.6 %copy-start.10 = (bf16[2,18,8,128]{3,2,1,0:T(8,128)(2,1)}, bf16[2,18,8,128]{3,2,1,0:T(8,128)(2,1)S(1)}, u32[]{:S(2)}) copy-start(bf16[2,18,8,128]{3,2,1,0:T(8,128)(2,1)S(1)} %collective-permute-done.18.refs_12_) | copy-start | bytes 221188
  102.7 6.1 %copy-start.39 = (bf16[68,128]{1,0:T(8,128)(2,1)S(1)}, bf16[68,128]{1,0:T(8,128)(2,1)}, u32[]{:S(2)}) copy-start(bf16[68,128]{1,0:T(8,128)(2,1)} %get-tuple-element.68) | copy-start | bytes 52228
  102.8 9.0 %copy-start.35 = (bf16[68,128]{1,0:T(8,128)(2,1)S(1)}, bf16[68,128]{1,0:T(8,128)(2,1)}, u32[]{:S(2)}) copy-start(bf16[68,128]{1,0:T(8,128)(2,1)} %get-tuple-element.67) | copy-start | bytes 52228
  102.8 30.8 %copy-start = (bf16[32,2048]{1,0:T(8,128)(2,1)S(1)}, bf16[32,2048]{1,0:T(8,128)(2,1)}, u32[]{:S(2)}) copy-start(bf16[32,2048]{1,0:T(8,128)(2,1)} %get-tuple-element.80.refs_4_) | copy-start | bytes 393220
  103.4 4.4 %collective-permute-start.27 = (bf16[68,128]{1,0:T(8,128)(2,1)S(1)}, bf16[68,128]{1,0:T(8,128)(2,1)S(1)}, u32[]{:S(2)}, u32[]{:S(2)}) collective-permute-start(bf16[68,128]{1,0:T(8,128)(2,1)S(1)} %copy-done.45), channel_id=1, source_target_pairs={{0,7},{1,6},{2,5},{3,4},{4,3},{5,2},{6,1},{7,0},{8,15},{9,14},{10,... | collective-permute-start | bytes 52232 | tf_op jit(solution)/shard_map/ppermute | solution.py:56
  103.7 5.2 %collective-permute-start.26 = (bf16[68,128]{1,0:T(8,128)(2,1)S(1)}, bf16[68,128]{1,0:T(8,128)(2,1)S(1)}, u32[]{:S(2)}, u32[]{:S(2)}) collective-permute-start(bf16[68,128]{1,0:T(8,128)(2,1)S(1)} %copy-done.44), channel_id=1, source_target_pairs={{0,6},{1,7},{2,4},{3,5},{4,2},{5,3},{6,0},{7,1},{8,14},{9,15},{10,... | collective-permute-start | bytes 52232 | tf_op jit(solution)/shard_map/ppermute | solution.py:56
  105.3 4.3 %collective-permute-start.25 = (bf16[68,128]{1,0:T(8,128)(2,1)S(1)}, bf16[68,128]{1,0:T(8,128)(2,1)S(1)}, u32[]{:S(2)}, u32[]{:S(2)}) collective-permute-start(bf16[68,128]{1,0:T(8,128)(2,1)S(1)} %copy-done.43), channel_id=1, source_target_pairs={{0,5},{1,4},{2,7},{3,6},{4,1},{5,0},{6,3},{7,2},{8,13},{9,12},{10,... | collective-permute-start | bytes 52232 | tf_op jit(solution)/shard_map/ppermute | solution.py:56
  106.4 3.8 %collective-permute-start.24 = (bf16[68,128]{1,0:T(8,128)(2,1)S(1)}, bf16[68,128]{1,0:T(8,128)(2,1)S(1)}, u32[]{:S(2)}, u32[]{:S(2)}) collective-permute-start(bf16[68,128]{1,0:T(8,128)(2,1)S(1)} %copy-done.42), channel_id=1, source_target_pairs={{0,4},{1,5},{2,6},{3,7},{4,0},{5,1},{6,2},{7,3},{8,12},{9,13},{10,... | collective-permute-start | bytes 52232 | tf_op jit(solution)/shard_map/ppermute | solution.py:56
  107.8 3.2 %collective-permute-start.23 = (bf16[68,128]{1,0:T(8,128)(2,1)S(1)}, bf16[68,128]{1,0:T(8,128)(2,1)S(1)}, u32[]{:S(2)}, u32[]{:S(2)}) collective-permute-start(bf16[68,128]{1,0:T(8,128)(2,1)S(1)} %copy-done.41), channel_id=1, source_target_pairs={{0,3},{1,2},{2,1},{3,0},{4,7},{5,6},{6,5},{7,4},{8,11},{9,10},{10,... | collective-permute-start | bytes 52232 | tf_op jit(solution)/shard_map/ppermute | solution.py:56
  107.8 3.9 %collective-permute-start.22 = (bf16[68,128]{1,0:T(8,128)(2,1)S(1)}, bf16[68,128]{1,0:T(8,128)(2,1)S(1)}, u32[]{:S(2)}, u32[]{:S(2)}) collective-permute-start(bf16[68,128]{1,0:T(8,128)(2,1)S(1)} %copy-done.40), channel_id=1, source_target_pairs={{0,2},{1,3},{2,0},{3,1},{4,6},{5,7},{6,4},{7,5},{8,10},{9,11},{10,... | collective-permute-start | bytes 52232 | tf_op jit(solution)/shard_map/ppermute | solution.py:56
  108.9 2.9 %collective-permute-start.21 = (bf16[68,128]{1,0:T(8,128)(2,1)S(1)}, bf16[68,128]{1,0:T(8,128)(2,1)S(1)}, u32[]{:S(2)}, u32[]{:S(2)}) collective-permute-start(bf16[68,128]{1,0:T(8,128)(2,1)S(1)} %copy-done.39), channel_id=1, source_target_pairs={{0,1},{1,0},{2,3},{3,2},{4,5},{5,4},{6,7},{7,6},{8,9},{9,8},{10,11... | collective-permute-start | bytes 52232 | tf_op jit(solution)/shard_map/ppermute | solution.py:56
  111.8 9.0 %copy-start.6 = (bf16[68,128]{1,0:T(8,128)(2,1)}, bf16[68,128]{1,0:T(8,128)(2,1)S(1)}, u32[]{:S(2)}) copy-start(bf16[68,128]{1,0:T(8,128)(2,1)S(1)} %add_convert_fusion.1.refs_0_) | copy-start | bytes 52228
  111.8 3.7 %collective-permute-start.28 = (bf16[68,128]{1,0:T(8,128)(2,1)S(1)}, bf16[68,128]{1,0:T(8,128)(2,1)S(1)}, u32[]{:S(2)}, u32[]{:S(2)}) collective-permute-start(bf16[68,128]{1,0:T(8,128)(2,1)S(1)} %add_convert_fusion.1.refs_0_), channel_id=1, source_target_pairs={{0,1},{1,0},{2,3},{3,2},{4,5},{5,4},{6,7},{7,6},{8,9},{9,8},{10,11... | collective-permute-start | bytes 52232 | tf_op jit(solution)/shard_map/ppermute | solution.py:56
  112.0 4.7 %collective-permute-start.29 = (bf16[68,128]{1,0:T(8,128)(2,1)S(1)}, bf16[68,128]{1,0:T(8,128)(2,1)S(1)}, u32[]{:S(2)}, u32[]{:S(2)}) collective-permute-start(bf16[68,128]{1,0:T(8,128)(2,1)S(1)} %add_convert_fusion.1.refs_0_), channel_id=1, source_target_pairs={{0,2},{1,3},{2,0},{3,1},{4,6},{5,7},{6,4},{7,5},{8,10},{9,11},{10,... | collective-permute-start | bytes 52232 | tf_op jit(solution)/shard_map/ppermute | solution.py:56
  113.1 5.0 %collective-permute-start.30 = (bf16[68,128]{1,0:T(8,128)(2,1)S(1)}, bf16[68,128]{1,0:T(8,128)(2,1)S(1)}, u32[]{:S(2)}, u32[]{:S(2)}) collective-permute-start(bf16[68,128]{1,0:T(8,128)(2,1)S(1)} %add_convert_fusion.1.refs_0_), channel_id=1, source_target_pairs={{0,3},{1,2},{2,1},{3,0},{4,7},{5,6},{6,5},{7,4},{8,11},{9,10},{10,... | collective-permute-start | bytes 52232 | tf_op jit(solution)/shard_map/ppermute | solution.py:56
  113.8 4.4 %collective-permute-start.31 = (bf16[68,128]{1,0:T(8,128)(2,1)S(1)}, bf16[68,128]{1,0:T(8,128)(2,1)S(1)}, u32[]{:S(2)}, u32[]{:S(2)}) collective-permute-start(bf16[68,128]{1,0:T(8,128)(2,1)S(1)} %add_convert_fusion.1.refs_0_), channel_id=1, source_target_pairs={{0,4},{1,5},{2,6},{3,7},{4,0},{5,1},{6,2},{7,3},{8,12},{9,13},{10,... | collective-permute-start | bytes 52232 | tf_op jit(solution)/shard_map/ppermute | solution.py:56
  114.5 3.7 %collective-permute-start.32 = (bf16[68,128]{1,0:T(8,128)(2,1)S(1)}, bf16[68,128]{1,0:T(8,128)(2,1)S(1)}, u32[]{:S(2)}, u32[]{:S(2)}) collective-permute-start(bf16[68,128]{1,0:T(8,128)(2,1)S(1)} %add_convert_fusion.1.refs_0_), channel_id=1, source_target_pairs={{0,5},{1,4},{2,7},{3,6},{4,1},{5,0},{6,3},{7,2},{8,13},{9,12},{10,... | collective-permute-start | bytes 52232 | tf_op jit(solution)/shard_map/ppermute | solution.py:56
  115.5 5.3 %copy-start.28 = (bf16[68,128]{1,0:T(8,128)(2,1)}, bf16[68,128]{1,0:T(8,128)(2,1)S(1)}, u32[]{:S(2)}) copy-start(bf16[68,128]{1,0:T(8,128)(2,1)S(1)} %collective-permute-done.28.refs_1_) | copy-start | bytes 52228
  115.5 4.7 %collective-permute-start.33 = (bf16[68,128]{1,0:T(8,128)(2,1)S(1)}, bf16[68,128]{1,0:T(8,128)(2,1)S(1)}, u32[]{:S(2)}, u32[]{:S(2)}) collective-permute-start(bf16[68,128]{1,0:T(8,128)(2,1)S(1)} %add_convert_fusion.1.refs_0_), channel_id=1, source_target_pairs={{0,6},{1,7},{2,4},{3,5},{4,2},{5,3},{6,0},{7,1},{8,14},{9,15},{10,... | collective-permute-start | bytes 52232 | tf_op jit(solution)/shard_map/ppermute | solution.py:56
  116.7 4.1 %collective-permute-start.34 = (bf16[68,128]{1,0:T(8,128)(2,1)S(1)}, bf16[68,128]{1,0:T(8,128)(2,1)S(1)}, u32[]{:S(2)}, u32[]{:S(2)}) collective-permute-start(bf16[68,128]{1,0:T(8,128)(2,1)S(1)} %add_convert_fusion.1.refs_0_), channel_id=1, source_target_pairs={{0,7},{1,6},{2,5},{3,4},{4,3},{5,2},{6,1},{7,0},{8,15},{9,14},{10,... | collective-permute-start | bytes 52232 | tf_op jit(solution)/shard_map/ppermute | solution.py:56
  123.0 36.5 %copy-start.38 = (bf16[136,128]{1,0:T(8,128)(2,1)S(1)}, bf16[136,128]{1,0:T(8,128)(2,1)}, u32[]{:S(2)}) copy-start(bf16[136,128]{1,0:T(8,128)(2,1)} %get-tuple-element.85) | copy-start | bytes 104452
  123.0 36.6 %copy-start.37 = (bf16[136,128]{1,0:T(8,128)(2,1)S(1)}, bf16[136,128]{1,0:T(8,128)(2,1)}, u32[]{:S(2)}) copy-start(bf16[136,128]{1,0:T(8,128)(2,1)} %get-tuple-element.86) | copy-start | bytes 104452
  123.0 38.5 %copy-start.36 = (bf16[136,128]{1,0:T(8,128)(2,1)S(1)}, bf16[136,128]{1,0:T(8,128)(2,1)}, u32[]{:S(2)}) copy-start(bf16[136,128]{1,0:T(8,128)(2,1)} %get-tuple-element.87) | copy-start | bytes 104452
  129.6 15.6 %collective-permute-start.35 = (f32[8,2048]{1,0:T(8,128)}, f32[8,2048]{1,0:T(8,128)S(1)}, u32[]{:S(2)}, u32[]{:S(2)}) collective-permute-start(f32[8,2048]{1,0:T(8,128)} %get-tuple-element.79), channel_id=1, source_target_pairs={{8,0},{16,8},{24,16},{9,1},{17,9},{25,17},{10,2},{18,10},{26,18},{... | collective-permute-start | bytes 196616 | tf_op jit(solution)/shard_map/ppermute | solution.py:67
  130.9 14.3 %collective-permute-start.39 = (f32[8,2048]{1,0:T(8,128)}, f32[8,2048]{1,0:T(8,128)S(1)}, u32[]{:S(2)}, u32[]{:S(2)}) collective-permute-start(f32[8,2048]{1,0:T(8,128)} %get-tuple-element.81.refs_8_), channel_id=1, source_target_pairs={{0,8},{8,16},{16,24},{24,0},{1,9},{9,17},{17,25},{25,1},{2,10},{10... | collective-permute-start | bytes 196616 | tf_op jit(solution)/shard_map/ppermute | solution.py:61
  133.6 27.9 %collective-permute-start.36 = (bf16[32,2048]{1,0:T(8,128)(2,1)S(1)}, bf16[32,2048]{1,0:T(8,128)(2,1)S(1)}, u32[]{:S(2)}, u32[]{:S(2)}) collective-permute-start(bf16[32,2048]{1,0:T(8,128)(2,1)S(1)} %copy-done), channel_id=1, source_target_pairs={{0,8},{8,16},{16,24},{24,0},{1,9},{9,17},{17,25},{25,1},{2,10},{10... | collective-permute-start | bytes 393224 | tf_op jit(solution)/shard_map/ppermute | solution.py:61
  133.7 30.1 %collective-permute-start.37 = (bf16[32,2048]{1,0:T(8,128)(2,1)S(1)}, bf16[32,2048]{1,0:T(8,128)(2,1)S(1)}, u32[]{:S(2)}, u32[]{:S(2)}) collective-permute-start(bf16[32,2048]{1,0:T(8,128)(2,1)S(1)} %copy-done), channel_id=1, source_target_pairs={{0,16},{8,24},{16,0},{24,8},{1,17},{9,25},{17,1},{25,9},{2,18},{10... | collective-permute-start | bytes 393224 | tf_op jit(solution)/shard_map/ppermute | solution.py:61
  135.4 28.5 %collective-permute-start.38 = (bf16[32,2048]{1,0:T(8,128)(2,1)S(1)}, bf16[32,2048]{1,0:T(8,128)(2,1)S(1)}, u32[]{:S(2)}, u32[]{:S(2)}) collective-permute-start(bf16[32,2048]{1,0:T(8,128)(2,1)S(1)} %copy-done), channel_id=1, source_target_pairs={{0,24},{8,0},{16,8},{24,16},{1,25},{9,1},{17,9},{25,17},{2,26},{10... | collective-permute-start | bytes 393224 | tf_op jit(solution)/shard_map/ppermute | solution.py:61
  145.2 18.7 %copy-start.14 = (f32[8,2048]{1,0:T(8,128)}, f32[8,2048]{1,0:T(8,128)S(1)}, u32[]{:S(2)}) copy-start(f32[8,2048]{1,0:T(8,128)S(1)} %collective-permute-done.35.refs_2_) | copy-start | bytes 196612
  145.2 14.3 %collective-permute-start.40 = (f32[8,2048]{1,0:T(8,128)}, f32[8,2048]{1,0:T(8,128)S(1)}, u32[]{:S(2)}, u32[]{:S(2)}) collective-permute-start(f32[8,2048]{1,0:T(8,128)} %get-tuple-element.81.refs_8_), channel_id=1, source_target_pairs={{0,16},{8,24},{16,0},{24,8},{1,17},{9,25},{17,1},{25,9},{2,18},{10... | collective-permute-start | bytes 196616 | tf_op jit(solution)/shard_map/ppermute | solution.py:61
  145.2 18.7 %copy-start.15 = (f32[8,2048]{1,0:T(8,128)}, f32[8,2048]{1,0:T(8,128)S(1)}, u32[]{:S(2)}) copy-start(f32[8,2048]{1,0:T(8,128)S(1)} %collective-permute-done.39.refs_9_) | copy-start | bytes 196612
  145.2 14.3 %collective-permute-start.41 = (f32[8,2048]{1,0:T(8,128)}, f32[8,2048]{1,0:T(8,128)S(1)}, u32[]{:S(2)}, u32[]{:S(2)}) collective-permute-start(f32[8,2048]{1,0:T(8,128)} %get-tuple-element.81.refs_8_), channel_id=1, source_target_pairs={{0,24},{8,0},{16,8},{24,16},{1,25},{9,1},{17,9},{25,17},{2,26},{10... | collective-permute-start | bytes 196616 | tf_op jit(solution)/shard_map/ppermute | solution.py:61
  159.5 7.0 %collective-permute-start.42 = (bf16[136,128]{1,0:T(8,128)(2,1)S(1)}, bf16[136,128]{1,0:T(8,128)(2,1)S(1)}, u32[]{:S(2)}, u32[]{:S(2)}) collective-permute-start(bf16[136,128]{1,0:T(8,128)(2,1)S(1)} %copy-done.38), channel_id=1, source_target_pairs={{0,8},{8,16},{16,24},{24,0},{1,9},{9,17},{17,25},{25,1},{2,10},{10... | collective-permute-start | bytes 104456 | tf_op jit(solution)/shard_map/ppermute | solution.py:61
  159.6 7.0 %collective-permute-start.43 = (bf16[136,128]{1,0:T(8,128)(2,1)S(1)}, bf16[136,128]{1,0:T(8,128)(2,1)S(1)}, u32[]{:S(2)}, u32[]{:S(2)}) collective-permute-start(bf16[136,128]{1,0:T(8,128)(2,1)S(1)} %copy-done.37), channel_id=1, source_target_pairs={{0,16},{8,24},{16,0},{24,8},{1,17},{9,25},{17,1},{25,9},{2,18},{10... | collective-permute-start | bytes 104456 | tf_op jit(solution)/shard_map/ppermute | solution.py:61
  161.5 5.1 %collective-permute-start.44 = (bf16[136,128]{1,0:T(8,128)(2,1)S(1)}, bf16[136,128]{1,0:T(8,128)(2,1)S(1)}, u32[]{:S(2)}, u32[]{:S(2)}) collective-permute-start(bf16[136,128]{1,0:T(8,128)(2,1)S(1)} %copy-done.36), channel_id=1, source_target_pairs={{0,24},{8,0},{16,8},{24,16},{1,25},{9,1},{17,9},{25,17},{2,26},{10... | collective-permute-start | bytes 104456 | tf_op jit(solution)/shard_map/ppermute | solution.py:61
  (29 other events, 63.6 us)
Sparse Core Ops, SparseCore 0:
  20.0 49.1 all-gather.2
  102.9 50.1 reduce-scatter.1

commit v2 on v1

--- a/solution.py
+++ b/solution.py
@@ -47,15 +47,6 @@
     return 1.0 / (1.0 + jnp.exp(-v))
 
 
-def piece_start(peers, mask, size):
-    return 0 if peers == 1 else (lax.axis_index("chan") ^ mask) * size
-
-
-def swap(block, axis, mask):
-    count = lax.axis_size(axis)
-    return lax.ppermute(block, axis, [(i, i ^ mask) for i in range(count)])
-
-
 def rotate(block, axis, distance):
     count = lax.axis_size(axis)
     return lax.ppermute(block, axis, [(i, (i + distance) % count) for i in range(count)])
@@ -81,8 +72,7 @@
     return total
 
 
-def conv_kernel(peers, input_ref, rim_ref, weight_ref, bias_ref, proj_ref, out_ref, *rest):
-    pieces, (ext, acc) = rest[:peers], rest[peers:]
+def conv_kernel(input_ref, rim_ref, weight_ref, bias_ref, proj_ref, out_ref, part_ref, ext, acc):
     step = pl.program_id(0)
     taps = weight_ref.shape[0]
     rows = input_ref.shape[0]
@@ -102,19 +92,16 @@
 
     @pl.when(step == pl.num_programs(0) - 1)
     def _():
-        size = rows // peers
-        for mask in range(peers):
-            first = piece_start(peers, mask, size)
-            pieces[mask][...] = acc[pl.ds(first, size), :].astype(BF)
-
-
-def conv_call(peers, conv_input, rim, weight, bias, proj_weight):
+        part_ref[...] = acc[...].astype(BF)
+
+
+def conv_call(conv_input, rim, weight, bias, proj_weight):
     rows, chans = conv_input.shape
     taps = weight.shape[0]
     wide = proj_weight.shape[0]
     width = min(512, chans)
     return pl.pallas_call(
-        functools.partial(conv_kernel, peers),
+        conv_kernel,
         grid=(chans // width,),
         in_specs=[
             columns(rows, width),
@@ -123,8 +110,8 @@
             columns(1, width),
             columns(wide, width),
         ],
-        out_specs=[columns(rows, width)] + [whole((rows // peers, wide))] * peers,
-        out_shape=[sds((rows, chans), BF)] + [sds((rows // peers, wide), BF)] * peers,
+        out_specs=[columns(rows, width), whole((rows, wide))],
+        out_shape=[sds((rows, chans), BF), sds((rows, wide), BF)],
         scratch_shapes=[pltpu.VMEM((rows + 8, width), F32), pltpu.VMEM((rows, wide), F32)],
         compiler_params=params(),
         name="conv_project",
@@ -141,13 +128,11 @@
             ]
 
 
-def local_kernel(
-    peers, low_rank, states, *refs
-):
-    parts, refs = refs[:peers], refs[peers:]
+def local_kernel(low_rank, states, places, *refs):
+    part_ref, refs = refs[0], refs[1:]
     (weight_ref, bias_ref, decay_ref, conv_ref, gate_ref, grad_ref) = refs[:6]
-    (dt_ref, fwd_ref, bwd_ref, coef_ref, low) = refs[6:11]
-    (proj, coef_v, coef, dts, dxs, gs, fwd, bwd, sem) = refs[11:]
+    (dt_ref, ends_ref, coef_ref, low) = refs[6:10]
+    (proj, coef_v, coef, dts, dxs, gs, fwd, bwd, sem) = refs[10:]
     step = pl.program_id(0)
     chunks = dts.shape[0]
     rows = conv_ref.shape[0]
@@ -155,10 +140,8 @@
 
     @pl.when(step == 0)
     def _():
-        size = rows // peers
-        for mask in range(peers):
-            proj[pl.ds(piece_start(peers, mask, size), size), :] = parts[mask][...].astype(F32)
-        low[...] = proj[:, :low_rank].astype(BF)
+        proj[...] = part_ref[...].astype(F32)
+        low[...] = part_ref[:, :low_rank]
         coef_v[...] = jnp.zeros_like(coef_v)
         coef_v[:, : 2 * states] = proj[:, low_rank:]
         coef_ref[...] = coef_v[...]
@@ -226,24 +209,24 @@
                     for target in (fwd, bwd):
                         target[v, states] = coarse
                         target[v, states + 1] = total[v] - coarse
-        fwd_ref[...] = fwd[...].astype(BF)
-        bwd_ref[...] = bwd[...].astype(BF)
-
-
-def local_call(parts, step_weight, step_bias, decay, conv_out, gate, grad, states):
-    peers = len(parts)
+        place = lax.axis_index("ctx")
+        for other in range(places):
+            ends_ref[other] = jnp.where(other > place, fwd[...], bwd[...]).astype(BF)
+
+
+def local_call(part, step_weight, step_bias, decay, conv_out, gate, grad, states, places):
     rows, chans = conv_out.shape
-    wide = parts[0].shape[1]
+    wide = part.shape[1]
     low_rank = step_weight.shape[0]
     chunks, _, groups, _ = decay.shape
     width = groups * 128
     message = (chunks, states + 2, groups, 128)
     big = pltpu.VMEM((chunks, rows * groups, 128), F32)
     return pl.pallas_call(
-        functools.partial(local_kernel, peers, low_rank, states),
+        functools.partial(local_kernel, low_rank, states, places),
         grid=(chunks,),
-        in_specs=[whole((rows // peers, wide))] * peers
-        + [
+        in_specs=[
+            whole((rows, wide)),
             columns(low_rank, width),
             columns(1, width),
             whole(decay.shape),
@@ -253,15 +236,13 @@
         ],
         out_specs=[
             pl.BlockSpec((1, rows * groups, 128), lambda i: (i, 0, 0)),
-            whole(message),
-            whole(message),
+            whole((places,) + message),
             whole((rows, 128)),
             whole((rows, low_rank)),
         ],
         out_shape=[
             sds((chunks, rows * groups, 128), F32),
-            sds(message, BF),
-            sds(message, BF),
+            sds((places,) + message, BF),
             sds((rows, 128), F32),
             sds((rows, low_rank), BF),
         ],
@@ -278,7 +259,7 @@
         ],
         compiler_params=params(),
         name="local_ends",
-    )(*parts, step_weight, step_bias, decay, conv_out, gate, grad)
+    )(part, step_weight, step_bias, decay, conv_out, gate, grad)
 
 
 def fold_sublanes(values):
@@ -303,12 +284,11 @@
     return values[0]
 
 
-def scan_kernel(peers, hops, states, *refs):
+def scan_kernel(places, states, *refs):
     (coef, low_ref, dt_ref, decay_ref, conv_ref, gate_ref, grad_ref, weight_ref, skip_ref) = refs[:9]
-    befores, refs = refs[9 : 9 + hops], refs[9 + hops :]
-    afters, refs = refs[:hops], refs[hops:]
-    (pre_ref, gate_out, scan_out, small_ref, prod_ref) = refs[:5]
-    pieces, refs = refs[5 : 5 + peers], refs[5 + peers :]
+    ends, refs = refs[9], refs[10:]
+    (pre_ref, gate_out, scan_out, small_ref, prod_ref, part_ref) = refs[:6]
+    refs = refs[6:]
     (xs, dxs, gs, ys, dds, qs, decayed, coef_out, coef_in, rate, decay_acc, acc, small) = refs
     step = pl.program_id(0)
     rows = conv_ref.shape[0]
@@ -330,20 +310,24 @@
                 dxs[first : first + 8, :] = conv[subs, lanes] * dt_ref[0, first : first + 8, :]
                 gs[first : first + 8, :] = grad[subs, lanes]
 
+    place = lax.axis_index("ctx")
+    for n in range(states):
+        rate[n] = -LOG2E * jnp.exp(decay_ref[0, n])
+    totals = [
+        ends[q, 0, states].astype(F32) + ends[q, 0, states + 1].astype(F32) for q in range(places)
+    ]
     state, carry = [], []
     for n in range(states):
-        rate[n] = -LOG2E * jnp.exp(decay_ref[0, n])
-    for n in range(states):
-        now = jnp.zeros((groups, 128), F32)
-        for message in befores[::-1]:
-            total = message[0, states].astype(F32) + message[0, states + 1].astype(F32)
-            now = jnp.exp2(rate[n] * total) * now + message[0, n].astype(F32)
-        state.append(now)
-        now = jnp.zeros((groups, 128), F32)
-        for message in afters[::-1]:
-            total = message[0, states].astype(F32) + message[0, states + 1].astype(F32)
-            now = jnp.exp2(rate[n] * total) * now + message[0, n].astype(F32)
-        carry.append(now)
+        before = jnp.zeros((groups, 128), F32)
+        after = jnp.zeros((groups, 128), F32)
+        for q in range(places - 1):
+            reached = jnp.exp2(rate[n] * totals[q]) * before + ends[q, 0, n].astype(F32)
+            before = jnp.where(q < place, reached, before)
+        for q in range(places - 1, 0, -1):
+            reached = jnp.exp2(rate[n] * totals[q]) * after + ends[q, 0, n].astype(F32)
+            after = jnp.where(q > place, reached, after)
+        state.append(before)
+        carry.append(after)
 
     def forward(index, state):
         state = list(state)
@@ -459,37 +443,38 @@
             coefs = coefs + dot(pick, source[at, :].astype(BF), NT)
     wide = dot(weight_ref[...], pre_bf, NT)
 
+    ranks, coef_rows, block = low_rank // places, 2 * states // places, acc.shape[0] // places
+
     @pl.when(step == 0)
     def _():
-        acc[:low_rank, :] = wide
-        acc[low_rank:, :] = coefs
-
-    @pl.when(step > 0)
-    def _():
-        acc[:low_rank, :] += wide
-        acc[low_rank:, :] += coefs
+        acc[...] = jnp.zeros_like(acc)
+
+    for q in range(places):
+        first = q * block
+        acc[first : first + ranks, :] += wide[q * ranks : (q + 1) * ranks, :]
+        acc[first + ranks : first + ranks + coef_rows, :] += coefs[
+            q * coef_rows : (q + 1) * coef_rows, :
+        ]
 
     @pl.when(step == pl.num_programs(0) - 1)
     def _():
-        size = acc.shape[0] // peers
-        for mask in range(peers):
-            first = piece_start(peers, mask, size)
-            pieces[mask][...] = acc[pl.ds(first, size), :].astype(BF)
-
-
-def scan_call(
-    peers, coef, low, dt, decay, conv_out, gate, grad, step_weight, skip, befores, afters
-):
+        part_ref[...] = acc[...].astype(BF)
+
+
+def padded(wide):
+    return (wide + 127) // 128 * 128
+
+
+def scan_call(places, coef, low, dt, decay, conv_out, gate, grad, step_weight, skip, ends):
     rows, chans = conv_out.shape
     low_rank = step_weight.shape[0]
     chunks, states, groups, _ = decay.shape
     width = groups * 128
-    hops = len(befores)
-    wide = low_rank + 2 * states
+    wide = padded(low_rank + 2 * states)
     lead = lambda *shape: pl.BlockSpec((1,) + shape, lambda i: (i,) + (0,) * len(shape))
     tall = pltpu.VMEM((rows * groups, 128), F32)
     return pl.pallas_call(
-        functools.partial(scan_kernel, peers, hops, states),
+        functools.partial(scan_kernel, places, states),
         grid=(chunks,),
         in_specs=[
             pl.BlockSpec(memory_space=pltpu.SMEM),
@@ -501,24 +486,24 @@
             columns(rows, width),
             columns(low_rank, width),
             columns(1, width),
-        ]
-        + [lead(states + 2, groups, 128)] * (2 * hops),
+            pl.BlockSpec((places, 1, states + 2, groups, 128), lambda i: (0, i, 0, 0, 0)),
+        ],
         out_specs=[
             columns(rows, width),
             columns(rows, width),
             columns(rows, width),
             columns(32, width),
             columns(low_rank, width),
-        ]
-        + [whole((wide // peers, rows))] * peers,
+            whole((wide, rows)),
+        ],
         out_shape=[
             sds((rows, chans), BF),
             sds((rows, chans), BF),
             sds((rows, chans), BF),
             sds((32, chans), BF),
             sds((low_rank, chans), BF),
-        ]
-        + [sds((wide // peers, rows), BF)] * peers,
+            sds((wide, rows), BF),
+        ],
         scratch_shapes=[
             tall,
             tall,
@@ -536,49 +521,21 @@
         ],
         compiler_params=params(),
         name="scan_gradients",
-    )(coef, low, dt, decay, conv_out, gate, grad, step_weight, skip, *befores, *afters)
-
-
-def gather_kernel(peers, places, low_rank, *refs):
-    parts, refs = refs[:peers], refs[peers:]
-    whole_ref, cuts, full = refs[0], refs[1 : 1 + places], refs[1 + places]
-    place = lax.axis_index("ctx")
-    size = full.shape[0] // peers
-    for mask in range(peers):
-        full[pl.ds(piece_start(peers, mask, size), size), :] = parts[mask][...].astype(F32)
-    whole_ref[...] = full[...].astype(BF)
-    rank_rows = low_rank // places
-    coef_rows = (full.shape[0] - low_rank) // places
-    for hop in range(places):
-        target = lax.rem(place + hop, places)
-        cuts[hop][...] = jnp.concatenate(
-            [
-                full[pl.ds(target * rank_rows, rank_rows), :],
-                full[pl.ds(low_rank + target * coef_rows, coef_rows), :],
-            ],
-            axis=0,
-        ).astype(BF)
-
-
-def gather_call(parts, places, low_rank):
-    size, rows = parts[0].shape
-    peers = len(parts)
-    cut = (size * peers // places, rows)
-    return pl.pallas_call(
-        functools.partial(gather_kernel, peers, places, low_rank),
-        out_shape=[sds((size * peers, rows), BF)] + [sds(cut, BF)] * places,
-        scratch_shapes=[pltpu.VMEM((size * peers, rows), F32)],
-        compiler_params=params(),
-        name="gather_back",
-    )(*parts)
-
-
-def conv_grad_kernel(back_ref, proj_ref, scan_ref, input_ref, rim_ref, weight_ref, bias_ref,
+    )(coef, low, dt, decay, conv_out, gate, grad, step_weight, skip, ends)
+
+
+def conv_grad_kernel(places, low_rank, back_ref, proj_ref, scan_ref, input_ref, rim_ref, weight_ref, bias_ref,
                      out_ref, tail_ref, head_ref, small_ref, ext, grad):
     taps = weight_ref.shape[0]
     rows = input_ref.shape[0]
     fill_extended(ext, rim_ref, input_ref, taps)
-    d_xc = dot(back_ref[...], proj_ref[...], TN)
+    wide = proj_ref.shape[0]
+    block = back_ref.shape[0] // places
+    ranks, coef_rows = low_rank // places, (wide - low_rank) // places
+    back = back_ref[...].astype(F32)
+    order = [back[q * block : q * block + ranks, :] for q in range(places)]
+    order += [back[q * block + ranks : q * block + ranks + coef_rows, :] for q in range(places)]
+    d_xc = dot(jnp.concatenate(order, axis=0).astype(BF), proj_ref[...], TN)
     sums = [jnp.zeros((1, input_ref.shape[1]), F32) for _ in range(taps + 1)]
     for start in range(0, rows, 16):
         here = slice(start, start + 16)
@@ -604,16 +561,16 @@
     )
 
 
-def conv_grad_call(back, proj_weight, scan_part, conv_input, rim, weight, bias):
+def conv_grad_call(places, low_rank, back, proj_weight, scan_part, conv_input, rim, weight, bias):
     rows, chans = conv_input.shape
     taps = weight.shape[0]
     wide = proj_weight.shape[0]
     width = min(512, chans)
     return pl.pallas_call(
-        conv_grad_kernel,
+        functools.partial(conv_grad_kernel, places, low_rank),
         grid=(chans // width,),
         in_specs=[
-            whole((wide, rows)),
+            whole(back.shape),
             columns(wide, width),
             columns(rows, width),
             columns(rows, width),
@@ -634,32 +591,39 @@
     )(back, proj_weight, scan_part, conv_input, rim, weight, bias)
 
 
-def rows_kernel(places, rank_rows, *refs):
-    cuts, conv_ref, out_ref, coef_ref = refs[:places], refs[places], refs[places + 1], refs[places + 2]
-    place = lax.axis_index("ctx")
+def rows_kernel(rank_rows, cut_ref, conv_ref, step_ref, out_ref, coef_ref, step_out):
+    places = conv_ref.shape[0]
+    block = cut_ref.shape[0] // places
     total = None
-    for hop in range(places):
-        source = lax.rem(place + places - hop, places)
-        part = dot(cuts[hop][...], conv_ref[source])
+    for q in range(places):
+        part = dot(cut_ref[q * block : (q + 1) * block, :], conv_ref[q])
         total = part if total is None else total + part
     out_ref[...] = total[:rank_rows, :]
-    coef_ref[...] = total[rank_rows:, :]
-
-
-def rows_call(cuts, conv_all, rank_rows):
+    coef_ref[...] = total[rank_rows : rank_rows + coef_ref.shape[0], :]
+    step_out[...] = step_ref[...].astype(F32)
+
+
+def rows_call(cuts, conv_all, steps, coef_rows):
     places, rows, chans = conv_all.shape
-    cut = cuts[0].shape
+    rank_rows = steps.shape[0]
     width = min(512, chans)
     return pl.pallas_call(
-        functools.partial(rows_kernel, places, rank_rows),
+        functools.partial(rows_kernel, rank_rows),
         grid=(chans // width,),
-        in_specs=[whole(cut)] * places
-        + [pl.BlockSpec((places, rows, width), lambda i: (0, 0, i))],
-        out_specs=[columns(rank_rows, width), columns(cut[0] - rank_rows, width)],
-        out_shape=[sds((rank_rows, chans), F32), sds((cut[0] - rank_rows, chans), F32)],
+        in_specs=[
+            whole(cuts.shape),
+            pl.BlockSpec((places, rows, width), lambda i: (0, 0, i)),
+            columns(rank_rows, width),
+        ],
+        out_specs=[
+            columns(rank_rows, width), columns(coef_rows, width), columns(rank_rows, width)
+        ],
+        out_shape=[
+            sds((rank_rows, chans), F32), sds((coef_rows, chans), F32), sds((rank_rows, chans), F32)
+        ],
         compiler_params=params(),
         name="row_gradients",
-    )(*cuts, conv_all)
+    )(cuts, conv_all, steps)
 
 
 def last_kernel(places, states, taps, *refs):
@@ -722,14 +686,15 @@
     )(main, tail, following, weight, *early, *late)
 
 
-def chan_sum(pieces):
-    if len(pieces) == 1:
-        return [lax.psum(pieces[0], "chan")]
-    total = pieces[0].astype(F32)
-    for mask in range(1, len(pieces)):
-        total = total + swap(pieces[mask], "chan", mask).astype(F32)
-    total = total.astype(BF)
-    return [total] + [swap(total, "chan", mask) for mask in range(1, len(pieces))]
+def exchange(block, axis):
+    return lax.all_to_all(block, axis, split_axis=0, concat_axis=0, tiled=True)
+
+
+def chan_sum(part):
+    peers = lax.axis_size("chan")
+    pieces = exchange(part, "chan").reshape((peers, part.shape[0] // peers, part.shape[1]))
+    total = jnp.sum(pieces.astype(F32), axis=0, keepdims=True).astype(BF)
+    return exchange(jnp.broadcast_to(total, pieces.shape).reshape(part.shape), "chan")
 
 
 def body(
@@ -748,9 +713,6 @@
     taps = conv_weight.shape[0]
     low_rank = step_weight.shape[0]
     states = decay_log.shape[0]
-    peers = lax.axis_size("chan")
-    if rows % (16 * peers) or peers & (peers - 1):
-        peers = 1
     places = lax.axis_size("ctx")
     groups = group_rows(chans)
     decay = decay_log.reshape(states, -1, groups, 128).transpose(1, 0, 2, 3)
@@ -759,28 +721,25 @@
     skip_gain = skip_gain[None, :]
 
     rim = shift(conv_input[rows - (taps - 1) :], "ctx", 1)
-    conv_out, *pieces = conv_call(peers, conv_input, rim, conv_weight, conv_bias, proj_weight)
+    conv_out, part = conv_call(conv_input, rim, conv_weight, conv_bias, proj_weight)
     conv_all = lax.all_gather(conv_out, "ctx")
-    parts = chan_sum(pieces)
-    dt, fwd, bwd, coef, low = local_call(
-        parts, step_weight, step_bias, decay, conv_out, gate_input, out_grad, states
+    dt, ends, coef, low = local_call(
+        chan_sum(part), step_weight, step_bias, decay, conv_out, gate_input, out_grad, states, places
     )
-    befores = [shift(fwd, "ctx", hop) for hop in range(1, places)]
-    afters = [shift(bwd, "ctx", -hop) for hop in range(1, places)]
-    pre_bf, grad_gate, scan_part, small, products, *pieces = scan_call(
-        peers, coef, low, dt, decay, conv_out, gate_input, out_grad, step_weight, skip_gain,
-        befores, afters,
+    ends = exchange(ends, "ctx")
+    pre_bf, grad_gate, scan_part, small, products, part = scan_call(
+        places, coef, low, dt, decay, conv_out, gate_input, out_grad, step_weight, skip_gain, ends
     )
-    grad_step = lax.psum_scatter(products, "ctx", scatter_dimension=0, tiled=True).astype(F32)
+    steps = lax.psum_scatter(products, "ctx", scatter_dimension=0, tiled=True)
     early = [small] + [rotate(small, "ctx", hop) for hop in range(1, places)]
-    back, *cuts = gather_call(chan_sum(pieces), places, low_rank)
-    cuts = [cuts[0]] + [rotate(cuts[hop], "ctx", hop) for hop in range(1, places)]
+    back = chan_sum(part)
+    cuts = exchange(back, "ctx")
     main, tail, head, sums = conv_grad_call(
-        back, proj_weight, scan_part, conv_input, rim, conv_weight, conv_bias
+        places, low_rank, back, proj_weight, scan_part, conv_input, rim, conv_weight, conv_bias
     )
     following = shift(head, "ctx", -1)
     late = [sums] + [rotate(sums, "ctx", hop) for hop in range(1, places)]
-    grad_proj, grad_coef = rows_call(cuts, conv_all, low_rank // places)
+    grad_proj, grad_coef, grad_step = rows_call(cuts, conv_all, steps, 2 * states // places)
     grad_input, conv_w, conv_b, step_b, decay_grad, skip = last_call(
         main, tail, following, conv_weight, early, late, states
     )

time: 181 us -> 178 us (0.983)
  blocking collectives: 0 us -> 48.5 us
  waiting for transfers between devices: 41.7 us -> 9.21 us
  starting transfers between devices: 56.3 us -> 41.6 us
  other arithmetic: 2.9 us -> 0.06 us
    all_to_all x0 -> x4, blocking collectives: none -> 48.5 us  [exchange(): return lax.all_to_all(block, axis, split_axis=0, concat_axis=0, tiled=True)]
    ppermute x28 -> x0, starting transfers between devices: 25.3 us -> none  [swap(): return lax.ppermute(block, axis, [(i, i ^ mask) for i in range(count)])]
    ppermute x9 -> x6, starting transfers between devices: 10.9 us -> 28.6 us  [rotate(): lax.ppermute(block, axis, [(i, (i + distance) % count) for i in range(cou...]
    ppermute x8 -> x2, waiting for transfers between devices: 17.5 us -> 1.43 us  [shift(): return lax.ppermute(block, axis, route)]
    ppermute x8 -> x2, starting transfers between devices: 20.1 us -> 6.22 us  [shift(): return lax.ppermute(block, axis, route)]
    ppermute x9 -> x6, waiting for transfers between devices: 14.3 us -> 2.65 us  [rotate(): lax.ppermute(block, axis, [(i, (i + distance) % count) for i in range(cou...]
    ppermute x28 -> x0, waiting for transfers between devices: 9.87 us -> none  [swap(): return lax.ppermute(block, axis, [(i, i ^ mask) for i in range(count)])]
    all_to_all x0 -> x2, starting transfers between devices: none -> 6.73 us  [exchange(): return lax.all_to_all(block, axis, split_axis=0, concat_axis=0, tiled=True)]
  transfers between devices with their start and end apart: 47 -> 12, of which waited for: 16 -> 4; matrix products, arithmetic and copies ran while one was open for 1% -> 1% of each run, Pallas kernels for 30% -> 27%
where the time goes in v2:
time: 178 us; the launch traced here: 177 us
  Pallas kernels  57.7 us (32%)
  blocking collectives  48.5 us (27%)
  starting transfers between devices  41.6 us (23%)
  between operations  14.3 us (8%)
  waiting for transfers between devices  9.21 us (5%)
  local copies, waits for them, and re-layouts  5.58 us (3%)
    all_to_all x4, blocking collectives, exchange(): return lax.all_to_all(block, axis, split_axis=0, concat_axis=0, tiled=True)  48.5 us
    ppermute x6, starting transfers between devices, rotate(): lax.ppermute(block, axis, [(i, (i + distance) % count) for i in range(cou...  28.6 us
    pallas_call x1, Pallas kernels, scan_call(): pl.pallas_call(functools.partial(scan_kernel, places, states), grid=(chun...  27 us
    pallas_call x1, Pallas kernels, local_call(): pl.pallas_call(functools.partial(local_kernel, low_rank, states, places),...  12.8 us
    all_to_all x2, starting transfers between devices, exchange(): return lax.all_to_all(block, axis, split_axis=0, concat_axis=0, tiled=True)  6.73 us
    pallas_call x1, Pallas kernels, conv_grad_call(): pl.pallas_call(functools.partial(conv_grad_kernel, places, low_rank), gri...  6.64 us
    ppermute x2, starting transfers between devices, shift(): return lax.ppermute(block, axis, route)  6.22 us
    all_to_all x2, waiting for transfers between devices, exchange(): return lax.all_to_all(block, axis, split_axis=0, concat_axis=0, tiled=True)  5.06 us
  transfers between devices with their start and end apart: 12, of which 4 were waited for; matrix products, arithmetic and copies ran while one was open for 1% of the time, Pallas kernels for 27%

profile of v2, /device:TPU:0, one launch (start us, length us, event | category | flops | bytes accessed | tf_op | source)
XLA Modules:
  0.0 177.0 jit_solution(14595103833600416124)
XLA Ops:
  7.2 0.0 all-gather.3.cloned.1.call-start
  7.2 0.8 slice.3
  8.0 4.9 %collective-permute-start = (bf16[3,2048]{1,0:T(4,128)(2,1)S(1)}, bf16[3,2048]{1,0:T(4,128)(2,1)S(1)}, u32[]{:S(2)}, u32[]{:S(2)}) collective-permute-start(bf16[3,2048]{1,0:T(4,128)(2,1)S(1)} %slice.3), channel_id=1, source_target_pairs={{0,8},{8,16},{16,24},{1,9},{9,17},{17,25},{2,10},{10,18},{18,26},{... | collective-permute-start | bytes 36872 | tf_op jit(solution)/shard_map/ppermute | solution.py:58
  12.9 1.4 collective-permute-done.rim_ref
  14.4 0.0 copy-start.8
  14.4 0.6 copy-done.8
  15.0 0.0 copy-start.7
  15.0 4.9 %conv_project.1 = (bf16[128,2048]{1,0:T(8,128)(2,1)}, bf16[128,544]{1,0:T(8,128)(2,1)}) custom-call(bf16[128,2048]{1,0:T(8,128)(2,1)} %input_ref.3, bf16[3,2048]{1,0:T(4,128)(2,1)} %copy-done.8, f32[4,2048]{1,0:T(4,128)} %refs_3_.1, f32[1,2048]{1,0:T(1,128)} %bitcast.28, bf16[544,2048]{1,0:T(8,128)(2,1)} %proj_ref.3), custom_call_target="tpu_custom_call" | custom-call | tf_op jit(solution)/shard_map/conv_project/pallas_call | solution.py:103
  19.8 0.0 all-gather.3.cloned.1.call-update
  19.9 9.6 %all_to_all.50 = bf16[8,16,544]{2,1,0:T(8,128)(2,1)S(1)} all-to-all(bf16[8,16,544]{2,1,0:T(8,128)(2,1)} %bitcast.26), channel_id=1, replica_groups=mesh['ctx'=4,'chan'=8] {'chan'}, dimensions={0} | all-to-all | bytes 278528 | tf_op jit(solution)/shard_map/all_to_all | solution.py:690
  29.5 0.7 broadcast_in_dim.22
  30.2 3.4 %all-to-all-start.1 = ((bf16[8,16,544]{2,1,0:T(8,128)(2,1)}), bf16[8,16,544]{2,1,0:T(8,128)(2,1)S(1)}, u32[]{:S(2)}, u32[]{:S(2)}) async-start(bf16[8,16,544]{2,1,0:T(8,128)(2,1)} %broadcast_in_dim.22), calls=%async_computation.1 | async-start | bytes 327680 | tf_op jit(solution)/shard_map/all_to_all | solution.py:690
  33.6 0.0 reduce-scatter.2.cloned.1.call-start
  33.7 0.0 copy-done.7
  33.7 0.7 copy.24
  34.4 5.1 %all-to-all-done.1 = bf16[8,16,544]{2,1,0:T(8,128)(2,1)S(1)} async-done(((bf16[8,16,544]{2,1,0:T(8,128)(2,1)}), bf16[8,16,544]{2,1,0:T(8,128)(2,1)S(1)}, u32[]{:S(2)}, u32[]{:S(2)}) %all-to-all-start.1) | async-done | bytes 139296 | tf_op jit(solution)/shard_map/all_to_all | solution.py:690
  39.4 0.0 copy-start
  39.4 0.7 copy-done
  40.1 12.8 %local_ends.1 = (f32[2,1024,128]{2,1,0:T(8,128)}, bf16[4,2,18,8,128]{4,3,2,1,0:T(8,128)(2,1)}, f32[128,128]{1,0:T(8,128)}, bf16[128,512]{1,0:T(8,128)(2,1)}) custom-call(bf16[128,544]{1,0:T(8,128)(2,1)} %bitcast.22, bf16[512,2048]{1,0:T(8,128)(2,1)} %refs_7_.1, f32[1,2048]{1,0:T(1,128)} %bitcast.30, f32[2,16,8,128]{3,2,1,0:T(8,128)} %bitcast.20, ...), custom_call_target="tpu_custom_call" | custom-call | tf_op jit(solution)/shard_map/local_ends/pallas_call | solution.py:225
  52.9 21.1 %all_to_all.51.refs_9_ = bf16[4,2,18,8,128]{4,3,2,1,0:T(8,128)(2,1)} all-to-all(bf16[4,2,18,8,128]{4,3,2,1,0:T(8,128)(2,1)} %get-tuple-element.39), channel_id=1, replica_groups=mesh['ctx'=4,'chan'=8] {'ctx'}, dimensions={0} | all-to-all | bytes 589824 | tf_op jit(solution)/shard_map/all_to_all | solution.py:690
  74.0 27.0 %scan_gradients.1 = (bf16[128,2048]{1,0:T(8,128)(2,1)}, bf16[128,2048]{1,0:T(8,128)(2,1)}, bf16[128,2048]{1,0:T(8,128)(2,1)}, bf16[32,2048]{1,0:T(8,128)(2,1)}, ...) custom-call(f32[128,128]{1,0:T(8,128)} %get-tuple-element.36.refs_0_, bf16[128,512]{1,0:T(8,128)(2,1)} %get-tuple-element.37.refs_1_, ...), custom_call_target="tpu_custom_call" | custom-call | tf_op jit(solution)/shard_map/scan_gradients/pallas_call | solution.py:476
  101.0 0.0 copy-start.2
  101.0 0.0 copy-start.3
  101.0 0.0 reduce-scatter.2.cloned.1.call-update
  101.0 0.9 copy-done.2
  101.9 8.8 %all_to_all.52 = bf16[8,80,128]{2,1,0:T(8,128)(2,1)S(1)} all-to-all(bf16[8,80,128]{2,1,0:T(8,128)(2,1)S(1)} %bitcast.25), channel_id=1, replica_groups=mesh['ctx'=4,'chan'=8] {'chan'}, dimensions={0} | all-to-all | bytes 327680 | tf_op jit(solution)/shard_map/all_to_all | solution.py:690
  110.8 8.9 %all_to_all.53 = bf16[8,80,128]{2,1,0:T(8,128)(2,1)} all-to-all(bf16[8,80,128]{2,1,0:T(8,128)(2,1)S(1)} %broadcast_in_dim.25), channel_id=1, replica_groups=mesh['ctx'=4,'chan'=8] {'chan'}, dimensions={0} | all-to-all | bytes 327680 | tf_op jit(solution)/shard_map/all_to_all | solution.py:690
  119.7 3.3 %all-to-all-start.5 = ((bf16[4,160,128]{2,1,0:T(8,128)(2,1)}), bf16[4,160,128]{2,1,0:T(8,128)(2,1)S(1)}, u32[]{:S(2)}, u32[]{:S(2)}) async-start(bf16[4,160,128]{2,1,0:T(8,128)(2,1)} %bitcast.8), calls=%async_computation.5 | async-start | bytes 327680 | tf_op jit(solution)/shard_map/all_to_all | solution.py:690
  123.1 0.0 copy-done.3
  123.1 2.0 %collective-permute-start.2 = (bf16[32,2048]{1,0:T(8,128)(2,1)S(1)}, bf16[32,2048]{1,0:T(8,128)(2,1)S(1)}, u32[]{:S(2)}, u32[]{:S(2)}) collective-permute-start(bf16[32,2048]{1,0:T(8,128)(2,1)S(1)} %copy-done.3), channel_id=1, source_target_pairs={{0,8},{8,16},{16,24},{24,0},{1,9},{9,17},{17,25},{25,1},{2,10},{10... | collective-permute-start | bytes 393224 | tf_op jit(solution)/shard_map/ppermute | solution.py:52
  125.1 2.4 %collective-permute-start.3 = (bf16[32,2048]{1,0:T(8,128)(2,1)S(1)}, bf16[32,2048]{1,0:T(8,128)(2,1)S(1)}, u32[]{:S(2)}, u32[]{:S(2)}) collective-permute-start(bf16[32,2048]{1,0:T(8,128)(2,1)S(1)} %copy-done.3), channel_id=1, source_target_pairs={{0,16},{8,24},{16,0},{24,8},{1,17},{9,25},{17,1},{25,9},{2,18},{10... | collective-permute-start | bytes 393224 | tf_op jit(solution)/shard_map/ppermute | solution.py:52
  127.4 1.5 collective-permute-start.4
  128.9 6.6 %conv_gradients.1 = (bf16[128,2048]{1,0:T(8,128)(2,1)}, f32[16,2048]{1,0:T(8,128)}, f32[8,2048]{1,0:T(8,128)}, f32[8,2048]{1,0:T(8,128)}) custom-call(bf16[640,128]{1,0:T(8,128)(2,1)} %bitcast.7.back_ref, bf16[544,2048]{1,0:T(8,128)(2,1)} %proj_ref.3, bf16[128,2048]{1,0:T(8,128)(2,1)} %get-tuple-element.41.scan_ref, bf16[128,2048]{1,0:T(8,128)(2,1)} %input_ref.3, ...), custom_call_target="tpu_custom_call" | custom-call | tf_op jit(solution)/shard_map/conv_gradients/pallas_call | solution.py:569
  135.5 1.3 collective-permute-start.1
  136.8 2.7 %collective-permute-start.5 = (f32[8,2048]{1,0:T(8,128)}, f32[8,2048]{1,0:T(8,128)S(1)}, u32[]{:S(2)}, u32[]{:S(2)}) collective-permute-start(f32[8,2048]{1,0:T(8,128)} %get-tuple-element.46.refs_8_), channel_id=1, source_target_pairs={{0,8},{8,16},{16,24},{24,0},{1,9},{9,17},{17,25},{25,1},{2,10},{10... | collective-permute-start | bytes 196616 | tf_op jit(solution)/shard_map/ppermute | solution.py:52
  139.5 0.1 collective-permute-done.2.refs_5_
  139.6 0.0 copy-start.4
  139.6 10.4 %collective-permute-start.6 = (f32[8,2048]{1,0:T(8,128)}, f32[8,2048]{1,0:T(8,128)S(1)}, u32[]{:S(2)}, u32[]{:S(2)}) collective-permute-start(f32[8,2048]{1,0:T(8,128)} %get-tuple-element.46.refs_8_), channel_id=1, source_target_pairs={{0,16},{8,24},{16,0},{24,8},{1,17},{9,25},{17,1},{25,9},{2,18},{10... | collective-permute-start | bytes 196616 | tf_op jit(solution)/shard_map/ppermute | solution.py:52
  150.0 0.0 collective-permute-done.3.refs_6_
  150.0 0.0 copy-start.5
  150.0 9.7 %collective-permute-start.7 = (f32[8,2048]{1,0:T(8,128)}, f32[8,2048]{1,0:T(8,128)S(1)}, u32[]{:S(2)}, u32[]{:S(2)}) collective-permute-start(f32[8,2048]{1,0:T(8,128)} %get-tuple-element.46.refs_8_), channel_id=1, source_target_pairs={{0,24},{8,0},{16,8},{24,16},{1,25},{9,1},{17,9},{25,17},{2,26},{10... | collective-permute-start | bytes 196616 | tf_op jit(solution)/shard_map/ppermute | solution.py:52
  159.7 0.0 collective-permute-done.4.refs_7_
  159.7 0.0 copy-start.6
  159.7 0.0 collective-permute-done.1.refs_2_
  159.7 0.0 copy-start.9
  159.7 0.0 collective-permute-done.5.refs_9_
  159.7 0.0 copy-start.10
  159.8 2.6 %collective-permute-done.6.refs_10_ = f32[8,2048]{1,0:T(8,128)S(1)} collective-permute-done((f32[8,2048]{1,0:T(8,128)}, f32[8,2048]{1,0:T(8,128)S(1)}, u32[]{:S(2)}, u32[]{:S(2)}) %collective-permute-start.6) | collective-permute-done | bytes 65568 | tf_op jit(solution)/shard_map/ppermute | solution.py:52
  162.3 0.0 copy-start.11
  162.3 0.0 collective-permute-done.7.refs_11_
  162.3 0.0 copy-done.4
  162.3 0.0 copy-done.5
  162.4 0.0 copy-done.6
  162.4 0.0 copy-done.9
  162.4 0.0 copy-done.10
  162.4 0.6 copy-done.11
  163.0 0.0 copy-done.12
  163.0 2.0 %last_rows.1 = (bf16[128,2048]{1,0:T(8,128)(2,1)}, f32[4,2048]{1,0:T(4,128)}, f32[1,2048]{1,0:T(1,128)}, f32[1,2048]{1,0:T(1,128)}, f32[16,2048]{1,0:T(8,128)}, /*index=5*/f32[1,2048]{1,0:T(1,128)}) custom-call(bf16[128,2048]{1,0:T(8,128)(2,1)} %get-tuple-element.42.refs_0_, f32[16,2048]{1,0:T(8,128)} %get-tuple-element.43.refs_1_, ...), custom_call_target="tpu_custom_call", output_to_operand_aliasing={{0}: (0, {})} | custom-call | tf_op jit(solution)/shard_map/last_rows/pallas_call | solution.py:660
  165.0 0.0 all-to-all-done.5
  165.0 0.0 copy-start.1
  165.0 0.0 all-gather.3.cloned.1.call-done
  165.0 0.0 reduce-scatter.2.cloned.1.call-done.step_ref
  165.1 0.6 copy-done.1
  165.7 4.4 %row_gradients.1 = (f32[128,2048]{1,0:T(8,128)}, f32[8,2048]{1,0:T(8,128)}, f32[128,2048]{1,0:T(8,128)}) custom-call(bf16[640,128]{1,0:T(8,128)(2,1)} %bitcast.23, bf16[4,128,2048]{2,1,0:T(8,128)(2,1)} %bitcast.19, bf16[128,2048]{1,0:T(8,128)(2,1)} %reduce-scatter.2.cloned.1.call-done.step_ref), custom_call_target="tpu_custom_call" | custom-call | tf_op jit(solution)/shard_map/row_gradients/pallas_call | solution.py:610
  (5 shorter events, 0.1 us)
Async XLA Ops:
  7.2 157.9 %all-gather.3.cloned.1.call-start = ((), (), s32[]{:S(2)}) async-start(), calls=%async_computation.8 | async-start | bytes 2621440 | tf_op jit(solution)/shard_map/all_gather | solution.py:725
  8.0 6.4 %collective-permute-start = (bf16[3,2048]{1,0:T(4,128)(2,1)S(1)}, bf16[3,2048]{1,0:T(4,128)(2,1)S(1)}, u32[]{:S(2)}, u32[]{:S(2)}) collective-permute-start(bf16[3,2048]{1,0:T(4,128)(2,1)S(1)} %slice.3), channel_id=1, source_target_pairs={{0,8},{8,16},{16,24},{1,9},{9,17},{17,25},{2,10},{10,18},{18,26},{... | collective-permute-start | bytes 36872 | tf_op jit(solution)/shard_map/ppermute | solution.py:58
  14.4 0.6 copy-start.8
  15.0 18.7 %copy-start.7 = (f32[16,2048]{1,0:T(8,128)S(1)}, f32[16,2048]{1,0:T(8,128)}, u32[]{:S(2)}) copy-start(f32[16,2048]{1,0:T(8,128)} %param.18) | copy-start | bytes 393220
  30.2 9.2 %all-to-all-start.1 = ((bf16[8,16,544]{2,1,0:T(8,128)(2,1)}), bf16[8,16,544]{2,1,0:T(8,128)(2,1)S(1)}, u32[]{:S(2)}, u32[]{:S(2)}) async-start(bf16[8,16,544]{2,1,0:T(8,128)(2,1)} %broadcast_in_dim.22), calls=%async_computation.1 | async-start | bytes 327680 | tf_op jit(solution)/shard_map/all_to_all | solution.py:690
  33.6 131.4 %reduce-scatter.2.cloned.1.call-start = ((), (), s32[]{:S(2)}) async-start(), calls=%async_computation.7 | async-start | bytes 2621440 | tf_op jit(solution)/shard_map/reduce_scatter | solution.py:733
  39.4 0.7 copy-start
  101.0 0.9 copy-start.2
  101.0 22.1 %copy-start.3 = (bf16[32,2048]{1,0:T(8,128)(2,1)S(1)}, bf16[32,2048]{1,0:T(8,128)(2,1)}, u32[]{:S(2)}) copy-start(bf16[32,2048]{1,0:T(8,128)(2,1)} %get-tuple-element.45.refs_4_) | copy-start | bytes 393220
  119.7 45.3 %all-to-all-start.5 = ((bf16[4,160,128]{2,1,0:T(8,128)(2,1)}), bf16[4,160,128]{2,1,0:T(8,128)(2,1)S(1)}, u32[]{:S(2)}, u32[]{:S(2)}) async-start(bf16[4,160,128]{2,1,0:T(8,128)(2,1)} %bitcast.8), calls=%async_computation.5 | async-start | bytes 327680 | tf_op jit(solution)/shard_map/all_to_all | solution.py:690
  123.1 16.5 %collective-permute-start.2 = (bf16[32,2048]{1,0:T(8,128)(2,1)S(1)}, bf16[32,2048]{1,0:T(8,128)(2,1)S(1)}, u32[]{:S(2)}, u32[]{:S(2)}) collective-permute-start(bf16[32,2048]{1,0:T(8,128)(2,1)S(1)} %copy-done.3), channel_id=1, source_target_pairs={{0,8},{8,16},{16,24},{24,0},{1,9},{9,17},{17,25},{25,1},{2,10},{10... | collective-permute-start | bytes 393224 | tf_op jit(solution)/shard_map/ppermute | solution.py:52
  125.1 25.0 %collective-permute-start.3 = (bf16[32,2048]{1,0:T(8,128)(2,1)S(1)}, bf16[32,2048]{1,0:T(8,128)(2,1)S(1)}, u32[]{:S(2)}, u32[]{:S(2)}) collective-permute-start(bf16[32,2048]{1,0:T(8,128)(2,1)S(1)} %copy-done.3), channel_id=1, source_target_pairs={{0,16},{8,24},{16,0},{24,8},{1,17},{9,25},{17,1},{25,9},{2,18},{10... | collective-permute-start | bytes 393224 | tf_op jit(solution)/shard_map/ppermute | solution.py:52
  127.4 32.3 %collective-permute-start.4 = (bf16[32,2048]{1,0:T(8,128)(2,1)S(1)}, bf16[32,2048]{1,0:T(8,128)(2,1)S(1)}, u32[]{:S(2)}, u32[]{:S(2)}) collective-permute-start(bf16[32,2048]{1,0:T(8,128)(2,1)S(1)} %copy-done.3), channel_id=1, source_target_pairs={{0,24},{8,0},{16,8},{24,16},{1,25},{9,1},{17,9},{25,17},{2,26},{10... | collective-permute-start | bytes 393224 | tf_op jit(solution)/shard_map/ppermute | solution.py:52
  135.5 24.2 %collective-permute-start.1 = (f32[8,2048]{1,0:T(8,128)}, f32[8,2048]{1,0:T(8,128)S(1)}, u32[]{:S(2)}, u32[]{:S(2)}) collective-permute-start(f32[8,2048]{1,0:T(8,128)} %get-tuple-element.44), channel_id=1, source_target_pairs={{8,0},{16,8},{24,16},{9,1},{17,9},{25,17},{10,2},{18,10},{26,18},{... | collective-permute-start | bytes 196616 | tf_op jit(solution)/shard_map/ppermute | solution.py:58
  136.8 22.9 %collective-permute-start.5 = (f32[8,2048]{1,0:T(8,128)}, f32[8,2048]{1,0:T(8,128)S(1)}, u32[]{:S(2)}, u32[]{:S(2)}) collective-permute-start(f32[8,2048]{1,0:T(8,128)} %get-tuple-element.46.refs_8_), channel_id=1, source_target_pairs={{0,8},{8,16},{16,24},{24,0},{1,9},{9,17},{17,25},{25,1},{2,10},{10... | collective-permute-start | bytes 196616 | tf_op jit(solution)/shard_map/ppermute | solution.py:52
  139.6 22.7 %copy-start.4 = (bf16[32,2048]{1,0:T(8,128)(2,1)}, bf16[32,2048]{1,0:T(8,128)(2,1)S(1)}, u32[]{:S(2)}) copy-start(bf16[32,2048]{1,0:T(8,128)(2,1)S(1)} %collective-permute-done.2.refs_5_) | copy-start | bytes 393220
  139.6 22.7 %collective-permute-start.6 = (f32[8,2048]{1,0:T(8,128)}, f32[8,2048]{1,0:T(8,128)S(1)}, u32[]{:S(2)}, u32[]{:S(2)}) collective-permute-start(f32[8,2048]{1,0:T(8,128)} %get-tuple-element.46.refs_8_), channel_id=1, source_target_pairs={{0,16},{8,24},{16,0},{24,8},{1,17},{9,25},{17,1},{25,9},{2,18},{10... | collective-permute-start | bytes 196616 | tf_op jit(solution)/shard_map/ppermute | solution.py:52
  150.0 12.3 %copy-start.5 = (bf16[32,2048]{1,0:T(8,128)(2,1)}, bf16[32,2048]{1,0:T(8,128)(2,1)S(1)}, u32[]{:S(2)}) copy-start(bf16[32,2048]{1,0:T(8,128)(2,1)S(1)} %collective-permute-done.3.refs_6_) | copy-start | bytes 393220
  150.0 12.3 %collective-permute-start.7 = (f32[8,2048]{1,0:T(8,128)}, f32[8,2048]{1,0:T(8,128)S(1)}, u32[]{:S(2)}, u32[]{:S(2)}) collective-permute-start(f32[8,2048]{1,0:T(8,128)} %get-tuple-element.46.refs_8_), channel_id=1, source_target_pairs={{0,24},{8,0},{16,8},{24,16},{1,25},{9,1},{17,9},{25,17},{2,26},{10... | collective-permute-start | bytes 196616 | tf_op jit(solution)/shard_map/ppermute | solution.py:52
  159.7 2.6 %copy-start.6 = (bf16[32,2048]{1,0:T(8,128)(2,1)}, bf16[32,2048]{1,0:T(8,128)(2,1)S(1)}, u32[]{:S(2)}) copy-start(bf16[32,2048]{1,0:T(8,128)(2,1)S(1)} %collective-permute-done.4.refs_7_) | copy-start | bytes 393220
  159.7 2.6 %copy-start.9 = (f32[8,2048]{1,0:T(8,128)}, f32[8,2048]{1,0:T(8,128)S(1)}, u32[]{:S(2)}) copy-start(f32[8,2048]{1,0:T(8,128)S(1)} %collective-permute-done.1.refs_2_) | copy-start | bytes 196612
  159.7 2.6 %copy-start.10 = (f32[8,2048]{1,0:T(8,128)}, f32[8,2048]{1,0:T(8,128)S(1)}, u32[]{:S(2)}) copy-start(f32[8,2048]{1,0:T(8,128)S(1)} %collective-permute-done.5.refs_9_) | copy-start | bytes 196612
  162.3 0.6 copy-start.11
  162.3 0.7 copy-start.12
  165.0 0.7 copy-start.1
Sparse Core Ops, SparseCore 0:
  20.0 54.0 all-gather.2
  101.2 55.9 reduce-scatter.1

commit v3 on v2

--- a/solution.py
+++ b/solution.py
@@ -129,7 +129,7 @@
 
 
 def local_kernel(low_rank, states, places, *refs):
-    part_ref, refs = refs[0], refs[1:]
+    parts, refs = refs[:2], refs[2:]
     (weight_ref, bias_ref, decay_ref, conv_ref, gate_ref, grad_ref) = refs[:6]
     (dt_ref, ends_ref, coef_ref, low) = refs[6:10]
     (proj, coef_v, coef, dts, dxs, gs, fwd, bwd, sem) = refs[10:]
@@ -140,8 +140,9 @@
 
     @pl.when(step == 0)
     def _():
-        proj[...] = part_ref[...].astype(F32)
-        low[...] = part_ref[:, :low_rank]
+        total = (parts[0][...].astype(F32) + parts[1][...].astype(F32)).astype(BF)
+        proj[...] = total.astype(F32)
+        low[...] = total[:, :low_rank]
         coef_v[...] = jnp.zeros_like(coef_v)
         coef_v[:, : 2 * states] = proj[:, low_rank:]
         coef_ref[...] = coef_v[...]
@@ -214,9 +215,9 @@
             ends_ref[other] = jnp.where(other > place, fwd[...], bwd[...]).astype(BF)
 
 
-def local_call(part, step_weight, step_bias, decay, conv_out, gate, grad, states, places):
+def local_call(parts, step_weight, step_bias, decay, conv_out, gate, grad, states, places):
     rows, chans = conv_out.shape
-    wide = part.shape[1]
+    wide = parts[0].shape[1]
     low_rank = step_weight.shape[0]
     chunks, _, groups, _ = decay.shape
     width = groups * 128
@@ -227,6 +228,7 @@
         grid=(chunks,),
         in_specs=[
             whole((rows, wide)),
+            whole((rows, wide)),
             columns(low_rank, width),
             columns(1, width),
             whole(decay.shape),
@@ -259,7 +261,7 @@
         ],
         compiler_params=params(),
         name="local_ends",
-    )(part, step_weight, step_bias, decay, conv_out, gate, grad)
+    )(*parts, step_weight, step_bias, decay, conv_out, gate, grad)
 
 
 def fold_sublanes(values):
@@ -284,13 +286,14 @@
     return values[0]
 
 
-def scan_kernel(places, states, *refs):
+def scan_kernel(places, states, opening, *refs):
     (coef, low_ref, dt_ref, decay_ref, conv_ref, gate_ref, grad_ref, weight_ref, skip_ref) = refs[:9]
     ends, refs = refs[9], refs[10:]
+    if not opening:
+        before_ref, refs = refs[0], refs[4:]
     (pre_ref, gate_out, scan_out, small_ref, prod_ref, part_ref) = refs[:6]
     refs = refs[6:]
     (xs, dxs, gs, ys, dds, qs, decayed, coef_out, coef_in, rate, decay_acc, acc, small) = refs
-    step = pl.program_id(0)
     rows = conv_ref.shape[0]
     groups = decay_ref.shape[2]
     low_rank = weight_ref.shape[0]
@@ -445,64 +448,67 @@
 
     ranks, coef_rows, block = low_rank // places, 2 * states // places, acc.shape[0] // places
 
-    @pl.when(step == 0)
-    def _():
-        acc[...] = jnp.zeros_like(acc)
-
+    acc[...] = jnp.zeros_like(acc) if opening else before_ref[...]
     for q in range(places):
-        first = q * block
-        acc[first : first + ranks, :] += wide[q * ranks : (q + 1) * ranks, :]
-        acc[first + ranks : first + ranks + coef_rows, :] += coefs[
+        at = q * block
+        acc[at : at + ranks, :] += wide[q * ranks : (q + 1) * ranks, :]
+        acc[at + ranks : at + ranks + coef_rows, :] += coefs[
             q * coef_rows : (q + 1) * coef_rows, :
         ]
-
-    @pl.when(step == pl.num_programs(0) - 1)
-    def _():
-        part_ref[...] = acc[...].astype(BF)
+    part_ref[...] = acc[...].astype(part_ref.dtype)
 
 
 def padded(wide):
     return (wide + 127) // 128 * 128
 
 
-def scan_call(places, coef, low, dt, decay, conv_out, gate, grad, step_weight, skip, ends):
+def scan_call(
+    places, chunk, coef, low, dt, decay, conv_out, gate, grad, step_weight, skip, ends, previous
+):
     rows, chans = conv_out.shape
     low_rank = step_weight.shape[0]
     chunks, states, groups, _ = decay.shape
     width = groups * 128
     wide = padded(low_rank + 2 * states)
-    lead = lambda *shape: pl.BlockSpec((1,) + shape, lambda i: (i,) + (0,) * len(shape))
+    lead = lambda *shape: pl.BlockSpec((1,) + shape, lambda i: (chunk,) + (0,) * len(shape))
+    here = lambda height: pl.BlockSpec((height, width), lambda i: (0, chunk))
     tall = pltpu.VMEM((rows * groups, 128), F32)
+    first, last = chunk == 0, chunk == chunks - 1
+    in_specs = [
+        pl.BlockSpec(memory_space=pltpu.SMEM),
+        whole((rows, low_rank)),
+        lead(rows * groups, 128),
+        lead(states, groups, 128),
+        here(rows),
+        here(rows),
+        here(rows),
+        here(low_rank),
+        here(1),
+        pl.BlockSpec((places, 1, states + 2, groups, 128), lambda i: (0, chunk, 0, 0, 0)),
+    ]
+    aliases = {}
+    if not first:
+        in_specs += [whole((wide, rows))] + [pl.BlockSpec(memory_space=pl.ANY)] * 3
+        aliases = {11: 1, 12: 2, 13: 3}
     return pl.pallas_call(
-        functools.partial(scan_kernel, places, states),
-        grid=(chunks,),
-        in_specs=[
-            pl.BlockSpec(memory_space=pltpu.SMEM),
-            whole((rows, low_rank)),
-            lead(rows * groups, 128),
-            lead(states, groups, 128),
-            columns(rows, width),
-            columns(rows, width),
-            columns(rows, width),
-            columns(low_rank, width),
-            columns(1, width),
-            pl.BlockSpec((places, 1, states + 2, groups, 128), lambda i: (0, i, 0, 0, 0)),
-        ],
+        functools.partial(scan_kernel, places, states, first),
+        grid=(1,),
+        in_specs=in_specs,
         out_specs=[
-            columns(rows, width),
-            columns(rows, width),
-            columns(rows, width),
-            columns(32, width),
-            columns(low_rank, width),
+            whole((rows, width)),
+            here(rows),
+            here(rows),
+            here(32),
+            whole((low_rank, width)),
             whole((wide, rows)),
         ],
         out_shape=[
-            sds((rows, chans), BF),
+            sds((rows, width), BF),
             sds((rows, chans), BF),
             sds((rows, chans), BF),
             sds((32, chans), BF),
-            sds((low_rank, chans), BF),
-            sds((wide, rows), BF),
+            sds((low_rank, width), BF),
+            sds((wide, rows), BF if last else F32),
         ],
         scratch_shapes=[
             tall,
@@ -519,20 +525,21 @@
             pltpu.VMEM((wide, rows), F32),
             pltpu.VMEM((32, width), F32),
         ],
+        input_output_aliases=aliases,
         compiler_params=params(),
         name="scan_gradients",
-    )(coef, low, dt, decay, conv_out, gate, grad, step_weight, skip, ends)
-
-
-def conv_grad_kernel(places, low_rank, back_ref, proj_ref, scan_ref, input_ref, rim_ref, weight_ref, bias_ref,
-                     out_ref, tail_ref, head_ref, small_ref, ext, grad):
+    )(coef, low, dt, decay, conv_out, gate, grad, step_weight, skip, ends, *previous)
+
+
+def conv_grad_kernel(places, low_rank, back_a, back_b, proj_ref, scan_ref, input_ref, rim_ref, weight_ref, bias_ref,
+                     out_ref, tail_ref, small_ref, ext, grad):
     taps = weight_ref.shape[0]
     rows = input_ref.shape[0]
     fill_extended(ext, rim_ref, input_ref, taps)
     wide = proj_ref.shape[0]
-    block = back_ref.shape[0] // places
+    block = back_a.shape[0] // places
     ranks, coef_rows = low_rank // places, (wide - low_rank) // places
-    back = back_ref[...].astype(F32)
+    back = (back_a[...].astype(F32) + back_b[...].astype(F32)).astype(BF).astype(F32)
     order = [back[q * block : q * block + ranks, :] for q in range(places)]
     order += [back[q * block + ranks : q * block + ranks + coef_rows, :] for q in range(places)]
     d_xc = dot(jnp.concatenate(order, axis=0).astype(BF), proj_ref[...], TN)
@@ -555,13 +562,12 @@
             total = total + weight_ref[tap : tap + 1, :] * grad[first : first + 16, :]
         out_ref[start : start + 16, :] = total.astype(BF)
     tail_ref[...] = total
-    head_ref[...] = grad[0:8, :]
     small_ref[...] = jnp.concatenate(
-        sums + [jnp.zeros((small_ref.shape[0] - taps - 1, small_ref.shape[1]), F32)], axis=0
-    )
-
-
-def conv_grad_call(places, low_rank, back, proj_weight, scan_part, conv_input, rim, weight, bias):
+        sums + [jnp.zeros((8 - taps - 1, small_ref.shape[1]), F32), grad[0:8, :]], axis=0
+    ).astype(BF)
+
+
+def conv_grad_call(places, low_rank, backs, proj_weight, scan_part, conv_input, rim, weight, bias):
     rows, chans = conv_input.shape
     taps = weight.shape[0]
     wide = proj_weight.shape[0]
@@ -570,7 +576,8 @@
         functools.partial(conv_grad_kernel, places, low_rank),
         grid=(chans // width,),
         in_specs=[
-            whole(back.shape),
+            whole(backs[0].shape),
+            whole(backs[1].shape),
             columns(wide, width),
             columns(rows, width),
             columns(rows, width),
@@ -578,43 +585,45 @@
             columns(taps, width),
             columns(1, width),
         ],
-        out_specs=[columns(rows, width), columns(16, width), columns(8, width), columns(8, width)],
-        out_shape=[
-            sds((rows, chans), BF),
-            sds((16, chans), F32),
-            sds((8, chans), F32),
-            sds((8, chans), F32),
-        ],
+        out_specs=[columns(rows, width), columns(16, width), columns(16, width)],
+        out_shape=[sds((rows, chans), BF), sds((16, chans), F32), sds((16, chans), BF)],
         scratch_shapes=[pltpu.VMEM((rows + 8, width), F32), pltpu.VMEM((rows + 8, width), F32)],
         compiler_params=params(),
         name="conv_gradients",
-    )(back, proj_weight, scan_part, conv_input, rim, weight, bias)
-
-
-def rows_kernel(rank_rows, cut_ref, conv_ref, step_ref, out_ref, coef_ref, step_out):
-    places = conv_ref.shape[0]
+    )(*backs, proj_weight, scan_part, conv_input, rim, weight, bias)
+
+
+def rows_kernel(places, rank_rows, chunks, *refs):
+    cut_ref, refs = refs[0], refs[1:]
+    blocks, refs = refs[: 2 * places - 1], refs[2 * places - 1 :]
+    steps, (out_ref, coef_ref, step_out) = refs[:chunks], refs[chunks:]
+    place = lax.axis_index("ctx")
     block = cut_ref.shape[0] // places
     total = None
-    for q in range(places):
-        part = dot(cut_ref[q * block : (q + 1) * block, :], conv_ref[q])
+    for hop, ref in zip([0] + [k for d in range(1, places) for k in (d, -d)], blocks):
+        source = lax.rem(place + places - hop, places)
+        cut = cut_ref[pl.ds(pl.multiple_of(source * block, 16 if block % 16 == 0 else 8), block), :]
+        part = dot(cut, ref[...])
         total = part if total is None else total + part
     out_ref[...] = total[:rank_rows, :]
     coef_ref[...] = total[rank_rows : rank_rows + coef_ref.shape[0], :]
-    step_out[...] = step_ref[...].astype(F32)
-
-
-def rows_call(cuts, conv_all, steps, coef_rows):
-    places, rows, chans = conv_all.shape
-    rank_rows = steps.shape[0]
-    width = min(512, chans)
+    for chunk in range(chunks):
+
+        @pl.when(pl.program_id(0) == chunk)
+        def _():
+            step_out[...] = steps[chunk][...].astype(F32)
+
+
+def rows_call(places, cuts, blocks, steps, coef_rows):
+    rows, chans = blocks[0].shape
+    rank_rows, width = steps[0].shape
+    chunks = len(steps)
     return pl.pallas_call(
-        functools.partial(rows_kernel, rank_rows),
-        grid=(chans // width,),
-        in_specs=[
-            whole(cuts.shape),
-            pl.BlockSpec((places, rows, width), lambda i: (0, 0, i)),
-            columns(rank_rows, width),
-        ],
+        functools.partial(rows_kernel, places, rank_rows, chunks),
+        grid=(chunks,),
+        in_specs=[whole(cuts.shape)]
+        + [columns(rows, width)] * len(blocks)
+        + [whole((rank_rows, width))] * chunks,
         out_specs=[
             columns(rank_rows, width), columns(coef_rows, width), columns(rank_rows, width)
         ],
@@ -623,19 +632,21 @@
         ],
         compiler_params=params(),
         name="row_gradients",
-    )(cuts, conv_all, steps)
+    )(cuts, *blocks, *steps)
 
 
 def last_kernel(places, states, taps, *refs):
-    (main_ref, tail_ref, next_ref, weight_ref) = refs[:4]
-    early, refs = refs[4 : 4 + places], refs[4 + places :]
+    (_, tail_ref, weight_ref) = refs[:3]
+    early, refs = refs[3 : 3 + places], refs[3 + places :]
     late, refs = refs[:places], refs[places:]
     (out_ref, conv_w, conv_b, step_b, decay, skip, fix) = refs
     fix[...] = tail_ref[...]
+    inside = lax.axis_index("ctx") < places - 1
+    following = jnp.where(inside, late[places - 1][8:16, :].astype(F32), 0.0)
     for row in range(taps - 1):
         extra = jnp.zeros((1, fix.shape[1]), F32)
         for tap in range(row + 1):
-            extra = extra + weight_ref[tap : tap + 1, :] * next_ref[row - tap : row - tap + 1, :]
+            extra = extra + weight_ref[tap : tap + 1, :] * following[row - tap : row - tap + 1, :]
         at = 16 - (taps - 1) + row
         fix[at : at + 1, :] += extra
     out_ref[...] = fix[...].astype(BF)
@@ -645,14 +656,14 @@
     decay[...] = total[:states, :]
     step_b[...] = total[states : states + 1, :]
     skip[...] = total[states + 1 : states + 2, :]
-    total = late[0][...]
+    total = late[0][...].astype(F32)
     for part in late[1:]:
-        total = total + part[...]
+        total = total + part[...].astype(F32)
     conv_w[...] = total[:taps, :]
     conv_b[...] = total[taps : taps + 1, :]
 
 
-def last_call(main, tail, following, weight, early, late, states):
+def last_call(main, tail, weight, early, late, states):
     rows, chans = main.shape
     taps = weight.shape[0]
     places = len(early)
@@ -660,9 +671,9 @@
     return pl.pallas_call(
         functools.partial(last_kernel, places, states, taps),
         grid=(1,),
-        in_specs=[pl.BlockSpec(memory_space=pl.ANY), columns(16, width), columns(8, width), columns(taps, width)]
+        in_specs=[pl.BlockSpec(memory_space=pl.ANY), columns(16, width), columns(taps, width)]
         + [columns(32, width)] * places
-        + [columns(8, width)] * places,
+        + [columns(16, width)] * places,
         out_specs=[
             pl.BlockSpec((16, width), lambda i: (rows // 16 - 1, i)),
             columns(taps, width),
@@ -683,18 +694,25 @@
         input_output_aliases={0: 0},
         compiler_params=params(),
         name="last_rows",
-    )(main, tail, following, weight, *early, *late)
+    )(main, tail, weight, *early, *late)
 
 
 def exchange(block, axis):
     return lax.all_to_all(block, axis, split_axis=0, concat_axis=0, tiled=True)
 
 
+def swap(block, axis, mask):
+    return lax.ppermute(block, axis, [(i, i ^ mask) for i in range(lax.axis_size(axis))])
+
+
 def chan_sum(part):
-    peers = lax.axis_size("chan")
-    pieces = exchange(part, "chan").reshape((peers, part.shape[0] // peers, part.shape[1]))
-    total = jnp.sum(pieces.astype(F32), axis=0, keepdims=True).astype(BF)
-    return exchange(jnp.broadcast_to(total, pieces.shape).reshape(part.shape), "chan")
+    mask, peers = 1, lax.axis_size("chan")
+    while True:
+        other = swap(part, "chan", mask)
+        mask *= 2
+        if mask == peers:
+            return part, other
+        part = (part.astype(F32) + other.astype(F32)).astype(BF)
 
 
 def body(
@@ -720,28 +738,45 @@
     step_bias = step_bias[None, :]
     skip_gain = skip_gain[None, :]
 
+    chunks = decay.shape[0]
     rim = shift(conv_input[rows - (taps - 1) :], "ctx", 1)
     conv_out, part = conv_call(conv_input, rim, conv_weight, conv_bias, proj_weight)
-    conv_all = lax.all_gather(conv_out, "ctx")
+    blocks = [conv_out]
+    right, left = shift(conv_out, "ctx", 1), shift(conv_out, "ctx", -1)
+    blocks += [right, left]
+    parts = chan_sum(part)
+    for hop in range(2, places):
+        if hop == 2:
+            parts, right, left = lax.optimization_barrier((parts, right, left))
+            right, left = shift(right, "ctx", 1), shift(left, "ctx", -1)
+            blocks += [right, left]
     dt, ends, coef, low = local_call(
-        chan_sum(part), step_weight, step_bias, decay, conv_out, gate_input, out_grad, states, places
+        parts, step_weight, step_bias, decay, conv_out, gate_input, out_grad, states, places
     )
     ends = exchange(ends, "ctx")
-    pre_bf, grad_gate, scan_part, small, products, part = scan_call(
-        places, coef, low, dt, decay, conv_out, gate_input, out_grad, step_weight, skip_gain, ends
+    for hop in range(3, places):
+        ends, right, left = lax.optimization_barrier((ends, right, left))
+        right, left = shift(right, "ctx", 1), shift(left, "ctx", -1)
+        blocks += [right, left]
+    previous, steps = [], []
+    for chunk in range(chunks):
+        pre_bf, grad_gate, scan_part, small, products, part = scan_call(
+            places, chunk, coef, low, dt, decay, conv_out, gate_input, out_grad, step_weight,
+            skip_gain, ends, previous,
+        )
+        previous = [part, grad_gate, scan_part, small]
+        steps.append(lax.psum_scatter(products, "ctx", scatter_dimension=0, tiled=True))
+    early = [small] + [rotate(small, "ctx", hop) for hop in range(1, places)]
+    backs = chan_sum(part)
+    back = (backs[0].astype(F32) + backs[1].astype(F32)).astype(BF)
+    cuts = exchange(back, "ctx")
+    main, tail, sums = conv_grad_call(
+        places, low_rank, backs, proj_weight, scan_part, conv_input, rim, conv_weight, conv_bias
     )
-    steps = lax.psum_scatter(products, "ctx", scatter_dimension=0, tiled=True)
-    early = [small] + [rotate(small, "ctx", hop) for hop in range(1, places)]
-    back = chan_sum(part)
-    cuts = exchange(back, "ctx")
-    main, tail, head, sums = conv_grad_call(
-        places, low_rank, back, proj_weight, scan_part, conv_input, rim, conv_weight, conv_bias
-    )
-    following = shift(head, "ctx", -1)
     late = [sums] + [rotate(sums, "ctx", hop) for hop in range(1, places)]
-    grad_proj, grad_coef, grad_step = rows_call(cuts, conv_all, steps, 2 * states // places)
+    grad_proj, grad_coef, grad_step = rows_call(places, cuts, blocks, steps, 2 * states // places)
     grad_input, conv_w, conv_b, step_b, decay_grad, skip = last_call(
-        main, tail, following, conv_weight, early, late, states
+        main, tail, conv_weight, early, late, states
     )
     return (
         grad_input,

time: 178 us -> 188 us (1.056)
  blocking collectives: 48.5 us -> 14 us
  waiting for transfers between devices: 9.21 us -> 40.8 us
  starting transfers between devices: 41.6 us -> 51 us
  other arithmetic: 0.06 us -> 2.76 us
  Pallas kernels: 57.7 us -> 60.4 us
    all_to_all x4 -> x1, blocking collectives: 48.5 us -> 14 us  [exchange(): return lax.all_to_all(block, axis, split_axis=0, concat_axis=0, tiled=True)]
    ppermute x6, waiting for transfers between devices: 2.65 us -> 21.3 us  [rotate(): lax.ppermute(block, axis, [(i, (i + distance) % count) for i in range(cou...]
    ppermute x0 -> x6, waiting for transfers between devices: none -> 15.4 us  [swap(): lax.ppermute(block, axis, [(i, i ^ mask) for i in range(lax.axis_size(axi...]
    ppermute x2 -> x7, starting transfers between devices: 6.22 us -> 18.9 us  [shift(): return lax.ppermute(block, axis, route)]
    ppermute x6, starting transfers between devices: 28.6 us -> 21.4 us  [rotate(): lax.ppermute(block, axis, [(i, (i + distance) % count) for i in range(cou...]
    ppermute x0 -> x6, starting transfers between devices: none -> 6.35 us  [swap(): lax.ppermute(block, axis, [(i, i ^ mask) for i in range(lax.axis_size(axi...]
    all_to_all x2 -> x1, waiting for transfers between devices: 5.06 us -> 0.01 us  [exchange(): return lax.all_to_all(block, axis, split_axis=0, concat_axis=0, tiled=True)]
    convert_element_type x0 -> x5, other arithmetic: none -> 2.76 us  [the longest x4 2.02 us: chan_sum(): part = (part.astype(F32) + other.astype(F32)).astype(BF)]
  transfers between devices with their start and end apart: 12 -> 22, of which waited for: 4 -> 10; matrix products, arithmetic and copies ran while one was open for 1% -> 2% of each run, Pallas kernels for 27% -> 12%
where the time goes in v3:
time: 188 us; the launch traced here: 187 us
  Pallas kernels  60.4 us (32%)
  starting transfers between devices  51 us (27%)
  waiting for transfers between devices  40.8 us (22%)
  between operations  14.4 us (8%)
  blocking collectives  14 us (7%)
  local copies, waits for them, and re-layouts  3.73 us (2%)
  other arithmetic  2.76 us (1%)
    pallas_call x2, Pallas kernels, scan_call(): pl.pallas_call(functools.partial(scan_kernel, places, states, first), gri...  29.5 us
    ppermute x6, starting transfers between devices, rotate(): lax.ppermute(block, axis, [(i, (i + distance) % count) for i in range(cou...  21.4 us
    ppermute x6, waiting for transfers between devices, rotate(): lax.ppermute(block, axis, [(i, (i + distance) % count) for i in range(cou...  21.3 us
    ppermute x7, starting transfers between devices, shift(): return lax.ppermute(block, axis, route)  18.9 us
    ppermute x6, waiting for transfers between devices, swap(): lax.ppermute(block, axis, [(i, i ^ mask) for i in range(lax.axis_size(axi...  15.4 us
    all_to_all x1, blocking collectives, exchange(): return lax.all_to_all(block, axis, split_axis=0, concat_axis=0, tiled=True)  14 us
    pallas_call x1, Pallas kernels, local_call(): pl.pallas_call(functools.partial(local_kernel, low_rank, states, places),...  12.9 us
    pallas_call x1, Pallas kernels, conv_grad_call(): pl.pallas_call(functools.partial(conv_grad_kernel, places, low_rank), gri...  6.71 us
  transfers between devices with their start and end apart: 22, of which 10 were waited for; matrix products, arithmetic and copies ran while one was open for 2% of the time, Pallas kernels for 12%

profile of v3, /device:TPU:0, one launch (start us, length us, event | category | flops | bytes accessed | tf_op | source)
XLA Modules:
  0.0 187.1 jit_solution(8770060793984755577)
XLA Ops:
  7.2 0.0 reduce-scatter.5.cloned.1.call-start
  7.2 0.8 slice.3
  8.0 4.9 %collective-permute-start = (bf16[3,2048]{1,0:T(4,128)(2,1)S(1)}, bf16[3,2048]{1,0:T(4,128)(2,1)S(1)}, u32[]{:S(2)}, u32[]{:S(2)}) collective-permute-start(bf16[3,2048]{1,0:T(4,128)(2,1)S(1)} %slice.3), channel_id=1, source_target_pairs={{0,8},{8,16},{16,24},{1,9},{9,17},{17,25},{2,10},{10,18},{18,26},{... | collective-permute-start | bytes 36872 | tf_op jit(solution)/shard_map/ppermute | solution.py:58
  13.0 1.4 collective-permute-done.rim_ref
  14.4 0.6 copy-done.16
  15.0 4.9 %conv_project.1 = (bf16[128,2048]{1,0:T(8,128)(2,1)}, bf16[128,544]{1,0:T(8,128)(2,1)}) custom-call(bf16[128,2048]{1,0:T(8,128)(2,1)} %input_ref.3, bf16[3,2048]{1,0:T(4,128)(2,1)} %copy-done.16, f32[4,2048]{1,0:T(4,128)} %refs_2_.3, f32[1,2048]{1,0:T(1,128)} %bitcast.22, bf16[544,2048]{1,0:T(8,128)(2,1)} %proj_ref.3), custom_call_target="tpu_custom_call" | custom-call | tf_op jit(solution)/shard_map/conv_project/pallas_call | solution.py:103
  19.9 0.0 collective-permute-start.1
  19.9 4.2 %collective-permute-start.4 = (bf16[128,2048]{1,0:T(8,128)(2,1)}, bf16[128,2048]{1,0:T(8,128)(2,1)S(1)}, u32[]{:S(2)}, u32[]{:S(2)}) collective-permute-start(bf16[128,2048]{1,0:T(8,128)(2,1)} %get-tuple-element.46.refs_5_.refs_4_.refs_1_), channel_id=1, source_target_pairs={{0,8},{8,16},{16,24},{1,9},{9,17},{17,25},{2,10},{10,18},{18,26},{... | collective-permute-start | bytes 1572872 | tf_op jit(solution)/shard_map/ppermute | solution.py:58
  24.1 1.3 collective-permute-start.5
  25.4 0.0 collective-permute-done.1
  25.4 1.0 add_convert_fusion.4
  26.4 1.6 collective-permute-start.2
  27.9 4.8 %collective-permute-done.2 = bf16[128,544]{1,0:T(8,128)(2,1)S(1)} collective-permute-done((bf16[128,544]{1,0:T(8,128)(2,1)S(1)}, bf16[128,544]{1,0:T(8,128)(2,1)S(1)}, u32[]{:S(2)}, u32[]{:S(2)}) %collective-permute-start.2) | collective-permute-done | bytes 139296 | tf_op jit(solution)/shard_map/ppermute | solution.py:705
  32.8 0.0 copy-start.3
  32.8 1.6 collective-permute-start.3
  34.4 4.0 %collective-permute-done.3.refs_1_ = bf16[128,544]{1,0:T(8,128)(2,1)S(1)} collective-permute-done((bf16[128,544]{1,0:T(8,128)(2,1)S(1)}, bf16[128,544]{1,0:T(8,128)(2,1)S(1)}, u32[]{:S(2)}, u32[]{:S(2)}) %collective-permute-start.3) | collective-permute-done | bytes 139296 | tf_op jit(solution)/shard_map/ppermute | solution.py:705
  38.4 0.0 collective-permute-done.4.refs_2_
  38.4 1.9 collective-permute-done.5.refs_3_
  40.3 3.5 %collective-permute-start.6 = (bf16[128,2048]{1,0:T(8,128)(2,1)S(1)}, bf16[128,2048]{1,0:T(8,128)(2,1)S(1)}, u32[]{:S(2)}, u32[]{:S(2)}) collective-permute-start(bf16[128,2048]{1,0:T(8,128)(2,1)S(1)} %collective-permute-done.4.refs_2_), channel_id=1, source_target_pairs={{0,8},{8,16},{16,24},{1,9},{9,17},{17,25},{2,10},{10,18},{18,26},{... | collective-permute-start | bytes 1572872 | tf_op jit(solution)/shard_map/ppermute | solution.py:58
  43.7 1.3 collective-permute-start.7
  45.1 0.7 copy.27
  45.7 12.9 %local_ends.1 = (f32[2,1024,128]{2,1,0:T(8,128)}, bf16[4,2,18,8,128]{4,3,2,1,0:T(8,128)(2,1)}, f32[128,128]{1,0:T(8,128)}, bf16[128,512]{1,0:T(8,128)(2,1)}) custom-call(bf16[128,544]{1,0:T(8,128)(2,1)} %copy-done.3, bf16[128,544]{1,0:T(8,128)(2,1)} %copy-done.11, bf16[512,2048]{1,0:T(8,128)(2,1)} %refs_7_.5, f32[1,2048]{1,0:T(1,128)} %bitcast.24, ...), custom_call_target="tpu_custom_call" | custom-call | tf_op jit(solution)/shard_map/local_ends/pallas_call | solution.py:226
  58.6 14.0 %all_to_all.16.refs_9_ = bf16[4,2,18,8,128]{4,3,2,1,0:T(8,128)(2,1)} all-to-all(bf16[4,2,18,8,128]{4,3,2,1,0:T(8,128)(2,1)} %get-tuple-element.52), channel_id=1, replica_groups=mesh['ctx'=4,'chan'=8] {'ctx'}, dimensions={0} | all-to-all | bytes 589824 | tf_op jit(solution)/shard_map/all_to_all | solution.py:701
  72.7 0.0 collective-permute-done.6.refs_4_
  72.7 0.0 collective-permute-done.7.refs_5_
  72.7 14.9 %scan_gradients.2 = (bf16[128,1024]{1,0:T(8,128)(2,1)}, bf16[128,2048]{1,0:T(8,128)(2,1)}, bf16[128,2048]{1,0:T(8,128)(2,1)}, bf16[32,2048]{1,0:T(8,128)(2,1)}, ...) custom-call(f32[128,128]{1,0:T(8,128)} %get-tuple-element.49.refs_0_, bf16[128,512]{1,0:T(8,128)(2,1)} %get-tuple-element.50.refs_1_, ...), custom_call_target="tpu_custom_call" | custom-call | tf_op jit(solution)/shard_map/scan_gradients/pallas_call | solution.py:493
  87.5 14.7 %scan_gradients.3 = (bf16[128,1024]{1,0:T(8,128)(2,1)}, bf16[128,2048]{1,0:T(8,128)(2,1)}, bf16[128,2048]{1,0:T(8,128)(2,1)}, bf16[32,2048]{1,0:T(8,128)(2,1)}, ...) custom-call(f32[128,128]{1,0:T(8,128)} %get-tuple-element.49.refs_0_, ...), custom_call_target="tpu_custom_call", output_to_operand_aliasing={{1}: (11, {}), {2}: (12, {}), {3}: (13, {})} | custom-call | tf_op jit(solution)/shard_map/scan_gradients/pallas_call | solution.py:493
  102.2 0.0 reduce-scatter.5.cloned.1.call-update
  102.2 0.0 reduce-scatter.3.cloned.1.call-start
  102.3 0.7 reduce-scatter.3.cloned.1.call-update
  103.0 0.1 collective-permute-start.8
  103.1 1.6 collective-permute-done.8
  104.7 1.0 add_convert_fusion.2
  105.6 1.6 collective-permute-start.9
  107.2 4.8 %collective-permute-done.9 = bf16[640,128]{1,0:T(8,128)(2,1)S(1)} collective-permute-done((bf16[640,128]{1,0:T(8,128)(2,1)S(1)}, bf16[640,128]{1,0:T(8,128)(2,1)S(1)}, u32[]{:S(2)}, u32[]{:S(2)}) %collective-permute-start.9) | collective-permute-done | bytes 163872 | tf_op jit(solution)/shard_map/ppermute | solution.py:705
  112.0 0.0 copy-start
  112.0 1.6 collective-permute-start.10
  113.6 2.4 %collective-permute-start.17 = (bf16[128,2048]{1,0:T(8,128)(2,1)S(1)}, bf16[128,2048]{1,0:T(8,128)(2,1)S(1)}, u32[]{:S(2)}, u32[]{:S(2)}) collective-permute-start(bf16[128,2048]{1,0:T(8,128)(2,1)S(1)} %collective-permute-done.6.refs_4_), channel_id=1, source_target_pairs={{0,8},{8,16},{16,24},{1,9},{9,17},{17,25},{2,10},{10,18},{18,26},{... | collective-permute-start | bytes 1572872 | tf_op jit(solution)/shard_map/ppermute | solution.py:58
  116.0 1.3 collective-permute-start.18
  117.3 0.3 collective-permute-done.10.back_b
  117.6 0.7 add_convert_fusion
  118.3 4.3 %all-to-all-start.1 = ((bf16[4,160,128]{2,1,0:T(8,128)(2,1)}), bf16[4,160,128]{2,1,0:T(8,128)(2,1)S(1)}, u32[]{:S(2)}, u32[]{:S(2)}) async-start(bf16[4,160,128]{2,1,0:T(8,128)(2,1)} %bitcast.4), calls=%async_computation.1 | async-start | bytes 327680 | tf_op jit(solution)/shard_map/all_to_all | solution.py:701
  122.6 2.0 %collective-permute-start.11 = (bf16[32,2048]{1,0:T(8,128)(2,1)S(1)}, bf16[32,2048]{1,0:T(8,128)(2,1)S(1)}, u32[]{:S(2)}, u32[]{:S(2)}) collective-permute-start(bf16[32,2048]{1,0:T(8,128)(2,1)S(1)} %copy-done.10), channel_id=1, source_target_pairs={{0,8},{8,16},{16,24},{24,0},{1,9},{9,17},{17,25},{25,1},{2,10},{10... | collective-permute-start | bytes 393224 | tf_op jit(solution)/shard_map/ppermute | solution.py:52
  124.6 2.4 %collective-permute-start.12 = (bf16[32,2048]{1,0:T(8,128)(2,1)S(1)}, bf16[32,2048]{1,0:T(8,128)(2,1)S(1)}, u32[]{:S(2)}, u32[]{:S(2)}) collective-permute-start(bf16[32,2048]{1,0:T(8,128)(2,1)S(1)} %copy-done.10), channel_id=1, source_target_pairs={{0,16},{8,24},{16,0},{24,8},{1,17},{9,25},{17,1},{25,9},{2,18},{10... | collective-permute-start | bytes 393224 | tf_op jit(solution)/shard_map/ppermute | solution.py:52
  127.0 1.5 collective-permute-start.13
  128.4 6.7 %conv_gradients.1 = (bf16[128,2048]{1,0:T(8,128)(2,1)}, f32[16,2048]{1,0:T(8,128)}, bf16[16,2048]{1,0:T(8,128)(2,1)}) custom-call(bf16[640,128]{1,0:T(8,128)(2,1)} %copy-done, bf16[640,128]{1,0:T(8,128)(2,1)} %copy-done.2, bf16[544,2048]{1,0:T(8,128)(2,1)} %proj_ref.3, bf16[128,2048]{1,0:T(8,128)(2,1)} %get-tuple-element.61.scan_ref, ...), custom_call_target="tpu_custom_call" | custom-call | tf_op jit(solution)/shard_map/conv_gradients/pallas_call | solution.py:575
  135.2 10.0 %collective-permute-done.11.refs_4_ = bf16[32,2048]{1,0:T(8,128)(2,1)S(1)} collective-permute-done((bf16[32,2048]{1,0:T(8,128)(2,1)S(1)}, bf16[32,2048]{1,0:T(8,128)(2,1)S(1)}, u32[]{:S(2)}, u32[]{:S(2)}) %collective-permute-start.11) | collective-permute-done | bytes 131104 | tf_op jit(solution)/shard_map/ppermute | solution.py:52
  145.2 5.8 %collective-permute-start.14 = (bf16[16,2048]{1,0:T(8,128)(2,1)}, bf16[16,2048]{1,0:T(8,128)(2,1)S(1)}, u32[]{:S(2)}, u32[]{:S(2)}) collective-permute-start(bf16[16,2048]{1,0:T(8,128)(2,1)} %get-tuple-element.65.refs_7_), channel_id=1, source_target_pairs={{0,8},{8,16},{16,24},{24,0},{1,9},{9,17},{17,25},{25,1},{2,10},{10... | collective-permute-start | bytes 196616 | tf_op jit(solution)/shard_map/ppermute | solution.py:52
  151.0 5.6 %collective-permute-done.12.refs_5_ = bf16[32,2048]{1,0:T(8,128)(2,1)S(1)} collective-permute-done((bf16[32,2048]{1,0:T(8,128)(2,1)S(1)}, bf16[32,2048]{1,0:T(8,128)(2,1)S(1)}, u32[]{:S(2)}, u32[]{:S(2)}) %collective-permute-start.12) | collective-permute-done | bytes 131104 | tf_op jit(solution)/shard_map/ppermute | solution.py:52
  156.6 0.0 collective-permute-start.15
  156.6 9.7 %collective-permute-start.16 = (bf16[16,2048]{1,0:T(8,128)(2,1)}, bf16[16,2048]{1,0:T(8,128)(2,1)S(1)}, u32[]{:S(2)}, u32[]{:S(2)}) collective-permute-start(bf16[16,2048]{1,0:T(8,128)(2,1)} %get-tuple-element.65.refs_7_), channel_id=1, source_target_pairs={{0,24},{8,0},{16,8},{24,16},{1,25},{9,1},{17,9},{25,17},{2,26},{10... | collective-permute-start | bytes 196616 | tf_op jit(solution)/shard_map/ppermute | solution.py:52
  166.4 5.7 %collective-permute-done.15.refs_9_ = bf16[16,2048]{1,0:T(8,128)(2,1)S(1)} collective-permute-done((bf16[16,2048]{1,0:T(8,128)(2,1)}, bf16[16,2048]{1,0:T(8,128)(2,1)S(1)}, u32[]{:S(2)}, u32[]{:S(2)}) %collective-permute-start.15) | collective-permute-done | bytes 65568 | tf_op jit(solution)/shard_map/ppermute | solution.py:52
  172.1 0.0 collective-permute-done.16.refs_10_
  172.1 0.6 copy-done.18
  172.7 0.0 copy-done.19
  172.7 2.0 %last_rows.1 = (bf16[128,2048]{1,0:T(8,128)(2,1)}, f32[4,2048]{1,0:T(4,128)}, f32[1,2048]{1,0:T(1,128)}, f32[1,2048]{1,0:T(1,128)}, f32[16,2048]{1,0:T(8,128)}, /*index=5*/f32[1,2048]{1,0:T(1,128)}) custom-call(bf16[128,2048]{1,0:T(8,128)(2,1)} %get-tuple-element.62.refs_0_, f32[16,2048]{1,0:T(8,128)} %get-tuple-element.63.refs_1_, ...), custom_call_target="tpu_custom_call", output_to_operand_aliasing={{0}: (0, {})} | custom-call | tf_op jit(solution)/shard_map/last_rows/pallas_call | solution.py:671
  174.7 0.0 collective-permute-done.17.refs_6_
  174.7 0.0 all-to-all-done.1
  174.8 0.0 reduce-scatter.5.cloned.1.call-done.refs_9_
  174.8 0.0 reduce-scatter.3.cloned.1.call-done.refs_8_
  174.8 0.7 copy-done.8
  175.5 0.2 copy-done.9
  175.7 0.1 copy-done.1
  175.8 4.5 %row_gradients.1 = (f32[128,2048]{1,0:T(8,128)}, f32[8,2048]{1,0:T(8,128)}, f32[128,2048]{1,0:T(8,128)}) custom-call(bf16[640,128]{1,0:T(8,128)(2,1)} %bitcast.17, bf16[128,2048]{1,0:T(8,128)(2,1)} %get-tuple-element.46.refs_5_.refs_4_.refs_1_, bf16[128,2048]{1,0:T(8,128)(2,1)} %copy-done.4, bf16[128,2048]{1,0:T(8,128)(2,1)} %copy-done.5, ...), custom_call_target="tpu_custom_call" | custom-call | tf_op jit(solution)/shard_map/row_gradients/pallas_call | solution.py:621
  (38 shorter events, 0.2 us)
Async XLA Ops:
  7.2 37.9 %copy-start.15 = (f32[16,2048]{1,0:T(8,128)S(1)}, f32[16,2048]{1,0:T(8,128)}, u32[]{:S(2)}) copy-start(f32[16,2048]{1,0:T(8,128)} %param.18) | copy-start | bytes 393220
  7.2 167.6 %reduce-scatter.5.cloned.1.call-start = ((), (), s32[]{:S(2)}) async-start(), calls=%async_computation.5 | async-start | bytes 1310720 | tf_op jit(solution)/shard_map/reduce_scatter | solution.py:768
  8.0 6.4 %collective-permute-start = (bf16[3,2048]{1,0:T(4,128)(2,1)S(1)}, bf16[3,2048]{1,0:T(4,128)(2,1)S(1)}, u32[]{:S(2)}, u32[]{:S(2)}) collective-permute-start(bf16[3,2048]{1,0:T(4,128)(2,1)S(1)} %slice.3), channel_id=1, source_target_pairs={{0,8},{8,16},{16,24},{1,9},{9,17},{17,25},{2,10},{10,18},{18,26},{... | collective-permute-start | bytes 36872 | tf_op jit(solution)/shard_map/ppermute | solution.py:58
  14.4 0.6 copy-start.16
  19.9 5.6 %collective-permute-start.1 = (bf16[128,544]{1,0:T(8,128)(2,1)}, bf16[128,544]{1,0:T(8,128)(2,1)S(1)}, u32[]{:S(2)}, u32[]{:S(2)}) collective-permute-start(bf16[128,544]{1,0:T(8,128)(2,1)} %get-tuple-element.45), channel_id=1, source_target_pairs={{0,1},{1,0},{2,3},{3,2},{4,5},{5,4},{6,7},{7,6},{8,9},{9,8},{10,11... | collective-permute-start | bytes 417800 | tf_op jit(solution)/shard_map/ppermute | solution.py:705
  19.9 18.5 %collective-permute-start.4 = (bf16[128,2048]{1,0:T(8,128)(2,1)}, bf16[128,2048]{1,0:T(8,128)(2,1)S(1)}, u32[]{:S(2)}, u32[]{:S(2)}) collective-permute-start(bf16[128,2048]{1,0:T(8,128)(2,1)} %get-tuple-element.46.refs_5_.refs_4_.refs_1_), channel_id=1, source_target_pairs={{0,8},{8,16},{16,24},{1,9},{9,17},{17,25},{2,10},{10,18},{18,26},{... | collective-permute-start | bytes 1572872 | tf_op jit(solution)/shard_map/ppermute | solution.py:58
  24.1 16.1 %collective-permute-start.5 = (bf16[128,2048]{1,0:T(8,128)(2,1)}, bf16[128,2048]{1,0:T(8,128)(2,1)S(1)}, u32[]{:S(2)}, u32[]{:S(2)}) collective-permute-start(bf16[128,2048]{1,0:T(8,128)(2,1)} %get-tuple-element.46.refs_5_.refs_4_.refs_1_), channel_id=1, source_target_pairs={{8,0},{16,8},{24,16},{9,1},{17,9},{25,17},{10,2},{18,10},{26,18},{... | collective-permute-start | bytes 1572872 | tf_op jit(solution)/shard_map/ppermute | solution.py:58
  26.4 6.4 %collective-permute-start.2 = (bf16[128,544]{1,0:T(8,128)(2,1)S(1)}, bf16[128,544]{1,0:T(8,128)(2,1)S(1)}, u32[]{:S(2)}, u32[]{:S(2)}) collective-permute-start(bf16[128,544]{1,0:T(8,128)(2,1)S(1)} %add_convert_fusion.4), channel_id=1, source_target_pairs={{0,2},{1,3},{2,0},{3,1},{4,6},{5,7},{6,4},{7,5},{8,10},{9,11},{10,... | collective-permute-start | bytes 417800 | tf_op jit(solution)/shard_map/ppermute | solution.py:705
  32.8 12.9 %copy-start.3 = (bf16[128,544]{1,0:T(8,128)(2,1)}, bf16[128,544]{1,0:T(8,128)(2,1)S(1)}, u32[]{:S(2)}) copy-start(bf16[128,544]{1,0:T(8,128)(2,1)S(1)} %add_convert_fusion.3.refs_0_) | copy-start | bytes 417796
  32.8 5.6 %collective-permute-start.3 = (bf16[128,544]{1,0:T(8,128)(2,1)S(1)}, bf16[128,544]{1,0:T(8,128)(2,1)S(1)}, u32[]{:S(2)}, u32[]{:S(2)}) collective-permute-start(bf16[128,544]{1,0:T(8,128)(2,1)S(1)} %add_convert_fusion.3.refs_0_), channel_id=1, source_target_pairs={{0,4},{1,5},{2,6},{3,7},{4,0},{5,1},{6,2},{7,3},{8,12},{9,13},{10,... | collective-permute-start | bytes 417800 | tf_op jit(solution)/shard_map/ppermute | solution.py:705
  38.4 7.4 %copy-start.11 = (bf16[128,544]{1,0:T(8,128)(2,1)}, bf16[128,544]{1,0:T(8,128)(2,1)S(1)}, u32[]{:S(2)}) copy-start(bf16[128,544]{1,0:T(8,128)(2,1)S(1)} %collective-permute-done.3.refs_1_) | copy-start | bytes 417796
  38.4 20.2 %copy-start.4 = (bf16[128,2048]{1,0:T(8,128)(2,1)}, bf16[128,2048]{1,0:T(8,128)(2,1)S(1)}, u32[]{:S(2)}) copy-start(bf16[128,2048]{1,0:T(8,128)(2,1)S(1)} %collective-permute-done.4.refs_2_) | copy-start | bytes 1572868
  40.2 18.4 %copy-start.5 = (bf16[128,2048]{1,0:T(8,128)(2,1)}, bf16[128,2048]{1,0:T(8,128)(2,1)S(1)}, u32[]{:S(2)}) copy-start(bf16[128,2048]{1,0:T(8,128)(2,1)S(1)} %collective-permute-done.5.refs_3_) | copy-start | bytes 1572868
  40.3 32.4 %collective-permute-start.6 = (bf16[128,2048]{1,0:T(8,128)(2,1)S(1)}, bf16[128,2048]{1,0:T(8,128)(2,1)S(1)}, u32[]{:S(2)}, u32[]{:S(2)}) collective-permute-start(bf16[128,2048]{1,0:T(8,128)(2,1)S(1)} %collective-permute-done.4.refs_2_), channel_id=1, source_target_pairs={{0,8},{8,16},{16,24},{1,9},{9,17},{17,25},{2,10},{10,18},{18,26},{... | collective-permute-start | bytes 1572872 | tf_op jit(solution)/shard_map/ppermute | solution.py:58
  43.7 28.9 %collective-permute-start.7 = (bf16[128,2048]{1,0:T(8,128)(2,1)S(1)}, bf16[128,2048]{1,0:T(8,128)(2,1)S(1)}, u32[]{:S(2)}, u32[]{:S(2)}) collective-permute-start(bf16[128,2048]{1,0:T(8,128)(2,1)S(1)} %collective-permute-done.5.refs_3_), channel_id=1, source_target_pairs={{8,0},{16,8},{24,16},{9,1},{17,9},{25,17},{10,2},{18,10},{26,18},{... | collective-permute-start | bytes 1572872 | tf_op jit(solution)/shard_map/ppermute | solution.py:58
  72.7 40.9 %copy-start.6 = (bf16[128,2048]{1,0:T(8,128)(2,1)}, bf16[128,2048]{1,0:T(8,128)(2,1)S(1)}, u32[]{:S(2)}) copy-start(bf16[128,2048]{1,0:T(8,128)(2,1)S(1)} %collective-permute-done.6.refs_4_) | copy-start | bytes 1572868
  72.7 43.3 %copy-start.7 = (bf16[128,2048]{1,0:T(8,128)(2,1)}, bf16[128,2048]{1,0:T(8,128)(2,1)S(1)}, u32[]{:S(2)}) copy-start(bf16[128,2048]{1,0:T(8,128)(2,1)S(1)} %collective-permute-done.7.refs_5_) | copy-start | bytes 1572868
  102.2 20.4 %copy-start.10 = (bf16[32,2048]{1,0:T(8,128)(2,1)S(1)}, bf16[32,2048]{1,0:T(8,128)(2,1)}, u32[]{:S(2)}) copy-start(bf16[32,2048]{1,0:T(8,128)(2,1)} %get-tuple-element.64.refs_3_) | copy-start | bytes 393220
  102.2 72.6 %reduce-scatter.3.cloned.1.call-start = ((), (), s32[]{:S(2)}) async-start(), calls=%async_computation.4 | async-start | bytes 1310720 | tf_op jit(solution)/shard_map/reduce_scatter | solution.py:768
  103.0 1.7 collective-permute-start.8
  105.6 6.3 %collective-permute-start.9 = (bf16[640,128]{1,0:T(8,128)(2,1)S(1)}, bf16[640,128]{1,0:T(8,128)(2,1)S(1)}, u32[]{:S(2)}, u32[]{:S(2)}) collective-permute-start(bf16[640,128]{1,0:T(8,128)(2,1)S(1)} %add_convert_fusion.2), channel_id=1, source_target_pairs={{0,2},{1,3},{2,0},{3,1},{4,6},{5,7},{6,4},{7,5},{8,10},{9,11},{10,... | collective-permute-start | bytes 491528 | tf_op jit(solution)/shard_map/ppermute | solution.py:705
  112.0 16.4 %copy-start = (bf16[640,128]{1,0:T(8,128)(2,1)}, bf16[640,128]{1,0:T(8,128)(2,1)S(1)}, u32[]{:S(2)}) copy-start(bf16[640,128]{1,0:T(8,128)(2,1)S(1)} %add_convert_fusion.1.back_a) | copy-start | bytes 491524
  112.0 5.6 %collective-permute-start.10 = (bf16[640,128]{1,0:T(8,128)(2,1)S(1)}, bf16[640,128]{1,0:T(8,128)(2,1)S(1)}, u32[]{:S(2)}, u32[]{:S(2)}) collective-permute-start(bf16[640,128]{1,0:T(8,128)(2,1)S(1)} %add_convert_fusion.1.back_a), channel_id=1, source_target_pairs={{0,4},{1,5},{2,6},{3,7},{4,0},{5,1},{6,2},{7,3},{8,12},{9,13},{10,... | collective-permute-start | bytes 491528 | tf_op jit(solution)/shard_map/ppermute | solution.py:705
  113.6 61.1 %collective-permute-start.17 = (bf16[128,2048]{1,0:T(8,128)(2,1)S(1)}, bf16[128,2048]{1,0:T(8,128)(2,1)S(1)}, u32[]{:S(2)}, u32[]{:S(2)}) collective-permute-start(bf16[128,2048]{1,0:T(8,128)(2,1)S(1)} %collective-permute-done.6.refs_4_), channel_id=1, source_target_pairs={{0,8},{8,16},{16,24},{1,9},{9,17},{17,25},{2,10},{10,18},{18,26},{... | collective-permute-start | bytes 1572872 | tf_op jit(solution)/shard_map/ppermute | solution.py:58
  116.0 58.7 %collective-permute-start.18 = (bf16[128,2048]{1,0:T(8,128)(2,1)S(1)}, bf16[128,2048]{1,0:T(8,128)(2,1)S(1)}, u32[]{:S(2)}, u32[]{:S(2)}) collective-permute-start(bf16[128,2048]{1,0:T(8,128)(2,1)S(1)} %collective-permute-done.7.refs_5_), channel_id=1, source_target_pairs={{8,0},{16,8},{24,16},{9,1},{17,9},{25,17},{10,2},{18,10},{26,18},{... | collective-permute-start | bytes 1572872 | tf_op jit(solution)/shard_map/ppermute | solution.py:58
  117.6 10.8 %copy-start.2 = (bf16[640,128]{1,0:T(8,128)(2,1)}, bf16[640,128]{1,0:T(8,128)(2,1)S(1)}, u32[]{:S(2)}) copy-start(bf16[640,128]{1,0:T(8,128)(2,1)S(1)} %collective-permute-done.10.back_b) | copy-start | bytes 491524
  118.3 56.4 %all-to-all-start.1 = ((bf16[4,160,128]{2,1,0:T(8,128)(2,1)}), bf16[4,160,128]{2,1,0:T(8,128)(2,1)S(1)}, u32[]{:S(2)}, u32[]{:S(2)}) async-start(bf16[4,160,128]{2,1,0:T(8,128)(2,1)} %bitcast.4), calls=%async_computation.1 | async-start | bytes 327680 | tf_op jit(solution)/shard_map/all_to_all | solution.py:701
  122.6 22.6 %collective-permute-start.11 = (bf16[32,2048]{1,0:T(8,128)(2,1)S(1)}, bf16[32,2048]{1,0:T(8,128)(2,1)S(1)}, u32[]{:S(2)}, u32[]{:S(2)}) collective-permute-start(bf16[32,2048]{1,0:T(8,128)(2,1)S(1)} %copy-done.10), channel_id=1, source_target_pairs={{0,8},{8,16},{16,24},{24,0},{1,9},{9,17},{17,25},{25,1},{2,10},{10... | collective-permute-start | bytes 393224 | tf_op jit(solution)/shard_map/ppermute | solution.py:52
  124.6 32.0 %collective-permute-start.12 = (bf16[32,2048]{1,0:T(8,128)(2,1)S(1)}, bf16[32,2048]{1,0:T(8,128)(2,1)S(1)}, u32[]{:S(2)}, u32[]{:S(2)}) collective-permute-start(bf16[32,2048]{1,0:T(8,128)(2,1)S(1)} %copy-done.10), channel_id=1, source_target_pairs={{0,16},{8,24},{16,0},{24,8},{1,17},{9,25},{17,1},{25,9},{2,18},{10... | collective-permute-start | bytes 393224 | tf_op jit(solution)/shard_map/ppermute | solution.py:52
  127.0 29.6 %collective-permute-start.13 = (bf16[32,2048]{1,0:T(8,128)(2,1)S(1)}, bf16[32,2048]{1,0:T(8,128)(2,1)S(1)}, u32[]{:S(2)}, u32[]{:S(2)}) collective-permute-start(bf16[32,2048]{1,0:T(8,128)(2,1)S(1)} %copy-done.10), channel_id=1, source_target_pairs={{0,24},{8,0},{16,8},{24,16},{1,25},{9,1},{17,9},{25,17},{2,26},{10... | collective-permute-start | bytes 393224 | tf_op jit(solution)/shard_map/ppermute | solution.py:52
  145.2 26.9 %copy-start.12 = (bf16[32,2048]{1,0:T(8,128)(2,1)}, bf16[32,2048]{1,0:T(8,128)(2,1)S(1)}, u32[]{:S(2)}) copy-start(bf16[32,2048]{1,0:T(8,128)(2,1)S(1)} %collective-permute-done.11.refs_4_) | copy-start | bytes 393220
  145.2 21.2 %collective-permute-start.14 = (bf16[16,2048]{1,0:T(8,128)(2,1)}, bf16[16,2048]{1,0:T(8,128)(2,1)S(1)}, u32[]{:S(2)}, u32[]{:S(2)}) collective-permute-start(bf16[16,2048]{1,0:T(8,128)(2,1)} %get-tuple-element.65.refs_7_), channel_id=1, source_target_pairs={{0,8},{8,16},{16,24},{24,0},{1,9},{9,17},{17,25},{25,1},{2,10},{10... | collective-permute-start | bytes 196616 | tf_op jit(solution)/shard_map/ppermute | solution.py:52
  156.6 15.5 %copy-start.13 = (bf16[32,2048]{1,0:T(8,128)(2,1)}, bf16[32,2048]{1,0:T(8,128)(2,1)S(1)}, u32[]{:S(2)}) copy-start(bf16[32,2048]{1,0:T(8,128)(2,1)S(1)} %collective-permute-done.12.refs_5_) | copy-start | bytes 393220
  156.6 15.5 %collective-permute-start.15 = (bf16[16,2048]{1,0:T(8,128)(2,1)}, bf16[16,2048]{1,0:T(8,128)(2,1)S(1)}, u32[]{:S(2)}, u32[]{:S(2)}) collective-permute-start(bf16[16,2048]{1,0:T(8,128)(2,1)} %get-tuple-element.65.refs_7_), channel_id=1, source_target_pairs={{0,16},{8,24},{16,0},{24,8},{1,17},{9,25},{17,1},{25,9},{2,18},{10... | collective-permute-start | bytes 196616 | tf_op jit(solution)/shard_map/ppermute | solution.py:52
  156.6 15.5 %copy-start.14 = (bf16[32,2048]{1,0:T(8,128)(2,1)}, bf16[32,2048]{1,0:T(8,128)(2,1)S(1)}, u32[]{:S(2)}) copy-start(bf16[32,2048]{1,0:T(8,128)(2,1)S(1)} %collective-permute-done.13.refs_6_) | copy-start | bytes 393220
  156.6 15.4 %collective-permute-start.16 = (bf16[16,2048]{1,0:T(8,128)(2,1)}, bf16[16,2048]{1,0:T(8,128)(2,1)S(1)}, u32[]{:S(2)}, u32[]{:S(2)}) collective-permute-start(bf16[16,2048]{1,0:T(8,128)(2,1)} %get-tuple-element.65.refs_7_), channel_id=1, source_target_pairs={{0,24},{8,0},{16,8},{24,16},{1,25},{9,1},{17,9},{25,17},{2,26},{10... | collective-permute-start | bytes 196616 | tf_op jit(solution)/shard_map/ppermute | solution.py:52
  166.3 5.7 %copy-start.17 = (bf16[16,2048]{1,0:T(8,128)(2,1)}, bf16[16,2048]{1,0:T(8,128)(2,1)S(1)}, u32[]{:S(2)}) copy-start(bf16[16,2048]{1,0:T(8,128)(2,1)S(1)} %collective-permute-done.14.refs_8_) | copy-start | bytes 196612
  172.1 0.6 copy-start.18
  172.1 0.7 copy-start.19
  174.7 0.8 copy-start.8
  174.7 1.0 copy-start.9
  174.7 1.0 copy-start.1
Sparse Core Ops, SparseCore 0:
  102.4 32.3 reduce-scatter.4
  137.7 36.0 reduce-scatter.2

commit v4 on v3

--- a/solution.py
+++ b/solution.py
@@ -131,8 +131,9 @@
 def local_kernel(low_rank, states, places, *refs):
     parts, refs = refs[:2], refs[2:]
     (weight_ref, bias_ref, decay_ref, conv_ref, gate_ref, grad_ref) = refs[:6]
-    (dt_ref, ends_ref, coef_ref, low) = refs[6:10]
-    (proj, coef_v, coef, dts, dxs, gs, fwd, bwd, sem) = refs[10:]
+    (dt_ref, coef_ref, low, low_t) = refs[6:10]
+    messages, refs = refs[10 : 9 + places], refs[9 + places :]
+    (proj, coef_v, coef, dts, dxs, gs, fwd, bwd, sem) = refs
     step = pl.program_id(0)
     chunks = dts.shape[0]
     rows = conv_ref.shape[0]
@@ -143,6 +144,7 @@
         total = (parts[0][...].astype(F32) + parts[1][...].astype(F32)).astype(BF)
         proj[...] = total.astype(F32)
         low[...] = total[:, :low_rank]
+        low_t[...] = jnp.transpose(proj[:, :low_rank]).astype(BF)
         coef_v[...] = jnp.zeros_like(coef_v)
         coef_v[:, : 2 * states] = proj[:, low_rank:]
         coef_ref[...] = coef_v[...]
@@ -211,8 +213,8 @@
                         target[v, states] = coarse
                         target[v, states + 1] = total[v] - coarse
         place = lax.axis_index("ctx")
-        for other in range(places):
-            ends_ref[other] = jnp.where(other > place, fwd[...], bwd[...]).astype(BF)
+        for mask, message in enumerate(messages, 1):
+            message[...] = jnp.where((place ^ mask) > place, fwd[...], bwd[...]).astype(BF)
 
 
 def local_call(parts, step_weight, step_bias, decay, conv_out, gate, grad, states, places):
@@ -238,16 +240,18 @@
         ],
         out_specs=[
             pl.BlockSpec((1, rows * groups, 128), lambda i: (i, 0, 0)),
-            whole((places,) + message),
             whole((rows, 128)),
             whole((rows, low_rank)),
-        ],
+            whole((low_rank, rows)),
+        ]
+        + [whole(message)] * (places - 1),
         out_shape=[
             sds((chunks, rows * groups, 128), F32),
-            sds((places,) + message, BF),
             sds((rows, 128), F32),
             sds((rows, low_rank), BF),
-        ],
+            sds((low_rank, rows), BF),
+        ]
+        + [sds(message, BF)] * (places - 1),
         scratch_shapes=[
             pltpu.VMEM((rows, wide), F32),
             pltpu.VMEM((rows, 128), F32),
@@ -287,13 +291,13 @@
 
 
 def scan_kernel(places, states, opening, *refs):
-    (coef, low_ref, dt_ref, decay_ref, conv_ref, gate_ref, grad_ref, weight_ref, skip_ref) = refs[:9]
-    ends, refs = refs[9], refs[10:]
+    (coef, dt_ref, decay_ref, conv_ref, gate_ref, grad_ref, weight_ref, skip_ref) = refs[:8]
+    messages, refs = refs[8 : 7 + places], refs[7 + places :]
     if not opening:
         before_ref, refs = refs[0], refs[4:]
-    (pre_ref, gate_out, scan_out, small_ref, prod_ref, part_ref) = refs[:6]
-    refs = refs[6:]
-    (xs, dxs, gs, ys, dds, qs, decayed, coef_out, coef_in, rate, decay_acc, acc, small) = refs
+    (pre_ref, gate_out, scan_out, small_ref, part_ref) = refs[:5]
+    refs = refs[5:]
+    (xs, dxs, gs, ys, dds, qs, decayed, coef_out, coef_in, rate, decay_acc, acc, ends) = refs
     rows = conv_ref.shape[0]
     groups = decay_ref.shape[2]
     low_rank = weight_ref.shape[0]
@@ -316,18 +320,19 @@
     place = lax.axis_index("ctx")
     for n in range(states):
         rate[n] = -LOG2E * jnp.exp(decay_ref[0, n])
-    totals = [
-        ends[q, 0, states].astype(F32) + ends[q, 0, states + 1].astype(F32) for q in range(places)
-    ]
+    ends[place] = jnp.zeros(ends.shape[1:], F32)
+    for mask, message in enumerate(messages, 1):
+        ends[place ^ mask] = message[0].astype(F32)
+    totals = [ends[q, states] + ends[q, states + 1] for q in range(places)]
     state, carry = [], []
     for n in range(states):
         before = jnp.zeros((groups, 128), F32)
         after = jnp.zeros((groups, 128), F32)
         for q in range(places - 1):
-            reached = jnp.exp2(rate[n] * totals[q]) * before + ends[q, 0, n].astype(F32)
+            reached = jnp.exp2(rate[n] * totals[q]) * before + ends[q, n]
             before = jnp.where(q < place, reached, before)
         for q in range(places - 1, 0, -1):
-            reached = jnp.exp2(rate[n] * totals[q]) * after + ends[q, 0, n].astype(F32)
+            reached = jnp.exp2(rate[n] * totals[q]) * after + ends[q, n]
             after = jnp.where(q > place, reached, after)
         state.append(before)
         carry.append(after)
@@ -386,11 +391,10 @@
     for n in range(states):
         decay_acc[n * groups : n * groups + groups, :] = gathered[n] * (rate[n] * LN2)
 
-    small[...] = jnp.zeros_like(small)
     for group in range(groups):
-        small[:states, group * 128 : group * 128 + 128] = decay_acc[
+        pre_ref[rows : rows + states, group * 128 : group * 128 + 128] = decay_acc[
             pl.ds(group, states, stride=groups), :
-        ]
+        ].astype(BF)
     skip = skip_ref[...]
     bias_sum = jnp.zeros((1, conv_ref.shape[1]), F32)
     skip_sum = jnp.zeros((1, conv_ref.shape[1]), F32)
@@ -431,12 +435,11 @@
         gate_out[here, :] = (
             grad * (out + skip * conv) * (sig * (1.0 + gate * (1.0 - sig)))
         ).astype(BF)
-    small[states : states + 1, :] = bias_sum
-    small[states + 1 : states + 2, :] = skip_sum
-    small_ref[...] = small[...].astype(BF)
-
-    pre_bf = pre_ref[...]
-    prod_ref[...] = dot(low_ref[...], pre_bf, TN).astype(BF)
+    small_ref[...] = jnp.concatenate(
+        [bias_sum, skip_sum, jnp.zeros((6, bias_sum.shape[1]), F32)], axis=0
+    )
+
+    pre_bf = pre_ref[:rows, :]
     lanes = lax.broadcasted_iota(jnp.int32, (2 * states, 128), 0)
     coefs = jnp.zeros((2 * states, rows), F32)
     for n in range(states):
@@ -463,7 +466,7 @@
 
 
 def scan_call(
-    places, chunk, coef, low, dt, decay, conv_out, gate, grad, step_weight, skip, ends, previous
+    places, chunk, coef, dt, decay, conv_out, gate, grad, step_weight, skip, messages, previous
 ):
     rows, chans = conv_out.shape
     low_rank = step_weight.shape[0]
@@ -476,7 +479,6 @@
     first, last = chunk == 0, chunk == chunks - 1
     in_specs = [
         pl.BlockSpec(memory_space=pltpu.SMEM),
-        whole((rows, low_rank)),
         lead(rows * groups, 128),
         lead(states, groups, 128),
         here(rows),
@@ -484,30 +486,28 @@
         here(rows),
         here(low_rank),
         here(1),
-        pl.BlockSpec((places, 1, states + 2, groups, 128), lambda i: (0, chunk, 0, 0, 0)),
     ]
+    in_specs += [lead(states + 2, groups, 128)] * (places - 1)
     aliases = {}
     if not first:
         in_specs += [whole((wide, rows))] + [pl.BlockSpec(memory_space=pl.ANY)] * 3
-        aliases = {11: 1, 12: 2, 13: 3}
+        aliases = {8 + places: 1, 9 + places: 2, 10 + places: 3}
     return pl.pallas_call(
         functools.partial(scan_kernel, places, states, first),
         grid=(1,),
         in_specs=in_specs,
         out_specs=[
-            whole((rows, width)),
+            whole((rows + states, width)),
             here(rows),
             here(rows),
-            here(32),
-            whole((low_rank, width)),
+            here(8),
             whole((wide, rows)),
         ],
         out_shape=[
-            sds((rows, width), BF),
+            sds((rows + states, width), BF),
             sds((rows, chans), BF),
             sds((rows, chans), BF),
-            sds((32, chans), BF),
-            sds((low_rank, width), BF),
+            sds((8, chans), F32),
             sds((wide, rows), BF if last else F32),
         ],
         scratch_shapes=[
@@ -523,15 +523,15 @@
             pltpu.VMEM((states, groups, 128), F32),
             pltpu.VMEM((states * groups, 128), F32),
             pltpu.VMEM((wide, rows), F32),
-            pltpu.VMEM((32, width), F32),
+            pltpu.VMEM((places, states + 2, groups, 128), F32),
         ],
         input_output_aliases=aliases,
         compiler_params=params(),
         name="scan_gradients",
-    )(coef, low, dt, decay, conv_out, gate, grad, step_weight, skip, ends, *previous)
-
-
-def conv_grad_kernel(places, low_rank, back_a, back_b, proj_ref, scan_ref, input_ref, rim_ref, weight_ref, bias_ref,
+    )(coef, dt, decay, conv_out, gate, grad, step_weight, skip, *messages, *previous)
+
+
+def conv_grad_kernel(places, low_rank, back_a, back_b, proj_ref, scan_ref, small_in, input_ref, rim_ref, weight_ref, bias_ref,
                      out_ref, tail_ref, small_ref, ext, grad):
     taps = weight_ref.shape[0]
     rows = input_ref.shape[0]
@@ -563,11 +563,11 @@
         out_ref[start : start + 16, :] = total.astype(BF)
     tail_ref[...] = total
     small_ref[...] = jnp.concatenate(
-        sums + [jnp.zeros((8 - taps - 1, small_ref.shape[1]), F32), grad[0:8, :]], axis=0
+        sums + [small_in[0 : 7 - taps, :], grad[0:8, :]], axis=0
     ).astype(BF)
 
 
-def conv_grad_call(places, low_rank, backs, proj_weight, scan_part, conv_input, rim, weight, bias):
+def conv_grad_call(places, low_rank, backs, proj_weight, scan_part, small, conv_input, rim, weight, bias):
     rows, chans = conv_input.shape
     taps = weight.shape[0]
     wide = proj_weight.shape[0]
@@ -580,6 +580,7 @@
             whole(backs[1].shape),
             columns(wide, width),
             columns(rows, width),
+            columns(8, width),
             columns(rows, width),
             columns(taps - 1, width),
             columns(taps, width),
@@ -590,56 +591,58 @@
         scratch_shapes=[pltpu.VMEM((rows + 8, width), F32), pltpu.VMEM((rows + 8, width), F32)],
         compiler_params=params(),
         name="conv_gradients",
-    )(*backs, proj_weight, scan_part, conv_input, rim, weight, bias)
+    )(*backs, proj_weight, scan_part, small, conv_input, rim, weight, bias)
 
 
 def rows_kernel(places, rank_rows, chunks, *refs):
     cut_ref, refs = refs[0], refs[1:]
-    blocks, refs = refs[: 2 * places - 1], refs[2 * places - 1 :]
-    steps, (out_ref, coef_ref, step_out) = refs[:chunks], refs[chunks:]
+    blocks, refs = refs[:places], refs[places:]
+    steps, refs = refs[: chunks * places], refs[chunks * places :]
+    out_ref, coef_ref, step_ref, decay_ref = refs
     place = lax.axis_index("ctx")
-    block = cut_ref.shape[0] // places
-    total = None
-    for hop, ref in zip([0] + [k for d in range(1, places) for k in (d, -d)], blocks):
-        source = lax.rem(place + places - hop, places)
-        cut = cut_ref[pl.ds(pl.multiple_of(source * block, 16 if block % 16 == 0 else 8), block), :]
-        part = dot(cut, ref[...])
-        total = part if total is None else total + part
+    rows = blocks[0].shape[0]
+    back_rows = cut_ref.shape[1] - rank_rows
+    total = jnp.zeros((back_rows, out_ref.shape[1]), F32)
+    for mask in range(places):
+        total = total + dot(cut_ref[place ^ mask, :back_rows, :], blocks[mask][...])
     out_ref[...] = total[:rank_rows, :]
     coef_ref[...] = total[rank_rows : rank_rows + coef_ref.shape[0], :]
     for chunk in range(chunks):
 
         @pl.when(pl.program_id(0) == chunk)
         def _():
-            step_out[...] = steps[chunk][...].astype(F32)
-
-
-def rows_call(places, cuts, blocks, steps, coef_rows):
+            total = jnp.zeros(step_ref.shape, F32)
+            decay = jnp.zeros(decay_ref.shape, F32)
+            for mask in range(places):
+                step = steps[chunk * places + mask]
+                total = total + dot(cut_ref[place ^ mask, back_rows:, :], step[:rows, :])
+                decay = decay + step[rows:, :].astype(F32)
+            step_ref[...] = total
+            decay_ref[...] = decay
+
+
+def rows_call(places, rank_rows, coef_rows, cuts, blocks, steps):
     rows, chans = blocks[0].shape
-    rank_rows, width = steps[0].shape
-    chunks = len(steps)
+    chunks = len(steps) // places
+    tall, width = steps[0].shape
+    heights = (rank_rows, coef_rows, rank_rows, tall - rows)
     return pl.pallas_call(
         functools.partial(rows_kernel, places, rank_rows, chunks),
         grid=(chunks,),
         in_specs=[whole(cuts.shape)]
-        + [columns(rows, width)] * len(blocks)
-        + [whole((rank_rows, width))] * chunks,
-        out_specs=[
-            columns(rank_rows, width), columns(coef_rows, width), columns(rank_rows, width)
-        ],
-        out_shape=[
-            sds((rank_rows, chans), F32), sds((coef_rows, chans), F32), sds((rank_rows, chans), F32)
-        ],
+        + [columns(rows, width)] * places
+        + [whole((tall, width))] * (chunks * places),
+        out_specs=[columns(height, width) for height in heights],
+        out_shape=[sds((height, chans), F32) for height in heights],
         compiler_params=params(),
         name="row_gradients",
     )(cuts, *blocks, *steps)
 
 
-def last_kernel(places, states, taps, *refs):
+def last_kernel(places, taps, *refs):
     (_, tail_ref, weight_ref) = refs[:3]
-    early, refs = refs[3 : 3 + places], refs[3 + places :]
-    late, refs = refs[:places], refs[places:]
-    (out_ref, conv_w, conv_b, step_b, decay, skip, fix) = refs
+    late, refs = refs[3 : 3 + places], refs[3 + places :]
+    (out_ref, conv_w, conv_b, step_b, skip, fix) = refs
     fix[...] = tail_ref[...]
     inside = lax.axis_index("ctx") < places - 1
     following = jnp.where(inside, late[places - 1][8:16, :].astype(F32), 0.0)
@@ -650,51 +653,35 @@
         at = 16 - (taps - 1) + row
         fix[at : at + 1, :] += extra
     out_ref[...] = fix[...].astype(BF)
-    total = early[0][...].astype(F32)
-    for part in early[1:]:
-        total = total + part[...].astype(F32)
-    decay[...] = total[:states, :]
-    step_b[...] = total[states : states + 1, :]
-    skip[...] = total[states + 1 : states + 2, :]
     total = late[0][...].astype(F32)
     for part in late[1:]:
         total = total + part[...].astype(F32)
     conv_w[...] = total[:taps, :]
     conv_b[...] = total[taps : taps + 1, :]
-
-
-def last_call(main, tail, weight, early, late, states):
+    step_b[...] = total[taps + 1 : taps + 2, :]
+    skip[...] = total[taps + 2 : taps + 3, :]
+
+
+def last_call(main, tail, weight, late):
     rows, chans = main.shape
     taps = weight.shape[0]
-    places = len(early)
-    width = chans
+    places = len(late)
     return pl.pallas_call(
-        functools.partial(last_kernel, places, states, taps),
+        functools.partial(last_kernel, places, taps),
         grid=(1,),
-        in_specs=[pl.BlockSpec(memory_space=pl.ANY), columns(16, width), columns(taps, width)]
-        + [columns(32, width)] * places
-        + [columns(16, width)] * places,
+        in_specs=[pl.BlockSpec(memory_space=pl.ANY), columns(16, chans), columns(taps, chans)]
+        + [columns(16, chans)] * places,
         out_specs=[
-            pl.BlockSpec((16, width), lambda i: (rows // 16 - 1, i)),
-            columns(taps, width),
-            columns(1, width),
-            columns(1, width),
-            columns(states, width),
-            columns(1, width),
-        ],
-        out_shape=[
-            sds((rows, chans), BF),
-            sds((taps, chans), F32),
-            sds((1, chans), F32),
-            sds((1, chans), F32),
-            sds((states, chans), F32),
-            sds((1, chans), F32),
-        ],
-        scratch_shapes=[pltpu.VMEM((16, width), F32)],
+            pl.BlockSpec((16, chans), lambda i: (rows // 16 - 1, i)),
+            columns(taps, chans),
+        ]
+        + [columns(1, chans)] * 3,
+        out_shape=[sds((rows, chans), BF), sds((taps, chans), F32)] + [sds((1, chans), F32)] * 3,
+        scratch_shapes=[pltpu.VMEM((16, chans), F32)],
         input_output_aliases={0: 0},
         compiler_params=params(),
         name="last_rows",
-    )(main, tail, weight, *early, *late)
+    )(main, tail, weight, *late)
 
 
 def exchange(block, axis):
@@ -741,43 +728,40 @@
     chunks = decay.shape[0]
     rim = shift(conv_input[rows - (taps - 1) :], "ctx", 1)
     conv_out, part = conv_call(conv_input, rim, conv_weight, conv_bias, proj_weight)
-    blocks = [conv_out]
-    right, left = shift(conv_out, "ctx", 1), shift(conv_out, "ctx", -1)
-    blocks += [right, left]
+    blocks = [conv_out] + [swap(conv_out, "ctx", mask) for mask in range(1, min(places, 3))]
     parts = chan_sum(part)
-    for hop in range(2, places):
-        if hop == 2:
-            parts, right, left = lax.optimization_barrier((parts, right, left))
-            right, left = shift(right, "ctx", 1), shift(left, "ctx", -1)
-            blocks += [right, left]
-    dt, ends, coef, low = local_call(
+    dt, coef, low, low_t, *messages = local_call(
         parts, step_weight, step_bias, decay, conv_out, gate_input, out_grad, states, places
     )
-    ends = exchange(ends, "ctx")
-    for hop in range(3, places):
-        ends, right, left = lax.optimization_barrier((ends, right, left))
-        right, left = shift(right, "ctx", 1), shift(left, "ctx", -1)
-        blocks += [right, left]
+    messages = [swap(message, "ctx", mask) for mask, message in enumerate(messages, 1)]
+    messages, held = lax.optimization_barrier((messages, conv_out))
+    blocks += [swap(held, "ctx", mask) for mask in range(3, places)]
     previous, steps = [], []
     for chunk in range(chunks):
-        pre_bf, grad_gate, scan_part, small, products, part = scan_call(
-            places, chunk, coef, low, dt, decay, conv_out, gate_input, out_grad, step_weight,
-            skip_gain, ends, previous,
+        pre_bf, grad_gate, scan_part, small, part = scan_call(
+            places, chunk, coef, dt, decay, conv_out, gate_input, out_grad, step_weight,
+            skip_gain, messages, previous,
         )
         previous = [part, grad_gate, scan_part, small]
-        steps.append(lax.psum_scatter(products, "ctx", scatter_dimension=0, tiled=True))
-    early = [small] + [rotate(small, "ctx", hop) for hop in range(1, places)]
+        steps += [pre_bf] + [swap(pre_bf, "ctx", mask) for mask in range(1, places)]
     backs = chan_sum(part)
-    back = (backs[0].astype(F32) + backs[1].astype(F32)).astype(BF)
-    cuts = exchange(back, "ctx")
+    cuts = jnp.concatenate(
+        [
+            (backs[0].astype(F32) + backs[1].astype(F32)).astype(BF).reshape(places, -1, rows),
+            low_t.reshape(places, -1, rows),
+        ],
+        axis=1,
+    )
+    cuts = exchange(cuts, "ctx")
     main, tail, sums = conv_grad_call(
-        places, low_rank, backs, proj_weight, scan_part, conv_input, rim, conv_weight, conv_bias
+        places, low_rank, backs, proj_weight, scan_part, small, conv_input, rim, conv_weight,
+        conv_bias,
     )
     late = [sums] + [rotate(sums, "ctx", hop) for hop in range(1, places)]
-    grad_proj, grad_coef, grad_step = rows_call(places, cuts, blocks, steps, 2 * states // places)
-    grad_input, conv_w, conv_b, step_b, decay_grad, skip = last_call(
-        main, tail, conv_weight, early, late, states
+    grad_proj, grad_coef, grad_step, decay_grad = rows_call(
+        places, low_rank // places, 2 * states // places, cuts, blocks, steps
     )
+    grad_input, conv_w, conv_b, step_b, skip = last_call(main, tail, conv_weight, late)
     return (
         grad_input,
         grad_gate,

time: 188 us -> 211 us (1.12)
  waiting for transfers between devices: 40.8 us -> 74.6 us
  starting transfers between devices: 51 us -> 66 us
  blocking collectives: 14 us -> 0 us
  between operations: 14.4 us -> 0.85 us
  local copies, waits for them, and re-layouts: 3.73 us -> 6.34 us
    ppermute x6 -> x18, waiting for transfers between devices: 15.4 us -> 53 us  [swap(): lax.ppermute(block, axis, [(i, i ^ mask) for i in range(lax.axis_size(axi...]
    ppermute x6 -> x18, starting transfers between devices: 6.35 us -> 22.4 us  [swap(): lax.ppermute(block, axis, [(i, i ^ mask) for i in range(lax.axis_size(axi...]
    all_to_all x1 -> x0, blocking collectives: 14 us -> none  [exchange(): return lax.all_to_all(block, axis, split_axis=0, concat_axis=0, tiled=True)]
    ppermute x7 -> x1, starting transfers between devices: 18.9 us -> 4.93 us  [shift(): return lax.ppermute(block, axis, route)]
    ppermute x6 -> x3, starting transfers between devices: 21.4 us -> 34.8 us  [rotate(): lax.ppermute(block, axis, [(i, (i + distance) % count) for i in range(cou...]
    unnamed x41 -> x49, local copies, waits for them, and re-layouts: 2.26 us -> 4.87 us
    ppermute x6 -> x3, waiting for transfers between devices: 21.3 us -> 20.1 us  [rotate(): lax.ppermute(block, axis, [(i, (i + distance) % count) for i in range(cou...]
  transfers between devices with their start and end apart: 22 -> 23, of which waited for: 10 -> 13; matrix products, arithmetic and copies ran while one was open for 2% -> 1% of each run, Pallas kernels for 12% -> 4%
where the time goes in v4:
time: 211 us; the launch traced here: 210 us
  waiting for transfers between devices  74.6 us (35%)
  starting transfers between devices  66 us (31%)
  Pallas kernels  59.5 us (28%)
  local copies, waits for them, and re-layouts  6.34 us (3%)
  other arithmetic  2.8 us (1%)
    ppermute x18, waiting for transfers between devices, swap(): lax.ppermute(block, axis, [(i, i ^ mask) for i in range(lax.axis_size(axi...  53 us
    ppermute x3, starting transfers between devices, rotate(): lax.ppermute(block, axis, [(i, (i + distance) % count) for i in range(cou...  34.8 us
    pallas_call x2, Pallas kernels, scan_call(): pl.pallas_call(functools.partial(scan_kernel, places, states, first), gri...  28.4 us
    ppermute x18, starting transfers between devices, swap(): lax.ppermute(block, axis, [(i, i ^ mask) for i in range(lax.axis_size(axi...  22.4 us
    ppermute x3, waiting for transfers between devices, rotate(): lax.ppermute(block, axis, [(i, (i + distance) % count) for i in range(cou...  20.1 us
    pallas_call x1, Pallas kernels, local_call(): pl.pallas_call(functools.partial(local_kernel, low_rank, states, places),...  12.8 us
    pallas_call x1, Pallas kernels, conv_grad_call(): pl.pallas_call(functools.partial(conv_grad_kernel, places, low_rank), gri...  6.8 us
    pallas_call x1, Pallas kernels, rows_call(): pl.pallas_call(functools.partial(rows_kernel, places, rank_rows, chunks),...  4.97 us
  transfers between devices with their start and end apart: 23, of which 13 were waited for; matrix products, arithmetic and copies ran while one was open for 1% of the time, Pallas kernels for 4%

profile of v4, /device:TPU:0, one launch (start us, length us, event | category | flops | bytes accessed | tf_op | source)
XLA Modules:
  0.0 210.1 jit_solution(5212349430687225085)
XLA Ops:
  0.7 0.8 slice.3
  1.5 4.9 %collective-permute-start = (bf16[3,2048]{1,0:T(4,128)(2,1)S(1)}, bf16[3,2048]{1,0:T(4,128)(2,1)S(1)}, u32[]{:S(2)}, u32[]{:S(2)}) collective-permute-start(bf16[3,2048]{1,0:T(4,128)(2,1)S(1)} %slice.3), channel_id=1, source_target_pairs={{0,8},{8,16},{16,24},{1,9},{9,17},{17,25},{2,10},{10,18},{18,26},{... | collective-permute-start | bytes 36872 | tf_op jit(solution)/shard_map/ppermute | solution.py:58
  6.4 1.4 collective-permute-done.rim_ref
  7.8 0.6 copy-done.20
  8.4 4.9 %conv_project.1 = (bf16[128,2048]{1,0:T(8,128)(2,1)}, bf16[128,544]{1,0:T(8,128)(2,1)}) custom-call(bf16[128,2048]{1,0:T(8,128)(2,1)} %input_ref.3, bf16[3,2048]{1,0:T(4,128)(2,1)} %copy-done.20, f32[4,2048]{1,0:T(4,128)} %refs_2_.3, f32[1,2048]{1,0:T(1,128)} %bitcast.23, bf16[544,2048]{1,0:T(8,128)(2,1)} %proj_ref.3), custom_call_target="tpu_custom_call" | custom-call | tf_op jit(solution)/shard_map/conv_project/pallas_call | solution.py:103
  13.3 0.0 collective-permute-start.1
  13.3 1.6 collective-permute-done.1
  14.9 1.0 add_convert_fusion.4
  15.9 1.6 collective-permute-start.2
  17.4 4.8 %collective-permute-done.2 = bf16[128,544]{1,0:T(8,128)(2,1)S(1)} collective-permute-done((bf16[128,544]{1,0:T(8,128)(2,1)S(1)}, bf16[128,544]{1,0:T(8,128)(2,1)S(1)}, u32[]{:S(2)}, u32[]{:S(2)}) %collective-permute-start.2) | collective-permute-done | bytes 139296 | tf_op jit(solution)/shard_map/ppermute | solution.py:692
  22.2 0.0 copy-start.4
  22.2 1.6 collective-permute-start.3
  23.8 0.7 copy.27
  24.5 3.2 %collective-permute-done.3.refs_1_ = bf16[128,544]{1,0:T(8,128)(2,1)S(1)} collective-permute-done((bf16[128,544]{1,0:T(8,128)(2,1)S(1)}, bf16[128,544]{1,0:T(8,128)(2,1)S(1)}, u32[]{:S(2)}, u32[]{:S(2)}) %collective-permute-start.3) | collective-permute-done | bytes 139296 | tf_op jit(solution)/shard_map/ppermute | solution.py:692
  27.7 0.7 copy-done.17
  28.4 12.8 %local_ends.1 = (f32[2,1024,128]{2,1,0:T(8,128)}, f32[128,128]{1,0:T(8,128)}, bf16[128,512]{1,0:T(8,128)(2,1)}, bf16[512,128]{1,0:T(8,128)(2,1)}, bf16[2,18,8,12...) custom-call(bf16[128,544]{1,0:T(8,128)(2,1)} %copy-done.4, ...), custom_call_target="tpu_custom_call" | custom-call | tf_op jit(solution)/shard_map/local_ends/pallas_call | solution.py:228
  41.2 2.4 %collective-permute-start.4 = (bf16[2,18,8,128]{3,2,1,0:T(8,128)(2,1)}, bf16[2,18,8,128]{3,2,1,0:T(8,128)(2,1)S(1)}, u32[]{:S(2)}, u32[]{:S(2)}) collective-permute-start(bf16[2,18,8,128]{3,2,1,0:T(8,128)(2,1)} %get-tuple-element.48), channel_id=1, source_target_pairs={{0,8},{8,0},{16,24},{24,16},{1,9},{9,1},{17,25},{25,17},{2,10},{10... | collective-permute-start | bytes 221192 | tf_op jit(solution)/shard_map/ppermute | solution.py:692
  43.6 2.6 %collective-permute-start.5 = (bf16[2,18,8,128]{3,2,1,0:T(8,128)(2,1)}, bf16[2,18,8,128]{3,2,1,0:T(8,128)(2,1)S(1)}, u32[]{:S(2)}, u32[]{:S(2)}) collective-permute-start(bf16[2,18,8,128]{3,2,1,0:T(8,128)(2,1)} %get-tuple-element.49), channel_id=1, source_target_pairs={{0,16},{8,24},{16,0},{24,8},{1,17},{9,25},{17,1},{25,9},{2,18},{10... | collective-permute-start | bytes 221192 | tf_op jit(solution)/shard_map/ppermute | solution.py:692
  46.2 0.0 collective-permute-start.6
  46.2 0.7 collective-permute-done.4.refs_8_
  46.8 3.8 %collective-permute-done.5.refs_9_ = bf16[2,18,8,128]{3,2,1,0:T(8,128)(2,1)S(1)} collective-permute-done((bf16[2,18,8,128]{3,2,1,0:T(8,128)(2,1)}, bf16[2,18,8,128]{3,2,1,0:T(8,128)(2,1)S(1)}, u32[]{:S(2)}, u32[]{:S(2)}) %collective-permute-start.5) | collective-permute-done | bytes 73760 | tf_op jit(solution)/shard_map/ppermute | solution.py:692
  50.6 1.9 collective-permute-done.6.refs_10_
  52.5 0.6 copy-done.16
  53.2 14.2 %scan_gradients.2 = (bf16[144,1024]{1,0:T(8,128)(2,1)}, bf16[128,2048]{1,0:T(8,128)(2,1)}, bf16[128,2048]{1,0:T(8,128)(2,1)}, f32[8,2048]{1,0:T(8,128)}, f32[640,128]{1,0:T(8,128)}) custom-call(f32[128,128]{1,0:T(8,128)} %get-tuple-element.46.refs_0_, f32[2,1024,128]{2,1,0:T(8,128)} %get-tuple-element.47.refs_1_, f32[2,16,8,128]{3,2,1,0:T(8,128)} %bitcast.15, ...), custom_call_target="tpu_custom_call" | custom-call | tf_op jit(solution)/shard_map/scan_gradients/pallas_call | solution.py:495
  67.3 14.2 %scan_gradients.3 = (bf16[144,1024]{1,0:T(8,128)(2,1)}, bf16[128,2048]{1,0:T(8,128)(2,1)}, bf16[128,2048]{1,0:T(8,128)(2,1)}, f32[8,2048]{1,0:T(8,128)}, bf16[640,128]{1,0:T(8,128)(2,1)}) custom-call(f32[128,128]{1,0:T(8,128)} %get-tuple-element.46.refs_0_, ...), custom_call_target="tpu_custom_call", output_to_operand_aliasing={{1}: (12, {}), {2}: (13, {}), {3}: (14, {})} | custom-call | tf_op jit(solution)/shard_map/scan_gradients/pallas_call | solution.py:495
  81.5 0.0 collective-permute-start.7
  81.5 1.6 collective-permute-done.7
  83.1 1.0 add_convert_fusion.2
  84.1 1.6 collective-permute-start.8
  85.7 4.8 %collective-permute-done.8 = bf16[640,128]{1,0:T(8,128)(2,1)S(1)} collective-permute-done((bf16[640,128]{1,0:T(8,128)(2,1)S(1)}, bf16[640,128]{1,0:T(8,128)(2,1)S(1)}, u32[]{:S(2)}, u32[]{:S(2)}) %collective-permute-start.8) | collective-permute-done | bytes 163872 | tf_op jit(solution)/shard_map/ppermute | solution.py:692
  90.5 1.6 collective-permute-start.9
  92.1 1.0 collective-permute-start.14
  93.1 0.7 collective-permute-start.13
  93.8 2.7 %collective-permute-start.21 = (bf16[144,1024]{1,0:T(8,128)(2,1)}, bf16[144,1024]{1,0:T(8,128)(2,1)}, u32[]{:S(2)}, u32[]{:S(2)}) collective-permute-start(bf16[144,1024]{1,0:T(8,128)(2,1)} %get-tuple-element.69.refs_9_), channel_id=1, source_target_pairs={{0,24},{8,16},{16,8},{24,0},{1,25},{9,17},{17,9},{25,1},{2,26},{10... | collective-permute-start | bytes 884744 | tf_op jit(solution)/shard_map/ppermute | solution.py:692
  96.5 0.1 collective-permute-start.20
  96.5 0.0 collective-permute-done.9.back_b
  96.6 1.4 collective-permute-start.15
  98.0 0.7 pad_maximum_fusion
  98.7 3.8 %all-to-all-start = ((bf16[4,288,128]{2,1,0:T(8,128)(2,1)}), bf16[4,288,128]{2,1,0:T(8,128)(2,1)S(1)}, u32[]{:S(2)}, u32[]{:S(2)}) async-start(bf16[4,288,128]{2,1,0:T(8,128)(2,1)} %pad_maximum_fusion), calls=%async_computation | async-start | bytes 589824 | tf_op jit(solution)/shard_map/all_to_all | solution.py:688
  102.6 6.8 %conv_gradients.1 = (bf16[128,2048]{1,0:T(8,128)(2,1)}, f32[16,2048]{1,0:T(8,128)}, bf16[16,2048]{1,0:T(8,128)(2,1)}) custom-call(bf16[640,128]{1,0:T(8,128)(2,1)} %copy-done.1, bf16[640,128]{1,0:T(8,128)(2,1)} %copy-done.3, bf16[544,2048]{1,0:T(8,128)(2,1)} %proj_ref.3, bf16[128,2048]{1,0:T(8,128)(2,1)} %get-tuple-element.59.scan_ref, ...), custom_call_target="tpu_custom_call" | custom-call | tf_op jit(solution)/shard_map/conv_gradients/pallas_call | solution.py:575
  109.4 8.7 %collective-permute-done.14.refs_3_ = bf16[128,2048]{1,0:T(8,128)(2,1)S(1)} collective-permute-done((bf16[128,2048]{1,0:T(8,128)(2,1)S(1)}, bf16[128,2048]{1,0:T(8,128)(2,1)S(1)}, u32[]{:S(2)}, u32[]{:S(2)}) %collective-permute-start.14) | collective-permute-done | bytes 524320 | tf_op jit(solution)/shard_map/ppermute | solution.py:692
  118.1 23.1 %collective-permute-start.12 = (bf16[16,2048]{1,0:T(8,128)(2,1)}, bf16[16,2048]{1,0:T(8,128)(2,1)S(1)}, u32[]{:S(2)}, u32[]{:S(2)}) collective-permute-start(bf16[16,2048]{1,0:T(8,128)(2,1)} %get-tuple-element.63.refs_3_), channel_id=1, source_target_pairs={{0,24},{8,0},{16,8},{24,16},{1,25},{9,1},{17,9},{25,17},{2,26},{10... | collective-permute-start | bytes 196616 | tf_op jit(solution)/shard_map/ppermute | solution.py:52
  141.2 0.0 collective-permute-done.13.refs_2_
  141.2 0.0 collective-permute-start.11
  141.2 0.0 collective-permute-done.21.refs_12_
  141.2 11.7 %collective-permute-start.10 = (bf16[16,2048]{1,0:T(8,128)(2,1)}, bf16[16,2048]{1,0:T(8,128)(2,1)S(1)}, u32[]{:S(2)}, u32[]{:S(2)}) collective-permute-start(bf16[16,2048]{1,0:T(8,128)(2,1)} %get-tuple-element.63.refs_3_), channel_id=1, source_target_pairs={{0,8},{8,16},{16,24},{24,0},{1,9},{9,17},{17,25},{25,1},{2,10},{10... | collective-permute-start | bytes 196616 | tf_op jit(solution)/shard_map/ppermute | solution.py:52
  152.9 5.8 %collective-permute-done.20.refs_11_ = bf16[144,1024]{1,0:T(8,128)(2,1)} collective-permute-done((bf16[144,1024]{1,0:T(8,128)(2,1)}, bf16[144,1024]{1,0:T(8,128)(2,1)}, u32[]{:S(2)}, u32[]{:S(2)}) %collective-permute-start.20) | collective-permute-done | bytes 294944 | tf_op jit(solution)/shard_map/ppermute | solution.py:692
  158.7 0.3 collective-permute-start.19
  159.0 0.0 collective-permute-done.12.refs_6_
  159.0 2.9 %collective-permute-start.18 = (bf16[144,1024]{1,0:T(8,128)(2,1)S(1)}, bf16[144,1024]{1,0:T(8,128)(2,1)S(1)}, u32[]{:S(2)}, u32[]{:S(2)}) collective-permute-start(bf16[144,1024]{1,0:T(8,128)(2,1)S(1)} %copy-done.8), channel_id=1, source_target_pairs={{0,24},{8,16},{16,8},{24,0},{1,25},{9,17},{17,9},{25,1},{2,26},{10... | collective-permute-start | bytes 884744 | tf_op jit(solution)/shard_map/ppermute | solution.py:692
  161.9 20.1 %collective-permute-done.11.refs_5_ = bf16[16,2048]{1,0:T(8,128)(2,1)S(1)} collective-permute-done((bf16[16,2048]{1,0:T(8,128)(2,1)}, bf16[16,2048]{1,0:T(8,128)(2,1)S(1)}, u32[]{:S(2)}, u32[]{:S(2)}) %collective-permute-start.11) | collective-permute-done | bytes 65568 | tf_op jit(solution)/shard_map/ppermute | solution.py:52
  182.0 0.7 collective-permute-start.17
  182.7 0.0 collective-permute-done.10.refs_4_
  182.7 1.4 collective-permute-start.16
  184.2 1.7 last_rows.1
  185.9 0.0 collective-permute-done.19.refs_10_
  185.9 0.0 collective-permute-done.18.refs_8_
  185.9 16.3 %collective-permute-done.17.refs_7_ = bf16[144,1024]{1,0:T(8,128)(2,1)S(1)} collective-permute-done((bf16[144,1024]{1,0:T(8,128)(2,1)S(1)}, bf16[144,1024]{1,0:T(8,128)(2,1)S(1)}, u32[]{:S(2)}, u32[]{:S(2)}) %collective-permute-start.17) | collective-permute-done | bytes 294944 | tf_op jit(solution)/shard_map/ppermute | solution.py:692
  202.2 0.7 copy-done.12
  202.9 0.7 copy-done.13
  203.6 0.0 collective-permute-done.15.refs_4_
  203.7 0.8 copy-done.7
  204.4 0.7 copy-done.2
  205.1 5.0 %row_gradients.1 = (f32[128,2048]{1,0:T(8,128)}, f32[8,2048]{1,0:T(8,128)}, f32[128,2048]{1,0:T(8,128)}, f32[16,2048]{1,0:T(8,128)}) custom-call(bf16[4,288,128]{2,1,0:T(8,128)(2,1)} %copy-done.2, bf16[128,2048]{1,0:T(8,128)(2,1)} %get-tuple-element.67.refs_5_.refs_3_.refs_1_, bf16[128,2048]{1,0:T(8,128)(2,1)} %copy-done.6, bf16[128,2048]{1,0:T(8,128)(2,1)} %copy-done.5, ...), custom_call_target="tpu_custom_call" | custom-call | tf_op jit(solution)/shard_map/row_gradients/pallas_call | solution.py:629
  (46 shorter events, 0.2 us)
Async XLA Ops:
  0.6 23.2 %copy-start.18 = (f32[16,2048]{1,0:T(8,128)S(1)}, f32[16,2048]{1,0:T(8,128)}, u32[]{:S(2)}) copy-start(f32[16,2048]{1,0:T(8,128)} %param.18) | copy-start | bytes 393220
  1.5 6.4 %collective-permute-start = (bf16[3,2048]{1,0:T(4,128)(2,1)S(1)}, bf16[3,2048]{1,0:T(4,128)(2,1)S(1)}, u32[]{:S(2)}, u32[]{:S(2)}) collective-permute-start(bf16[3,2048]{1,0:T(4,128)(2,1)S(1)} %slice.3), channel_id=1, source_target_pairs={{0,8},{8,16},{16,24},{1,9},{9,17},{17,25},{2,10},{10,18},{18,26},{... | collective-permute-start | bytes 36872 | tf_op jit(solution)/shard_map/ppermute | solution.py:58
  7.8 0.6 copy-start.20
  13.3 1.6 collective-permute-start.1
  15.9 6.3 %collective-permute-start.2 = (bf16[128,544]{1,0:T(8,128)(2,1)S(1)}, bf16[128,544]{1,0:T(8,128)(2,1)S(1)}, u32[]{:S(2)}, u32[]{:S(2)}) collective-permute-start(bf16[128,544]{1,0:T(8,128)(2,1)S(1)} %add_convert_fusion.4), channel_id=1, source_target_pairs={{0,2},{1,3},{2,0},{3,1},{4,6},{5,7},{6,4},{7,5},{8,10},{9,11},{10,... | collective-permute-start | bytes 417800 | tf_op jit(solution)/shard_map/ppermute | solution.py:692
  22.2 5.5 %copy-start.4 = (bf16[128,544]{1,0:T(8,128)(2,1)}, bf16[128,544]{1,0:T(8,128)(2,1)S(1)}, u32[]{:S(2)}) copy-start(bf16[128,544]{1,0:T(8,128)(2,1)S(1)} %add_convert_fusion.3.refs_0_) | copy-start | bytes 417796
  22.2 5.5 %collective-permute-start.3 = (bf16[128,544]{1,0:T(8,128)(2,1)S(1)}, bf16[128,544]{1,0:T(8,128)(2,1)S(1)}, u32[]{:S(2)}, u32[]{:S(2)}) collective-permute-start(bf16[128,544]{1,0:T(8,128)(2,1)S(1)} %add_convert_fusion.3.refs_0_), channel_id=1, source_target_pairs={{0,4},{1,5},{2,6},{3,7},{4,0},{5,1},{6,2},{7,3},{8,12},{9,13},{10,... | collective-permute-start | bytes 417800 | tf_op jit(solution)/shard_map/ppermute | solution.py:692
  27.7 0.7 copy-start.17
  41.2 5.6 %collective-permute-start.4 = (bf16[2,18,8,128]{3,2,1,0:T(8,128)(2,1)}, bf16[2,18,8,128]{3,2,1,0:T(8,128)(2,1)S(1)}, u32[]{:S(2)}, u32[]{:S(2)}) collective-permute-start(bf16[2,18,8,128]{3,2,1,0:T(8,128)(2,1)} %get-tuple-element.48), channel_id=1, source_target_pairs={{0,8},{8,0},{16,24},{24,16},{1,9},{9,1},{17,25},{25,17},{2,10},{10... | collective-permute-start | bytes 221192 | tf_op jit(solution)/shard_map/ppermute | solution.py:692
  43.6 7.0 %collective-permute-start.5 = (bf16[2,18,8,128]{3,2,1,0:T(8,128)(2,1)}, bf16[2,18,8,128]{3,2,1,0:T(8,128)(2,1)S(1)}, u32[]{:S(2)}, u32[]{:S(2)}) collective-permute-start(bf16[2,18,8,128]{3,2,1,0:T(8,128)(2,1)} %get-tuple-element.49), channel_id=1, source_target_pairs={{0,16},{8,24},{16,0},{24,8},{1,17},{9,25},{17,1},{25,9},{2,18},{10... | collective-permute-start | bytes 221192 | tf_op jit(solution)/shard_map/ppermute | solution.py:692
  46.2 6.4 %collective-permute-start.6 = (bf16[2,18,8,128]{3,2,1,0:T(8,128)(2,1)}, bf16[2,18,8,128]{3,2,1,0:T(8,128)(2,1)S(1)}, u32[]{:S(2)}, u32[]{:S(2)}) collective-permute-start(bf16[2,18,8,128]{3,2,1,0:T(8,128)(2,1)} %get-tuple-element.50), channel_id=1, source_target_pairs={{0,24},{8,16},{16,8},{24,0},{1,25},{9,17},{17,9},{25,1},{2,26},{10... | collective-permute-start | bytes 221192 | tf_op jit(solution)/shard_map/ppermute | solution.py:692
  46.8 5.7 %copy-start.14 = (bf16[2,18,8,128]{3,2,1,0:T(8,128)(2,1)}, bf16[2,18,8,128]{3,2,1,0:T(8,128)(2,1)S(1)}, u32[]{:S(2)}) copy-start(bf16[2,18,8,128]{3,2,1,0:T(8,128)(2,1)S(1)} %collective-permute-done.4.refs_8_) | copy-start | bytes 221188
  50.6 1.9 copy-start.15
  52.5 0.6 copy-start.16
  67.3 24.7 %copy-start = (bf16[128,2048]{1,0:T(8,128)(2,1)S(1)}, bf16[128,2048]{1,0:T(8,128)(2,1)}, u32[]{:S(2)}) copy-start(bf16[128,2048]{1,0:T(8,128)(2,1)} %get-tuple-element.67.refs_5_.refs_3_.refs_1_) | copy-start | bytes 1572868
  67.3 30.7 %copy-start.19 = (bf16[512,128]{1,0:T(8,128)(2,1)S(1)}, bf16[512,128]{1,0:T(8,128)(2,1)}, u32[]{:S(2)}) copy-start(bf16[512,128]{1,0:T(8,128)(2,1)} %get-tuple-element.66) | copy-start | bytes 393220
  81.5 1.6 collective-permute-start.7
  84.1 6.3 %collective-permute-start.8 = (bf16[640,128]{1,0:T(8,128)(2,1)S(1)}, bf16[640,128]{1,0:T(8,128)(2,1)S(1)}, u32[]{:S(2)}, u32[]{:S(2)}) collective-permute-start(bf16[640,128]{1,0:T(8,128)(2,1)S(1)} %add_convert_fusion.2), channel_id=1, source_target_pairs={{0,2},{1,3},{2,0},{3,1},{4,6},{5,7},{6,4},{7,5},{8,10},{9,11},{10,... | collective-permute-start | bytes 491528 | tf_op jit(solution)/shard_map/ppermute | solution.py:692
  90.5 12.1 %copy-start.1 = (bf16[640,128]{1,0:T(8,128)(2,1)}, bf16[640,128]{1,0:T(8,128)(2,1)S(1)}, u32[]{:S(2)}) copy-start(bf16[640,128]{1,0:T(8,128)(2,1)S(1)} %add_convert_fusion.1.back_a) | copy-start | bytes 491524
  90.5 6.1 %collective-permute-start.9 = (bf16[640,128]{1,0:T(8,128)(2,1)S(1)}, bf16[640,128]{1,0:T(8,128)(2,1)S(1)}, u32[]{:S(2)}, u32[]{:S(2)}) collective-permute-start(bf16[640,128]{1,0:T(8,128)(2,1)S(1)} %add_convert_fusion.1.back_a), channel_id=1, source_target_pairs={{0,4},{1,5},{2,6},{3,7},{4,0},{5,1},{6,2},{7,3},{8,12},{9,13},{10,... | collective-permute-start | bytes 491528 | tf_op jit(solution)/shard_map/ppermute | solution.py:692
  92.1 26.0 %collective-permute-start.14 = (bf16[128,2048]{1,0:T(8,128)(2,1)S(1)}, bf16[128,2048]{1,0:T(8,128)(2,1)S(1)}, u32[]{:S(2)}, u32[]{:S(2)}) collective-permute-start(bf16[128,2048]{1,0:T(8,128)(2,1)S(1)} %copy-done), channel_id=1, source_target_pairs={{0,16},{8,24},{16,0},{24,8},{1,17},{9,25},{17,1},{25,9},{2,18},{10... | collective-permute-start | bytes 1572872 | tf_op jit(solution)/shard_map/ppermute | solution.py:692
  93.1 48.1 %collective-permute-start.13 = (bf16[128,2048]{1,0:T(8,128)(2,1)S(1)}, bf16[128,2048]{1,0:T(8,128)(2,1)S(1)}, u32[]{:S(2)}, u32[]{:S(2)}) collective-permute-start(bf16[128,2048]{1,0:T(8,128)(2,1)S(1)} %copy-done), channel_id=1, source_target_pairs={{0,8},{8,0},{16,24},{24,16},{1,9},{9,1},{17,25},{25,17},{2,10},{10... | collective-permute-start | bytes 1572872 | tf_op jit(solution)/shard_map/ppermute | solution.py:692
  93.8 47.4 %collective-permute-start.21 = (bf16[144,1024]{1,0:T(8,128)(2,1)}, bf16[144,1024]{1,0:T(8,128)(2,1)}, u32[]{:S(2)}, u32[]{:S(2)}) collective-permute-start(bf16[144,1024]{1,0:T(8,128)(2,1)} %get-tuple-element.69.refs_9_), channel_id=1, source_target_pairs={{0,24},{8,16},{16,8},{24,0},{1,25},{9,17},{17,9},{25,1},{2,26},{10... | collective-permute-start | bytes 884744 | tf_op jit(solution)/shard_map/ppermute | solution.py:692
  96.5 62.2 %collective-permute-start.20 = (bf16[144,1024]{1,0:T(8,128)(2,1)}, bf16[144,1024]{1,0:T(8,128)(2,1)}, u32[]{:S(2)}, u32[]{:S(2)}) collective-permute-start(bf16[144,1024]{1,0:T(8,128)(2,1)} %get-tuple-element.69.refs_9_), channel_id=1, source_target_pairs={{0,16},{8,24},{16,0},{24,8},{1,17},{9,25},{17,1},{25,9},{2,18},{10... | collective-permute-start | bytes 884744 | tf_op jit(solution)/shard_map/ppermute | solution.py:692
  96.5 6.0 %copy-start.3 = (bf16[640,128]{1,0:T(8,128)(2,1)}, bf16[640,128]{1,0:T(8,128)(2,1)S(1)}, u32[]{:S(2)}) copy-start(bf16[640,128]{1,0:T(8,128)(2,1)S(1)} %collective-permute-done.9.back_b) | copy-start | bytes 491524
  96.6 107.1 %collective-permute-start.15 = (bf16[128,2048]{1,0:T(8,128)(2,1)S(1)}, bf16[128,2048]{1,0:T(8,128)(2,1)S(1)}, u32[]{:S(2)}, u32[]{:S(2)}) collective-permute-start(bf16[128,2048]{1,0:T(8,128)(2,1)S(1)} %copy-done), channel_id=1, source_target_pairs={{0,24},{8,16},{16,8},{24,0},{1,25},{9,17},{17,9},{25,1},{2,26},{10... | collective-permute-start | bytes 1572872 | tf_op jit(solution)/shard_map/ppermute | solution.py:692
  98.7 60.0 %copy-start.9 = (bf16[144,1024]{1,0:T(8,128)(2,1)S(1)}, bf16[144,1024]{1,0:T(8,128)(2,1)}, u32[]{:S(2)}) copy-start(bf16[144,1024]{1,0:T(8,128)(2,1)} %get-tuple-element.69.refs_9_) | copy-start | bytes 884740
  98.7 60.3 %copy-start.8 = (bf16[144,1024]{1,0:T(8,128)(2,1)S(1)}, bf16[144,1024]{1,0:T(8,128)(2,1)}, u32[]{:S(2)}) copy-start(bf16[144,1024]{1,0:T(8,128)(2,1)} %get-tuple-element.68.refs_5_) | copy-start | bytes 884740
  98.7 104.9 %all-to-all-start = ((bf16[4,288,128]{2,1,0:T(8,128)(2,1)}), bf16[4,288,128]{2,1,0:T(8,128)(2,1)S(1)}, u32[]{:S(2)}, u32[]{:S(2)}) async-start(bf16[4,288,128]{2,1,0:T(8,128)(2,1)} %pad_maximum_fusion), calls=%async_computation | async-start | bytes 589824 | tf_op jit(solution)/shard_map/all_to_all | solution.py:688
  118.1 85.5 %copy-start.5 = (bf16[128,2048]{1,0:T(8,128)(2,1)}, bf16[128,2048]{1,0:T(8,128)(2,1)S(1)}, u32[]{:S(2)}) copy-start(bf16[128,2048]{1,0:T(8,128)(2,1)S(1)} %collective-permute-done.14.refs_3_) | copy-start | bytes 1572868
  118.1 40.9 %collective-permute-start.12 = (bf16[16,2048]{1,0:T(8,128)(2,1)}, bf16[16,2048]{1,0:T(8,128)(2,1)S(1)}, u32[]{:S(2)}, u32[]{:S(2)}) collective-permute-start(bf16[16,2048]{1,0:T(8,128)(2,1)} %get-tuple-element.63.refs_3_), channel_id=1, source_target_pairs={{0,24},{8,0},{16,8},{24,16},{1,25},{9,1},{17,9},{25,17},{2,26},{10... | collective-permute-start | bytes 196616 | tf_op jit(solution)/shard_map/ppermute | solution.py:52
  141.2 62.5 %copy-start.6 = (bf16[128,2048]{1,0:T(8,128)(2,1)}, bf16[128,2048]{1,0:T(8,128)(2,1)S(1)}, u32[]{:S(2)}) copy-start(bf16[128,2048]{1,0:T(8,128)(2,1)S(1)} %collective-permute-done.13.refs_2_) | copy-start | bytes 1572868
  141.2 40.8 %collective-permute-start.11 = (bf16[16,2048]{1,0:T(8,128)(2,1)}, bf16[16,2048]{1,0:T(8,128)(2,1)S(1)}, u32[]{:S(2)}, u32[]{:S(2)}) collective-permute-start(bf16[16,2048]{1,0:T(8,128)(2,1)} %get-tuple-element.63.refs_3_), channel_id=1, source_target_pairs={{0,16},{8,24},{16,0},{24,8},{1,17},{9,25},{17,1},{25,9},{2,18},{10... | collective-permute-start | bytes 196616 | tf_op jit(solution)/shard_map/ppermute | solution.py:52
  141.2 41.5 %collective-permute-start.10 = (bf16[16,2048]{1,0:T(8,128)(2,1)}, bf16[16,2048]{1,0:T(8,128)(2,1)S(1)}, u32[]{:S(2)}, u32[]{:S(2)}) collective-permute-start(bf16[16,2048]{1,0:T(8,128)(2,1)} %get-tuple-element.63.refs_3_), channel_id=1, source_target_pairs={{0,8},{8,16},{16,24},{24,0},{1,9},{9,17},{17,25},{25,1},{2,10},{10... | collective-permute-start | bytes 196616 | tf_op jit(solution)/shard_map/ppermute | solution.py:52
  158.7 27.2 %collective-permute-start.19 = (bf16[144,1024]{1,0:T(8,128)(2,1)S(1)}, bf16[144,1024]{1,0:T(8,128)(2,1)S(1)}, u32[]{:S(2)}, u32[]{:S(2)}) collective-permute-start(bf16[144,1024]{1,0:T(8,128)(2,1)S(1)} %copy-done.9), channel_id=1, source_target_pairs={{0,8},{8,0},{16,24},{24,16},{1,9},{9,1},{17,25},{25,17},{2,10},{10... | collective-permute-start | bytes 884744 | tf_op jit(solution)/shard_map/ppermute | solution.py:692
  159.0 25.2 %copy-start.21 = (bf16[16,2048]{1,0:T(8,128)(2,1)}, bf16[16,2048]{1,0:T(8,128)(2,1)S(1)}, u32[]{:S(2)}) copy-start(bf16[16,2048]{1,0:T(8,128)(2,1)S(1)} %collective-permute-done.12.refs_6_) | copy-start | bytes 196612
  159.0 26.9 %collective-permute-start.18 = (bf16[144,1024]{1,0:T(8,128)(2,1)S(1)}, bf16[144,1024]{1,0:T(8,128)(2,1)S(1)}, u32[]{:S(2)}, u32[]{:S(2)}) collective-permute-start(bf16[144,1024]{1,0:T(8,128)(2,1)S(1)} %copy-done.8), channel_id=1, source_target_pairs={{0,24},{8,16},{16,8},{24,0},{1,25},{9,17},{17,9},{25,1},{2,26},{10... | collective-permute-start | bytes 884744 | tf_op jit(solution)/shard_map/ppermute | solution.py:692
  182.0 2.2 %copy-start.22 = (bf16[16,2048]{1,0:T(8,128)(2,1)}, bf16[16,2048]{1,0:T(8,128)(2,1)S(1)}, u32[]{:S(2)}) copy-start(bf16[16,2048]{1,0:T(8,128)(2,1)S(1)} %collective-permute-done.11.refs_5_) | copy-start | bytes 196612
  182.0 20.2 %collective-permute-start.17 = (bf16[144,1024]{1,0:T(8,128)(2,1)S(1)}, bf16[144,1024]{1,0:T(8,128)(2,1)S(1)}, u32[]{:S(2)}, u32[]{:S(2)}) collective-permute-start(bf16[144,1024]{1,0:T(8,128)(2,1)S(1)} %copy-done.8), channel_id=1, source_target_pairs={{0,16},{8,24},{16,0},{24,8},{1,17},{9,25},{17,1},{25,9},{2,18},{10... | collective-permute-start | bytes 884744 | tf_op jit(solution)/shard_map/ppermute | solution.py:692
  182.7 1.4 copy-start.23
  182.7 19.4 %collective-permute-start.16 = (bf16[144,1024]{1,0:T(8,128)(2,1)S(1)}, bf16[144,1024]{1,0:T(8,128)(2,1)S(1)}, u32[]{:S(2)}, u32[]{:S(2)}) collective-permute-start(bf16[144,1024]{1,0:T(8,128)(2,1)S(1)} %copy-done.8), channel_id=1, source_target_pairs={{0,8},{8,0},{16,24},{24,16},{1,9},{9,1},{17,25},{25,17},{2,10},{10... | collective-permute-start | bytes 884744 | tf_op jit(solution)/shard_map/ppermute | solution.py:692
  185.9 16.3 %copy-start.10 = (bf16[144,1024]{1,0:T(8,128)(2,1)}, bf16[144,1024]{1,0:T(8,128)(2,1)S(1)}, u32[]{:S(2)}) copy-start(bf16[144,1024]{1,0:T(8,128)(2,1)S(1)} %collective-permute-done.19.refs_10_) | copy-start | bytes 884740
  185.9 16.3 %copy-start.11 = (bf16[144,1024]{1,0:T(8,128)(2,1)}, bf16[144,1024]{1,0:T(8,128)(2,1)S(1)}, u32[]{:S(2)}) copy-start(bf16[144,1024]{1,0:T(8,128)(2,1)S(1)} %collective-permute-done.18.refs_8_) | copy-start | bytes 884740
  202.2 0.7 copy-start.12
  202.9 0.7 copy-start.13
  203.6 0.8 copy-start.7
  204.4 0.7 copy-start.2

commit v5 on v4

--- a/solution.py
+++ b/solution.py
@@ -594,17 +594,41 @@
     )(*backs, proj_weight, scan_part, small, conv_input, rim, weight, bias)
 
 
+def cut_kernel(places, *refs):
+    back_a, back_b, low_t = refs[:3]
+    cuts, (back,) = refs[3 : 3 + places], refs[3 + places :]
+    place = lax.axis_index("ctx")
+    back_rows, ranks = back.shape[0] // places, low_t.shape[0] // places
+    back[...] = back_a[...].astype(F32) + back_b[...].astype(F32)
+    for mask in range(places):
+        other = place ^ mask
+        cuts[mask][:back_rows, :] = back[pl.ds(other * back_rows, back_rows), :].astype(BF)
+        cuts[mask][back_rows:, :] = low_t[pl.ds(pl.multiple_of(other * ranks, 16), ranks), :]
+
+
+def cut_call(places, backs, low_t):
+    wide, rows = backs[0].shape
+    cut = ((wide + low_t.shape[0]) // places, rows)
+    return pl.pallas_call(
+        functools.partial(cut_kernel, places),
+        out_shape=[sds(cut, BF)] * places,
+        scratch_shapes=[pltpu.VMEM((wide, rows), F32)],
+        compiler_params=params(),
+        name="cut_rows",
+    )(*backs, low_t)
+
+
 def rows_kernel(places, rank_rows, chunks, *refs):
-    cut_ref, refs = refs[0], refs[1:]
+    cuts, refs = refs[:places], refs[places:]
     blocks, refs = refs[:places], refs[places:]
     steps, refs = refs[: chunks * places], refs[chunks * places :]
     out_ref, coef_ref, step_ref, decay_ref = refs
     place = lax.axis_index("ctx")
     rows = blocks[0].shape[0]
-    back_rows = cut_ref.shape[1] - rank_rows
+    back_rows = cuts[0].shape[0] - rank_rows
     total = jnp.zeros((back_rows, out_ref.shape[1]), F32)
-    for mask in range(places):
-        total = total + dot(cut_ref[place ^ mask, :back_rows, :], blocks[mask][...])
+    for cut, block in zip(cuts, blocks):
+        total = total + dot(cut[:back_rows, :], block[...])
     out_ref[...] = total[:rank_rows, :]
     coef_ref[...] = total[rank_rows : rank_rows + coef_ref.shape[0], :]
     for chunk in range(chunks):
@@ -615,7 +639,7 @@
             decay = jnp.zeros(decay_ref.shape, F32)
             for mask in range(places):
                 step = steps[chunk * places + mask]
-                total = total + dot(cut_ref[place ^ mask, back_rows:, :], step[:rows, :])
+                total = total + dot(cuts[mask][back_rows:, :], step[:rows, :])
                 decay = decay + step[rows:, :].astype(F32)
             step_ref[...] = total
             decay_ref[...] = decay
@@ -623,20 +647,20 @@
 
 def rows_call(places, rank_rows, coef_rows, cuts, blocks, steps):
     rows, chans = blocks[0].shape
-    chunks = len(steps) // places
     tall, width = steps[0].shape
+    chunks = chans // width
     heights = (rank_rows, coef_rows, rank_rows, tall - rows)
     return pl.pallas_call(
         functools.partial(rows_kernel, places, rank_rows, chunks),
         grid=(chunks,),
-        in_specs=[whole(cuts.shape)]
+        in_specs=[whole(cuts[0].shape)] * places
         + [columns(rows, width)] * places
-        + [whole((tall, width))] * (chunks * places),
+        + [whole((tall, width))] * len(steps),
         out_specs=[columns(height, width) for height in heights],
         out_shape=[sds((height, chans), F32) for height in heights],
         compiler_params=params(),
         name="row_gradients",
-    )(cuts, *blocks, *steps)
+    )(*cuts, *blocks, *steps)
 
 
 def last_kernel(places, taps, *refs):
@@ -690,6 +714,20 @@
 
 def swap(block, axis, mask):
     return lax.ppermute(block, axis, [(i, i ^ mask) for i in range(lax.axis_size(axis))])
+
+
+tie = lax.optimization_barrier
+
+
+def spread(block):
+    return [block] + [swap(block, "ctx", mask) for mask in range(1, min(lax.axis_size("ctx"), 3))]
+
+
+def spread_on(blocks):
+    places = lax.axis_size("ctx")
+    if places == 4:
+        return blocks + [swap(blocks[2], "ctx", 1)]
+    return blocks + [swap(blocks[0], "ctx", mask) for mask in range(3, places)]
 
 
 def chan_sum(part):
@@ -728,35 +766,39 @@
     chunks = decay.shape[0]
     rim = shift(conv_input[rows - (taps - 1) :], "ctx", 1)
     conv_out, part = conv_call(conv_input, rim, conv_weight, conv_bias, proj_weight)
-    blocks = [conv_out] + [swap(conv_out, "ctx", mask) for mask in range(1, min(places, 3))]
+    blocks = spread(conv_out)
     parts = chan_sum(part)
     dt, coef, low, low_t, *messages = local_call(
         parts, step_weight, step_bias, decay, conv_out, gate_input, out_grad, states, places
     )
+    messages, blocks = tie((messages, blocks))
     messages = [swap(message, "ctx", mask) for mask, message in enumerate(messages, 1)]
-    messages, held = lax.optimization_barrier((messages, conv_out))
-    blocks += [swap(held, "ctx", mask) for mask in range(3, places)]
-    previous, steps = [], []
+    messages, blocks = tie((messages, blocks))
+    blocks = spread_on(blocks)
+    previous, steps, fresh = [], [], None
     for chunk in range(chunks):
-        pre_bf, grad_gate, scan_part, small, part = scan_call(
+        message, grad_gate, scan_part, small, part = scan_call(
             places, chunk, coef, dt, decay, conv_out, gate_input, out_grad, step_weight,
             skip_gain, messages, previous,
         )
         previous = [part, grad_gate, scan_part, small]
-        steps += [pre_bf] + [swap(pre_bf, "ctx", mask) for mask in range(1, places)]
+        if chunk == 0:
+            previous, blocks = tie((previous, blocks))
+        if fresh is not None:
+            previous, fresh = tie((previous, fresh))
+            steps += spread_on(fresh)
+        fresh = spread(message)
+    part, grad_gate, scan_part, small = previous
     backs = chan_sum(part)
-    cuts = jnp.concatenate(
-        [
-            (backs[0].astype(F32) + backs[1].astype(F32)).astype(BF).reshape(places, -1, rows),
-            low_t.reshape(places, -1, rows),
-        ],
-        axis=1,
-    )
-    cuts = exchange(cuts, "ctx")
+    backs, steps, fresh = tie((backs, steps, fresh))
+    steps += spread_on(fresh)
+    cuts = cut_call(places, backs, low_t)
+    cuts = [cuts[0]] + [swap(cut, "ctx", mask) for mask, cut in enumerate(cuts[1:], 1)]
     main, tail, sums = conv_grad_call(
         places, low_rank, backs, proj_weight, scan_part, small, conv_input, rim, conv_weight,
         conv_bias,
     )
+    sums, cuts, steps = tie((sums, cuts, steps))
     late = [sums] + [rotate(sums, "ctx", hop) for hop in range(1, places)]
     grad_proj, grad_coef, grad_step, decay_grad = rows_call(
         places, low_rank // places, 2 * states // places, cuts, blocks, steps

time: 211 us -> 138 us (0.65)
  waiting for transfers between devices: 74.6 us -> 32 us
  starting transfers between devices: 66 us -> 37.5 us
  local copies, waits for them, and re-layouts: 6.34 us -> 3.49 us
    ppermute x3, starting transfers between devices: 34.8 us -> 3.87 us  [rotate(): lax.ppermute(block, axis, [(i, (i + distance) % count) for i in range(cou...]
    ppermute x18 -> x21, waiting for transfers between devices: 53 us -> 30.5 us  [swap(): lax.ppermute(block, axis, [(i, i ^ mask) for i in range(lax.axis_size(axi...]
    ppermute x3, waiting for transfers between devices: 20.1 us -> 0.01 us  [rotate(): lax.ppermute(block, axis, [(i, (i + distance) % count) for i in range(cou...]
    ppermute x18 -> x21, starting transfers between devices: 22.4 us -> 28.7 us  [swap(): lax.ppermute(block, axis, [(i, i ^ mask) for i in range(lax.axis_size(axi...]
    all_to_all x1 -> x0, starting transfers between devices: 3.84 us -> none  [exchange(): return lax.all_to_all(block, axis, split_axis=0, concat_axis=0, tiled=True)]
    unnamed x49, local copies, waits for them, and re-layouts: 4.87 us -> 2.01 us
  transfers between devices with their start and end apart: 23 -> 25, of which waited for: 13 -> 9; matrix products, arithmetic and copies ran while one was open for 1% -> 1% of each run, Pallas kernels for 4% -> 40%
where the time goes in v5:
time: 138 us; the launch traced here: 137 us
  Pallas kernels  61.5 us (45%)
  starting transfers between devices  37.5 us (27%)
  waiting for transfers between devices  32 us (23%)
  local copies, waits for them, and re-layouts  3.49 us (3%)
  other arithmetic  2.02 us (1%)
    ppermute x21, waiting for transfers between devices, swap(): lax.ppermute(block, axis, [(i, i ^ mask) for i in range(lax.axis_size(axi...  30.5 us
    ppermute x21, starting transfers between devices, swap(): lax.ppermute(block, axis, [(i, i ^ mask) for i in range(lax.axis_size(axi...  28.7 us
    pallas_call x2, Pallas kernels, scan_call(): pl.pallas_call(functools.partial(scan_kernel, places, states, first), gri...  28.4 us
    pallas_call x1, Pallas kernels, local_call(): pl.pallas_call(functools.partial(local_kernel, low_rank, states, places),...  12.8 us
    pallas_call x1, Pallas kernels, conv_grad_call(): pl.pallas_call(functools.partial(conv_grad_kernel, places, low_rank), gri...  6.78 us
    pallas_call x1, Pallas kernels, rows_call(): pl.pallas_call(functools.partial(rows_kernel, places, rank_rows, chunks),...  4.99 us
    ppermute x1, starting transfers between devices, shift(): return lax.ppermute(block, axis, route)  4.93 us
    pallas_call x1, Pallas kernels, conv_call(): pl.pallas_call(conv_kernel, grid=(chans // width,), in_specs=[columns(row...  4.85 us
  transfers between devices with their start and end apart: 25, of which 9 were waited for; matrix products, arithmetic and copies ran while one was open for 1% of the time, Pallas kernels for 40%

profile of v5, /device:TPU:0, one launch (start us, length us, event | category | flops | bytes accessed | tf_op | source)
XLA Modules:
  0.0 137.4 jit_solution(9881014883291652235)
XLA Ops:
  0.7 0.8 slice.3
  1.5 4.9 %collective-permute-start = (bf16[3,2048]{1,0:T(4,128)(2,1)S(1)}, bf16[3,2048]{1,0:T(4,128)(2,1)S(1)}, u32[]{:S(2)}, u32[]{:S(2)}) collective-permute-start(bf16[3,2048]{1,0:T(4,128)(2,1)S(1)} %slice.3), channel_id=1, source_target_pairs={{0,8},{8,16},{16,24},{1,9},{9,17},{17,25},{2,10},{10,18},{18,26},{... | collective-permute-start | bytes 36872 | tf_op jit(solution)/shard_map/ppermute | solution.py:58
  6.4 1.4 %collective-permute-done.rim_ref = bf16[3,2048]{1,0:T(4,128)(2,1)S(1)} collective-permute-done((bf16[3,2048]{1,0:T(4,128)(2,1)S(1)}, bf16[3,2048]{1,0:T(4,128)(2,1)S(1)}, u32[]{:S(2)}, u32[]{:S(2)}) %collective-permute-start) | collective-permute-done | bytes 12320 | tf_op jit(solution)/shard_map/ppermute | solution.py:58
  7.8 0.6 copy-done.20
  8.4 4.8 %conv_project.1 = (bf16[128,2048]{1,0:T(8,128)(2,1)}, bf16[128,544]{1,0:T(8,128)(2,1)}) custom-call(bf16[128,2048]{1,0:T(8,128)(2,1)} %input_ref.3, bf16[3,2048]{1,0:T(4,128)(2,1)} %copy-done.20, f32[4,2048]{1,0:T(4,128)} %refs_2_.3, f32[1,2048]{1,0:T(1,128)} %bitcast.19, bf16[544,2048]{1,0:T(8,128)(2,1)} %proj_ref.3), custom_call_target="tpu_custom_call" | custom-call | tf_op jit(solution)/shard_map/conv_project/pallas_call | solution.py:103
  13.3 0.0 collective-permute-start.1
  13.3 2.4 %collective-permute-start.4 = (bf16[128,2048]{1,0:T(8,128)(2,1)}, bf16[128,2048]{1,0:T(8,128)(2,1)S(1)}, u32[]{:S(2)}, u32[]{:S(2)}) collective-permute-start(bf16[128,2048]{1,0:T(8,128)(2,1)} %get-tuple-element.156.refs_5_.refs_3_.refs_4_), channel_id=1, source_target_pairs={{0,8},{8,0},{16,24},{24,16},{1,9},{9,1},{17,25},{25,17},{2,10},{10... | collective-permute-start | bytes 1572872 | tf_op jit(solution)/shard_map/ppermute | solution.py:716
  15.6 2.6 %collective-permute-start.5 = (bf16[128,2048]{1,0:T(8,128)(2,1)}, bf16[128,2048]{1,0:T(8,128)(2,1)S(1)}, u32[]{:S(2)}, u32[]{:S(2)}) collective-permute-start(bf16[128,2048]{1,0:T(8,128)(2,1)} %get-tuple-element.156.refs_5_.refs_3_.refs_4_), channel_id=1, source_target_pairs={{0,16},{8,24},{16,0},{24,8},{1,17},{9,25},{17,1},{25,9},{2,18},{10... | collective-permute-start | bytes 1572872 | tf_op jit(solution)/shard_map/ppermute | solution.py:716
  18.2 0.0 collective-permute-done.1
  18.2 1.0 add_convert_fusion.3
  19.2 1.6 %collective-permute-start.2 = (bf16[128,544]{1,0:T(8,128)(2,1)S(1)}, bf16[128,544]{1,0:T(8,128)(2,1)S(1)}, u32[]{:S(2)}, u32[]{:S(2)}) collective-permute-start(bf16[128,544]{1,0:T(8,128)(2,1)S(1)} %add_convert_fusion.3), channel_id=1, source_target_pairs={{0,2},{1,3},{2,0},{3,1},{4,6},{5,7},{6,4},{7,5},{8,10},{9,11},{10,... | collective-permute-start | bytes 417800 | tf_op jit(solution)/shard_map/ppermute | solution.py:716
  20.8 4.5 %collective-permute-done.2 = bf16[128,544]{1,0:T(8,128)(2,1)S(1)} collective-permute-done((bf16[128,544]{1,0:T(8,128)(2,1)S(1)}, bf16[128,544]{1,0:T(8,128)(2,1)S(1)}, u32[]{:S(2)}, u32[]{:S(2)}) %collective-permute-start.2) | collective-permute-done | bytes 139296 | tf_op jit(solution)/shard_map/ppermute | solution.py:716
  25.3 0.0 copy-start.2
  25.3 1.6 %collective-permute-start.3 = (bf16[128,544]{1,0:T(8,128)(2,1)S(1)}, bf16[128,544]{1,0:T(8,128)(2,1)S(1)}, u32[]{:S(2)}, u32[]{:S(2)}) collective-permute-start(bf16[128,544]{1,0:T(8,128)(2,1)S(1)} %add_convert_fusion.2.refs_0_), channel_id=1, source_target_pairs={{0,4},{1,5},{2,6},{3,7},{4,0},{5,1},{6,2},{7,3},{8,12},{9,13},{10,... | collective-permute-start | bytes 417800 | tf_op jit(solution)/shard_map/ppermute | solution.py:716
  26.9 0.7 copy.27
  27.6 3.1 %collective-permute-done.3.refs_1_ = bf16[128,544]{1,0:T(8,128)(2,1)S(1)} collective-permute-done((bf16[128,544]{1,0:T(8,128)(2,1)S(1)}, bf16[128,544]{1,0:T(8,128)(2,1)S(1)}, u32[]{:S(2)}, u32[]{:S(2)}) %collective-permute-start.3) | collective-permute-done | bytes 139296 | tf_op jit(solution)/shard_map/ppermute | solution.py:716
  30.7 0.7 copy-done.15
  31.4 12.8 %local_ends.1 = (f32[2,1024,128]{2,1,0:T(8,128)}, f32[128,128]{1,0:T(8,128)}, bf16[128,512]{1,0:T(8,128)(2,1)}, bf16[512,128]{1,0:T(8,128)(2,1)}, bf16[2,18,8,12...) custom-call(bf16[128,544]{1,0:T(8,128)(2,1)} %copy-done.2, ...), custom_call_target="tpu_custom_call" | custom-call | tf_op jit(solution)/shard_map/local_ends/pallas_call | solution.py:228
  44.2 0.0 collective-permute-done.4.refs_5_
  44.2 0.0 collective-permute-done.5.refs_6_
  44.2 0.5 collective-permute-start.6
  44.8 1.4 %collective-permute-start.7 = (bf16[2,18,8,128]{3,2,1,0:T(8,128)(2,1)}, bf16[2,18,8,128]{3,2,1,0:T(8,128)(2,1)S(1)}, u32[]{:S(2)}, u32[]{:S(2)}) collective-permute-start(bf16[2,18,8,128]{3,2,1,0:T(8,128)(2,1)} %get-tuple-element.101), channel_id=1, source_target_pairs={{0,16},{8,24},{16,0},{24,8},{1,17},{9,25},{17,1},{25,9},{2,18},{10... | collective-permute-start | bytes 221192 | tf_op jit(solution)/shard_map/ppermute | solution.py:716
  46.2 2.5 %collective-permute-start.8 = (bf16[2,18,8,128]{3,2,1,0:T(8,128)(2,1)}, bf16[2,18,8,128]{3,2,1,0:T(8,128)(2,1)S(1)}, u32[]{:S(2)}, u32[]{:S(2)}) collective-permute-start(bf16[2,18,8,128]{3,2,1,0:T(8,128)(2,1)} %get-tuple-element.102), channel_id=1, source_target_pairs={{0,24},{8,16},{16,8},{24,0},{1,25},{9,17},{17,9},{25,1},{2,26},{10... | collective-permute-start | bytes 221192 | tf_op jit(solution)/shard_map/ppermute | solution.py:716
  48.7 0.4 collective-permute-done.6.refs_8_
  49.1 1.4 %collective-permute-done.7.refs_9_ = bf16[2,18,8,128]{3,2,1,0:T(8,128)(2,1)S(1)} collective-permute-done((bf16[2,18,8,128]{3,2,1,0:T(8,128)(2,1)}, bf16[2,18,8,128]{3,2,1,0:T(8,128)(2,1)S(1)}, u32[]{:S(2)}, u32[]{:S(2)}) %collective-permute-start.7) | collective-permute-done | bytes 73760 | tf_op jit(solution)/shard_map/ppermute | solution.py:716
  50.5 2.1 %collective-permute-done.8.refs_10_ = bf16[2,18,8,128]{3,2,1,0:T(8,128)(2,1)S(1)} collective-permute-done((bf16[2,18,8,128]{3,2,1,0:T(8,128)(2,1)}, bf16[2,18,8,128]{3,2,1,0:T(8,128)(2,1)S(1)}, u32[]{:S(2)}, u32[]{:S(2)}) %collective-permute-start.8) | collective-permute-done | bytes 73760 | tf_op jit(solution)/shard_map/ppermute | solution.py:716
  52.7 0.8 collective-permute-start.9
  53.5 14.2 %scan_gradients.2 = (bf16[144,1024]{1,0:T(8,128)(2,1)}, bf16[128,2048]{1,0:T(8,128)(2,1)}, bf16[128,2048]{1,0:T(8,128)(2,1)}, f32[8,2048]{1,0:T(8,128)}, f32[640,128]{1,0:T(8,128)}) custom-call(f32[128,128]{1,0:T(8,128)} %get-tuple-element.95.refs_0_, f32[2,1024,128]{2,1,0:T(8,128)} %get-tuple-element.96.refs_1_, f32[2,16,8,128]{3,2,1,0:T(8,128)} %bitcast.13, ...), custom_call_target="tpu_custom_call" | custom-call | tf_op jit(solution)/shard_map/scan_gradients/pallas_call | solution.py:495
  67.7 1.3 collective-permute-start.10
  69.0 2.3 %collective-permute-start.11 = (bf16[144,1024]{1,0:T(8,128)(2,1)}, bf16[144,1024]{1,0:T(8,128)(2,1)S(1)}, u32[]{:S(2)}, u32[]{:S(2)}) collective-permute-start(bf16[144,1024]{1,0:T(8,128)(2,1)} %get-tuple-element.160.refs_8_), channel_id=1, source_target_pairs={{0,16},{8,24},{16,0},{24,8},{1,17},{9,25},{17,1},{25,9},{2,18},{10... | collective-permute-start | bytes 884744 | tf_op jit(solution)/shard_map/ppermute | solution.py:716
  71.3 0.0 collective-permute-done.9.refs_7_
  71.3 14.3 %scan_gradients.3 = (bf16[144,1024]{1,0:T(8,128)(2,1)}, bf16[128,2048]{1,0:T(8,128)(2,1)}, bf16[128,2048]{1,0:T(8,128)(2,1)}, f32[8,2048]{1,0:T(8,128)}, bf16[640,128]{1,0:T(8,128)(2,1)}) custom-call(f32[128,128]{1,0:T(8,128)} %get-tuple-element.95.refs_0_, ...), custom_call_target="tpu_custom_call", output_to_operand_aliasing={{1}: (12, {}), {2}: (13, {}), {3}: (14, {})} | custom-call | tf_op jit(solution)/shard_map/scan_gradients/pallas_call | solution.py:495
  85.6 0.0 collective-permute-done.10.refs_9_
  85.6 0.0 collective-permute-done.11.refs_10_
  85.6 0.1 collective-permute-start.12
  85.7 1.6 %collective-permute-done.12 = bf16[640,128]{1,0:T(8,128)(2,1)S(1)} collective-permute-done((bf16[640,128]{1,0:T(8,128)(2,1)}, bf16[640,128]{1,0:T(8,128)(2,1)S(1)}, u32[]{:S(2)}, u32[]{:S(2)}) %collective-permute-start.12) | collective-permute-done | bytes 163872 | tf_op jit(solution)/shard_map/ppermute | solution.py:716
  87.3 1.0 add_convert_fusion.1
  88.3 1.6 %collective-permute-start.13 = (bf16[640,128]{1,0:T(8,128)(2,1)S(1)}, bf16[640,128]{1,0:T(8,128)(2,1)S(1)}, u32[]{:S(2)}, u32[]{:S(2)}) collective-permute-start(bf16[640,128]{1,0:T(8,128)(2,1)S(1)} %add_convert_fusion.1), channel_id=1, source_target_pairs={{0,2},{1,3},{2,0},{3,1},{4,6},{5,7},{6,4},{7,5},{8,10},{9,11},{10,... | collective-permute-start | bytes 491528 | tf_op jit(solution)/shard_map/ppermute | solution.py:716
  89.8 1.4 %collective-permute-start.16 = (bf16[144,1024]{1,0:T(8,128)(2,1)}, bf16[144,1024]{1,0:T(8,128)(2,1)S(1)}, u32[]{:S(2)}, u32[]{:S(2)}) collective-permute-start(bf16[144,1024]{1,0:T(8,128)(2,1)} %get-tuple-element.164.refs_12_), channel_id=1, source_target_pairs={{0,8},{8,0},{16,24},{24,16},{1,9},{9,1},{17,25},{25,17},{2,10},{10... | collective-permute-start | bytes 884744 | tf_op jit(solution)/shard_map/ppermute | solution.py:716
  91.2 0.0 collective-permute-start.17
  91.2 1.2 collective-permute-start.15
  92.4 2.1 %collective-permute-done.13 = bf16[640,128]{1,0:T(8,128)(2,1)S(1)} collective-permute-done((bf16[640,128]{1,0:T(8,128)(2,1)S(1)}, bf16[640,128]{1,0:T(8,128)(2,1)S(1)}, u32[]{:S(2)}, u32[]{:S(2)}) %collective-permute-start.13) | collective-permute-done | bytes 163872 | tf_op jit(solution)/shard_map/ppermute | solution.py:716
  94.6 0.0 copy-start
  94.6 1.6 %collective-permute-start.14 = (bf16[640,128]{1,0:T(8,128)(2,1)S(1)}, bf16[640,128]{1,0:T(8,128)(2,1)S(1)}, u32[]{:S(2)}, u32[]{:S(2)}) collective-permute-start(bf16[640,128]{1,0:T(8,128)(2,1)S(1)} %add_convert_fusion.back_a.refs_0_), channel_id=1, source_target_pairs={{0,4},{1,5},{2,6},{3,7},{4,0},{5,1},{6,2},{7,3},{8,12},{9,13},{10,... | collective-permute-start | bytes 491528 | tf_op jit(solution)/shard_map/ppermute | solution.py:716
  96.2 15.2 %collective-permute-done.15.refs_11_ = bf16[144,1024]{1,0:T(8,128)(2,1)S(1)} collective-permute-done((bf16[144,1024]{1,0:T(8,128)(2,1)S(1)}, bf16[144,1024]{1,0:T(8,128)(2,1)S(1)}, u32[]{:S(2)}, u32[]{:S(2)}) %collective-permute-start.15) | collective-permute-done | bytes 294944 | tf_op jit(solution)/shard_map/ppermute | solution.py:716
  111.4 0.0 collective-permute-done.16.refs_13_
  111.5 1.5 %collective-permute-start.21 = (bf16[144,1024]{1,0:T(8,128)(2,1)S(1)}, bf16[144,1024]{1,0:T(8,128)(2,1)S(1)}, u32[]{:S(2)}, u32[]{:S(2)}) collective-permute-start(bf16[144,1024]{1,0:T(8,128)(2,1)S(1)} %collective-permute-done.17.refs_14_), channel_id=1, source_target_pairs={{0,8},{8,0},{16,24},{24,16},{1,9},{9,1},{17,25},{25,17},{2,10},{10... | collective-permute-start | bytes 884744 | tf_op jit(solution)/shard_map/ppermute | solution.py:716
  113.0 1.9 %cut_rows.1 = (bf16[288,128]{1,0:T(8,128)(2,1)}, bf16[288,128]{1,0:T(8,128)(2,1)}, bf16[288,128]{1,0:T(8,128)(2,1)}, bf16[288,128]{1,0:T(8,128)(2,1)}) custom-call(bf16[640,128]{1,0:T(8,128)(2,1)} %copy-done, bf16[640,128]{1,0:T(8,128)(2,1)} %copy-done.1, bf16[512,128]{1,0:T(8,128)(2,1)} %get-tuple-element.137.refs_2_), custom_call_target="tpu_custom_call" | custom-call | tf_op jit(solution)/shard_map/cut_rows/pallas_call | solution.py:612
  114.8 0.6 collective-permute-start.18
  115.5 0.6 collective-permute-start.19
  116.1 3.1 %collective-permute-start.20 = (bf16[288,128]{1,0:T(8,128)(2,1)}, bf16[288,128]{1,0:T(8,128)(2,1)S(1)}, u32[]{:S(2)}, u32[]{:S(2)}) collective-permute-start(bf16[288,128]{1,0:T(8,128)(2,1)} %get-tuple-element.141), channel_id=1, source_target_pairs={{0,24},{8,16},{16,8},{24,0},{1,25},{9,17},{17,9},{25,1},{2,26},{10... | collective-permute-start | bytes 221192 | tf_op jit(solution)/shard_map/ppermute | solution.py:716
  119.2 6.8 %conv_gradients.1 = (bf16[128,2048]{1,0:T(8,128)(2,1)}, f32[16,2048]{1,0:T(8,128)}, bf16[16,2048]{1,0:T(8,128)(2,1)}) custom-call(bf16[640,128]{1,0:T(8,128)(2,1)} %copy-done, bf16[640,128]{1,0:T(8,128)(2,1)} %copy-done.1, bf16[544,2048]{1,0:T(8,128)(2,1)} %proj_ref.3, bf16[128,2048]{1,0:T(8,128)(2,1)} %get-tuple-element.132.scan_ref, ...), custom_call_target="tpu_custom_call" | custom-call | tf_op jit(solution)/shard_map/conv_gradients/pallas_call | solution.py:575
  126.0 0.0 collective-permute-done.18.refs_1_
  126.1 0.0 collective-permute-done.21.refs_15_
  126.1 0.1 collective-permute-start.22
  126.2 1.9 %collective-permute-start.23 = (bf16[16,2048]{1,0:T(8,128)(2,1)}, bf16[16,2048]{1,0:T(8,128)(2,1)S(1)}, u32[]{:S(2)}, u32[]{:S(2)}) collective-permute-start(bf16[16,2048]{1,0:T(8,128)(2,1)} %get-tuple-element.149.refs_3_), channel_id=1, source_target_pairs={{0,16},{8,24},{16,0},{24,8},{1,17},{9,25},{17,1},{25,9},{2,18},{10... | collective-permute-start | bytes 196616 | tf_op jit(solution)/shard_map/ppermute | solution.py:52
  128.0 2.0 %collective-permute-start.24 = (bf16[16,2048]{1,0:T(8,128)(2,1)}, bf16[16,2048]{1,0:T(8,128)(2,1)S(1)}, u32[]{:S(2)}, u32[]{:S(2)}) collective-permute-start(bf16[16,2048]{1,0:T(8,128)(2,1)} %get-tuple-element.149.refs_3_), channel_id=1, source_target_pairs={{0,24},{8,0},{16,8},{24,16},{1,25},{9,1},{17,9},{25,17},{2,26},{10... | collective-permute-start | bytes 196616 | tf_op jit(solution)/shard_map/ppermute | solution.py:52
  130.0 5.0 %row_gradients.1 = (f32[128,2048]{1,0:T(8,128)}, f32[8,2048]{1,0:T(8,128)}, f32[128,2048]{1,0:T(8,128)}, f32[16,2048]{1,0:T(8,128)}) custom-call(bf16[288,128]{1,0:T(8,128)(2,1)} %get-tuple-element.152.refs_0_, bf16[288,128]{1,0:T(8,128)(2,1)} %copy-done.17, bf16[288,128]{1,0:T(8,128)(2,1)} %copy-done.18, bf16[288,128]{1,0:T(8,128)(2,1)} %copy-done.19, ...), custom_call_target="tpu_custom_call" | custom-call | tf_op jit(solution)/shard_map/row_gradients/pallas_call | solution.py:653
  135.0 0.0 collective-permute-done.23.refs_5_
  135.1 0.0 collective-permute-done.24.refs_6_
  135.1 0.6 copy-done.21
  135.7 0.0 copy-done.22
  135.7 0.0 copy-done.23
  135.7 1.7 %last_rows.1 = (bf16[128,2048]{1,0:T(8,128)(2,1)}, f32[4,2048]{1,0:T(4,128)}, f32[1,2048]{1,0:T(1,128)}, f32[1,2048]{1,0:T(1,128)}, f32[1,2048]{1,0:T(1,128)}) custom-call(bf16[128,2048]{1,0:T(8,128)(2,1)} %get-tuple-element.134.refs_0_, f32[16,2048]{1,0:T(8,128)} %get-tuple-element.135.refs_1_, f32[4,2048]{1,0:T(4,128)} %refs_2_.3, ...), custom_call_target="tpu_custom_call", output_to_operand_aliasing={{0}: (0, {})} | custom-call | tf_op jit(solution)/shard_map/last_rows/pallas_call | solution.py:693
  (49 shorter events, 0.2 us)
Async XLA Ops:
  0.6 26.3 %copy-start.16 = (f32[16,2048]{1,0:T(8,128)S(1)}, f32[16,2048]{1,0:T(8,128)}, u32[]{:S(2)}) copy-start(f32[16,2048]{1,0:T(8,128)} %param.18) | copy-start | bytes 393220
  1.5 6.4 %collective-permute-start = (bf16[3,2048]{1,0:T(4,128)(2,1)S(1)}, bf16[3,2048]{1,0:T(4,128)(2,1)S(1)}, u32[]{:S(2)}, u32[]{:S(2)}) collective-permute-start(bf16[3,2048]{1,0:T(4,128)(2,1)S(1)} %slice.3), channel_id=1, source_target_pairs={{0,8},{8,16},{16,24},{1,9},{9,17},{17,25},{2,10},{10,18},{18,26},{... | collective-permute-start | bytes 36872 | tf_op jit(solution)/shard_map/ppermute | solution.py:58
  7.8 0.6 copy-start.20
  13.3 5.0 %collective-permute-start.1 = (bf16[128,544]{1,0:T(8,128)(2,1)}, bf16[128,544]{1,0:T(8,128)(2,1)S(1)}, u32[]{:S(2)}, u32[]{:S(2)}) collective-permute-start(bf16[128,544]{1,0:T(8,128)(2,1)} %get-tuple-element.93), channel_id=1, source_target_pairs={{0,1},{1,0},{2,3},{3,2},{4,5},{5,4},{6,7},{7,6},{8,9},{9,8},{10,11... | collective-permute-start | bytes 417800 | tf_op jit(solution)/shard_map/ppermute | solution.py:716
  13.3 30.9 %collective-permute-start.4 = (bf16[128,2048]{1,0:T(8,128)(2,1)}, bf16[128,2048]{1,0:T(8,128)(2,1)S(1)}, u32[]{:S(2)}, u32[]{:S(2)}) collective-permute-start(bf16[128,2048]{1,0:T(8,128)(2,1)} %get-tuple-element.156.refs_5_.refs_3_.refs_4_), channel_id=1, source_target_pairs={{0,8},{8,0},{16,24},{24,16},{1,9},{9,1},{17,25},{25,17},{2,10},{10... | collective-permute-start | bytes 1572872 | tf_op jit(solution)/shard_map/ppermute | solution.py:716
  15.6 28.6 %collective-permute-start.5 = (bf16[128,2048]{1,0:T(8,128)(2,1)}, bf16[128,2048]{1,0:T(8,128)(2,1)S(1)}, u32[]{:S(2)}, u32[]{:S(2)}) collective-permute-start(bf16[128,2048]{1,0:T(8,128)(2,1)} %get-tuple-element.156.refs_5_.refs_3_.refs_4_), channel_id=1, source_target_pairs={{0,16},{8,24},{16,0},{24,8},{1,17},{9,25},{17,1},{25,9},{2,18},{10... | collective-permute-start | bytes 1572872 | tf_op jit(solution)/shard_map/ppermute | solution.py:716
  19.2 6.0 %collective-permute-start.2 = (bf16[128,544]{1,0:T(8,128)(2,1)S(1)}, bf16[128,544]{1,0:T(8,128)(2,1)S(1)}, u32[]{:S(2)}, u32[]{:S(2)}) collective-permute-start(bf16[128,544]{1,0:T(8,128)(2,1)S(1)} %add_convert_fusion.3), channel_id=1, source_target_pairs={{0,2},{1,3},{2,0},{3,1},{4,6},{5,7},{6,4},{7,5},{8,10},{9,11},{10,... | collective-permute-start | bytes 417800 | tf_op jit(solution)/shard_map/ppermute | solution.py:716
  25.3 5.4 %copy-start.2 = (bf16[128,544]{1,0:T(8,128)(2,1)}, bf16[128,544]{1,0:T(8,128)(2,1)S(1)}, u32[]{:S(2)}) copy-start(bf16[128,544]{1,0:T(8,128)(2,1)S(1)} %add_convert_fusion.2.refs_0_) | copy-start | bytes 417796
  25.3 5.4 %collective-permute-start.3 = (bf16[128,544]{1,0:T(8,128)(2,1)S(1)}, bf16[128,544]{1,0:T(8,128)(2,1)S(1)}, u32[]{:S(2)}, u32[]{:S(2)}) collective-permute-start(bf16[128,544]{1,0:T(8,128)(2,1)S(1)} %add_convert_fusion.2.refs_0_), channel_id=1, source_target_pairs={{0,4},{1,5},{2,6},{3,7},{4,0},{5,1},{6,2},{7,3},{8,12},{9,13},{10,... | collective-permute-start | bytes 417800 | tf_op jit(solution)/shard_map/ppermute | solution.py:716
  30.7 0.7 copy-start.15
  44.2 23.4 %copy-start.3 = (bf16[128,2048]{1,0:T(8,128)(2,1)}, bf16[128,2048]{1,0:T(8,128)(2,1)S(1)}, u32[]{:S(2)}) copy-start(bf16[128,2048]{1,0:T(8,128)(2,1)S(1)} %collective-permute-done.4.refs_5_) | copy-start | bytes 1572868
  44.2 23.4 %copy-start.4 = (bf16[128,2048]{1,0:T(8,128)(2,1)}, bf16[128,2048]{1,0:T(8,128)(2,1)S(1)}, u32[]{:S(2)}) copy-start(bf16[128,2048]{1,0:T(8,128)(2,1)S(1)} %collective-permute-done.5.refs_6_) | copy-start | bytes 1572868
  44.2 4.9 %collective-permute-start.6 = (bf16[2,18,8,128]{3,2,1,0:T(8,128)(2,1)}, bf16[2,18,8,128]{3,2,1,0:T(8,128)(2,1)S(1)}, u32[]{:S(2)}, u32[]{:S(2)}) collective-permute-start(bf16[2,18,8,128]{3,2,1,0:T(8,128)(2,1)} %get-tuple-element.100), channel_id=1, source_target_pairs={{0,8},{8,0},{16,24},{24,16},{1,9},{9,1},{17,25},{25,17},{2,10},{10... | collective-permute-start | bytes 221192 | tf_op jit(solution)/shard_map/ppermute | solution.py:716
  44.8 5.8 %collective-permute-start.7 = (bf16[2,18,8,128]{3,2,1,0:T(8,128)(2,1)}, bf16[2,18,8,128]{3,2,1,0:T(8,128)(2,1)S(1)}, u32[]{:S(2)}, u32[]{:S(2)}) collective-permute-start(bf16[2,18,8,128]{3,2,1,0:T(8,128)(2,1)} %get-tuple-element.101), channel_id=1, source_target_pairs={{0,16},{8,24},{16,0},{24,8},{1,17},{9,25},{17,1},{25,9},{2,18},{10... | collective-permute-start | bytes 221192 | tf_op jit(solution)/shard_map/ppermute | solution.py:716
  46.2 6.4 %collective-permute-start.8 = (bf16[2,18,8,128]{3,2,1,0:T(8,128)(2,1)}, bf16[2,18,8,128]{3,2,1,0:T(8,128)(2,1)S(1)}, u32[]{:S(2)}, u32[]{:S(2)}) collective-permute-start(bf16[2,18,8,128]{3,2,1,0:T(8,128)(2,1)} %get-tuple-element.102), channel_id=1, source_target_pairs={{0,24},{8,16},{16,8},{24,0},{1,25},{9,17},{17,9},{25,1},{2,26},{10... | collective-permute-start | bytes 221192 | tf_op jit(solution)/shard_map/ppermute | solution.py:716
  49.1 4.3 %copy-start.12 = (bf16[2,18,8,128]{3,2,1,0:T(8,128)(2,1)}, bf16[2,18,8,128]{3,2,1,0:T(8,128)(2,1)S(1)}, u32[]{:S(2)}) copy-start(bf16[2,18,8,128]{3,2,1,0:T(8,128)(2,1)S(1)} %collective-permute-done.6.refs_8_) | copy-start | bytes 221188
  50.5 2.9 %copy-start.13 = (bf16[2,18,8,128]{3,2,1,0:T(8,128)(2,1)}, bf16[2,18,8,128]{3,2,1,0:T(8,128)(2,1)S(1)}, u32[]{:S(2)}) copy-start(bf16[2,18,8,128]{3,2,1,0:T(8,128)(2,1)S(1)} %collective-permute-done.7.refs_9_) | copy-start | bytes 221188
  52.7 0.8 copy-start.14
  52.7 18.6 %collective-permute-start.9 = (bf16[128,2048]{1,0:T(8,128)(2,1)S(1)}, bf16[128,2048]{1,0:T(8,128)(2,1)S(1)}, u32[]{:S(2)}, u32[]{:S(2)}) collective-permute-start(bf16[128,2048]{1,0:T(8,128)(2,1)S(1)} %collective-permute-done.5.refs_6_), channel_id=1, source_target_pairs={{0,8},{8,0},{16,24},{24,16},{1,9},{9,1},{17,25},{25,17},{2,10},{10... | collective-permute-start | bytes 1572872 | tf_op jit(solution)/shard_map/ppermute | solution.py:716
  67.7 17.9 %collective-permute-start.10 = (bf16[144,1024]{1,0:T(8,128)(2,1)}, bf16[144,1024]{1,0:T(8,128)(2,1)S(1)}, u32[]{:S(2)}, u32[]{:S(2)}) collective-permute-start(bf16[144,1024]{1,0:T(8,128)(2,1)} %get-tuple-element.160.refs_8_), channel_id=1, source_target_pairs={{0,8},{8,0},{16,24},{24,16},{1,9},{9,1},{17,25},{25,17},{2,10},{10... | collective-permute-start | bytes 884744 | tf_op jit(solution)/shard_map/ppermute | solution.py:716
  69.0 16.6 %collective-permute-start.11 = (bf16[144,1024]{1,0:T(8,128)(2,1)}, bf16[144,1024]{1,0:T(8,128)(2,1)S(1)}, u32[]{:S(2)}, u32[]{:S(2)}) collective-permute-start(bf16[144,1024]{1,0:T(8,128)(2,1)} %get-tuple-element.160.refs_8_), channel_id=1, source_target_pairs={{0,16},{8,24},{16,0},{24,8},{1,17},{9,25},{17,1},{25,9},{2,18},{10... | collective-permute-start | bytes 884744 | tf_op jit(solution)/shard_map/ppermute | solution.py:716
  71.3 14.3 %copy-start.5 = (bf16[128,2048]{1,0:T(8,128)(2,1)}, bf16[128,2048]{1,0:T(8,128)(2,1)S(1)}, u32[]{:S(2)}) copy-start(bf16[128,2048]{1,0:T(8,128)(2,1)S(1)} %collective-permute-done.9.refs_7_) | copy-start | bytes 1572868
  85.6 40.4 %copy-start.6 = (bf16[144,1024]{1,0:T(8,128)(2,1)}, bf16[144,1024]{1,0:T(8,128)(2,1)S(1)}, u32[]{:S(2)}) copy-start(bf16[144,1024]{1,0:T(8,128)(2,1)S(1)} %collective-permute-done.10.refs_9_) | copy-start | bytes 884740
  85.6 40.4 %copy-start.7 = (bf16[144,1024]{1,0:T(8,128)(2,1)}, bf16[144,1024]{1,0:T(8,128)(2,1)S(1)}, u32[]{:S(2)}) copy-start(bf16[144,1024]{1,0:T(8,128)(2,1)S(1)} %collective-permute-done.11.refs_10_) | copy-start | bytes 884740
  85.6 1.7 %collective-permute-start.12 = (bf16[640,128]{1,0:T(8,128)(2,1)}, bf16[640,128]{1,0:T(8,128)(2,1)S(1)}, u32[]{:S(2)}, u32[]{:S(2)}) collective-permute-start(bf16[640,128]{1,0:T(8,128)(2,1)} %get-tuple-element.125), channel_id=1, source_target_pairs={{0,1},{1,0},{2,3},{3,2},{4,5},{5,4},{6,7},{7,6},{8,9},{9,8},{10,11... | collective-permute-start | bytes 491528 | tf_op jit(solution)/shard_map/ppermute | solution.py:716
  88.3 6.3 %collective-permute-start.13 = (bf16[640,128]{1,0:T(8,128)(2,1)S(1)}, bf16[640,128]{1,0:T(8,128)(2,1)S(1)}, u32[]{:S(2)}, u32[]{:S(2)}) collective-permute-start(bf16[640,128]{1,0:T(8,128)(2,1)S(1)} %add_convert_fusion.1), channel_id=1, source_target_pairs={{0,2},{1,3},{2,0},{3,1},{4,6},{5,7},{6,4},{7,5},{8,10},{9,11},{10,... | collective-permute-start | bytes 491528 | tf_op jit(solution)/shard_map/ppermute | solution.py:716
  89.8 21.6 %collective-permute-start.16 = (bf16[144,1024]{1,0:T(8,128)(2,1)}, bf16[144,1024]{1,0:T(8,128)(2,1)S(1)}, u32[]{:S(2)}, u32[]{:S(2)}) collective-permute-start(bf16[144,1024]{1,0:T(8,128)(2,1)} %get-tuple-element.164.refs_12_), channel_id=1, source_target_pairs={{0,8},{8,0},{16,24},{24,16},{1,9},{9,1},{17,25},{25,17},{2,10},{10... | collective-permute-start | bytes 884744 | tf_op jit(solution)/shard_map/ppermute | solution.py:716
  91.2 20.2 %collective-permute-start.17 = (bf16[144,1024]{1,0:T(8,128)(2,1)}, bf16[144,1024]{1,0:T(8,128)(2,1)S(1)}, u32[]{:S(2)}, u32[]{:S(2)}) collective-permute-start(bf16[144,1024]{1,0:T(8,128)(2,1)} %get-tuple-element.164.refs_12_), channel_id=1, source_target_pairs={{0,16},{8,24},{16,0},{24,8},{1,17},{9,25},{17,1},{25,9},{2,18},{10... | collective-permute-start | bytes 884744 | tf_op jit(solution)/shard_map/ppermute | solution.py:716
  91.2 20.2 %collective-permute-start.15 = (bf16[144,1024]{1,0:T(8,128)(2,1)S(1)}, bf16[144,1024]{1,0:T(8,128)(2,1)S(1)}, u32[]{:S(2)}, u32[]{:S(2)}) collective-permute-start(bf16[144,1024]{1,0:T(8,128)(2,1)S(1)} %collective-permute-done.11.refs_10_), channel_id=1, source_target_pairs={{0,8},{8,0},{16,24},{24,16},{1,9},{9,1},{17,25},{25,17},{2,10},{10... | collective-permute-start | bytes 884744 | tf_op jit(solution)/shard_map/ppermute | solution.py:716
  94.6 18.3 %copy-start = (bf16[640,128]{1,0:T(8,128)(2,1)}, bf16[640,128]{1,0:T(8,128)(2,1)S(1)}, u32[]{:S(2)}) copy-start(bf16[640,128]{1,0:T(8,128)(2,1)S(1)} %add_convert_fusion.back_a.refs_0_) | copy-start | bytes 491524
  94.6 16.8 %collective-permute-start.14 = (bf16[640,128]{1,0:T(8,128)(2,1)S(1)}, bf16[640,128]{1,0:T(8,128)(2,1)S(1)}, u32[]{:S(2)}, u32[]{:S(2)}) collective-permute-start(bf16[640,128]{1,0:T(8,128)(2,1)S(1)} %add_convert_fusion.back_a.refs_0_), channel_id=1, source_target_pairs={{0,4},{1,5},{2,6},{3,7},{4,0},{5,1},{6,2},{7,3},{8,12},{9,13},{10,... | collective-permute-start | bytes 491528 | tf_op jit(solution)/shard_map/ppermute | solution.py:716
  111.4 18.6 %copy-start.10 = (bf16[144,1024]{1,0:T(8,128)(2,1)}, bf16[144,1024]{1,0:T(8,128)(2,1)S(1)}, u32[]{:S(2)}) copy-start(bf16[144,1024]{1,0:T(8,128)(2,1)S(1)} %collective-permute-done.15.refs_11_) | copy-start | bytes 884740
  111.4 18.5 %copy-start.8 = (bf16[144,1024]{1,0:T(8,128)(2,1)}, bf16[144,1024]{1,0:T(8,128)(2,1)S(1)}, u32[]{:S(2)}) copy-start(bf16[144,1024]{1,0:T(8,128)(2,1)S(1)} %collective-permute-done.16.refs_13_) | copy-start | bytes 884740
  111.4 18.5 %copy-start.9 = (bf16[144,1024]{1,0:T(8,128)(2,1)}, bf16[144,1024]{1,0:T(8,128)(2,1)S(1)}, u32[]{:S(2)}) copy-start(bf16[144,1024]{1,0:T(8,128)(2,1)S(1)} %collective-permute-done.17.refs_14_) | copy-start | bytes 884740
  111.5 1.5 %copy-start.1 = (bf16[640,128]{1,0:T(8,128)(2,1)}, bf16[640,128]{1,0:T(8,128)(2,1)S(1)}, u32[]{:S(2)}) copy-start(bf16[640,128]{1,0:T(8,128)(2,1)S(1)} %collective-permute-done.14.back_b.refs_1_) | copy-start | bytes 491524
  111.5 14.6 %collective-permute-start.21 = (bf16[144,1024]{1,0:T(8,128)(2,1)S(1)}, bf16[144,1024]{1,0:T(8,128)(2,1)S(1)}, u32[]{:S(2)}, u32[]{:S(2)}) collective-permute-start(bf16[144,1024]{1,0:T(8,128)(2,1)S(1)} %collective-permute-done.17.refs_14_), channel_id=1, source_target_pairs={{0,8},{8,0},{16,24},{24,16},{1,9},{9,1},{17,25},{25,17},{2,10},{10... | collective-permute-start | bytes 884744 | tf_op jit(solution)/shard_map/ppermute | solution.py:716
  114.8 11.2 %collective-permute-start.18 = (bf16[288,128]{1,0:T(8,128)(2,1)}, bf16[288,128]{1,0:T(8,128)(2,1)S(1)}, u32[]{:S(2)}, u32[]{:S(2)}) collective-permute-start(bf16[288,128]{1,0:T(8,128)(2,1)} %get-tuple-element.139), channel_id=1, source_target_pairs={{0,8},{8,0},{16,24},{24,16},{1,9},{9,1},{17,25},{25,17},{2,10},{10... | collective-permute-start | bytes 221192 | tf_op jit(solution)/shard_map/ppermute | solution.py:716
  115.5 10.6 %collective-permute-start.19 = (bf16[288,128]{1,0:T(8,128)(2,1)}, bf16[288,128]{1,0:T(8,128)(2,1)S(1)}, u32[]{:S(2)}, u32[]{:S(2)}) collective-permute-start(bf16[288,128]{1,0:T(8,128)(2,1)} %get-tuple-element.140), channel_id=1, source_target_pairs={{0,16},{8,24},{16,0},{24,8},{1,17},{9,25},{17,1},{25,9},{2,18},{10... | collective-permute-start | bytes 221192 | tf_op jit(solution)/shard_map/ppermute | solution.py:716
  116.1 10.0 %collective-permute-start.20 = (bf16[288,128]{1,0:T(8,128)(2,1)}, bf16[288,128]{1,0:T(8,128)(2,1)S(1)}, u32[]{:S(2)}, u32[]{:S(2)}) collective-permute-start(bf16[288,128]{1,0:T(8,128)(2,1)} %get-tuple-element.141), channel_id=1, source_target_pairs={{0,24},{8,16},{16,8},{24,0},{1,25},{9,17},{17,9},{25,1},{2,26},{10... | collective-permute-start | bytes 221192 | tf_op jit(solution)/shard_map/ppermute | solution.py:716
  126.0 4.0 %copy-start.17 = (bf16[288,128]{1,0:T(8,128)(2,1)}, bf16[288,128]{1,0:T(8,128)(2,1)S(1)}, u32[]{:S(2)}) copy-start(bf16[288,128]{1,0:T(8,128)(2,1)S(1)} %collective-permute-done.18.refs_1_) | copy-start | bytes 221188
  126.0 3.9 %copy-start.18 = (bf16[288,128]{1,0:T(8,128)(2,1)}, bf16[288,128]{1,0:T(8,128)(2,1)S(1)}, u32[]{:S(2)}) copy-start(bf16[288,128]{1,0:T(8,128)(2,1)S(1)} %collective-permute-done.19.refs_2_) | copy-start | bytes 221188
  126.1 3.9 %copy-start.19 = (bf16[288,128]{1,0:T(8,128)(2,1)}, bf16[288,128]{1,0:T(8,128)(2,1)S(1)}, u32[]{:S(2)}) copy-start(bf16[288,128]{1,0:T(8,128)(2,1)S(1)} %collective-permute-done.20.refs_3_) | copy-start | bytes 221188
  126.1 3.9 %copy-start.11 = (bf16[144,1024]{1,0:T(8,128)(2,1)}, bf16[144,1024]{1,0:T(8,128)(2,1)S(1)}, u32[]{:S(2)}) copy-start(bf16[144,1024]{1,0:T(8,128)(2,1)S(1)} %collective-permute-done.21.refs_15_) | copy-start | bytes 884740
  126.1 8.9 %collective-permute-start.22 = (bf16[16,2048]{1,0:T(8,128)(2,1)}, bf16[16,2048]{1,0:T(8,128)(2,1)S(1)}, u32[]{:S(2)}, u32[]{:S(2)}) collective-permute-start(bf16[16,2048]{1,0:T(8,128)(2,1)} %get-tuple-element.149.refs_3_), channel_id=1, source_target_pairs={{0,8},{8,16},{16,24},{24,0},{1,9},{9,17},{17,25},{25,1},{2,10},{10... | collective-permute-start | bytes 196616 | tf_op jit(solution)/shard_map/ppermute | solution.py:52
  126.2 8.9 %collective-permute-start.23 = (bf16[16,2048]{1,0:T(8,128)(2,1)}, bf16[16,2048]{1,0:T(8,128)(2,1)S(1)}, u32[]{:S(2)}, u32[]{:S(2)}) collective-permute-start(bf16[16,2048]{1,0:T(8,128)(2,1)} %get-tuple-element.149.refs_3_), channel_id=1, source_target_pairs={{0,16},{8,24},{16,0},{24,8},{1,17},{9,25},{17,1},{25,9},{2,18},{10... | collective-permute-start | bytes 196616 | tf_op jit(solution)/shard_map/ppermute | solution.py:52
  128.0 7.0 %collective-permute-start.24 = (bf16[16,2048]{1,0:T(8,128)(2,1)}, bf16[16,2048]{1,0:T(8,128)(2,1)S(1)}, u32[]{:S(2)}, u32[]{:S(2)}) collective-permute-start(bf16[16,2048]{1,0:T(8,128)(2,1)} %get-tuple-element.149.refs_3_), channel_id=1, source_target_pairs={{0,24},{8,0},{16,8},{24,16},{1,25},{9,1},{17,9},{25,17},{2,26},{10... | collective-permute-start | bytes 196616 | tf_op jit(solution)/shard_map/ppermute | solution.py:52
  135.0 0.6 copy-start.21
  135.0 0.6 copy-start.22
  135.1 0.6 copy-start.23

commit v6 on v5

--- a/solution.py
+++ b/solution.py
@@ -44,7 +44,7 @@
 
 
 def sigmoid(v):
-    return 1.0 / (1.0 + jnp.exp(-v))
+    return 0.5 + 0.5 * jnp.tanh(0.5 * v)
 
 
 def rotate(block, axis, distance):
@@ -268,26 +268,11 @@
     )(*parts, step_weight, step_bias, decay, conv_out, gate, grad)
 
 
-def fold_sublanes(values):
-    rows = lax.broadcasted_iota(jnp.int32, (8, 128), 0)
-    if values[0].shape[0] != 8:
-        result = jnp.zeros((8, 128), F32)
-        for i, value in enumerate(values):
-            result = jnp.where(rows == i, jnp.sum(value, axis=0, keepdims=True), result)
-        return result
-    distance = 4
-    while len(values) > 1:
-        half = len(values) // 2
-        low = (rows & distance) == 0
-        values = [
-            jnp.where(low, a, b) + pltpu.roll(jnp.where(low, b, a), distance, 0)
-            if distance == 4
-            else jnp.where(low, a, pltpu.roll(b, distance, 0))
-            + jnp.where(low, pltpu.roll(a, 8 - distance, 0), b)
-            for a, b in zip(values[:half], values[half:])
-        ]
-        distance //= 2
-    return values[0]
+def fold_rows(products, base, groups, target, first):
+    total = products[pl.ds(base, 8, stride=groups), :]
+    for row in range(1, groups):
+        total = total + products[pl.ds(base + row, 8, stride=groups), :]
+    target[pl.ds(pl.multiple_of(first, 8), 8), :] = total
 
 
 def scan_kernel(places, states, opening, *refs):
@@ -297,7 +282,7 @@
         before_ref, refs = refs[0], refs[4:]
     (pre_ref, gate_out, scan_out, small_ref, part_ref) = refs[:5]
     refs = refs[5:]
-    (xs, dxs, gs, ys, dds, qs, decayed, coef_out, coef_in, rate, decay_acc, acc, ends) = refs
+    (xs, dxs, gs, ys, dds, qs, decayed, coef_out, coef_in, rate, decay_acc, acc, ends, products) = refs
     rows = conv_ref.shape[0]
     groups = decay_ref.shape[2]
     low_rank = weight_ref.shape[0]
@@ -345,16 +330,15 @@
             size, drive, grad = dt_ref[0, at, :], dxs[at, :], gs[at, :]
             result = jnp.zeros((groups, 128), F32)
             for lead in range(0, states, 8):
-                products = []
+                base = (sub * states + lead) * groups
                 for n in range(lead, lead + 8):
                     kept = jnp.exp2(size * rate[n]) * state[n]
                     decayed[token, n] = kept
                     state[n] = kept + drive * coef[token, n]
                     result = result + state[n] * coef[token, states + n]
-                    products.append(state[n] * grad)
-                coef_out[pl.ds(pl.multiple_of(token * states + lead, 8), 8), :] = fold_sublanes(
-                    products
-                )
+                    row = base + (n - lead) * groups
+                    products[row : row + groups, :] = state[n] * grad
+                fold_rows(products, base, groups, coef_out, token * states + lead)
             ys[at, :] = result
         return state
 
@@ -370,18 +354,18 @@
             slope = jnp.zeros((groups, 128), F32)
             inner = jnp.zeros((groups, 128), F32)
             for lead in range(0, states, 8):
-                products = []
+                base = (sub * states + lead) * groups
                 for n in range(lead, lead + 8):
                     adjoint = carry[n] + grad * coef[token, states + n]
-                    carry[n] = jnp.exp2(size * rate[n]) * adjoint
-                    weighted = adjoint * decayed[token, n]
-                    slope = slope + weighted * rate[n]
-                    gathered[n] = gathered[n] + weighted * size
+                    power = size * rate[n]
+                    carry[n] = jnp.exp2(power) * adjoint
+                    weighted = adjoint * decayed[token, n] * power
+                    slope = slope + weighted
+                    gathered[n] = gathered[n] + weighted
                     inner = inner + adjoint * coef[token, n]
-                    products.append(adjoint * drive)
-                coef_in[pl.ds(pl.multiple_of(token * states + lead, 8), 8), :] = fold_sublanes(
-                    products
-                )
+                    row = base + (n - lead) * groups
+                    products[row : row + groups, :] = adjoint * drive
+                fold_rows(products, base, groups, coef_in, token * states + lead)
             dds[at, :] = slope
             qs[at, :] = inner
         return carry, gathered
@@ -389,7 +373,7 @@
     zeros = [jnp.zeros((groups, 128), F32)] * states
     _, gathered = lax.fori_loop(0, rows // 8, backward, (carry, zeros))
     for n in range(states):
-        decay_acc[n * groups : n * groups + groups, :] = gathered[n] * (rate[n] * LN2)
+        decay_acc[n * groups : n * groups + groups, :] = gathered[n] * LN2
 
     for group in range(groups):
         pre_ref[rows : rows + states, group * 128 : group * 128 + 128] = decay_acc[
@@ -425,9 +409,9 @@
         grad = grad_ref[here, :].astype(F32)
         sig = sigmoid(gate)
         scan_grad = grad * gate * sig
-        tiny = size * (1.0 - 0.5 * size * (1.0 - size * (1.0 / 3.0) * (1.0 - 0.25 * size)))
-        step_slope = jnp.where(size < 0.03, tiny, 1.0 - jnp.exp(-size))
-        d_pre = (LN2 * slope + conv * inner) * step_slope
+        tiny = 1.0 - 0.5 * size * (1.0 - size * (1.0 / 3.0) * (1.0 - 0.25 * size))
+        ratio = jnp.where(size < 0.03, tiny, (1.0 - jnp.exp(-size)) / jnp.maximum(size, 0.03))
+        d_pre = (LN2 * slope + conv * inner * size) * ratio
         pre_ref[here, :] = d_pre.astype(BF)
         bias_sum = bias_sum + jnp.sum(d_pre, axis=0, keepdims=True)
         skip_sum = skip_sum + jnp.sum(scan_grad * conv, axis=0, keepdims=True)
@@ -524,6 +508,7 @@
             pltpu.VMEM((states * groups, 128), F32),
             pltpu.VMEM((wide, rows), F32),
             pltpu.VMEM((places, states + 2, groups, 128), F32),
+            pltpu.VMEM((8 * states * groups, 128), F32),
         ],
         input_output_aliases=aliases,
         compiler_params=params(),
@@ -790,7 +775,11 @@
         fresh = spread(message)
     part, grad_gate, scan_part, small = previous
     backs = chan_sum(part)
-    backs, steps, fresh = tie((backs, steps, fresh))
+    if places == 4:
+        backs, steps, far = tie((backs, steps, fresh[2]))
+        fresh = fresh[:2] + [far]
+    else:
+        backs, steps, fresh = tie((backs, steps, fresh))
     steps += spread_on(fresh)
     cuts = cut_call(places, backs, low_t)
     cuts = [cuts[0]] + [swap(cut, "ctx", mask) for mask, cut in enumerate(cuts[1:], 1)]

time: 138 us -> 134 us (0.971)
  waiting for transfers between devices: 32 us -> 28.9 us
    ppermute x21, waiting for transfers between devices: 30.5 us -> 27.5 us  [swap(): lax.ppermute(block, axis, [(i, i ^ mask) for i in range(lax.axis_size(axi...]
  transfers between devices with their start and end apart: 25 -> 25, of which waited for: 9 -> 12; matrix products, arithmetic and copies ran while one was open for 1% -> 1% of each run, Pallas kernels for 40% -> 41%
where the time goes in v6:
time: 134 us
  Pallas kernels  60.8 us (45%)
  starting transfers between devices  36.9 us (28%)
  waiting for transfers between devices  28.9 us (22%)
  local copies, waits for them, and re-layouts  4.09 us (3%)
  other arithmetic  2.02 us (2%)
    pallas_call x2, Pallas kernels, scan_call(): pl.pallas_call(functools.partial(scan_kernel, places, states, first), gri...  27.9 us
    ppermute x21, starting transfers between devices, swap(): lax.ppermute(block, axis, [(i, i ^ mask) for i in range(lax.axis_size(axi...  27.5 us
    ppermute x21, waiting for transfers between devices, swap(): lax.ppermute(block, axis, [(i, i ^ mask) for i in range(lax.axis_size(axi...  27.5 us
    pallas_call x1, Pallas kernels, local_call(): pl.pallas_call(functools.partial(local_kernel, low_rank, states, places),...  12.8 us
    pallas_call x1, Pallas kernels, conv_grad_call(): pl.pallas_call(functools.partial(conv_grad_kernel, places, low_rank), gri...  6.75 us
    pallas_call x1, Pallas kernels, rows_call(): pl.pallas_call(functools.partial(rows_kernel, places, rank_rows, chunks),...  4.99 us
    ppermute x1, starting transfers between devices, shift(): return lax.ppermute(block, axis, route)  4.93 us
    pallas_call x1, Pallas kernels, conv_call(): pl.pallas_call(conv_kernel, grid=(chans // width,), in_specs=[columns(row...  4.83 us
  transfers between devices with their start and end apart: 25, of which 12 were waited for; matrix products, arithmetic and copies ran while one was open for 1% of the time, Pallas kernels for 41%

profile of v6, /device:TPU:0, one launch (start us, length us, event | category | flops | bytes accessed | tf_op | source)
XLA Modules:
  0.0 133.6 jit_solution(4686180144120204479)
XLA Ops:
  0.7 0.8 slice.3
  1.5 4.9 %collective-permute-start = (bf16[3,2048]{1,0:T(4,128)(2,1)S(1)}, bf16[3,2048]{1,0:T(4,128)(2,1)S(1)}, u32[]{:S(2)}, u32[]{:S(2)}) collective-permute-start(bf16[3,2048]{1,0:T(4,128)(2,1)S(1)} %slice.3), channel_id=1, source_target_pairs={{0,8},{8,16},{16,24},{1,9},{9,17},{17,25},{2,10},{10,18},{18,26},{... | collective-permute-start | bytes 36872 | tf_op jit(solution)/shard_map/ppermute | solution.py:58
  6.4 1.4 %collective-permute-done.rim_ref = bf16[3,2048]{1,0:T(4,128)(2,1)S(1)} collective-permute-done((bf16[3,2048]{1,0:T(4,128)(2,1)S(1)}, bf16[3,2048]{1,0:T(4,128)(2,1)S(1)}, u32[]{:S(2)}, u32[]{:S(2)}) %collective-permute-start) | collective-permute-done | bytes 12320 | tf_op jit(solution)/shard_map/ppermute | solution.py:58
  7.8 0.6 copy-done.20
  8.4 4.8 %conv_project.1 = (bf16[128,2048]{1,0:T(8,128)(2,1)}, bf16[128,544]{1,0:T(8,128)(2,1)}) custom-call(bf16[128,2048]{1,0:T(8,128)(2,1)} %input_ref.3, bf16[3,2048]{1,0:T(4,128)(2,1)} %copy-done.20, f32[4,2048]{1,0:T(4,128)} %refs_2_.3, f32[1,2048]{1,0:T(1,128)} %bitcast.19, bf16[544,2048]{1,0:T(8,128)(2,1)} %proj_ref.3), custom_call_target="tpu_custom_call" | custom-call | tf_op jit(solution)/shard_map/conv_project/pallas_call | solution.py:103
  13.3 0.0 collective-permute-start.1
  13.3 2.4 %collective-permute-start.4 = (bf16[128,2048]{1,0:T(8,128)(2,1)}, bf16[128,2048]{1,0:T(8,128)(2,1)S(1)}, u32[]{:S(2)}, u32[]{:S(2)}) collective-permute-start(bf16[128,2048]{1,0:T(8,128)(2,1)} %get-tuple-element.152.refs_5_.refs_3_.refs_4_), channel_id=1, source_target_pairs={{0,8},{8,0},{16,24},{24,16},{1,9},{9,1},{17,25},{25,17},{2,10},{10... | collective-permute-start | bytes 1572872 | tf_op jit(solution)/shard_map/ppermute | solution.py:701
  15.6 2.6 %collective-permute-start.5 = (bf16[128,2048]{1,0:T(8,128)(2,1)}, bf16[128,2048]{1,0:T(8,128)(2,1)S(1)}, u32[]{:S(2)}, u32[]{:S(2)}) collective-permute-start(bf16[128,2048]{1,0:T(8,128)(2,1)} %get-tuple-element.152.refs_5_.refs_3_.refs_4_), channel_id=1, source_target_pairs={{0,16},{8,24},{16,0},{24,8},{1,17},{9,25},{17,1},{25,9},{2,18},{10... | collective-permute-start | bytes 1572872 | tf_op jit(solution)/shard_map/ppermute | solution.py:701
  18.2 1.0 add_convert_fusion.3
  19.2 1.6 %collective-permute-start.2 = (bf16[128,544]{1,0:T(8,128)(2,1)S(1)}, bf16[128,544]{1,0:T(8,128)(2,1)S(1)}, u32[]{:S(2)}, u32[]{:S(2)}) collective-permute-start(bf16[128,544]{1,0:T(8,128)(2,1)S(1)} %add_convert_fusion.3), channel_id=1, source_target_pairs={{0,2},{1,3},{2,0},{3,1},{4,6},{5,7},{6,4},{7,5},{8,10},{9,11},{10,... | collective-permute-start | bytes 417800 | tf_op jit(solution)/shard_map/ppermute | solution.py:701
  20.7 4.5 %collective-permute-done.2 = bf16[128,544]{1,0:T(8,128)(2,1)S(1)} collective-permute-done((bf16[128,544]{1,0:T(8,128)(2,1)S(1)}, bf16[128,544]{1,0:T(8,128)(2,1)S(1)}, u32[]{:S(2)}, u32[]{:S(2)}) %collective-permute-start.2) | collective-permute-done | bytes 139296 | tf_op jit(solution)/shard_map/ppermute | solution.py:701
  25.3 0.0 copy-start.2
  25.3 1.6 %collective-permute-start.3 = (bf16[128,544]{1,0:T(8,128)(2,1)S(1)}, bf16[128,544]{1,0:T(8,128)(2,1)S(1)}, u32[]{:S(2)}, u32[]{:S(2)}) collective-permute-start(bf16[128,544]{1,0:T(8,128)(2,1)S(1)} %add_convert_fusion.2.refs_0_), channel_id=1, source_target_pairs={{0,4},{1,5},{2,6},{3,7},{4,0},{5,1},{6,2},{7,3},{8,12},{9,13},{10,... | collective-permute-start | bytes 417800 | tf_op jit(solution)/shard_map/ppermute | solution.py:701
  26.9 0.7 copy.27
  27.6 3.1 %collective-permute-done.3.refs_1_ = bf16[128,544]{1,0:T(8,128)(2,1)S(1)} collective-permute-done((bf16[128,544]{1,0:T(8,128)(2,1)S(1)}, bf16[128,544]{1,0:T(8,128)(2,1)S(1)}, u32[]{:S(2)}, u32[]{:S(2)}) %collective-permute-start.3) | collective-permute-done | bytes 139296 | tf_op jit(solution)/shard_map/ppermute | solution.py:701
  30.7 0.7 copy-done.15
  31.3 12.8 %local_ends.1 = (f32[2,1024,128]{2,1,0:T(8,128)}, f32[128,128]{1,0:T(8,128)}, bf16[128,512]{1,0:T(8,128)(2,1)}, bf16[512,128]{1,0:T(8,128)(2,1)}, bf16[2,18,8,12...) custom-call(bf16[128,544]{1,0:T(8,128)(2,1)} %copy-done.2, ...), custom_call_target="tpu_custom_call" | custom-call | tf_op jit(solution)/shard_map/local_ends/pallas_call | solution.py:228
  44.2 0.0 collective-permute-done.4.refs_5_
  44.2 0.5 collective-permute-start.6
  44.7 1.4 %collective-permute-start.7 = (bf16[2,18,8,128]{3,2,1,0:T(8,128)(2,1)}, bf16[2,18,8,128]{3,2,1,0:T(8,128)(2,1)S(1)}, u32[]{:S(2)}, u32[]{:S(2)}) collective-permute-start(bf16[2,18,8,128]{3,2,1,0:T(8,128)(2,1)} %get-tuple-element.99), channel_id=1, source_target_pairs={{0,16},{8,24},{16,0},{24,8},{1,17},{9,25},{17,1},{25,9},{2,18},{10... | collective-permute-start | bytes 221192 | tf_op jit(solution)/shard_map/ppermute | solution.py:701
  46.2 2.5 %collective-permute-start.8 = (bf16[2,18,8,128]{3,2,1,0:T(8,128)(2,1)}, bf16[2,18,8,128]{3,2,1,0:T(8,128)(2,1)S(1)}, u32[]{:S(2)}, u32[]{:S(2)}) collective-permute-start(bf16[2,18,8,128]{3,2,1,0:T(8,128)(2,1)} %get-tuple-element.100), channel_id=1, source_target_pairs={{0,24},{8,16},{16,8},{24,0},{1,25},{9,17},{17,9},{25,1},{2,26},{10... | collective-permute-start | bytes 221192 | tf_op jit(solution)/shard_map/ppermute | solution.py:701
  48.7 0.4 collective-permute-done.6.refs_8_
  49.1 1.4 %collective-permute-done.7.refs_9_ = bf16[2,18,8,128]{3,2,1,0:T(8,128)(2,1)S(1)} collective-permute-done((bf16[2,18,8,128]{3,2,1,0:T(8,128)(2,1)}, bf16[2,18,8,128]{3,2,1,0:T(8,128)(2,1)S(1)}, u32[]{:S(2)}, u32[]{:S(2)}) %collective-permute-start.7) | collective-permute-done | bytes 73760 | tf_op jit(solution)/shard_map/ppermute | solution.py:701
  50.5 2.1 %collective-permute-done.8.refs_10_ = bf16[2,18,8,128]{3,2,1,0:T(8,128)(2,1)S(1)} collective-permute-done((bf16[2,18,8,128]{3,2,1,0:T(8,128)(2,1)}, bf16[2,18,8,128]{3,2,1,0:T(8,128)(2,1)S(1)}, u32[]{:S(2)}, u32[]{:S(2)}) %collective-permute-start.8) | collective-permute-done | bytes 73760 | tf_op jit(solution)/shard_map/ppermute | solution.py:701
  52.6 0.8 collective-permute-start.9
  53.4 13.9 %scan_gradients.2 = (bf16[144,1024]{1,0:T(8,128)(2,1)}, bf16[128,2048]{1,0:T(8,128)(2,1)}, bf16[128,2048]{1,0:T(8,128)(2,1)}, f32[8,2048]{1,0:T(8,128)}, f32[640,128]{1,0:T(8,128)}) custom-call(f32[128,128]{1,0:T(8,128)} %get-tuple-element.93.refs_0_, f32[2,1024,128]{2,1,0:T(8,128)} %get-tuple-element.94.refs_1_, f32[2,16,8,128]{3,2,1,0:T(8,128)} %bitcast.13, ...), custom_call_target="tpu_custom_call" | custom-call | tf_op jit(solution)/shard_map/scan_gradients/pallas_call | solution.py:479
  67.3 1.3 collective-permute-start.10
  68.6 2.3 %collective-permute-start.11 = (bf16[144,1024]{1,0:T(8,128)(2,1)}, bf16[144,1024]{1,0:T(8,128)(2,1)S(1)}, u32[]{:S(2)}, u32[]{:S(2)}) collective-permute-start(bf16[144,1024]{1,0:T(8,128)(2,1)} %get-tuple-element.156.refs_8_), channel_id=1, source_target_pairs={{0,16},{8,24},{16,0},{24,8},{1,17},{9,25},{17,1},{25,9},{2,18},{10... | collective-permute-start | bytes 884744 | tf_op jit(solution)/shard_map/ppermute | solution.py:701
  71.0 0.0 collective-permute-done.9.refs_7_
  71.0 14.0 %scan_gradients.3 = (bf16[144,1024]{1,0:T(8,128)(2,1)}, bf16[128,2048]{1,0:T(8,128)(2,1)}, bf16[128,2048]{1,0:T(8,128)(2,1)}, f32[8,2048]{1,0:T(8,128)}, bf16[640,128]{1,0:T(8,128)(2,1)}) custom-call(f32[128,128]{1,0:T(8,128)} %get-tuple-element.93.refs_0_, ...), custom_call_target="tpu_custom_call", output_to_operand_aliasing={{1}: (12, {}), {2}: (13, {}), {3}: (14, {})} | custom-call | tf_op jit(solution)/shard_map/scan_gradients/pallas_call | solution.py:479
  85.0 0.0 collective-permute-done.11.refs_10_
  85.0 0.1 collective-permute-start.12
  85.1 1.6 %collective-permute-done.12 = bf16[640,128]{1,0:T(8,128)(2,1)S(1)} collective-permute-done((bf16[640,128]{1,0:T(8,128)(2,1)}, bf16[640,128]{1,0:T(8,128)(2,1)S(1)}, u32[]{:S(2)}, u32[]{:S(2)}) %collective-permute-start.12) | collective-permute-done | bytes 163872 | tf_op jit(solution)/shard_map/ppermute | solution.py:701
  86.7 1.0 add_convert_fusion.1
  87.7 1.6 %collective-permute-start.13 = (bf16[640,128]{1,0:T(8,128)(2,1)S(1)}, bf16[640,128]{1,0:T(8,128)(2,1)S(1)}, u32[]{:S(2)}, u32[]{:S(2)}) collective-permute-start(bf16[640,128]{1,0:T(8,128)(2,1)S(1)} %add_convert_fusion.1), channel_id=1, source_target_pairs={{0,2},{1,3},{2,0},{3,1},{4,6},{5,7},{6,4},{7,5},{8,10},{9,11},{10,... | collective-permute-start | bytes 491528 | tf_op jit(solution)/shard_map/ppermute | solution.py:701
  89.2 1.4 %collective-permute-start.15 = (bf16[144,1024]{1,0:T(8,128)(2,1)S(1)}, bf16[144,1024]{1,0:T(8,128)(2,1)S(1)}, u32[]{:S(2)}, u32[]{:S(2)}) collective-permute-start(bf16[144,1024]{1,0:T(8,128)(2,1)S(1)} %collective-permute-done.11.refs_10_), channel_id=1, source_target_pairs={{0,8},{8,0},{16,24},{24,16},{1,9},{9,1},{17,25},{25,17},{2,10},{10... | collective-permute-start | bytes 884744 | tf_op jit(solution)/shard_map/ppermute | solution.py:701
  90.6 0.0 collective-permute-start.16
  90.6 3.3 %collective-permute-done.13 = bf16[640,128]{1,0:T(8,128)(2,1)S(1)} collective-permute-done((bf16[640,128]{1,0:T(8,128)(2,1)S(1)}, bf16[640,128]{1,0:T(8,128)(2,1)S(1)}, u32[]{:S(2)}, u32[]{:S(2)}) %collective-permute-start.13) | collective-permute-done | bytes 163872 | tf_op jit(solution)/shard_map/ppermute | solution.py:701
  94.0 0.0 copy-start
  94.0 1.6 %collective-permute-start.14 = (bf16[640,128]{1,0:T(8,128)(2,1)S(1)}, bf16[640,128]{1,0:T(8,128)(2,1)S(1)}, u32[]{:S(2)}, u32[]{:S(2)}) collective-permute-start(bf16[640,128]{1,0:T(8,128)(2,1)S(1)} %add_convert_fusion.back_a.refs_0_), channel_id=1, source_target_pairs={{0,4},{1,5},{2,6},{3,7},{4,0},{5,1},{6,2},{7,3},{8,12},{9,13},{10,... | collective-permute-start | bytes 491528 | tf_op jit(solution)/shard_map/ppermute | solution.py:701
  95.6 1.4 %collective-permute-start.20 = (bf16[144,1024]{1,0:T(8,128)(2,1)}, bf16[144,1024]{1,0:T(8,128)(2,1)S(1)}, u32[]{:S(2)}, u32[]{:S(2)}) collective-permute-start(bf16[144,1024]{1,0:T(8,128)(2,1)} %get-tuple-element.160.refs_12_), channel_id=1, source_target_pairs={{0,8},{8,0},{16,24},{24,16},{1,9},{9,1},{17,25},{25,17},{2,10},{10... | collective-permute-start | bytes 884744 | tf_op jit(solution)/shard_map/ppermute | solution.py:701
  97.0 6.2 %collective-permute-done.15.refs_11_ = bf16[144,1024]{1,0:T(8,128)(2,1)S(1)} collective-permute-done((bf16[144,1024]{1,0:T(8,128)(2,1)S(1)}, bf16[144,1024]{1,0:T(8,128)(2,1)S(1)}, u32[]{:S(2)}, u32[]{:S(2)}) %collective-permute-start.15) | collective-permute-done | bytes 294944 | tf_op jit(solution)/shard_map/ppermute | solution.py:701
  103.2 3.5 %collective-permute-done.16.refs_14_ = bf16[144,1024]{1,0:T(8,128)(2,1)S(1)} collective-permute-done((bf16[144,1024]{1,0:T(8,128)(2,1)}, bf16[144,1024]{1,0:T(8,128)(2,1)S(1)}, u32[]{:S(2)}, u32[]{:S(2)}) %collective-permute-start.16) | collective-permute-done | bytes 294944 | tf_op jit(solution)/shard_map/ppermute | solution.py:701
  106.7 0.0 collective-permute-done.14.back_b.refs_1_
  106.7 0.1 collective-permute-start.21
  106.8 0.6 copy-done.1
  107.4 1.9 %cut_rows.1 = (bf16[288,128]{1,0:T(8,128)(2,1)}, bf16[288,128]{1,0:T(8,128)(2,1)}, bf16[288,128]{1,0:T(8,128)(2,1)}, bf16[288,128]{1,0:T(8,128)(2,1)}) custom-call(bf16[640,128]{1,0:T(8,128)(2,1)} %copy-done, bf16[640,128]{1,0:T(8,128)(2,1)} %copy-done.1, bf16[512,128]{1,0:T(8,128)(2,1)} %get-tuple-element.135.refs_2_), custom_call_target="tpu_custom_call" | custom-call | tf_op jit(solution)/shard_map/cut_rows/pallas_call | solution.py:597
  109.3 1.4 %collective-permute-start.17 = (bf16[288,128]{1,0:T(8,128)(2,1)}, bf16[288,128]{1,0:T(8,128)(2,1)S(1)}, u32[]{:S(2)}, u32[]{:S(2)}) collective-permute-start(bf16[288,128]{1,0:T(8,128)(2,1)} %get-tuple-element.137), channel_id=1, source_target_pairs={{0,8},{8,0},{16,24},{24,16},{1,9},{9,1},{17,25},{25,17},{2,10},{10... | collective-permute-start | bytes 221192 | tf_op jit(solution)/shard_map/ppermute | solution.py:701
  110.7 1.0 collective-permute-start.18
  111.7 1.9 %collective-permute-start.19 = (bf16[288,128]{1,0:T(8,128)(2,1)}, bf16[288,128]{1,0:T(8,128)(2,1)S(1)}, u32[]{:S(2)}, u32[]{:S(2)}) collective-permute-start(bf16[288,128]{1,0:T(8,128)(2,1)} %get-tuple-element.139), channel_id=1, source_target_pairs={{0,24},{8,16},{16,8},{24,0},{1,25},{9,17},{17,9},{25,1},{2,26},{10... | collective-permute-start | bytes 221192 | tf_op jit(solution)/shard_map/ppermute | solution.py:701
  113.6 6.7 %conv_gradients.1 = (bf16[128,2048]{1,0:T(8,128)(2,1)}, f32[16,2048]{1,0:T(8,128)}, bf16[16,2048]{1,0:T(8,128)(2,1)}) custom-call(bf16[640,128]{1,0:T(8,128)(2,1)} %copy-done, bf16[640,128]{1,0:T(8,128)(2,1)} %copy-done.1, bf16[544,2048]{1,0:T(8,128)(2,1)} %proj_ref.3, bf16[128,2048]{1,0:T(8,128)(2,1)} %get-tuple-element.130.scan_ref, ...), custom_call_target="tpu_custom_call" | custom-call | tf_op jit(solution)/shard_map/conv_gradients/pallas_call | solution.py:560
  120.4 0.5 collective-permute-done.17.refs_1_
  120.9 0.8 collective-permute-done.19.refs_3_
  121.8 0.0 collective-permute-done.21.refs_15_
  121.8 0.1 collective-permute-start.22
  121.8 3.7 %collective-permute-start.23 = (bf16[16,2048]{1,0:T(8,128)(2,1)}, bf16[16,2048]{1,0:T(8,128)(2,1)S(1)}, u32[]{:S(2)}, u32[]{:S(2)}) collective-permute-start(bf16[16,2048]{1,0:T(8,128)(2,1)} %get-tuple-element.145.refs_3_), channel_id=1, source_target_pairs={{0,16},{8,24},{16,0},{24,8},{1,17},{9,25},{17,1},{25,9},{2,18},{10... | collective-permute-start | bytes 196616 | tf_op jit(solution)/shard_map/ppermute | solution.py:52
  125.5 0.7 collective-permute-start.24
  126.3 5.0 %row_gradients.1 = (f32[128,2048]{1,0:T(8,128)}, f32[8,2048]{1,0:T(8,128)}, f32[128,2048]{1,0:T(8,128)}, f32[16,2048]{1,0:T(8,128)}) custom-call(bf16[288,128]{1,0:T(8,128)(2,1)} %get-tuple-element.148.refs_0_, bf16[288,128]{1,0:T(8,128)(2,1)} %copy-done.17, bf16[288,128]{1,0:T(8,128)(2,1)} %copy-done.18, bf16[288,128]{1,0:T(8,128)(2,1)} %copy-done.19, ...), custom_call_target="tpu_custom_call" | custom-call | tf_op jit(solution)/shard_map/row_gradients/pallas_call | solution.py:638
  131.3 0.0 collective-permute-done.23.refs_5_
  131.3 0.0 collective-permute-done.24.refs_6_
  131.3 0.6 copy-done.21
  131.9 0.0 copy-done.22
  131.9 0.0 copy-done.23
  131.9 1.7 %last_rows.1 = (bf16[128,2048]{1,0:T(8,128)(2,1)}, f32[4,2048]{1,0:T(4,128)}, f32[1,2048]{1,0:T(1,128)}, f32[1,2048]{1,0:T(1,128)}, f32[1,2048]{1,0:T(1,128)}) custom-call(bf16[128,2048]{1,0:T(8,128)(2,1)} %get-tuple-element.132.refs_0_, f32[16,2048]{1,0:T(8,128)} %get-tuple-element.133.refs_1_, f32[4,2048]{1,0:T(4,128)} %refs_2_.3, ...), custom_call_target="tpu_custom_call", output_to_operand_aliasing={{0}: (0, {})} | custom-call | tf_op jit(solution)/shard_map/last_rows/pallas_call | solution.py:678
  (49 shorter events, 0.2 us)
Async XLA Ops:
  0.6 26.2 %copy-start.16 = (f32[16,2048]{1,0:T(8,128)S(1)}, f32[16,2048]{1,0:T(8,128)}, u32[]{:S(2)}) copy-start(f32[16,2048]{1,0:T(8,128)} %param.18) | copy-start | bytes 393220
  1.5 6.4 %collective-permute-start = (bf16[3,2048]{1,0:T(4,128)(2,1)S(1)}, bf16[3,2048]{1,0:T(4,128)(2,1)S(1)}, u32[]{:S(2)}, u32[]{:S(2)}) collective-permute-start(bf16[3,2048]{1,0:T(4,128)(2,1)S(1)} %slice.3), channel_id=1, source_target_pairs={{0,8},{8,16},{16,24},{1,9},{9,17},{17,25},{2,10},{10,18},{18,26},{... | collective-permute-start | bytes 36872 | tf_op jit(solution)/shard_map/ppermute | solution.py:58
  7.8 0.6 copy-start.20
  13.3 5.0 %collective-permute-start.1 = (bf16[128,544]{1,0:T(8,128)(2,1)}, bf16[128,544]{1,0:T(8,128)(2,1)S(1)}, u32[]{:S(2)}, u32[]{:S(2)}) collective-permute-start(bf16[128,544]{1,0:T(8,128)(2,1)} %get-tuple-element.91), channel_id=1, source_target_pairs={{0,1},{1,0},{2,3},{3,2},{4,5},{5,4},{6,7},{7,6},{8,9},{9,8},{10,11... | collective-permute-start | bytes 417800 | tf_op jit(solution)/shard_map/ppermute | solution.py:701
  13.3 30.9 %collective-permute-start.4 = (bf16[128,2048]{1,0:T(8,128)(2,1)}, bf16[128,2048]{1,0:T(8,128)(2,1)S(1)}, u32[]{:S(2)}, u32[]{:S(2)}) collective-permute-start(bf16[128,2048]{1,0:T(8,128)(2,1)} %get-tuple-element.152.refs_5_.refs_3_.refs_4_), channel_id=1, source_target_pairs={{0,8},{8,0},{16,24},{24,16},{1,9},{9,1},{17,25},{25,17},{2,10},{10... | collective-permute-start | bytes 1572872 | tf_op jit(solution)/shard_map/ppermute | solution.py:701
  15.6 28.6 %collective-permute-start.5 = (bf16[128,2048]{1,0:T(8,128)(2,1)}, bf16[128,2048]{1,0:T(8,128)(2,1)S(1)}, u32[]{:S(2)}, u32[]{:S(2)}) collective-permute-start(bf16[128,2048]{1,0:T(8,128)(2,1)} %get-tuple-element.152.refs_5_.refs_3_.refs_4_), channel_id=1, source_target_pairs={{0,16},{8,24},{16,0},{24,8},{1,17},{9,25},{17,1},{25,9},{2,18},{10... | collective-permute-start | bytes 1572872 | tf_op jit(solution)/shard_map/ppermute | solution.py:701
  19.2 6.0 %collective-permute-start.2 = (bf16[128,544]{1,0:T(8,128)(2,1)S(1)}, bf16[128,544]{1,0:T(8,128)(2,1)S(1)}, u32[]{:S(2)}, u32[]{:S(2)}) collective-permute-start(bf16[128,544]{1,0:T(8,128)(2,1)S(1)} %add_convert_fusion.3), channel_id=1, source_target_pairs={{0,2},{1,3},{2,0},{3,1},{4,6},{5,7},{6,4},{7,5},{8,10},{9,11},{10,... | collective-permute-start | bytes 417800 | tf_op jit(solution)/shard_map/ppermute | solution.py:701
  25.3 5.4 %copy-start.2 = (bf16[128,544]{1,0:T(8,128)(2,1)}, bf16[128,544]{1,0:T(8,128)(2,1)S(1)}, u32[]{:S(2)}) copy-start(bf16[128,544]{1,0:T(8,128)(2,1)S(1)} %add_convert_fusion.2.refs_0_) | copy-start | bytes 417796
  25.3 5.4 %collective-permute-start.3 = (bf16[128,544]{1,0:T(8,128)(2,1)S(1)}, bf16[128,544]{1,0:T(8,128)(2,1)S(1)}, u32[]{:S(2)}, u32[]{:S(2)}) collective-permute-start(bf16[128,544]{1,0:T(8,128)(2,1)S(1)} %add_convert_fusion.2.refs_0_), channel_id=1, source_target_pairs={{0,4},{1,5},{2,6},{3,7},{4,0},{5,1},{6,2},{7,3},{8,12},{9,13},{10,... | collective-permute-start | bytes 417800 | tf_op jit(solution)/shard_map/ppermute | solution.py:701
  30.7 0.7 copy-start.15
  44.2 23.2 %copy-start.3 = (bf16[128,2048]{1,0:T(8,128)(2,1)}, bf16[128,2048]{1,0:T(8,128)(2,1)S(1)}, u32[]{:S(2)}) copy-start(bf16[128,2048]{1,0:T(8,128)(2,1)S(1)} %collective-permute-done.4.refs_5_) | copy-start | bytes 1572868
  44.2 23.1 %copy-start.4 = (bf16[128,2048]{1,0:T(8,128)(2,1)}, bf16[128,2048]{1,0:T(8,128)(2,1)S(1)}, u32[]{:S(2)}) copy-start(bf16[128,2048]{1,0:T(8,128)(2,1)S(1)} %collective-permute-done.5.refs_6_) | copy-start | bytes 1572868
  44.2 4.9 %collective-permute-start.6 = (bf16[2,18,8,128]{3,2,1,0:T(8,128)(2,1)}, bf16[2,18,8,128]{3,2,1,0:T(8,128)(2,1)S(1)}, u32[]{:S(2)}, u32[]{:S(2)}) collective-permute-start(bf16[2,18,8,128]{3,2,1,0:T(8,128)(2,1)} %get-tuple-element.98), channel_id=1, source_target_pairs={{0,8},{8,0},{16,24},{24,16},{1,9},{9,1},{17,25},{25,17},{2,10},{10... | collective-permute-start | bytes 221192 | tf_op jit(solution)/shard_map/ppermute | solution.py:701
  44.7 5.8 %collective-permute-start.7 = (bf16[2,18,8,128]{3,2,1,0:T(8,128)(2,1)}, bf16[2,18,8,128]{3,2,1,0:T(8,128)(2,1)S(1)}, u32[]{:S(2)}, u32[]{:S(2)}) collective-permute-start(bf16[2,18,8,128]{3,2,1,0:T(8,128)(2,1)} %get-tuple-element.99), channel_id=1, source_target_pairs={{0,16},{8,24},{16,0},{24,8},{1,17},{9,25},{17,1},{25,9},{2,18},{10... | collective-permute-start | bytes 221192 | tf_op jit(solution)/shard_map/ppermute | solution.py:701
  46.2 6.4 %collective-permute-start.8 = (bf16[2,18,8,128]{3,2,1,0:T(8,128)(2,1)}, bf16[2,18,8,128]{3,2,1,0:T(8,128)(2,1)S(1)}, u32[]{:S(2)}, u32[]{:S(2)}) collective-permute-start(bf16[2,18,8,128]{3,2,1,0:T(8,128)(2,1)} %get-tuple-element.100), channel_id=1, source_target_pairs={{0,24},{8,16},{16,8},{24,0},{1,25},{9,17},{17,9},{25,1},{2,26},{10... | collective-permute-start | bytes 221192 | tf_op jit(solution)/shard_map/ppermute | solution.py:701
  49.1 4.3 %copy-start.12 = (bf16[2,18,8,128]{3,2,1,0:T(8,128)(2,1)}, bf16[2,18,8,128]{3,2,1,0:T(8,128)(2,1)S(1)}, u32[]{:S(2)}) copy-start(bf16[2,18,8,128]{3,2,1,0:T(8,128)(2,1)S(1)} %collective-permute-done.6.refs_8_) | copy-start | bytes 221188
  50.5 2.9 %copy-start.13 = (bf16[2,18,8,128]{3,2,1,0:T(8,128)(2,1)}, bf16[2,18,8,128]{3,2,1,0:T(8,128)(2,1)S(1)}, u32[]{:S(2)}) copy-start(bf16[2,18,8,128]{3,2,1,0:T(8,128)(2,1)S(1)} %collective-permute-done.7.refs_9_) | copy-start | bytes 221188
  52.6 0.8 copy-start.14
  52.6 18.4 %collective-permute-start.9 = (bf16[128,2048]{1,0:T(8,128)(2,1)S(1)}, bf16[128,2048]{1,0:T(8,128)(2,1)S(1)}, u32[]{:S(2)}, u32[]{:S(2)}) collective-permute-start(bf16[128,2048]{1,0:T(8,128)(2,1)S(1)} %collective-permute-done.5.refs_6_), channel_id=1, source_target_pairs={{0,8},{8,0},{16,24},{24,16},{1,9},{9,1},{17,25},{25,17},{2,10},{10... | collective-permute-start | bytes 1572872 | tf_op jit(solution)/shard_map/ppermute | solution.py:701
  67.3 17.6 %collective-permute-start.10 = (bf16[144,1024]{1,0:T(8,128)(2,1)}, bf16[144,1024]{1,0:T(8,128)(2,1)S(1)}, u32[]{:S(2)}, u32[]{:S(2)}) collective-permute-start(bf16[144,1024]{1,0:T(8,128)(2,1)} %get-tuple-element.156.refs_8_), channel_id=1, source_target_pairs={{0,8},{8,0},{16,24},{24,16},{1,9},{9,1},{17,25},{25,17},{2,10},{10... | collective-permute-start | bytes 884744 | tf_op jit(solution)/shard_map/ppermute | solution.py:701
  68.6 16.4 %collective-permute-start.11 = (bf16[144,1024]{1,0:T(8,128)(2,1)}, bf16[144,1024]{1,0:T(8,128)(2,1)S(1)}, u32[]{:S(2)}, u32[]{:S(2)}) collective-permute-start(bf16[144,1024]{1,0:T(8,128)(2,1)} %get-tuple-element.156.refs_8_), channel_id=1, source_target_pairs={{0,16},{8,24},{16,0},{24,8},{1,17},{9,25},{17,1},{25,9},{2,18},{10... | collective-permute-start | bytes 884744 | tf_op jit(solution)/shard_map/ppermute | solution.py:701
  71.0 14.0 %copy-start.5 = (bf16[128,2048]{1,0:T(8,128)(2,1)}, bf16[128,2048]{1,0:T(8,128)(2,1)S(1)}, u32[]{:S(2)}) copy-start(bf16[128,2048]{1,0:T(8,128)(2,1)S(1)} %collective-permute-done.9.refs_7_) | copy-start | bytes 1572868
  85.0 35.4 %copy-start.6 = (bf16[144,1024]{1,0:T(8,128)(2,1)}, bf16[144,1024]{1,0:T(8,128)(2,1)S(1)}, u32[]{:S(2)}) copy-start(bf16[144,1024]{1,0:T(8,128)(2,1)S(1)} %collective-permute-done.10.refs_9_) | copy-start | bytes 884740
  85.0 35.4 %copy-start.7 = (bf16[144,1024]{1,0:T(8,128)(2,1)}, bf16[144,1024]{1,0:T(8,128)(2,1)S(1)}, u32[]{:S(2)}) copy-start(bf16[144,1024]{1,0:T(8,128)(2,1)S(1)} %collective-permute-done.11.refs_10_) | copy-start | bytes 884740
  85.0 1.7 %collective-permute-start.12 = (bf16[640,128]{1,0:T(8,128)(2,1)}, bf16[640,128]{1,0:T(8,128)(2,1)S(1)}, u32[]{:S(2)}, u32[]{:S(2)}) collective-permute-start(bf16[640,128]{1,0:T(8,128)(2,1)} %get-tuple-element.123), channel_id=1, source_target_pairs={{0,1},{1,0},{2,3},{3,2},{4,5},{5,4},{6,7},{7,6},{8,9},{9,8},{10,11... | collective-permute-start | bytes 491528 | tf_op jit(solution)/shard_map/ppermute | solution.py:701
  87.7 6.3 %collective-permute-start.13 = (bf16[640,128]{1,0:T(8,128)(2,1)S(1)}, bf16[640,128]{1,0:T(8,128)(2,1)S(1)}, u32[]{:S(2)}, u32[]{:S(2)}) collective-permute-start(bf16[640,128]{1,0:T(8,128)(2,1)S(1)} %add_convert_fusion.1), channel_id=1, source_target_pairs={{0,2},{1,3},{2,0},{3,1},{4,6},{5,7},{6,4},{7,5},{8,10},{9,11},{10,... | collective-permute-start | bytes 491528 | tf_op jit(solution)/shard_map/ppermute | solution.py:701
  89.2 14.0 %collective-permute-start.15 = (bf16[144,1024]{1,0:T(8,128)(2,1)S(1)}, bf16[144,1024]{1,0:T(8,128)(2,1)S(1)}, u32[]{:S(2)}, u32[]{:S(2)}) collective-permute-start(bf16[144,1024]{1,0:T(8,128)(2,1)S(1)} %collective-permute-done.11.refs_10_), channel_id=1, source_target_pairs={{0,8},{8,0},{16,24},{24,16},{1,9},{9,1},{17,25},{25,17},{2,10},{10... | collective-permute-start | bytes 884744 | tf_op jit(solution)/shard_map/ppermute | solution.py:701
  90.6 16.1 %collective-permute-start.16 = (bf16[144,1024]{1,0:T(8,128)(2,1)}, bf16[144,1024]{1,0:T(8,128)(2,1)S(1)}, u32[]{:S(2)}, u32[]{:S(2)}) collective-permute-start(bf16[144,1024]{1,0:T(8,128)(2,1)} %get-tuple-element.160.refs_12_), channel_id=1, source_target_pairs={{0,16},{8,24},{16,0},{24,8},{1,17},{9,25},{17,1},{25,9},{2,18},{10... | collective-permute-start | bytes 884744 | tf_op jit(solution)/shard_map/ppermute | solution.py:701
  94.0 12.8 %copy-start = (bf16[640,128]{1,0:T(8,128)(2,1)}, bf16[640,128]{1,0:T(8,128)(2,1)S(1)}, u32[]{:S(2)}) copy-start(bf16[640,128]{1,0:T(8,128)(2,1)S(1)} %add_convert_fusion.back_a.refs_0_) | copy-start | bytes 491524
  94.0 12.7 %collective-permute-start.14 = (bf16[640,128]{1,0:T(8,128)(2,1)S(1)}, bf16[640,128]{1,0:T(8,128)(2,1)S(1)}, u32[]{:S(2)}, u32[]{:S(2)}) collective-permute-start(bf16[640,128]{1,0:T(8,128)(2,1)S(1)} %add_convert_fusion.back_a.refs_0_), channel_id=1, source_target_pairs={{0,4},{1,5},{2,6},{3,7},{4,0},{5,1},{6,2},{7,3},{8,12},{9,13},{10,... | collective-permute-start | bytes 491528 | tf_op jit(solution)/shard_map/ppermute | solution.py:701
  95.6 24.8 %collective-permute-start.20 = (bf16[144,1024]{1,0:T(8,128)(2,1)}, bf16[144,1024]{1,0:T(8,128)(2,1)S(1)}, u32[]{:S(2)}, u32[]{:S(2)}) collective-permute-start(bf16[144,1024]{1,0:T(8,128)(2,1)} %get-tuple-element.160.refs_12_), channel_id=1, source_target_pairs={{0,8},{8,0},{16,24},{24,16},{1,9},{9,1},{17,25},{25,17},{2,10},{10... | collective-permute-start | bytes 884744 | tf_op jit(solution)/shard_map/ppermute | solution.py:701
  103.2 23.0 %copy-start.8 = (bf16[144,1024]{1,0:T(8,128)(2,1)}, bf16[144,1024]{1,0:T(8,128)(2,1)S(1)}, u32[]{:S(2)}) copy-start(bf16[144,1024]{1,0:T(8,128)(2,1)S(1)} %collective-permute-done.15.refs_11_) | copy-start | bytes 884740
  106.7 19.5 %copy-start.9 = (bf16[144,1024]{1,0:T(8,128)(2,1)}, bf16[144,1024]{1,0:T(8,128)(2,1)S(1)}, u32[]{:S(2)}) copy-start(bf16[144,1024]{1,0:T(8,128)(2,1)S(1)} %collective-permute-done.16.refs_14_) | copy-start | bytes 884740
  106.7 0.7 copy-start.1
  106.7 15.0 %collective-permute-start.21 = (bf16[144,1024]{1,0:T(8,128)(2,1)S(1)}, bf16[144,1024]{1,0:T(8,128)(2,1)S(1)}, u32[]{:S(2)}, u32[]{:S(2)}) collective-permute-start(bf16[144,1024]{1,0:T(8,128)(2,1)S(1)} %collective-permute-done.16.refs_14_), channel_id=1, source_target_pairs={{0,8},{8,0},{16,24},{24,16},{1,9},{9,1},{17,25},{25,17},{2,10},{10... | collective-permute-start | bytes 884744 | tf_op jit(solution)/shard_map/ppermute | solution.py:701
  109.3 11.6 %collective-permute-start.17 = (bf16[288,128]{1,0:T(8,128)(2,1)}, bf16[288,128]{1,0:T(8,128)(2,1)S(1)}, u32[]{:S(2)}, u32[]{:S(2)}) collective-permute-start(bf16[288,128]{1,0:T(8,128)(2,1)} %get-tuple-element.137), channel_id=1, source_target_pairs={{0,8},{8,0},{16,24},{24,16},{1,9},{9,1},{17,25},{25,17},{2,10},{10... | collective-permute-start | bytes 221192 | tf_op jit(solution)/shard_map/ppermute | solution.py:701
  110.7 10.2 %collective-permute-start.18 = (bf16[288,128]{1,0:T(8,128)(2,1)}, bf16[288,128]{1,0:T(8,128)(2,1)S(1)}, u32[]{:S(2)}, u32[]{:S(2)}) collective-permute-start(bf16[288,128]{1,0:T(8,128)(2,1)} %get-tuple-element.138), channel_id=1, source_target_pairs={{0,16},{8,24},{16,0},{24,8},{1,17},{9,25},{17,1},{25,9},{2,18},{10... | collective-permute-start | bytes 221192 | tf_op jit(solution)/shard_map/ppermute | solution.py:701
  111.7 10.0 %collective-permute-start.19 = (bf16[288,128]{1,0:T(8,128)(2,1)}, bf16[288,128]{1,0:T(8,128)(2,1)S(1)}, u32[]{:S(2)}, u32[]{:S(2)}) collective-permute-start(bf16[288,128]{1,0:T(8,128)(2,1)} %get-tuple-element.139), channel_id=1, source_target_pairs={{0,24},{8,16},{16,8},{24,0},{1,25},{9,17},{17,9},{25,1},{2,26},{10... | collective-permute-start | bytes 221192 | tf_op jit(solution)/shard_map/ppermute | solution.py:701
  120.4 5.8 %copy-start.10 = (bf16[144,1024]{1,0:T(8,128)(2,1)}, bf16[144,1024]{1,0:T(8,128)(2,1)S(1)}, u32[]{:S(2)}) copy-start(bf16[144,1024]{1,0:T(8,128)(2,1)S(1)} %collective-permute-done.20.refs_13_) | copy-start | bytes 884740
  120.9 5.3 %copy-start.17 = (bf16[288,128]{1,0:T(8,128)(2,1)}, bf16[288,128]{1,0:T(8,128)(2,1)S(1)}, u32[]{:S(2)}) copy-start(bf16[288,128]{1,0:T(8,128)(2,1)S(1)} %collective-permute-done.17.refs_1_) | copy-start | bytes 221188
  120.9 5.3 %copy-start.18 = (bf16[288,128]{1,0:T(8,128)(2,1)}, bf16[288,128]{1,0:T(8,128)(2,1)S(1)}, u32[]{:S(2)}) copy-start(bf16[288,128]{1,0:T(8,128)(2,1)S(1)} %collective-permute-done.18.refs_2_) | copy-start | bytes 221188
  121.8 4.5 %copy-start.19 = (bf16[288,128]{1,0:T(8,128)(2,1)}, bf16[288,128]{1,0:T(8,128)(2,1)S(1)}, u32[]{:S(2)}) copy-start(bf16[288,128]{1,0:T(8,128)(2,1)S(1)} %collective-permute-done.19.refs_3_) | copy-start | bytes 221188
  121.8 4.5 %copy-start.11 = (bf16[144,1024]{1,0:T(8,128)(2,1)}, bf16[144,1024]{1,0:T(8,128)(2,1)S(1)}, u32[]{:S(2)}) copy-start(bf16[144,1024]{1,0:T(8,128)(2,1)S(1)} %collective-permute-done.21.refs_15_) | copy-start | bytes 884740
  121.8 9.5 %collective-permute-start.22 = (bf16[16,2048]{1,0:T(8,128)(2,1)}, bf16[16,2048]{1,0:T(8,128)(2,1)S(1)}, u32[]{:S(2)}, u32[]{:S(2)}) collective-permute-start(bf16[16,2048]{1,0:T(8,128)(2,1)} %get-tuple-element.145.refs_3_), channel_id=1, source_target_pairs={{0,8},{8,16},{16,24},{24,0},{1,9},{9,17},{17,25},{25,1},{2,10},{10... | collective-permute-start | bytes 196616 | tf_op jit(solution)/shard_map/ppermute | solution.py:52
  121.8 9.5 %collective-permute-start.23 = (bf16[16,2048]{1,0:T(8,128)(2,1)}, bf16[16,2048]{1,0:T(8,128)(2,1)S(1)}, u32[]{:S(2)}, u32[]{:S(2)}) collective-permute-start(bf16[16,2048]{1,0:T(8,128)(2,1)} %get-tuple-element.145.refs_3_), channel_id=1, source_target_pairs={{0,16},{8,24},{16,0},{24,8},{1,17},{9,25},{17,1},{25,9},{2,18},{10... | collective-permute-start | bytes 196616 | tf_op jit(solution)/shard_map/ppermute | solution.py:52
  125.5 5.8 %collective-permute-start.24 = (bf16[16,2048]{1,0:T(8,128)(2,1)}, bf16[16,2048]{1,0:T(8,128)(2,1)S(1)}, u32[]{:S(2)}, u32[]{:S(2)}) collective-permute-start(bf16[16,2048]{1,0:T(8,128)(2,1)} %get-tuple-element.145.refs_3_), channel_id=1, source_target_pairs={{0,24},{8,0},{16,8},{24,16},{1,25},{9,1},{17,9},{25,17},{2,26},{10... | collective-permute-start | bytes 196616 | tf_op jit(solution)/shard_map/ppermute | solution.py:52
  131.3 0.6 copy-start.21
  131.3 0.6 copy-start.22
  131.3 0.6 copy-start.23

commit v7 on v6

--- a/solution.py
+++ b/solution.py
@@ -282,7 +282,7 @@
         before_ref, refs = refs[0], refs[4:]
     (pre_ref, gate_out, scan_out, small_ref, part_ref) = refs[:5]
     refs = refs[5:]
-    (xs, dxs, gs, ys, dds, qs, decayed, coef_out, coef_in, rate, decay_acc, acc, ends, products) = refs
+    (xs, dxs, gs, ys, dds, qs, decayed, coef_out, coef_in, rate, decay_acc, acc, ends, products, factors) = refs
     rows = conv_ref.shape[0]
     groups = decay_ref.shape[2]
     low_rank = weight_ref.shape[0]
@@ -332,7 +332,9 @@
             for lead in range(0, states, 8):
                 base = (sub * states + lead) * groups
                 for n in range(lead, lead + 8):
-                    kept = jnp.exp2(size * rate[n]) * state[n]
+                    factor = jnp.exp2(size * rate[n])
+                    kept = factor * state[n]
+                    factors[token, n] = factor
                     decayed[token, n] = kept
                     state[n] = kept + drive * coef[token, n]
                     result = result + state[n] * coef[token, states + n]
@@ -357,9 +359,8 @@
                 base = (sub * states + lead) * groups
                 for n in range(lead, lead + 8):
                     adjoint = carry[n] + grad * coef[token, states + n]
-                    power = size * rate[n]
-                    carry[n] = jnp.exp2(power) * adjoint
-                    weighted = adjoint * decayed[token, n] * power
+                    carry[n] = factors[token, n] * adjoint
+                    weighted = adjoint * decayed[token, n] * (size * rate[n])
                     slope = slope + weighted
                     gathered[n] = gathered[n] + weighted
                     inner = inner + adjoint * coef[token, n]
@@ -509,6 +510,7 @@
             pltpu.VMEM((wide, rows), F32),
             pltpu.VMEM((places, states + 2, groups, 128), F32),
             pltpu.VMEM((8 * states * groups, 128), F32),
+            pltpu.VMEM((rows, states, groups, 128), F32),
         ],
         input_output_aliases=aliases,
         compiler_params=params(),
@@ -760,7 +762,7 @@
     messages = [swap(message, "ctx", mask) for mask, message in enumerate(messages, 1)]
     messages, blocks = tie((messages, blocks))
     blocks = spread_on(blocks)
-    previous, steps, fresh = [], [], None
+    previous, steps = [], []
     for chunk in range(chunks):
         message, grad_gate, scan_part, small, part = scan_call(
             places, chunk, coef, dt, decay, conv_out, gate_input, out_grad, step_weight,
@@ -769,18 +771,13 @@
         previous = [part, grad_gate, scan_part, small]
         if chunk == 0:
             previous, blocks = tie((previous, blocks))
-        if fresh is not None:
-            previous, fresh = tie((previous, fresh))
-            steps += spread_on(fresh)
-        fresh = spread(message)
+        else:
+            previous, steps[-1] = tie((previous, steps[-1]))
+        steps.append(spread(message))
     part, grad_gate, scan_part, small = previous
     backs = chan_sum(part)
-    if places == 4:
-        backs, steps, far = tie((backs, steps, fresh[2]))
-        fresh = fresh[:2] + [far]
-    else:
-        backs, steps, fresh = tie((backs, steps, fresh))
-    steps += spread_on(fresh)
+    backs, steps = tie((backs, steps))
+    steps = [block for step in steps for block in spread_on(step)]
     cuts = cut_call(places, backs, low_t)
     cuts = [cuts[0]] + [swap(cut, "ctx", mask) for mask, cut in enumerate(cuts[1:], 1)]
     main, tail, sums = conv_grad_call(

time: 134 us -> 137 us (1.022)
  waiting for transfers between devices: 28.9 us -> 32.5 us
    ppermute x21, waiting for transfers between devices: 27.5 us -> 31.1 us  [swap(): lax.ppermute(block, axis, [(i, i ^ mask) for i in range(lax.axis_size(axi...]
  transfers between devices with their start and end apart: 25 -> 25, of which waited for: 12 -> 12; matrix products, arithmetic and copies ran while one was open for 1% -> 1% of each run, Pallas kernels for 41% -> 39%
where the time goes in v7:
time: 137 us; the launch traced here: 136 us
  Pallas kernels  60.3 us (44%)
  starting transfers between devices  36.9 us (27%)
  waiting for transfers between devices  32.5 us (24%)
  local copies, waits for them, and re-layouts  3.48 us (3%)
  other arithmetic  2.02 us (1%)
    ppermute x21, waiting for transfers between devices, swap(): lax.ppermute(block, axis, [(i, i ^ mask) for i in range(lax.axis_size(axi...  31.1 us
    ppermute x21, starting transfers between devices, swap(): lax.ppermute(block, axis, [(i, i ^ mask) for i in range(lax.axis_size(axi...  28.1 us
    pallas_call x2, Pallas kernels, scan_call(): pl.pallas_call(functools.partial(scan_kernel, places, states, first), gri...  27.4 us
    pallas_call x1, Pallas kernels, local_call(): pl.pallas_call(functools.partial(local_kernel, low_rank, states, places),...  12.8 us
    pallas_call x1, Pallas kernels, conv_grad_call(): pl.pallas_call(functools.partial(conv_grad_kernel, places, low_rank), gri...  6.75 us
    pallas_call x1, Pallas kernels, rows_call(): pl.pallas_call(functools.partial(rows_kernel, places, rank_rows, chunks),...  4.98 us
    ppermute x1, starting transfers between devices, shift(): return lax.ppermute(block, axis, route)  4.93 us
    pallas_call x1, Pallas kernels, conv_call(): pl.pallas_call(conv_kernel, grid=(chans // width,), in_specs=[columns(row...  4.83 us
  transfers between devices with their start and end apart: 25, of which 12 were waited for; matrix products, arithmetic and copies ran while one was open for 1% of the time, Pallas kernels for 39%

profile of v7, /device:TPU:0, one launch (start us, length us, event | category | flops | bytes accessed | tf_op | source)
XLA Modules:
  0.0 136.2 jit_solution(7396467735309659499)
XLA Ops:
  0.7 0.8 slice.3
  1.5 4.9 %collective-permute-start = (bf16[3,2048]{1,0:T(4,128)(2,1)S(1)}, bf16[3,2048]{1,0:T(4,128)(2,1)S(1)}, u32[]{:S(2)}, u32[]{:S(2)}) collective-permute-start(bf16[3,2048]{1,0:T(4,128)(2,1)S(1)} %slice.3), channel_id=1, source_target_pairs={{0,8},{8,16},{16,24},{1,9},{9,17},{17,25},{2,10},{10,18},{18,26},{... | collective-permute-start | bytes 36872 | tf_op jit(solution)/shard_map/ppermute | solution.py:58
  6.4 1.4 %collective-permute-done.rim_ref = bf16[3,2048]{1,0:T(4,128)(2,1)S(1)} collective-permute-done((bf16[3,2048]{1,0:T(4,128)(2,1)S(1)}, bf16[3,2048]{1,0:T(4,128)(2,1)S(1)}, u32[]{:S(2)}, u32[]{:S(2)}) %collective-permute-start) | collective-permute-done | bytes 12320 | tf_op jit(solution)/shard_map/ppermute | solution.py:58
  7.8 0.6 copy-done.20
  8.4 4.8 %conv_project.1 = (bf16[128,2048]{1,0:T(8,128)(2,1)}, bf16[128,544]{1,0:T(8,128)(2,1)}) custom-call(bf16[128,2048]{1,0:T(8,128)(2,1)} %input_ref.3, bf16[3,2048]{1,0:T(4,128)(2,1)} %copy-done.20, f32[4,2048]{1,0:T(4,128)} %refs_2_.3, f32[1,2048]{1,0:T(1,128)} %bitcast.19, bf16[544,2048]{1,0:T(8,128)(2,1)} %proj_ref.3), custom_call_target="tpu_custom_call" | custom-call | tf_op jit(solution)/shard_map/conv_project/pallas_call | solution.py:103
  13.3 0.0 collective-permute-start.1
  13.3 2.4 %collective-permute-start.4 = (bf16[128,2048]{1,0:T(8,128)(2,1)}, bf16[128,2048]{1,0:T(8,128)(2,1)S(1)}, u32[]{:S(2)}, u32[]{:S(2)}) collective-permute-start(bf16[128,2048]{1,0:T(8,128)(2,1)} %get-tuple-element.154.refs_5_.refs_3_.refs_4_), channel_id=1, source_target_pairs={{0,8},{8,0},{16,24},{24,16},{1,9},{9,1},{17,25},{25,17},{2,10},{10... | collective-permute-start | bytes 1572872 | tf_op jit(solution)/shard_map/ppermute | solution.py:703
  15.6 2.6 %collective-permute-start.5 = (bf16[128,2048]{1,0:T(8,128)(2,1)}, bf16[128,2048]{1,0:T(8,128)(2,1)S(1)}, u32[]{:S(2)}, u32[]{:S(2)}) collective-permute-start(bf16[128,2048]{1,0:T(8,128)(2,1)} %get-tuple-element.154.refs_5_.refs_3_.refs_4_), channel_id=1, source_target_pairs={{0,16},{8,24},{16,0},{24,8},{1,17},{9,25},{17,1},{25,9},{2,18},{10... | collective-permute-start | bytes 1572872 | tf_op jit(solution)/shard_map/ppermute | solution.py:703
  18.2 0.0 collective-permute-done.1
  18.2 1.0 add_convert_fusion.3
  19.2 1.6 %collective-permute-start.2 = (bf16[128,544]{1,0:T(8,128)(2,1)S(1)}, bf16[128,544]{1,0:T(8,128)(2,1)S(1)}, u32[]{:S(2)}, u32[]{:S(2)}) collective-permute-start(bf16[128,544]{1,0:T(8,128)(2,1)S(1)} %add_convert_fusion.3), channel_id=1, source_target_pairs={{0,2},{1,3},{2,0},{3,1},{4,6},{5,7},{6,4},{7,5},{8,10},{9,11},{10,... | collective-permute-start | bytes 417800 | tf_op jit(solution)/shard_map/ppermute | solution.py:703
  20.7 4.5 %collective-permute-done.2 = bf16[128,544]{1,0:T(8,128)(2,1)S(1)} collective-permute-done((bf16[128,544]{1,0:T(8,128)(2,1)S(1)}, bf16[128,544]{1,0:T(8,128)(2,1)S(1)}, u32[]{:S(2)}, u32[]{:S(2)}) %collective-permute-start.2) | collective-permute-done | bytes 139296 | tf_op jit(solution)/shard_map/ppermute | solution.py:703
  25.3 0.0 copy-start.2
  25.3 1.6 %collective-permute-start.3 = (bf16[128,544]{1,0:T(8,128)(2,1)S(1)}, bf16[128,544]{1,0:T(8,128)(2,1)S(1)}, u32[]{:S(2)}, u32[]{:S(2)}) collective-permute-start(bf16[128,544]{1,0:T(8,128)(2,1)S(1)} %add_convert_fusion.2.refs_0_), channel_id=1, source_target_pairs={{0,4},{1,5},{2,6},{3,7},{4,0},{5,1},{6,2},{7,3},{8,12},{9,13},{10,... | collective-permute-start | bytes 417800 | tf_op jit(solution)/shard_map/ppermute | solution.py:703
  26.9 0.7 copy.27
  27.6 3.1 %collective-permute-done.3.refs_1_ = bf16[128,544]{1,0:T(8,128)(2,1)S(1)} collective-permute-done((bf16[128,544]{1,0:T(8,128)(2,1)S(1)}, bf16[128,544]{1,0:T(8,128)(2,1)S(1)}, u32[]{:S(2)}, u32[]{:S(2)}) %collective-permute-start.3) | collective-permute-done | bytes 139296 | tf_op jit(solution)/shard_map/ppermute | solution.py:703
  30.7 0.7 copy-done.15
  31.3 12.8 %local_ends.1 = (f32[2,1024,128]{2,1,0:T(8,128)}, f32[128,128]{1,0:T(8,128)}, bf16[128,512]{1,0:T(8,128)(2,1)}, bf16[512,128]{1,0:T(8,128)(2,1)}, bf16[2,18,8,12...) custom-call(bf16[128,544]{1,0:T(8,128)(2,1)} %copy-done.2, ...), custom_call_target="tpu_custom_call" | custom-call | tf_op jit(solution)/shard_map/local_ends/pallas_call | solution.py:228
  44.2 0.0 collective-permute-done.4.refs_5_
  44.2 0.0 collective-permute-done.5.refs_6_
  44.2 0.5 collective-permute-start.6
  44.7 1.4 %collective-permute-start.7 = (bf16[2,18,8,128]{3,2,1,0:T(8,128)(2,1)}, bf16[2,18,8,128]{3,2,1,0:T(8,128)(2,1)S(1)}, u32[]{:S(2)}, u32[]{:S(2)}) collective-permute-start(bf16[2,18,8,128]{3,2,1,0:T(8,128)(2,1)} %get-tuple-element.100), channel_id=1, source_target_pairs={{0,16},{8,24},{16,0},{24,8},{1,17},{9,25},{17,1},{25,9},{2,18},{10... | collective-permute-start | bytes 221192 | tf_op jit(solution)/shard_map/ppermute | solution.py:703
  46.2 2.5 %collective-permute-start.8 = (bf16[2,18,8,128]{3,2,1,0:T(8,128)(2,1)}, bf16[2,18,8,128]{3,2,1,0:T(8,128)(2,1)S(1)}, u32[]{:S(2)}, u32[]{:S(2)}) collective-permute-start(bf16[2,18,8,128]{3,2,1,0:T(8,128)(2,1)} %get-tuple-element.101), channel_id=1, source_target_pairs={{0,24},{8,16},{16,8},{24,0},{1,25},{9,17},{17,9},{25,1},{2,26},{10... | collective-permute-start | bytes 221192 | tf_op jit(solution)/shard_map/ppermute | solution.py:703
  48.7 0.4 collective-permute-done.6.refs_8_
  49.1 1.4 %collective-permute-done.7.refs_9_ = bf16[2,18,8,128]{3,2,1,0:T(8,128)(2,1)S(1)} collective-permute-done((bf16[2,18,8,128]{3,2,1,0:T(8,128)(2,1)}, bf16[2,18,8,128]{3,2,1,0:T(8,128)(2,1)S(1)}, u32[]{:S(2)}, u32[]{:S(2)}) %collective-permute-start.7) | collective-permute-done | bytes 73760 | tf_op jit(solution)/shard_map/ppermute | solution.py:703
  50.5 2.1 %collective-permute-done.8.refs_10_ = bf16[2,18,8,128]{3,2,1,0:T(8,128)(2,1)S(1)} collective-permute-done((bf16[2,18,8,128]{3,2,1,0:T(8,128)(2,1)}, bf16[2,18,8,128]{3,2,1,0:T(8,128)(2,1)S(1)}, u32[]{:S(2)}, u32[]{:S(2)}) %collective-permute-start.8) | collective-permute-done | bytes 73760 | tf_op jit(solution)/shard_map/ppermute | solution.py:703
  52.6 0.8 collective-permute-start.9
  53.4 13.7 %scan_gradients.2 = (bf16[144,1024]{1,0:T(8,128)(2,1)}, bf16[128,2048]{1,0:T(8,128)(2,1)}, bf16[128,2048]{1,0:T(8,128)(2,1)}, f32[8,2048]{1,0:T(8,128)}, f32[640,128]{1,0:T(8,128)}) custom-call(f32[128,128]{1,0:T(8,128)} %get-tuple-element.94.refs_0_, f32[2,1024,128]{2,1,0:T(8,128)} %get-tuple-element.95.refs_1_, f32[2,16,8,128]{3,2,1,0:T(8,128)} %bitcast.13, ...), custom_call_target="tpu_custom_call" | custom-call | tf_op jit(solution)/shard_map/scan_gradients/pallas_call | solution.py:480
  67.1 1.3 collective-permute-start.10
  68.4 2.3 %collective-permute-start.11 = (bf16[144,1024]{1,0:T(8,128)(2,1)}, bf16[144,1024]{1,0:T(8,128)(2,1)S(1)}, u32[]{:S(2)}, u32[]{:S(2)}) collective-permute-start(bf16[144,1024]{1,0:T(8,128)(2,1)} %get-tuple-element.158.refs_8_), channel_id=1, source_target_pairs={{0,16},{8,24},{16,0},{24,8},{1,17},{9,25},{17,1},{25,9},{2,18},{10... | collective-permute-start | bytes 884744 | tf_op jit(solution)/shard_map/ppermute | solution.py:703
  70.7 0.0 collective-permute-done.9.refs_7_
  70.7 13.7 %scan_gradients.3 = (bf16[144,1024]{1,0:T(8,128)(2,1)}, bf16[128,2048]{1,0:T(8,128)(2,1)}, bf16[128,2048]{1,0:T(8,128)(2,1)}, f32[8,2048]{1,0:T(8,128)}, bf16[640,128]{1,0:T(8,128)(2,1)}) custom-call(f32[128,128]{1,0:T(8,128)} %get-tuple-element.94.refs_0_, ...), custom_call_target="tpu_custom_call", output_to_operand_aliasing={{1}: (12, {}), {2}: (13, {}), {3}: (14, {})} | custom-call | tf_op jit(solution)/shard_map/scan_gradients/pallas_call | solution.py:480
  84.5 0.0 collective-permute-done.10.refs_9_
  84.5 0.0 collective-permute-done.11.refs_10_
  84.5 0.1 collective-permute-start.12
  84.6 1.6 %collective-permute-done.12 = bf16[640,128]{1,0:T(8,128)(2,1)S(1)} collective-permute-done((bf16[640,128]{1,0:T(8,128)(2,1)}, bf16[640,128]{1,0:T(8,128)(2,1)S(1)}, u32[]{:S(2)}, u32[]{:S(2)}) %collective-permute-start.12) | collective-permute-done | bytes 163872 | tf_op jit(solution)/shard_map/ppermute | solution.py:703
  86.2 1.0 add_convert_fusion.1
  87.2 1.6 %collective-permute-start.13 = (bf16[640,128]{1,0:T(8,128)(2,1)S(1)}, bf16[640,128]{1,0:T(8,128)(2,1)S(1)}, u32[]{:S(2)}, u32[]{:S(2)}) collective-permute-start(bf16[640,128]{1,0:T(8,128)(2,1)S(1)} %add_convert_fusion.1), channel_id=1, source_target_pairs={{0,2},{1,3},{2,0},{3,1},{4,6},{5,7},{6,4},{7,5},{8,10},{9,11},{10,... | collective-permute-start | bytes 491528 | tf_op jit(solution)/shard_map/ppermute | solution.py:703
  88.7 1.4 %collective-permute-start.15 = (bf16[144,1024]{1,0:T(8,128)(2,1)}, bf16[144,1024]{1,0:T(8,128)(2,1)S(1)}, u32[]{:S(2)}, u32[]{:S(2)}) collective-permute-start(bf16[144,1024]{1,0:T(8,128)(2,1)} %get-tuple-element.162.refs_12_), channel_id=1, source_target_pairs={{0,8},{8,0},{16,24},{24,16},{1,9},{9,1},{17,25},{25,17},{2,10},{10... | collective-permute-start | bytes 884744 | tf_op jit(solution)/shard_map/ppermute | solution.py:703
  90.1 0.0 collective-permute-start.16
  90.1 3.3 %collective-permute-done.13 = bf16[640,128]{1,0:T(8,128)(2,1)S(1)} collective-permute-done((bf16[640,128]{1,0:T(8,128)(2,1)S(1)}, bf16[640,128]{1,0:T(8,128)(2,1)S(1)}, u32[]{:S(2)}, u32[]{:S(2)}) %collective-permute-start.13) | collective-permute-done | bytes 163872 | tf_op jit(solution)/shard_map/ppermute | solution.py:703
  93.5 0.0 copy-start
  93.5 1.6 %collective-permute-start.14 = (bf16[640,128]{1,0:T(8,128)(2,1)S(1)}, bf16[640,128]{1,0:T(8,128)(2,1)S(1)}, u32[]{:S(2)}, u32[]{:S(2)}) collective-permute-start(bf16[640,128]{1,0:T(8,128)(2,1)S(1)} %add_convert_fusion.back_a.refs_0_), channel_id=1, source_target_pairs={{0,4},{1,5},{2,6},{3,7},{4,0},{5,1},{6,2},{7,3},{8,12},{9,13},{10,... | collective-permute-start | bytes 491528 | tf_op jit(solution)/shard_map/ppermute | solution.py:703
  95.1 6.9 %collective-permute-done.15.refs_13_ = bf16[144,1024]{1,0:T(8,128)(2,1)S(1)} collective-permute-done((bf16[144,1024]{1,0:T(8,128)(2,1)}, bf16[144,1024]{1,0:T(8,128)(2,1)S(1)}, u32[]{:S(2)}, u32[]{:S(2)}) %collective-permute-start.15) | collective-permute-done | bytes 294944 | tf_op jit(solution)/shard_map/ppermute | solution.py:703
  102.1 4.0 %collective-permute-done.16.refs_14_ = bf16[144,1024]{1,0:T(8,128)(2,1)S(1)} collective-permute-done((bf16[144,1024]{1,0:T(8,128)(2,1)}, bf16[144,1024]{1,0:T(8,128)(2,1)S(1)}, u32[]{:S(2)}, u32[]{:S(2)}) %collective-permute-start.16) | collective-permute-done | bytes 294944 | tf_op jit(solution)/shard_map/ppermute | solution.py:703
  106.1 0.1 collective-permute-start.20
  106.2 2.0 %collective-permute-start.21 = (bf16[144,1024]{1,0:T(8,128)(2,1)S(1)}, bf16[144,1024]{1,0:T(8,128)(2,1)S(1)}, u32[]{:S(2)}, u32[]{:S(2)}) collective-permute-start(bf16[144,1024]{1,0:T(8,128)(2,1)S(1)} %collective-permute-done.16.refs_14_), channel_id=1, source_target_pairs={{0,8},{8,0},{16,24},{24,16},{1,9},{9,1},{17,25},{25,17},{2,10},{10... | collective-permute-start | bytes 884744 | tf_op jit(solution)/shard_map/ppermute | solution.py:703
  108.2 1.8 %cut_rows.1 = (bf16[288,128]{1,0:T(8,128)(2,1)}, bf16[288,128]{1,0:T(8,128)(2,1)}, bf16[288,128]{1,0:T(8,128)(2,1)}, bf16[288,128]{1,0:T(8,128)(2,1)}) custom-call(bf16[640,128]{1,0:T(8,128)(2,1)} %copy-done, bf16[640,128]{1,0:T(8,128)(2,1)} %copy-done.1, bf16[512,128]{1,0:T(8,128)(2,1)} %get-tuple-element.136.refs_2_), custom_call_target="tpu_custom_call" | custom-call | tf_op jit(solution)/shard_map/cut_rows/pallas_call | solution.py:599
  110.1 0.1 collective-permute-start.17
  110.1 0.2 collective-permute-start.18
  110.4 4.1 %collective-permute-start.19 = (bf16[288,128]{1,0:T(8,128)(2,1)}, bf16[288,128]{1,0:T(8,128)(2,1)S(1)}, u32[]{:S(2)}, u32[]{:S(2)}) collective-permute-start(bf16[288,128]{1,0:T(8,128)(2,1)} %get-tuple-element.140), channel_id=1, source_target_pairs={{0,24},{8,16},{16,8},{24,0},{1,25},{9,17},{17,9},{25,1},{2,26},{10... | collective-permute-start | bytes 221192 | tf_op jit(solution)/shard_map/ppermute | solution.py:703
  114.5 6.8 %conv_gradients.1 = (bf16[128,2048]{1,0:T(8,128)(2,1)}, f32[16,2048]{1,0:T(8,128)}, bf16[16,2048]{1,0:T(8,128)(2,1)}) custom-call(bf16[640,128]{1,0:T(8,128)(2,1)} %copy-done, bf16[640,128]{1,0:T(8,128)(2,1)} %copy-done.1, bf16[544,2048]{1,0:T(8,128)(2,1)} %proj_ref.3, bf16[128,2048]{1,0:T(8,128)(2,1)} %get-tuple-element.131.scan_ref, ...), custom_call_target="tpu_custom_call" | custom-call | tf_op jit(solution)/shard_map/conv_gradients/pallas_call | solution.py:562
  121.2 2.9 %collective-permute-done.17.refs_1_ = bf16[288,128]{1,0:T(8,128)(2,1)S(1)} collective-permute-done((bf16[288,128]{1,0:T(8,128)(2,1)}, bf16[288,128]{1,0:T(8,128)(2,1)S(1)}, u32[]{:S(2)}, u32[]{:S(2)}) %collective-permute-start.17) | collective-permute-done | bytes 73760 | tf_op jit(solution)/shard_map/ppermute | solution.py:703
  124.1 0.0 collective-permute-done.18.refs_2_
  124.1 0.8 collective-permute-done.19.refs_3_
  124.9 0.1 collective-permute-start.22
  125.0 2.7 %collective-permute-start.23 = (bf16[16,2048]{1,0:T(8,128)(2,1)}, bf16[16,2048]{1,0:T(8,128)(2,1)S(1)}, u32[]{:S(2)}, u32[]{:S(2)}) collective-permute-start(bf16[16,2048]{1,0:T(8,128)(2,1)} %get-tuple-element.147.refs_3_), channel_id=1, source_target_pairs={{0,16},{8,24},{16,0},{24,8},{1,17},{9,25},{17,1},{25,9},{2,18},{10... | collective-permute-start | bytes 196616 | tf_op jit(solution)/shard_map/ppermute | solution.py:52
  127.7 1.1 collective-permute-start.24
  128.8 5.0 %row_gradients.1 = (f32[128,2048]{1,0:T(8,128)}, f32[8,2048]{1,0:T(8,128)}, f32[128,2048]{1,0:T(8,128)}, f32[16,2048]{1,0:T(8,128)}) custom-call(bf16[288,128]{1,0:T(8,128)(2,1)} %get-tuple-element.150.refs_0_, bf16[288,128]{1,0:T(8,128)(2,1)} %copy-done.17, bf16[288,128]{1,0:T(8,128)(2,1)} %copy-done.18, bf16[288,128]{1,0:T(8,128)(2,1)} %copy-done.19, ...), custom_call_target="tpu_custom_call" | custom-call | tf_op jit(solution)/shard_map/row_gradients/pallas_call | solution.py:640
  133.8 0.0 collective-permute-done.22.refs_4_
  133.9 0.6 copy-done.21
  134.5 0.0 copy-done.22
  134.5 0.0 copy-done.23
  134.5 1.7 %last_rows.1 = (bf16[128,2048]{1,0:T(8,128)(2,1)}, f32[4,2048]{1,0:T(4,128)}, f32[1,2048]{1,0:T(1,128)}, f32[1,2048]{1,0:T(1,128)}, f32[1,2048]{1,0:T(1,128)}) custom-call(bf16[128,2048]{1,0:T(8,128)(2,1)} %get-tuple-element.133.refs_0_, f32[16,2048]{1,0:T(8,128)} %get-tuple-element.134.refs_1_, f32[4,2048]{1,0:T(4,128)} %refs_2_.3, ...), custom_call_target="tpu_custom_call", output_to_operand_aliasing={{0}: (0, {})} | custom-call | tf_op jit(solution)/shard_map/last_rows/pallas_call | solution.py:680
  (49 shorter events, 0.2 us)
Async XLA Ops:
  0.6 26.2 %copy-start.16 = (f32[16,2048]{1,0:T(8,128)S(1)}, f32[16,2048]{1,0:T(8,128)}, u32[]{:S(2)}) copy-start(f32[16,2048]{1,0:T(8,128)} %param.18) | copy-start | bytes 393220
  1.5 6.4 %collective-permute-start = (bf16[3,2048]{1,0:T(4,128)(2,1)S(1)}, bf16[3,2048]{1,0:T(4,128)(2,1)S(1)}, u32[]{:S(2)}, u32[]{:S(2)}) collective-permute-start(bf16[3,2048]{1,0:T(4,128)(2,1)S(1)} %slice.3), channel_id=1, source_target_pairs={{0,8},{8,16},{16,24},{1,9},{9,17},{17,25},{2,10},{10,18},{18,26},{... | collective-permute-start | bytes 36872 | tf_op jit(solution)/shard_map/ppermute | solution.py:58
  7.8 0.6 copy-start.20
  13.3 5.0 %collective-permute-start.1 = (bf16[128,544]{1,0:T(8,128)(2,1)}, bf16[128,544]{1,0:T(8,128)(2,1)S(1)}, u32[]{:S(2)}, u32[]{:S(2)}) collective-permute-start(bf16[128,544]{1,0:T(8,128)(2,1)} %get-tuple-element.92), channel_id=1, source_target_pairs={{0,1},{1,0},{2,3},{3,2},{4,5},{5,4},{6,7},{7,6},{8,9},{9,8},{10,11... | collective-permute-start | bytes 417800 | tf_op jit(solution)/shard_map/ppermute | solution.py:703
  13.3 30.9 %collective-permute-start.4 = (bf16[128,2048]{1,0:T(8,128)(2,1)}, bf16[128,2048]{1,0:T(8,128)(2,1)S(1)}, u32[]{:S(2)}, u32[]{:S(2)}) collective-permute-start(bf16[128,2048]{1,0:T(8,128)(2,1)} %get-tuple-element.154.refs_5_.refs_3_.refs_4_), channel_id=1, source_target_pairs={{0,8},{8,0},{16,24},{24,16},{1,9},{9,1},{17,25},{25,17},{2,10},{10... | collective-permute-start | bytes 1572872 | tf_op jit(solution)/shard_map/ppermute | solution.py:703
  15.6 28.6 %collective-permute-start.5 = (bf16[128,2048]{1,0:T(8,128)(2,1)}, bf16[128,2048]{1,0:T(8,128)(2,1)S(1)}, u32[]{:S(2)}, u32[]{:S(2)}) collective-permute-start(bf16[128,2048]{1,0:T(8,128)(2,1)} %get-tuple-element.154.refs_5_.refs_3_.refs_4_), channel_id=1, source_target_pairs={{0,16},{8,24},{16,0},{24,8},{1,17},{9,25},{17,1},{25,9},{2,18},{10... | collective-permute-start | bytes 1572872 | tf_op jit(solution)/shard_map/ppermute | solution.py:703
  19.2 6.0 %collective-permute-start.2 = (bf16[128,544]{1,0:T(8,128)(2,1)S(1)}, bf16[128,544]{1,0:T(8,128)(2,1)S(1)}, u32[]{:S(2)}, u32[]{:S(2)}) collective-permute-start(bf16[128,544]{1,0:T(8,128)(2,1)S(1)} %add_convert_fusion.3), channel_id=1, source_target_pairs={{0,2},{1,3},{2,0},{3,1},{4,6},{5,7},{6,4},{7,5},{8,10},{9,11},{10,... | collective-permute-start | bytes 417800 | tf_op jit(solution)/shard_map/ppermute | solution.py:703
  25.3 5.4 %copy-start.2 = (bf16[128,544]{1,0:T(8,128)(2,1)}, bf16[128,544]{1,0:T(8,128)(2,1)S(1)}, u32[]{:S(2)}) copy-start(bf16[128,544]{1,0:T(8,128)(2,1)S(1)} %add_convert_fusion.2.refs_0_) | copy-start | bytes 417796
  25.3 5.4 %collective-permute-start.3 = (bf16[128,544]{1,0:T(8,128)(2,1)S(1)}, bf16[128,544]{1,0:T(8,128)(2,1)S(1)}, u32[]{:S(2)}, u32[]{:S(2)}) collective-permute-start(bf16[128,544]{1,0:T(8,128)(2,1)S(1)} %add_convert_fusion.2.refs_0_), channel_id=1, source_target_pairs={{0,4},{1,5},{2,6},{3,7},{4,0},{5,1},{6,2},{7,3},{8,12},{9,13},{10,... | collective-permute-start | bytes 417800 | tf_op jit(solution)/shard_map/ppermute | solution.py:703
  30.7 0.7 copy-start.15
  44.2 22.9 %copy-start.3 = (bf16[128,2048]{1,0:T(8,128)(2,1)}, bf16[128,2048]{1,0:T(8,128)(2,1)S(1)}, u32[]{:S(2)}) copy-start(bf16[128,2048]{1,0:T(8,128)(2,1)S(1)} %collective-permute-done.4.refs_5_) | copy-start | bytes 1572868
  44.2 22.9 %copy-start.4 = (bf16[128,2048]{1,0:T(8,128)(2,1)}, bf16[128,2048]{1,0:T(8,128)(2,1)S(1)}, u32[]{:S(2)}) copy-start(bf16[128,2048]{1,0:T(8,128)(2,1)S(1)} %collective-permute-done.5.refs_6_) | copy-start | bytes 1572868
  44.2 4.9 %collective-permute-start.6 = (bf16[2,18,8,128]{3,2,1,0:T(8,128)(2,1)}, bf16[2,18,8,128]{3,2,1,0:T(8,128)(2,1)S(1)}, u32[]{:S(2)}, u32[]{:S(2)}) collective-permute-start(bf16[2,18,8,128]{3,2,1,0:T(8,128)(2,1)} %get-tuple-element.99), channel_id=1, source_target_pairs={{0,8},{8,0},{16,24},{24,16},{1,9},{9,1},{17,25},{25,17},{2,10},{10... | collective-permute-start | bytes 221192 | tf_op jit(solution)/shard_map/ppermute | solution.py:703
  44.7 5.8 %collective-permute-start.7 = (bf16[2,18,8,128]{3,2,1,0:T(8,128)(2,1)}, bf16[2,18,8,128]{3,2,1,0:T(8,128)(2,1)S(1)}, u32[]{:S(2)}, u32[]{:S(2)}) collective-permute-start(bf16[2,18,8,128]{3,2,1,0:T(8,128)(2,1)} %get-tuple-element.100), channel_id=1, source_target_pairs={{0,16},{8,24},{16,0},{24,8},{1,17},{9,25},{17,1},{25,9},{2,18},{10... | collective-permute-start | bytes 221192 | tf_op jit(solution)/shard_map/ppermute | solution.py:703
  46.2 6.4 %collective-permute-start.8 = (bf16[2,18,8,128]{3,2,1,0:T(8,128)(2,1)}, bf16[2,18,8,128]{3,2,1,0:T(8,128)(2,1)S(1)}, u32[]{:S(2)}, u32[]{:S(2)}) collective-permute-start(bf16[2,18,8,128]{3,2,1,0:T(8,128)(2,1)} %get-tuple-element.101), channel_id=1, source_target_pairs={{0,24},{8,16},{16,8},{24,0},{1,25},{9,17},{17,9},{25,1},{2,26},{10... | collective-permute-start | bytes 221192 | tf_op jit(solution)/shard_map/ppermute | solution.py:703
  49.1 4.3 %copy-start.12 = (bf16[2,18,8,128]{3,2,1,0:T(8,128)(2,1)}, bf16[2,18,8,128]{3,2,1,0:T(8,128)(2,1)S(1)}, u32[]{:S(2)}) copy-start(bf16[2,18,8,128]{3,2,1,0:T(8,128)(2,1)S(1)} %collective-permute-done.6.refs_8_) | copy-start | bytes 221188
  50.5 2.9 %copy-start.13 = (bf16[2,18,8,128]{3,2,1,0:T(8,128)(2,1)}, bf16[2,18,8,128]{3,2,1,0:T(8,128)(2,1)S(1)}, u32[]{:S(2)}) copy-start(bf16[2,18,8,128]{3,2,1,0:T(8,128)(2,1)S(1)} %collective-permute-done.7.refs_9_) | copy-start | bytes 221188
  52.6 0.8 copy-start.14
  52.6 18.1 %collective-permute-start.9 = (bf16[128,2048]{1,0:T(8,128)(2,1)S(1)}, bf16[128,2048]{1,0:T(8,128)(2,1)S(1)}, u32[]{:S(2)}, u32[]{:S(2)}) collective-permute-start(bf16[128,2048]{1,0:T(8,128)(2,1)S(1)} %collective-permute-done.5.refs_6_), channel_id=1, source_target_pairs={{0,8},{8,0},{16,24},{24,16},{1,9},{9,1},{17,25},{25,17},{2,10},{10... | collective-permute-start | bytes 1572872 | tf_op jit(solution)/shard_map/ppermute | solution.py:703
  67.1 17.4 %collective-permute-start.10 = (bf16[144,1024]{1,0:T(8,128)(2,1)}, bf16[144,1024]{1,0:T(8,128)(2,1)S(1)}, u32[]{:S(2)}, u32[]{:S(2)}) collective-permute-start(bf16[144,1024]{1,0:T(8,128)(2,1)} %get-tuple-element.158.refs_8_), channel_id=1, source_target_pairs={{0,8},{8,0},{16,24},{24,16},{1,9},{9,1},{17,25},{25,17},{2,10},{10... | collective-permute-start | bytes 884744 | tf_op jit(solution)/shard_map/ppermute | solution.py:703
  68.4 16.1 %collective-permute-start.11 = (bf16[144,1024]{1,0:T(8,128)(2,1)}, bf16[144,1024]{1,0:T(8,128)(2,1)S(1)}, u32[]{:S(2)}, u32[]{:S(2)}) collective-permute-start(bf16[144,1024]{1,0:T(8,128)(2,1)} %get-tuple-element.158.refs_8_), channel_id=1, source_target_pairs={{0,16},{8,24},{16,0},{24,8},{1,17},{9,25},{17,1},{25,9},{2,18},{10... | collective-permute-start | bytes 884744 | tf_op jit(solution)/shard_map/ppermute | solution.py:703
  70.7 13.7 %copy-start.5 = (bf16[128,2048]{1,0:T(8,128)(2,1)}, bf16[128,2048]{1,0:T(8,128)(2,1)S(1)}, u32[]{:S(2)}) copy-start(bf16[128,2048]{1,0:T(8,128)(2,1)S(1)} %collective-permute-done.9.refs_7_) | copy-start | bytes 1572868
  84.5 36.7 %copy-start.6 = (bf16[144,1024]{1,0:T(8,128)(2,1)}, bf16[144,1024]{1,0:T(8,128)(2,1)S(1)}, u32[]{:S(2)}) copy-start(bf16[144,1024]{1,0:T(8,128)(2,1)S(1)} %collective-permute-done.10.refs_9_) | copy-start | bytes 884740
  84.5 36.7 %copy-start.7 = (bf16[144,1024]{1,0:T(8,128)(2,1)}, bf16[144,1024]{1,0:T(8,128)(2,1)S(1)}, u32[]{:S(2)}) copy-start(bf16[144,1024]{1,0:T(8,128)(2,1)S(1)} %collective-permute-done.11.refs_10_) | copy-start | bytes 884740
  84.5 1.7 %collective-permute-start.12 = (bf16[640,128]{1,0:T(8,128)(2,1)}, bf16[640,128]{1,0:T(8,128)(2,1)S(1)}, u32[]{:S(2)}, u32[]{:S(2)}) collective-permute-start(bf16[640,128]{1,0:T(8,128)(2,1)} %get-tuple-element.124), channel_id=1, source_target_pairs={{0,1},{1,0},{2,3},{3,2},{4,5},{5,4},{6,7},{7,6},{8,9},{9,8},{10,11... | collective-permute-start | bytes 491528 | tf_op jit(solution)/shard_map/ppermute | solution.py:703
  87.2 6.3 %collective-permute-start.13 = (bf16[640,128]{1,0:T(8,128)(2,1)S(1)}, bf16[640,128]{1,0:T(8,128)(2,1)S(1)}, u32[]{:S(2)}, u32[]{:S(2)}) collective-permute-start(bf16[640,128]{1,0:T(8,128)(2,1)S(1)} %add_convert_fusion.1), channel_id=1, source_target_pairs={{0,2},{1,3},{2,0},{3,1},{4,6},{5,7},{6,4},{7,5},{8,10},{9,11},{10,... | collective-permute-start | bytes 491528 | tf_op jit(solution)/shard_map/ppermute | solution.py:703
  88.7 13.3 %collective-permute-start.15 = (bf16[144,1024]{1,0:T(8,128)(2,1)}, bf16[144,1024]{1,0:T(8,128)(2,1)S(1)}, u32[]{:S(2)}, u32[]{:S(2)}) collective-permute-start(bf16[144,1024]{1,0:T(8,128)(2,1)} %get-tuple-element.162.refs_12_), channel_id=1, source_target_pairs={{0,8},{8,0},{16,24},{24,16},{1,9},{9,1},{17,25},{25,17},{2,10},{10... | collective-permute-start | bytes 884744 | tf_op jit(solution)/shard_map/ppermute | solution.py:703
  90.1 16.0 %collective-permute-start.16 = (bf16[144,1024]{1,0:T(8,128)(2,1)}, bf16[144,1024]{1,0:T(8,128)(2,1)S(1)}, u32[]{:S(2)}, u32[]{:S(2)}) collective-permute-start(bf16[144,1024]{1,0:T(8,128)(2,1)} %get-tuple-element.162.refs_12_), channel_id=1, source_target_pairs={{0,16},{8,24},{16,0},{24,8},{1,17},{9,25},{17,1},{25,9},{2,18},{10... | collective-permute-start | bytes 884744 | tf_op jit(solution)/shard_map/ppermute | solution.py:703
  93.5 14.7 %copy-start = (bf16[640,128]{1,0:T(8,128)(2,1)}, bf16[640,128]{1,0:T(8,128)(2,1)S(1)}, u32[]{:S(2)}) copy-start(bf16[640,128]{1,0:T(8,128)(2,1)S(1)} %add_convert_fusion.back_a.refs_0_) | copy-start | bytes 491524
  93.5 12.6 %collective-permute-start.14 = (bf16[640,128]{1,0:T(8,128)(2,1)S(1)}, bf16[640,128]{1,0:T(8,128)(2,1)S(1)}, u32[]{:S(2)}, u32[]{:S(2)}) collective-permute-start(bf16[640,128]{1,0:T(8,128)(2,1)S(1)} %add_convert_fusion.back_a.refs_0_), channel_id=1, source_target_pairs={{0,4},{1,5},{2,6},{3,7},{4,0},{5,1},{6,2},{7,3},{8,12},{9,13},{10,... | collective-permute-start | bytes 491528 | tf_op jit(solution)/shard_map/ppermute | solution.py:703
  102.1 26.7 %copy-start.8 = (bf16[144,1024]{1,0:T(8,128)(2,1)}, bf16[144,1024]{1,0:T(8,128)(2,1)S(1)}, u32[]{:S(2)}) copy-start(bf16[144,1024]{1,0:T(8,128)(2,1)S(1)} %collective-permute-done.15.refs_13_) | copy-start | bytes 884740
  106.1 22.7 %copy-start.9 = (bf16[144,1024]{1,0:T(8,128)(2,1)}, bf16[144,1024]{1,0:T(8,128)(2,1)S(1)}, u32[]{:S(2)}) copy-start(bf16[144,1024]{1,0:T(8,128)(2,1)S(1)} %collective-permute-done.16.refs_14_) | copy-start | bytes 884740
  106.1 2.1 %copy-start.1 = (bf16[640,128]{1,0:T(8,128)(2,1)}, bf16[640,128]{1,0:T(8,128)(2,1)S(1)}, u32[]{:S(2)}) copy-start(bf16[640,128]{1,0:T(8,128)(2,1)S(1)} %collective-permute-done.14.back_b.refs_1_) | copy-start | bytes 491524
  106.1 18.8 %collective-permute-start.20 = (bf16[144,1024]{1,0:T(8,128)(2,1)S(1)}, bf16[144,1024]{1,0:T(8,128)(2,1)S(1)}, u32[]{:S(2)}, u32[]{:S(2)}) collective-permute-start(bf16[144,1024]{1,0:T(8,128)(2,1)S(1)} %collective-permute-done.11.refs_10_), channel_id=1, source_target_pairs={{0,8},{8,0},{16,24},{24,16},{1,9},{9,1},{17,25},{25,17},{2,10},{10... | collective-permute-start | bytes 884744 | tf_op jit(solution)/shard_map/ppermute | solution.py:703
  106.2 18.7 %collective-permute-start.21 = (bf16[144,1024]{1,0:T(8,128)(2,1)S(1)}, bf16[144,1024]{1,0:T(8,128)(2,1)S(1)}, u32[]{:S(2)}, u32[]{:S(2)}) collective-permute-start(bf16[144,1024]{1,0:T(8,128)(2,1)S(1)} %collective-permute-done.16.refs_14_), channel_id=1, source_target_pairs={{0,8},{8,0},{16,24},{24,16},{1,9},{9,1},{17,25},{25,17},{2,10},{10... | collective-permute-start | bytes 884744 | tf_op jit(solution)/shard_map/ppermute | solution.py:703
  110.1 14.0 %collective-permute-start.17 = (bf16[288,128]{1,0:T(8,128)(2,1)}, bf16[288,128]{1,0:T(8,128)(2,1)S(1)}, u32[]{:S(2)}, u32[]{:S(2)}) collective-permute-start(bf16[288,128]{1,0:T(8,128)(2,1)} %get-tuple-element.138), channel_id=1, source_target_pairs={{0,8},{8,0},{16,24},{24,16},{1,9},{9,1},{17,25},{25,17},{2,10},{10... | collective-permute-start | bytes 221192 | tf_op jit(solution)/shard_map/ppermute | solution.py:703
  110.1 14.0 %collective-permute-start.18 = (bf16[288,128]{1,0:T(8,128)(2,1)}, bf16[288,128]{1,0:T(8,128)(2,1)S(1)}, u32[]{:S(2)}, u32[]{:S(2)}) collective-permute-start(bf16[288,128]{1,0:T(8,128)(2,1)} %get-tuple-element.139), channel_id=1, source_target_pairs={{0,16},{8,24},{16,0},{24,8},{1,17},{9,25},{17,1},{25,9},{2,18},{10... | collective-permute-start | bytes 221192 | tf_op jit(solution)/shard_map/ppermute | solution.py:703
  110.4 14.5 %collective-permute-start.19 = (bf16[288,128]{1,0:T(8,128)(2,1)}, bf16[288,128]{1,0:T(8,128)(2,1)S(1)}, u32[]{:S(2)}, u32[]{:S(2)}) collective-permute-start(bf16[288,128]{1,0:T(8,128)(2,1)} %get-tuple-element.140), channel_id=1, source_target_pairs={{0,24},{8,16},{16,8},{24,0},{1,25},{9,17},{17,9},{25,1},{2,26},{10... | collective-permute-start | bytes 221192 | tf_op jit(solution)/shard_map/ppermute | solution.py:703
  124.1 4.7 %copy-start.17 = (bf16[288,128]{1,0:T(8,128)(2,1)}, bf16[288,128]{1,0:T(8,128)(2,1)S(1)}, u32[]{:S(2)}) copy-start(bf16[288,128]{1,0:T(8,128)(2,1)S(1)} %collective-permute-done.17.refs_1_) | copy-start | bytes 221188
  124.1 4.7 %copy-start.18 = (bf16[288,128]{1,0:T(8,128)(2,1)}, bf16[288,128]{1,0:T(8,128)(2,1)S(1)}, u32[]{:S(2)}) copy-start(bf16[288,128]{1,0:T(8,128)(2,1)S(1)} %collective-permute-done.18.refs_2_) | copy-start | bytes 221188
  124.9 3.9 %copy-start.19 = (bf16[288,128]{1,0:T(8,128)(2,1)}, bf16[288,128]{1,0:T(8,128)(2,1)S(1)}, u32[]{:S(2)}) copy-start(bf16[288,128]{1,0:T(8,128)(2,1)S(1)} %collective-permute-done.19.refs_3_) | copy-start | bytes 221188
  124.9 3.9 %copy-start.10 = (bf16[144,1024]{1,0:T(8,128)(2,1)}, bf16[144,1024]{1,0:T(8,128)(2,1)S(1)}, u32[]{:S(2)}) copy-start(bf16[144,1024]{1,0:T(8,128)(2,1)S(1)} %collective-permute-done.20.refs_11_) | copy-start | bytes 884740
  124.9 3.9 %copy-start.11 = (bf16[144,1024]{1,0:T(8,128)(2,1)}, bf16[144,1024]{1,0:T(8,128)(2,1)S(1)}, u32[]{:S(2)}) copy-start(bf16[144,1024]{1,0:T(8,128)(2,1)S(1)} %collective-permute-done.21.refs_15_) | copy-start | bytes 884740
  124.9 8.9 %collective-permute-start.22 = (bf16[16,2048]{1,0:T(8,128)(2,1)}, bf16[16,2048]{1,0:T(8,128)(2,1)S(1)}, u32[]{:S(2)}, u32[]{:S(2)}) collective-permute-start(bf16[16,2048]{1,0:T(8,128)(2,1)} %get-tuple-element.147.refs_3_), channel_id=1, source_target_pairs={{0,8},{8,16},{16,24},{24,0},{1,9},{9,17},{17,25},{25,1},{2,10},{10... | collective-permute-start | bytes 196616 | tf_op jit(solution)/shard_map/ppermute | solution.py:52
  125.0 8.9 %collective-permute-start.23 = (bf16[16,2048]{1,0:T(8,128)(2,1)}, bf16[16,2048]{1,0:T(8,128)(2,1)S(1)}, u32[]{:S(2)}, u32[]{:S(2)}) collective-permute-start(bf16[16,2048]{1,0:T(8,128)(2,1)} %get-tuple-element.147.refs_3_), channel_id=1, source_target_pairs={{0,16},{8,24},{16,0},{24,8},{1,17},{9,25},{17,1},{25,9},{2,18},{10... | collective-permute-start | bytes 196616 | tf_op jit(solution)/shard_map/ppermute | solution.py:52
  127.7 6.2 %collective-permute-start.24 = (bf16[16,2048]{1,0:T(8,128)(2,1)}, bf16[16,2048]{1,0:T(8,128)(2,1)S(1)}, u32[]{:S(2)}, u32[]{:S(2)}) collective-permute-start(bf16[16,2048]{1,0:T(8,128)(2,1)} %get-tuple-element.147.refs_3_), channel_id=1, source_target_pairs={{0,24},{8,0},{16,8},{24,16},{1,25},{9,1},{17,9},{25,17},{2,26},{10... | collective-permute-start | bytes 196616 | tf_op jit(solution)/shard_map/ppermute | solution.py:52
  133.8 0.6 copy-start.21
  133.8 0.6 copy-start.22
  133.9 0.6 copy-start.23

commit v8 on v7

--- a/solution.py
+++ b/solution.py
@@ -131,9 +131,9 @@
 def local_kernel(low_rank, states, places, *refs):
     parts, refs = refs[:2], refs[2:]
     (weight_ref, bias_ref, decay_ref, conv_ref, gate_ref, grad_ref) = refs[:6]
-    (dt_ref, coef_ref, low, low_t) = refs[6:10]
-    messages, refs = refs[10 : 9 + places], refs[9 + places :]
-    (proj, coef_v, coef, dts, dxs, gs, fwd, bwd, sem) = refs
+    (dt_ref, coef_ref, low) = refs[6:9]
+    messages, refs = refs[9 : 8 + places], refs[8 + places :]
+    (coef_v, coef, dts, dxs, gs, fwd, bwd, sem) = refs
     step = pl.program_id(0)
     chunks = dts.shape[0]
     rows = conv_ref.shape[0]
@@ -142,13 +142,11 @@
     @pl.when(step == 0)
     def _():
         total = (parts[0][...].astype(F32) + parts[1][...].astype(F32)).astype(BF)
-        proj[...] = total.astype(F32)
         low[...] = total[:, :low_rank]
-        low_t[...] = jnp.transpose(proj[:, :low_rank]).astype(BF)
         coef_v[...] = jnp.zeros_like(coef_v)
-        coef_v[:, : 2 * states] = proj[:, low_rank:]
-        coef_ref[...] = coef_v[...]
-        copy = pltpu.make_async_copy(coef_v, coef, sem)
+        coef_v[:, : 2 * states] = total[:, low_rank:].astype(F32)
+        coef_ref[...] = jnp.transpose(coef_v[...])[: 2 * states, :]
+        copy = pltpu.make_async_copy(coef_ref, coef, sem)
         copy.start()
         copy.wait()
 
@@ -191,9 +189,9 @@
                         total = [a + b for a, b in zip(total, size)]
                     for k, (n, v) in enumerate(pairs):
                         factor = jnp.exp2(size[v] * rates[k])
-                        state[k] = factor * state[k] + drive[v] * coef[token, n]
+                        state[k] = factor * state[k] + drive[v] * coef[n, token]
                         run[k] = run[k] * factor
-                        head[k] = head[k] + run[k] * (grad[v] * coef[token, states + n])
+                        head[k] = head[k] + run[k] * (grad[v] * coef[states + n, token])
                 return state, run, head, total
 
             many = [zero] * len(pairs)
@@ -240,22 +238,19 @@
         ],
         out_specs=[
             pl.BlockSpec((1, rows * groups, 128), lambda i: (i, 0, 0)),
-            whole((rows, 128)),
+            whole((2 * states, rows)),
             whole((rows, low_rank)),
-            whole((low_rank, rows)),
         ]
         + [whole(message)] * (places - 1),
         out_shape=[
             sds((chunks, rows * groups, 128), F32),
-            sds((rows, 128), F32),
+            sds((2 * states, rows), F32),
             sds((rows, low_rank), BF),
-            sds((low_rank, rows), BF),
         ]
         + [sds(message, BF)] * (places - 1),
         scratch_shapes=[
-            pltpu.VMEM((rows, wide), F32),
             pltpu.VMEM((rows, 128), F32),
-            pltpu.SMEM((rows, 128), F32),
+            pltpu.SMEM((2 * states, rows), F32),
             big,
             big,
             big,
@@ -268,11 +263,11 @@
     )(*parts, step_weight, step_bias, decay, conv_out, gate, grad)
 
 
-def fold_rows(products, base, groups, target, first):
+def fold_rows(products, base, groups, target, first, stride):
     total = products[pl.ds(base, 8, stride=groups), :]
     for row in range(1, groups):
         total = total + products[pl.ds(base + row, 8, stride=groups), :]
-    target[pl.ds(pl.multiple_of(first, 8), 8), :] = total
+    target[pl.ds(first, 8, stride=stride), :] = total
 
 
 def scan_kernel(places, states, opening, *refs):
@@ -336,11 +331,11 @@
                     kept = factor * state[n]
                     factors[token, n] = factor
                     decayed[token, n] = kept
-                    state[n] = kept + drive * coef[token, n]
-                    result = result + state[n] * coef[token, states + n]
+                    state[n] = kept + drive * coef[n, token]
+                    result = result + state[n] * coef[states + n, token]
                     row = base + (n - lead) * groups
                     products[row : row + groups, :] = state[n] * grad
-                fold_rows(products, base, groups, coef_out, token * states + lead)
+                fold_rows(products, base, groups, coef_out, lead * rows + token, rows)
             ys[at, :] = result
         return state
 
@@ -358,15 +353,15 @@
             for lead in range(0, states, 8):
                 base = (sub * states + lead) * groups
                 for n in range(lead, lead + 8):
-                    adjoint = carry[n] + grad * coef[token, states + n]
+                    adjoint = carry[n] + grad * coef[states + n, token]
                     carry[n] = factors[token, n] * adjoint
                     weighted = adjoint * decayed[token, n] * (size * rate[n])
                     slope = slope + weighted
                     gathered[n] = gathered[n] + weighted
-                    inner = inner + adjoint * coef[token, n]
+                    inner = inner + adjoint * coef[n, token]
                     row = base + (n - lead) * groups
                     products[row : row + groups, :] = adjoint * drive
-                fold_rows(products, base, groups, coef_in, token * states + lead)
+                fold_rows(products, base, groups, coef_in, lead * rows + token, rows)
             dds[at, :] = slope
             qs[at, :] = inner
         return carry, gathered
@@ -425,13 +420,15 @@
     )
 
     pre_bf = pre_ref[:rows, :]
-    lanes = lax.broadcasted_iota(jnp.int32, (2 * states, 128), 0)
-    coefs = jnp.zeros((2 * states, rows), F32)
-    for n in range(states):
-        at = pl.ds(n, rows, stride=states)
-        for kind, source in enumerate((coef_in, coef_out)):
-            pick = jnp.where(lanes == kind * states + n, 1.0, 0.0).astype(BF)
-            coefs = coefs + dot(pick, source[at, :].astype(BF), NT)
+    ones = jnp.ones((8, 128), BF)
+    coefs = jnp.concatenate(
+        [
+            sums[:1, n * rows : n * rows + rows]
+            for sums in (dot(ones, source[...].astype(BF), NT) for source in (coef_in, coef_out))
+            for n in range(states)
+        ],
+        axis=0,
+    )
     wide = dot(weight_ref[...], pre_bf, NT)
 
     ranks, coef_rows, block = low_rank // places, 2 * states // places, acc.shape[0] // places
@@ -581,73 +578,90 @@
     )(*backs, proj_weight, scan_part, small, conv_input, rim, weight, bias)
 
 
-def cut_kernel(places, *refs):
-    back_a, back_b, low_t = refs[:3]
-    cuts, (back,) = refs[3 : 3 + places], refs[3 + places :]
+def cut_kernel(places, back_a, back_b, *refs):
+    cuts, (back,) = refs[:places], refs[places:]
     place = lax.axis_index("ctx")
-    back_rows, ranks = back.shape[0] // places, low_t.shape[0] // places
+    height = back.shape[0] // places
     back[...] = back_a[...].astype(F32) + back_b[...].astype(F32)
     for mask in range(places):
-        other = place ^ mask
-        cuts[mask][:back_rows, :] = back[pl.ds(other * back_rows, back_rows), :].astype(BF)
-        cuts[mask][back_rows:, :] = low_t[pl.ds(pl.multiple_of(other * ranks, 16), ranks), :]
-
-
-def cut_call(places, backs, low_t):
+        cuts[mask][...] = back[pl.ds((place ^ mask) * height, height), :].astype(BF)
+
+
+def cut_call(places, backs):
     wide, rows = backs[0].shape
-    cut = ((wide + low_t.shape[0]) // places, rows)
     return pl.pallas_call(
         functools.partial(cut_kernel, places),
-        out_shape=[sds(cut, BF)] * places,
+        out_shape=[sds((wide // places, rows), BF)] * places,
         scratch_shapes=[pltpu.VMEM((wide, rows), F32)],
         compiler_params=params(),
         name="cut_rows",
-    )(*backs, low_t)
-
-
-def rows_kernel(places, rank_rows, chunks, *refs):
-    cuts, refs = refs[:places], refs[places:]
-    blocks, refs = refs[:places], refs[places:]
-    steps, refs = refs[: chunks * places], refs[chunks * places :]
-    out_ref, coef_ref, step_ref, decay_ref = refs
+    )(*backs)
+
+
+def step_kernel(chunks, ranks, near, *refs):
+    lows, steps, (mine_ref, theirs_ref) = refs[:near], refs[near:-2], refs[-2:]
     place = lax.axis_index("ctx")
-    rows = blocks[0].shape[0]
-    back_rows = cuts[0].shape[0] - rank_rows
-    total = jnp.zeros((back_rows, out_ref.shape[1]), F32)
-    for cut, block in zip(cuts, blocks):
-        total = total + dot(cut[:back_rows, :], block[...])
-    out_ref[...] = total[:rank_rows, :]
-    coef_ref[...] = total[rank_rows : rank_rows + coef_ref.shape[0], :]
+    rows = lows[0].shape[1]
+    pair = pl.ds(pl.multiple_of(lax.div(place, 2) * (2 * ranks), 16), 2 * ranks)
+    odd = lax.rem(place, 2) == 1
     for chunk in range(chunks):
 
         @pl.when(pl.program_id(0) == chunk)
         def _():
-            total = jnp.zeros(step_ref.shape, F32)
-            decay = jnp.zeros(decay_ref.shape, F32)
-            for mask in range(places):
-                step = steps[chunk * places + mask]
-                total = total + dot(cuts[mask][back_rows:, :], step[:rows, :])
+            total = jnp.zeros((2 * ranks, mine_ref.shape[1]), F32)
+            decay = jnp.zeros((mine_ref.shape[0] - ranks, mine_ref.shape[1]), F32)
+            for low, step in zip(lows, steps[chunk * near : (chunk + 1) * near]):
+                total = total + dot(low[pair, :], step[:rows, :])
                 decay = decay + step[rows:, :].astype(F32)
-            step_ref[...] = total
-            decay_ref[...] = decay
-
-
-def rows_call(places, rank_rows, coef_rows, cuts, blocks, steps):
+            mine_ref[:ranks, :] = jnp.where(odd, total[ranks:, :], total[:ranks, :])
+            theirs_ref[:ranks, :] = jnp.where(odd, total[:ranks, :], total[ranks:, :]).astype(BF)
+            mine_ref[ranks:, :] = decay
+            theirs_ref[ranks:, :] = decay.astype(BF)
+
+
+def step_call(ranks, lows, steps):
+    rows = lows[0].shape[1]
+    chunks = len(steps) // len(lows)
+    tall, width = steps[0].shape
+    height = ranks + tall - rows
+    return pl.pallas_call(
+        functools.partial(step_kernel, chunks, ranks, len(lows)),
+        grid=(chunks,),
+        in_specs=[whole(lows[0].shape)] * len(lows) + [whole((tall, width))] * len(steps),
+        out_specs=[columns(height, width)] * 2,
+        out_shape=[sds((height, width * chunks), F32), sds((height, width * chunks), BF)],
+        compiler_params=params(),
+        name="step_products",
+    )(*lows, *steps)
+
+
+def rows_kernel(ranks, places, *refs):
+    cuts, blocks, refs = refs[:places], refs[places : 2 * places], refs[2 * places :]
+    mine_ref, theirs_ref, out_ref, coef_ref, step_ref, decay_ref = refs
+    total = jnp.zeros((cuts[0].shape[0], out_ref.shape[1]), F32)
+    for cut, block in zip(cuts, blocks):
+        total = total + dot(cut[...], block[...])
+    out_ref[...] = total[:ranks, :]
+    coef_ref[...] = total[ranks : ranks + coef_ref.shape[0], :]
+    step_ref[...] = mine_ref[:ranks, :] + theirs_ref[:ranks, :].astype(F32)
+    decay_ref[...] = mine_ref[ranks:, :] + theirs_ref[ranks:, :].astype(F32)
+
+
+def rows_call(ranks, coef_rows, cuts, blocks, mine, theirs):
     rows, chans = blocks[0].shape
-    tall, width = steps[0].shape
-    chunks = chans // width
-    heights = (rank_rows, coef_rows, rank_rows, tall - rows)
+    width = min(1024, chans)
+    heights = (ranks, coef_rows, ranks, mine.shape[0] - ranks)
     return pl.pallas_call(
-        functools.partial(rows_kernel, places, rank_rows, chunks),
-        grid=(chunks,),
-        in_specs=[whole(cuts[0].shape)] * places
-        + [columns(rows, width)] * places
-        + [whole((tall, width))] * len(steps),
+        functools.partial(rows_kernel, ranks, len(cuts)),
+        grid=(chans // width,),
+        in_specs=[whole(cuts[0].shape)] * len(cuts)
+        + [columns(rows, width)] * len(blocks)
+        + [columns(mine.shape[0], width)] * 2,
         out_specs=[columns(height, width) for height in heights],
         out_shape=[sds((height, chans), F32) for height in heights],
         compiler_params=params(),
         name="row_gradients",
-    )(*cuts, *blocks, *steps)
+    )(*cuts, *blocks, mine, theirs)
 
 
 def last_kernel(places, taps, *refs):
@@ -715,6 +729,10 @@
     if places == 4:
         return blocks + [swap(blocks[2], "ctx", 1)]
     return blocks + [swap(blocks[0], "ctx", mask) for mask in range(3, places)]
+
+
+def gather_near(block):
+    return [block] + [swap(block, "ctx", mask) for mask in range(2, lax.axis_size("ctx"), 2)]
 
 
 def chan_sum(part):
@@ -755,13 +773,14 @@
     conv_out, part = conv_call(conv_input, rim, conv_weight, conv_bias, proj_weight)
     blocks = spread(conv_out)
     parts = chan_sum(part)
-    dt, coef, low, low_t, *messages = local_call(
+    dt, coef, low, *messages = local_call(
         parts, step_weight, step_bias, decay, conv_out, gate_input, out_grad, states, places
     )
     messages, blocks = tie((messages, blocks))
     messages = [swap(message, "ctx", mask) for mask, message in enumerate(messages, 1)]
-    messages, blocks = tie((messages, blocks))
+    messages, blocks, low = tie((messages, blocks, low))
     blocks = spread_on(blocks)
+    lows = gather_near(jnp.transpose(low))
     previous, steps = [], []
     for chunk in range(chunks):
         message, grad_gate, scan_part, small, part = scan_call(
@@ -772,22 +791,24 @@
         if chunk == 0:
             previous, blocks = tie((previous, blocks))
         else:
-            previous, steps[-1] = tie((previous, steps[-1]))
-        steps.append(spread(message))
+            previous, steps, lows = tie((previous, steps, lows))
+        steps += gather_near(message)
     part, grad_gate, scan_part, small = previous
     backs = chan_sum(part)
-    backs, steps = tie((backs, steps))
-    steps = [block for step in steps for block in spread_on(step)]
-    cuts = cut_call(places, backs, low_t)
+    cuts = cut_call(places, backs)
+    cuts, lows = tie((cuts, lows))
     cuts = [cuts[0]] + [swap(cut, "ctx", mask) for mask, cut in enumerate(cuts[1:], 1)]
+    mine, theirs = step_call(low_rank // places, lows, steps)
+    backs, theirs = tie((backs, theirs))
+    theirs = swap(theirs, "ctx", 1)
     main, tail, sums = conv_grad_call(
         places, low_rank, backs, proj_weight, scan_part, small, conv_input, rim, conv_weight,
         conv_bias,
     )
-    sums, cuts, steps = tie((sums, cuts, steps))
+    sums, cuts = tie((sums, cuts))
     late = [sums] + [rotate(sums, "ctx", hop) for hop in range(1, places)]
     grad_proj, grad_coef, grad_step, decay_grad = rows_call(
-        places, low_rank // places, 2 * states // places, cuts, blocks, steps
+        low_rank // places, 2 * states // places, cuts, blocks, mine, theirs
     )
     grad_input, conv_w, conv_b, step_b, skip = last_call(main, tail, conv_weight, late)
     return (

time: 137 us -> 145 us (1.058)
  waiting for transfers between devices: 32.5 us -> 39.7 us
  starting transfers between devices: 36.9 us -> 32.8 us
  Pallas kernels: 60.3 us -> 63.3 us
  local copies, waits for them, and re-layouts: 3.48 us -> 5.75 us
    ppermute x3, waiting for transfers between devices: 0.01 us -> 5.89 us  [rotate(): lax.ppermute(block, axis, [(i, (i + distance) % count) for i in range(cou...]
    ppermute x21 -> x19, starting transfers between devices: 28.1 us -> 25.3 us  [swap(): lax.ppermute(block, axis, [(i, i ^ mask) for i in range(lax.axis_size(axi...]
    unnamed x49, local copies, waits for them, and re-layouts: 2.01 us -> 4.16 us
    pallas_call x2, Pallas kernels: 27.4 us -> 29.4 us  [scan_call(): pl.pallas_call(functools.partial(scan_kernel, places, states, first), gri...]
    pallas_call x2 -> x3, Pallas kernels: 6.82 us -> 8.52 us  [the longest x1 3.65 us: rows_call(): pl.pallas_call(functools.partial(rows_kernel, ranks, len(cuts)), grid=(ch...]
    ppermute x21 -> x19, waiting for transfers between devices: 31.1 us -> 32.4 us  [swap(): lax.ppermute(block, axis, [(i, i ^ mask) for i in range(lax.axis_size(axi...]
  transfers between devices with their start and end apart: 25 -> 23, of which waited for: 12 -> 14; matrix products, arithmetic and copies ran while one was open for 1% -> 1% of each run, Pallas kernels for 39% -> 36%
where the time goes in v8:
time: 145 us; the launch traced here: 144 us
  Pallas kernels  63.3 us (44%)
  waiting for transfers between devices  39.7 us (27%)
  starting transfers between devices  32.8 us (23%)
  local copies, waits for them, and re-layouts  5.75 us (4%)
  other arithmetic  2.02 us (1%)
    ppermute x19, waiting for transfers between devices, swap(): lax.ppermute(block, axis, [(i, i ^ mask) for i in range(lax.axis_size(axi...  32.4 us
    pallas_call x2, Pallas kernels, scan_call(): pl.pallas_call(functools.partial(scan_kernel, places, states, first), gri...  29.4 us
    ppermute x19, starting transfers between devices, swap(): lax.ppermute(block, axis, [(i, i ^ mask) for i in range(lax.axis_size(axi...  25.3 us
    pallas_call x1, Pallas kernels, local_call(): pl.pallas_call(functools.partial(local_kernel, low_rank, states, places),...  12.1 us
    pallas_call x1, Pallas kernels, conv_grad_call(): pl.pallas_call(functools.partial(conv_grad_kernel, places, low_rank), gri...  6.75 us
    ppermute x3, waiting for transfers between devices, rotate(): lax.ppermute(block, axis, [(i, (i + distance) % count) for i in range(cou...  5.89 us
    ppermute x1, starting transfers between devices, shift(): return lax.ppermute(block, axis, route)  4.93 us
    pallas_call x1, Pallas kernels, conv_call(): pl.pallas_call(conv_kernel, grid=(chans // width,), in_specs=[columns(row...  4.84 us
  transfers between devices with their start and end apart: 23, of which 14 were waited for; matrix products, arithmetic and copies ran while one was open for 1% of the time, Pallas kernels for 36%

profile of v8, /device:TPU:0, one launch (start us, length us, event | category | flops | bytes accessed | tf_op | source)
XLA Modules:
  0.0 144.4 jit_solution(11506448217052726086)
XLA Ops:
  0.7 0.8 slice.3
  1.5 4.9 %collective-permute-start = (bf16[3,2048]{1,0:T(4,128)(2,1)S(1)}, bf16[3,2048]{1,0:T(4,128)(2,1)S(1)}, u32[]{:S(2)}, u32[]{:S(2)}) collective-permute-start(bf16[3,2048]{1,0:T(4,128)(2,1)S(1)} %slice.3), channel_id=1, source_target_pairs={{0,8},{8,16},{16,24},{1,9},{9,17},{17,25},{2,10},{10,18},{18,26},{... | collective-permute-start | bytes 36872 | tf_op jit(solution)/shard_map/ppermute | solution.py:58
  6.4 1.4 collective-permute-done.rim_ref
  7.8 0.6 copy-done.17
  8.4 4.8 %conv_project.1 = (bf16[128,2048]{1,0:T(8,128)(2,1)}, bf16[128,544]{1,0:T(8,128)(2,1)}) custom-call(bf16[128,2048]{1,0:T(8,128)(2,1)} %input_ref.3, bf16[3,2048]{1,0:T(4,128)(2,1)} %copy-done.17, f32[4,2048]{1,0:T(4,128)} %refs_2_.3, f32[1,2048]{1,0:T(1,128)} %bitcast.22, bf16[544,2048]{1,0:T(8,128)(2,1)} %proj_ref.3), custom_call_target="tpu_custom_call" | custom-call | tf_op jit(solution)/shard_map/conv_project/pallas_call | solution.py:103
  13.3 0.0 collective-permute-start.1
  13.3 3.4 %collective-permute-start.5 = (bf16[128,2048]{1,0:T(8,128)(2,1)}, bf16[128,2048]{1,0:T(8,128)(2,1)S(1)}, u32[]{:S(2)}, u32[]{:S(2)}) collective-permute-start(bf16[128,2048]{1,0:T(8,128)(2,1)} %get-tuple-element.154.refs_5_.refs_3_.refs_4_), channel_id=1, source_target_pairs={{0,16},{8,24},{16,0},{24,8},{1,17},{9,25},{17,1},{25,9},{2,18},{10... | collective-permute-start | bytes 1572872 | tf_op jit(solution)/shard_map/ppermute | solution.py:717
  16.6 1.6 %collective-permute-start.4 = (bf16[128,2048]{1,0:T(8,128)(2,1)}, bf16[128,2048]{1,0:T(8,128)(2,1)S(1)}, u32[]{:S(2)}, u32[]{:S(2)}) collective-permute-start(bf16[128,2048]{1,0:T(8,128)(2,1)} %get-tuple-element.154.refs_5_.refs_3_.refs_4_), channel_id=1, source_target_pairs={{0,8},{8,0},{16,24},{24,16},{1,9},{9,1},{17,25},{25,17},{2,10},{10... | collective-permute-start | bytes 1572872 | tf_op jit(solution)/shard_map/ppermute | solution.py:717
  18.2 0.0 collective-permute-done.1
  18.2 1.0 add_convert_fusion.3
  19.2 1.6 %collective-permute-start.2 = (bf16[128,544]{1,0:T(8,128)(2,1)S(1)}, bf16[128,544]{1,0:T(8,128)(2,1)S(1)}, u32[]{:S(2)}, u32[]{:S(2)}) collective-permute-start(bf16[128,544]{1,0:T(8,128)(2,1)S(1)} %add_convert_fusion.3), channel_id=1, source_target_pairs={{0,2},{1,3},{2,0},{3,1},{4,6},{5,7},{6,4},{7,5},{8,10},{9,11},{10,... | collective-permute-start | bytes 417800 | tf_op jit(solution)/shard_map/ppermute | solution.py:717
  20.8 4.5 %collective-permute-done.2 = bf16[128,544]{1,0:T(8,128)(2,1)S(1)} collective-permute-done((bf16[128,544]{1,0:T(8,128)(2,1)S(1)}, bf16[128,544]{1,0:T(8,128)(2,1)S(1)}, u32[]{:S(2)}, u32[]{:S(2)}) %collective-permute-start.2) | collective-permute-done | bytes 139296 | tf_op jit(solution)/shard_map/ppermute | solution.py:717
  25.3 0.0 copy-start.2
  25.3 1.6 %collective-permute-start.3 = (bf16[128,544]{1,0:T(8,128)(2,1)S(1)}, bf16[128,544]{1,0:T(8,128)(2,1)S(1)}, u32[]{:S(2)}, u32[]{:S(2)}) collective-permute-start(bf16[128,544]{1,0:T(8,128)(2,1)S(1)} %add_convert_fusion.2.refs_0_), channel_id=1, source_target_pairs={{0,4},{1,5},{2,6},{3,7},{4,0},{5,1},{6,2},{7,3},{8,12},{9,13},{10,... | collective-permute-start | bytes 417800 | tf_op jit(solution)/shard_map/ppermute | solution.py:717
  26.9 0.7 copy.29
  27.6 3.1 %collective-permute-done.3.refs_1_ = bf16[128,544]{1,0:T(8,128)(2,1)S(1)} collective-permute-done((bf16[128,544]{1,0:T(8,128)(2,1)S(1)}, bf16[128,544]{1,0:T(8,128)(2,1)S(1)}, u32[]{:S(2)}, u32[]{:S(2)}) %collective-permute-start.3) | collective-permute-done | bytes 139296 | tf_op jit(solution)/shard_map/ppermute | solution.py:717
  30.7 0.7 copy-done.13
  31.4 12.1 %local_ends.1 = (f32[2,1024,128]{2,1,0:T(8,128)}, f32[32,128]{1,0:T(8,128)}, bf16[128,512]{1,0:T(8,128)(2,1)}, bf16[2,18,8,128]{3,2,1,0:T(8,128)(2,1)}, bf16[2,1...) custom-call(bf16[128,544]{1,0:T(8,128)(2,1)} %copy-done.2, bf16[128,544]{1,0:T(8,128)(2,1)} %copy-done.13, ...), custom_call_target="tpu_custom_call" | custom-call | tf_op jit(solution)/shard_map/local_ends/pallas_call | solution.py:226
  43.4 0.0 collective-permute-done.5.refs_6_
  43.5 0.0 collective-permute-done.4.refs_5_
  43.5 0.5 collective-permute-start.6
  44.0 1.4 %collective-permute-start.7 = (bf16[2,18,8,128]{3,2,1,0:T(8,128)(2,1)}, bf16[2,18,8,128]{3,2,1,0:T(8,128)(2,1)S(1)}, u32[]{:S(2)}, u32[]{:S(2)}) collective-permute-start(bf16[2,18,8,128]{3,2,1,0:T(8,128)(2,1)} %get-tuple-element.97), channel_id=1, source_target_pairs={{0,16},{8,24},{16,0},{24,8},{1,17},{9,25},{17,1},{25,9},{2,18},{10... | collective-permute-start | bytes 221192 | tf_op jit(solution)/shard_map/ppermute | solution.py:717
  45.4 2.5 %collective-permute-start.8 = (bf16[2,18,8,128]{3,2,1,0:T(8,128)(2,1)}, bf16[2,18,8,128]{3,2,1,0:T(8,128)(2,1)S(1)}, u32[]{:S(2)}, u32[]{:S(2)}) collective-permute-start(bf16[2,18,8,128]{3,2,1,0:T(8,128)(2,1)} %get-tuple-element.98), channel_id=1, source_target_pairs={{0,24},{8,16},{16,8},{24,0},{1,25},{9,17},{17,9},{25,1},{2,26},{10... | collective-permute-start | bytes 221192 | tf_op jit(solution)/shard_map/ppermute | solution.py:717
  47.9 0.2 collective-permute-done.6.refs_8_
  48.1 3.7 %collective-permute-done.7.refs_9_ = bf16[2,18,8,128]{3,2,1,0:T(8,128)(2,1)S(1)} collective-permute-done((bf16[2,18,8,128]{3,2,1,0:T(8,128)(2,1)}, bf16[2,18,8,128]{3,2,1,0:T(8,128)(2,1)S(1)}, u32[]{:S(2)}, u32[]{:S(2)}) %collective-permute-start.7) | collective-permute-done | bytes 73760 | tf_op jit(solution)/shard_map/ppermute | solution.py:717
  51.8 0.0 collective-permute-done.8.refs_10_
  51.8 1.3 collective-permute-start.9
  53.2 14.6 %scan_gradients.2 = (bf16[144,1024]{1,0:T(8,128)(2,1)}, bf16[128,2048]{1,0:T(8,128)(2,1)}, bf16[128,2048]{1,0:T(8,128)(2,1)}, f32[8,2048]{1,0:T(8,128)}, f32[640,128]{1,0:T(8,128)}) custom-call(f32[32,128]{1,0:T(8,128)} %get-tuple-element.91.refs_0_, f32[2,1024,128]{2,1,0:T(8,128)} %get-tuple-element.92.refs_1_, f32[2,16,8,128]{3,2,1,0:T(8,128)} %bitcast.14, ...), custom_call_target="tpu_custom_call" | custom-call | tf_op jit(solution)/shard_map/scan_gradients/pallas_call | solution.py:477
  67.8 1.8 %collective-permute-start.10 = (bf16[144,1024]{1,0:T(8,128)(2,1)}, bf16[144,1024]{1,0:T(8,128)(2,1)S(1)}, u32[]{:S(2)}, u32[]{:S(2)}) collective-permute-start(bf16[144,1024]{1,0:T(8,128)(2,1)} %get-tuple-element.132.refs_2_), channel_id=1, source_target_pairs={{0,16},{8,24},{16,0},{24,8},{1,17},{9,25},{17,1},{25,9},{2,18},{10... | collective-permute-start | bytes 884744 | tf_op jit(solution)/shard_map/ppermute | solution.py:717
  69.6 0.1 copy.26
  69.8 1.2 collective-permute-start.11
  71.0 14.8 %scan_gradients.3 = (bf16[144,1024]{1,0:T(8,128)(2,1)}, bf16[128,2048]{1,0:T(8,128)(2,1)}, bf16[128,2048]{1,0:T(8,128)(2,1)}, f32[8,2048]{1,0:T(8,128)}, bf16[640,128]{1,0:T(8,128)(2,1)}) custom-call(f32[32,128]{1,0:T(8,128)} %get-tuple-element.91.refs_0_, ...), custom_call_target="tpu_custom_call", output_to_operand_aliasing={{1}: (12, {}), {2}: (13, {}), {3}: (14, {})} | custom-call | tf_op jit(solution)/shard_map/scan_gradients/pallas_call | solution.py:477
  85.8 1.1 collective-permute-done.11.refs_1_
  86.9 0.1 collective-permute-start.12
  87.0 1.6 %collective-permute-done.12 = bf16[640,128]{1,0:T(8,128)(2,1)S(1)} collective-permute-done((bf16[640,128]{1,0:T(8,128)(2,1)}, bf16[640,128]{1,0:T(8,128)(2,1)S(1)}, u32[]{:S(2)}, u32[]{:S(2)}) %collective-permute-start.12) | collective-permute-done | bytes 163872 | tf_op jit(solution)/shard_map/ppermute | solution.py:717
  88.6 1.0 add_convert_fusion.1
  89.5 1.6 %collective-permute-start.13 = (bf16[640,128]{1,0:T(8,128)(2,1)S(1)}, bf16[640,128]{1,0:T(8,128)(2,1)S(1)}, u32[]{:S(2)}, u32[]{:S(2)}) collective-permute-start(bf16[640,128]{1,0:T(8,128)(2,1)S(1)} %add_convert_fusion.1), channel_id=1, source_target_pairs={{0,2},{1,3},{2,0},{3,1},{4,6},{5,7},{6,4},{7,5},{8,10},{9,11},{10,... | collective-permute-start | bytes 491528 | tf_op jit(solution)/shard_map/ppermute | solution.py:717
  91.1 0.7 collective-permute-start.15
  91.8 4.0 %collective-permute-done.13 = bf16[640,128]{1,0:T(8,128)(2,1)S(1)} collective-permute-done((bf16[640,128]{1,0:T(8,128)(2,1)S(1)}, bf16[640,128]{1,0:T(8,128)(2,1)S(1)}, u32[]{:S(2)}, u32[]{:S(2)}) %collective-permute-start.13) | collective-permute-done | bytes 163872 | tf_op jit(solution)/shard_map/ppermute | solution.py:717
  95.9 1.6 %collective-permute-start.14 = (bf16[640,128]{1,0:T(8,128)(2,1)S(1)}, bf16[640,128]{1,0:T(8,128)(2,1)S(1)}, u32[]{:S(2)}, u32[]{:S(2)}) collective-permute-start(bf16[640,128]{1,0:T(8,128)(2,1)S(1)} %add_convert_fusion.back_a), channel_id=1, source_target_pairs={{0,4},{1,5},{2,6},{3,7},{4,0},{5,1},{6,2},{7,3},{8,12},{9,13},{10,... | collective-permute-start | bytes 491528 | tf_op jit(solution)/shard_map/ppermute | solution.py:717
  97.5 3.9 %collective-permute-done.14.back_b = bf16[640,128]{1,0:T(8,128)(2,1)S(1)} collective-permute-done((bf16[640,128]{1,0:T(8,128)(2,1)S(1)}, bf16[640,128]{1,0:T(8,128)(2,1)S(1)}, u32[]{:S(2)}, u32[]{:S(2)}) %collective-permute-start.14) | collective-permute-done | bytes 163872 | tf_op jit(solution)/shard_map/ppermute | solution.py:717
  101.4 0.7 copy-done.1
  102.1 1.7 %cut_rows.1 = (bf16[160,128]{1,0:T(8,128)(2,1)}, bf16[160,128]{1,0:T(8,128)(2,1)}, bf16[160,128]{1,0:T(8,128)(2,1)}, bf16[160,128]{1,0:T(8,128)(2,1)}) custom-call(bf16[640,128]{1,0:T(8,128)(2,1)} %copy-done, bf16[640,128]{1,0:T(8,128)(2,1)} %copy-done.1), custom_call_target="tpu_custom_call" | custom-call | tf_op jit(solution)/shard_map/cut_rows/pallas_call | solution.py:592
  103.8 3.1 %collective-permute-done.15.refs_5_ = bf16[144,1024]{1,0:T(8,128)(2,1)S(1)} collective-permute-done((bf16[144,1024]{1,0:T(8,128)(2,1)}, bf16[144,1024]{1,0:T(8,128)(2,1)S(1)}, u32[]{:S(2)}, u32[]{:S(2)}) %collective-permute-start.15) | collective-permute-done | bytes 294944 | tf_op jit(solution)/shard_map/ppermute | solution.py:717
  106.9 0.7 copy-done.9
  107.6 3.1 %step_products.1 = (f32[144,2048]{1,0:T(8,128)}, bf16[144,2048]{1,0:T(8,128)(2,1)}) custom-call(bf16[512,128]{1,0:T(8,128)(2,1)} %bitcast.18, bf16[512,128]{1,0:T(8,128)(2,1)} %copy-done.16, bf16[144,1024]{1,0:T(8,128)(2,1)} %get-tuple-element.132.refs_2_, bf16[144,1024]{1,0:T(8,128)(2,1)} %copy-done.8, bf16[144,1024]{1,0:T(8,128)(2,1)} %get-tuple-element.134.refs_4_, ...), custom_call_target="tpu_custom_call" | custom-call | tf_op jit(solution)/shard_map/step_products/pallas_call | solution.py:627
  110.8 0.0 collective-permute-start.22
  110.8 2.0 %collective-permute-start.16 = (bf16[160,128]{1,0:T(8,128)(2,1)}, bf16[160,128]{1,0:T(8,128)(2,1)S(1)}, u32[]{:S(2)}, u32[]{:S(2)}) collective-permute-start(bf16[160,128]{1,0:T(8,128)(2,1)} %get-tuple-element.144), channel_id=1, source_target_pairs={{0,8},{8,0},{16,24},{24,16},{1,9},{9,1},{17,25},{25,17},{2,10},{10... | collective-permute-start | bytes 122888 | tf_op jit(solution)/shard_map/ppermute | solution.py:717
  112.8 0.7 collective-permute-start.17
  113.4 1.8 %collective-permute-start.18 = (bf16[160,128]{1,0:T(8,128)(2,1)}, bf16[160,128]{1,0:T(8,128)(2,1)S(1)}, u32[]{:S(2)}, u32[]{:S(2)}) collective-permute-start(bf16[160,128]{1,0:T(8,128)(2,1)} %get-tuple-element.146), channel_id=1, source_target_pairs={{0,24},{8,16},{16,8},{24,0},{1,25},{9,17},{17,9},{25,1},{2,26},{10... | collective-permute-start | bytes 122888 | tf_op jit(solution)/shard_map/ppermute | solution.py:717
  115.2 6.7 %conv_gradients.1 = (bf16[128,2048]{1,0:T(8,128)(2,1)}, f32[16,2048]{1,0:T(8,128)}, bf16[16,2048]{1,0:T(8,128)(2,1)}) custom-call(bf16[640,128]{1,0:T(8,128)(2,1)} %copy-done, bf16[640,128]{1,0:T(8,128)(2,1)} %copy-done.1, bf16[544,2048]{1,0:T(8,128)(2,1)} %proj_ref.3, bf16[128,2048]{1,0:T(8,128)(2,1)} %get-tuple-element.138.scan_ref, ...), custom_call_target="tpu_custom_call" | custom-call | tf_op jit(solution)/shard_map/conv_gradients/pallas_call | solution.py:559
  121.9 6.3 %collective-permute-done.16.refs_1_ = bf16[160,128]{1,0:T(8,128)(2,1)S(1)} collective-permute-done((bf16[160,128]{1,0:T(8,128)(2,1)}, bf16[160,128]{1,0:T(8,128)(2,1)S(1)}, u32[]{:S(2)}, u32[]{:S(2)}) %collective-permute-start.16) | collective-permute-done | bytes 40992 | tf_op jit(solution)/shard_map/ppermute | solution.py:717
  128.3 0.0 collective-permute-done.17.refs_2_
  128.3 0.9 collective-permute-done.18.refs_3_
  129.2 1.8 %collective-permute-start.21 = (bf16[16,2048]{1,0:T(8,128)(2,1)}, bf16[16,2048]{1,0:T(8,128)(2,1)S(1)}, u32[]{:S(2)}, u32[]{:S(2)}) collective-permute-start(bf16[16,2048]{1,0:T(8,128)(2,1)} %get-tuple-element.147.refs_3_), channel_id=1, source_target_pairs={{0,24},{8,0},{16,8},{24,16},{1,25},{9,1},{17,9},{25,17},{2,26},{10... | collective-permute-start | bytes 196616 | tf_op jit(solution)/shard_map/ppermute | solution.py:52
  130.9 0.0 collective-permute-start.20
  130.9 0.7 collective-permute-start.19
  131.7 2.1 %collective-permute-done.21.refs_6_ = bf16[16,2048]{1,0:T(8,128)(2,1)S(1)} collective-permute-done((bf16[16,2048]{1,0:T(8,128)(2,1)}, bf16[16,2048]{1,0:T(8,128)(2,1)S(1)}, u32[]{:S(2)}, u32[]{:S(2)}) %collective-permute-start.21) | collective-permute-done | bytes 65568 | tf_op jit(solution)/shard_map/ppermute | solution.py:52
  133.7 3.8 %collective-permute-done.20.refs_5_ = bf16[16,2048]{1,0:T(8,128)(2,1)S(1)} collective-permute-done((bf16[16,2048]{1,0:T(8,128)(2,1)}, bf16[16,2048]{1,0:T(8,128)(2,1)S(1)}, u32[]{:S(2)}, u32[]{:S(2)}) %collective-permute-start.20) | collective-permute-done | bytes 65568 | tf_op jit(solution)/shard_map/ppermute | solution.py:52
  137.6 0.6 copy-done.19
  138.2 0.0 copy-done.20
  138.2 1.7 %last_rows.1 = (bf16[128,2048]{1,0:T(8,128)(2,1)}, f32[4,2048]{1,0:T(4,128)}, f32[1,2048]{1,0:T(1,128)}, f32[1,2048]{1,0:T(1,128)}, f32[1,2048]{1,0:T(1,128)}) custom-call(bf16[128,2048]{1,0:T(8,128)(2,1)} %get-tuple-element.140.refs_0_, f32[16,2048]{1,0:T(8,128)} %get-tuple-element.141.refs_1_, f32[4,2048]{1,0:T(4,128)} %refs_2_.3, ...), custom_call_target="tpu_custom_call", output_to_operand_aliasing={{0}: (0, {})} | custom-call | tf_op jit(solution)/shard_map/last_rows/pallas_call | solution.py:694
  140.0 0.8 copy-done.3
  140.7 3.7 %row_gradients.1 = (f32[128,2048]{1,0:T(8,128)}, f32[8,2048]{1,0:T(8,128)}, f32[128,2048]{1,0:T(8,128)}, f32[16,2048]{1,0:T(8,128)}) custom-call(bf16[160,128]{1,0:T(8,128)(2,1)} %get-tuple-element.150.refs_0_, bf16[160,128]{1,0:T(8,128)(2,1)} %copy-done.21, bf16[160,128]{1,0:T(8,128)(2,1)} %copy-done.22, bf16[160,128]{1,0:T(8,128)(2,1)} %copy-done.23, ...), custom_call_target="tpu_custom_call" | custom-call | tf_op jit(solution)/shard_map/row_gradients/pallas_call | solution.py:654
  (47 shorter events, 0.2 us)
Async XLA Ops:
  0.6 26.3 %copy-start.14 = (f32[16,2048]{1,0:T(8,128)S(1)}, f32[16,2048]{1,0:T(8,128)}, u32[]{:S(2)}) copy-start(f32[16,2048]{1,0:T(8,128)} %param.18) | copy-start | bytes 393220
  1.5 6.4 %collective-permute-start = (bf16[3,2048]{1,0:T(4,128)(2,1)S(1)}, bf16[3,2048]{1,0:T(4,128)(2,1)S(1)}, u32[]{:S(2)}, u32[]{:S(2)}) collective-permute-start(bf16[3,2048]{1,0:T(4,128)(2,1)S(1)} %slice.3), channel_id=1, source_target_pairs={{0,8},{8,16},{16,24},{1,9},{9,17},{17,25},{2,10},{10,18},{18,26},{... | collective-permute-start | bytes 36872 | tf_op jit(solution)/shard_map/ppermute | solution.py:58
  7.8 0.6 copy-start.17
  13.3 5.0 %collective-permute-start.1 = (bf16[128,544]{1,0:T(8,128)(2,1)}, bf16[128,544]{1,0:T(8,128)(2,1)S(1)}, u32[]{:S(2)}, u32[]{:S(2)}) collective-permute-start(bf16[128,544]{1,0:T(8,128)(2,1)} %get-tuple-element.89), channel_id=1, source_target_pairs={{0,1},{1,0},{2,3},{3,2},{4,5},{5,4},{6,7},{7,6},{8,9},{9,8},{10,11... | collective-permute-start | bytes 417800 | tf_op jit(solution)/shard_map/ppermute | solution.py:717
  13.3 30.2 %collective-permute-start.5 = (bf16[128,2048]{1,0:T(8,128)(2,1)}, bf16[128,2048]{1,0:T(8,128)(2,1)S(1)}, u32[]{:S(2)}, u32[]{:S(2)}) collective-permute-start(bf16[128,2048]{1,0:T(8,128)(2,1)} %get-tuple-element.154.refs_5_.refs_3_.refs_4_), channel_id=1, source_target_pairs={{0,16},{8,24},{16,0},{24,8},{1,17},{9,25},{17,1},{25,9},{2,18},{10... | collective-permute-start | bytes 1572872 | tf_op jit(solution)/shard_map/ppermute | solution.py:717
  16.6 26.8 %collective-permute-start.4 = (bf16[128,2048]{1,0:T(8,128)(2,1)}, bf16[128,2048]{1,0:T(8,128)(2,1)S(1)}, u32[]{:S(2)}, u32[]{:S(2)}) collective-permute-start(bf16[128,2048]{1,0:T(8,128)(2,1)} %get-tuple-element.154.refs_5_.refs_3_.refs_4_), channel_id=1, source_target_pairs={{0,8},{8,0},{16,24},{24,16},{1,9},{9,1},{17,25},{25,17},{2,10},{10... | collective-permute-start | bytes 1572872 | tf_op jit(solution)/shard_map/ppermute | solution.py:717
  19.2 6.0 %collective-permute-start.2 = (bf16[128,544]{1,0:T(8,128)(2,1)S(1)}, bf16[128,544]{1,0:T(8,128)(2,1)S(1)}, u32[]{:S(2)}, u32[]{:S(2)}) collective-permute-start(bf16[128,544]{1,0:T(8,128)(2,1)S(1)} %add_convert_fusion.3), channel_id=1, source_target_pairs={{0,2},{1,3},{2,0},{3,1},{4,6},{5,7},{6,4},{7,5},{8,10},{9,11},{10,... | collective-permute-start | bytes 417800 | tf_op jit(solution)/shard_map/ppermute | solution.py:717
  25.3 5.4 %copy-start.2 = (bf16[128,544]{1,0:T(8,128)(2,1)}, bf16[128,544]{1,0:T(8,128)(2,1)S(1)}, u32[]{:S(2)}) copy-start(bf16[128,544]{1,0:T(8,128)(2,1)S(1)} %add_convert_fusion.2.refs_0_) | copy-start | bytes 417796
  25.3 5.4 %collective-permute-start.3 = (bf16[128,544]{1,0:T(8,128)(2,1)S(1)}, bf16[128,544]{1,0:T(8,128)(2,1)S(1)}, u32[]{:S(2)}, u32[]{:S(2)}) collective-permute-start(bf16[128,544]{1,0:T(8,128)(2,1)S(1)} %add_convert_fusion.2.refs_0_), channel_id=1, source_target_pairs={{0,4},{1,5},{2,6},{3,7},{4,0},{5,1},{6,2},{7,3},{8,12},{9,13},{10,... | collective-permute-start | bytes 417800 | tf_op jit(solution)/shard_map/ppermute | solution.py:717
  30.7 0.7 copy-start.13
  43.4 24.3 %copy-start.4 = (bf16[128,2048]{1,0:T(8,128)(2,1)}, bf16[128,2048]{1,0:T(8,128)(2,1)S(1)}, u32[]{:S(2)}) copy-start(bf16[128,2048]{1,0:T(8,128)(2,1)S(1)} %collective-permute-done.5.refs_6_) | copy-start | bytes 1572868
  43.5 24.3 %copy-start.5 = (bf16[128,2048]{1,0:T(8,128)(2,1)}, bf16[128,2048]{1,0:T(8,128)(2,1)S(1)}, u32[]{:S(2)}) copy-start(bf16[128,2048]{1,0:T(8,128)(2,1)S(1)} %collective-permute-done.4.refs_5_) | copy-start | bytes 1572868
  43.5 4.6 %collective-permute-start.6 = (bf16[2,18,8,128]{3,2,1,0:T(8,128)(2,1)}, bf16[2,18,8,128]{3,2,1,0:T(8,128)(2,1)S(1)}, u32[]{:S(2)}, u32[]{:S(2)}) collective-permute-start(bf16[2,18,8,128]{3,2,1,0:T(8,128)(2,1)} %get-tuple-element.96), channel_id=1, source_target_pairs={{0,8},{8,0},{16,24},{24,16},{1,9},{9,1},{17,25},{25,17},{2,10},{10... | collective-permute-start | bytes 221192 | tf_op jit(solution)/shard_map/ppermute | solution.py:717
  44.0 7.8 %collective-permute-start.7 = (bf16[2,18,8,128]{3,2,1,0:T(8,128)(2,1)}, bf16[2,18,8,128]{3,2,1,0:T(8,128)(2,1)S(1)}, u32[]{:S(2)}, u32[]{:S(2)}) collective-permute-start(bf16[2,18,8,128]{3,2,1,0:T(8,128)(2,1)} %get-tuple-element.97), channel_id=1, source_target_pairs={{0,16},{8,24},{16,0},{24,8},{1,17},{9,25},{17,1},{25,9},{2,18},{10... | collective-permute-start | bytes 221192 | tf_op jit(solution)/shard_map/ppermute | solution.py:717
  45.4 6.4 %collective-permute-start.8 = (bf16[2,18,8,128]{3,2,1,0:T(8,128)(2,1)}, bf16[2,18,8,128]{3,2,1,0:T(8,128)(2,1)S(1)}, u32[]{:S(2)}, u32[]{:S(2)}) collective-permute-start(bf16[2,18,8,128]{3,2,1,0:T(8,128)(2,1)} %get-tuple-element.98), channel_id=1, source_target_pairs={{0,24},{8,16},{16,8},{24,0},{1,25},{9,17},{17,9},{25,1},{2,26},{10... | collective-permute-start | bytes 221192 | tf_op jit(solution)/shard_map/ppermute | solution.py:717
  48.1 5.1 %copy-start.10 = (bf16[2,18,8,128]{3,2,1,0:T(8,128)(2,1)}, bf16[2,18,8,128]{3,2,1,0:T(8,128)(2,1)S(1)}, u32[]{:S(2)}) copy-start(bf16[2,18,8,128]{3,2,1,0:T(8,128)(2,1)S(1)} %collective-permute-done.6.refs_8_) | copy-start | bytes 221188
  51.8 1.4 copy-start.11
  51.8 1.4 copy-start.12
  51.8 19.2 %collective-permute-start.9 = (bf16[128,2048]{1,0:T(8,128)(2,1)S(1)}, bf16[128,2048]{1,0:T(8,128)(2,1)S(1)}, u32[]{:S(2)}, u32[]{:S(2)}) collective-permute-start(bf16[128,2048]{1,0:T(8,128)(2,1)S(1)} %collective-permute-done.5.refs_6_), channel_id=1, source_target_pairs={{0,8},{8,0},{16,24},{24,16},{1,9},{9,1},{17,25},{25,17},{2,10},{10... | collective-permute-start | bytes 1572872 | tf_op jit(solution)/shard_map/ppermute | solution.py:717
  53.2 16.5 %copy-start.15 = (bf16[128,512]{1,0:T(8,128)(2,1)S(1)}, bf16[128,512]{1,0:T(8,128)(2,1)}, u32[]{:S(2)}) copy-start(bf16[128,512]{1,0:T(8,128)(2,1)} %get-tuple-element.122) | copy-start | bytes 393220
  67.8 19.1 %collective-permute-start.10 = (bf16[144,1024]{1,0:T(8,128)(2,1)}, bf16[144,1024]{1,0:T(8,128)(2,1)S(1)}, u32[]{:S(2)}, u32[]{:S(2)}) collective-permute-start(bf16[144,1024]{1,0:T(8,128)(2,1)} %get-tuple-element.132.refs_2_), channel_id=1, source_target_pairs={{0,16},{8,24},{16,0},{24,8},{1,17},{9,25},{17,1},{25,9},{2,18},{10... | collective-permute-start | bytes 884744 | tf_op jit(solution)/shard_map/ppermute | solution.py:717
  69.8 16.0 %copy-start.7 = (bf16[128,512]{0,1:T(8,128)(2,1)}, bf16[128,512]{0,1:T(8,128)(2,1)S(1)}, u32[]{:S(2)}) copy-start(bf16[128,512]{0,1:T(8,128)(2,1)S(1)} %copy.26) | copy-start | bytes 393220
  69.8 17.1 %collective-permute-start.11 = (bf16[512,128]{1,0:T(8,128)(2,1)S(1)}, bf16[512,128]{1,0:T(8,128)(2,1)S(1)}, u32[]{:S(2)}, u32[]{:S(2)}) collective-permute-start(bf16[512,128]{1,0:T(8,128)(2,1)S(1)} %bitcast.17), channel_id=1, source_target_pairs={{0,16},{8,24},{16,0},{24,8},{1,17},{9,25},{17,1},{25,9},{2,18},{10... | collective-permute-start | bytes 393224 | tf_op jit(solution)/shard_map/ppermute | solution.py:717
  71.0 14.8 %copy-start.6 = (bf16[128,2048]{1,0:T(8,128)(2,1)}, bf16[128,2048]{1,0:T(8,128)(2,1)S(1)}, u32[]{:S(2)}) copy-start(bf16[128,2048]{1,0:T(8,128)(2,1)S(1)} %collective-permute-done.9.refs_7_) | copy-start | bytes 1572868
  86.9 20.0 %copy-start.16 = (bf16[512,128]{1,0:T(8,128)(2,1)}, bf16[512,128]{1,0:T(8,128)(2,1)S(1)}, u32[]{:S(2)}) copy-start(bf16[512,128]{1,0:T(8,128)(2,1)S(1)} %collective-permute-done.11.refs_1_) | copy-start | bytes 393220
  86.9 20.0 %copy-start.8 = (bf16[144,1024]{1,0:T(8,128)(2,1)}, bf16[144,1024]{1,0:T(8,128)(2,1)S(1)}, u32[]{:S(2)}) copy-start(bf16[144,1024]{1,0:T(8,128)(2,1)S(1)} %collective-permute-done.10.refs_3_) | copy-start | bytes 884740
  86.9 1.7 %collective-permute-start.12 = (bf16[640,128]{1,0:T(8,128)(2,1)}, bf16[640,128]{1,0:T(8,128)(2,1)S(1)}, u32[]{:S(2)}, u32[]{:S(2)}) collective-permute-start(bf16[640,128]{1,0:T(8,128)(2,1)} %get-tuple-element.123), channel_id=1, source_target_pairs={{0,1},{1,0},{2,3},{3,2},{4,5},{5,4},{6,7},{7,6},{8,9},{9,8},{10,11... | collective-permute-start | bytes 491528 | tf_op jit(solution)/shard_map/ppermute | solution.py:717
  89.5 6.3 %collective-permute-start.13 = (bf16[640,128]{1,0:T(8,128)(2,1)S(1)}, bf16[640,128]{1,0:T(8,128)(2,1)S(1)}, u32[]{:S(2)}, u32[]{:S(2)}) collective-permute-start(bf16[640,128]{1,0:T(8,128)(2,1)S(1)} %add_convert_fusion.1), channel_id=1, source_target_pairs={{0,2},{1,3},{2,0},{3,1},{4,6},{5,7},{6,4},{7,5},{8,10},{9,11},{10,... | collective-permute-start | bytes 491528 | tf_op jit(solution)/shard_map/ppermute | solution.py:717
  91.1 15.8 %collective-permute-start.15 = (bf16[144,1024]{1,0:T(8,128)(2,1)}, bf16[144,1024]{1,0:T(8,128)(2,1)S(1)}, u32[]{:S(2)}, u32[]{:S(2)}) collective-permute-start(bf16[144,1024]{1,0:T(8,128)(2,1)} %get-tuple-element.134.refs_4_), channel_id=1, source_target_pairs={{0,16},{8,24},{16,0},{24,8},{1,17},{9,25},{17,1},{25,9},{2,18},{10... | collective-permute-start | bytes 884744 | tf_op jit(solution)/shard_map/ppermute | solution.py:717
  95.9 5.5 %copy-start = (bf16[640,128]{1,0:T(8,128)(2,1)}, bf16[640,128]{1,0:T(8,128)(2,1)S(1)}, u32[]{:S(2)}) copy-start(bf16[640,128]{1,0:T(8,128)(2,1)S(1)} %add_convert_fusion.back_a) | copy-start | bytes 491524
  95.9 5.5 %collective-permute-start.14 = (bf16[640,128]{1,0:T(8,128)(2,1)S(1)}, bf16[640,128]{1,0:T(8,128)(2,1)S(1)}, u32[]{:S(2)}, u32[]{:S(2)}) collective-permute-start(bf16[640,128]{1,0:T(8,128)(2,1)S(1)} %add_convert_fusion.back_a), channel_id=1, source_target_pairs={{0,4},{1,5},{2,6},{3,7},{4,0},{5,1},{6,2},{7,3},{8,12},{9,13},{10,... | collective-permute-start | bytes 491528 | tf_op jit(solution)/shard_map/ppermute | solution.py:717
  101.4 0.7 copy-start.1
  106.9 0.7 copy-start.9
  110.8 29.2 %collective-permute-start.22 = (bf16[144,2048]{1,0:T(8,128)(2,1)}, bf16[144,2048]{1,0:T(8,128)(2,1)S(1)}, u32[]{:S(2)}, u32[]{:S(2)}) collective-permute-start(bf16[144,2048]{1,0:T(8,128)(2,1)} %get-tuple-element.159), channel_id=1, source_target_pairs={{0,8},{8,0},{16,24},{24,16},{1,9},{9,1},{17,25},{25,17},{2,10},{10... | collective-permute-start | bytes 1769480 | tf_op jit(solution)/shard_map/ppermute | solution.py:717
  110.8 17.5 %collective-permute-start.16 = (bf16[160,128]{1,0:T(8,128)(2,1)}, bf16[160,128]{1,0:T(8,128)(2,1)S(1)}, u32[]{:S(2)}, u32[]{:S(2)}) collective-permute-start(bf16[160,128]{1,0:T(8,128)(2,1)} %get-tuple-element.144), channel_id=1, source_target_pairs={{0,8},{8,0},{16,24},{24,16},{1,9},{9,1},{17,25},{25,17},{2,10},{10... | collective-permute-start | bytes 122888 | tf_op jit(solution)/shard_map/ppermute | solution.py:717
  112.8 15.5 %collective-permute-start.17 = (bf16[160,128]{1,0:T(8,128)(2,1)}, bf16[160,128]{1,0:T(8,128)(2,1)S(1)}, u32[]{:S(2)}, u32[]{:S(2)}) collective-permute-start(bf16[160,128]{1,0:T(8,128)(2,1)} %get-tuple-element.145), channel_id=1, source_target_pairs={{0,16},{8,24},{16,0},{24,8},{1,17},{9,25},{17,1},{25,9},{2,18},{10... | collective-permute-start | bytes 122888 | tf_op jit(solution)/shard_map/ppermute | solution.py:717
  113.4 15.7 %collective-permute-start.18 = (bf16[160,128]{1,0:T(8,128)(2,1)}, bf16[160,128]{1,0:T(8,128)(2,1)S(1)}, u32[]{:S(2)}, u32[]{:S(2)}) collective-permute-start(bf16[160,128]{1,0:T(8,128)(2,1)} %get-tuple-element.146), channel_id=1, source_target_pairs={{0,24},{8,16},{16,8},{24,0},{1,25},{9,17},{17,9},{25,1},{2,26},{10... | collective-permute-start | bytes 122888 | tf_op jit(solution)/shard_map/ppermute | solution.py:717
  128.3 11.7 %copy-start.21 = (bf16[160,128]{1,0:T(8,128)(2,1)}, bf16[160,128]{1,0:T(8,128)(2,1)S(1)}, u32[]{:S(2)}) copy-start(bf16[160,128]{1,0:T(8,128)(2,1)S(1)} %collective-permute-done.16.refs_1_) | copy-start | bytes 122884
  128.3 11.7 %copy-start.22 = (bf16[160,128]{1,0:T(8,128)(2,1)}, bf16[160,128]{1,0:T(8,128)(2,1)S(1)}, u32[]{:S(2)}) copy-start(bf16[160,128]{1,0:T(8,128)(2,1)S(1)} %collective-permute-done.17.refs_2_) | copy-start | bytes 122884
  129.2 10.8 %copy-start.23 = (bf16[160,128]{1,0:T(8,128)(2,1)}, bf16[160,128]{1,0:T(8,128)(2,1)S(1)}, u32[]{:S(2)}) copy-start(bf16[160,128]{1,0:T(8,128)(2,1)S(1)} %collective-permute-done.18.refs_3_) | copy-start | bytes 122884
  129.2 4.6 %collective-permute-start.21 = (bf16[16,2048]{1,0:T(8,128)(2,1)}, bf16[16,2048]{1,0:T(8,128)(2,1)S(1)}, u32[]{:S(2)}, u32[]{:S(2)}) collective-permute-start(bf16[16,2048]{1,0:T(8,128)(2,1)} %get-tuple-element.147.refs_3_), channel_id=1, source_target_pairs={{0,24},{8,0},{16,8},{24,16},{1,25},{9,1},{17,9},{25,17},{2,26},{10... | collective-permute-start | bytes 196616 | tf_op jit(solution)/shard_map/ppermute | solution.py:52
  130.9 6.6 %collective-permute-start.20 = (bf16[16,2048]{1,0:T(8,128)(2,1)}, bf16[16,2048]{1,0:T(8,128)(2,1)S(1)}, u32[]{:S(2)}, u32[]{:S(2)}) collective-permute-start(bf16[16,2048]{1,0:T(8,128)(2,1)} %get-tuple-element.147.refs_3_), channel_id=1, source_target_pairs={{0,16},{8,24},{16,0},{24,8},{1,17},{9,25},{17,1},{25,9},{2,18},{10... | collective-permute-start | bytes 196616 | tf_op jit(solution)/shard_map/ppermute | solution.py:52
  130.9 6.6 %collective-permute-start.19 = (bf16[16,2048]{1,0:T(8,128)(2,1)}, bf16[16,2048]{1,0:T(8,128)(2,1)S(1)}, u32[]{:S(2)}, u32[]{:S(2)}) collective-permute-start(bf16[16,2048]{1,0:T(8,128)(2,1)} %get-tuple-element.147.refs_3_), channel_id=1, source_target_pairs={{0,8},{8,16},{16,24},{24,0},{1,9},{9,17},{17,25},{25,1},{2,10},{10... | collective-permute-start | bytes 196616 | tf_op jit(solution)/shard_map/ppermute | solution.py:52
  133.7 3.8 %copy-start.18 = (bf16[16,2048]{1,0:T(8,128)(2,1)}, bf16[16,2048]{1,0:T(8,128)(2,1)S(1)}, u32[]{:S(2)}) copy-start(bf16[16,2048]{1,0:T(8,128)(2,1)S(1)} %collective-permute-done.21.refs_6_) | copy-start | bytes 196612
  137.6 0.6 copy-start.19
  137.6 0.6 copy-start.20
  139.9 0.8 copy-start.3

commit v9 on v8

--- a/solution.py
+++ b/solution.py
@@ -131,9 +131,9 @@
 def local_kernel(low_rank, states, places, *refs):
     parts, refs = refs[:2], refs[2:]
     (weight_ref, bias_ref, decay_ref, conv_ref, gate_ref, grad_ref) = refs[:6]
-    (dt_ref, coef_ref, low) = refs[6:9]
-    messages, refs = refs[9 : 8 + places], refs[8 + places :]
-    (coef_v, coef, dts, dxs, gs, fwd, bwd, sem) = refs
+    (dt_ref, dx_ref, g_ref, coef_ref, low) = refs[6:11]
+    messages, refs = refs[11 : 10 + places], refs[10 + places :]
+    (coef_v, coef, tiles, dts, dxs, gs, fwd, bwd, sem) = refs
     step = pl.program_id(0)
     chunks = dts.shape[0]
     rows = conv_ref.shape[0]
@@ -163,15 +163,25 @@
                 first = ((start // 8 + half) * groups + group) * 8
                 lanes = slice(group * 128, group * 128 + 128)
                 subs = slice(half * 8, half * 8 + 8)
-                dts[step, first : first + 8, :] = size[subs, lanes]
-                dt_ref[0, first : first + 8, :] = size[subs, lanes]
-                dxs[step, first : first + 8, :] = drive[subs, lanes]
-                gs[step, first : first + 8, :] = grad[subs, lanes]
+                tiles[0, first : first + 8, :] = size[subs, lanes]
+                tiles[1, first : first + 8, :] = drive[subs, lanes]
+                tiles[2, first : first + 8, :] = grad[subs, lanes]
+
+    def relay(index, _):
+        for sub in range(8):
+            token = index * 8 + sub
+            at = pl.ds(index * groups * 8 + sub, groups, stride=8)
+            for kind, (held, out) in enumerate(((dts, dt_ref), (dxs, dx_ref), (gs, g_ref))):
+                row = tiles[kind, at, :]
+                held[step, token] = row
+                out[0, token] = row
+        return 0
+
+    lax.fori_loop(0, rows // 8, relay, 0)
 
     @pl.when(step == chunks - 1)
     def _():
         batch = 4
-        span = groups * 8
         zero = jnp.zeros((groups, 128), F32)
         for lead in range(0, states, batch):
             pairs = [(n, v) for n in range(lead, lead + batch) for v in range(chunks)]
@@ -181,10 +191,9 @@
                 state, run, head, total = (list(part) for part in carry)
                 for sub in range(8):
                     token = index * 8 + sub
-                    at = pl.ds(index * span + sub, groups, stride=8)
-                    size = [dts[v, at, :] for v in range(chunks)]
-                    drive = [dxs[v, at, :] for v in range(chunks)]
-                    grad = [gs[v, at, :] for v in range(chunks)]
+                    size = [dts[v, token] for v in range(chunks)]
+                    drive = [dxs[v, token] for v in range(chunks)]
+                    grad = [gs[v, token] for v in range(chunks)]
                     if lead == 0:
                         total = [a + b for a, b in zip(total, size)]
                     for k, (n, v) in enumerate(pairs):
@@ -222,7 +231,8 @@
     chunks, _, groups, _ = decay.shape
     width = groups * 128
     message = (chunks, states + 2, groups, 128)
-    big = pltpu.VMEM((chunks, rows * groups, 128), F32)
+    dense = (chunks, rows, groups, 128)
+    big = pltpu.VMEM(dense, F32)
     return pl.pallas_call(
         functools.partial(local_kernel, low_rank, states, places),
         grid=(chunks,),
@@ -237,13 +247,13 @@
             columns(rows, width),
         ],
         out_specs=[
-            pl.BlockSpec((1, rows * groups, 128), lambda i: (i, 0, 0)),
+            *[pl.BlockSpec((1, rows, groups, 128), lambda i: (i, 0, 0, 0))] * 3,
             whole((2 * states, rows)),
             whole((rows, low_rank)),
         ]
         + [whole(message)] * (places - 1),
         out_shape=[
-            sds((chunks, rows * groups, 128), F32),
+            *[sds(dense, F32)] * 3,
             sds((2 * states, rows), F32),
             sds((rows, low_rank), BF),
         ]
@@ -251,6 +261,7 @@
         scratch_shapes=[
             pltpu.VMEM((rows, 128), F32),
             pltpu.SMEM((2 * states, rows), F32),
+            pltpu.VMEM((3, rows * groups, 128), F32),
             big,
             big,
             big,
@@ -263,39 +274,26 @@
     )(*parts, step_weight, step_bias, decay, conv_out, gate, grad)
 
 
-def fold_rows(products, base, groups, target, first, stride):
+def fold_rows(products, base, groups, target, first):
     total = products[pl.ds(base, 8, stride=groups), :]
     for row in range(1, groups):
         total = total + products[pl.ds(base + row, 8, stride=groups), :]
-    target[pl.ds(first, 8, stride=stride), :] = total
+    target[pl.ds(pl.multiple_of(first, 8), 8), :] = total
 
 
 def scan_kernel(places, states, opening, *refs):
-    (coef, dt_ref, decay_ref, conv_ref, gate_ref, grad_ref, weight_ref, skip_ref) = refs[:8]
-    messages, refs = refs[8 : 7 + places], refs[7 + places :]
+    (coef, dt_ref, dx_ref, g_ref, decay_ref, skips_ref) = refs[:6]
+    (conv_ref, gate_ref, grad_ref, weight_ref, skip_ref) = refs[6:11]
+    messages, refs = refs[11 : 10 + places], refs[10 + places :]
     if not opening:
         before_ref, refs = refs[0], refs[4:]
     (pre_ref, gate_out, scan_out, small_ref, part_ref) = refs[:5]
     refs = refs[5:]
-    (xs, dxs, gs, ys, dds, qs, decayed, coef_out, coef_in, rate, decay_acc, acc, ends, products, factors) = refs
+    (ys, dds, qs, decayed, coef_out, coef_in, rate, decay_acc, acc, ends, products, factors) = refs
     rows = conv_ref.shape[0]
     groups = decay_ref.shape[2]
     low_rank = weight_ref.shape[0]
     span = groups * 8
-
-    for start in range(0, rows, 16):
-        here = slice(start, start + 16)
-        conv = conv_ref[here, :].astype(F32)
-        gate = gate_ref[here, :].astype(F32)
-        grad = grad_ref[here, :].astype(F32) * gate * sigmoid(gate)
-        for half in range(2):
-            for group in range(groups):
-                first = ((start // 8 + half) * groups + group) * 8
-                lanes = slice(group * 128, group * 128 + 128)
-                subs = slice(half * 8, half * 8 + 8)
-                xs[first : first + 8, :] = conv[subs, lanes]
-                dxs[first : first + 8, :] = conv[subs, lanes] * dt_ref[0, first : first + 8, :]
-                gs[first : first + 8, :] = grad[subs, lanes]
 
     place = lax.axis_index("ctx")
     for n in range(states):
@@ -322,7 +320,7 @@
         for sub in range(8):
             token = index * 8 + sub
             at = pl.ds(index * span + sub, groups, stride=8)
-            size, drive, grad = dt_ref[0, at, :], dxs[at, :], gs[at, :]
+            size, drive, grad = dt_ref[0, token], dx_ref[0, token], g_ref[0, token]
             result = jnp.zeros((groups, 128), F32)
             for lead in range(0, states, 8):
                 base = (sub * states + lead) * groups
@@ -335,7 +333,7 @@
                     result = result + state[n] * coef[states + n, token]
                     row = base + (n - lead) * groups
                     products[row : row + groups, :] = state[n] * grad
-                fold_rows(products, base, groups, coef_out, lead * rows + token, rows)
+                fold_rows(products, base, groups, coef_out, token * states + lead)
             ys[at, :] = result
         return state
 
@@ -347,7 +345,7 @@
         for sub in range(7, -1, -1):
             token = index * 8 + sub
             at = pl.ds(index * span + sub, groups, stride=8)
-            size, drive, grad = dt_ref[0, at, :], dxs[at, :], gs[at, :]
+            size, drive, grad = dt_ref[0, token], dx_ref[0, token], g_ref[0, token]
             slope = jnp.zeros((groups, 128), F32)
             inner = jnp.zeros((groups, 128), F32)
             for lead in range(0, states, 8):
@@ -361,9 +359,11 @@
                     inner = inner + adjoint * coef[n, token]
                     row = base + (n - lead) * groups
                     products[row : row + groups, :] = adjoint * drive
-                fold_rows(products, base, groups, coef_in, lead * rows + token, rows)
-            dds[at, :] = slope
-            qs[at, :] = inner
+                fold_rows(products, base, groups, coef_in, token * states + lead)
+            tiny = 1.0 - 0.5 * size * (1.0 - size * (1.0 / 3.0) * (1.0 - 0.25 * size))
+            ratio = jnp.where(size < 0.03, tiny, (1.0 - jnp.exp(-size)) / jnp.maximum(size, 0.03))
+            dds[at, :] = (LN2 * slope + drive * inner) * ratio
+            qs[at, :] = size * inner + skips_ref[0] * grad
         return carry, gathered
 
     zeros = [jnp.zeros((groups, 128), F32)] * states
@@ -396,22 +396,17 @@
                 axis=0,
             )
 
-        size = natural(lambda first: dt_ref[0, first : first + 8, :])
-        inner = natural(lambda first: qs[first : first + 8, :])
-        slope = natural(lambda first: dds[first : first + 8, :])
+        d_pre = natural(lambda first: dds[first : first + 8, :])
         out = natural(lambda first: ys[first : first + 8, :])
         conv = conv_ref[here, :].astype(F32)
         gate = gate_ref[here, :].astype(F32)
         grad = grad_ref[here, :].astype(F32)
         sig = sigmoid(gate)
         scan_grad = grad * gate * sig
-        tiny = 1.0 - 0.5 * size * (1.0 - size * (1.0 / 3.0) * (1.0 - 0.25 * size))
-        ratio = jnp.where(size < 0.03, tiny, (1.0 - jnp.exp(-size)) / jnp.maximum(size, 0.03))
-        d_pre = (LN2 * slope + conv * inner * size) * ratio
         pre_ref[here, :] = d_pre.astype(BF)
         bias_sum = bias_sum + jnp.sum(d_pre, axis=0, keepdims=True)
         skip_sum = skip_sum + jnp.sum(scan_grad * conv, axis=0, keepdims=True)
-        scan_out[here, :] = (size * inner + skip * scan_grad).astype(BF)
+        scan_out[here, :] = natural(lambda first: qs[first : first + 8, :]).astype(BF)
         gate_out[here, :] = (
             grad * (out + skip * conv) * (sig * (1.0 + gate * (1.0 - sig)))
         ).astype(BF)
@@ -420,15 +415,13 @@
     )
 
     pre_bf = pre_ref[:rows, :]
-    ones = jnp.ones((8, 128), BF)
-    coefs = jnp.concatenate(
-        [
-            sums[:1, n * rows : n * rows + rows]
-            for sums in (dot(ones, source[...].astype(BF), NT) for source in (coef_in, coef_out))
-            for n in range(states)
-        ],
-        axis=0,
-    )
+    lanes = lax.broadcasted_iota(jnp.int32, (2 * states, 128), 0)
+    coefs = jnp.zeros((2 * states, rows), F32)
+    for n in range(states):
+        at = pl.ds(n, rows, stride=states)
+        for kind, source in enumerate((coef_in, coef_out)):
+            pick = jnp.where(lanes == kind * states + n, 1.0, 0.0).astype(BF)
+            coefs = coefs + dot(pick, source[at, :].astype(BF), NT)
     wide = dot(weight_ref[...], pre_bf, NT)
 
     ranks, coef_rows, block = low_rank // places, 2 * states // places, acc.shape[0] // places
@@ -448,7 +441,8 @@
 
 
 def scan_call(
-    places, chunk, coef, dt, decay, conv_out, gate, grad, step_weight, skip, messages, previous
+    places, chunk, coef, dense, decay, skips, conv_out, gate, grad, step_weight, skip, messages,
+    previous,
 ):
     rows, chans = conv_out.shape
     low_rank = step_weight.shape[0]
@@ -461,8 +455,11 @@
     first, last = chunk == 0, chunk == chunks - 1
     in_specs = [
         pl.BlockSpec(memory_space=pltpu.SMEM),
-        lead(rows * groups, 128),
+        lead(rows, groups, 128),
+        lead(rows, groups, 128),
+        lead(rows, groups, 128),
         lead(states, groups, 128),
+        lead(groups, 128),
         here(rows),
         here(rows),
         here(rows),
@@ -473,7 +470,7 @@
     aliases = {}
     if not first:
         in_specs += [whole((wide, rows))] + [pl.BlockSpec(memory_space=pl.ANY)] * 3
-        aliases = {8 + places: 1, 9 + places: 2, 10 + places: 3}
+        aliases = {11 + places: 1, 12 + places: 2, 13 + places: 3}
     return pl.pallas_call(
         functools.partial(scan_kernel, places, states, first),
         grid=(1,),
@@ -496,9 +493,6 @@
             tall,
             tall,
             tall,
-            tall,
-            tall,
-            tall,
             pltpu.VMEM((rows, states, groups, 128), F32),
             pltpu.VMEM((rows * states, 128), F32),
             pltpu.VMEM((rows * states, 128), F32),
@@ -512,7 +506,9 @@
         input_output_aliases=aliases,
         compiler_params=params(),
         name="scan_gradients",
-    )(coef, dt, decay, conv_out, gate, grad, step_weight, skip, *messages, *previous)
+    )(
+        coef, *dense, decay, skips, conv_out, gate, grad, step_weight, skip, *messages, *previous
+    )
 
 
 def conv_grad_kernel(places, low_rank, back_a, back_b, proj_ref, scan_ref, small_in, input_ref, rim_ref, weight_ref, bias_ref,
@@ -598,38 +594,34 @@
     )(*backs)
 
 
-def step_kernel(chunks, ranks, near, *refs):
-    lows, steps, (mine_ref, theirs_ref) = refs[:near], refs[near:-2], refs[-2:]
+def step_kernel(ranks, near, *refs):
+    lows, steps, (mine_ref, theirs_ref) = refs[:near], refs[near : 2 * near], refs[2 * near :]
     place = lax.axis_index("ctx")
     rows = lows[0].shape[1]
     pair = pl.ds(pl.multiple_of(lax.div(place, 2) * (2 * ranks), 16), 2 * ranks)
     odd = lax.rem(place, 2) == 1
-    for chunk in range(chunks):
-
-        @pl.when(pl.program_id(0) == chunk)
-        def _():
-            total = jnp.zeros((2 * ranks, mine_ref.shape[1]), F32)
-            decay = jnp.zeros((mine_ref.shape[0] - ranks, mine_ref.shape[1]), F32)
-            for low, step in zip(lows, steps[chunk * near : (chunk + 1) * near]):
-                total = total + dot(low[pair, :], step[:rows, :])
-                decay = decay + step[rows:, :].astype(F32)
-            mine_ref[:ranks, :] = jnp.where(odd, total[ranks:, :], total[:ranks, :])
-            theirs_ref[:ranks, :] = jnp.where(odd, total[:ranks, :], total[ranks:, :]).astype(BF)
-            mine_ref[ranks:, :] = decay
-            theirs_ref[ranks:, :] = decay.astype(BF)
+    total = jnp.zeros((2 * ranks, mine_ref.shape[1]), F32)
+    decay = jnp.zeros((mine_ref.shape[0] - ranks, mine_ref.shape[1]), F32)
+    for low, step in zip(lows, steps):
+        total = total + dot(low[pair, :], step[:rows, :])
+        decay = decay + step[rows:, :].astype(F32)
+    mine_ref[:ranks, :] = jnp.where(odd, total[ranks:, :], total[:ranks, :])
+    theirs_ref[:ranks, :] = jnp.where(odd, total[:ranks, :], total[ranks:, :]).astype(BF)
+    mine_ref[ranks:, :] = decay
+    theirs_ref[ranks:, :] = decay.astype(BF)
 
 
 def step_call(ranks, lows, steps):
     rows = lows[0].shape[1]
-    chunks = len(steps) // len(lows)
-    tall, width = steps[0].shape
+    tall, chans = steps[0].shape
+    width = min(512, chans)
     height = ranks + tall - rows
     return pl.pallas_call(
-        functools.partial(step_kernel, chunks, ranks, len(lows)),
-        grid=(chunks,),
-        in_specs=[whole(lows[0].shape)] * len(lows) + [whole((tall, width))] * len(steps),
+        functools.partial(step_kernel, ranks, len(lows)),
+        grid=(chans // width,),
+        in_specs=[whole(lows[0].shape)] * len(lows) + [columns(tall, width)] * len(steps),
         out_specs=[columns(height, width)] * 2,
-        out_shape=[sds((height, width * chunks), F32), sds((height, width * chunks), BF)],
+        out_shape=[sds((height, chans), F32), sds((height, chans), BF)],
         compiler_params=params(),
         name="step_products",
     )(*lows, *steps)
@@ -637,31 +629,36 @@
 
 def rows_kernel(ranks, places, *refs):
     cuts, blocks, refs = refs[:places], refs[places : 2 * places], refs[2 * places :]
-    mine_ref, theirs_ref, out_ref, coef_ref, step_ref, decay_ref = refs
+    products, (out_ref, coef_ref, step_ref, decay_ref) = refs[:-4], refs[-4:]
     total = jnp.zeros((cuts[0].shape[0], out_ref.shape[1]), F32)
     for cut, block in zip(cuts, blocks):
         total = total + dot(cut[...], block[...])
     out_ref[...] = total[:ranks, :]
     coef_ref[...] = total[ranks : ranks + coef_ref.shape[0], :]
-    step_ref[...] = mine_ref[:ranks, :] + theirs_ref[:ranks, :].astype(F32)
-    decay_ref[...] = mine_ref[ranks:, :] + theirs_ref[ranks:, :].astype(F32)
-
-
-def rows_call(ranks, coef_rows, cuts, blocks, mine, theirs):
+    for chunk in range(len(products) // 2):
+
+        @pl.when(pl.program_id(0) == chunk)
+        def _():
+            mine, theirs = products[2 * chunk : 2 * chunk + 2]
+            step_ref[...] = mine[:ranks, :] + theirs[:ranks, :].astype(F32)
+            decay_ref[...] = mine[ranks:, :] + theirs[ranks:, :].astype(F32)
+
+
+def rows_call(ranks, coef_rows, cuts, blocks, products):
     rows, chans = blocks[0].shape
-    width = min(1024, chans)
-    heights = (ranks, coef_rows, ranks, mine.shape[0] - ranks)
+    height, width = products[0].shape
+    heights = (ranks, coef_rows, ranks, height - ranks)
     return pl.pallas_call(
         functools.partial(rows_kernel, ranks, len(cuts)),
         grid=(chans // width,),
         in_specs=[whole(cuts[0].shape)] * len(cuts)
         + [columns(rows, width)] * len(blocks)
-        + [columns(mine.shape[0], width)] * 2,
+        + [whole((height, width))] * len(products),
         out_specs=[columns(height, width) for height in heights],
         out_shape=[sds((height, chans), F32) for height in heights],
         compiler_params=params(),
         name="row_gradients",
-    )(*cuts, *blocks, mine, theirs)
+    )(*cuts, *blocks, *products)
 
 
 def last_kernel(places, taps, *refs):
@@ -764,6 +761,7 @@
     places = lax.axis_size("ctx")
     groups = group_rows(chans)
     decay = decay_log.reshape(states, -1, groups, 128).transpose(1, 0, 2, 3)
+    skips = skip_gain.reshape(-1, groups, 128)
     conv_bias = conv_bias[None, :]
     step_bias = step_bias[None, :]
     skip_gain = skip_gain[None, :]
@@ -773,7 +771,7 @@
     conv_out, part = conv_call(conv_input, rim, conv_weight, conv_bias, proj_weight)
     blocks = spread(conv_out)
     parts = chan_sum(part)
-    dt, coef, low, *messages = local_call(
+    dt, dx, g, coef, low, *messages = local_call(
         parts, step_weight, step_bias, decay, conv_out, gate_input, out_grad, states, places
     )
     messages, blocks = tie((messages, blocks))
@@ -784,23 +782,29 @@
     previous, steps = [], []
     for chunk in range(chunks):
         message, grad_gate, scan_part, small, part = scan_call(
-            places, chunk, coef, dt, decay, conv_out, gate_input, out_grad, step_weight,
-            skip_gain, messages, previous,
+            places, chunk, coef, (dt, dx, g), decay, skips, conv_out, gate_input, out_grad,
+            step_weight, skip_gain, messages, previous,
         )
         previous = [part, grad_gate, scan_part, small]
         if chunk == 0:
             previous, blocks = tie((previous, blocks))
         else:
-            previous, steps, lows = tie((previous, steps, lows))
-        steps += gather_near(message)
+            previous, steps[-1], lows = tie((previous, steps[-1], lows))
+        steps.append(gather_near(message))
     part, grad_gate, scan_part, small = previous
+    ranks = low_rank // places
+    products = []
+    for step in steps[:-1]:
+        mine, theirs = step_call(ranks, lows, step)
+        products += [mine, swap(theirs, "ctx", 1)]
     backs = chan_sum(part)
+    backs, products = tie((backs, products))
     cuts = cut_call(places, backs)
     cuts, lows = tie((cuts, lows))
     cuts = [cuts[0]] + [swap(cut, "ctx", mask) for mask, cut in enumerate(cuts[1:], 1)]
-    mine, theirs = step_call(low_rank // places, lows, steps)
+    mine, theirs = step_call(ranks, lows, steps[-1])
     backs, theirs = tie((backs, theirs))
-    theirs = swap(theirs, "ctx", 1)
+    products += [mine, swap(theirs, "ctx", 1)]
     main, tail, sums = conv_grad_call(
         places, low_rank, backs, proj_weight, scan_part, small, conv_input, rim, conv_weight,
         conv_bias,
@@ -808,8 +812,9 @@
     sums, cuts = tie((sums, cuts))
     late = [sums] + [rotate(sums, "ctx", hop) for hop in range(1, places)]
     grad_proj, grad_coef, grad_step, decay_grad = rows_call(
-        low_rank // places, 2 * states // places, cuts, blocks, mine, theirs
+        ranks, 2 * states // places, cuts, blocks, products
     )
+    late, grad_proj = tie((late, grad_proj))
     grad_input, conv_w, conv_b, step_b, skip = last_call(main, tail, conv_weight, late)
     return (
         grad_input,

time: 145 us -> 137 us (0.945)
  waiting for transfers between devices: 39.7 us -> 26.2 us
  starting transfers between devices: 32.8 us -> 36.3 us
  Pallas kernels: 63.3 us -> 65.6 us
    ppermute x19 -> x20, waiting for transfers between devices: 32.4 us -> 24.7 us  [swap(): lax.ppermute(block, axis, [(i, i ^ mask) for i in range(lax.axis_size(axi...]
    ppermute x3, waiting for transfers between devices: 5.89 us -> 0.01 us  [rotate(): lax.ppermute(block, axis, [(i, (i + distance) % count) for i in range(cou...]
    ppermute x3, starting transfers between devices: 2.5 us -> 4.4 us  [rotate(): lax.ppermute(block, axis, [(i, (i + distance) % count) for i in range(cou...]
    pallas_call x1 -> x2, Pallas kernels: 3.14 us -> 4.96 us  [step_call(): pl.pallas_call(functools.partial(step_kernel, ranks, len(lows)), grid=(ch...]
    ppermute x19 -> x20, starting transfers between devices: 25.3 us -> 27 us  [swap(): lax.ppermute(block, axis, [(i, i ^ mask) for i in range(lax.axis_size(axi...]
    unnamed x49 -> x51, local copies, waits for them, and re-layouts: 4.16 us -> 4.11 us
  transfers between devices with their start and end apart: 23 -> 24, of which waited for: 14 -> 9; matrix products, arithmetic and copies ran while one was open for 1% -> 1% of each run, Pallas kernels for 36% -> 41%
where the time goes in v9:
time: 137 us
  Pallas kernels  65.6 us (48%)
  starting transfers between devices  36.3 us (26%)
  waiting for transfers between devices  26.2 us (19%)
  local copies, waits for them, and re-layouts  5.7 us (4%)
  other arithmetic  2.02 us (1%)
    pallas_call x2, Pallas kernels, scan_call(): pl.pallas_call(functools.partial(scan_kernel, places, states, first), gri...  29.1 us
    ppermute x20, starting transfers between devices, swap(): lax.ppermute(block, axis, [(i, i ^ mask) for i in range(lax.axis_size(axi...  27 us
    ppermute x20, waiting for transfers between devices, swap(): lax.ppermute(block, axis, [(i, i ^ mask) for i in range(lax.axis_size(axi...  24.7 us
    pallas_call x1, Pallas kernels, local_call(): pl.pallas_call(functools.partial(local_kernel, low_rank, states, places),...  12.5 us
    pallas_call x1, Pallas kernels, conv_grad_call(): pl.pallas_call(functools.partial(conv_grad_kernel, places, low_rank), gri...  6.75 us
    pallas_call x2, Pallas kernels, step_call(): pl.pallas_call(functools.partial(step_kernel, ranks, len(lows)), grid=(ch...  4.96 us
    ppermute x1, starting transfers between devices, shift(): return lax.ppermute(block, axis, route)  4.93 us
    pallas_call x1, Pallas kernels, conv_call(): pl.pallas_call(conv_kernel, grid=(chans // width,), in_specs=[columns(row...  4.83 us
  transfers between devices with their start and end apart: 24, of which 9 were waited for; matrix products, arithmetic and copies ran while one was open for 1% of the time, Pallas kernels for 41%

profile of v9, /device:TPU:0, one launch (start us, length us, event | category | flops | bytes accessed | tf_op | source)
XLA Modules:
  0.0 136.8 jit_solution(6945027956837917552)
XLA Ops:
  0.7 0.8 slice.3
  1.5 4.9 %collective-permute-start = (bf16[3,2048]{1,0:T(4,128)(2,1)S(1)}, bf16[3,2048]{1,0:T(4,128)(2,1)S(1)}, u32[]{:S(2)}, u32[]{:S(2)}) collective-permute-start(bf16[3,2048]{1,0:T(4,128)(2,1)S(1)} %slice.3), channel_id=1, source_target_pairs={{0,8},{8,16},{16,24},{1,9},{9,17},{17,25},{2,10},{10,18},{18,26},{... | collective-permute-start | bytes 36872 | tf_op jit(solution)/shard_map/ppermute | solution.py:58
  6.4 1.4 %collective-permute-done.rim_ref = bf16[3,2048]{1,0:T(4,128)(2,1)S(1)} collective-permute-done((bf16[3,2048]{1,0:T(4,128)(2,1)S(1)}, bf16[3,2048]{1,0:T(4,128)(2,1)S(1)}, u32[]{:S(2)}, u32[]{:S(2)}) %collective-permute-start) | collective-permute-done | bytes 12320 | tf_op jit(solution)/shard_map/ppermute | solution.py:58
  7.8 0.6 copy-done.18
  8.4 4.8 %conv_project.1 = (bf16[128,2048]{1,0:T(8,128)(2,1)}, bf16[128,544]{1,0:T(8,128)(2,1)}) custom-call(bf16[128,2048]{1,0:T(8,128)(2,1)} %input_ref.3, bf16[3,2048]{1,0:T(4,128)(2,1)} %copy-done.18, f32[4,2048]{1,0:T(4,128)} %refs_2_.3, f32[1,2048]{1,0:T(1,128)} %bitcast.26, bf16[544,2048]{1,0:T(8,128)(2,1)} %proj_ref.3), custom_call_target="tpu_custom_call" | custom-call | tf_op jit(solution)/shard_map/conv_project/pallas_call | solution.py:103
  13.3 2.4 %collective-permute-start.4 = (bf16[128,2048]{1,0:T(8,128)(2,1)}, bf16[128,2048]{1,0:T(8,128)(2,1)S(1)}, u32[]{:S(2)}, u32[]{:S(2)}) collective-permute-start(bf16[128,2048]{1,0:T(8,128)(2,1)} %get-tuple-element.171.refs_5_.refs_6_.refs_4_), channel_id=1, source_target_pairs={{0,8},{8,0},{16,24},{24,16},{1,9},{9,1},{17,25},{25,17},{2,10},{10... | collective-permute-start | bytes 1572872 | tf_op jit(solution)/shard_map/ppermute | solution.py:714
  15.6 2.6 %collective-permute-start.5 = (bf16[128,2048]{1,0:T(8,128)(2,1)}, bf16[128,2048]{1,0:T(8,128)(2,1)S(1)}, u32[]{:S(2)}, u32[]{:S(2)}) collective-permute-start(bf16[128,2048]{1,0:T(8,128)(2,1)} %get-tuple-element.171.refs_5_.refs_6_.refs_4_), channel_id=1, source_target_pairs={{0,16},{8,24},{16,0},{24,8},{1,17},{9,25},{17,1},{25,9},{2,18},{10... | collective-permute-start | bytes 1572872 | tf_op jit(solution)/shard_map/ppermute | solution.py:714
  18.2 0.0 collective-permute-done.1
  18.2 1.0 add_convert_fusion.3
  19.2 1.6 %collective-permute-start.2 = (bf16[128,544]{1,0:T(8,128)(2,1)S(1)}, bf16[128,544]{1,0:T(8,128)(2,1)S(1)}, u32[]{:S(2)}, u32[]{:S(2)}) collective-permute-start(bf16[128,544]{1,0:T(8,128)(2,1)S(1)} %add_convert_fusion.3), channel_id=1, source_target_pairs={{0,2},{1,3},{2,0},{3,1},{4,6},{5,7},{6,4},{7,5},{8,10},{9,11},{10,... | collective-permute-start | bytes 417800 | tf_op jit(solution)/shard_map/ppermute | solution.py:714
  20.7 4.5 %collective-permute-done.2 = bf16[128,544]{1,0:T(8,128)(2,1)S(1)} collective-permute-done((bf16[128,544]{1,0:T(8,128)(2,1)S(1)}, bf16[128,544]{1,0:T(8,128)(2,1)S(1)}, u32[]{:S(2)}, u32[]{:S(2)}) %collective-permute-start.2) | collective-permute-done | bytes 139296 | tf_op jit(solution)/shard_map/ppermute | solution.py:714
  25.3 0.0 copy-start.3
  25.3 1.6 %collective-permute-start.3 = (bf16[128,544]{1,0:T(8,128)(2,1)S(1)}, bf16[128,544]{1,0:T(8,128)(2,1)S(1)}, u32[]{:S(2)}, u32[]{:S(2)}) collective-permute-start(bf16[128,544]{1,0:T(8,128)(2,1)S(1)} %add_convert_fusion.2.refs_0_), channel_id=1, source_target_pairs={{0,4},{1,5},{2,6},{3,7},{4,0},{5,1},{6,2},{7,3},{8,12},{9,13},{10,... | collective-permute-start | bytes 417800 | tf_op jit(solution)/shard_map/ppermute | solution.py:714
  26.9 0.7 copy.29
  27.6 3.1 %collective-permute-done.3.refs_1_ = bf16[128,544]{1,0:T(8,128)(2,1)S(1)} collective-permute-done((bf16[128,544]{1,0:T(8,128)(2,1)S(1)}, bf16[128,544]{1,0:T(8,128)(2,1)S(1)}, u32[]{:S(2)}, u32[]{:S(2)}) %collective-permute-start.3) | collective-permute-done | bytes 139296 | tf_op jit(solution)/shard_map/ppermute | solution.py:714
  30.7 0.7 copy-done.15
  31.3 12.5 %local_ends.1 = (f32[2,128,8,128]{3,2,1,0:T(8,128)}, f32[2,128,8,128]{3,2,1,0:T(8,128)}, f32[2,128,8,128]{3,2,1,0:T(8,128)}, f32[32,128]{1,0:T(8,128)}, bf16[128...) custom-call(bf16[128,544]{1,0:T(8,128)(2,1)} %copy-done.3, ...), custom_call_target="tpu_custom_call" | custom-call | tf_op jit(solution)/shard_map/local_ends/pallas_call | solution.py:236
  43.9 0.0 collective-permute-done.5.refs_6_
  43.9 0.5 collective-permute-start.6
  44.5 1.4 %collective-permute-start.7 = (bf16[2,18,8,128]{3,2,1,0:T(8,128)(2,1)}, bf16[2,18,8,128]{3,2,1,0:T(8,128)(2,1)S(1)}, u32[]{:S(2)}, u32[]{:S(2)}) collective-permute-start(bf16[2,18,8,128]{3,2,1,0:T(8,128)(2,1)} %get-tuple-element.112), channel_id=1, source_target_pairs={{0,16},{8,24},{16,0},{24,8},{1,17},{9,25},{17,1},{25,9},{2,18},{10... | collective-permute-start | bytes 221192 | tf_op jit(solution)/shard_map/ppermute | solution.py:714
  45.9 2.5 %collective-permute-start.8 = (bf16[2,18,8,128]{3,2,1,0:T(8,128)(2,1)}, bf16[2,18,8,128]{3,2,1,0:T(8,128)(2,1)S(1)}, u32[]{:S(2)}, u32[]{:S(2)}) collective-permute-start(bf16[2,18,8,128]{3,2,1,0:T(8,128)(2,1)} %get-tuple-element.113), channel_id=1, source_target_pairs={{0,24},{8,16},{16,8},{24,0},{1,25},{9,17},{17,9},{25,1},{2,26},{10... | collective-permute-start | bytes 221192 | tf_op jit(solution)/shard_map/ppermute | solution.py:714
  48.4 0.4 collective-permute-done.6.refs_11_
  48.7 1.5 %collective-permute-done.7.refs_12_ = bf16[2,18,8,128]{3,2,1,0:T(8,128)(2,1)S(1)} collective-permute-done((bf16[2,18,8,128]{3,2,1,0:T(8,128)(2,1)}, bf16[2,18,8,128]{3,2,1,0:T(8,128)(2,1)S(1)}, u32[]{:S(2)}, u32[]{:S(2)}) %collective-permute-start.7) | collective-permute-done | bytes 73760 | tf_op jit(solution)/shard_map/ppermute | solution.py:714
  50.2 2.1 %collective-permute-done.8.refs_13_ = bf16[2,18,8,128]{3,2,1,0:T(8,128)(2,1)S(1)} collective-permute-done((bf16[2,18,8,128]{3,2,1,0:T(8,128)(2,1)}, bf16[2,18,8,128]{3,2,1,0:T(8,128)(2,1)S(1)}, u32[]{:S(2)}, u32[]{:S(2)}) %collective-permute-start.8) | collective-permute-done | bytes 73760 | tf_op jit(solution)/shard_map/ppermute | solution.py:714
  52.4 0.8 collective-permute-start.9
  53.2 14.5 %scan_gradients.2 = (bf16[144,1024]{1,0:T(8,128)(2,1)}, bf16[128,2048]{1,0:T(8,128)(2,1)}, bf16[128,2048]{1,0:T(8,128)(2,1)}, f32[8,2048]{1,0:T(8,128)}, f32[640,128]{1,0:T(8,128)}) custom-call(f32[32,128]{1,0:T(8,128)} %get-tuple-element.104.refs_0_, f32[2,128,8,128]{3,2,1,0:T(8,128)} %get-tuple-element.105.refs_1_, ...), custom_call_target="tpu_custom_call" | custom-call | tf_op jit(solution)/shard_map/scan_gradients/pallas_call | solution.py:474
  67.6 3.0 %collective-permute-start.10 = (bf16[144,1024]{1,0:T(8,128)(2,1)}, bf16[144,1024]{1,0:T(8,128)(2,1)S(1)}, u32[]{:S(2)}, u32[]{:S(2)}) collective-permute-start(bf16[144,1024]{1,0:T(8,128)(2,1)} %get-tuple-element.141.refs_2_), channel_id=1, source_target_pairs={{0,16},{8,24},{16,0},{24,8},{1,17},{9,25},{17,1},{25,9},{2,18},{10... | collective-permute-start | bytes 884744 | tf_op jit(solution)/shard_map/ppermute | solution.py:714
  70.7 0.1 copy.26
  70.8 0.1 collective-permute-start.11
  70.9 0.0 collective-permute-done.9.refs_7_
  70.9 14.6 %scan_gradients.3 = (bf16[144,1024]{1,0:T(8,128)(2,1)}, bf16[128,2048]{1,0:T(8,128)(2,1)}, bf16[128,2048]{1,0:T(8,128)(2,1)}, f32[8,2048]{1,0:T(8,128)}, bf16[640,128]{1,0:T(8,128)(2,1)}) custom-call(f32[32,128]{1,0:T(8,128)} %get-tuple-element.104.refs_0_, ...), custom_call_target="tpu_custom_call", output_to_operand_aliasing={{1}: (15, {}), {2}: (16, {}), {3}: (17, {})} | custom-call | tf_op jit(solution)/shard_map/scan_gradients/pallas_call | solution.py:474
  85.5 0.8 collective-permute-done.11.refs_1_
  86.4 0.0 collective-permute-done.10.refs_3_
  86.4 0.1 collective-permute-start.12
  86.4 1.6 %collective-permute-done.12 = bf16[640,128]{1,0:T(8,128)(2,1)S(1)} collective-permute-done((bf16[640,128]{1,0:T(8,128)(2,1)}, bf16[640,128]{1,0:T(8,128)(2,1)S(1)}, u32[]{:S(2)}, u32[]{:S(2)}) %collective-permute-start.12) | collective-permute-done | bytes 163872 | tf_op jit(solution)/shard_map/ppermute | solution.py:714
  88.0 1.0 add_convert_fusion.1
  89.0 1.6 %collective-permute-start.13 = (bf16[640,128]{1,0:T(8,128)(2,1)S(1)}, bf16[640,128]{1,0:T(8,128)(2,1)S(1)}, u32[]{:S(2)}, u32[]{:S(2)}) collective-permute-start(bf16[640,128]{1,0:T(8,128)(2,1)S(1)} %add_convert_fusion.1), channel_id=1, source_target_pairs={{0,2},{1,3},{2,0},{3,1},{4,6},{5,7},{6,4},{7,5},{8,10},{9,11},{10,... | collective-permute-start | bytes 491528 | tf_op jit(solution)/shard_map/ppermute | solution.py:714
  90.6 2.5 %step_products.2 = (f32[144,1024]{1,0:T(8,128)}, bf16[144,1024]{1,0:T(8,128)(2,1)}) custom-call(bf16[512,128]{1,0:T(8,128)(2,1)} %bitcast.18, bf16[512,128]{1,0:T(8,128)(2,1)} %copy-done.7, bf16[144,1024]{1,0:T(8,128)(2,1)} %get-tuple-element.141.refs_2_, bf16[144,1024]{1,0:T(8,128)(2,1)} %copy-done.8), custom_call_target="tpu_custom_call" | custom-call | tf_op jit(solution)/shard_map/step_products/pallas_call | solution.py:619
  93.1 0.4 collective-permute-start.15
  93.4 2.5 %collective-permute-start.16 = (bf16[144,1024]{1,0:T(8,128)(2,1)}, bf16[144,1024]{1,0:T(8,128)(2,1)S(1)}, u32[]{:S(2)}, u32[]{:S(2)}) collective-permute-start(bf16[144,1024]{1,0:T(8,128)(2,1)} %get-tuple-element.153.refs_2_), channel_id=1, source_target_pairs={{0,16},{8,24},{16,0},{24,8},{1,17},{9,25},{17,1},{25,9},{2,18},{10... | collective-permute-start | bytes 884744 | tf_op jit(solution)/shard_map/ppermute | solution.py:714
  96.0 0.0 copy-start
  96.0 1.6 %collective-permute-start.14 = (bf16[640,128]{1,0:T(8,128)(2,1)S(1)}, bf16[640,128]{1,0:T(8,128)(2,1)S(1)}, u32[]{:S(2)}, u32[]{:S(2)}) collective-permute-start(bf16[640,128]{1,0:T(8,128)(2,1)S(1)} %add_convert_fusion.back_a), channel_id=1, source_target_pairs={{0,4},{1,5},{2,6},{3,7},{4,0},{5,1},{6,2},{7,3},{8,12},{9,13},{10,... | collective-permute-start | bytes 491528 | tf_op jit(solution)/shard_map/ppermute | solution.py:714
  97.6 10.7 %collective-permute-done.15.refs_9_ = bf16[144,1024]{1,0:T(8,128)(2,1)S(1)} collective-permute-done((bf16[144,1024]{1,0:T(8,128)(2,1)}, bf16[144,1024]{1,0:T(8,128)(2,1)S(1)}, u32[]{:S(2)}, u32[]{:S(2)}) %collective-permute-start.15) | collective-permute-done | bytes 294944 | tf_op jit(solution)/shard_map/ppermute | solution.py:714
  108.4 0.0 collective-permute-done.14.back_b
  108.4 0.7 copy-done.2
  109.1 1.7 %cut_rows.1 = (bf16[160,128]{1,0:T(8,128)(2,1)}, bf16[160,128]{1,0:T(8,128)(2,1)}, bf16[160,128]{1,0:T(8,128)(2,1)}, bf16[160,128]{1,0:T(8,128)(2,1)}) custom-call(bf16[640,128]{1,0:T(8,128)(2,1)} %copy-done, bf16[640,128]{1,0:T(8,128)(2,1)} %copy-done.2), custom_call_target="tpu_custom_call" | custom-call | tf_op jit(solution)/shard_map/cut_rows/pallas_call | solution.py:588
  110.8 0.0 collective-permute-done.16.refs_3_
  110.8 0.7 copy-done.9
  111.5 2.5 %step_products.3 = (f32[144,1024]{1,0:T(8,128)}, bf16[144,1024]{1,0:T(8,128)(2,1)}) custom-call(bf16[512,128]{1,0:T(8,128)(2,1)} %bitcast.19, bf16[512,128]{1,0:T(8,128)(2,1)} %copy-done.7, bf16[144,1024]{1,0:T(8,128)(2,1)} %get-tuple-element.153.refs_2_, bf16[144,1024]{1,0:T(8,128)(2,1)} %copy-done.9), custom_call_target="tpu_custom_call" | custom-call | tf_op jit(solution)/shard_map/step_products/pallas_call | solution.py:619
  114.0 2.0 %collective-permute-start.17 = (bf16[160,128]{1,0:T(8,128)(2,1)}, bf16[160,128]{1,0:T(8,128)(2,1)S(1)}, u32[]{:S(2)}, u32[]{:S(2)}) collective-permute-start(bf16[160,128]{1,0:T(8,128)(2,1)} %get-tuple-element.163), channel_id=1, source_target_pairs={{0,8},{8,0},{16,24},{24,16},{1,9},{9,1},{17,25},{25,17},{2,10},{10... | collective-permute-start | bytes 122888 | tf_op jit(solution)/shard_map/ppermute | solution.py:714
  116.0 0.4 collective-permute-start.18
  116.4 2.0 %collective-permute-start.19 = (bf16[160,128]{1,0:T(8,128)(2,1)}, bf16[160,128]{1,0:T(8,128)(2,1)S(1)}, u32[]{:S(2)}, u32[]{:S(2)}) collective-permute-start(bf16[160,128]{1,0:T(8,128)(2,1)} %get-tuple-element.165), channel_id=1, source_target_pairs={{0,24},{8,16},{16,8},{24,0},{1,25},{9,17},{17,9},{25,1},{2,26},{10... | collective-permute-start | bytes 122888 | tf_op jit(solution)/shard_map/ppermute | solution.py:714
  118.4 6.7 %conv_gradients.1 = (bf16[128,2048]{1,0:T(8,128)(2,1)}, f32[16,2048]{1,0:T(8,128)}, bf16[16,2048]{1,0:T(8,128)(2,1)}) custom-call(bf16[640,128]{1,0:T(8,128)(2,1)} %copy-done, bf16[640,128]{1,0:T(8,128)(2,1)} %copy-done.2, bf16[544,2048]{1,0:T(8,128)(2,1)} %proj_ref.3, bf16[128,2048]{1,0:T(8,128)(2,1)} %get-tuple-element.157.scan_ref, ...), custom_call_target="tpu_custom_call" | custom-call | tf_op jit(solution)/shard_map/conv_gradients/pallas_call | solution.py:555
  125.2 0.0 collective-permute-done.17.refs_1_
  125.2 0.0 collective-permute-done.18.refs_2_
  125.2 1.1 collective-permute-start.20
  126.4 1.3 collective-permute-start.21
  127.7 2.0 %collective-permute-start.22 = (bf16[16,2048]{1,0:T(8,128)(2,1)}, bf16[16,2048]{1,0:T(8,128)(2,1)S(1)}, u32[]{:S(2)}, u32[]{:S(2)}) collective-permute-start(bf16[16,2048]{1,0:T(8,128)(2,1)} %get-tuple-element.180.refs_3_), channel_id=1, source_target_pairs={{0,24},{8,0},{16,8},{24,16},{1,25},{9,1},{17,9},{25,17},{2,26},{10... | collective-permute-start | bytes 196616 | tf_op jit(solution)/shard_map/ppermute | solution.py:52
  129.7 0.7 copy-done.11
  130.4 4.0 %row_gradients.1 = (f32[128,2048]{1,0:T(8,128)}, f32[8,2048]{1,0:T(8,128)}, f32[128,2048]{1,0:T(8,128)}, f32[16,2048]{1,0:T(8,128)}) custom-call(bf16[160,128]{1,0:T(8,128)(2,1)} %get-tuple-element.167.refs_0_, bf16[160,128]{1,0:T(8,128)(2,1)} %copy-done.22, bf16[160,128]{1,0:T(8,128)(2,1)} %copy-done.23, bf16[160,128]{1,0:T(8,128)(2,1)} %copy-done.24, ...), custom_call_target="tpu_custom_call" | custom-call | tf_op jit(solution)/shard_map/row_gradients/pallas_call | solution.py:651
  134.4 0.6 copy-done.19
  135.0 0.0 copy-done.20
  135.0 0.0 copy-done.21
  135.1 1.7 %last_rows.1 = (bf16[128,2048]{1,0:T(8,128)(2,1)}, f32[4,2048]{1,0:T(4,128)}, f32[1,2048]{1,0:T(1,128)}, f32[1,2048]{1,0:T(1,128)}, f32[1,2048]{1,0:T(1,128)}) custom-call(bf16[128,2048]{1,0:T(8,128)(2,1)} %get-tuple-element.159.refs_0_, f32[16,2048]{1,0:T(8,128)} %get-tuple-element.160.refs_1_, f32[4,2048]{1,0:T(4,128)} %refs_2_.3, ...), custom_call_target="tpu_custom_call", output_to_operand_aliasing={{0}: (0, {})} | custom-call | tf_op jit(solution)/shard_map/last_rows/pallas_call | solution.py:691
  (52 shorter events, 0.2 us)
Async XLA Ops:
  0.6 26.2 %copy-start.16 = (f32[16,2048]{1,0:T(8,128)S(1)}, f32[16,2048]{1,0:T(8,128)}, u32[]{:S(2)}) copy-start(f32[16,2048]{1,0:T(8,128)} %param.18) | copy-start | bytes 393220
  1.5 6.4 %collective-permute-start = (bf16[3,2048]{1,0:T(4,128)(2,1)S(1)}, bf16[3,2048]{1,0:T(4,128)(2,1)S(1)}, u32[]{:S(2)}, u32[]{:S(2)}) collective-permute-start(bf16[3,2048]{1,0:T(4,128)(2,1)S(1)} %slice.3), channel_id=1, source_target_pairs={{0,8},{8,16},{16,24},{1,9},{9,17},{17,25},{2,10},{10,18},{18,26},{... | collective-permute-start | bytes 36872 | tf_op jit(solution)/shard_map/ppermute | solution.py:58
  7.8 0.6 copy-start.18
  13.3 5.0 %collective-permute-start.1 = (bf16[128,544]{1,0:T(8,128)(2,1)}, bf16[128,544]{1,0:T(8,128)(2,1)S(1)}, u32[]{:S(2)}, u32[]{:S(2)}) collective-permute-start(bf16[128,544]{1,0:T(8,128)(2,1)} %get-tuple-element.102), channel_id=1, source_target_pairs={{0,1},{1,0},{2,3},{3,2},{4,5},{5,4},{6,7},{7,6},{8,9},{9,8},{10,11... | collective-permute-start | bytes 417800 | tf_op jit(solution)/shard_map/ppermute | solution.py:714
  13.3 30.6 %collective-permute-start.4 = (bf16[128,2048]{1,0:T(8,128)(2,1)}, bf16[128,2048]{1,0:T(8,128)(2,1)S(1)}, u32[]{:S(2)}, u32[]{:S(2)}) collective-permute-start(bf16[128,2048]{1,0:T(8,128)(2,1)} %get-tuple-element.171.refs_5_.refs_6_.refs_4_), channel_id=1, source_target_pairs={{0,8},{8,0},{16,24},{24,16},{1,9},{9,1},{17,25},{25,17},{2,10},{10... | collective-permute-start | bytes 1572872 | tf_op jit(solution)/shard_map/ppermute | solution.py:714
  15.6 28.3 %collective-permute-start.5 = (bf16[128,2048]{1,0:T(8,128)(2,1)}, bf16[128,2048]{1,0:T(8,128)(2,1)S(1)}, u32[]{:S(2)}, u32[]{:S(2)}) collective-permute-start(bf16[128,2048]{1,0:T(8,128)(2,1)} %get-tuple-element.171.refs_5_.refs_6_.refs_4_), channel_id=1, source_target_pairs={{0,16},{8,24},{16,0},{24,8},{1,17},{9,25},{17,1},{25,9},{2,18},{10... | collective-permute-start | bytes 1572872 | tf_op jit(solution)/shard_map/ppermute | solution.py:714
  19.2 6.0 %collective-permute-start.2 = (bf16[128,544]{1,0:T(8,128)(2,1)S(1)}, bf16[128,544]{1,0:T(8,128)(2,1)S(1)}, u32[]{:S(2)}, u32[]{:S(2)}) collective-permute-start(bf16[128,544]{1,0:T(8,128)(2,1)S(1)} %add_convert_fusion.3), channel_id=1, source_target_pairs={{0,2},{1,3},{2,0},{3,1},{4,6},{5,7},{6,4},{7,5},{8,10},{9,11},{10,... | collective-permute-start | bytes 417800 | tf_op jit(solution)/shard_map/ppermute | solution.py:714
  25.3 5.4 %copy-start.3 = (bf16[128,544]{1,0:T(8,128)(2,1)}, bf16[128,544]{1,0:T(8,128)(2,1)S(1)}, u32[]{:S(2)}) copy-start(bf16[128,544]{1,0:T(8,128)(2,1)S(1)} %add_convert_fusion.2.refs_0_) | copy-start | bytes 417796
  25.3 5.4 %collective-permute-start.3 = (bf16[128,544]{1,0:T(8,128)(2,1)S(1)}, bf16[128,544]{1,0:T(8,128)(2,1)S(1)}, u32[]{:S(2)}, u32[]{:S(2)}) collective-permute-start(bf16[128,544]{1,0:T(8,128)(2,1)S(1)} %add_convert_fusion.2.refs_0_), channel_id=1, source_target_pairs={{0,4},{1,5},{2,6},{3,7},{4,0},{5,1},{6,2},{7,3},{8,12},{9,13},{10,... | collective-permute-start | bytes 417800 | tf_op jit(solution)/shard_map/ppermute | solution.py:714
  30.7 0.7 copy-start.15
  43.9 23.7 %copy-start.4 = (bf16[128,2048]{1,0:T(8,128)(2,1)}, bf16[128,2048]{1,0:T(8,128)(2,1)S(1)}, u32[]{:S(2)}) copy-start(bf16[128,2048]{1,0:T(8,128)(2,1)S(1)} %collective-permute-done.4.refs_5_) | copy-start | bytes 1572868
  43.9 23.7 %copy-start.5 = (bf16[128,2048]{1,0:T(8,128)(2,1)}, bf16[128,2048]{1,0:T(8,128)(2,1)S(1)}, u32[]{:S(2)}) copy-start(bf16[128,2048]{1,0:T(8,128)(2,1)S(1)} %collective-permute-done.5.refs_6_) | copy-start | bytes 1572868
  43.9 4.8 %collective-permute-start.6 = (bf16[2,18,8,128]{3,2,1,0:T(8,128)(2,1)}, bf16[2,18,8,128]{3,2,1,0:T(8,128)(2,1)S(1)}, u32[]{:S(2)}, u32[]{:S(2)}) collective-permute-start(bf16[2,18,8,128]{3,2,1,0:T(8,128)(2,1)} %get-tuple-element.111), channel_id=1, source_target_pairs={{0,8},{8,0},{16,24},{24,16},{1,9},{9,1},{17,25},{25,17},{2,10},{10... | collective-permute-start | bytes 221192 | tf_op jit(solution)/shard_map/ppermute | solution.py:714
  44.5 5.8 %collective-permute-start.7 = (bf16[2,18,8,128]{3,2,1,0:T(8,128)(2,1)}, bf16[2,18,8,128]{3,2,1,0:T(8,128)(2,1)S(1)}, u32[]{:S(2)}, u32[]{:S(2)}) collective-permute-start(bf16[2,18,8,128]{3,2,1,0:T(8,128)(2,1)} %get-tuple-element.112), channel_id=1, source_target_pairs={{0,16},{8,24},{16,0},{24,8},{1,17},{9,25},{17,1},{25,9},{2,18},{10... | collective-permute-start | bytes 221192 | tf_op jit(solution)/shard_map/ppermute | solution.py:714
  45.9 6.4 %collective-permute-start.8 = (bf16[2,18,8,128]{3,2,1,0:T(8,128)(2,1)}, bf16[2,18,8,128]{3,2,1,0:T(8,128)(2,1)S(1)}, u32[]{:S(2)}, u32[]{:S(2)}) collective-permute-start(bf16[2,18,8,128]{3,2,1,0:T(8,128)(2,1)} %get-tuple-element.113), channel_id=1, source_target_pairs={{0,24},{8,16},{16,8},{24,0},{1,25},{9,17},{17,9},{25,1},{2,26},{10... | collective-permute-start | bytes 221192 | tf_op jit(solution)/shard_map/ppermute | solution.py:714
  48.7 4.4 %copy-start.12 = (bf16[2,18,8,128]{3,2,1,0:T(8,128)(2,1)}, bf16[2,18,8,128]{3,2,1,0:T(8,128)(2,1)S(1)}, u32[]{:S(2)}) copy-start(bf16[2,18,8,128]{3,2,1,0:T(8,128)(2,1)S(1)} %collective-permute-done.6.refs_11_) | copy-start | bytes 221188
  50.2 2.9 %copy-start.13 = (bf16[2,18,8,128]{3,2,1,0:T(8,128)(2,1)}, bf16[2,18,8,128]{3,2,1,0:T(8,128)(2,1)S(1)}, u32[]{:S(2)}) copy-start(bf16[2,18,8,128]{3,2,1,0:T(8,128)(2,1)S(1)} %collective-permute-done.7.refs_12_) | copy-start | bytes 221188
  52.3 0.8 copy-start.14
  52.4 18.5 %collective-permute-start.9 = (bf16[128,2048]{1,0:T(8,128)(2,1)S(1)}, bf16[128,2048]{1,0:T(8,128)(2,1)S(1)}, u32[]{:S(2)}, u32[]{:S(2)}) collective-permute-start(bf16[128,2048]{1,0:T(8,128)(2,1)S(1)} %collective-permute-done.5.refs_6_), channel_id=1, source_target_pairs={{0,8},{8,0},{16,24},{24,16},{1,9},{9,1},{17,25},{25,17},{2,10},{10... | collective-permute-start | bytes 1572872 | tf_op jit(solution)/shard_map/ppermute | solution.py:714
  53.1 17.5 %copy-start.17 = (bf16[128,512]{1,0:T(8,128)(2,1)S(1)}, bf16[128,512]{1,0:T(8,128)(2,1)}, u32[]{:S(2)}) copy-start(bf16[128,512]{1,0:T(8,128)(2,1)} %get-tuple-element.137) | copy-start | bytes 393220
  67.6 18.7 %collective-permute-start.10 = (bf16[144,1024]{1,0:T(8,128)(2,1)}, bf16[144,1024]{1,0:T(8,128)(2,1)S(1)}, u32[]{:S(2)}, u32[]{:S(2)}) collective-permute-start(bf16[144,1024]{1,0:T(8,128)(2,1)} %get-tuple-element.141.refs_2_), channel_id=1, source_target_pairs={{0,16},{8,24},{16,0},{24,8},{1,17},{9,25},{17,1},{25,9},{2,18},{10... | collective-permute-start | bytes 884744 | tf_op jit(solution)/shard_map/ppermute | solution.py:714
  70.8 14.7 %copy-start.1 = (bf16[128,512]{0,1:T(8,128)(2,1)}, bf16[128,512]{0,1:T(8,128)(2,1)S(1)}, u32[]{:S(2)}) copy-start(bf16[128,512]{0,1:T(8,128)(2,1)S(1)} %copy.26) | copy-start | bytes 393220
  70.8 15.6 %collective-permute-start.11 = (bf16[512,128]{1,0:T(8,128)(2,1)S(1)}, bf16[512,128]{1,0:T(8,128)(2,1)S(1)}, u32[]{:S(2)}, u32[]{:S(2)}) collective-permute-start(bf16[512,128]{1,0:T(8,128)(2,1)S(1)} %bitcast.17), channel_id=1, source_target_pairs={{0,16},{8,24},{16,0},{24,8},{1,17},{9,25},{17,1},{25,9},{2,18},{10... | collective-permute-start | bytes 393224 | tf_op jit(solution)/shard_map/ppermute | solution.py:714
  70.9 14.6 %copy-start.6 = (bf16[128,2048]{1,0:T(8,128)(2,1)}, bf16[128,2048]{1,0:T(8,128)(2,1)S(1)}, u32[]{:S(2)}) copy-start(bf16[128,2048]{1,0:T(8,128)(2,1)S(1)} %collective-permute-done.9.refs_7_) | copy-start | bytes 1572868
  86.4 4.2 %copy-start.7 = (bf16[512,128]{1,0:T(8,128)(2,1)}, bf16[512,128]{1,0:T(8,128)(2,1)S(1)}, u32[]{:S(2)}) copy-start(bf16[512,128]{1,0:T(8,128)(2,1)S(1)} %collective-permute-done.11.refs_1_) | copy-start | bytes 393220
  86.4 4.2 %copy-start.8 = (bf16[144,1024]{1,0:T(8,128)(2,1)}, bf16[144,1024]{1,0:T(8,128)(2,1)S(1)}, u32[]{:S(2)}) copy-start(bf16[144,1024]{1,0:T(8,128)(2,1)S(1)} %collective-permute-done.10.refs_3_) | copy-start | bytes 884740
  86.4 1.7 %collective-permute-start.12 = (bf16[640,128]{1,0:T(8,128)(2,1)}, bf16[640,128]{1,0:T(8,128)(2,1)S(1)}, u32[]{:S(2)}, u32[]{:S(2)}) collective-permute-start(bf16[640,128]{1,0:T(8,128)(2,1)} %get-tuple-element.138), channel_id=1, source_target_pairs={{0,1},{1,0},{2,3},{3,2},{4,5},{5,4},{6,7},{7,6},{8,9},{9,8},{10,11... | collective-permute-start | bytes 491528 | tf_op jit(solution)/shard_map/ppermute | solution.py:714
  89.0 7.0 %collective-permute-start.13 = (bf16[640,128]{1,0:T(8,128)(2,1)S(1)}, bf16[640,128]{1,0:T(8,128)(2,1)S(1)}, u32[]{:S(2)}, u32[]{:S(2)}) collective-permute-start(bf16[640,128]{1,0:T(8,128)(2,1)S(1)} %add_convert_fusion.1), channel_id=1, source_target_pairs={{0,2},{1,3},{2,0},{3,1},{4,6},{5,7},{6,4},{7,5},{8,10},{9,11},{10,... | collective-permute-start | bytes 491528 | tf_op jit(solution)/shard_map/ppermute | solution.py:714
  93.1 15.3 %collective-permute-start.15 = (bf16[144,1024]{1,0:T(8,128)(2,1)}, bf16[144,1024]{1,0:T(8,128)(2,1)S(1)}, u32[]{:S(2)}, u32[]{:S(2)}) collective-permute-start(bf16[144,1024]{1,0:T(8,128)(2,1)} %get-tuple-element.144), channel_id=1, source_target_pairs={{0,8},{8,0},{16,24},{24,16},{1,9},{9,1},{17,25},{25,17},{2,10},{10... | collective-permute-start | bytes 884744 | tf_op jit(solution)/shard_map/ppermute | solution.py:714
  93.4 17.4 %collective-permute-start.16 = (bf16[144,1024]{1,0:T(8,128)(2,1)}, bf16[144,1024]{1,0:T(8,128)(2,1)S(1)}, u32[]{:S(2)}, u32[]{:S(2)}) collective-permute-start(bf16[144,1024]{1,0:T(8,128)(2,1)} %get-tuple-element.153.refs_2_), channel_id=1, source_target_pairs={{0,16},{8,24},{16,0},{24,8},{1,17},{9,25},{17,1},{25,9},{2,18},{10... | collective-permute-start | bytes 884744 | tf_op jit(solution)/shard_map/ppermute | solution.py:714
  96.0 12.3 %copy-start = (bf16[640,128]{1,0:T(8,128)(2,1)}, bf16[640,128]{1,0:T(8,128)(2,1)S(1)}, u32[]{:S(2)}) copy-start(bf16[640,128]{1,0:T(8,128)(2,1)S(1)} %add_convert_fusion.back_a) | copy-start | bytes 491524
  96.0 12.3 %collective-permute-start.14 = (bf16[640,128]{1,0:T(8,128)(2,1)S(1)}, bf16[640,128]{1,0:T(8,128)(2,1)S(1)}, u32[]{:S(2)}, u32[]{:S(2)}) collective-permute-start(bf16[640,128]{1,0:T(8,128)(2,1)S(1)} %add_convert_fusion.back_a), channel_id=1, source_target_pairs={{0,4},{1,5},{2,6},{3,7},{4,0},{5,1},{6,2},{7,3},{8,12},{9,13},{10,... | collective-permute-start | bytes 491528 | tf_op jit(solution)/shard_map/ppermute | solution.py:714
  108.4 21.3 %copy-start.10 = (bf16[144,1024]{1,0:T(8,128)(2,1)}, bf16[144,1024]{1,0:T(8,128)(2,1)S(1)}, u32[]{:S(2)}) copy-start(bf16[144,1024]{1,0:T(8,128)(2,1)S(1)} %collective-permute-done.15.refs_9_) | copy-start | bytes 884740
  108.4 0.7 copy-start.2
  110.8 0.7 copy-start.9
  114.0 15.7 %collective-permute-start.23 = (bf16[144,1024]{1,0:T(8,128)(2,1)}, bf16[144,1024]{1,0:T(8,128)(2,1)S(1)}, u32[]{:S(2)}, u32[]{:S(2)}) collective-permute-start(bf16[144,1024]{1,0:T(8,128)(2,1)} %get-tuple-element.178), channel_id=1, source_target_pairs={{0,8},{8,0},{16,24},{24,16},{1,9},{9,1},{17,25},{25,17},{2,10},{10... | collective-permute-start | bytes 884744 | tf_op jit(solution)/shard_map/ppermute | solution.py:714
  114.0 11.2 %collective-permute-start.17 = (bf16[160,128]{1,0:T(8,128)(2,1)}, bf16[160,128]{1,0:T(8,128)(2,1)S(1)}, u32[]{:S(2)}, u32[]{:S(2)}) collective-permute-start(bf16[160,128]{1,0:T(8,128)(2,1)} %get-tuple-element.163), channel_id=1, source_target_pairs={{0,8},{8,0},{16,24},{24,16},{1,9},{9,1},{17,25},{25,17},{2,10},{10... | collective-permute-start | bytes 122888 | tf_op jit(solution)/shard_map/ppermute | solution.py:714
  116.0 9.2 %collective-permute-start.18 = (bf16[160,128]{1,0:T(8,128)(2,1)}, bf16[160,128]{1,0:T(8,128)(2,1)S(1)}, u32[]{:S(2)}, u32[]{:S(2)}) collective-permute-start(bf16[160,128]{1,0:T(8,128)(2,1)} %get-tuple-element.164), channel_id=1, source_target_pairs={{0,16},{8,24},{16,0},{24,8},{1,17},{9,25},{17,1},{25,9},{2,18},{10... | collective-permute-start | bytes 122888 | tf_op jit(solution)/shard_map/ppermute | solution.py:714
  116.4 8.8 %collective-permute-start.19 = (bf16[160,128]{1,0:T(8,128)(2,1)}, bf16[160,128]{1,0:T(8,128)(2,1)S(1)}, u32[]{:S(2)}, u32[]{:S(2)}) collective-permute-start(bf16[160,128]{1,0:T(8,128)(2,1)} %get-tuple-element.165), channel_id=1, source_target_pairs={{0,24},{8,16},{16,8},{24,0},{1,25},{9,17},{17,9},{25,1},{2,26},{10... | collective-permute-start | bytes 122888 | tf_op jit(solution)/shard_map/ppermute | solution.py:714
  125.2 4.5 %copy-start.22 = (bf16[160,128]{1,0:T(8,128)(2,1)}, bf16[160,128]{1,0:T(8,128)(2,1)S(1)}, u32[]{:S(2)}) copy-start(bf16[160,128]{1,0:T(8,128)(2,1)S(1)} %collective-permute-done.17.refs_1_) | copy-start | bytes 122884
  125.2 4.4 %copy-start.23 = (bf16[160,128]{1,0:T(8,128)(2,1)}, bf16[160,128]{1,0:T(8,128)(2,1)S(1)}, u32[]{:S(2)}) copy-start(bf16[160,128]{1,0:T(8,128)(2,1)S(1)} %collective-permute-done.18.refs_2_) | copy-start | bytes 122884
  125.2 4.4 %copy-start.24 = (bf16[160,128]{1,0:T(8,128)(2,1)}, bf16[160,128]{1,0:T(8,128)(2,1)S(1)}, u32[]{:S(2)}) copy-start(bf16[160,128]{1,0:T(8,128)(2,1)S(1)} %collective-permute-done.19.refs_3_) | copy-start | bytes 122884
  125.2 9.1 %collective-permute-start.20 = (bf16[16,2048]{1,0:T(8,128)(2,1)}, bf16[16,2048]{1,0:T(8,128)(2,1)S(1)}, u32[]{:S(2)}, u32[]{:S(2)}) collective-permute-start(bf16[16,2048]{1,0:T(8,128)(2,1)} %get-tuple-element.180.refs_3_), channel_id=1, source_target_pairs={{0,8},{8,16},{16,24},{24,0},{1,9},{9,17},{17,25},{25,1},{2,10},{10... | collective-permute-start | bytes 196616 | tf_op jit(solution)/shard_map/ppermute | solution.py:52
  126.4 8.0 %collective-permute-start.21 = (bf16[16,2048]{1,0:T(8,128)(2,1)}, bf16[16,2048]{1,0:T(8,128)(2,1)S(1)}, u32[]{:S(2)}, u32[]{:S(2)}) collective-permute-start(bf16[16,2048]{1,0:T(8,128)(2,1)} %get-tuple-element.180.refs_3_), channel_id=1, source_target_pairs={{0,16},{8,24},{16,0},{24,8},{1,17},{9,25},{17,1},{25,9},{2,18},{10... | collective-permute-start | bytes 196616 | tf_op jit(solution)/shard_map/ppermute | solution.py:52
  127.7 6.7 %collective-permute-start.22 = (bf16[16,2048]{1,0:T(8,128)(2,1)}, bf16[16,2048]{1,0:T(8,128)(2,1)S(1)}, u32[]{:S(2)}, u32[]{:S(2)}) collective-permute-start(bf16[16,2048]{1,0:T(8,128)(2,1)} %get-tuple-element.180.refs_3_), channel_id=1, source_target_pairs={{0,24},{8,0},{16,8},{24,16},{1,25},{9,1},{17,9},{25,17},{2,26},{10... | collective-permute-start | bytes 196616 | tf_op jit(solution)/shard_map/ppermute | solution.py:52
  129.6 0.7 copy-start.11
  134.4 0.6 copy-start.19
  134.4 0.6 copy-start.20
  134.4 0.6 copy-start.21

commit v10 on v9

--- a/solution.py
+++ b/solution.py
@@ -130,10 +130,10 @@
 
 def local_kernel(low_rank, states, places, *refs):
     parts, refs = refs[:2], refs[2:]
-    (weight_ref, bias_ref, decay_ref, conv_ref, gate_ref, grad_ref) = refs[:6]
-    (dt_ref, dx_ref, g_ref, coef_ref, low) = refs[6:11]
+    (coef, weight_ref, bias_ref, decay_ref, conv_ref, gate_ref, grad_ref) = refs[:7]
+    (dt_ref, dx_ref, g_ref, low) = refs[7:11]
     messages, refs = refs[11 : 10 + places], refs[10 + places :]
-    (coef_v, coef, tiles, dts, dxs, gs, fwd, bwd, sem) = refs
+    (tiles, dts, dxs, gs, fwd, bwd) = refs
     step = pl.program_id(0)
     chunks = dts.shape[0]
     rows = conv_ref.shape[0]
@@ -143,12 +143,6 @@
     def _():
         total = (parts[0][...].astype(F32) + parts[1][...].astype(F32)).astype(BF)
         low[...] = total[:, :low_rank]
-        coef_v[...] = jnp.zeros_like(coef_v)
-        coef_v[:, : 2 * states] = total[:, low_rank:].astype(F32)
-        coef_ref[...] = jnp.transpose(coef_v[...])[: 2 * states, :]
-        copy = pltpu.make_async_copy(coef_ref, coef, sem)
-        copy.start()
-        copy.wait()
 
     pre = dot(low[...], weight_ref[...]) + bias_ref[...]
     for start in range(0, rows, 16):
@@ -191,6 +185,7 @@
                 state, run, head, total = (list(part) for part in carry)
                 for sub in range(8):
                     token = index * 8 + sub
+                    base = token * (2 * states)
                     size = [dts[v, token] for v in range(chunks)]
                     drive = [dxs[v, token] for v in range(chunks)]
                     grad = [gs[v, token] for v in range(chunks)]
@@ -198,9 +193,9 @@
                         total = [a + b for a, b in zip(total, size)]
                     for k, (n, v) in enumerate(pairs):
                         factor = jnp.exp2(size[v] * rates[k])
-                        state[k] = factor * state[k] + drive[v] * coef[n, token]
+                        state[k] = factor * state[k] + drive[v] * coef[base + n]
                         run[k] = run[k] * factor
-                        head[k] = head[k] + run[k] * (grad[v] * coef[states + n, token])
+                        head[k] = head[k] + run[k] * (grad[v] * coef[base + (states + n)])
                 return state, run, head, total
 
             many = [zero] * len(pairs)
@@ -224,7 +219,7 @@
             message[...] = jnp.where((place ^ mask) > place, fwd[...], bwd[...]).astype(BF)
 
 
-def local_call(parts, step_weight, step_bias, decay, conv_out, gate, grad, states, places):
+def local_call(parts, coef, step_weight, step_bias, decay, conv_out, gate, grad, states, places):
     rows, chans = conv_out.shape
     wide = parts[0].shape[1]
     low_rank = step_weight.shape[0]
@@ -239,6 +234,7 @@
         in_specs=[
             whole((rows, wide)),
             whole((rows, wide)),
+            pl.BlockSpec(memory_space=pltpu.SMEM),
             columns(low_rank, width),
             columns(1, width),
             whole(decay.shape),
@@ -248,30 +244,25 @@
         ],
         out_specs=[
             *[pl.BlockSpec((1, rows, groups, 128), lambda i: (i, 0, 0, 0))] * 3,
-            whole((2 * states, rows)),
             whole((rows, low_rank)),
         ]
         + [whole(message)] * (places - 1),
         out_shape=[
             *[sds(dense, F32)] * 3,
-            sds((2 * states, rows), F32),
             sds((rows, low_rank), BF),
         ]
         + [sds(message, BF)] * (places - 1),
         scratch_shapes=[
-            pltpu.VMEM((rows, 128), F32),
-            pltpu.SMEM((2 * states, rows), F32),
             pltpu.VMEM((3, rows * groups, 128), F32),
             big,
             big,
             big,
             pltpu.VMEM(message, F32),
             pltpu.VMEM(message, F32),
-            pltpu.SemaphoreType.DMA,
         ],
         compiler_params=params(),
         name="local_ends",
-    )(*parts, step_weight, step_bias, decay, conv_out, gate, grad)
+    )(*parts, coef, step_weight, step_bias, decay, conv_out, gate, grad)
 
 
 def fold_rows(products, base, groups, target, first):
@@ -320,6 +311,7 @@
         for sub in range(8):
             token = index * 8 + sub
             at = pl.ds(index * span + sub, groups, stride=8)
+            scalar = token * (2 * states)
             size, drive, grad = dt_ref[0, token], dx_ref[0, token], g_ref[0, token]
             result = jnp.zeros((groups, 128), F32)
             for lead in range(0, states, 8):
@@ -329,8 +321,8 @@
                     kept = factor * state[n]
                     factors[token, n] = factor
                     decayed[token, n] = kept
-                    state[n] = kept + drive * coef[n, token]
-                    result = result + state[n] * coef[states + n, token]
+                    state[n] = kept + drive * coef[scalar + n]
+                    result = result + state[n] * coef[scalar + (states + n)]
                     row = base + (n - lead) * groups
                     products[row : row + groups, :] = state[n] * grad
                 fold_rows(products, base, groups, coef_out, token * states + lead)
@@ -345,18 +337,19 @@
         for sub in range(7, -1, -1):
             token = index * 8 + sub
             at = pl.ds(index * span + sub, groups, stride=8)
+            scalar = token * (2 * states)
             size, drive, grad = dt_ref[0, token], dx_ref[0, token], g_ref[0, token]
             slope = jnp.zeros((groups, 128), F32)
             inner = jnp.zeros((groups, 128), F32)
             for lead in range(0, states, 8):
                 base = (sub * states + lead) * groups
                 for n in range(lead, lead + 8):
-                    adjoint = carry[n] + grad * coef[states + n, token]
+                    adjoint = carry[n] + grad * coef[scalar + (states + n)]
                     carry[n] = factors[token, n] * adjoint
                     weighted = adjoint * decayed[token, n] * (size * rate[n])
                     slope = slope + weighted
                     gathered[n] = gathered[n] + weighted
-                    inner = inner + adjoint * coef[n, token]
+                    inner = inner + adjoint * coef[scalar + n]
                     row = base + (n - lead) * groups
                     products[row : row + groups, :] = adjoint * drive
                 fold_rows(products, base, groups, coef_in, token * states + lead)
@@ -771,8 +764,10 @@
     conv_out, part = conv_call(conv_input, rim, conv_weight, conv_bias, proj_weight)
     blocks = spread(conv_out)
     parts = chan_sum(part)
-    dt, dx, g, coef, low, *messages = local_call(
-        parts, step_weight, step_bias, decay, conv_out, gate_input, out_grad, states, places
+    coef = (parts[0][:, low_rank:].astype(F32) + parts[1][:, low_rank:].astype(F32)).astype(BF)
+    coef = coef.astype(F32).reshape(-1)
+    dt, dx, g, low, *messages = local_call(
+        parts, coef, step_weight, step_bias, decay, conv_out, gate_input, out_grad, states, places
     )
     messages, blocks = tie((messages, blocks))
     messages = [swap(message, "ctx", mask) for mask, message in enumerate(messages, 1)]
@@ -794,25 +789,27 @@
     part, grad_gate, scan_part, small = previous
     ranks = low_rank // places
     products = []
+    backs = chan_sum(part)
+    if chunks > 1:
+        near, lows = tie((backs[0], lows))
+        backs = (near, backs[1])
     for step in steps[:-1]:
         mine, theirs = step_call(ranks, lows, step)
         products += [mine, swap(theirs, "ctx", 1)]
-    backs = chan_sum(part)
-    backs, products = tie((backs, products))
     cuts = cut_call(places, backs)
     cuts, lows = tie((cuts, lows))
     cuts = [cuts[0]] + [swap(cut, "ctx", mask) for mask, cut in enumerate(cuts[1:], 1)]
     mine, theirs = step_call(ranks, lows, steps[-1])
     backs, theirs = tie((backs, theirs))
-    products += [mine, swap(theirs, "ctx", 1)]
+    latest = [mine, swap(theirs, "ctx", 1)]
     main, tail, sums = conv_grad_call(
         places, low_rank, backs, proj_weight, scan_part, small, conv_input, rim, conv_weight,
         conv_bias,
     )
-    sums, cuts = tie((sums, cuts))
+    sums, cuts, products = tie((sums, cuts, products))
     late = [sums] + [rotate(sums, "ctx", hop) for hop in range(1, places)]
     grad_proj, grad_coef, grad_step, decay_grad = rows_call(
-        ranks, 2 * states // places, cuts, blocks, products
+        ranks, 2 * states // places, cuts, blocks, products + latest
     )
     late, grad_proj = tie((late, grad_proj))
     grad_input, conv_w, conv_b, step_b, skip = last_call(main, tail, conv_weight, late)

time: 137 us -> 134 us (0.978)
  starting transfers between devices: 36.3 us -> 31.7 us
  waiting for transfers between devices: 26.2 us -> 29.5 us
  Pallas kernels: 65.6 us -> 63.1 us
    ppermute x20, starting transfers between devices: 27 us -> 22.9 us  [swap(): lax.ppermute(block, axis, [(i, i ^ mask) for i in range(lax.axis_size(axi...]
    ppermute x20, waiting for transfers between devices: 24.7 us -> 28.1 us  [swap(): lax.ppermute(block, axis, [(i, i ^ mask) for i in range(lax.axis_size(axi...]
    pallas_call x2, Pallas kernels: 29.1 us -> 27.5 us  [scan_call(): pl.pallas_call(functools.partial(scan_kernel, places, states, first), gri...]
  transfers between devices with their start and end apart: 24 -> 24, of which waited for: 9 -> 14; matrix products, arithmetic and copies ran while one was open for 1% -> 1% of each run, Pallas kernels for 41% -> 42%
where the time goes in v10:
time: 134 us
  Pallas kernels  63.1 us (47%)
  starting transfers between devices  31.7 us (24%)
  waiting for transfers between devices  29.5 us (22%)
  local copies, waits for them, and re-layouts  6.26 us (5%)
  other arithmetic  2.02 us (2%)
    ppermute x20, waiting for transfers between devices, swap(): lax.ppermute(block, axis, [(i, i ^ mask) for i in range(lax.axis_size(axi...  28.1 us
    pallas_call x2, Pallas kernels, scan_call(): pl.pallas_call(functools.partial(scan_kernel, places, states, first), gri...  27.5 us
    ppermute x20, starting transfers between devices, swap(): lax.ppermute(block, axis, [(i, i ^ mask) for i in range(lax.axis_size(axi...  22.9 us
    pallas_call x1, Pallas kernels, local_call(): pl.pallas_call(functools.partial(local_kernel, low_rank, states, places),...  11.7 us
    pallas_call x1, Pallas kernels, conv_grad_call(): pl.pallas_call(functools.partial(conv_grad_kernel, places, low_rank), gri...  6.75 us
    pallas_call x2, Pallas kernels, step_call(): pl.pallas_call(functools.partial(step_kernel, ranks, len(lows)), grid=(ch...  4.96 us
    ppermute x1, starting transfers between devices, shift(): return lax.ppermute(block, axis, route)  4.93 us
    pallas_call x1, Pallas kernels, conv_call(): pl.pallas_call(conv_kernel, grid=(chans // width,), in_specs=[columns(row...  4.82 us
  transfers between devices with their start and end apart: 24, of which 14 were waited for; matrix products, arithmetic and copies ran while one was open for 1% of the time, Pallas kernels for 42%

profile of v10, /device:TPU:0, one launch (start us, length us, event | category | flops | bytes accessed | tf_op | source)
XLA Modules:
  0.0 133.5 jit_solution(6069858180365172134)
XLA Ops:
  0.7 0.8 slice.9
  1.5 4.9 %collective-permute-start = (bf16[3,2048]{1,0:T(4,128)(2,1)S(1)}, bf16[3,2048]{1,0:T(4,128)(2,1)S(1)}, u32[]{:S(2)}, u32[]{:S(2)}) collective-permute-start(bf16[3,2048]{1,0:T(4,128)(2,1)S(1)} %slice.9), channel_id=1, source_target_pairs={{0,8},{8,16},{16,24},{1,9},{9,17},{17,25},{2,10},{10,18},{18,26},{... | collective-permute-start | bytes 36872 | tf_op jit(solution)/shard_map/ppermute | solution.py:58
  6.4 1.4 %collective-permute-done.rim_ref = bf16[3,2048]{1,0:T(4,128)(2,1)S(1)} collective-permute-done((bf16[3,2048]{1,0:T(4,128)(2,1)S(1)}, bf16[3,2048]{1,0:T(4,128)(2,1)S(1)}, u32[]{:S(2)}, u32[]{:S(2)}) %collective-permute-start) | collective-permute-done | bytes 12320 | tf_op jit(solution)/shard_map/ppermute | solution.py:58
  7.8 0.6 copy-done.18
  8.4 4.8 %conv_project.1 = (bf16[128,2048]{1,0:T(8,128)(2,1)}, bf16[128,544]{1,0:T(8,128)(2,1)}) custom-call(bf16[128,2048]{1,0:T(8,128)(2,1)} %input_ref.3, bf16[3,2048]{1,0:T(4,128)(2,1)} %copy-done.18, f32[4,2048]{1,0:T(4,128)} %refs_2_.1, f32[1,2048]{1,0:T(1,128)} %bitcast.26, bf16[544,2048]{1,0:T(8,128)(2,1)} %proj_ref.3), custom_call_target="tpu_custom_call" | custom-call | tf_op jit(solution)/shard_map/conv_project/pallas_call | solution.py:103
  13.3 0.0 collective-permute-start.1
  13.3 1.6 %collective-permute-done.1 = bf16[128,544]{1,0:T(8,128)(2,1)S(1)} collective-permute-done((bf16[128,544]{1,0:T(8,128)(2,1)}, bf16[128,544]{1,0:T(8,128)(2,1)S(1)}, u32[]{:S(2)}, u32[]{:S(2)}) %collective-permute-start.1) | collective-permute-done | bytes 139296 | tf_op jit(solution)/shard_map/ppermute | solution.py:707
  14.9 1.0 add_convert_fusion.3
  15.8 1.6 %collective-permute-start.2 = (bf16[128,544]{1,0:T(8,128)(2,1)S(1)}, bf16[128,544]{1,0:T(8,128)(2,1)S(1)}, u32[]{:S(2)}, u32[]{:S(2)}) collective-permute-start(bf16[128,544]{1,0:T(8,128)(2,1)S(1)} %add_convert_fusion.3), channel_id=1, source_target_pairs={{0,2},{1,3},{2,0},{3,1},{4,6},{5,7},{6,4},{7,5},{8,10},{9,11},{10,... | collective-permute-start | bytes 417800 | tf_op jit(solution)/shard_map/ppermute | solution.py:707
  17.4 2.3 %collective-permute-start.4 = (bf16[128,2048]{1,0:T(8,128)(2,1)}, bf16[128,2048]{1,0:T(8,128)(2,1)S(1)}, u32[]{:S(2)}, u32[]{:S(2)}) collective-permute-start(bf16[128,2048]{1,0:T(8,128)(2,1)} %get-tuple-element.171.refs_6_.refs_4_), channel_id=1, source_target_pairs={{0,8},{8,0},{16,24},{24,16},{1,9},{9,1},{17,25},{25,17},{2,10},{10... | collective-permute-start | bytes 1572872 | tf_op jit(solution)/shard_map/ppermute | solution.py:707
  19.7 2.6 %collective-permute-start.5 = (bf16[128,2048]{1,0:T(8,128)(2,1)}, bf16[128,2048]{1,0:T(8,128)(2,1)S(1)}, u32[]{:S(2)}, u32[]{:S(2)}) collective-permute-start(bf16[128,2048]{1,0:T(8,128)(2,1)} %get-tuple-element.171.refs_6_.refs_4_), channel_id=1, source_target_pairs={{0,16},{8,24},{16,0},{24,8},{1,17},{9,25},{17,1},{25,9},{2,18},{10... | collective-permute-start | bytes 1572872 | tf_op jit(solution)/shard_map/ppermute | solution.py:707
  22.3 0.0 collective-permute-done.2
  22.3 0.0 copy-start.2
  22.3 1.6 %collective-permute-start.3 = (bf16[128,544]{1,0:T(8,128)(2,1)S(1)}, bf16[128,544]{1,0:T(8,128)(2,1)S(1)}, u32[]{:S(2)}, u32[]{:S(2)}) collective-permute-start(bf16[128,544]{1,0:T(8,128)(2,1)S(1)} %add_convert_fusion.2.refs_0_), channel_id=1, source_target_pairs={{0,4},{1,5},{2,6},{3,7},{4,0},{5,1},{6,2},{7,3},{8,12},{9,13},{10,... | collective-permute-start | bytes 417800 | tf_op jit(solution)/shard_map/ppermute | solution.py:707
  23.9 0.7 copy.29
  24.6 3.2 %collective-permute-done.3.refs_1_ = bf16[128,544]{1,0:T(8,128)(2,1)S(1)} collective-permute-done((bf16[128,544]{1,0:T(8,128)(2,1)S(1)}, bf16[128,544]{1,0:T(8,128)(2,1)S(1)}, u32[]{:S(2)}, u32[]{:S(2)}) %collective-permute-start.3) | collective-permute-done | bytes 139296 | tf_op jit(solution)/shard_map/ppermute | solution.py:707
  27.8 0.7 reshape.36.refs_2_.refs_0_
  28.5 11.7 %local_ends.1 = (f32[2,128,8,128]{3,2,1,0:T(8,128)}, f32[2,128,8,128]{3,2,1,0:T(8,128)}, f32[2,128,8,128]{3,2,1,0:T(8,128)}, bf16[128,512]{1,0:T(8,128)(2,1)}, b...) custom-call(bf16[128,544]{1,0:T(8,128)(2,1)} %copy-done.2, ...), custom_call_target="tpu_custom_call" | custom-call | tf_op jit(solution)/shard_map/local_ends/pallas_call | solution.py:231
  40.2 2.7 %collective-permute-done.4.refs_5_ = bf16[128,2048]{1,0:T(8,128)(2,1)S(1)} collective-permute-done((bf16[128,2048]{1,0:T(8,128)(2,1)}, bf16[128,2048]{1,0:T(8,128)(2,1)S(1)}, u32[]{:S(2)}, u32[]{:S(2)}) %collective-permute-start.4) | collective-permute-done | bytes 524320 | tf_op jit(solution)/shard_map/ppermute | solution.py:707
  42.9 2.6 %collective-permute-done.5.refs_6_ = bf16[128,2048]{1,0:T(8,128)(2,1)S(1)} collective-permute-done((bf16[128,2048]{1,0:T(8,128)(2,1)}, bf16[128,2048]{1,0:T(8,128)(2,1)S(1)}, u32[]{:S(2)}, u32[]{:S(2)}) %collective-permute-start.5) | collective-permute-done | bytes 524320 | tf_op jit(solution)/shard_map/ppermute | solution.py:707
  45.5 0.4 collective-permute-start.6
  45.9 2.6 %collective-permute-start.7 = (bf16[2,18,8,128]{3,2,1,0:T(8,128)(2,1)}, bf16[2,18,8,128]{3,2,1,0:T(8,128)(2,1)S(1)}, u32[]{:S(2)}, u32[]{:S(2)}) collective-permute-start(bf16[2,18,8,128]{3,2,1,0:T(8,128)(2,1)} %get-tuple-element.111), channel_id=1, source_target_pairs={{0,16},{8,24},{16,0},{24,8},{1,17},{9,25},{17,1},{25,9},{2,18},{10... | collective-permute-start | bytes 221192 | tf_op jit(solution)/shard_map/ppermute | solution.py:707
  48.6 1.3 collective-permute-start.8
  49.9 1.8 %collective-permute-done.6.refs_11_ = bf16[2,18,8,128]{3,2,1,0:T(8,128)(2,1)S(1)} collective-permute-done((bf16[2,18,8,128]{3,2,1,0:T(8,128)(2,1)}, bf16[2,18,8,128]{3,2,1,0:T(8,128)(2,1)S(1)}, u32[]{:S(2)}, u32[]{:S(2)}) %collective-permute-start.6) | collective-permute-done | bytes 73760 | tf_op jit(solution)/shard_map/ppermute | solution.py:707
  51.7 1.1 collective-permute-done.7.refs_12_
  52.8 3.0 %collective-permute-done.8.refs_13_ = bf16[2,18,8,128]{3,2,1,0:T(8,128)(2,1)S(1)} collective-permute-done((bf16[2,18,8,128]{3,2,1,0:T(8,128)(2,1)}, bf16[2,18,8,128]{3,2,1,0:T(8,128)(2,1)S(1)}, u32[]{:S(2)}, u32[]{:S(2)}) %collective-permute-start.8) | collective-permute-done | bytes 73760 | tf_op jit(solution)/shard_map/ppermute | solution.py:707
  55.7 0.6 copy-done.14
  56.4 13.6 %scan_gradients.2 = (bf16[144,1024]{1,0:T(8,128)(2,1)}, bf16[128,2048]{1,0:T(8,128)(2,1)}, bf16[128,2048]{1,0:T(8,128)(2,1)}, f32[8,2048]{1,0:T(8,128)}, f32[640,128]{1,0:T(8,128)}) custom-call(f32[4096]{0:T(1024)} %reshape.36.refs_2_.refs_0_, f32[2,128,8,128]{3,2,1,0:T(8,128)} %get-tuple-element.104.refs_1_, f32[2,128,8,128]{3,2,1,0:T(8,128)} %get-tuple-element.105.refs_2_, ...), custom_call_target="tpu_custom_call" | custom-call | tf_op jit(solution)/shard_map/scan_gradients/pallas_call | solution.py:467
  70.0 0.6 collective-permute-start.10
  70.6 0.1 copy.26
  70.8 2.4 %collective-permute-start.11 = (bf16[512,128]{1,0:T(8,128)(2,1)S(1)}, bf16[512,128]{1,0:T(8,128)(2,1)S(1)}, u32[]{:S(2)}, u32[]{:S(2)}) collective-permute-start(bf16[512,128]{1,0:T(8,128)(2,1)S(1)} %bitcast.17), channel_id=1, source_target_pairs={{0,16},{8,24},{16,0},{24,8},{1,17},{9,25},{17,1},{25,9},{2,18},{10... | collective-permute-start | bytes 393224 | tf_op jit(solution)/shard_map/ppermute | solution.py:707
  73.2 13.8 %scan_gradients.3 = (bf16[144,1024]{1,0:T(8,128)(2,1)}, bf16[128,2048]{1,0:T(8,128)(2,1)}, bf16[128,2048]{1,0:T(8,128)(2,1)}, f32[8,2048]{1,0:T(8,128)}, bf16[640,128]{1,0:T(8,128)(2,1)}) custom-call(f32[4096]{0:T(1024)} %reshape.36.refs_2_.refs_0_, ...), custom_call_target="tpu_custom_call", output_to_operand_aliasing={{1}: (15, {}), {2}: (16, {}), {3}: (17, {})} | custom-call | tf_op jit(solution)/shard_map/scan_gradients/pallas_call | solution.py:467
  87.1 0.7 collective-permute-done.11.refs_1_
  87.8 0.1 collective-permute-start.12
  87.9 1.6 %collective-permute-done.12 = bf16[640,128]{1,0:T(8,128)(2,1)S(1)} collective-permute-done((bf16[640,128]{1,0:T(8,128)(2,1)}, bf16[640,128]{1,0:T(8,128)(2,1)S(1)}, u32[]{:S(2)}, u32[]{:S(2)}) %collective-permute-start.12) | collective-permute-done | bytes 163872 | tf_op jit(solution)/shard_map/ppermute | solution.py:707
  89.5 1.0 add_convert_fusion.1
  90.4 0.6 collective-permute-start.13
  91.0 0.0 collective-permute-start.15
  91.0 5.7 %collective-permute-done.13 = bf16[640,128]{1,0:T(8,128)(2,1)S(1)} collective-permute-done((bf16[640,128]{1,0:T(8,128)(2,1)S(1)}, bf16[640,128]{1,0:T(8,128)(2,1)S(1)}, u32[]{:S(2)}, u32[]{:S(2)}) %collective-permute-start.13) | collective-permute-done | bytes 163872 | tf_op jit(solution)/shard_map/ppermute | solution.py:707
  96.8 1.6 %collective-permute-start.14 = (bf16[640,128]{1,0:T(8,128)(2,1)S(1)}, bf16[640,128]{1,0:T(8,128)(2,1)S(1)}, u32[]{:S(2)}, u32[]{:S(2)}) collective-permute-start(bf16[640,128]{1,0:T(8,128)(2,1)S(1)} %add_convert_fusion.back_a), channel_id=1, source_target_pairs={{0,4},{1,5},{2,6},{3,7},{4,0},{5,1},{6,2},{7,3},{8,12},{9,13},{10,... | collective-permute-start | bytes 491528 | tf_op jit(solution)/shard_map/ppermute | solution.py:707
  98.4 2.5 %step_products.3 = (f32[144,1024]{1,0:T(8,128)}, bf16[144,1024]{1,0:T(8,128)(2,1)}) custom-call(bf16[512,128]{1,0:T(8,128)(2,1)} %bitcast.18, bf16[512,128]{1,0:T(8,128)(2,1)} %copy-done.7, bf16[144,1024]{1,0:T(8,128)(2,1)} %get-tuple-element.162.refs_2_, bf16[144,1024]{1,0:T(8,128)(2,1)} %copy-done.8), custom_call_target="tpu_custom_call" | custom-call | tf_op jit(solution)/shard_map/step_products/pallas_call | solution.py:612
  100.9 0.7 collective-permute-start.19
  101.6 0.7 collective-permute-done.14.back_b
  102.3 0.7 copy-done.3
  103.0 1.7 %cut_rows.1 = (bf16[160,128]{1,0:T(8,128)(2,1)}, bf16[160,128]{1,0:T(8,128)(2,1)}, bf16[160,128]{1,0:T(8,128)(2,1)}, bf16[160,128]{1,0:T(8,128)(2,1)}) custom-call(bf16[640,128]{1,0:T(8,128)(2,1)} %copy-done, bf16[640,128]{1,0:T(8,128)(2,1)} %copy-done.3), custom_call_target="tpu_custom_call" | custom-call | tf_op jit(solution)/shard_map/cut_rows/pallas_call | solution.py:581
  104.7 2.7 %collective-permute-done.15.refs_3_ = bf16[144,1024]{1,0:T(8,128)(2,1)S(1)} collective-permute-done((bf16[144,1024]{1,0:T(8,128)(2,1)}, bf16[144,1024]{1,0:T(8,128)(2,1)S(1)}, u32[]{:S(2)}, u32[]{:S(2)}) %collective-permute-start.15) | collective-permute-done | bytes 294944 | tf_op jit(solution)/shard_map/ppermute | solution.py:707
  107.4 0.7 copy-done.9
  108.1 2.5 %step_products.2 = (f32[144,1024]{1,0:T(8,128)}, bf16[144,1024]{1,0:T(8,128)(2,1)}) custom-call(bf16[512,128]{1,0:T(8,128)(2,1)} %bitcast.19, bf16[512,128]{1,0:T(8,128)(2,1)} %copy-done.7, bf16[144,1024]{1,0:T(8,128)(2,1)} %get-tuple-element.149.refs_2_, bf16[144,1024]{1,0:T(8,128)(2,1)} %copy-done.9), custom_call_target="tpu_custom_call" | custom-call | tf_op jit(solution)/shard_map/step_products/pallas_call | solution.py:612
  110.5 0.0 collective-permute-start.23
  110.5 2.0 %collective-permute-start.16 = (bf16[160,128]{1,0:T(8,128)(2,1)}, bf16[160,128]{1,0:T(8,128)(2,1)S(1)}, u32[]{:S(2)}, u32[]{:S(2)}) collective-permute-start(bf16[160,128]{1,0:T(8,128)(2,1)} %get-tuple-element.159), channel_id=1, source_target_pairs={{0,8},{8,0},{16,24},{24,16},{1,9},{9,1},{17,25},{25,17},{2,10},{10... | collective-permute-start | bytes 122888 | tf_op jit(solution)/shard_map/ppermute | solution.py:707
  112.6 2.4 %collective-permute-start.18 = (bf16[160,128]{1,0:T(8,128)(2,1)}, bf16[160,128]{1,0:T(8,128)(2,1)S(1)}, u32[]{:S(2)}, u32[]{:S(2)}) collective-permute-start(bf16[160,128]{1,0:T(8,128)(2,1)} %get-tuple-element.161), channel_id=1, source_target_pairs={{0,24},{8,16},{16,8},{24,0},{1,25},{9,17},{17,9},{25,1},{2,26},{10... | collective-permute-start | bytes 122888 | tf_op jit(solution)/shard_map/ppermute | solution.py:707
  115.0 6.7 %conv_gradients.1 = (bf16[128,2048]{1,0:T(8,128)(2,1)}, f32[16,2048]{1,0:T(8,128)}, bf16[16,2048]{1,0:T(8,128)(2,1)}) custom-call(bf16[640,128]{1,0:T(8,128)(2,1)} %copy-done, bf16[640,128]{1,0:T(8,128)(2,1)} %copy-done.3, bf16[544,2048]{1,0:T(8,128)(2,1)} %proj_ref.3, bf16[128,2048]{1,0:T(8,128)(2,1)} %get-tuple-element.153.scan_ref, ...), custom_call_target="tpu_custom_call" | custom-call | tf_op jit(solution)/shard_map/conv_gradients/pallas_call | solution.py:548
  121.7 0.8 collective-permute-done.16.refs_1_
  122.5 0.0 collective-permute-done.17.refs_2_
  122.5 0.0 collective-permute-done.19.refs_9_
  122.6 0.4 collective-permute-start.20
  122.9 1.8 %collective-permute-start.21 = (bf16[16,2048]{1,0:T(8,128)(2,1)}, bf16[16,2048]{1,0:T(8,128)(2,1)S(1)}, u32[]{:S(2)}, u32[]{:S(2)}) collective-permute-start(bf16[16,2048]{1,0:T(8,128)(2,1)} %get-tuple-element.180.refs_3_), channel_id=1, source_target_pairs={{0,16},{8,24},{16,0},{24,8},{1,17},{9,25},{17,1},{25,9},{2,18},{10... | collective-permute-start | bytes 196616 | tf_op jit(solution)/shard_map/ppermute | solution.py:52
  124.8 1.7 %collective-permute-start.22 = (bf16[16,2048]{1,0:T(8,128)(2,1)}, bf16[16,2048]{1,0:T(8,128)(2,1)S(1)}, u32[]{:S(2)}, u32[]{:S(2)}) collective-permute-start(bf16[16,2048]{1,0:T(8,128)(2,1)} %get-tuple-element.180.refs_3_), channel_id=1, source_target_pairs={{0,24},{8,0},{16,8},{24,16},{1,25},{9,1},{17,9},{25,17},{2,26},{10... | collective-permute-start | bytes 196616 | tf_op jit(solution)/shard_map/ppermute | solution.py:52
  126.5 0.7 copy-done.11
  127.1 4.0 %row_gradients.1 = (f32[128,2048]{1,0:T(8,128)}, f32[8,2048]{1,0:T(8,128)}, f32[128,2048]{1,0:T(8,128)}, f32[16,2048]{1,0:T(8,128)}) custom-call(bf16[160,128]{1,0:T(8,128)(2,1)} %get-tuple-element.167.refs_0_, bf16[160,128]{1,0:T(8,128)(2,1)} %copy-done.22, bf16[160,128]{1,0:T(8,128)(2,1)} %copy-done.23, bf16[160,128]{1,0:T(8,128)(2,1)} %copy-done.24, ...), custom_call_target="tpu_custom_call" | custom-call | tf_op jit(solution)/shard_map/row_gradients/pallas_call | solution.py:644
  131.2 0.6 copy-done.19
  131.8 0.0 copy-done.20
  131.8 0.0 copy-done.21
  131.8 1.7 %last_rows.1 = (bf16[128,2048]{1,0:T(8,128)(2,1)}, f32[4,2048]{1,0:T(4,128)}, f32[1,2048]{1,0:T(1,128)}, f32[1,2048]{1,0:T(1,128)}, f32[1,2048]{1,0:T(1,128)}) custom-call(bf16[128,2048]{1,0:T(8,128)(2,1)} %get-tuple-element.155.refs_0_, f32[16,2048]{1,0:T(8,128)} %get-tuple-element.156.refs_1_, f32[4,2048]{1,0:T(4,128)} %refs_2_.1, ...), custom_call_target="tpu_custom_call", output_to_operand_aliasing={{0}: (0, {})} | custom-call | tf_op jit(solution)/shard_map/last_rows/pallas_call | solution.py:684
  (54 shorter events, 0.2 us)
Async XLA Ops:
  0.6 23.3 %copy-start.16 = (f32[16,2048]{1,0:T(8,128)S(1)}, f32[16,2048]{1,0:T(8,128)}, u32[]{:S(2)}) copy-start(f32[16,2048]{1,0:T(8,128)} %param.18) | copy-start | bytes 393220
  1.5 6.4 %collective-permute-start = (bf16[3,2048]{1,0:T(4,128)(2,1)S(1)}, bf16[3,2048]{1,0:T(4,128)(2,1)S(1)}, u32[]{:S(2)}, u32[]{:S(2)}) collective-permute-start(bf16[3,2048]{1,0:T(4,128)(2,1)S(1)} %slice.9), channel_id=1, source_target_pairs={{0,8},{8,16},{16,24},{1,9},{9,17},{17,25},{2,10},{10,18},{18,26},{... | collective-permute-start | bytes 36872 | tf_op jit(solution)/shard_map/ppermute | solution.py:58
  7.8 0.6 copy-start.18
  13.3 1.6 %collective-permute-start.1 = (bf16[128,544]{1,0:T(8,128)(2,1)}, bf16[128,544]{1,0:T(8,128)(2,1)S(1)}, u32[]{:S(2)}, u32[]{:S(2)}) collective-permute-start(bf16[128,544]{1,0:T(8,128)(2,1)} %get-tuple-element.102), channel_id=1, source_target_pairs={{0,1},{1,0},{2,3},{3,2},{4,5},{5,4},{6,7},{7,6},{8,9},{9,8},{10,11... | collective-permute-start | bytes 417800 | tf_op jit(solution)/shard_map/ppermute | solution.py:707
  15.8 6.4 %collective-permute-start.2 = (bf16[128,544]{1,0:T(8,128)(2,1)S(1)}, bf16[128,544]{1,0:T(8,128)(2,1)S(1)}, u32[]{:S(2)}, u32[]{:S(2)}) collective-permute-start(bf16[128,544]{1,0:T(8,128)(2,1)S(1)} %add_convert_fusion.3), channel_id=1, source_target_pairs={{0,2},{1,3},{2,0},{3,1},{4,6},{5,7},{6,4},{7,5},{8,10},{9,11},{10,... | collective-permute-start | bytes 417800 | tf_op jit(solution)/shard_map/ppermute | solution.py:707
  17.4 25.6 %collective-permute-start.4 = (bf16[128,2048]{1,0:T(8,128)(2,1)}, bf16[128,2048]{1,0:T(8,128)(2,1)S(1)}, u32[]{:S(2)}, u32[]{:S(2)}) collective-permute-start(bf16[128,2048]{1,0:T(8,128)(2,1)} %get-tuple-element.171.refs_6_.refs_4_), channel_id=1, source_target_pairs={{0,8},{8,0},{16,24},{24,16},{1,9},{9,1},{17,25},{25,17},{2,10},{10... | collective-permute-start | bytes 1572872 | tf_op jit(solution)/shard_map/ppermute | solution.py:707
  19.7 25.8 %collective-permute-start.5 = (bf16[128,2048]{1,0:T(8,128)(2,1)}, bf16[128,2048]{1,0:T(8,128)(2,1)S(1)}, u32[]{:S(2)}, u32[]{:S(2)}) collective-permute-start(bf16[128,2048]{1,0:T(8,128)(2,1)} %get-tuple-element.171.refs_6_.refs_4_), channel_id=1, source_target_pairs={{0,16},{8,24},{16,0},{24,8},{1,17},{9,25},{17,1},{25,9},{2,18},{10... | collective-permute-start | bytes 1572872 | tf_op jit(solution)/shard_map/ppermute | solution.py:707
  22.3 6.2 %copy-start.2 = (bf16[128,544]{1,0:T(8,128)(2,1)}, bf16[128,544]{1,0:T(8,128)(2,1)S(1)}, u32[]{:S(2)}) copy-start(bf16[128,544]{1,0:T(8,128)(2,1)S(1)} %add_convert_fusion.2.refs_0_) | copy-start | bytes 417796
  22.3 5.5 %collective-permute-start.3 = (bf16[128,544]{1,0:T(8,128)(2,1)S(1)}, bf16[128,544]{1,0:T(8,128)(2,1)S(1)}, u32[]{:S(2)}, u32[]{:S(2)}) collective-permute-start(bf16[128,544]{1,0:T(8,128)(2,1)S(1)} %add_convert_fusion.2.refs_0_), channel_id=1, source_target_pairs={{0,4},{1,5},{2,6},{3,7},{4,0},{5,1},{6,2},{7,3},{8,12},{9,13},{10,... | collective-permute-start | bytes 417800 | tf_op jit(solution)/shard_map/ppermute | solution.py:707
  27.8 0.7 copy-start.15
  42.9 27.1 %copy-start.4 = (bf16[128,2048]{1,0:T(8,128)(2,1)}, bf16[128,2048]{1,0:T(8,128)(2,1)S(1)}, u32[]{:S(2)}) copy-start(bf16[128,2048]{1,0:T(8,128)(2,1)S(1)} %collective-permute-done.4.refs_5_) | copy-start | bytes 1572868
  45.5 24.5 %copy-start.5 = (bf16[128,2048]{1,0:T(8,128)(2,1)}, bf16[128,2048]{1,0:T(8,128)(2,1)S(1)}, u32[]{:S(2)}) copy-start(bf16[128,2048]{1,0:T(8,128)(2,1)S(1)} %collective-permute-done.5.refs_6_) | copy-start | bytes 1572868
  45.5 6.2 %collective-permute-start.6 = (bf16[2,18,8,128]{3,2,1,0:T(8,128)(2,1)}, bf16[2,18,8,128]{3,2,1,0:T(8,128)(2,1)S(1)}, u32[]{:S(2)}, u32[]{:S(2)}) collective-permute-start(bf16[2,18,8,128]{3,2,1,0:T(8,128)(2,1)} %get-tuple-element.110), channel_id=1, source_target_pairs={{0,8},{8,0},{16,24},{24,16},{1,9},{9,1},{17,25},{25,17},{2,10},{10... | collective-permute-start | bytes 221192 | tf_op jit(solution)/shard_map/ppermute | solution.py:707
  45.9 6.8 %collective-permute-start.7 = (bf16[2,18,8,128]{3,2,1,0:T(8,128)(2,1)}, bf16[2,18,8,128]{3,2,1,0:T(8,128)(2,1)S(1)}, u32[]{:S(2)}, u32[]{:S(2)}) collective-permute-start(bf16[2,18,8,128]{3,2,1,0:T(8,128)(2,1)} %get-tuple-element.111), channel_id=1, source_target_pairs={{0,16},{8,24},{16,0},{24,8},{1,17},{9,25},{17,1},{25,9},{2,18},{10... | collective-permute-start | bytes 221192 | tf_op jit(solution)/shard_map/ppermute | solution.py:707
  48.6 7.2 %collective-permute-start.8 = (bf16[2,18,8,128]{3,2,1,0:T(8,128)(2,1)}, bf16[2,18,8,128]{3,2,1,0:T(8,128)(2,1)S(1)}, u32[]{:S(2)}, u32[]{:S(2)}) collective-permute-start(bf16[2,18,8,128]{3,2,1,0:T(8,128)(2,1)} %get-tuple-element.112), channel_id=1, source_target_pairs={{0,24},{8,16},{16,8},{24,0},{1,25},{9,17},{17,9},{25,1},{2,26},{10... | collective-permute-start | bytes 221192 | tf_op jit(solution)/shard_map/ppermute | solution.py:707
  51.7 4.1 %copy-start.12 = (bf16[2,18,8,128]{3,2,1,0:T(8,128)(2,1)}, bf16[2,18,8,128]{3,2,1,0:T(8,128)(2,1)S(1)}, u32[]{:S(2)}) copy-start(bf16[2,18,8,128]{3,2,1,0:T(8,128)(2,1)S(1)} %collective-permute-done.6.refs_11_) | copy-start | bytes 221188
  52.8 3.0 %copy-start.13 = (bf16[2,18,8,128]{3,2,1,0:T(8,128)(2,1)}, bf16[2,18,8,128]{3,2,1,0:T(8,128)(2,1)S(1)}, u32[]{:S(2)}) copy-start(bf16[2,18,8,128]{3,2,1,0:T(8,128)(2,1)S(1)} %collective-permute-done.7.refs_12_) | copy-start | bytes 221188
  55.7 0.6 copy-start.14
  55.7 17.5 %collective-permute-start.9 = (bf16[128,2048]{1,0:T(8,128)(2,1)S(1)}, bf16[128,2048]{1,0:T(8,128)(2,1)S(1)}, u32[]{:S(2)}, u32[]{:S(2)}) collective-permute-start(bf16[128,2048]{1,0:T(8,128)(2,1)S(1)} %collective-permute-done.5.refs_6_), channel_id=1, source_target_pairs={{0,8},{8,0},{16,24},{24,16},{1,9},{9,1},{17,25},{25,17},{2,10},{10... | collective-permute-start | bytes 1572872 | tf_op jit(solution)/shard_map/ppermute | solution.py:707
  56.4 14.3 %copy-start.17 = (bf16[128,512]{1,0:T(8,128)(2,1)S(1)}, bf16[128,512]{1,0:T(8,128)(2,1)}, u32[]{:S(2)}) copy-start(bf16[128,512]{1,0:T(8,128)(2,1)} %get-tuple-element.136) | copy-start | bytes 393220
  70.0 17.8 %collective-permute-start.10 = (bf16[144,1024]{1,0:T(8,128)(2,1)}, bf16[144,1024]{1,0:T(8,128)(2,1)S(1)}, u32[]{:S(2)}, u32[]{:S(2)}) collective-permute-start(bf16[144,1024]{1,0:T(8,128)(2,1)} %get-tuple-element.162.refs_2_), channel_id=1, source_target_pairs={{0,16},{8,24},{16,0},{24,8},{1,17},{9,25},{17,1},{25,9},{2,18},{10... | collective-permute-start | bytes 884744 | tf_op jit(solution)/shard_map/ppermute | solution.py:707
  70.8 16.3 %copy-start.1 = (bf16[128,512]{0,1:T(8,128)(2,1)}, bf16[128,512]{0,1:T(8,128)(2,1)S(1)}, u32[]{:S(2)}) copy-start(bf16[128,512]{0,1:T(8,128)(2,1)S(1)} %copy.26) | copy-start | bytes 393220
  70.8 17.0 %collective-permute-start.11 = (bf16[512,128]{1,0:T(8,128)(2,1)S(1)}, bf16[512,128]{1,0:T(8,128)(2,1)S(1)}, u32[]{:S(2)}, u32[]{:S(2)}) collective-permute-start(bf16[512,128]{1,0:T(8,128)(2,1)S(1)} %bitcast.17), channel_id=1, source_target_pairs={{0,16},{8,24},{16,0},{24,8},{1,17},{9,25},{17,1},{25,9},{2,18},{10... | collective-permute-start | bytes 393224 | tf_op jit(solution)/shard_map/ppermute | solution.py:707
  73.2 13.8 %copy-start.6 = (bf16[128,2048]{1,0:T(8,128)(2,1)}, bf16[128,2048]{1,0:T(8,128)(2,1)S(1)}, u32[]{:S(2)}) copy-start(bf16[128,2048]{1,0:T(8,128)(2,1)S(1)} %collective-permute-done.9.refs_7_) | copy-start | bytes 1572868
  87.8 10.6 %copy-start.7 = (bf16[512,128]{1,0:T(8,128)(2,1)}, bf16[512,128]{1,0:T(8,128)(2,1)S(1)}, u32[]{:S(2)}) copy-start(bf16[512,128]{1,0:T(8,128)(2,1)S(1)} %collective-permute-done.11.refs_1_) | copy-start | bytes 393220
  87.8 10.6 %copy-start.8 = (bf16[144,1024]{1,0:T(8,128)(2,1)}, bf16[144,1024]{1,0:T(8,128)(2,1)S(1)}, u32[]{:S(2)}) copy-start(bf16[144,1024]{1,0:T(8,128)(2,1)S(1)} %collective-permute-done.10.refs_3_) | copy-start | bytes 884740
  87.8 1.7 %collective-permute-start.12 = (bf16[640,128]{1,0:T(8,128)(2,1)}, bf16[640,128]{1,0:T(8,128)(2,1)S(1)}, u32[]{:S(2)}, u32[]{:S(2)}) collective-permute-start(bf16[640,128]{1,0:T(8,128)(2,1)} %get-tuple-element.137), channel_id=1, source_target_pairs={{0,1},{1,0},{2,3},{3,2},{4,5},{5,4},{6,7},{7,6},{8,9},{9,8},{10,11... | collective-permute-start | bytes 491528 | tf_op jit(solution)/shard_map/ppermute | solution.py:707
  90.4 6.3 %collective-permute-start.13 = (bf16[640,128]{1,0:T(8,128)(2,1)S(1)}, bf16[640,128]{1,0:T(8,128)(2,1)S(1)}, u32[]{:S(2)}, u32[]{:S(2)}) collective-permute-start(bf16[640,128]{1,0:T(8,128)(2,1)S(1)} %add_convert_fusion.1), channel_id=1, source_target_pairs={{0,2},{1,3},{2,0},{3,1},{4,6},{5,7},{6,4},{7,5},{8,10},{9,11},{10,... | collective-permute-start | bytes 491528 | tf_op jit(solution)/shard_map/ppermute | solution.py:707
  91.0 16.3 %collective-permute-start.15 = (bf16[144,1024]{1,0:T(8,128)(2,1)}, bf16[144,1024]{1,0:T(8,128)(2,1)S(1)}, u32[]{:S(2)}, u32[]{:S(2)}) collective-permute-start(bf16[144,1024]{1,0:T(8,128)(2,1)} %get-tuple-element.149.refs_2_), channel_id=1, source_target_pairs={{0,16},{8,24},{16,0},{24,8},{1,17},{9,25},{17,1},{25,9},{2,18},{10... | collective-permute-start | bytes 884744 | tf_op jit(solution)/shard_map/ppermute | solution.py:707
  96.8 5.5 %copy-start = (bf16[640,128]{1,0:T(8,128)(2,1)}, bf16[640,128]{1,0:T(8,128)(2,1)S(1)}, u32[]{:S(2)}) copy-start(bf16[640,128]{1,0:T(8,128)(2,1)S(1)} %add_convert_fusion.back_a) | copy-start | bytes 491524
  96.8 5.5 %collective-permute-start.14 = (bf16[640,128]{1,0:T(8,128)(2,1)S(1)}, bf16[640,128]{1,0:T(8,128)(2,1)S(1)}, u32[]{:S(2)}, u32[]{:S(2)}) collective-permute-start(bf16[640,128]{1,0:T(8,128)(2,1)S(1)} %add_convert_fusion.back_a), channel_id=1, source_target_pairs={{0,4},{1,5},{2,6},{3,7},{4,0},{5,1},{6,2},{7,3},{8,12},{9,13},{10,... | collective-permute-start | bytes 491528 | tf_op jit(solution)/shard_map/ppermute | solution.py:707
  100.9 21.7 %collective-permute-start.19 = (bf16[144,1024]{1,0:T(8,128)(2,1)}, bf16[144,1024]{1,0:T(8,128)(2,1)S(1)}, u32[]{:S(2)}, u32[]{:S(2)}) collective-permute-start(bf16[144,1024]{1,0:T(8,128)(2,1)} %get-tuple-element.165), channel_id=1, source_target_pairs={{0,8},{8,0},{16,24},{24,16},{1,9},{9,1},{17,25},{25,17},{2,10},{10... | collective-permute-start | bytes 884744 | tf_op jit(solution)/shard_map/ppermute | solution.py:707
  102.3 0.7 copy-start.3
  107.3 0.7 copy-start.9
  110.5 15.9 %collective-permute-start.23 = (bf16[144,1024]{1,0:T(8,128)(2,1)}, bf16[144,1024]{1,0:T(8,128)(2,1)S(1)}, u32[]{:S(2)}, u32[]{:S(2)}) collective-permute-start(bf16[144,1024]{1,0:T(8,128)(2,1)} %get-tuple-element.178), channel_id=1, source_target_pairs={{0,8},{8,0},{16,24},{24,16},{1,9},{9,1},{17,25},{25,17},{2,10},{10... | collective-permute-start | bytes 884744 | tf_op jit(solution)/shard_map/ppermute | solution.py:707
  110.5 12.0 %collective-permute-start.16 = (bf16[160,128]{1,0:T(8,128)(2,1)}, bf16[160,128]{1,0:T(8,128)(2,1)S(1)}, u32[]{:S(2)}, u32[]{:S(2)}) collective-permute-start(bf16[160,128]{1,0:T(8,128)(2,1)} %get-tuple-element.159), channel_id=1, source_target_pairs={{0,8},{8,0},{16,24},{24,16},{1,9},{9,1},{17,25},{25,17},{2,10},{10... | collective-permute-start | bytes 122888 | tf_op jit(solution)/shard_map/ppermute | solution.py:707
  112.6 10.0 %collective-permute-start.17 = (bf16[160,128]{1,0:T(8,128)(2,1)}, bf16[160,128]{1,0:T(8,128)(2,1)S(1)}, u32[]{:S(2)}, u32[]{:S(2)}) collective-permute-start(bf16[160,128]{1,0:T(8,128)(2,1)} %get-tuple-element.160), channel_id=1, source_target_pairs={{0,16},{8,24},{16,0},{24,8},{1,17},{9,25},{17,1},{25,9},{2,18},{10... | collective-permute-start | bytes 122888 | tf_op jit(solution)/shard_map/ppermute | solution.py:707
  112.6 10.0 %collective-permute-start.18 = (bf16[160,128]{1,0:T(8,128)(2,1)}, bf16[160,128]{1,0:T(8,128)(2,1)S(1)}, u32[]{:S(2)}, u32[]{:S(2)}) collective-permute-start(bf16[160,128]{1,0:T(8,128)(2,1)} %get-tuple-element.161), channel_id=1, source_target_pairs={{0,24},{8,16},{16,8},{24,0},{1,25},{9,17},{17,9},{25,1},{2,26},{10... | collective-permute-start | bytes 122888 | tf_op jit(solution)/shard_map/ppermute | solution.py:707
  122.5 3.9 %copy-start.22 = (bf16[160,128]{1,0:T(8,128)(2,1)}, bf16[160,128]{1,0:T(8,128)(2,1)S(1)}, u32[]{:S(2)}) copy-start(bf16[160,128]{1,0:T(8,128)(2,1)S(1)} %collective-permute-done.16.refs_1_) | copy-start | bytes 122884
  122.5 3.9 %copy-start.23 = (bf16[160,128]{1,0:T(8,128)(2,1)}, bf16[160,128]{1,0:T(8,128)(2,1)S(1)}, u32[]{:S(2)}) copy-start(bf16[160,128]{1,0:T(8,128)(2,1)S(1)} %collective-permute-done.17.refs_2_) | copy-start | bytes 122884
  122.5 3.9 %copy-start.24 = (bf16[160,128]{1,0:T(8,128)(2,1)}, bf16[160,128]{1,0:T(8,128)(2,1)S(1)}, u32[]{:S(2)}) copy-start(bf16[160,128]{1,0:T(8,128)(2,1)S(1)} %collective-permute-done.18.refs_3_) | copy-start | bytes 122884
  122.6 3.9 %copy-start.10 = (bf16[144,1024]{1,0:T(8,128)(2,1)}, bf16[144,1024]{1,0:T(8,128)(2,1)S(1)}, u32[]{:S(2)}) copy-start(bf16[144,1024]{1,0:T(8,128)(2,1)S(1)} %collective-permute-done.19.refs_9_) | copy-start | bytes 884740
  122.6 8.6 %collective-permute-start.20 = (bf16[16,2048]{1,0:T(8,128)(2,1)}, bf16[16,2048]{1,0:T(8,128)(2,1)S(1)}, u32[]{:S(2)}, u32[]{:S(2)}) collective-permute-start(bf16[16,2048]{1,0:T(8,128)(2,1)} %get-tuple-element.180.refs_3_), channel_id=1, source_target_pairs={{0,8},{8,16},{16,24},{24,0},{1,9},{9,17},{17,25},{25,1},{2,10},{10... | collective-permute-start | bytes 196616 | tf_op jit(solution)/shard_map/ppermute | solution.py:52
  122.9 8.2 %collective-permute-start.21 = (bf16[16,2048]{1,0:T(8,128)(2,1)}, bf16[16,2048]{1,0:T(8,128)(2,1)S(1)}, u32[]{:S(2)}, u32[]{:S(2)}) collective-permute-start(bf16[16,2048]{1,0:T(8,128)(2,1)} %get-tuple-element.180.refs_3_), channel_id=1, source_target_pairs={{0,16},{8,24},{16,0},{24,8},{1,17},{9,25},{17,1},{25,9},{2,18},{10... | collective-permute-start | bytes 196616 | tf_op jit(solution)/shard_map/ppermute | solution.py:52
  124.8 6.4 %collective-permute-start.22 = (bf16[16,2048]{1,0:T(8,128)(2,1)}, bf16[16,2048]{1,0:T(8,128)(2,1)S(1)}, u32[]{:S(2)}, u32[]{:S(2)}) collective-permute-start(bf16[16,2048]{1,0:T(8,128)(2,1)} %get-tuple-element.180.refs_3_), channel_id=1, source_target_pairs={{0,24},{8,0},{16,8},{24,16},{1,25},{9,1},{17,9},{25,17},{2,26},{10... | collective-permute-start | bytes 196616 | tf_op jit(solution)/shard_map/ppermute | solution.py:52
  126.4 0.7 copy-start.11
  131.2 0.6 copy-start.19
  131.2 0.6 copy-start.20
  131.2 0.6 copy-start.21

commit v11 on v10

--- a/solution.py
+++ b/solution.py
@@ -11,7 +11,7 @@
 F32 = jnp.float32
 LOG2E = 1.4426950408889634
 LN2 = 0.6931471805599453
-VMEM_BYTES = 56 * 1024 * 1024
+MIB = 1024 * 1024
 NT = (((1,), (1,)), ((), ()))
 TN = (((0,), (0,)), ((), ()))
 
@@ -27,8 +27,8 @@
     return lax.dot_general(a, b, dims, preferred_element_type=F32)
 
 
-def params(**more):
-    return pltpu.CompilerParams(vmem_limit_bytes=VMEM_BYTES, **more)
+def params(mebibytes):
+    return pltpu.CompilerParams(vmem_limit_bytes=mebibytes * MIB)
 
 
 def sds(shape, dtype):
@@ -99,7 +99,7 @@
     rows, chans = conv_input.shape
     taps = weight.shape[0]
     wide = proj_weight.shape[0]
-    width = min(512, chans)
+    width = min(1024, chans)
     return pl.pallas_call(
         conv_kernel,
         grid=(chans // width,),
@@ -113,7 +113,7 @@
         out_specs=[columns(rows, width), whole((rows, wide))],
         out_shape=[sds((rows, chans), BF), sds((rows, wide), BF)],
         scratch_shapes=[pltpu.VMEM((rows + 8, width), F32), pltpu.VMEM((rows, wide), F32)],
-        compiler_params=params(),
+        compiler_params=params(16),
         name="conv_project",
     )(conv_input, rim, weight, bias, proj_weight)
 
@@ -260,7 +260,7 @@
             pltpu.VMEM(message, F32),
             pltpu.VMEM(message, F32),
         ],
-        compiler_params=params(),
+        compiler_params=params(26),
         name="local_ends",
     )(*parts, coef, step_weight, step_bias, decay, conv_out, gate, grad)
 
@@ -497,7 +497,7 @@
             pltpu.VMEM((rows, states, groups, 128), F32),
         ],
         input_output_aliases=aliases,
-        compiler_params=params(),
+        compiler_params=params(38),
         name="scan_gradients",
     )(
         coef, *dense, decay, skips, conv_out, gate, grad, step_weight, skip, *messages, *previous
@@ -505,17 +505,23 @@
 
 
 def conv_grad_kernel(places, low_rank, back_a, back_b, proj_ref, scan_ref, small_in, input_ref, rim_ref, weight_ref, bias_ref,
-                     out_ref, tail_ref, small_ref, ext, grad):
+                     out_ref, tail_ref, small_ref, ext, grad, back_t):
     taps = weight_ref.shape[0]
     rows = input_ref.shape[0]
     fill_extended(ext, rim_ref, input_ref, taps)
     wide = proj_ref.shape[0]
     block = back_a.shape[0] // places
     ranks, coef_rows = low_rank // places, (wide - low_rank) // places
-    back = (back_a[...].astype(F32) + back_b[...].astype(F32)).astype(BF).astype(F32)
-    order = [back[q * block : q * block + ranks, :] for q in range(places)]
-    order += [back[q * block + ranks : q * block + ranks + coef_rows, :] for q in range(places)]
-    d_xc = dot(jnp.concatenate(order, axis=0).astype(BF), proj_ref[...], TN)
+
+    @pl.when(pl.program_id(0) == 0)
+    def _():
+        back = back_a[...].astype(F32) + back_b[...].astype(F32)
+        order = [back[q * block : q * block + ranks, :] for q in range(places)]
+        order += [back[q * block + ranks : q * block + ranks + coef_rows, :] for q in range(places)]
+        order += [jnp.zeros((padded(wide) - wide, back.shape[1]), F32)]
+        back_t[...] = jnp.transpose(jnp.concatenate(order, axis=0))[:, :wide].astype(BF)
+
+    d_xc = dot(back_t[...], proj_ref[...])
     sums = [jnp.zeros((1, input_ref.shape[1]), F32) for _ in range(taps + 1)]
     for start in range(0, rows, 16):
         here = slice(start, start + 16)
@@ -544,7 +550,7 @@
     rows, chans = conv_input.shape
     taps = weight.shape[0]
     wide = proj_weight.shape[0]
-    width = min(512, chans)
+    width = min(1024, chans)
     return pl.pallas_call(
         functools.partial(conv_grad_kernel, places, low_rank),
         grid=(chans // width,),
@@ -561,8 +567,12 @@
         ],
         out_specs=[columns(rows, width), columns(16, width), columns(16, width)],
         out_shape=[sds((rows, chans), BF), sds((16, chans), F32), sds((16, chans), BF)],
-        scratch_shapes=[pltpu.VMEM((rows + 8, width), F32), pltpu.VMEM((rows + 8, width), F32)],
-        compiler_params=params(),
+        scratch_shapes=[
+            pltpu.VMEM((rows + 8, width), F32),
+            pltpu.VMEM((rows + 8, width), F32),
+            pltpu.VMEM((rows, wide), BF),
+        ],
+        compiler_params=params(18),
         name="conv_gradients",
     )(*backs, proj_weight, scan_part, small, conv_input, rim, weight, bias)
 
@@ -582,7 +592,7 @@
         functools.partial(cut_kernel, places),
         out_shape=[sds((wide // places, rows), BF)] * places,
         scratch_shapes=[pltpu.VMEM((wide, rows), F32)],
-        compiler_params=params(),
+        compiler_params=params(8),
         name="cut_rows",
     )(*backs)
 
@@ -615,7 +625,7 @@
         in_specs=[whole(lows[0].shape)] * len(lows) + [columns(tall, width)] * len(steps),
         out_specs=[columns(height, width)] * 2,
         out_shape=[sds((height, chans), F32), sds((height, chans), BF)],
-        compiler_params=params(),
+        compiler_params=params(16),
         name="step_products",
     )(*lows, *steps)
 
@@ -649,7 +659,7 @@
         + [whole((height, width))] * len(products),
         out_specs=[columns(height, width) for height in heights],
         out_shape=[sds((height, chans), F32) for height in heights],
-        compiler_params=params(),
+        compiler_params=params(20),
         name="row_gradients",
     )(*cuts, *blocks, *products)
 
@@ -694,7 +704,7 @@
         out_shape=[sds((rows, chans), BF), sds((taps, chans), F32)] + [sds((1, chans), F32)] * 3,
         scratch_shapes=[pltpu.VMEM((16, chans), F32)],
         input_output_aliases={0: 0},
-        compiler_params=params(),
+        compiler_params=params(8),
         name="last_rows",
     )(main, tail, weight, *late)
 
@@ -769,7 +779,6 @@
     dt, dx, g, low, *messages = local_call(
         parts, coef, step_weight, step_bias, decay, conv_out, gate_input, out_grad, states, places
     )
-    messages, blocks = tie((messages, blocks))
     messages = [swap(message, "ctx", mask) for mask, message in enumerate(messages, 1)]
     messages, blocks, low = tie((messages, blocks, low))
     blocks = spread_on(blocks)

time: 134 us -> 138 us (1.030)
  local copies, waits for them, and re-layouts: 6.26 us -> 23.6 us
  Pallas kernels: 63.1 us -> 47.4 us
  starting transfers between devices: 31.7 us -> 37.6 us
  waiting for transfers between devices: 29.5 us -> 27.1 us
  other arithmetic: 2.02 us -> 0.19 us
    unnamed x51 -> x83, local copies, waits for them, and re-layouts: 3.99 us -> 21.8 us
    ppermute x20, starting transfers between devices: 22.9 us -> 27.7 us  [swap(): lax.ppermute(block, axis, [(i, i ^ mask) for i in range(lax.axis_size(axi...]
    ppermute x20, waiting for transfers between devices: 28.1 us -> 24.3 us  [swap(): lax.ppermute(block, axis, [(i, i ^ mask) for i in range(lax.axis_size(axi...]
    pallas_call x2, Pallas kernels: 27.5 us -> 24.1 us  [scan_call(): pl.pallas_call(functools.partial(scan_kernel, places, states, first), gri...]
    pallas_call x2, Pallas kernels: 4.96 us -> 2.36 us  [step_call(): pl.pallas_call(functools.partial(step_kernel, ranks, len(lows)), grid=(ch...]
    pallas_call x1, Pallas kernels: 4.82 us -> 2.25 us  [conv_call(): pl.pallas_call(conv_kernel, grid=(chans // width,), in_specs=[columns(row...]
    pallas_call x1, Pallas kernels: 11.7 us -> 9.57 us  [local_call(): pl.pallas_call(functools.partial(local_kernel, low_rank, states, places),...]
    convert_element_type x4, other arithmetic: 2.02 us -> 0.18 us  [chan_sum(): part = (part.astype(F32) + other.astype(F32)).astype(BF)]
  transfers between devices with their start and end apart: 24 -> 24, of which waited for: 14 -> 13; matrix products, arithmetic and copies ran while one was open for 1% -> 1% of each run, Pallas kernels for 42% -> 32%
where the time goes in v11:
time: 138 us; the launch traced here: 137 us
  Pallas kernels  47.4 us (34%)
  starting transfers between devices  37.6 us (27%)
  waiting for transfers between devices  27.1 us (20%)
  local copies, waits for them, and re-layouts  23.6 us (17%)
    ppermute x20, starting transfers between devices, swap(): lax.ppermute(block, axis, [(i, i ^ mask) for i in range(lax.axis_size(axi...  27.7 us
    ppermute x20, waiting for transfers between devices, swap(): lax.ppermute(block, axis, [(i, i ^ mask) for i in range(lax.axis_size(axi...  24.3 us
    pallas_call x2, Pallas kernels, scan_call(): pl.pallas_call(functools.partial(scan_kernel, places, states, first), gri...  24.1 us
    unnamed x83, local copies, waits for them, and re-layouts  21.8 us
    pallas_call x1, Pallas kernels, local_call(): pl.pallas_call(functools.partial(local_kernel, low_rank, states, places),...  9.57 us
    pallas_call x1, Pallas kernels, conv_grad_call(): pl.pallas_call(functools.partial(conv_grad_kernel, places, low_rank), gri...  5.09 us
    ppermute x1, starting transfers between devices, shift(): return lax.ppermute(block, axis, route)  4.93 us
    ppermute x3, starting transfers between devices, rotate(): lax.ppermute(block, axis, [(i, (i + distance) % count) for i in range(cou...  4.9 us
  transfers between devices with their start and end apart: 24, of which 13 were waited for; matrix products, arithmetic and copies ran while one was open for 1% of the time, Pallas kernels for 32%

profile of v11, /device:TPU:0, one launch (start us, length us, event | category | flops | bytes accessed | tf_op | source)
XLA Modules:
  0.0 136.9 jit_solution(7143355005468408273)
XLA Ops:
  0.6 0.8 slice.9
  1.4 4.9 %collective-permute-start = (bf16[3,2048]{1,0:T(4,128)(2,1)S(1)}, bf16[3,2048]{1,0:T(4,128)(2,1)S(1)}, u32[]{:S(2)}, u32[]{:S(2)}) collective-permute-start(bf16[3,2048]{1,0:T(4,128)(2,1)S(1)} %slice.9), channel_id=1, source_target_pairs={{0,8},{8,16},{16,24},{1,9},{9,17},{17,25},{2,10},{10,18},{18,26},{... | collective-permute-start | bytes 36872 | tf_op jit(solution)/shard_map/ppermute | solution.py:58
  6.4 1.4 %collective-permute-done.rim_ref = bf16[3,2048]{1,0:T(4,128)(2,1)S(1)} collective-permute-done((bf16[3,2048]{1,0:T(4,128)(2,1)S(1)}, bf16[3,2048]{1,0:T(4,128)(2,1)S(1)}, u32[]{:S(2)}, u32[]{:S(2)}) %collective-permute-start) | collective-permute-done | bytes 12320 | tf_op jit(solution)/shard_map/ppermute | solution.py:58
  7.8 1.6 %copy-done.1 = bf16[544,2048]{1,0:T(8,128)(2,1)S(1)} copy-done((bf16[544,2048]{1,0:T(8,128)(2,1)S(1)}, bf16[544,2048]{1,0:T(8,128)(2,1)}, u32[]{:S(2)}) %copy-start.1) | copy-done | bytes 2228248
  9.4 1.0 copy-done.13
  10.5 0.8 copy-done.19
  11.2 0.7 copy-done.37
  11.9 2.3 %conv_project.1 = (bf16[128,2048]{1,0:T(8,128)(2,1)S(1)}, bf16[128,544]{1,0:T(8,128)(2,1)S(1)}) custom-call(bf16[128,2048]{1,0:T(8,128)(2,1)S(1)} %copy-done.13, bf16[3,2048]{1,0:T(4,128)(2,1)S(1)} %collective-permute-done.rim_ref, f32[4,2048]{1,0:T(4,128)S(1)} %copy-done.19, f32[1,2048]{1,0:T(1,128)S(1)} %bitcast.24, bf16[544,2048]{1,0:T(8,128)(2,1)S(1)} %copy-done.1), custom_call_target="tpu_custom_call" | custom-call | tf_op jit(solution)/shard_map/conv_project/pallas_call | solution.py:103
  14.3 1.4 %collective-permute-done.1 = bf16[128,544]{1,0:T(8,128)(2,1)S(1)} collective-permute-done((bf16[128,544]{1,0:T(8,128)(2,1)S(1)}, bf16[128,544]{1,0:T(8,128)(2,1)S(1)}, u32[]{:S(2)}, u32[]{:S(2)}) %collective-permute-start.1) | collective-permute-done | bytes 139296 | tf_op jit(solution)/shard_map/ppermute | solution.py:717
  15.7 1.6 %collective-permute-start.2 = (bf16[128,544]{1,0:T(8,128)(2,1)S(1)}, bf16[128,544]{1,0:T(8,128)(2,1)S(1)}, u32[]{:S(2)}, u32[]{:S(2)}) collective-permute-start(bf16[128,544]{1,0:T(8,128)(2,1)S(1)} %add_convert_fusion.3), channel_id=1, source_target_pairs={{0,2},{1,3},{2,0},{3,1},{4,6},{5,7},{6,4},{7,5},{8,10},{9,11},{10,... | collective-permute-start | bytes 417800 | tf_op jit(solution)/shard_map/ppermute | solution.py:717
  17.2 2.3 %collective-permute-start.7 = (bf16[128,2048]{1,0:T(8,128)(2,1)S(1)}, bf16[128,2048]{1,0:T(8,128)(2,1)}, u32[]{:S(2)}, u32[]{:S(2)}) collective-permute-start(bf16[128,2048]{1,0:T(8,128)(2,1)S(1)} %get-tuple-element.159.refs_6_.refs_4_), channel_id=1, source_target_pairs={{0,8},{8,0},{16,24},{24,16},{1,9},{9,1},{17,25},{25,17},{2,10},{10... | collective-permute-start | bytes 1572872 | tf_op jit(solution)/shard_map/ppermute | solution.py:717
  19.5 2.6 %collective-permute-start.8 = (bf16[128,2048]{1,0:T(8,128)(2,1)S(1)}, bf16[128,2048]{1,0:T(8,128)(2,1)}, u32[]{:S(2)}, u32[]{:S(2)}) collective-permute-start(bf16[128,2048]{1,0:T(8,128)(2,1)S(1)} %get-tuple-element.159.refs_6_.refs_4_), channel_id=1, source_target_pairs={{0,16},{8,24},{16,0},{24,8},{1,17},{9,25},{17,1},{25,9},{2,18},{10... | collective-permute-start | bytes 1572872 | tf_op jit(solution)/shard_map/ppermute | solution.py:717
  22.2 1.6 %collective-permute-start.3 = (bf16[128,544]{1,0:T(8,128)(2,1)S(1)}, bf16[128,544]{1,0:T(8,128)(2,1)S(1)}, u32[]{:S(2)}, u32[]{:S(2)}) collective-permute-start(bf16[128,544]{1,0:T(8,128)(2,1)S(1)} %add_convert_fusion.2.refs_0_), channel_id=1, source_target_pairs={{0,4},{1,5},{2,6},{3,7},{4,0},{5,1},{6,2},{7,3},{8,12},{9,13},{10,... | collective-permute-start | bytes 417800 | tf_op jit(solution)/shard_map/ppermute | solution.py:717
  23.8 3.8 %collective-permute-done.3.refs_1_ = bf16[128,544]{1,0:T(8,128)(2,1)S(1)} collective-permute-done((bf16[128,544]{1,0:T(8,128)(2,1)S(1)}, bf16[128,544]{1,0:T(8,128)(2,1)S(1)}, u32[]{:S(2)}, u32[]{:S(2)}) %collective-permute-start.3) | collective-permute-done | bytes 139296 | tf_op jit(solution)/shard_map/ppermute | solution.py:717
  27.7 0.7 copy-done.30
  28.5 1.0 copy-done.4
  29.5 0.9 copy-done.31
  30.4 9.6 %local_ends.1 = (f32[2,128,8,128]{3,2,1,0:T(8,128)S(1)}, f32[2,128,8,128]{3,2,1,0:T(8,128)S(1)}, f32[2,128,8,128]{3,2,1,0:T(8,128)S(1)}, bf16[128,512]{1,0:T(8,1...) custom-call(bf16[128,544]{1,0:T(8,128)(2,1)S(1)} %add_convert_fusion, ...), custom_call_target="tpu_custom_call" | custom-call | tf_op jit(solution)/shard_map/local_ends/pallas_call | solution.py:231
  40.0 0.6 copy-done.32
  40.7 2.3 %collective-permute-start.4 = (bf16[2,18,8,128]{3,2,1,0:T(8,128)(2,1)S(1)}, bf16[2,18,8,128]{3,2,1,0:T(8,128)(2,1)S(1)}, u32[]{:S(2)}, u32[]{:S(2)}) collective-permute-start(bf16[2,18,8,128]{3,2,1,0:T(8,128)(2,1)S(1)} %get-tuple-element.101), channel_id=1, source_target_pairs={{0,8},{8,0},{16,24},{24,16},{1,9},{9,1},{17,25},{25,17},{2,10},{10... | collective-permute-start | bytes 221192 | tf_op jit(solution)/shard_map/ppermute | solution.py:717
  43.0 2.6 %collective-permute-start.5 = (bf16[2,18,8,128]{3,2,1,0:T(8,128)(2,1)S(1)}, bf16[2,18,8,128]{3,2,1,0:T(8,128)(2,1)S(1)}, u32[]{:S(2)}, u32[]{:S(2)}) collective-permute-start(bf16[2,18,8,128]{3,2,1,0:T(8,128)(2,1)S(1)} %get-tuple-element.102), channel_id=1, source_target_pairs={{0,16},{8,24},{16,0},{24,8},{1,17},{9,25},{17,1},{25,9},{2,18},{10... | collective-permute-start | bytes 221192 | tf_op jit(solution)/shard_map/ppermute | solution.py:717
  45.5 0.6 collective-permute-done.4.refs_11_
  46.1 3.8 %collective-permute-done.5.refs_12_ = bf16[2,18,8,128]{3,2,1,0:T(8,128)(2,1)S(1)} collective-permute-done((bf16[2,18,8,128]{3,2,1,0:T(8,128)(2,1)S(1)}, bf16[2,18,8,128]{3,2,1,0:T(8,128)(2,1)S(1)}, u32[]{:S(2)}, u32[]{:S(2)}) %collective-permute-start.5) | collective-permute-done | bytes 73760 | tf_op jit(solution)/shard_map/ppermute | solution.py:717
  49.9 1.8 %collective-permute-done.6.refs_13_ = bf16[2,18,8,128]{3,2,1,0:T(8,128)(2,1)S(1)} collective-permute-done((bf16[2,18,8,128]{3,2,1,0:T(8,128)(2,1)S(1)}, bf16[2,18,8,128]{3,2,1,0:T(8,128)(2,1)S(1)}, u32[]{:S(2)}, u32[]{:S(2)}) %collective-permute-start.6) | collective-permute-done | bytes 73760 | tf_op jit(solution)/shard_map/ppermute | solution.py:717
  51.8 0.7 copy-done.28
  52.5 0.7 copy-done.33
  53.2 12.2 %scan_gradients.2 = (bf16[144,1024]{1,0:T(8,128)(2,1)}, bf16[128,2048]{1,0:T(8,128)(2,1)}, bf16[128,2048]{1,0:T(8,128)(2,1)S(1)}, f32[8,2048]{1,0:T(8,128)S(1)}, f32[640,128]{1,0:T(8,128)S(1)}) custom-call(f32[4096]{0:T(1024)S(1)} %copy-done.28, f32[2,128,8,128]{3,2,1,0:T(8,128)S(1)} %get-tuple-element.98.refs_1_, ...), custom_call_target="tpu_custom_call" | custom-call | tf_op jit(solution)/shard_map/scan_gradients/pallas_call | solution.py:467
  65.4 0.8 copy-done.15
  66.2 0.7 copy-done.17
  67.0 0.6 copy-done.23
  67.6 2.0 %collective-permute-start.10 = (bf16[144,1024]{1,0:T(8,128)(2,1)}, bf16[144,1024]{1,0:T(8,128)(2,1)}, u32[]{:S(2)}, u32[]{:S(2)}) collective-permute-start(bf16[144,1024]{1,0:T(8,128)(2,1)} %get-tuple-element.150.refs_2_), channel_id=1, source_target_pairs={{0,16},{8,24},{16,0},{24,8},{1,17},{9,25},{17,1},{25,9},{2,18},{10... | collective-permute-start | bytes 884744 | tf_op jit(solution)/shard_map/ppermute | solution.py:717
  69.6 1.0 copy.26
  70.7 1.0 collective-permute-start.11
  71.6 1.0 copy-done.6
  72.7 1.2 copy-done.8
  73.9 1.2 copy-done.10
  75.1 1.2 copy-done.12
  76.3 1.0 copy-done.16
  77.4 1.0 copy-done.18
  78.3 0.9 copy-done.22
  79.2 0.8 copy-done.24
  80.1 0.7 copy-done.29
  80.8 0.7 copy-done.34
  81.5 11.9 %scan_gradients.3 = (bf16[144,1024]{1,0:T(8,128)(2,1)S(1)}, bf16[128,2048]{1,0:T(8,128)(2,1)}, bf16[128,2048]{1,0:T(8,128)(2,1)S(1)}, f32[8,2048]{1,0:T(8,128)S(1)}, bf16[640,128]{1,0:T(8,128)(2,1)S(1)}) custom-call(f32[4096]{0:T(1024)S(1)} %copy-done.29, ...), custom_call_target="tpu_custom_call", output_to_operand_aliasing={{1}: (15, {}), {2}: (16, {}), {3}: (17, {})} | custom-call | tf_op jit(solution)/shard_map/scan_gradients/pallas_call | solution.py:467
  93.6 1.4 %collective-permute-done.12 = bf16[640,128]{1,0:T(8,128)(2,1)S(1)} collective-permute-done((bf16[640,128]{1,0:T(8,128)(2,1)S(1)}, bf16[640,128]{1,0:T(8,128)(2,1)S(1)}, u32[]{:S(2)}, u32[]{:S(2)}) %collective-permute-start.12) | collective-permute-done | bytes 163872 | tf_op jit(solution)/shard_map/ppermute | solution.py:717
  95.0 1.7 %collective-permute-start.13 = (bf16[640,128]{1,0:T(8,128)(2,1)S(1)}, bf16[640,128]{1,0:T(8,128)(2,1)S(1)}, u32[]{:S(2)}, u32[]{:S(2)}) collective-permute-start(bf16[640,128]{1,0:T(8,128)(2,1)S(1)} %add_convert_fusion.1), channel_id=1, source_target_pairs={{0,2},{1,3},{2,0},{3,1},{4,6},{5,7},{6,4},{7,5},{8,10},{9,11},{10,... | collective-permute-start | bytes 491528 | tf_op jit(solution)/shard_map/ppermute | solution.py:717
  96.7 1.7 %collective-permute-start.15 = (bf16[144,1024]{1,0:T(8,128)(2,1)S(1)}, bf16[144,1024]{1,0:T(8,128)(2,1)S(1)}, u32[]{:S(2)}, u32[]{:S(2)}) collective-permute-start(bf16[144,1024]{1,0:T(8,128)(2,1)S(1)} %get-tuple-element.137.refs_2_), channel_id=1, source_target_pairs={{0,16},{8,24},{16,0},{24,8},{1,17},{9,25},{17,1},{25,9},{2,18},{10... | collective-permute-start | bytes 884744 | tf_op jit(solution)/shard_map/ppermute | solution.py:717
  98.4 2.9 %collective-permute-done.13 = bf16[640,128]{1,0:T(8,128)(2,1)S(1)} collective-permute-done((bf16[640,128]{1,0:T(8,128)(2,1)S(1)}, bf16[640,128]{1,0:T(8,128)(2,1)S(1)}, u32[]{:S(2)}, u32[]{:S(2)}) %collective-permute-start.13) | collective-permute-done | bytes 163872 | tf_op jit(solution)/shard_map/ppermute | solution.py:717
  101.3 1.6 %collective-permute-start.14 = (bf16[640,128]{1,0:T(8,128)(2,1)S(1)}, bf16[640,128]{1,0:T(8,128)(2,1)S(1)}, u32[]{:S(2)}, u32[]{:S(2)}) collective-permute-start(bf16[640,128]{1,0:T(8,128)(2,1)S(1)} %add_convert_fusion.back_a), channel_id=1, source_target_pairs={{0,4},{1,5},{2,6},{3,7},{4,0},{5,1},{6,2},{7,3},{8,12},{9,13},{10,... | collective-permute-start | bytes 491528 | tf_op jit(solution)/shard_map/ppermute | solution.py:717
  102.9 1.6 %step_products.3 = (f32[144,1024]{1,0:T(8,128)S(1)}, bf16[144,1024]{1,0:T(8,128)(2,1)S(1)}) custom-call(bf16[512,128]{1,0:T(8,128)(2,1)S(1)} %bitcast.18, bf16[512,128]{1,0:T(8,128)(2,1)S(1)} %collective-permute-done.11.refs_1_, bf16[144,1024]{1,0:T(8,128)(2,1)} %get-tuple-element.150.refs_2_, bf16[144,1024]{1,0:T(8,128)(2,1)} %collective-permute-done.10.refs_3_), custom_call_target="tpu_custom_call" | custom-call | tf_op jit(solution)/shard_map/step_products/pallas_call | solution.py:622
  104.6 2.1 %collective-permute-start.19 = (bf16[144,1024]{1,0:T(8,128)(2,1)S(1)}, bf16[144,1024]{1,0:T(8,128)(2,1)S(1)}, u32[]{:S(2)}, u32[]{:S(2)}) collective-permute-start(bf16[144,1024]{1,0:T(8,128)(2,1)S(1)} %get-tuple-element.153), channel_id=1, source_target_pairs={{0,8},{8,0},{16,24},{24,16},{1,9},{9,1},{17,25},{25,17},{2,10},{10... | collective-permute-start | bytes 884744 | tf_op jit(solution)/shard_map/ppermute | solution.py:717
  106.9 5.9 %collective-permute-done.15.refs_3_ = bf16[144,1024]{1,0:T(8,128)(2,1)S(1)} collective-permute-done((bf16[144,1024]{1,0:T(8,128)(2,1)S(1)}, bf16[144,1024]{1,0:T(8,128)(2,1)S(1)}, u32[]{:S(2)}, u32[]{:S(2)}) %collective-permute-start.15) | collective-permute-done | bytes 294944 | tf_op jit(solution)/shard_map/ppermute | solution.py:717
  112.8 0.7 step_products.2
  113.6 2.0 %collective-permute-start.16 = (bf16[160,128]{1,0:T(8,128)(2,1)S(1)}, bf16[160,128]{1,0:T(8,128)(2,1)S(1)}, u32[]{:S(2)}, u32[]{:S(2)}) collective-permute-start(bf16[160,128]{1,0:T(8,128)(2,1)S(1)} %get-tuple-element.147), channel_id=1, source_target_pairs={{0,8},{8,0},{16,24},{24,16},{1,9},{9,1},{17,25},{25,17},{2,10},{10... | collective-permute-start | bytes 122888 | tf_op jit(solution)/shard_map/ppermute | solution.py:717
  115.6 1.1 collective-permute-start.17
  116.7 1.4 %collective-permute-start.18 = (bf16[160,128]{1,0:T(8,128)(2,1)S(1)}, bf16[160,128]{1,0:T(8,128)(2,1)S(1)}, u32[]{:S(2)}, u32[]{:S(2)}) collective-permute-start(bf16[160,128]{1,0:T(8,128)(2,1)S(1)} %get-tuple-element.149), channel_id=1, source_target_pairs={{0,24},{8,16},{16,8},{24,0},{1,25},{9,17},{17,9},{25,1},{2,26},{10... | collective-permute-start | bytes 122888 | tf_op jit(solution)/shard_map/ppermute | solution.py:717
  118.1 0.8 copy-done.26
  119.0 5.1 %conv_gradients.1 = (bf16[128,2048]{1,0:T(8,128)(2,1)}, f32[16,2048]{1,0:T(8,128)S(1)}, bf16[16,2048]{1,0:T(8,128)(2,1)S(1)}) custom-call(bf16[640,128]{1,0:T(8,128)(2,1)S(1)} %add_convert_fusion.back_a, bf16[640,128]{1,0:T(8,128)(2,1)S(1)} %collective-permute-done.14.back_b, bf16[544,2048]{1,0:T(8,128)(2,1)S(1)} %copy-done.2, ...), custom_call_target="tpu_custom_call" | custom-call | tf_op jit(solution)/shard_map/conv_gradients/pallas_call | solution.py:554
  124.1 2.5 %collective-permute-done.16.refs_1_ = bf16[160,128]{1,0:T(8,128)(2,1)S(1)} collective-permute-done((bf16[160,128]{1,0:T(8,128)(2,1)S(1)}, bf16[160,128]{1,0:T(8,128)(2,1)S(1)}, u32[]{:S(2)}, u32[]{:S(2)}) %collective-permute-start.16) | collective-permute-done | bytes 40992 | tf_op jit(solution)/shard_map/ppermute | solution.py:717
  126.7 4.4 %collective-permute-start.21 = (bf16[16,2048]{1,0:T(8,128)(2,1)S(1)}, bf16[16,2048]{1,0:T(8,128)(2,1)S(1)}, u32[]{:S(2)}, u32[]{:S(2)}) collective-permute-start(bf16[16,2048]{1,0:T(8,128)(2,1)S(1)} %get-tuple-element.168.refs_3_), channel_id=1, source_target_pairs={{0,16},{8,24},{16,0},{24,8},{1,17},{9,25},{17,1},{25,9},{2,18},{10... | collective-permute-start | bytes 196616 | tf_op jit(solution)/shard_map/ppermute | solution.py:52
  131.5 3.2 %row_gradients.1 = (f32[128,2048]{1,0:T(8,128)}, f32[8,2048]{1,0:T(8,128)}, f32[128,2048]{1,0:T(8,128)}, f32[16,2048]{1,0:T(8,128)}) custom-call(bf16[160,128]{1,0:T(8,128)(2,1)S(1)} %get-tuple-element.155.refs_0_, bf16[160,128]{1,0:T(8,128)(2,1)S(1)} %collective-permute-done.16.refs_1_, bf16[160,128]{1,0:T(8,128)(2,1)S(1)} %collective-permute-done.17.refs_2_, ...), custom_call_target="tpu_custom_call" | custom-call | tf_op jit(solution)/shard_map/row_gradients/pallas_call | solution.py:654
  134.7 0.9 collective-permute-done.21.refs_5_
  135.7 0.5 collective-permute-done.22.refs_6_
  136.2 0.7 last_rows.1
  (86 shorter events, 1.5 us)
Async XLA Ops:
  1.4 6.4 %collective-permute-start = (bf16[3,2048]{1,0:T(4,128)(2,1)S(1)}, bf16[3,2048]{1,0:T(4,128)(2,1)S(1)}, u32[]{:S(2)}, u32[]{:S(2)}) collective-permute-start(bf16[3,2048]{1,0:T(4,128)(2,1)S(1)} %slice.9), channel_id=1, source_target_pairs={{0,8},{8,16},{16,24},{1,9},{9,17},{17,25},{2,10},{10,18},{18,26},{... | collective-permute-start | bytes 36872 | tf_op jit(solution)/shard_map/ppermute | solution.py:58
  7.8 19.9 %copy-start.35 = (bf16[3,2048]{1,0:T(4,128)(2,1)}, bf16[3,2048]{1,0:T(4,128)(2,1)S(1)}, u32[]{:S(2)}) copy-start(bf16[3,2048]{1,0:T(4,128)(2,1)S(1)} %collective-permute-done.rim_ref) | copy-start | bytes 36868
  7.8 1.6 %copy-start.1 = (bf16[544,2048]{1,0:T(8,128)(2,1)S(1)}, bf16[544,2048]{1,0:T(8,128)(2,1)}, u32[]{:S(2)}) copy-start(bf16[544,2048]{1,0:T(8,128)(2,1)} %proj_ref.3) | copy-start | bytes 6684676
  9.4 1.0 copy-start.13
  10.5 0.8 copy-start.19
  11.2 0.7 copy-start.37
  11.9 11.9 %copy-start.40 = (f32[16,2048]{1,0:T(8,128)S(1)}, f32[16,2048]{1,0:T(8,128)}, u32[]{:S(2)}) copy-start(f32[16,2048]{1,0:T(8,128)} %param.18) | copy-start | bytes 393220
  11.9 16.5 %copy-start = (bf16[512,2048]{1,0:T(8,128)(2,1)S(1)}, bf16[512,2048]{1,0:T(8,128)(2,1)}, u32[]{:S(2)}) copy-start(bf16[512,2048]{1,0:T(8,128)(2,1)} %refs_9_.3) | copy-start | bytes 6291460
  11.9 16.5 %copy-start.3 = (bf16[128,2048]{1,0:T(8,128)(2,1)S(1)}, bf16[128,2048]{1,0:T(8,128)(2,1)}, u32[]{:S(2)}) copy-start(bf16[128,2048]{1,0:T(8,128)(2,1)} %refs_7_.5) | copy-start | bytes 1572868
  11.9 16.5 %copy-start.39 = (f32[2048]{0:T(1024)S(1)}, f32[2048]{0:T(1024)}, u32[]{:S(2)}) copy-start(f32[2048]{0:T(1024)} %param.17) | copy-start | bytes 24580
  14.2 1.5 %collective-permute-start.1 = (bf16[128,544]{1,0:T(8,128)(2,1)S(1)}, bf16[128,544]{1,0:T(8,128)(2,1)S(1)}, u32[]{:S(2)}, u32[]{:S(2)}) collective-permute-start(bf16[128,544]{1,0:T(8,128)(2,1)S(1)} %get-tuple-element.96), channel_id=1, source_target_pairs={{0,1},{1,0},{2,3},{3,2},{4,5},{5,4},{6,7},{7,6},{8,9},{9,8},{10,11... | collective-permute-start | bytes 417800 | tf_op jit(solution)/shard_map/ppermute | solution.py:717
  15.7 6.4 %collective-permute-start.2 = (bf16[128,544]{1,0:T(8,128)(2,1)S(1)}, bf16[128,544]{1,0:T(8,128)(2,1)S(1)}, u32[]{:S(2)}, u32[]{:S(2)}) collective-permute-start(bf16[128,544]{1,0:T(8,128)(2,1)S(1)} %add_convert_fusion.3), channel_id=1, source_target_pairs={{0,2},{1,3},{2,0},{3,1},{4,6},{5,7},{6,4},{7,5},{8,10},{9,11},{10,... | collective-permute-start | bytes 417800 | tf_op jit(solution)/shard_map/ppermute | solution.py:717
  17.2 34.5 %collective-permute-start.7 = (bf16[128,2048]{1,0:T(8,128)(2,1)S(1)}, bf16[128,2048]{1,0:T(8,128)(2,1)}, u32[]{:S(2)}, u32[]{:S(2)}) collective-permute-start(bf16[128,2048]{1,0:T(8,128)(2,1)S(1)} %get-tuple-element.159.refs_6_.refs_4_), channel_id=1, source_target_pairs={{0,8},{8,0},{16,24},{24,16},{1,9},{9,1},{17,25},{25,17},{2,10},{10... | collective-permute-start | bytes 1572872 | tf_op jit(solution)/shard_map/ppermute | solution.py:717
  19.5 32.2 %collective-permute-start.8 = (bf16[128,2048]{1,0:T(8,128)(2,1)S(1)}, bf16[128,2048]{1,0:T(8,128)(2,1)}, u32[]{:S(2)}, u32[]{:S(2)}) collective-permute-start(bf16[128,2048]{1,0:T(8,128)(2,1)S(1)} %get-tuple-element.159.refs_6_.refs_4_), channel_id=1, source_target_pairs={{0,16},{8,24},{16,0},{24,8},{1,17},{9,25},{17,1},{25,9},{2,18},{10... | collective-permute-start | bytes 1572872 | tf_op jit(solution)/shard_map/ppermute | solution.py:717
  22.2 5.5 %collective-permute-start.3 = (bf16[128,544]{1,0:T(8,128)(2,1)S(1)}, bf16[128,544]{1,0:T(8,128)(2,1)S(1)}, u32[]{:S(2)}, u32[]{:S(2)}) collective-permute-start(bf16[128,544]{1,0:T(8,128)(2,1)S(1)} %add_convert_fusion.2.refs_0_), channel_id=1, source_target_pairs={{0,4},{1,5},{2,6},{3,7},{4,0},{5,1},{6,2},{7,3},{8,12},{9,13},{10,... | collective-permute-start | bytes 417800 | tf_op jit(solution)/shard_map/ppermute | solution.py:717
  27.7 0.7 copy-start.30
  28.4 11.6 %copy-start.27 = (f32[4096]{0:T(1024)}, f32[4096]{0:T(1024)S(1)}, u32[]{:S(2)}) copy-start(f32[4096]{0:T(1024)S(1)} %reshape.36.refs_2_.refs_0_) | copy-start | bytes 49156
  28.5 1.0 copy-start.4
  29.5 0.9 copy-start.31
  30.4 21.4 %copy-start.5 = (bf16[128,2048]{1,0:T(8,128)(2,1)S(1)}, bf16[128,2048]{1,0:T(8,128)(2,1)}, u32[]{:S(2)}) copy-start(bf16[128,2048]{1,0:T(8,128)(2,1)} %refs_8_.5) | copy-start | bytes 1572868
  40.0 0.7 copy-start.32
  40.7 24.7 %copy-start.7 = (f32[2,128,8,128]{3,2,1,0:T(8,128)}, f32[2,128,8,128]{3,2,1,0:T(8,128)S(1)}, u32[]{:S(2)}) copy-start(f32[2,128,8,128]{3,2,1,0:T(8,128)S(1)} %get-tuple-element.98.refs_1_) | copy-start | bytes 3145732
  40.7 24.7 %copy-start.9 = (f32[2,128,8,128]{3,2,1,0:T(8,128)}, f32[2,128,8,128]{3,2,1,0:T(8,128)S(1)}, u32[]{:S(2)}) copy-start(f32[2,128,8,128]{3,2,1,0:T(8,128)S(1)} %get-tuple-element.99.refs_2_) | copy-start | bytes 3145732
  40.7 24.7 %copy-start.11 = (f32[2,128,8,128]{3,2,1,0:T(8,128)}, f32[2,128,8,128]{3,2,1,0:T(8,128)S(1)}, u32[]{:S(2)}) copy-start(f32[2,128,8,128]{3,2,1,0:T(8,128)S(1)} %get-tuple-element.100.refs_3_) | copy-start | bytes 3145732
  40.7 5.4 %collective-permute-start.4 = (bf16[2,18,8,128]{3,2,1,0:T(8,128)(2,1)S(1)}, bf16[2,18,8,128]{3,2,1,0:T(8,128)(2,1)S(1)}, u32[]{:S(2)}, u32[]{:S(2)}) collective-permute-start(bf16[2,18,8,128]{3,2,1,0:T(8,128)(2,1)S(1)} %get-tuple-element.101), channel_id=1, source_target_pairs={{0,8},{8,0},{16,24},{24,16},{1,9},{9,1},{17,25},{25,17},{2,10},{10... | collective-permute-start | bytes 221192 | tf_op jit(solution)/shard_map/ppermute | solution.py:717
  43.0 6.9 %collective-permute-start.5 = (bf16[2,18,8,128]{3,2,1,0:T(8,128)(2,1)S(1)}, bf16[2,18,8,128]{3,2,1,0:T(8,128)(2,1)S(1)}, u32[]{:S(2)}, u32[]{:S(2)}) collective-permute-start(bf16[2,18,8,128]{3,2,1,0:T(8,128)(2,1)S(1)} %get-tuple-element.102), channel_id=1, source_target_pairs={{0,16},{8,24},{16,0},{24,8},{1,17},{9,25},{17,1},{25,9},{2,18},{10... | collective-permute-start | bytes 221192 | tf_op jit(solution)/shard_map/ppermute | solution.py:717
  45.5 6.2 %collective-permute-start.6 = (bf16[2,18,8,128]{3,2,1,0:T(8,128)(2,1)S(1)}, bf16[2,18,8,128]{3,2,1,0:T(8,128)(2,1)S(1)}, u32[]{:S(2)}, u32[]{:S(2)}) collective-permute-start(bf16[2,18,8,128]{3,2,1,0:T(8,128)(2,1)S(1)} %get-tuple-element.103), channel_id=1, source_target_pairs={{0,24},{8,16},{16,8},{24,0},{1,25},{9,17},{17,9},{25,1},{2,26},{10... | collective-permute-start | bytes 221192 | tf_op jit(solution)/shard_map/ppermute | solution.py:717
  51.7 13.7 %copy-start.21 = (bf16[2,18,8,128]{3,2,1,0:T(8,128)(2,1)}, bf16[2,18,8,128]{3,2,1,0:T(8,128)(2,1)S(1)}, u32[]{:S(2)}) copy-start(bf16[2,18,8,128]{3,2,1,0:T(8,128)(2,1)S(1)} %collective-permute-done.6.refs_13_) | copy-start | bytes 221188
  51.7 19.9 %collective-permute-start.9 = (bf16[128,2048]{1,0:T(8,128)(2,1)}, bf16[128,2048]{1,0:T(8,128)(2,1)}, u32[]{:S(2)}, u32[]{:S(2)}) collective-permute-start(bf16[128,2048]{1,0:T(8,128)(2,1)} %collective-permute-done.8.refs_6_), channel_id=1, source_target_pairs={{0,8},{8,0},{16,24},{24,16},{1,9},{9,1},{17,25},{25,17},{2,10},{10... | collective-permute-start | bytes 1572872 | tf_op jit(solution)/shard_map/ppermute | solution.py:717
  51.8 0.7 copy-start.28
  52.5 0.7 copy-start.33
  65.4 0.8 copy-start.15
  66.2 0.7 copy-start.17
  67.6 25.9 %collective-permute-start.10 = (bf16[144,1024]{1,0:T(8,128)(2,1)}, bf16[144,1024]{1,0:T(8,128)(2,1)}, u32[]{:S(2)}, u32[]{:S(2)}) collective-permute-start(bf16[144,1024]{1,0:T(8,128)(2,1)} %get-tuple-element.150.refs_2_), channel_id=1, source_target_pairs={{0,16},{8,24},{16,0},{24,8},{1,17},{9,25},{17,1},{25,9},{2,18},{10... | collective-permute-start | bytes 884744 | tf_op jit(solution)/shard_map/ppermute | solution.py:717
  70.7 22.8 %collective-permute-start.11 = (bf16[512,128]{1,0:T(8,128)(2,1)S(1)}, bf16[512,128]{1,0:T(8,128)(2,1)S(1)}, u32[]{:S(2)}, u32[]{:S(2)}) collective-permute-start(bf16[512,128]{1,0:T(8,128)(2,1)S(1)} %bitcast.17), channel_id=1, source_target_pairs={{0,16},{8,24},{16,0},{24,8},{1,17},{9,25},{17,1},{25,9},{2,18},{10... | collective-permute-start | bytes 393224 | tf_op jit(solution)/shard_map/ppermute | solution.py:717
  71.6 1.0 copy-start.6
  72.7 1.2 copy-start.8
  73.9 1.2 copy-start.10
  75.1 1.2 copy-start.12
  76.3 1.0 copy-start.16
  77.4 1.0 copy-start.18
  78.3 0.9 copy-start.22
  79.2 0.8 copy-start.24
  80.1 0.7 copy-start.29
  80.8 0.7 copy-start.34
  93.4 13.5 %copy-start.25 = (f32[8,2048]{1,0:T(8,128)}, f32[8,2048]{1,0:T(8,128)S(1)}, u32[]{:S(2)}) copy-start(f32[8,2048]{1,0:T(8,128)S(1)} %get-tuple-element.142.small_in) | copy-start | bytes 196612
  93.4 24.7 %copy-start.2 = (bf16[544,2048]{1,0:T(8,128)(2,1)S(1)}, bf16[544,2048]{1,0:T(8,128)(2,1)}, u32[]{:S(2)}) copy-start(bf16[544,2048]{1,0:T(8,128)(2,1)} %proj_ref.3) | copy-start | bytes 6684676
  93.4 24.7 %copy-start.14 = (bf16[128,2048]{1,0:T(8,128)(2,1)S(1)}, bf16[128,2048]{1,0:T(8,128)(2,1)}, u32[]{:S(2)}) copy-start(bf16[128,2048]{1,0:T(8,128)(2,1)} %input_ref.3) | copy-start | bytes 1572868
  93.4 24.7 %copy-start.20 = (f32[4,2048]{1,0:T(4,128)S(1)}, f32[4,2048]{1,0:T(4,128)}, u32[]{:S(2)}) copy-start(f32[4,2048]{1,0:T(4,128)} %refs_2_.1) | copy-start | bytes 98308
  93.4 24.7 %copy-start.36 = (bf16[3,2048]{1,0:T(4,128)(2,1)S(1)}, bf16[3,2048]{1,0:T(4,128)(2,1)}, u32[]{:S(2)}) copy-start(bf16[3,2048]{1,0:T(4,128)(2,1)} %copy-done.35) | copy-start | bytes 36868
  93.4 24.7 %copy-start.38 = (f32[2048]{0:T(1024)S(1)}, f32[2048]{0:T(1024)}, u32[]{:S(2)}) copy-start(f32[2048]{0:T(1024)} %param.14) | copy-start | bytes 24580
  93.5 1.5 %collective-permute-start.12 = (bf16[640,128]{1,0:T(8,128)(2,1)S(1)}, bf16[640,128]{1,0:T(8,128)(2,1)S(1)}, u32[]{:S(2)}, u32[]{:S(2)}) collective-permute-start(bf16[640,128]{1,0:T(8,128)(2,1)S(1)} %get-tuple-element.125), channel_id=1, source_target_pairs={{0,1},{1,0},{2,3},{3,2},{4,5},{5,4},{6,7},{7,6},{8,9},{9,8},{10,11... | collective-permute-start | bytes 491528 | tf_op jit(solution)/shard_map/ppermute | solution.py:717
  95.0 6.3 %collective-permute-start.13 = (bf16[640,128]{1,0:T(8,128)(2,1)S(1)}, bf16[640,128]{1,0:T(8,128)(2,1)S(1)}, u32[]{:S(2)}, u32[]{:S(2)}) collective-permute-start(bf16[640,128]{1,0:T(8,128)(2,1)S(1)} %add_convert_fusion.1), channel_id=1, source_target_pairs={{0,2},{1,3},{2,0},{3,1},{4,6},{5,7},{6,4},{7,5},{8,10},{9,11},{10,... | collective-permute-start | bytes 491528 | tf_op jit(solution)/shard_map/ppermute | solution.py:717
  96.7 16.1 %collective-permute-start.15 = (bf16[144,1024]{1,0:T(8,128)(2,1)S(1)}, bf16[144,1024]{1,0:T(8,128)(2,1)S(1)}, u32[]{:S(2)}, u32[]{:S(2)}) collective-permute-start(bf16[144,1024]{1,0:T(8,128)(2,1)S(1)} %get-tuple-element.137.refs_2_), channel_id=1, source_target_pairs={{0,16},{8,24},{16,0},{24,8},{1,17},{9,25},{17,1},{25,9},{2,18},{10... | collective-permute-start | bytes 884744 | tf_op jit(solution)/shard_map/ppermute | solution.py:717
  101.3 5.5 %collective-permute-start.14 = (bf16[640,128]{1,0:T(8,128)(2,1)S(1)}, bf16[640,128]{1,0:T(8,128)(2,1)S(1)}, u32[]{:S(2)}, u32[]{:S(2)}) collective-permute-start(bf16[640,128]{1,0:T(8,128)(2,1)S(1)} %add_convert_fusion.back_a), channel_id=1, source_target_pairs={{0,4},{1,5},{2,6},{3,7},{4,0},{5,1},{6,2},{7,3},{8,12},{9,13},{10,... | collective-permute-start | bytes 491528 | tf_op jit(solution)/shard_map/ppermute | solution.py:717
  104.6 22.0 %collective-permute-start.19 = (bf16[144,1024]{1,0:T(8,128)(2,1)S(1)}, bf16[144,1024]{1,0:T(8,128)(2,1)S(1)}, u32[]{:S(2)}, u32[]{:S(2)}) collective-permute-start(bf16[144,1024]{1,0:T(8,128)(2,1)S(1)} %get-tuple-element.153), channel_id=1, source_target_pairs={{0,8},{8,0},{16,24},{24,16},{1,9},{9,1},{17,25},{25,17},{2,10},{10... | collective-permute-start | bytes 884744 | tf_op jit(solution)/shard_map/ppermute | solution.py:717
  113.5 18.0 %collective-permute-start.23 = (bf16[144,1024]{1,0:T(8,128)(2,1)S(1)}, bf16[144,1024]{1,0:T(8,128)(2,1)S(1)}, u32[]{:S(2)}, u32[]{:S(2)}) collective-permute-start(bf16[144,1024]{1,0:T(8,128)(2,1)S(1)} %get-tuple-element.166), channel_id=1, source_target_pairs={{0,8},{8,0},{16,24},{24,16},{1,9},{9,1},{17,25},{25,17},{2,10},{10... | collective-permute-start | bytes 884744 | tf_op jit(solution)/shard_map/ppermute | solution.py:717
  113.6 13.0 %collective-permute-start.16 = (bf16[160,128]{1,0:T(8,128)(2,1)S(1)}, bf16[160,128]{1,0:T(8,128)(2,1)S(1)}, u32[]{:S(2)}, u32[]{:S(2)}) collective-permute-start(bf16[160,128]{1,0:T(8,128)(2,1)S(1)} %get-tuple-element.147), channel_id=1, source_target_pairs={{0,8},{8,0},{16,24},{24,16},{1,9},{9,1},{17,25},{25,17},{2,10},{10... | collective-permute-start | bytes 122888 | tf_op jit(solution)/shard_map/ppermute | solution.py:717
  115.6 11.0 %collective-permute-start.17 = (bf16[160,128]{1,0:T(8,128)(2,1)S(1)}, bf16[160,128]{1,0:T(8,128)(2,1)S(1)}, u32[]{:S(2)}, u32[]{:S(2)}) collective-permute-start(bf16[160,128]{1,0:T(8,128)(2,1)S(1)} %get-tuple-element.148), channel_id=1, source_target_pairs={{0,16},{8,24},{16,0},{24,8},{1,17},{9,25},{17,1},{25,9},{2,18},{10... | collective-permute-start | bytes 122888 | tf_op jit(solution)/shard_map/ppermute | solution.py:717
  116.7 9.9 %collective-permute-start.18 = (bf16[160,128]{1,0:T(8,128)(2,1)S(1)}, bf16[160,128]{1,0:T(8,128)(2,1)S(1)}, u32[]{:S(2)}, u32[]{:S(2)}) collective-permute-start(bf16[160,128]{1,0:T(8,128)(2,1)S(1)} %get-tuple-element.149), channel_id=1, source_target_pairs={{0,24},{8,16},{16,8},{24,0},{1,25},{9,17},{17,9},{25,1},{2,26},{10... | collective-permute-start | bytes 122888 | tf_op jit(solution)/shard_map/ppermute | solution.py:717
  118.1 0.8 copy-start.26
  126.6 8.1 %collective-permute-start.20 = (bf16[16,2048]{1,0:T(8,128)(2,1)S(1)}, bf16[16,2048]{1,0:T(8,128)(2,1)S(1)}, u32[]{:S(2)}, u32[]{:S(2)}) collective-permute-start(bf16[16,2048]{1,0:T(8,128)(2,1)S(1)} %get-tuple-element.168.refs_3_), channel_id=1, source_target_pairs={{0,8},{8,16},{16,24},{24,0},{1,9},{9,17},{17,25},{25,1},{2,10},{10... | collective-permute-start | bytes 196616 | tf_op jit(solution)/shard_map/ppermute | solution.py:52
  126.7 9.0 %collective-permute-start.21 = (bf16[16,2048]{1,0:T(8,128)(2,1)S(1)}, bf16[16,2048]{1,0:T(8,128)(2,1)S(1)}, u32[]{:S(2)}, u32[]{:S(2)}) collective-permute-start(bf16[16,2048]{1,0:T(8,128)(2,1)S(1)} %get-tuple-element.168.refs_3_), channel_id=1, source_target_pairs={{0,16},{8,24},{16,0},{24,8},{1,17},{9,25},{17,1},{25,9},{2,18},{10... | collective-permute-start | bytes 196616 | tf_op jit(solution)/shard_map/ppermute | solution.py:52
  131.1 5.1 %collective-permute-start.22 = (bf16[16,2048]{1,0:T(8,128)(2,1)S(1)}, bf16[16,2048]{1,0:T(8,128)(2,1)S(1)}, u32[]{:S(2)}, u32[]{:S(2)}) collective-permute-start(bf16[16,2048]{1,0:T(8,128)(2,1)S(1)} %get-tuple-element.168.refs_3_), channel_id=1, source_target_pairs={{0,24},{8,0},{16,8},{24,16},{1,25},{9,1},{17,9},{25,17},{2,26},{10... | collective-permute-start | bytes 196616 | tf_op jit(solution)/shard_map/ppermute | solution.py:52
  (1 other events, 0.6 us)

commit v12 on v11

--- a/solution.py
+++ b/solution.py
@@ -113,7 +113,7 @@
         out_specs=[columns(rows, width), whole((rows, wide))],
         out_shape=[sds((rows, chans), BF), sds((rows, wide), BF)],
         scratch_shapes=[pltpu.VMEM((rows + 8, width), F32), pltpu.VMEM((rows, wide), F32)],
-        compiler_params=params(16),
+        compiler_params=params(58),
         name="conv_project",
     )(conv_input, rim, weight, bias, proj_weight)
 
@@ -260,7 +260,7 @@
             pltpu.VMEM(message, F32),
             pltpu.VMEM(message, F32),
         ],
-        compiler_params=params(26),
+        compiler_params=params(58),
         name="local_ends",
     )(*parts, coef, step_weight, step_bias, decay, conv_out, gate, grad)
 
@@ -497,7 +497,7 @@
             pltpu.VMEM((rows, states, groups, 128), F32),
         ],
         input_output_aliases=aliases,
-        compiler_params=params(38),
+        compiler_params=params(58),
         name="scan_gradients",
     )(
         coef, *dense, decay, skips, conv_out, gate, grad, step_weight, skip, *messages, *previous
@@ -631,13 +631,31 @@
 
 
 def rows_kernel(ranks, places, *refs):
-    cuts, blocks, refs = refs[:places], refs[places : 2 * places], refs[2 * places :]
-    products, (out_ref, coef_ref, step_ref, decay_ref) = refs[:-4], refs[-4:]
+    cuts, blocks, (out_ref, coef_ref) = refs[:places], refs[places:-2], refs[-2:]
     total = jnp.zeros((cuts[0].shape[0], out_ref.shape[1]), F32)
     for cut, block in zip(cuts, blocks):
         total = total + dot(cut[...], block[...])
     out_ref[...] = total[:ranks, :]
     coef_ref[...] = total[ranks : ranks + coef_ref.shape[0], :]
+
+
+def rows_call(ranks, coef_rows, cuts, blocks):
+    rows, chans = blocks[0].shape
+    width = min(1024, chans)
+    return pl.pallas_call(
+        functools.partial(rows_kernel, ranks, len(cuts)),
+        grid=(chans // width,),
+        in_specs=[whole(cuts[0].shape)] * len(cuts) + [columns(rows, width)] * len(blocks),
+        out_specs=[columns(ranks, width), columns(coef_rows, width)],
+        out_shape=[sds((ranks, chans), F32), sds((coef_rows, chans), F32)],
+        compiler_params=params(16),
+        name="row_gradients",
+    )(*cuts, *blocks)
+
+
+def total_kernel(*refs):
+    products, (step_ref, decay_ref) = refs[:-2], refs[-2:]
+    ranks = step_ref.shape[0]
     for chunk in range(len(products) // 2):
 
         @pl.when(pl.program_id(0) == chunk)
@@ -647,21 +665,19 @@
             decay_ref[...] = mine[ranks:, :] + theirs[ranks:, :].astype(F32)
 
 
-def rows_call(ranks, coef_rows, cuts, blocks, products):
-    rows, chans = blocks[0].shape
+def total_call(ranks, products):
     height, width = products[0].shape
-    heights = (ranks, coef_rows, ranks, height - ranks)
+    chunks = len(products) // 2
+    heights = (ranks, height - ranks)
     return pl.pallas_call(
-        functools.partial(rows_kernel, ranks, len(cuts)),
-        grid=(chans // width,),
-        in_specs=[whole(cuts[0].shape)] * len(cuts)
-        + [columns(rows, width)] * len(blocks)
-        + [whole((height, width))] * len(products),
-        out_specs=[columns(height, width) for height in heights],
-        out_shape=[sds((height, chans), F32) for height in heights],
-        compiler_params=params(20),
-        name="row_gradients",
-    )(*cuts, *blocks, *products)
+        total_kernel,
+        grid=(chunks,),
+        in_specs=[whole((height, width))] * len(products),
+        out_specs=[columns(tall, width) for tall in heights],
+        out_shape=[sds((tall, chunks * width), F32) for tall in heights],
+        compiler_params=params(12),
+        name="step_gradients",
+    )(*products)
 
 
 def last_kernel(places, taps, *refs):
@@ -806,21 +822,19 @@
         mine, theirs = step_call(ranks, lows, step)
         products += [mine, swap(theirs, "ctx", 1)]
     cuts = cut_call(places, backs)
-    cuts, lows = tie((cuts, lows))
     cuts = [cuts[0]] + [swap(cut, "ctx", mask) for mask, cut in enumerate(cuts[1:], 1)]
-    mine, theirs = step_call(ranks, lows, steps[-1])
-    backs, theirs = tie((backs, theirs))
-    latest = [mine, swap(theirs, "ctx", 1)]
     main, tail, sums = conv_grad_call(
         places, low_rank, backs, proj_weight, scan_part, small, conv_input, rim, conv_weight,
         conv_bias,
     )
-    sums, cuts, products = tie((sums, cuts, products))
+    sums, cuts, products, steps[-1], lows = tie((sums, cuts, products, steps[-1], lows))
+    mine, theirs = step_call(ranks, lows, steps[-1])
+    products += [mine, swap(theirs, "ctx", 1)]
     late = [sums] + [rotate(sums, "ctx", hop) for hop in range(1, places)]
-    grad_proj, grad_coef, grad_step, decay_grad = rows_call(
-        ranks, 2 * states // places, cuts, blocks, products + latest
-    )
-    late, grad_proj = tie((late, grad_proj))
+    grad_proj, grad_coef = rows_call(ranks, 2 * states // places, cuts, blocks)
+    products, grad_proj = tie((products, grad_proj))
+    grad_step, decay_grad = total_call(ranks, products)
+    late, grad_step = tie((late, grad_step))
     grad_input, conv_w, conv_b, step_b, skip = last_call(main, tail, conv_weight, late)
     return (
         grad_input,

time: 138 us -> 127 us (0.920)
  local copies, waits for them, and re-layouts: 23.6 us -> 3.8 us
  Pallas kernels: 47.4 us -> 53.5 us
  waiting for transfers between devices: 27.1 us -> 31.1 us
  starting transfers between devices: 37.6 us -> 35.3 us
  other arithmetic: 0.19 us -> 2.02 us
    unnamed x83 -> x37, local copies, waits for them, and re-layouts: 21.8 us -> 1.53 us
    pallas_call x2, Pallas kernels: 24.1 us -> 27.4 us  [scan_call(): pl.pallas_call(functools.partial(scan_kernel, places, states, first), gri...]
    ppermute x20, starting transfers between devices: 27.7 us -> 24.7 us  [swap(): lax.ppermute(block, axis, [(i, i ^ mask) for i in range(lax.axis_size(axi...]
    ppermute x20, waiting for transfers between devices: 24.3 us -> 26.9 us  [swap(): lax.ppermute(block, axis, [(i, i ^ mask) for i in range(lax.axis_size(axi...]
    pallas_call x1, Pallas kernels: 9.57 us -> 11.7 us  [local_call(): pl.pallas_call(functools.partial(local_kernel, low_rank, states, places),...]
    pallas_call x1, Pallas kernels: 2.25 us -> 4.15 us  [conv_call(): pl.pallas_call(conv_kernel, grid=(chans // width,), in_specs=[columns(row...]
    convert_element_type x4, other arithmetic: 0.18 us -> 2.01 us  [chan_sum(): part = (part.astype(F32) + other.astype(F32)).astype(BF)]
  transfers between devices with their start and end apart: 24 -> 24, of which waited for: 13 -> 12; matrix products, arithmetic and copies ran while one was open for 1% -> 1% of each run, Pallas kernels for 32% -> 38%
where the time goes in v12:
time: 127 us
  Pallas kernels  53.5 us (42%)
  starting transfers between devices  35.3 us (28%)
  waiting for transfers between devices  31.1 us (24%)
  local copies, waits for them, and re-layouts  3.8 us (3%)
  other arithmetic  2.02 us (2%)
    pallas_call x2, Pallas kernels, scan_call(): pl.pallas_call(functools.partial(scan_kernel, places, states, first), gri...  27.4 us
    ppermute x20, waiting for transfers between devices, swap(): lax.ppermute(block, axis, [(i, i ^ mask) for i in range(lax.axis_size(axi...  26.9 us
    ppermute x20, starting transfers between devices, swap(): lax.ppermute(block, axis, [(i, i ^ mask) for i in range(lax.axis_size(axi...  24.7 us
    pallas_call x1, Pallas kernels, local_call(): pl.pallas_call(functools.partial(local_kernel, low_rank, states, places),...  11.7 us
    ppermute x3, starting transfers between devices, rotate(): lax.ppermute(block, axis, [(i, (i + distance) % count) for i in range(cou...  5.69 us
    pallas_call x1, Pallas kernels, conv_grad_call(): pl.pallas_call(functools.partial(conv_grad_kernel, places, low_rank), gri...  5.09 us
    ppermute x1, starting transfers between devices, shift(): return lax.ppermute(block, axis, route)  4.93 us
    pallas_call x1, Pallas kernels, conv_call(): pl.pallas_call(conv_kernel, grid=(chans // width,), in_specs=[columns(row...  4.15 us
  transfers between devices with their start and end apart: 24, of which 12 were waited for; matrix products, arithmetic and copies ran while one was open for 1% of the time, Pallas kernels for 38%

profile of v12, /device:TPU:0, one launch (start us, length us, event | category | flops | bytes accessed | tf_op | source)
XLA Modules:
  0.0 126.6 jit_solution(6785041776803082407)
XLA Ops:
  0.7 0.8 slice.9
  1.5 4.9 %collective-permute-start = (bf16[3,2048]{1,0:T(4,128)(2,1)S(1)}, bf16[3,2048]{1,0:T(4,128)(2,1)S(1)}, u32[]{:S(2)}, u32[]{:S(2)}) collective-permute-start(bf16[3,2048]{1,0:T(4,128)(2,1)S(1)} %slice.9), channel_id=1, source_target_pairs={{0,8},{8,16},{16,24},{1,9},{9,17},{17,25},{2,10},{10,18},{18,26},{... | collective-permute-start | bytes 36872 | tf_op jit(solution)/shard_map/ppermute | solution.py:58
  6.4 1.4 %collective-permute-done.rim_ref = bf16[3,2048]{1,0:T(4,128)(2,1)S(1)} collective-permute-done((bf16[3,2048]{1,0:T(4,128)(2,1)S(1)}, bf16[3,2048]{1,0:T(4,128)(2,1)S(1)}, u32[]{:S(2)}, u32[]{:S(2)}) %collective-permute-start) | collective-permute-done | bytes 12320 | tf_op jit(solution)/shard_map/ppermute | solution.py:58
  7.8 0.6 copy-done.8
  8.4 4.2 %conv_project.1 = (bf16[128,2048]{1,0:T(8,128)(2,1)}, bf16[128,544]{1,0:T(8,128)(2,1)}) custom-call(bf16[128,2048]{1,0:T(8,128)(2,1)} %input_ref.3, bf16[3,2048]{1,0:T(4,128)(2,1)} %copy-done.8, f32[4,2048]{1,0:T(4,128)} %refs_2_.1, f32[1,2048]{1,0:T(1,128)} %bitcast.17, bf16[544,2048]{1,0:T(8,128)(2,1)} %proj_ref.3), custom_call_target="tpu_custom_call" | custom-call | tf_op jit(solution)/shard_map/conv_project/pallas_call | solution.py:103
  12.6 1.6 %collective-permute-done.1 = bf16[128,544]{1,0:T(8,128)(2,1)S(1)} collective-permute-done((bf16[128,544]{1,0:T(8,128)(2,1)}, bf16[128,544]{1,0:T(8,128)(2,1)S(1)}, u32[]{:S(2)}, u32[]{:S(2)}) %collective-permute-start.1) | collective-permute-done | bytes 139296 | tf_op jit(solution)/shard_map/ppermute | solution.py:733
  14.2 1.0 add_convert_fusion.3
  15.2 1.6 %collective-permute-start.2 = (bf16[128,544]{1,0:T(8,128)(2,1)S(1)}, bf16[128,544]{1,0:T(8,128)(2,1)S(1)}, u32[]{:S(2)}, u32[]{:S(2)}) collective-permute-start(bf16[128,544]{1,0:T(8,128)(2,1)S(1)} %add_convert_fusion.3), channel_id=1, source_target_pairs={{0,2},{1,3},{2,0},{3,1},{4,6},{5,7},{6,4},{7,5},{8,10},{9,11},{10,... | collective-permute-start | bytes 417800 | tf_op jit(solution)/shard_map/ppermute | solution.py:733
  16.7 2.3 %collective-permute-start.7 = (bf16[128,2048]{1,0:T(8,128)(2,1)}, bf16[128,2048]{1,0:T(8,128)(2,1)S(1)}, u32[]{:S(2)}, u32[]{:S(2)}) collective-permute-start(bf16[128,2048]{1,0:T(8,128)(2,1)} %get-tuple-element.158.refs_6_.refs_4_), channel_id=1, source_target_pairs={{0,8},{8,0},{16,24},{24,16},{1,9},{9,1},{17,25},{25,17},{2,10},{10... | collective-permute-start | bytes 1572872 | tf_op jit(solution)/shard_map/ppermute | solution.py:733
  19.0 2.6 %collective-permute-start.8 = (bf16[128,2048]{1,0:T(8,128)(2,1)}, bf16[128,2048]{1,0:T(8,128)(2,1)S(1)}, u32[]{:S(2)}, u32[]{:S(2)}) collective-permute-start(bf16[128,2048]{1,0:T(8,128)(2,1)} %get-tuple-element.158.refs_6_.refs_4_), channel_id=1, source_target_pairs={{0,16},{8,24},{16,0},{24,8},{1,17},{9,25},{17,1},{25,9},{2,18},{10... | collective-permute-start | bytes 1572872 | tf_op jit(solution)/shard_map/ppermute | solution.py:733
  21.6 0.0 collective-permute-done.2
  21.6 0.0 copy-start.11
  21.7 1.6 %collective-permute-start.3 = (bf16[128,544]{1,0:T(8,128)(2,1)S(1)}, bf16[128,544]{1,0:T(8,128)(2,1)S(1)}, u32[]{:S(2)}, u32[]{:S(2)}) collective-permute-start(bf16[128,544]{1,0:T(8,128)(2,1)S(1)} %add_convert_fusion.2.refs_0_), channel_id=1, source_target_pairs={{0,4},{1,5},{2,6},{3,7},{4,0},{5,1},{6,2},{7,3},{8,12},{9,13},{10,... | collective-permute-start | bytes 417800 | tf_op jit(solution)/shard_map/ppermute | solution.py:733
  23.3 0.7 copy.29
  23.9 3.2 %collective-permute-done.3.refs_1_ = bf16[128,544]{1,0:T(8,128)(2,1)S(1)} collective-permute-done((bf16[128,544]{1,0:T(8,128)(2,1)S(1)}, bf16[128,544]{1,0:T(8,128)(2,1)S(1)}, u32[]{:S(2)}, u32[]{:S(2)}) %collective-permute-start.3) | collective-permute-done | bytes 139296 | tf_op jit(solution)/shard_map/ppermute | solution.py:733
  27.1 0.7 reshape.36.refs_2_.refs_0_
  27.8 11.7 %local_ends.1 = (f32[2,128,8,128]{3,2,1,0:T(8,128)}, f32[2,128,8,128]{3,2,1,0:T(8,128)}, f32[2,128,8,128]{3,2,1,0:T(8,128)}, bf16[128,512]{1,0:T(8,128)(2,1)}, b...) custom-call(bf16[128,544]{1,0:T(8,128)(2,1)} %copy-done.11, ...), custom_call_target="tpu_custom_call" | custom-call | tf_op jit(solution)/shard_map/local_ends/pallas_call | solution.py:231
  39.5 2.2 %collective-permute-start.4 = (bf16[2,18,8,128]{3,2,1,0:T(8,128)(2,1)}, bf16[2,18,8,128]{3,2,1,0:T(8,128)(2,1)S(1)}, u32[]{:S(2)}, u32[]{:S(2)}) collective-permute-start(bf16[2,18,8,128]{3,2,1,0:T(8,128)(2,1)} %get-tuple-element.101), channel_id=1, source_target_pairs={{0,8},{8,0},{16,24},{24,16},{1,9},{9,1},{17,25},{25,17},{2,10},{10... | collective-permute-start | bytes 221192 | tf_op jit(solution)/shard_map/ppermute | solution.py:733
  41.8 2.6 %collective-permute-start.5 = (bf16[2,18,8,128]{3,2,1,0:T(8,128)(2,1)}, bf16[2,18,8,128]{3,2,1,0:T(8,128)(2,1)S(1)}, u32[]{:S(2)}, u32[]{:S(2)}) collective-permute-start(bf16[2,18,8,128]{3,2,1,0:T(8,128)(2,1)} %get-tuple-element.102), channel_id=1, source_target_pairs={{0,16},{8,24},{16,0},{24,8},{1,17},{9,25},{17,1},{25,9},{2,18},{10... | collective-permute-start | bytes 221192 | tf_op jit(solution)/shard_map/ppermute | solution.py:733
  44.3 0.6 collective-permute-done.4.refs_11_
  45.0 4.6 %collective-permute-done.5.refs_12_ = bf16[2,18,8,128]{3,2,1,0:T(8,128)(2,1)S(1)} collective-permute-done((bf16[2,18,8,128]{3,2,1,0:T(8,128)(2,1)}, bf16[2,18,8,128]{3,2,1,0:T(8,128)(2,1)S(1)}, u32[]{:S(2)}, u32[]{:S(2)}) %collective-permute-start.5) | collective-permute-done | bytes 73760 | tf_op jit(solution)/shard_map/ppermute | solution.py:733
  49.6 1.2 collective-permute-done.6.refs_13_
  50.8 1.0 collective-permute-start.9
  51.8 13.6 %scan_gradients.2 = (bf16[144,1024]{1,0:T(8,128)(2,1)}, bf16[128,2048]{1,0:T(8,128)(2,1)}, bf16[128,2048]{1,0:T(8,128)(2,1)}, f32[8,2048]{1,0:T(8,128)}, f32[640,128]{1,0:T(8,128)}) custom-call(f32[4096]{0:T(1024)} %reshape.36.refs_2_.refs_0_, f32[2,128,8,128]{3,2,1,0:T(8,128)} %get-tuple-element.98.refs_1_, f32[2,128,8,128]{3,2,1,0:T(8,128)} %get-tuple-element.99.refs_2_, ...), custom_call_target="tpu_custom_call" | custom-call | tf_op jit(solution)/shard_map/scan_gradients/pallas_call | solution.py:467
  65.4 1.6 %collective-permute-start.10 = (bf16[144,1024]{1,0:T(8,128)(2,1)}, bf16[144,1024]{1,0:T(8,128)(2,1)S(1)}, u32[]{:S(2)}, u32[]{:S(2)}) collective-permute-start(bf16[144,1024]{1,0:T(8,128)(2,1)} %get-tuple-element.140.refs_2_), channel_id=1, source_target_pairs={{0,16},{8,24},{16,0},{24,8},{1,17},{9,25},{17,1},{25,9},{2,18},{10... | collective-permute-start | bytes 884744 | tf_op jit(solution)/shard_map/ppermute | solution.py:733
  67.0 0.1 copy.26
  67.1 1.4 %collective-permute-start.11 = (bf16[512,128]{1,0:T(8,128)(2,1)S(1)}, bf16[512,128]{1,0:T(8,128)(2,1)S(1)}, u32[]{:S(2)}, u32[]{:S(2)}) collective-permute-start(bf16[512,128]{1,0:T(8,128)(2,1)S(1)} %bitcast.14), channel_id=1, source_target_pairs={{0,16},{8,24},{16,0},{24,8},{1,17},{9,25},{17,1},{25,9},{2,18},{10... | collective-permute-start | bytes 393224 | tf_op jit(solution)/shard_map/ppermute | solution.py:733
  68.5 0.0 copy-start.9
  68.6 0.0 copy-start.10
  68.6 13.8 %scan_gradients.3 = (bf16[144,1024]{1,0:T(8,128)(2,1)}, bf16[128,2048]{1,0:T(8,128)(2,1)}, bf16[128,2048]{1,0:T(8,128)(2,1)}, f32[8,2048]{1,0:T(8,128)}, bf16[640,128]{1,0:T(8,128)(2,1)}) custom-call(f32[4096]{0:T(1024)} %reshape.36.refs_2_.refs_0_, ...), custom_call_target="tpu_custom_call", output_to_operand_aliasing={{1}: (15, {}), {2}: (16, {}), {3}: (17, {})} | custom-call | tf_op jit(solution)/shard_map/scan_gradients/pallas_call | solution.py:467
  82.4 3.4 %collective-permute-done.11.refs_1_ = bf16[512,128]{1,0:T(8,128)(2,1)S(1)} collective-permute-done((bf16[512,128]{1,0:T(8,128)(2,1)S(1)}, bf16[512,128]{1,0:T(8,128)(2,1)S(1)}, u32[]{:S(2)}, u32[]{:S(2)}) %collective-permute-start.11) | collective-permute-done | bytes 131104 | tf_op jit(solution)/shard_map/ppermute | solution.py:733
  85.8 0.0 collective-permute-done.10.refs_3_
  85.8 0.0 collective-permute-start.12
  85.8 1.6 %collective-permute-done.12 = bf16[640,128]{1,0:T(8,128)(2,1)S(1)} collective-permute-done((bf16[640,128]{1,0:T(8,128)(2,1)}, bf16[640,128]{1,0:T(8,128)(2,1)S(1)}, u32[]{:S(2)}, u32[]{:S(2)}) %collective-permute-start.12) | collective-permute-done | bytes 163872 | tf_op jit(solution)/shard_map/ppermute | solution.py:733
  87.4 1.0 add_convert_fusion.1
  88.4 0.2 collective-permute-start.13
  88.6 0.0 collective-permute-start.19
  88.6 6.1 %collective-permute-done.13 = bf16[640,128]{1,0:T(8,128)(2,1)S(1)} collective-permute-done((bf16[640,128]{1,0:T(8,128)(2,1)S(1)}, bf16[640,128]{1,0:T(8,128)(2,1)S(1)}, u32[]{:S(2)}, u32[]{:S(2)}) %collective-permute-start.13) | collective-permute-done | bytes 163872 | tf_op jit(solution)/shard_map/ppermute | solution.py:733
  94.7 0.7 step_products.2
  95.5 0.5 collective-permute-start.18
  96.0 1.5 %collective-permute-start.14 = (bf16[640,128]{1,0:T(8,128)(2,1)S(1)}, bf16[640,128]{1,0:T(8,128)(2,1)S(1)}, u32[]{:S(2)}, u32[]{:S(2)}) collective-permute-start(bf16[640,128]{1,0:T(8,128)(2,1)S(1)} %add_convert_fusion.back_a), channel_id=1, source_target_pairs={{0,4},{1,5},{2,6},{3,7},{4,0},{5,1},{6,2},{7,3},{8,12},{9,13},{10,... | collective-permute-start | bytes 491528 | tf_op jit(solution)/shard_map/ppermute | solution.py:733
  97.5 3.8 %collective-permute-done.14.back_b = bf16[640,128]{1,0:T(8,128)(2,1)S(1)} collective-permute-done((bf16[640,128]{1,0:T(8,128)(2,1)S(1)}, bf16[640,128]{1,0:T(8,128)(2,1)S(1)}, u32[]{:S(2)}, u32[]{:S(2)}) %collective-permute-start.14) | collective-permute-done | bytes 163872 | tf_op jit(solution)/shard_map/ppermute | solution.py:733
  101.3 0.1 cut_rows.1
  101.4 1.6 %collective-permute-start.15 = (bf16[160,128]{1,0:T(8,128)(2,1)S(1)}, bf16[160,128]{1,0:T(8,128)(2,1)S(1)}, u32[]{:S(2)}, u32[]{:S(2)}) collective-permute-start(bf16[160,128]{1,0:T(8,128)(2,1)S(1)} %get-tuple-element.135), channel_id=1, source_target_pairs={{0,8},{8,0},{16,24},{24,16},{1,9},{9,1},{17,25},{25,17},{2,10},{10... | collective-permute-start | bytes 122888 | tf_op jit(solution)/shard_map/ppermute | solution.py:733
  103.0 2.0 %collective-permute-start.16 = (bf16[160,128]{1,0:T(8,128)(2,1)S(1)}, bf16[160,128]{1,0:T(8,128)(2,1)S(1)}, u32[]{:S(2)}, u32[]{:S(2)}) collective-permute-start(bf16[160,128]{1,0:T(8,128)(2,1)S(1)} %get-tuple-element.136), channel_id=1, source_target_pairs={{0,16},{8,24},{16,0},{24,8},{1,17},{9,25},{17,1},{25,9},{2,18},{10... | collective-permute-start | bytes 122888 | tf_op jit(solution)/shard_map/ppermute | solution.py:733
  105.0 1.3 %collective-permute-start.17 = (bf16[160,128]{1,0:T(8,128)(2,1)S(1)}, bf16[160,128]{1,0:T(8,128)(2,1)S(1)}, u32[]{:S(2)}, u32[]{:S(2)}) collective-permute-start(bf16[160,128]{1,0:T(8,128)(2,1)S(1)} %get-tuple-element.137), channel_id=1, source_target_pairs={{0,24},{8,16},{16,8},{24,0},{1,25},{9,17},{17,9},{25,1},{2,26},{10... | collective-permute-start | bytes 122888 | tf_op jit(solution)/shard_map/ppermute | solution.py:733
  106.3 0.0 copy-start.7
  106.4 0.8 copy-done.7
  107.2 5.1 %conv_gradients.1 = (bf16[128,2048]{1,0:T(8,128)(2,1)}, f32[16,2048]{1,0:T(8,128)S(1)}, bf16[16,2048]{1,0:T(8,128)(2,1)S(1)}) custom-call(bf16[640,128]{1,0:T(8,128)(2,1)S(1)} %add_convert_fusion.back_a, bf16[640,128]{1,0:T(8,128)(2,1)S(1)} %collective-permute-done.14.back_b, bf16[544,2048]{1,0:T(8,128)(2,1)S(1)} %copy-done, ...), custom_call_target="tpu_custom_call" | custom-call | tf_op jit(solution)/shard_map/conv_gradients/pallas_call | solution.py:554
  112.3 0.0 collective-permute-done.19.refs_3_
  112.3 0.0 collective-permute-done.15.refs_1_
  112.3 0.0 collective-permute-done.16.refs_2_
  112.3 0.0 collective-permute-done.18.refs_1_
  112.3 0.7 step_products.3
  113.1 0.7 collective-permute-start.23
  113.8 1.4 %collective-permute-start.20 = (bf16[16,2048]{1,0:T(8,128)(2,1)S(1)}, bf16[16,2048]{1,0:T(8,128)(2,1)S(1)}, u32[]{:S(2)}, u32[]{:S(2)}) collective-permute-start(bf16[16,2048]{1,0:T(8,128)(2,1)S(1)} %get-tuple-element.168.refs_3_), channel_id=1, source_target_pairs={{0,8},{8,16},{16,24},{24,0},{1,9},{9,17},{17,25},{25,1},{2,10},{10... | collective-permute-start | bytes 196616 | tf_op jit(solution)/shard_map/ppermute | solution.py:52
  115.2 2.0 %collective-permute-start.21 = (bf16[16,2048]{1,0:T(8,128)(2,1)S(1)}, bf16[16,2048]{1,0:T(8,128)(2,1)S(1)}, u32[]{:S(2)}, u32[]{:S(2)}) collective-permute-start(bf16[16,2048]{1,0:T(8,128)(2,1)S(1)} %get-tuple-element.168.refs_3_), channel_id=1, source_target_pairs={{0,16},{8,24},{16,0},{24,8},{1,17},{9,25},{17,1},{25,9},{2,18},{10... | collective-permute-start | bytes 196616 | tf_op jit(solution)/shard_map/ppermute | solution.py:52
  117.2 2.3 %collective-permute-start.22 = (bf16[16,2048]{1,0:T(8,128)(2,1)S(1)}, bf16[16,2048]{1,0:T(8,128)(2,1)S(1)}, u32[]{:S(2)}, u32[]{:S(2)}) collective-permute-start(bf16[16,2048]{1,0:T(8,128)(2,1)S(1)} %get-tuple-element.168.refs_3_), channel_id=1, source_target_pairs={{0,24},{8,0},{16,8},{24,16},{1,25},{9,1},{17,9},{25,17},{2,26},{10... | collective-permute-start | bytes 196616 | tf_op jit(solution)/shard_map/ppermute | solution.py:52
  119.4 1.9 %row_gradients.1 = (f32[128,2048]{1,0:T(8,128)}, f32[8,2048]{1,0:T(8,128)}) custom-call(bf16[160,128]{1,0:T(8,128)(2,1)S(1)} %get-tuple-element.154.refs_0_, bf16[160,128]{1,0:T(8,128)(2,1)S(1)} %collective-permute-done.15.refs_1_, bf16[160,128]{1,0:T(8,128)(2,1)S(1)} %collective-permute-done.16.refs_2_, ...), custom_call_target="tpu_custom_call" | custom-call | tf_op jit(solution)/shard_map/row_gradients/pallas_call | solution.py:645
  121.4 0.7 collective-permute-done.23.refs_3_
  122.1 1.1 step_gradients.1
  123.2 2.7 %collective-permute-done.20.refs_4_ = bf16[16,2048]{1,0:T(8,128)(2,1)S(1)} collective-permute-done((bf16[16,2048]{1,0:T(8,128)(2,1)S(1)}, bf16[16,2048]{1,0:T(8,128)(2,1)S(1)}, u32[]{:S(2)}, u32[]{:S(2)}) %collective-permute-start.20) | collective-permute-done | bytes 65568 | tf_op jit(solution)/shard_map/ppermute | solution.py:52
  125.9 0.0 collective-permute-done.21.refs_5_
  125.9 0.7 last_rows.1
  (41 shorter events, 0.2 us)
Async XLA Ops:
  0.6 22.6 %copy-start.16 = (f32[16,2048]{1,0:T(8,128)S(1)}, f32[16,2048]{1,0:T(8,128)}, u32[]{:S(2)}) copy-start(f32[16,2048]{1,0:T(8,128)} %param.18) | copy-start | bytes 393220
  1.5 6.4 %collective-permute-start = (bf16[3,2048]{1,0:T(4,128)(2,1)S(1)}, bf16[3,2048]{1,0:T(4,128)(2,1)S(1)}, u32[]{:S(2)}, u32[]{:S(2)}) collective-permute-start(bf16[3,2048]{1,0:T(4,128)(2,1)S(1)} %slice.9), channel_id=1, source_target_pairs={{0,8},{8,16},{16,24},{1,9},{9,17},{17,25},{2,10},{10,18},{18,26},{... | collective-permute-start | bytes 36872 | tf_op jit(solution)/shard_map/ppermute | solution.py:58
  7.8 0.6 copy-start.8
  12.6 1.6 %collective-permute-start.1 = (bf16[128,544]{1,0:T(8,128)(2,1)}, bf16[128,544]{1,0:T(8,128)(2,1)S(1)}, u32[]{:S(2)}, u32[]{:S(2)}) collective-permute-start(bf16[128,544]{1,0:T(8,128)(2,1)} %get-tuple-element.96), channel_id=1, source_target_pairs={{0,1},{1,0},{2,3},{3,2},{4,5},{5,4},{6,7},{7,6},{8,9},{9,8},{10,11... | collective-permute-start | bytes 417800 | tf_op jit(solution)/shard_map/ppermute | solution.py:733
  15.2 6.4 %collective-permute-start.2 = (bf16[128,544]{1,0:T(8,128)(2,1)S(1)}, bf16[128,544]{1,0:T(8,128)(2,1)S(1)}, u32[]{:S(2)}, u32[]{:S(2)}) collective-permute-start(bf16[128,544]{1,0:T(8,128)(2,1)S(1)} %add_convert_fusion.3), channel_id=1, source_target_pairs={{0,2},{1,3},{2,0},{3,1},{4,6},{5,7},{6,4},{7,5},{8,10},{9,11},{10,... | collective-permute-start | bytes 417800 | tf_op jit(solution)/shard_map/ppermute | solution.py:733
  16.7 34.1 %collective-permute-start.7 = (bf16[128,2048]{1,0:T(8,128)(2,1)}, bf16[128,2048]{1,0:T(8,128)(2,1)S(1)}, u32[]{:S(2)}, u32[]{:S(2)}) collective-permute-start(bf16[128,2048]{1,0:T(8,128)(2,1)} %get-tuple-element.158.refs_6_.refs_4_), channel_id=1, source_target_pairs={{0,8},{8,0},{16,24},{24,16},{1,9},{9,1},{17,25},{25,17},{2,10},{10... | collective-permute-start | bytes 1572872 | tf_op jit(solution)/shard_map/ppermute | solution.py:733
  19.0 31.8 %collective-permute-start.8 = (bf16[128,2048]{1,0:T(8,128)(2,1)}, bf16[128,2048]{1,0:T(8,128)(2,1)S(1)}, u32[]{:S(2)}, u32[]{:S(2)}) collective-permute-start(bf16[128,2048]{1,0:T(8,128)(2,1)} %get-tuple-element.158.refs_6_.refs_4_), channel_id=1, source_target_pairs={{0,16},{8,24},{16,0},{24,8},{1,17},{9,25},{17,1},{25,9},{2,18},{10... | collective-permute-start | bytes 1572872 | tf_op jit(solution)/shard_map/ppermute | solution.py:733
  21.6 6.2 %copy-start.11 = (bf16[128,544]{1,0:T(8,128)(2,1)}, bf16[128,544]{1,0:T(8,128)(2,1)S(1)}, u32[]{:S(2)}) copy-start(bf16[128,544]{1,0:T(8,128)(2,1)S(1)} %add_convert_fusion.2.refs_0_) | copy-start | bytes 417796
  21.7 5.5 %collective-permute-start.3 = (bf16[128,544]{1,0:T(8,128)(2,1)S(1)}, bf16[128,544]{1,0:T(8,128)(2,1)S(1)}, u32[]{:S(2)}, u32[]{:S(2)}) collective-permute-start(bf16[128,544]{1,0:T(8,128)(2,1)S(1)} %add_convert_fusion.2.refs_0_), channel_id=1, source_target_pairs={{0,4},{1,5},{2,6},{3,7},{4,0},{5,1},{6,2},{7,3},{8,12},{9,13},{10,... | collective-permute-start | bytes 417800 | tf_op jit(solution)/shard_map/ppermute | solution.py:733
  27.1 0.7 copy-start.15
  39.5 5.4 %collective-permute-start.4 = (bf16[2,18,8,128]{3,2,1,0:T(8,128)(2,1)}, bf16[2,18,8,128]{3,2,1,0:T(8,128)(2,1)S(1)}, u32[]{:S(2)}, u32[]{:S(2)}) collective-permute-start(bf16[2,18,8,128]{3,2,1,0:T(8,128)(2,1)} %get-tuple-element.101), channel_id=1, source_target_pairs={{0,8},{8,0},{16,24},{24,16},{1,9},{9,1},{17,25},{25,17},{2,10},{10... | collective-permute-start | bytes 221192 | tf_op jit(solution)/shard_map/ppermute | solution.py:733
  41.8 7.8 %collective-permute-start.5 = (bf16[2,18,8,128]{3,2,1,0:T(8,128)(2,1)}, bf16[2,18,8,128]{3,2,1,0:T(8,128)(2,1)S(1)}, u32[]{:S(2)}, u32[]{:S(2)}) collective-permute-start(bf16[2,18,8,128]{3,2,1,0:T(8,128)(2,1)} %get-tuple-element.102), channel_id=1, source_target_pairs={{0,16},{8,24},{16,0},{24,8},{1,17},{9,25},{17,1},{25,9},{2,18},{10... | collective-permute-start | bytes 221192 | tf_op jit(solution)/shard_map/ppermute | solution.py:733
  44.3 6.5 %collective-permute-start.6 = (bf16[2,18,8,128]{3,2,1,0:T(8,128)(2,1)}, bf16[2,18,8,128]{3,2,1,0:T(8,128)(2,1)S(1)}, u32[]{:S(2)}, u32[]{:S(2)}) collective-permute-start(bf16[2,18,8,128]{3,2,1,0:T(8,128)(2,1)} %get-tuple-element.103), channel_id=1, source_target_pairs={{0,24},{8,16},{16,8},{24,0},{1,25},{9,17},{17,9},{25,1},{2,26},{10... | collective-permute-start | bytes 221192 | tf_op jit(solution)/shard_map/ppermute | solution.py:733
  45.0 6.8 %copy-start.12 = (bf16[2,18,8,128]{3,2,1,0:T(8,128)(2,1)}, bf16[2,18,8,128]{3,2,1,0:T(8,128)(2,1)S(1)}, u32[]{:S(2)}) copy-start(bf16[2,18,8,128]{3,2,1,0:T(8,128)(2,1)S(1)} %collective-permute-done.4.refs_11_) | copy-start | bytes 221188
  49.6 2.2 %copy-start.13 = (bf16[2,18,8,128]{3,2,1,0:T(8,128)(2,1)}, bf16[2,18,8,128]{3,2,1,0:T(8,128)(2,1)S(1)}, u32[]{:S(2)}) copy-start(bf16[2,18,8,128]{3,2,1,0:T(8,128)(2,1)S(1)} %collective-permute-done.5.refs_12_) | copy-start | bytes 221188
  50.8 1.0 copy-start.14
  50.8 17.7 %collective-permute-start.9 = (bf16[128,2048]{1,0:T(8,128)(2,1)S(1)}, bf16[128,2048]{1,0:T(8,128)(2,1)S(1)}, u32[]{:S(2)}, u32[]{:S(2)}) collective-permute-start(bf16[128,2048]{1,0:T(8,128)(2,1)S(1)} %collective-permute-done.8.refs_6_), channel_id=1, source_target_pairs={{0,8},{8,0},{16,24},{24,16},{1,9},{9,1},{17,25},{25,17},{2,10},{10... | collective-permute-start | bytes 1572872 | tf_op jit(solution)/shard_map/ppermute | solution.py:733
  51.8 15.2 %copy-start.17 = (bf16[128,512]{1,0:T(8,128)(2,1)S(1)}, bf16[128,512]{1,0:T(8,128)(2,1)}, u32[]{:S(2)}) copy-start(bf16[128,512]{1,0:T(8,128)(2,1)} %get-tuple-element.124) | copy-start | bytes 393220
  65.4 20.4 %collective-permute-start.10 = (bf16[144,1024]{1,0:T(8,128)(2,1)}, bf16[144,1024]{1,0:T(8,128)(2,1)S(1)}, u32[]{:S(2)}, u32[]{:S(2)}) collective-permute-start(bf16[144,1024]{1,0:T(8,128)(2,1)} %get-tuple-element.140.refs_2_), channel_id=1, source_target_pairs={{0,16},{8,24},{16,0},{24,8},{1,17},{9,25},{17,1},{25,9},{2,18},{10... | collective-permute-start | bytes 884744 | tf_op jit(solution)/shard_map/ppermute | solution.py:733
  67.1 18.7 %collective-permute-start.11 = (bf16[512,128]{1,0:T(8,128)(2,1)S(1)}, bf16[512,128]{1,0:T(8,128)(2,1)S(1)}, u32[]{:S(2)}, u32[]{:S(2)}) collective-permute-start(bf16[512,128]{1,0:T(8,128)(2,1)S(1)} %bitcast.14), channel_id=1, source_target_pairs={{0,16},{8,24},{16,0},{24,8},{1,17},{9,25},{17,1},{25,9},{2,18},{10... | collective-permute-start | bytes 393224 | tf_op jit(solution)/shard_map/ppermute | solution.py:733
  68.5 26.2 %copy-start.6 = (bf16[144,1024]{1,0:T(8,128)(2,1)S(1)}, bf16[144,1024]{1,0:T(8,128)(2,1)}, u32[]{:S(2)}) copy-start(bf16[144,1024]{1,0:T(8,128)(2,1)} %get-tuple-element.140.refs_2_) | copy-start | bytes 884740
  68.5 37.8 %copy-start = (bf16[544,2048]{1,0:T(8,128)(2,1)S(1)}, bf16[544,2048]{1,0:T(8,128)(2,1)}, u32[]{:S(2)}) copy-start(bf16[544,2048]{1,0:T(8,128)(2,1)} %proj_ref.3) | copy-start | bytes 6684676
  68.5 37.8 %copy-start.4 = (f32[4,2048]{1,0:T(4,128)S(1)}, f32[4,2048]{1,0:T(4,128)}, u32[]{:S(2)}) copy-start(f32[4,2048]{1,0:T(4,128)} %refs_2_.1) | copy-start | bytes 98308
  68.5 37.8 %copy-start.9 = (bf16[3,2048]{1,0:T(4,128)(2,1)S(1)}, bf16[3,2048]{1,0:T(4,128)(2,1)}, u32[]{:S(2)}) copy-start(bf16[3,2048]{1,0:T(4,128)(2,1)} %copy-done.8) | copy-start | bytes 36868
  68.6 37.8 %copy-start.10 = (f32[2048]{0:T(1024)S(1)}, f32[2048]{0:T(1024)}, u32[]{:S(2)}) copy-start(f32[2048]{0:T(1024)} %param.14) | copy-start | bytes 24580
  82.4 24.0 %copy-start.2 = (bf16[128,2048]{1,0:T(8,128)(2,1)S(1)}, bf16[128,2048]{1,0:T(8,128)(2,1)}, u32[]{:S(2)}) copy-start(bf16[128,2048]{1,0:T(8,128)(2,1)} %input_ref.3) | copy-start | bytes 1572868
  82.4 24.0 %copy-start.3 = (bf16[128,2048]{1,0:T(8,128)(2,1)S(1)}, bf16[128,2048]{1,0:T(8,128)(2,1)}, u32[]{:S(2)}) copy-start(bf16[128,2048]{1,0:T(8,128)(2,1)} %get-tuple-element.129.scan_ref) | copy-start | bytes 1572868
  85.8 1.6 %collective-permute-start.12 = (bf16[640,128]{1,0:T(8,128)(2,1)}, bf16[640,128]{1,0:T(8,128)(2,1)S(1)}, u32[]{:S(2)}, u32[]{:S(2)}) collective-permute-start(bf16[640,128]{1,0:T(8,128)(2,1)} %get-tuple-element.125), channel_id=1, source_target_pairs={{0,1},{1,0},{2,3},{3,2},{4,5},{5,4},{6,7},{7,6},{8,9},{9,8},{10,11... | collective-permute-start | bytes 491528 | tf_op jit(solution)/shard_map/ppermute | solution.py:733
  88.4 6.3 %collective-permute-start.13 = (bf16[640,128]{1,0:T(8,128)(2,1)S(1)}, bf16[640,128]{1,0:T(8,128)(2,1)S(1)}, u32[]{:S(2)}, u32[]{:S(2)}) collective-permute-start(bf16[640,128]{1,0:T(8,128)(2,1)S(1)} %add_convert_fusion.1), channel_id=1, source_target_pairs={{0,2},{1,3},{2,0},{3,1},{4,6},{5,7},{6,4},{7,5},{8,10},{9,11},{10,... | collective-permute-start | bytes 491528 | tf_op jit(solution)/shard_map/ppermute | solution.py:733
  88.6 23.7 %collective-permute-start.19 = (bf16[144,1024]{1,0:T(8,128)(2,1)}, bf16[144,1024]{1,0:T(8,128)(2,1)S(1)}, u32[]{:S(2)}, u32[]{:S(2)}) collective-permute-start(bf16[144,1024]{1,0:T(8,128)(2,1)} %get-tuple-element.150.refs_2_), channel_id=1, source_target_pairs={{0,16},{8,24},{16,0},{24,8},{1,17},{9,25},{17,1},{25,9},{2,18},{10... | collective-permute-start | bytes 884744 | tf_op jit(solution)/shard_map/ppermute | solution.py:733
  95.5 16.8 %copy-start.5 = (bf16[144,1024]{1,0:T(8,128)(2,1)S(1)}, bf16[144,1024]{1,0:T(8,128)(2,1)}, u32[]{:S(2)}) copy-start(bf16[144,1024]{1,0:T(8,128)(2,1)} %get-tuple-element.150.refs_2_) | copy-start | bytes 884740
  95.5 16.8 %collective-permute-start.18 = (bf16[144,1024]{1,0:T(8,128)(2,1)S(1)}, bf16[144,1024]{1,0:T(8,128)(2,1)S(1)}, u32[]{:S(2)}, u32[]{:S(2)}) collective-permute-start(bf16[144,1024]{1,0:T(8,128)(2,1)S(1)} %get-tuple-element.143), channel_id=1, source_target_pairs={{0,8},{8,0},{16,24},{24,16},{1,9},{9,1},{17,25},{25,17},{2,10},{10... | collective-permute-start | bytes 884744 | tf_op jit(solution)/shard_map/ppermute | solution.py:733
  96.0 5.3 %collective-permute-start.14 = (bf16[640,128]{1,0:T(8,128)(2,1)S(1)}, bf16[640,128]{1,0:T(8,128)(2,1)S(1)}, u32[]{:S(2)}, u32[]{:S(2)}) collective-permute-start(bf16[640,128]{1,0:T(8,128)(2,1)S(1)} %add_convert_fusion.back_a), channel_id=1, source_target_pairs={{0,4},{1,5},{2,6},{3,7},{4,0},{5,1},{6,2},{7,3},{8,12},{9,13},{10,... | collective-permute-start | bytes 491528 | tf_op jit(solution)/shard_map/ppermute | solution.py:733
  101.4 10.9 %collective-permute-start.15 = (bf16[160,128]{1,0:T(8,128)(2,1)S(1)}, bf16[160,128]{1,0:T(8,128)(2,1)S(1)}, u32[]{:S(2)}, u32[]{:S(2)}) collective-permute-start(bf16[160,128]{1,0:T(8,128)(2,1)S(1)} %get-tuple-element.135), channel_id=1, source_target_pairs={{0,8},{8,0},{16,24},{24,16},{1,9},{9,1},{17,25},{25,17},{2,10},{10... | collective-permute-start | bytes 122888 | tf_op jit(solution)/shard_map/ppermute | solution.py:733
  103.0 9.3 %collective-permute-start.16 = (bf16[160,128]{1,0:T(8,128)(2,1)S(1)}, bf16[160,128]{1,0:T(8,128)(2,1)S(1)}, u32[]{:S(2)}, u32[]{:S(2)}) collective-permute-start(bf16[160,128]{1,0:T(8,128)(2,1)S(1)} %get-tuple-element.136), channel_id=1, source_target_pairs={{0,16},{8,24},{16,0},{24,8},{1,17},{9,25},{17,1},{25,9},{2,18},{10... | collective-permute-start | bytes 122888 | tf_op jit(solution)/shard_map/ppermute | solution.py:733
  105.0 14.4 %copy-start.1 = (bf16[128,2048]{1,0:T(8,128)(2,1)S(1)}, bf16[128,2048]{1,0:T(8,128)(2,1)}, u32[]{:S(2)}) copy-start(bf16[128,2048]{1,0:T(8,128)(2,1)} %get-tuple-element.158.refs_6_.refs_4_) | copy-start | bytes 1572868
  105.0 7.3 %collective-permute-start.17 = (bf16[160,128]{1,0:T(8,128)(2,1)S(1)}, bf16[160,128]{1,0:T(8,128)(2,1)S(1)}, u32[]{:S(2)}, u32[]{:S(2)}) collective-permute-start(bf16[160,128]{1,0:T(8,128)(2,1)S(1)} %get-tuple-element.137), channel_id=1, source_target_pairs={{0,24},{8,16},{16,8},{24,0},{1,25},{9,17},{17,9},{25,1},{2,26},{10... | collective-permute-start | bytes 122888 | tf_op jit(solution)/shard_map/ppermute | solution.py:733
  106.3 0.8 copy-start.7
  113.1 9.1 %collective-permute-start.23 = (bf16[144,1024]{1,0:T(8,128)(2,1)S(1)}, bf16[144,1024]{1,0:T(8,128)(2,1)S(1)}, u32[]{:S(2)}, u32[]{:S(2)}) collective-permute-start(bf16[144,1024]{1,0:T(8,128)(2,1)S(1)} %get-tuple-element.153), channel_id=1, source_target_pairs={{0,8},{8,0},{16,24},{24,16},{1,9},{9,1},{17,25},{25,17},{2,10},{10... | collective-permute-start | bytes 884744 | tf_op jit(solution)/shard_map/ppermute | solution.py:733
  113.8 12.2 %collective-permute-start.20 = (bf16[16,2048]{1,0:T(8,128)(2,1)S(1)}, bf16[16,2048]{1,0:T(8,128)(2,1)S(1)}, u32[]{:S(2)}, u32[]{:S(2)}) collective-permute-start(bf16[16,2048]{1,0:T(8,128)(2,1)S(1)} %get-tuple-element.168.refs_3_), channel_id=1, source_target_pairs={{0,8},{8,16},{16,24},{24,0},{1,9},{9,17},{17,25},{25,1},{2,10},{10... | collective-permute-start | bytes 196616 | tf_op jit(solution)/shard_map/ppermute | solution.py:52
  115.2 10.8 %collective-permute-start.21 = (bf16[16,2048]{1,0:T(8,128)(2,1)S(1)}, bf16[16,2048]{1,0:T(8,128)(2,1)S(1)}, u32[]{:S(2)}, u32[]{:S(2)}) collective-permute-start(bf16[16,2048]{1,0:T(8,128)(2,1)S(1)} %get-tuple-element.168.refs_3_), channel_id=1, source_target_pairs={{0,16},{8,24},{16,0},{24,8},{1,17},{9,25},{17,1},{25,9},{2,18},{10... | collective-permute-start | bytes 196616 | tf_op jit(solution)/shard_map/ppermute | solution.py:52
  117.2 8.7 %collective-permute-start.22 = (bf16[16,2048]{1,0:T(8,128)(2,1)S(1)}, bf16[16,2048]{1,0:T(8,128)(2,1)S(1)}, u32[]{:S(2)}, u32[]{:S(2)}) collective-permute-start(bf16[16,2048]{1,0:T(8,128)(2,1)S(1)} %get-tuple-element.168.refs_3_), channel_id=1, source_target_pairs={{0,24},{8,0},{16,8},{24,16},{1,25},{9,1},{17,9},{25,17},{2,26},{10... | collective-permute-start | bytes 196616 | tf_op jit(solution)/shard_map/ppermute | solution.py:52

commit v13 on v12

--- a/solution.py
+++ b/solution.py
@@ -441,7 +441,8 @@
     low_rank = step_weight.shape[0]
     chunks, states, groups, _ = decay.shape
     width = groups * 128
-    wide = padded(low_rank + 2 * states)
+    wide = (low_rank + 2 * states) // places
+    wide = (wide + 15) // 16 * 16 * places
     lead = lambda *shape: pl.BlockSpec((1,) + shape, lambda i: (chunk,) + (0,) * len(shape))
     here = lambda height: pl.BlockSpec((height, width), lambda i: (0, chunk))
     tall = pltpu.VMEM((rows * groups, 128), F32)
@@ -798,7 +799,7 @@
     messages = [swap(message, "ctx", mask) for mask, message in enumerate(messages, 1)]
     messages, blocks, low = tie((messages, blocks, low))
     blocks = spread_on(blocks)
-    lows = gather_near(jnp.transpose(low))
+    low = jnp.transpose(low)
     previous, steps = [], []
     for chunk in range(chunks):
         message, grad_gate, scan_part, small, part = scan_call(
@@ -809,15 +810,14 @@
         if chunk == 0:
             previous, blocks = tie((previous, blocks))
         else:
-            previous, steps[-1], lows = tie((previous, steps[-1], lows))
+            previous, steps[-1], low = tie((previous, steps[-1], low))
         steps.append(gather_near(message))
     part, grad_gate, scan_part, small = previous
     ranks = low_rank // places
     products = []
     backs = chan_sum(part)
-    if chunks > 1:
-        near, lows = tie((backs[0], lows))
-        backs = (near, backs[1])
+    lows = gather_near(low)
+    backs, lows = tie((backs, lows))
     for step in steps[:-1]:
         mine, theirs = step_call(ranks, lows, step)
         products += [mine, swap(theirs, "ctx", 1)]

time: 127 us -> 136 us (1.071)
  waiting for transfers between devices: 31.1 us -> 40.4 us
    ppermute x20, waiting for transfers between devices: 26.9 us -> 37.1 us  [swap(): lax.ppermute(block, axis, [(i, i ^ mask) for i in range(lax.axis_size(axi...]
  transfers between devices with their start and end apart: 24 -> 24, of which waited for: 12 -> 12; matrix products, arithmetic and copies ran while one was open for 1% -> 1% of each run, Pallas kernels for 38% -> 35%
where the time goes in v13:
time: 136 us
  Pallas kernels  53.4 us (39%)
  waiting for transfers between devices  40.4 us (30%)
  starting transfers between devices  34.9 us (26%)
  local copies, waits for them, and re-layouts  4.33 us (3%)
  other arithmetic  2.01 us (1%)
    ppermute x20, waiting for transfers between devices, swap(): lax.ppermute(block, axis, [(i, i ^ mask) for i in range(lax.axis_size(axi...  37.1 us
    pallas_call x2, Pallas kernels, scan_call(): pl.pallas_call(functools.partial(scan_kernel, places, states, first), gri...  27.3 us
    ppermute x20, starting transfers between devices, swap(): lax.ppermute(block, axis, [(i, i ^ mask) for i in range(lax.axis_size(axi...  24.9 us
    pallas_call x1, Pallas kernels, local_call(): pl.pallas_call(functools.partial(local_kernel, low_rank, states, places),...  11.7 us
    ppermute x3, starting transfers between devices, rotate(): lax.ppermute(block, axis, [(i, (i + distance) % count) for i in range(cou...  5.12 us
    pallas_call x1, Pallas kernels, conv_grad_call(): pl.pallas_call(functools.partial(conv_grad_kernel, places, low_rank), gri...  5.09 us
    ppermute x1, starting transfers between devices, shift(): return lax.ppermute(block, axis, route)  4.93 us
    pallas_call x1, Pallas kernels, conv_call(): pl.pallas_call(conv_kernel, grid=(chans // width,), in_specs=[columns(row...  4.15 us
  transfers between devices with their start and end apart: 24, of which 12 were waited for; matrix products, arithmetic and copies ran while one was open for 1% of the time, Pallas kernels for 35%

profile of v13, /device:TPU:0, one launch (start us, length us, event | category | flops | bytes accessed | tf_op | source)
XLA Modules:
  0.0 135.9 jit_solution(17696734487354744438)
XLA Ops:
  0.7 0.8 slice.9
  1.5 4.9 %collective-permute-start = (bf16[3,2048]{1,0:T(4,128)(2,1)S(1)}, bf16[3,2048]{1,0:T(4,128)(2,1)S(1)}, u32[]{:S(2)}, u32[]{:S(2)}) collective-permute-start(bf16[3,2048]{1,0:T(4,128)(2,1)S(1)} %slice.9), channel_id=1, source_target_pairs={{0,8},{8,16},{16,24},{1,9},{9,17},{17,25},{2,10},{10,18},{18,26},{... | collective-permute-start | bytes 36872 | tf_op jit(solution)/shard_map/ppermute | solution.py:58
  6.4 1.4 %collective-permute-done.rim_ref = bf16[3,2048]{1,0:T(4,128)(2,1)S(1)} collective-permute-done((bf16[3,2048]{1,0:T(4,128)(2,1)S(1)}, bf16[3,2048]{1,0:T(4,128)(2,1)S(1)}, u32[]{:S(2)}, u32[]{:S(2)}) %collective-permute-start) | collective-permute-done | bytes 12320 | tf_op jit(solution)/shard_map/ppermute | solution.py:58
  7.8 0.6 copy-done.8
  8.4 4.2 %conv_project.1 = (bf16[128,2048]{1,0:T(8,128)(2,1)}, bf16[128,544]{1,0:T(8,128)(2,1)}) custom-call(bf16[128,2048]{1,0:T(8,128)(2,1)} %input_ref.3, bf16[3,2048]{1,0:T(4,128)(2,1)} %copy-done.8, f32[4,2048]{1,0:T(4,128)} %refs_2_.1, f32[1,2048]{1,0:T(1,128)} %bitcast.17, bf16[544,2048]{1,0:T(8,128)(2,1)} %proj_ref.3), custom_call_target="tpu_custom_call" | custom-call | tf_op jit(solution)/shard_map/conv_project/pallas_call | solution.py:103
  12.6 0.0 collective-permute-start.1
  12.6 1.6 %collective-permute-done.1 = bf16[128,544]{1,0:T(8,128)(2,1)S(1)} collective-permute-done((bf16[128,544]{1,0:T(8,128)(2,1)}, bf16[128,544]{1,0:T(8,128)(2,1)S(1)}, u32[]{:S(2)}, u32[]{:S(2)}) %collective-permute-start.1) | collective-permute-done | bytes 139296 | tf_op jit(solution)/shard_map/ppermute | solution.py:734
  14.2 1.0 add_convert_fusion.1
  15.2 1.6 %collective-permute-start.2 = (bf16[128,544]{1,0:T(8,128)(2,1)S(1)}, bf16[128,544]{1,0:T(8,128)(2,1)S(1)}, u32[]{:S(2)}, u32[]{:S(2)}) collective-permute-start(bf16[128,544]{1,0:T(8,128)(2,1)S(1)} %add_convert_fusion.1), channel_id=1, source_target_pairs={{0,2},{1,3},{2,0},{3,1},{4,6},{5,7},{6,4},{7,5},{8,10},{9,11},{10,... | collective-permute-start | bytes 417800 | tf_op jit(solution)/shard_map/ppermute | solution.py:734
  16.7 3.3 %collective-permute-start.8 = (bf16[128,2048]{1,0:T(8,128)(2,1)}, bf16[128,2048]{1,0:T(8,128)(2,1)S(1)}, u32[]{:S(2)}, u32[]{:S(2)}) collective-permute-start(bf16[128,2048]{1,0:T(8,128)(2,1)} %get-tuple-element.158.refs_6_.refs_4_), channel_id=1, source_target_pairs={{0,16},{8,24},{16,0},{24,8},{1,17},{9,25},{17,1},{25,9},{2,18},{10... | collective-permute-start | bytes 1572872 | tf_op jit(solution)/shard_map/ppermute | solution.py:734
  20.0 1.6 %collective-permute-start.7 = (bf16[128,2048]{1,0:T(8,128)(2,1)}, bf16[128,2048]{1,0:T(8,128)(2,1)S(1)}, u32[]{:S(2)}, u32[]{:S(2)}) collective-permute-start(bf16[128,2048]{1,0:T(8,128)(2,1)} %get-tuple-element.158.refs_6_.refs_4_), channel_id=1, source_target_pairs={{0,8},{8,0},{16,24},{24,16},{1,9},{9,1},{17,25},{25,17},{2,10},{10... | collective-permute-start | bytes 1572872 | tf_op jit(solution)/shard_map/ppermute | solution.py:734
  21.6 0.0 collective-permute-done.2
  21.6 0.0 copy-start.11
  21.7 1.6 %collective-permute-start.3 = (bf16[128,544]{1,0:T(8,128)(2,1)S(1)}, bf16[128,544]{1,0:T(8,128)(2,1)S(1)}, u32[]{:S(2)}, u32[]{:S(2)}) collective-permute-start(bf16[128,544]{1,0:T(8,128)(2,1)S(1)} %add_convert_fusion.refs_0_), channel_id=1, source_target_pairs={{0,4},{1,5},{2,6},{3,7},{4,0},{5,1},{6,2},{7,3},{8,12},{9,13},{10,... | collective-permute-start | bytes 417800 | tf_op jit(solution)/shard_map/ppermute | solution.py:734
  23.3 0.7 copy.29
  23.9 3.2 %collective-permute-done.3.refs_1_ = bf16[128,544]{1,0:T(8,128)(2,1)S(1)} collective-permute-done((bf16[128,544]{1,0:T(8,128)(2,1)S(1)}, bf16[128,544]{1,0:T(8,128)(2,1)S(1)}, u32[]{:S(2)}, u32[]{:S(2)}) %collective-permute-start.3) | collective-permute-done | bytes 139296 | tf_op jit(solution)/shard_map/ppermute | solution.py:734
  27.1 0.7 reshape.36.refs_2_.refs_0_
  27.8 11.7 %local_ends.1 = (f32[2,128,8,128]{3,2,1,0:T(8,128)}, f32[2,128,8,128]{3,2,1,0:T(8,128)}, f32[2,128,8,128]{3,2,1,0:T(8,128)}, bf16[128,512]{1,0:T(8,128)(2,1)}, b...) custom-call(bf16[128,544]{1,0:T(8,128)(2,1)} %copy-done.11, ...), custom_call_target="tpu_custom_call" | custom-call | tf_op jit(solution)/shard_map/local_ends/pallas_call | solution.py:231
  39.5 2.2 %collective-permute-start.4 = (bf16[2,18,8,128]{3,2,1,0:T(8,128)(2,1)}, bf16[2,18,8,128]{3,2,1,0:T(8,128)(2,1)S(1)}, u32[]{:S(2)}, u32[]{:S(2)}) collective-permute-start(bf16[2,18,8,128]{3,2,1,0:T(8,128)(2,1)} %get-tuple-element.101), channel_id=1, source_target_pairs={{0,8},{8,0},{16,24},{24,16},{1,9},{9,1},{17,25},{25,17},{2,10},{10... | collective-permute-start | bytes 221192 | tf_op jit(solution)/shard_map/ppermute | solution.py:734
  41.8 2.6 %collective-permute-start.5 = (bf16[2,18,8,128]{3,2,1,0:T(8,128)(2,1)}, bf16[2,18,8,128]{3,2,1,0:T(8,128)(2,1)S(1)}, u32[]{:S(2)}, u32[]{:S(2)}) collective-permute-start(bf16[2,18,8,128]{3,2,1,0:T(8,128)(2,1)} %get-tuple-element.102), channel_id=1, source_target_pairs={{0,16},{8,24},{16,0},{24,8},{1,17},{9,25},{17,1},{25,9},{2,18},{10... | collective-permute-start | bytes 221192 | tf_op jit(solution)/shard_map/ppermute | solution.py:734
  44.3 0.0 collective-permute-start.6
  44.3 1.7 %collective-permute-done.4.refs_11_ = bf16[2,18,8,128]{3,2,1,0:T(8,128)(2,1)S(1)} collective-permute-done((bf16[2,18,8,128]{3,2,1,0:T(8,128)(2,1)}, bf16[2,18,8,128]{3,2,1,0:T(8,128)(2,1)S(1)}, u32[]{:S(2)}, u32[]{:S(2)}) %collective-permute-start.4) | collective-permute-done | bytes 73760 | tf_op jit(solution)/shard_map/ppermute | solution.py:734
  46.1 2.7 %collective-permute-done.5.refs_12_ = bf16[2,18,8,128]{3,2,1,0:T(8,128)(2,1)S(1)} collective-permute-done((bf16[2,18,8,128]{3,2,1,0:T(8,128)(2,1)}, bf16[2,18,8,128]{3,2,1,0:T(8,128)(2,1)S(1)}, u32[]{:S(2)}, u32[]{:S(2)}) %collective-permute-start.5) | collective-permute-done | bytes 73760 | tf_op jit(solution)/shard_map/ppermute | solution.py:734
  48.8 1.9 %collective-permute-done.6.refs_13_ = bf16[2,18,8,128]{3,2,1,0:T(8,128)(2,1)S(1)} collective-permute-done((bf16[2,18,8,128]{3,2,1,0:T(8,128)(2,1)}, bf16[2,18,8,128]{3,2,1,0:T(8,128)(2,1)S(1)}, u32[]{:S(2)}, u32[]{:S(2)}) %collective-permute-start.6) | collective-permute-done | bytes 73760 | tf_op jit(solution)/shard_map/ppermute | solution.py:734
  50.7 0.1 collective-permute-start.9
  50.8 0.5 copy-done.14
  51.3 13.6 %scan_gradients.2 = (bf16[144,1024]{1,0:T(8,128)(2,1)}, bf16[128,2048]{1,0:T(8,128)(2,1)}, bf16[128,2048]{1,0:T(8,128)(2,1)}, f32[8,2048]{1,0:T(8,128)}, f32[576,128]{1,0:T(8,128)}) custom-call(f32[4096]{0:T(1024)} %reshape.36.refs_2_.refs_0_, f32[2,128,8,128]{3,2,1,0:T(8,128)} %get-tuple-element.98.refs_1_, f32[2,128,8,128]{3,2,1,0:T(8,128)} %get-tuple-element.99.refs_2_, ...), custom_call_target="tpu_custom_call" | custom-call | tf_op jit(solution)/shard_map/scan_gradients/pallas_call | solution.py:468
  64.9 1.9 %collective-permute-start.10 = (bf16[144,1024]{1,0:T(8,128)(2,1)}, bf16[144,1024]{1,0:T(8,128)(2,1)S(1)}, u32[]{:S(2)}, u32[]{:S(2)}) collective-permute-start(bf16[144,1024]{1,0:T(8,128)(2,1)} %get-tuple-element.140.refs_2_), channel_id=1, source_target_pairs={{0,16},{8,24},{16,0},{24,8},{1,17},{9,25},{17,1},{25,9},{2,18},{10... | collective-permute-start | bytes 884744 | tf_op jit(solution)/shard_map/ppermute | solution.py:734
  66.8 0.1 copy.26
  66.9 0.0 copy-start
  67.0 0.0 copy-start.4
  67.0 0.0 copy-start.9
  67.0 0.0 copy-start.10
  67.0 13.7 %scan_gradients.3 = (bf16[144,1024]{1,0:T(8,128)(2,1)}, bf16[128,2048]{1,0:T(8,128)(2,1)}, bf16[128,2048]{1,0:T(8,128)(2,1)}, f32[8,2048]{1,0:T(8,128)}, bf16[576,128]{1,0:T(8,128)(2,1)}) custom-call(f32[4096]{0:T(1024)} %reshape.36.refs_2_.refs_0_, ...), custom_call_target="tpu_custom_call", output_to_operand_aliasing={{1}: (15, {}), {2}: (16, {}), {3}: (17, {})} | custom-call | tf_op jit(solution)/shard_map/scan_gradients/pallas_call | solution.py:468
  80.7 0.0 copy-start.3
  80.8 0.1 collective-permute-start.11
  80.8 1.6 %collective-permute-done.11 = bf16[576,128]{1,0:T(8,128)(2,1)S(1)} collective-permute-done((bf16[576,128]{1,0:T(8,128)(2,1)}, bf16[576,128]{1,0:T(8,128)(2,1)S(1)}, u32[]{:S(2)}, u32[]{:S(2)}) %collective-permute-start.11) | collective-permute-done | bytes 147488 | tf_op jit(solution)/shard_map/ppermute | solution.py:734
  82.4 1.0 add_convert_fusion.3
  83.4 0.8 collective-permute-start.12
  84.2 5.1 %collective-permute-done.12 = bf16[576,128]{1,0:T(8,128)(2,1)S(1)} collective-permute-done((bf16[576,128]{1,0:T(8,128)(2,1)S(1)}, bf16[576,128]{1,0:T(8,128)(2,1)S(1)}, u32[]{:S(2)}, u32[]{:S(2)}) %collective-permute-start.12) | collective-permute-done | bytes 147488 | tf_op jit(solution)/shard_map/ppermute | solution.py:734
  89.4 1.6 %collective-permute-start.13 = (bf16[576,128]{1,0:T(8,128)(2,1)S(1)}, bf16[576,128]{1,0:T(8,128)(2,1)S(1)}, u32[]{:S(2)}, u32[]{:S(2)}) collective-permute-start(bf16[576,128]{1,0:T(8,128)(2,1)S(1)} %add_convert_fusion.2.back_a), channel_id=1, source_target_pairs={{0,4},{1,5},{2,6},{3,7},{4,0},{5,1},{6,2},{7,3},{8,12},{9,13},{10,... | collective-permute-start | bytes 442376 | tf_op jit(solution)/shard_map/ppermute | solution.py:734
  91.0 1.3 collective-permute-start.14
  92.3 1.6 %collective-permute-start.19 = (bf16[144,1024]{1,0:T(8,128)(2,1)}, bf16[144,1024]{1,0:T(8,128)(2,1)S(1)}, u32[]{:S(2)}, u32[]{:S(2)}) collective-permute-start(bf16[144,1024]{1,0:T(8,128)(2,1)} %get-tuple-element.150.refs_2_), channel_id=1, source_target_pairs={{0,16},{8,24},{16,0},{24,8},{1,17},{9,25},{17,1},{25,9},{2,18},{10... | collective-permute-start | bytes 884744 | tf_op jit(solution)/shard_map/ppermute | solution.py:734
  93.9 12.5 %collective-permute-done.14.refs_1_ = bf16[512,128]{1,0:T(8,128)(2,1)S(1)} collective-permute-done((bf16[512,128]{1,0:T(8,128)(2,1)S(1)}, bf16[512,128]{1,0:T(8,128)(2,1)S(1)}, u32[]{:S(2)}, u32[]{:S(2)}) %collective-permute-start.14) | collective-permute-done | bytes 131104 | tf_op jit(solution)/shard_map/ppermute | solution.py:734
  106.4 0.7 step_products.2
  107.1 0.1 collective-permute-start.18
  107.2 0.1 cut_rows.1
  107.2 2.1 %collective-permute-start.15 = (bf16[144,128]{1,0:T(8,128)(2,1)S(1)}, bf16[144,128]{1,0:T(8,128)(2,1)S(1)}, u32[]{:S(2)}, u32[]{:S(2)}) collective-permute-start(bf16[144,128]{1,0:T(8,128)(2,1)S(1)} %get-tuple-element.135), channel_id=1, source_target_pairs={{0,8},{8,0},{16,24},{24,16},{1,9},{9,1},{17,25},{25,17},{2,10},{10... | collective-permute-start | bytes 110600 | tf_op jit(solution)/shard_map/ppermute | solution.py:734
  109.3 0.3 collective-permute-start.16
  109.6 2.1 %collective-permute-start.17 = (bf16[144,128]{1,0:T(8,128)(2,1)S(1)}, bf16[144,128]{1,0:T(8,128)(2,1)S(1)}, u32[]{:S(2)}, u32[]{:S(2)}) collective-permute-start(bf16[144,128]{1,0:T(8,128)(2,1)S(1)} %get-tuple-element.137), channel_id=1, source_target_pairs={{0,24},{8,16},{16,8},{24,0},{1,25},{9,17},{17,9},{25,1},{2,26},{10... | collective-permute-start | bytes 110600 | tf_op jit(solution)/shard_map/ppermute | solution.py:734
  111.8 0.0 copy-start.7
  111.8 0.8 copy-done.7
  112.6 5.1 %conv_gradients.1 = (bf16[128,2048]{1,0:T(8,128)(2,1)}, f32[16,2048]{1,0:T(8,128)S(1)}, bf16[16,2048]{1,0:T(8,128)(2,1)S(1)}) custom-call(bf16[576,128]{1,0:T(8,128)(2,1)S(1)} %add_convert_fusion.2.back_a, bf16[576,128]{1,0:T(8,128)(2,1)S(1)} %collective-permute-done.13.back_b, bf16[544,2048]{1,0:T(8,128)(2,1)S(1)} %copy-done, ...), custom_call_target="tpu_custom_call" | custom-call | tf_op jit(solution)/shard_map/conv_gradients/pallas_call | solution.py:555
  117.7 2.7 %collective-permute-done.15.refs_1_ = bf16[144,128]{1,0:T(8,128)(2,1)S(1)} collective-permute-done((bf16[144,128]{1,0:T(8,128)(2,1)S(1)}, bf16[144,128]{1,0:T(8,128)(2,1)S(1)}, u32[]{:S(2)}, u32[]{:S(2)}) %collective-permute-start.15) | collective-permute-done | bytes 36896 | tf_op jit(solution)/shard_map/ppermute | solution.py:734
  120.5 0.7 step_products.3
  121.2 0.1 collective-permute-start.23
  121.3 2.6 %collective-permute-start.22 = (bf16[16,2048]{1,0:T(8,128)(2,1)S(1)}, bf16[16,2048]{1,0:T(8,128)(2,1)S(1)}, u32[]{:S(2)}, u32[]{:S(2)}) collective-permute-start(bf16[16,2048]{1,0:T(8,128)(2,1)S(1)} %get-tuple-element.168.refs_3_), channel_id=1, source_target_pairs={{0,24},{8,0},{16,8},{24,16},{1,25},{9,1},{17,9},{25,17},{2,26},{10... | collective-permute-start | bytes 196616 | tf_op jit(solution)/shard_map/ppermute | solution.py:52
  123.9 0.9 collective-permute-start.21
  124.8 1.6 %collective-permute-start.20 = (bf16[16,2048]{1,0:T(8,128)(2,1)S(1)}, bf16[16,2048]{1,0:T(8,128)(2,1)S(1)}, u32[]{:S(2)}, u32[]{:S(2)}) collective-permute-start(bf16[16,2048]{1,0:T(8,128)(2,1)S(1)} %get-tuple-element.168.refs_3_), channel_id=1, source_target_pairs={{0,8},{8,16},{16,24},{24,0},{1,9},{9,17},{17,25},{25,1},{2,10},{10... | collective-permute-start | bytes 196616 | tf_op jit(solution)/shard_map/ppermute | solution.py:52
  126.4 1.9 %row_gradients.1 = (f32[128,2048]{1,0:T(8,128)}, f32[8,2048]{1,0:T(8,128)}) custom-call(bf16[144,128]{1,0:T(8,128)(2,1)S(1)} %get-tuple-element.154.refs_0_, bf16[144,128]{1,0:T(8,128)(2,1)S(1)} %collective-permute-done.15.refs_1_, bf16[144,128]{1,0:T(8,128)(2,1)S(1)} %collective-permute-done.16.refs_2_, ...), custom_call_target="tpu_custom_call" | custom-call | tf_op jit(solution)/shard_map/row_gradients/pallas_call | solution.py:646
  128.3 4.0 %collective-permute-done.23.refs_3_ = bf16[144,1024]{1,0:T(8,128)(2,1)S(1)} collective-permute-done((bf16[144,1024]{1,0:T(8,128)(2,1)S(1)}, bf16[144,1024]{1,0:T(8,128)(2,1)S(1)}, u32[]{:S(2)}, u32[]{:S(2)}) %collective-permute-start.23) | collective-permute-done | bytes 294944 | tf_op jit(solution)/shard_map/ppermute | solution.py:734
  132.3 1.1 step_gradients.1
  133.4 1.8 %collective-permute-done.20.refs_4_ = bf16[16,2048]{1,0:T(8,128)(2,1)S(1)} collective-permute-done((bf16[16,2048]{1,0:T(8,128)(2,1)S(1)}, bf16[16,2048]{1,0:T(8,128)(2,1)S(1)}, u32[]{:S(2)}, u32[]{:S(2)}) %collective-permute-start.20) | collective-permute-done | bytes 65568 | tf_op jit(solution)/shard_map/ppermute | solution.py:52
  135.2 0.7 last_rows.1
  (41 shorter events, 0.2 us)
Async XLA Ops:
  0.6 22.6 %copy-start.16 = (f32[16,2048]{1,0:T(8,128)S(1)}, f32[16,2048]{1,0:T(8,128)}, u32[]{:S(2)}) copy-start(f32[16,2048]{1,0:T(8,128)} %param.18) | copy-start | bytes 393220
  1.5 6.4 %collective-permute-start = (bf16[3,2048]{1,0:T(4,128)(2,1)S(1)}, bf16[3,2048]{1,0:T(4,128)(2,1)S(1)}, u32[]{:S(2)}, u32[]{:S(2)}) collective-permute-start(bf16[3,2048]{1,0:T(4,128)(2,1)S(1)} %slice.9), channel_id=1, source_target_pairs={{0,8},{8,16},{16,24},{1,9},{9,17},{17,25},{2,10},{10,18},{18,26},{... | collective-permute-start | bytes 36872 | tf_op jit(solution)/shard_map/ppermute | solution.py:58
  7.8 0.6 copy-start.8
  12.6 1.6 %collective-permute-start.1 = (bf16[128,544]{1,0:T(8,128)(2,1)}, bf16[128,544]{1,0:T(8,128)(2,1)S(1)}, u32[]{:S(2)}, u32[]{:S(2)}) collective-permute-start(bf16[128,544]{1,0:T(8,128)(2,1)} %get-tuple-element.96), channel_id=1, source_target_pairs={{0,1},{1,0},{2,3},{3,2},{4,5},{5,4},{6,7},{7,6},{8,9},{9,8},{10,11... | collective-permute-start | bytes 417800 | tf_op jit(solution)/shard_map/ppermute | solution.py:734
  15.2 6.4 %collective-permute-start.2 = (bf16[128,544]{1,0:T(8,128)(2,1)S(1)}, bf16[128,544]{1,0:T(8,128)(2,1)S(1)}, u32[]{:S(2)}, u32[]{:S(2)}) collective-permute-start(bf16[128,544]{1,0:T(8,128)(2,1)S(1)} %add_convert_fusion.1), channel_id=1, source_target_pairs={{0,2},{1,3},{2,0},{3,1},{4,6},{5,7},{6,4},{7,5},{8,10},{9,11},{10,... | collective-permute-start | bytes 417800 | tf_op jit(solution)/shard_map/ppermute | solution.py:734
  16.7 34.0 %collective-permute-start.8 = (bf16[128,2048]{1,0:T(8,128)(2,1)}, bf16[128,2048]{1,0:T(8,128)(2,1)S(1)}, u32[]{:S(2)}, u32[]{:S(2)}) collective-permute-start(bf16[128,2048]{1,0:T(8,128)(2,1)} %get-tuple-element.158.refs_6_.refs_4_), channel_id=1, source_target_pairs={{0,16},{8,24},{16,0},{24,8},{1,17},{9,25},{17,1},{25,9},{2,18},{10... | collective-permute-start | bytes 1572872 | tf_op jit(solution)/shard_map/ppermute | solution.py:734
  20.0 30.7 %collective-permute-start.7 = (bf16[128,2048]{1,0:T(8,128)(2,1)}, bf16[128,2048]{1,0:T(8,128)(2,1)S(1)}, u32[]{:S(2)}, u32[]{:S(2)}) collective-permute-start(bf16[128,2048]{1,0:T(8,128)(2,1)} %get-tuple-element.158.refs_6_.refs_4_), channel_id=1, source_target_pairs={{0,8},{8,0},{16,24},{24,16},{1,9},{9,1},{17,25},{25,17},{2,10},{10... | collective-permute-start | bytes 1572872 | tf_op jit(solution)/shard_map/ppermute | solution.py:734
  21.6 6.2 %copy-start.11 = (bf16[128,544]{1,0:T(8,128)(2,1)}, bf16[128,544]{1,0:T(8,128)(2,1)S(1)}, u32[]{:S(2)}) copy-start(bf16[128,544]{1,0:T(8,128)(2,1)S(1)} %add_convert_fusion.refs_0_) | copy-start | bytes 417796
  21.7 5.5 %collective-permute-start.3 = (bf16[128,544]{1,0:T(8,128)(2,1)S(1)}, bf16[128,544]{1,0:T(8,128)(2,1)S(1)}, u32[]{:S(2)}, u32[]{:S(2)}) collective-permute-start(bf16[128,544]{1,0:T(8,128)(2,1)S(1)} %add_convert_fusion.refs_0_), channel_id=1, source_target_pairs={{0,4},{1,5},{2,6},{3,7},{4,0},{5,1},{6,2},{7,3},{8,12},{9,13},{10,... | collective-permute-start | bytes 417800 | tf_op jit(solution)/shard_map/ppermute | solution.py:734
  27.1 0.7 copy-start.15
  39.5 6.6 %collective-permute-start.4 = (bf16[2,18,8,128]{3,2,1,0:T(8,128)(2,1)}, bf16[2,18,8,128]{3,2,1,0:T(8,128)(2,1)S(1)}, u32[]{:S(2)}, u32[]{:S(2)}) collective-permute-start(bf16[2,18,8,128]{3,2,1,0:T(8,128)(2,1)} %get-tuple-element.101), channel_id=1, source_target_pairs={{0,8},{8,0},{16,24},{24,16},{1,9},{9,1},{17,25},{25,17},{2,10},{10... | collective-permute-start | bytes 221192 | tf_op jit(solution)/shard_map/ppermute | solution.py:734
  41.8 7.1 %collective-permute-start.5 = (bf16[2,18,8,128]{3,2,1,0:T(8,128)(2,1)}, bf16[2,18,8,128]{3,2,1,0:T(8,128)(2,1)S(1)}, u32[]{:S(2)}, u32[]{:S(2)}) collective-permute-start(bf16[2,18,8,128]{3,2,1,0:T(8,128)(2,1)} %get-tuple-element.102), channel_id=1, source_target_pairs={{0,16},{8,24},{16,0},{24,8},{1,17},{9,25},{17,1},{25,9},{2,18},{10... | collective-permute-start | bytes 221192 | tf_op jit(solution)/shard_map/ppermute | solution.py:734
  44.3 6.4 %collective-permute-start.6 = (bf16[2,18,8,128]{3,2,1,0:T(8,128)(2,1)}, bf16[2,18,8,128]{3,2,1,0:T(8,128)(2,1)S(1)}, u32[]{:S(2)}, u32[]{:S(2)}) collective-permute-start(bf16[2,18,8,128]{3,2,1,0:T(8,128)(2,1)} %get-tuple-element.103), channel_id=1, source_target_pairs={{0,24},{8,16},{16,8},{24,0},{1,25},{9,17},{17,9},{25,1},{2,26},{10... | collective-permute-start | bytes 221192 | tf_op jit(solution)/shard_map/ppermute | solution.py:734
  46.1 4.7 %copy-start.12 = (bf16[2,18,8,128]{3,2,1,0:T(8,128)(2,1)}, bf16[2,18,8,128]{3,2,1,0:T(8,128)(2,1)S(1)}, u32[]{:S(2)}) copy-start(bf16[2,18,8,128]{3,2,1,0:T(8,128)(2,1)S(1)} %collective-permute-done.4.refs_11_) | copy-start | bytes 221188
  48.8 2.0 %copy-start.13 = (bf16[2,18,8,128]{3,2,1,0:T(8,128)(2,1)}, bf16[2,18,8,128]{3,2,1,0:T(8,128)(2,1)S(1)}, u32[]{:S(2)}) copy-start(bf16[2,18,8,128]{3,2,1,0:T(8,128)(2,1)S(1)} %collective-permute-done.5.refs_12_) | copy-start | bytes 221188
  50.7 0.6 copy-start.14
  50.7 16.2 %collective-permute-start.9 = (bf16[128,2048]{1,0:T(8,128)(2,1)S(1)}, bf16[128,2048]{1,0:T(8,128)(2,1)S(1)}, u32[]{:S(2)}, u32[]{:S(2)}) collective-permute-start(bf16[128,2048]{1,0:T(8,128)(2,1)S(1)} %collective-permute-done.8.refs_6_), channel_id=1, source_target_pairs={{0,8},{8,0},{16,24},{24,16},{1,9},{9,1},{17,25},{25,17},{2,10},{10... | collective-permute-start | bytes 1572872 | tf_op jit(solution)/shard_map/ppermute | solution.py:734
  51.3 15.5 %copy-start.17 = (bf16[128,512]{1,0:T(8,128)(2,1)S(1)}, bf16[128,512]{1,0:T(8,128)(2,1)}, u32[]{:S(2)}) copy-start(bf16[128,512]{1,0:T(8,128)(2,1)} %get-tuple-element.124) | copy-start | bytes 393220
  64.9 15.8 %collective-permute-start.10 = (bf16[144,1024]{1,0:T(8,128)(2,1)}, bf16[144,1024]{1,0:T(8,128)(2,1)S(1)}, u32[]{:S(2)}, u32[]{:S(2)}) collective-permute-start(bf16[144,1024]{1,0:T(8,128)(2,1)} %get-tuple-element.140.refs_2_), channel_id=1, source_target_pairs={{0,16},{8,24},{16,0},{24,8},{1,17},{9,25},{17,1},{25,9},{2,18},{10... | collective-permute-start | bytes 884744 | tf_op jit(solution)/shard_map/ppermute | solution.py:734
  66.9 39.4 %copy-start.6 = (bf16[144,1024]{1,0:T(8,128)(2,1)S(1)}, bf16[144,1024]{1,0:T(8,128)(2,1)}, u32[]{:S(2)}) copy-start(bf16[144,1024]{1,0:T(8,128)(2,1)} %get-tuple-element.140.refs_2_) | copy-start | bytes 884740
  66.9 44.8 %copy-start = (bf16[544,2048]{1,0:T(8,128)(2,1)S(1)}, bf16[544,2048]{1,0:T(8,128)(2,1)}, u32[]{:S(2)}) copy-start(bf16[544,2048]{1,0:T(8,128)(2,1)} %proj_ref.3) | copy-start | bytes 6684676
  67.0 44.8 %copy-start.4 = (f32[4,2048]{1,0:T(4,128)S(1)}, f32[4,2048]{1,0:T(4,128)}, u32[]{:S(2)}) copy-start(f32[4,2048]{1,0:T(4,128)} %refs_2_.1) | copy-start | bytes 98308
  67.0 44.8 %copy-start.9 = (bf16[3,2048]{1,0:T(4,128)(2,1)S(1)}, bf16[3,2048]{1,0:T(4,128)(2,1)}, u32[]{:S(2)}) copy-start(bf16[3,2048]{1,0:T(4,128)(2,1)} %copy-done.8) | copy-start | bytes 36868
  67.0 44.8 %copy-start.10 = (f32[2048]{0:T(1024)S(1)}, f32[2048]{0:T(1024)}, u32[]{:S(2)}) copy-start(f32[2048]{0:T(1024)} %param.14) | copy-start | bytes 24580
  80.7 31.0 %copy-start.2 = (bf16[128,2048]{1,0:T(8,128)(2,1)S(1)}, bf16[128,2048]{1,0:T(8,128)(2,1)}, u32[]{:S(2)}) copy-start(bf16[128,2048]{1,0:T(8,128)(2,1)} %input_ref.3) | copy-start | bytes 1572868
  80.7 31.0 %copy-start.3 = (bf16[128,2048]{1,0:T(8,128)(2,1)S(1)}, bf16[128,2048]{1,0:T(8,128)(2,1)}, u32[]{:S(2)}) copy-start(bf16[128,2048]{1,0:T(8,128)(2,1)} %get-tuple-element.129.scan_ref) | copy-start | bytes 1572868
  80.8 1.6 %collective-permute-start.11 = (bf16[576,128]{1,0:T(8,128)(2,1)}, bf16[576,128]{1,0:T(8,128)(2,1)S(1)}, u32[]{:S(2)}, u32[]{:S(2)}) collective-permute-start(bf16[576,128]{1,0:T(8,128)(2,1)} %get-tuple-element.125), channel_id=1, source_target_pairs={{0,1},{1,0},{2,3},{3,2},{4,5},{5,4},{6,7},{7,6},{8,9},{9,8},{10,11... | collective-permute-start | bytes 442376 | tf_op jit(solution)/shard_map/ppermute | solution.py:734
  83.4 6.0 %collective-permute-start.12 = (bf16[576,128]{1,0:T(8,128)(2,1)S(1)}, bf16[576,128]{1,0:T(8,128)(2,1)S(1)}, u32[]{:S(2)}, u32[]{:S(2)}) collective-permute-start(bf16[576,128]{1,0:T(8,128)(2,1)S(1)} %add_convert_fusion.3), channel_id=1, source_target_pairs={{0,2},{1,3},{2,0},{3,1},{4,6},{5,7},{6,4},{7,5},{8,10},{9,11},{10,... | collective-permute-start | bytes 442376 | tf_op jit(solution)/shard_map/ppermute | solution.py:734
  89.4 17.0 %collective-permute-start.13 = (bf16[576,128]{1,0:T(8,128)(2,1)S(1)}, bf16[576,128]{1,0:T(8,128)(2,1)S(1)}, u32[]{:S(2)}, u32[]{:S(2)}) collective-permute-start(bf16[576,128]{1,0:T(8,128)(2,1)S(1)} %add_convert_fusion.2.back_a), channel_id=1, source_target_pairs={{0,4},{1,5},{2,6},{3,7},{4,0},{5,1},{6,2},{7,3},{8,12},{9,13},{10,... | collective-permute-start | bytes 442376 | tf_op jit(solution)/shard_map/ppermute | solution.py:734
  91.0 15.4 %collective-permute-start.14 = (bf16[512,128]{1,0:T(8,128)(2,1)S(1)}, bf16[512,128]{1,0:T(8,128)(2,1)S(1)}, u32[]{:S(2)}, u32[]{:S(2)}) collective-permute-start(bf16[512,128]{1,0:T(8,128)(2,1)S(1)} %bitcast.14), channel_id=1, source_target_pairs={{0,16},{8,24},{16,0},{24,8},{1,17},{9,25},{17,1},{25,9},{2,18},{10... | collective-permute-start | bytes 393224 | tf_op jit(solution)/shard_map/ppermute | solution.py:734
  92.3 28.2 %copy-start.5 = (bf16[144,1024]{1,0:T(8,128)(2,1)S(1)}, bf16[144,1024]{1,0:T(8,128)(2,1)}, u32[]{:S(2)}) copy-start(bf16[144,1024]{1,0:T(8,128)(2,1)} %get-tuple-element.150.refs_2_) | copy-start | bytes 884740
  92.3 25.4 %collective-permute-start.19 = (bf16[144,1024]{1,0:T(8,128)(2,1)}, bf16[144,1024]{1,0:T(8,128)(2,1)S(1)}, u32[]{:S(2)}, u32[]{:S(2)}) collective-permute-start(bf16[144,1024]{1,0:T(8,128)(2,1)} %get-tuple-element.150.refs_2_), channel_id=1, source_target_pairs={{0,16},{8,24},{16,0},{24,8},{1,17},{9,25},{17,1},{25,9},{2,18},{10... | collective-permute-start | bytes 884744 | tf_op jit(solution)/shard_map/ppermute | solution.py:734
  107.1 13.4 %collective-permute-start.18 = (bf16[144,1024]{1,0:T(8,128)(2,1)S(1)}, bf16[144,1024]{1,0:T(8,128)(2,1)S(1)}, u32[]{:S(2)}, u32[]{:S(2)}) collective-permute-start(bf16[144,1024]{1,0:T(8,128)(2,1)S(1)} %get-tuple-element.143), channel_id=1, source_target_pairs={{0,8},{8,0},{16,24},{24,16},{1,9},{9,1},{17,25},{25,17},{2,10},{10... | collective-permute-start | bytes 884744 | tf_op jit(solution)/shard_map/ppermute | solution.py:734
  107.2 13.2 %collective-permute-start.15 = (bf16[144,128]{1,0:T(8,128)(2,1)S(1)}, bf16[144,128]{1,0:T(8,128)(2,1)S(1)}, u32[]{:S(2)}, u32[]{:S(2)}) collective-permute-start(bf16[144,128]{1,0:T(8,128)(2,1)S(1)} %get-tuple-element.135), channel_id=1, source_target_pairs={{0,8},{8,0},{16,24},{24,16},{1,9},{9,1},{17,25},{25,17},{2,10},{10... | collective-permute-start | bytes 110600 | tf_op jit(solution)/shard_map/ppermute | solution.py:734
  109.3 11.1 %collective-permute-start.16 = (bf16[144,128]{1,0:T(8,128)(2,1)S(1)}, bf16[144,128]{1,0:T(8,128)(2,1)S(1)}, u32[]{:S(2)}, u32[]{:S(2)}) collective-permute-start(bf16[144,128]{1,0:T(8,128)(2,1)S(1)} %get-tuple-element.136), channel_id=1, source_target_pairs={{0,16},{8,24},{16,0},{24,8},{1,17},{9,25},{17,1},{25,9},{2,18},{10... | collective-permute-start | bytes 110600 | tf_op jit(solution)/shard_map/ppermute | solution.py:734
  109.6 16.8 %copy-start.1 = (bf16[128,2048]{1,0:T(8,128)(2,1)S(1)}, bf16[128,2048]{1,0:T(8,128)(2,1)}, u32[]{:S(2)}) copy-start(bf16[128,2048]{1,0:T(8,128)(2,1)} %get-tuple-element.158.refs_6_.refs_4_) | copy-start | bytes 1572868
  109.6 10.8 %collective-permute-start.17 = (bf16[144,128]{1,0:T(8,128)(2,1)S(1)}, bf16[144,128]{1,0:T(8,128)(2,1)S(1)}, u32[]{:S(2)}, u32[]{:S(2)}) collective-permute-start(bf16[144,128]{1,0:T(8,128)(2,1)S(1)} %get-tuple-element.137), channel_id=1, source_target_pairs={{0,24},{8,16},{16,8},{24,0},{1,25},{9,17},{17,9},{25,1},{2,26},{10... | collective-permute-start | bytes 110600 | tf_op jit(solution)/shard_map/ppermute | solution.py:734
  111.8 0.8 copy-start.7
  121.2 11.1 %collective-permute-start.23 = (bf16[144,1024]{1,0:T(8,128)(2,1)S(1)}, bf16[144,1024]{1,0:T(8,128)(2,1)S(1)}, u32[]{:S(2)}, u32[]{:S(2)}) collective-permute-start(bf16[144,1024]{1,0:T(8,128)(2,1)S(1)} %get-tuple-element.153), channel_id=1, source_target_pairs={{0,8},{8,0},{16,24},{24,16},{1,9},{9,1},{17,25},{25,17},{2,10},{10... | collective-permute-start | bytes 884744 | tf_op jit(solution)/shard_map/ppermute | solution.py:734
  121.3 12.1 %collective-permute-start.22 = (bf16[16,2048]{1,0:T(8,128)(2,1)S(1)}, bf16[16,2048]{1,0:T(8,128)(2,1)S(1)}, u32[]{:S(2)}, u32[]{:S(2)}) collective-permute-start(bf16[16,2048]{1,0:T(8,128)(2,1)S(1)} %get-tuple-element.168.refs_3_), channel_id=1, source_target_pairs={{0,24},{8,0},{16,8},{24,16},{1,25},{9,1},{17,9},{25,17},{2,26},{10... | collective-permute-start | bytes 196616 | tf_op jit(solution)/shard_map/ppermute | solution.py:52
  123.9 9.5 %collective-permute-start.21 = (bf16[16,2048]{1,0:T(8,128)(2,1)S(1)}, bf16[16,2048]{1,0:T(8,128)(2,1)S(1)}, u32[]{:S(2)}, u32[]{:S(2)}) collective-permute-start(bf16[16,2048]{1,0:T(8,128)(2,1)S(1)} %get-tuple-element.168.refs_3_), channel_id=1, source_target_pairs={{0,16},{8,24},{16,0},{24,8},{1,17},{9,25},{17,1},{25,9},{2,18},{10... | collective-permute-start | bytes 196616 | tf_op jit(solution)/shard_map/ppermute | solution.py:52
  124.8 10.5 %collective-permute-start.20 = (bf16[16,2048]{1,0:T(8,128)(2,1)S(1)}, bf16[16,2048]{1,0:T(8,128)(2,1)S(1)}, u32[]{:S(2)}, u32[]{:S(2)}) collective-permute-start(bf16[16,2048]{1,0:T(8,128)(2,1)S(1)} %get-tuple-element.168.refs_3_), channel_id=1, source_target_pairs={{0,8},{8,16},{16,24},{24,0},{1,9},{9,17},{17,25},{25,1},{2,10},{10... | collective-permute-start | bytes 196616 | tf_op jit(solution)/shard_map/ppermute | solution.py:52

commit v14 on v12

--- a/solution.py
+++ b/solution.py
@@ -441,7 +441,8 @@
     low_rank = step_weight.shape[0]
     chunks, states, groups, _ = decay.shape
     width = groups * 128
-    wide = padded(low_rank + 2 * states)
+    wide = (low_rank + 2 * states) // places
+    wide = (wide + 15) // 16 * 16 * places
     lead = lambda *shape: pl.BlockSpec((1,) + shape, lambda i: (chunk,) + (0,) * len(shape))
     here = lambda height: pl.BlockSpec((height, width), lambda i: (0, chunk))
     tall = pltpu.VMEM((rows * groups, 128), F32)
@@ -601,12 +602,11 @@
     lows, steps, (mine_ref, theirs_ref) = refs[:near], refs[near : 2 * near], refs[2 * near :]
     place = lax.axis_index("ctx")
     rows = lows[0].shape[1]
-    pair = pl.ds(pl.multiple_of(lax.div(place, 2) * (2 * ranks), 16), 2 * ranks)
     odd = lax.rem(place, 2) == 1
     total = jnp.zeros((2 * ranks, mine_ref.shape[1]), F32)
     decay = jnp.zeros((mine_ref.shape[0] - ranks, mine_ref.shape[1]), F32)
     for low, step in zip(lows, steps):
-        total = total + dot(low[pair, :], step[:rows, :])
+        total = total + dot(low[...], step[:rows, :])
         decay = decay + step[rows:, :].astype(F32)
     mine_ref[:ranks, :] = jnp.where(odd, total[ranks:, :], total[:ranks, :])
     theirs_ref[:ranks, :] = jnp.where(odd, total[:ranks, :], total[ranks:, :]).astype(BF)
@@ -798,7 +798,14 @@
     messages = [swap(message, "ctx", mask) for mask, message in enumerate(messages, 1)]
     messages, blocks, low = tie((messages, blocks, low))
     blocks = spread_on(blocks)
-    lows = gather_near(jnp.transpose(low))
+    ranks = low_rank // places
+    lows = [
+        lax.dynamic_slice_in_dim(
+            jnp.transpose(low), ((lax.axis_index("ctx") ^ mask) // 2) * 2 * ranks, 2 * ranks
+        )
+        for mask in range(0, places, 2)
+    ]
+    lows = lows[:1] + [swap(rows_, "ctx", 2 * k) for k, rows_ in enumerate(lows[1:], 1)]
     previous, steps = [], []
     for chunk in range(chunks):
         message, grad_gate, scan_part, small, part = scan_call(

time: 127 us -> 123 us (0.969)
  waiting for transfers between devices: 31.1 us -> 25.9 us
    ppermute x20, waiting for transfers between devices: 26.9 us -> 21.9 us  [swap(): lax.ppermute(block, axis, [(i, i ^ mask) for i in range(lax.axis_size(axi...]
    ppermute x20, starting transfers between devices: 24.7 us -> 26.3 us  [swap(): lax.ppermute(block, axis, [(i, i ^ mask) for i in range(lax.axis_size(axi...]
  transfers between devices with their start and end apart: 24 -> 24, of which waited for: 12 -> 12; matrix products, arithmetic and copies ran while one was open for 1% -> 1% of each run, Pallas kernels for 38% -> 39%
where the time goes in v14:
time: 123 us
  Pallas kernels  53.4 us (43%)
  starting transfers between devices  36.1 us (29%)
  waiting for transfers between devices  25.9 us (21%)
  local copies, waits for them, and re-layouts  4.34 us (4%)
  other arithmetic  2.01 us (2%)
    pallas_call x2, Pallas kernels, scan_call(): pl.pallas_call(functools.partial(scan_kernel, places, states, first), gri...  27.3 us
    ppermute x20, starting transfers between devices, swap(): lax.ppermute(block, axis, [(i, i ^ mask) for i in range(lax.axis_size(axi...  26.3 us
    ppermute x20, waiting for transfers between devices, swap(): lax.ppermute(block, axis, [(i, i ^ mask) for i in range(lax.axis_size(axi...  21.9 us
    pallas_call x1, Pallas kernels, local_call(): pl.pallas_call(functools.partial(local_kernel, low_rank, states, places),...  11.7 us
    pallas_call x1, Pallas kernels, conv_grad_call(): pl.pallas_call(functools.partial(conv_grad_kernel, places, low_rank), gri...  5.09 us
    ppermute x1, starting transfers between devices, shift(): return lax.ppermute(block, axis, route)  4.93 us
    ppermute x3, starting transfers between devices, rotate(): lax.ppermute(block, axis, [(i, (i + distance) % count) for i in range(cou...  4.89 us
    pallas_call x1, Pallas kernels, conv_call(): pl.pallas_call(conv_kernel, grid=(chans // width,), in_specs=[columns(row...  4.15 us
  transfers between devices with their start and end apart: 24, of which 12 were waited for; matrix products, arithmetic and copies ran while one was open for 1% of the time, Pallas kernels for 39%

profile of v14, /device:TPU:0, one launch (start us, length us, event | category | flops | bytes accessed | tf_op | source)
XLA Modules:
  0.0 122.7 jit_solution(1369690015488563818)
XLA Ops:
  0.7 0.8 slice.9
  1.5 4.9 %collective-permute-start = (bf16[3,2048]{1,0:T(4,128)(2,1)S(1)}, bf16[3,2048]{1,0:T(4,128)(2,1)S(1)}, u32[]{:S(2)}, u32[]{:S(2)}) collective-permute-start(bf16[3,2048]{1,0:T(4,128)(2,1)S(1)} %slice.9), channel_id=1, source_target_pairs={{0,8},{8,16},{16,24},{1,9},{9,17},{17,25},{2,10},{10,18},{18,26},{... | collective-permute-start | bytes 36872 | tf_op jit(solution)/shard_map/ppermute | solution.py:58
  6.4 1.4 %collective-permute-done.rim_ref = bf16[3,2048]{1,0:T(4,128)(2,1)S(1)} collective-permute-done((bf16[3,2048]{1,0:T(4,128)(2,1)S(1)}, bf16[3,2048]{1,0:T(4,128)(2,1)S(1)}, u32[]{:S(2)}, u32[]{:S(2)}) %collective-permute-start) | collective-permute-done | bytes 12320 | tf_op jit(solution)/shard_map/ppermute | solution.py:58
  7.8 0.6 copy-done.8
  8.4 4.2 %conv_project.1 = (bf16[128,2048]{1,0:T(8,128)(2,1)}, bf16[128,544]{1,0:T(8,128)(2,1)}) custom-call(bf16[128,2048]{1,0:T(8,128)(2,1)} %input_ref.3, bf16[3,2048]{1,0:T(4,128)(2,1)} %copy-done.8, f32[4,2048]{1,0:T(4,128)} %refs_2_.1, f32[1,2048]{1,0:T(1,128)} %bitcast.17, bf16[544,2048]{1,0:T(8,128)(2,1)} %proj_ref.3), custom_call_target="tpu_custom_call" | custom-call | tf_op jit(solution)/shard_map/conv_project/pallas_call | solution.py:103
  12.6 0.0 collective-permute-start.1
  12.6 1.6 %collective-permute-done.1 = bf16[128,544]{1,0:T(8,128)(2,1)S(1)} collective-permute-done((bf16[128,544]{1,0:T(8,128)(2,1)}, bf16[128,544]{1,0:T(8,128)(2,1)S(1)}, u32[]{:S(2)}, u32[]{:S(2)}) %collective-permute-start.1) | collective-permute-done | bytes 139296 | tf_op jit(solution)/shard_map/ppermute | solution.py:733
  14.2 1.0 add_convert_fusion.1
  15.2 1.6 %collective-permute-start.2 = (bf16[128,544]{1,0:T(8,128)(2,1)S(1)}, bf16[128,544]{1,0:T(8,128)(2,1)S(1)}, u32[]{:S(2)}, u32[]{:S(2)}) collective-permute-start(bf16[128,544]{1,0:T(8,128)(2,1)S(1)} %add_convert_fusion.1), channel_id=1, source_target_pairs={{0,2},{1,3},{2,0},{3,1},{4,6},{5,7},{6,4},{7,5},{8,10},{9,11},{10,... | collective-permute-start | bytes 417800 | tf_op jit(solution)/shard_map/ppermute | solution.py:733
  16.7 3.3 %collective-permute-start.8 = (bf16[128,2048]{1,0:T(8,128)(2,1)}, bf16[128,2048]{1,0:T(8,128)(2,1)S(1)}, u32[]{:S(2)}, u32[]{:S(2)}) collective-permute-start(bf16[128,2048]{1,0:T(8,128)(2,1)} %get-tuple-element.158.refs_6_.refs_4_), channel_id=1, source_target_pairs={{0,16},{8,24},{16,0},{24,8},{1,17},{9,25},{17,1},{25,9},{2,18},{10... | collective-permute-start | bytes 1572872 | tf_op jit(solution)/shard_map/ppermute | solution.py:733
  20.0 1.6 %collective-permute-start.7 = (bf16[128,2048]{1,0:T(8,128)(2,1)}, bf16[128,2048]{1,0:T(8,128)(2,1)S(1)}, u32[]{:S(2)}, u32[]{:S(2)}) collective-permute-start(bf16[128,2048]{1,0:T(8,128)(2,1)} %get-tuple-element.158.refs_6_.refs_4_), channel_id=1, source_target_pairs={{0,8},{8,0},{16,24},{24,16},{1,9},{9,1},{17,25},{25,17},{2,10},{10... | collective-permute-start | bytes 1572872 | tf_op jit(solution)/shard_map/ppermute | solution.py:733
  21.6 0.0 copy-start.11
  21.7 1.6 %collective-permute-start.3 = (bf16[128,544]{1,0:T(8,128)(2,1)S(1)}, bf16[128,544]{1,0:T(8,128)(2,1)S(1)}, u32[]{:S(2)}, u32[]{:S(2)}) collective-permute-start(bf16[128,544]{1,0:T(8,128)(2,1)S(1)} %add_convert_fusion.refs_0_), channel_id=1, source_target_pairs={{0,4},{1,5},{2,6},{3,7},{4,0},{5,1},{6,2},{7,3},{8,12},{9,13},{10,... | collective-permute-start | bytes 417800 | tf_op jit(solution)/shard_map/ppermute | solution.py:733
  23.3 0.7 copy.31
  23.9 3.2 %collective-permute-done.3.refs_1_ = bf16[128,544]{1,0:T(8,128)(2,1)S(1)} collective-permute-done((bf16[128,544]{1,0:T(8,128)(2,1)S(1)}, bf16[128,544]{1,0:T(8,128)(2,1)S(1)}, u32[]{:S(2)}, u32[]{:S(2)}) %collective-permute-start.3) | collective-permute-done | bytes 139296 | tf_op jit(solution)/shard_map/ppermute | solution.py:733
  27.1 0.7 reshape.36.refs_2_.refs_0_
  27.8 11.7 %local_ends.1 = (f32[2,128,8,128]{3,2,1,0:T(8,128)}, f32[2,128,8,128]{3,2,1,0:T(8,128)}, f32[2,128,8,128]{3,2,1,0:T(8,128)}, bf16[128,512]{1,0:T(8,128)(2,1)}, b...) custom-call(bf16[128,544]{1,0:T(8,128)(2,1)} %copy-done.11, ...), custom_call_target="tpu_custom_call" | custom-call | tf_op jit(solution)/shard_map/local_ends/pallas_call | solution.py:231
  39.5 2.2 %collective-permute-start.4 = (bf16[2,18,8,128]{3,2,1,0:T(8,128)(2,1)}, bf16[2,18,8,128]{3,2,1,0:T(8,128)(2,1)S(1)}, u32[]{:S(2)}, u32[]{:S(2)}) collective-permute-start(bf16[2,18,8,128]{3,2,1,0:T(8,128)(2,1)} %get-tuple-element.101), channel_id=1, source_target_pairs={{0,8},{8,0},{16,24},{24,16},{1,9},{9,1},{17,25},{25,17},{2,10},{10... | collective-permute-start | bytes 221192 | tf_op jit(solution)/shard_map/ppermute | solution.py:733
  41.8 2.6 %collective-permute-start.5 = (bf16[2,18,8,128]{3,2,1,0:T(8,128)(2,1)}, bf16[2,18,8,128]{3,2,1,0:T(8,128)(2,1)S(1)}, u32[]{:S(2)}, u32[]{:S(2)}) collective-permute-start(bf16[2,18,8,128]{3,2,1,0:T(8,128)(2,1)} %get-tuple-element.102), channel_id=1, source_target_pairs={{0,16},{8,24},{16,0},{24,8},{1,17},{9,25},{17,1},{25,9},{2,18},{10... | collective-permute-start | bytes 221192 | tf_op jit(solution)/shard_map/ppermute | solution.py:733
  44.4 1.7 %collective-permute-done.4.refs_11_ = bf16[2,18,8,128]{3,2,1,0:T(8,128)(2,1)S(1)} collective-permute-done((bf16[2,18,8,128]{3,2,1,0:T(8,128)(2,1)}, bf16[2,18,8,128]{3,2,1,0:T(8,128)(2,1)S(1)}, u32[]{:S(2)}, u32[]{:S(2)}) %collective-permute-start.4) | collective-permute-done | bytes 73760 | tf_op jit(solution)/shard_map/ppermute | solution.py:733
  46.1 2.7 %collective-permute-done.5.refs_12_ = bf16[2,18,8,128]{3,2,1,0:T(8,128)(2,1)S(1)} collective-permute-done((bf16[2,18,8,128]{3,2,1,0:T(8,128)(2,1)}, bf16[2,18,8,128]{3,2,1,0:T(8,128)(2,1)S(1)}, u32[]{:S(2)}, u32[]{:S(2)}) %collective-permute-start.5) | collective-permute-done | bytes 73760 | tf_op jit(solution)/shard_map/ppermute | solution.py:733
  48.8 1.9 %collective-permute-done.6.refs_13_ = bf16[2,18,8,128]{3,2,1,0:T(8,128)(2,1)S(1)} collective-permute-done((bf16[2,18,8,128]{3,2,1,0:T(8,128)(2,1)}, bf16[2,18,8,128]{3,2,1,0:T(8,128)(2,1)S(1)}, u32[]{:S(2)}, u32[]{:S(2)}) %collective-permute-start.6) | collective-permute-done | bytes 73760 | tf_op jit(solution)/shard_map/ppermute | solution.py:733
  50.7 0.0 collective-permute-done.8.refs_6_
  50.7 0.0 collective-permute-done.7.refs_5_
  50.7 0.1 collective-permute-start.9
  50.8 0.5 copy-done.14
  51.3 13.6 %scan_gradients.2 = (bf16[144,1024]{1,0:T(8,128)(2,1)}, bf16[128,2048]{1,0:T(8,128)(2,1)}, bf16[128,2048]{1,0:T(8,128)(2,1)}, f32[8,2048]{1,0:T(8,128)}, f32[576,128]{1,0:T(8,128)}) custom-call(f32[4096]{0:T(1024)} %reshape.36.refs_2_.refs_0_, f32[2,128,8,128]{3,2,1,0:T(8,128)} %get-tuple-element.98.refs_1_, f32[2,128,8,128]{3,2,1,0:T(8,128)} %get-tuple-element.99.refs_2_, ...), custom_call_target="tpu_custom_call" | custom-call | tf_op jit(solution)/shard_map/scan_gradients/pallas_call | solution.py:468
  64.9 1.9 %collective-permute-start.10 = (bf16[144,1024]{1,0:T(8,128)(2,1)}, bf16[144,1024]{1,0:T(8,128)(2,1)S(1)}, u32[]{:S(2)}, u32[]{:S(2)}) collective-permute-start(bf16[144,1024]{1,0:T(8,128)(2,1)} %get-tuple-element.140.refs_2_), channel_id=1, source_target_pairs={{0,16},{8,24},{16,0},{24,8},{1,17},{9,25},{17,1},{25,9},{2,18},{10... | collective-permute-start | bytes 884744 | tf_op jit(solution)/shard_map/ppermute | solution.py:733
  66.8 0.1 copy.27
  67.0 1.1 collective-permute-start.11
  68.1 0.0 copy-start.9
  68.1 0.0 copy-start.10
  68.1 13.7 %scan_gradients.3 = (bf16[144,1024]{1,0:T(8,128)(2,1)}, bf16[128,2048]{1,0:T(8,128)(2,1)}, bf16[128,2048]{1,0:T(8,128)(2,1)}, f32[8,2048]{1,0:T(8,128)}, bf16[576,128]{1,0:T(8,128)(2,1)}) custom-call(f32[4096]{0:T(1024)} %reshape.36.refs_2_.refs_0_, ...), custom_call_target="tpu_custom_call", output_to_operand_aliasing={{1}: (15, {}), {2}: (16, {}), {3}: (17, {})} | custom-call | tf_op jit(solution)/shard_map/scan_gradients/pallas_call | solution.py:468
  81.9 0.0 copy-start.3
  81.9 0.0 collective-permute-done.11.refs_1_
  81.9 0.1 collective-permute-start.12
  82.0 1.6 %collective-permute-done.12 = bf16[576,128]{1,0:T(8,128)(2,1)S(1)} collective-permute-done((bf16[576,128]{1,0:T(8,128)(2,1)}, bf16[576,128]{1,0:T(8,128)(2,1)S(1)}, u32[]{:S(2)}, u32[]{:S(2)}) %collective-permute-start.12) | collective-permute-done | bytes 147488 | tf_op jit(solution)/shard_map/ppermute | solution.py:733
  83.5 1.0 add_convert_fusion.3
  84.5 2.1 %collective-permute-start.13 = (bf16[576,128]{1,0:T(8,128)(2,1)S(1)}, bf16[576,128]{1,0:T(8,128)(2,1)S(1)}, u32[]{:S(2)}, u32[]{:S(2)}) collective-permute-start(bf16[576,128]{1,0:T(8,128)(2,1)S(1)} %add_convert_fusion.3), channel_id=1, source_target_pairs={{0,2},{1,3},{2,0},{3,1},{4,6},{5,7},{6,4},{7,5},{8,10},{9,11},{10,... | collective-permute-start | bytes 442376 | tf_op jit(solution)/shard_map/ppermute | solution.py:733
  86.6 0.6 collective-permute-start.19
  87.2 3.5 %collective-permute-done.13 = bf16[576,128]{1,0:T(8,128)(2,1)S(1)} collective-permute-done((bf16[576,128]{1,0:T(8,128)(2,1)S(1)}, bf16[576,128]{1,0:T(8,128)(2,1)S(1)}, u32[]{:S(2)}, u32[]{:S(2)}) %collective-permute-start.13) | collective-permute-done | bytes 147488 | tf_op jit(solution)/shard_map/ppermute | solution.py:733
  90.8 0.7 step_products.2
  91.5 1.6 %collective-permute-start.18 = (bf16[144,1024]{1,0:T(8,128)(2,1)S(1)}, bf16[144,1024]{1,0:T(8,128)(2,1)S(1)}, u32[]{:S(2)}, u32[]{:S(2)}) collective-permute-start(bf16[144,1024]{1,0:T(8,128)(2,1)S(1)} %get-tuple-element.143), channel_id=1, source_target_pairs={{0,8},{8,0},{16,24},{24,16},{1,9},{9,1},{17,25},{25,17},{2,10},{10... | collective-permute-start | bytes 884744 | tf_op jit(solution)/shard_map/ppermute | solution.py:733
  93.1 1.5 %collective-permute-start.14 = (bf16[576,128]{1,0:T(8,128)(2,1)S(1)}, bf16[576,128]{1,0:T(8,128)(2,1)S(1)}, u32[]{:S(2)}, u32[]{:S(2)}) collective-permute-start(bf16[576,128]{1,0:T(8,128)(2,1)S(1)} %add_convert_fusion.2.back_a), channel_id=1, source_target_pairs={{0,4},{1,5},{2,6},{3,7},{4,0},{5,1},{6,2},{7,3},{8,12},{9,13},{10,... | collective-permute-start | bytes 442376 | tf_op jit(solution)/shard_map/ppermute | solution.py:733
  94.6 3.6 %collective-permute-done.14.back_b = bf16[576,128]{1,0:T(8,128)(2,1)S(1)} collective-permute-done((bf16[576,128]{1,0:T(8,128)(2,1)S(1)}, bf16[576,128]{1,0:T(8,128)(2,1)S(1)}, u32[]{:S(2)}, u32[]{:S(2)}) %collective-permute-start.14) | collective-permute-done | bytes 147488 | tf_op jit(solution)/shard_map/ppermute | solution.py:733
  98.3 0.1 cut_rows.1
  98.3 0.6 collective-permute-start.15
  98.9 1.6 %collective-permute-start.16 = (bf16[144,128]{1,0:T(8,128)(2,1)S(1)}, bf16[144,128]{1,0:T(8,128)(2,1)S(1)}, u32[]{:S(2)}, u32[]{:S(2)}) collective-permute-start(bf16[144,128]{1,0:T(8,128)(2,1)S(1)} %get-tuple-element.136), channel_id=1, source_target_pairs={{0,16},{8,24},{16,0},{24,8},{1,17},{9,25},{17,1},{25,9},{2,18},{10... | collective-permute-start | bytes 110600 | tf_op jit(solution)/shard_map/ppermute | solution.py:733
  100.5 2.3 %collective-permute-start.17 = (bf16[144,128]{1,0:T(8,128)(2,1)S(1)}, bf16[144,128]{1,0:T(8,128)(2,1)S(1)}, u32[]{:S(2)}, u32[]{:S(2)}) collective-permute-start(bf16[144,128]{1,0:T(8,128)(2,1)S(1)} %get-tuple-element.137), channel_id=1, source_target_pairs={{0,24},{8,16},{16,8},{24,0},{1,25},{9,17},{17,9},{25,1},{2,26},{10... | collective-permute-start | bytes 110600 | tf_op jit(solution)/shard_map/ppermute | solution.py:733
  102.8 0.0 copy-start.7
  102.8 0.8 copy-done.7
  103.7 5.1 %conv_gradients.1 = (bf16[128,2048]{1,0:T(8,128)(2,1)}, f32[16,2048]{1,0:T(8,128)S(1)}, bf16[16,2048]{1,0:T(8,128)(2,1)S(1)}) custom-call(bf16[576,128]{1,0:T(8,128)(2,1)S(1)} %add_convert_fusion.2.back_a, bf16[576,128]{1,0:T(8,128)(2,1)S(1)} %collective-permute-done.14.back_b, bf16[544,2048]{1,0:T(8,128)(2,1)S(1)} %copy-done, ...), custom_call_target="tpu_custom_call" | custom-call | tf_op jit(solution)/shard_map/conv_gradients/pallas_call | solution.py:555
  108.7 0.0 collective-permute-done.19.refs_3_
  108.8 0.7 step_products.3
  109.5 0.1 collective-permute-start.23
  109.6 2.4 %collective-permute-start.22 = (bf16[16,2048]{1,0:T(8,128)(2,1)S(1)}, bf16[16,2048]{1,0:T(8,128)(2,1)S(1)}, u32[]{:S(2)}, u32[]{:S(2)}) collective-permute-start(bf16[16,2048]{1,0:T(8,128)(2,1)S(1)} %get-tuple-element.168.refs_3_), channel_id=1, source_target_pairs={{0,24},{8,0},{16,8},{24,16},{1,25},{9,1},{17,9},{25,17},{2,26},{10... | collective-permute-start | bytes 196616 | tf_op jit(solution)/shard_map/ppermute | solution.py:52
  112.0 1.1 collective-permute-start.21
  113.1 1.4 %collective-permute-start.20 = (bf16[16,2048]{1,0:T(8,128)(2,1)S(1)}, bf16[16,2048]{1,0:T(8,128)(2,1)S(1)}, u32[]{:S(2)}, u32[]{:S(2)}) collective-permute-start(bf16[16,2048]{1,0:T(8,128)(2,1)S(1)} %get-tuple-element.168.refs_3_), channel_id=1, source_target_pairs={{0,8},{8,16},{16,24},{24,0},{1,9},{9,17},{17,25},{25,1},{2,10},{10... | collective-permute-start | bytes 196616 | tf_op jit(solution)/shard_map/ppermute | solution.py:52
  114.5 1.9 %row_gradients.1 = (f32[128,2048]{1,0:T(8,128)}, f32[8,2048]{1,0:T(8,128)}) custom-call(bf16[144,128]{1,0:T(8,128)(2,1)S(1)} %get-tuple-element.154.refs_0_, bf16[144,128]{1,0:T(8,128)(2,1)S(1)} %collective-permute-done.15.refs_1_, bf16[144,128]{1,0:T(8,128)(2,1)S(1)} %collective-permute-done.16.refs_2_, ...), custom_call_target="tpu_custom_call" | custom-call | tf_op jit(solution)/shard_map/row_gradients/pallas_call | solution.py:645
  116.4 2.0 %collective-permute-done.23.refs_3_ = bf16[144,1024]{1,0:T(8,128)(2,1)S(1)} collective-permute-done((bf16[144,1024]{1,0:T(8,128)(2,1)S(1)}, bf16[144,1024]{1,0:T(8,128)(2,1)S(1)}, u32[]{:S(2)}, u32[]{:S(2)}) %collective-permute-start.23) | collective-permute-done | bytes 294944 | tf_op jit(solution)/shard_map/ppermute | solution.py:733
  118.4 1.1 step_gradients.1
  119.5 0.2 collective-permute-done.22.refs_6_
  119.7 2.3 %collective-permute-done.20.refs_4_ = bf16[16,2048]{1,0:T(8,128)(2,1)S(1)} collective-permute-done((bf16[16,2048]{1,0:T(8,128)(2,1)S(1)}, bf16[16,2048]{1,0:T(8,128)(2,1)S(1)}, u32[]{:S(2)}, u32[]{:S(2)}) %collective-permute-start.20) | collective-permute-done | bytes 65568 | tf_op jit(solution)/shard_map/ppermute | solution.py:52
  122.0 0.7 last_rows.1
  (42 shorter events, 0.2 us)
Async XLA Ops:
  0.6 22.6 %copy-start.16 = (f32[16,2048]{1,0:T(8,128)S(1)}, f32[16,2048]{1,0:T(8,128)}, u32[]{:S(2)}) copy-start(f32[16,2048]{1,0:T(8,128)} %param.18) | copy-start | bytes 393220
  1.5 6.4 %collective-permute-start = (bf16[3,2048]{1,0:T(4,128)(2,1)S(1)}, bf16[3,2048]{1,0:T(4,128)(2,1)S(1)}, u32[]{:S(2)}, u32[]{:S(2)}) collective-permute-start(bf16[3,2048]{1,0:T(4,128)(2,1)S(1)} %slice.9), channel_id=1, source_target_pairs={{0,8},{8,16},{16,24},{1,9},{9,17},{17,25},{2,10},{10,18},{18,26},{... | collective-permute-start | bytes 36872 | tf_op jit(solution)/shard_map/ppermute | solution.py:58
  7.8 0.6 copy-start.8
  12.6 1.6 %collective-permute-start.1 = (bf16[128,544]{1,0:T(8,128)(2,1)}, bf16[128,544]{1,0:T(8,128)(2,1)S(1)}, u32[]{:S(2)}, u32[]{:S(2)}) collective-permute-start(bf16[128,544]{1,0:T(8,128)(2,1)} %get-tuple-element.96), channel_id=1, source_target_pairs={{0,1},{1,0},{2,3},{3,2},{4,5},{5,4},{6,7},{7,6},{8,9},{9,8},{10,11... | collective-permute-start | bytes 417800 | tf_op jit(solution)/shard_map/ppermute | solution.py:733
  15.2 6.4 %collective-permute-start.2 = (bf16[128,544]{1,0:T(8,128)(2,1)S(1)}, bf16[128,544]{1,0:T(8,128)(2,1)S(1)}, u32[]{:S(2)}, u32[]{:S(2)}) collective-permute-start(bf16[128,544]{1,0:T(8,128)(2,1)S(1)} %add_convert_fusion.1), channel_id=1, source_target_pairs={{0,2},{1,3},{2,0},{3,1},{4,6},{5,7},{6,4},{7,5},{8,10},{9,11},{10,... | collective-permute-start | bytes 417800 | tf_op jit(solution)/shard_map/ppermute | solution.py:733
  16.7 34.0 %collective-permute-start.8 = (bf16[128,2048]{1,0:T(8,128)(2,1)}, bf16[128,2048]{1,0:T(8,128)(2,1)S(1)}, u32[]{:S(2)}, u32[]{:S(2)}) collective-permute-start(bf16[128,2048]{1,0:T(8,128)(2,1)} %get-tuple-element.158.refs_6_.refs_4_), channel_id=1, source_target_pairs={{0,16},{8,24},{16,0},{24,8},{1,17},{9,25},{17,1},{25,9},{2,18},{10... | collective-permute-start | bytes 1572872 | tf_op jit(solution)/shard_map/ppermute | solution.py:733
  20.0 30.7 %collective-permute-start.7 = (bf16[128,2048]{1,0:T(8,128)(2,1)}, bf16[128,2048]{1,0:T(8,128)(2,1)S(1)}, u32[]{:S(2)}, u32[]{:S(2)}) collective-permute-start(bf16[128,2048]{1,0:T(8,128)(2,1)} %get-tuple-element.158.refs_6_.refs_4_), channel_id=1, source_target_pairs={{0,8},{8,0},{16,24},{24,16},{1,9},{9,1},{17,25},{25,17},{2,10},{10... | collective-permute-start | bytes 1572872 | tf_op jit(solution)/shard_map/ppermute | solution.py:733
  21.6 6.2 %copy-start.11 = (bf16[128,544]{1,0:T(8,128)(2,1)}, bf16[128,544]{1,0:T(8,128)(2,1)S(1)}, u32[]{:S(2)}) copy-start(bf16[128,544]{1,0:T(8,128)(2,1)S(1)} %add_convert_fusion.refs_0_) | copy-start | bytes 417796
  21.7 5.5 %collective-permute-start.3 = (bf16[128,544]{1,0:T(8,128)(2,1)S(1)}, bf16[128,544]{1,0:T(8,128)(2,1)S(1)}, u32[]{:S(2)}, u32[]{:S(2)}) collective-permute-start(bf16[128,544]{1,0:T(8,128)(2,1)S(1)} %add_convert_fusion.refs_0_), channel_id=1, source_target_pairs={{0,4},{1,5},{2,6},{3,7},{4,0},{5,1},{6,2},{7,3},{8,12},{9,13},{10,... | collective-permute-start | bytes 417800 | tf_op jit(solution)/shard_map/ppermute | solution.py:733
  27.1 0.7 copy-start.15
  39.5 6.6 %collective-permute-start.4 = (bf16[2,18,8,128]{3,2,1,0:T(8,128)(2,1)}, bf16[2,18,8,128]{3,2,1,0:T(8,128)(2,1)S(1)}, u32[]{:S(2)}, u32[]{:S(2)}) collective-permute-start(bf16[2,18,8,128]{3,2,1,0:T(8,128)(2,1)} %get-tuple-element.101), channel_id=1, source_target_pairs={{0,8},{8,0},{16,24},{24,16},{1,9},{9,1},{17,25},{25,17},{2,10},{10... | collective-permute-start | bytes 221192 | tf_op jit(solution)/shard_map/ppermute | solution.py:733
  41.8 7.1 %collective-permute-start.5 = (bf16[2,18,8,128]{3,2,1,0:T(8,128)(2,1)}, bf16[2,18,8,128]{3,2,1,0:T(8,128)(2,1)S(1)}, u32[]{:S(2)}, u32[]{:S(2)}) collective-permute-start(bf16[2,18,8,128]{3,2,1,0:T(8,128)(2,1)} %get-tuple-element.102), channel_id=1, source_target_pairs={{0,16},{8,24},{16,0},{24,8},{1,17},{9,25},{17,1},{25,9},{2,18},{10... | collective-permute-start | bytes 221192 | tf_op jit(solution)/shard_map/ppermute | solution.py:733
  44.4 6.4 %collective-permute-start.6 = (bf16[2,18,8,128]{3,2,1,0:T(8,128)(2,1)}, bf16[2,18,8,128]{3,2,1,0:T(8,128)(2,1)S(1)}, u32[]{:S(2)}, u32[]{:S(2)}) collective-permute-start(bf16[2,18,8,128]{3,2,1,0:T(8,128)(2,1)} %get-tuple-element.103), channel_id=1, source_target_pairs={{0,24},{8,16},{16,8},{24,0},{1,25},{9,17},{17,9},{25,1},{2,26},{10... | collective-permute-start | bytes 221192 | tf_op jit(solution)/shard_map/ppermute | solution.py:733
  46.1 4.7 %copy-start.12 = (bf16[2,18,8,128]{3,2,1,0:T(8,128)(2,1)}, bf16[2,18,8,128]{3,2,1,0:T(8,128)(2,1)S(1)}, u32[]{:S(2)}) copy-start(bf16[2,18,8,128]{3,2,1,0:T(8,128)(2,1)S(1)} %collective-permute-done.4.refs_11_) | copy-start | bytes 221188
  48.8 2.0 %copy-start.13 = (bf16[2,18,8,128]{3,2,1,0:T(8,128)(2,1)}, bf16[2,18,8,128]{3,2,1,0:T(8,128)(2,1)S(1)}, u32[]{:S(2)}) copy-start(bf16[2,18,8,128]{3,2,1,0:T(8,128)(2,1)S(1)} %collective-permute-done.5.refs_12_) | copy-start | bytes 221188
  50.7 0.6 copy-start.14
  50.7 17.4 %collective-permute-start.9 = (bf16[128,2048]{1,0:T(8,128)(2,1)S(1)}, bf16[128,2048]{1,0:T(8,128)(2,1)S(1)}, u32[]{:S(2)}, u32[]{:S(2)}) collective-permute-start(bf16[128,2048]{1,0:T(8,128)(2,1)S(1)} %collective-permute-done.8.refs_6_), channel_id=1, source_target_pairs={{0,8},{8,0},{16,24},{24,16},{1,9},{9,1},{17,25},{25,17},{2,10},{10... | collective-permute-start | bytes 1572872 | tf_op jit(solution)/shard_map/ppermute | solution.py:733
  51.3 15.5 %copy-start.17 = (bf16[128,512]{1,0:T(8,128)(2,1)S(1)}, bf16[128,512]{1,0:T(8,128)(2,1)}, u32[]{:S(2)}) copy-start(bf16[128,512]{1,0:T(8,128)(2,1)} %get-tuple-element.124) | copy-start | bytes 393220
  64.9 17.0 %collective-permute-start.10 = (bf16[144,1024]{1,0:T(8,128)(2,1)}, bf16[144,1024]{1,0:T(8,128)(2,1)S(1)}, u32[]{:S(2)}, u32[]{:S(2)}) collective-permute-start(bf16[144,1024]{1,0:T(8,128)(2,1)} %get-tuple-element.140.refs_2_), channel_id=1, source_target_pairs={{0,16},{8,24},{16,0},{24,8},{1,17},{9,25},{17,1},{25,9},{2,18},{10... | collective-permute-start | bytes 884744 | tf_op jit(solution)/shard_map/ppermute | solution.py:733
  67.0 14.9 %collective-permute-start.11 = (bf16[256,128]{1,0:T(8,128)(2,1)S(1)}, bf16[256,128]{1,0:T(8,128)(2,1)S(1)}, u32[]{:S(2)}, u32[]{:S(2)}) collective-permute-start(bf16[256,128]{1,0:T(8,128)(2,1)S(1)} %get-tuple-element.182), channel_id=1, source_target_pairs={{0,16},{8,24},{16,0},{24,8},{1,17},{9,25},{17,1},{25,9},{2,18},{10... | collective-permute-start | bytes 196616 | tf_op jit(solution)/shard_map/ppermute | solution.py:733
  68.1 22.7 %copy-start.5 = (bf16[144,1024]{1,0:T(8,128)(2,1)S(1)}, bf16[144,1024]{1,0:T(8,128)(2,1)}, u32[]{:S(2)}) copy-start(bf16[144,1024]{1,0:T(8,128)(2,1)} %get-tuple-element.140.refs_2_) | copy-start | bytes 884740
  68.1 34.7 %copy-start = (bf16[544,2048]{1,0:T(8,128)(2,1)S(1)}, bf16[544,2048]{1,0:T(8,128)(2,1)}, u32[]{:S(2)}) copy-start(bf16[544,2048]{1,0:T(8,128)(2,1)} %proj_ref.3) | copy-start | bytes 6684676
  68.1 34.7 %copy-start.4 = (f32[4,2048]{1,0:T(4,128)S(1)}, f32[4,2048]{1,0:T(4,128)}, u32[]{:S(2)}) copy-start(f32[4,2048]{1,0:T(4,128)} %refs_2_.1) | copy-start | bytes 98308
  68.1 34.7 %copy-start.9 = (bf16[3,2048]{1,0:T(4,128)(2,1)S(1)}, bf16[3,2048]{1,0:T(4,128)(2,1)}, u32[]{:S(2)}) copy-start(bf16[3,2048]{1,0:T(4,128)(2,1)} %copy-done.8) | copy-start | bytes 36868
  68.1 34.7 %copy-start.10 = (f32[2048]{0:T(1024)S(1)}, f32[2048]{0:T(1024)}, u32[]{:S(2)}) copy-start(f32[2048]{0:T(1024)} %param.14) | copy-start | bytes 24580
  81.9 20.9 %copy-start.2 = (bf16[128,2048]{1,0:T(8,128)(2,1)S(1)}, bf16[128,2048]{1,0:T(8,128)(2,1)}, u32[]{:S(2)}) copy-start(bf16[128,2048]{1,0:T(8,128)(2,1)} %input_ref.3) | copy-start | bytes 1572868
  81.9 20.9 %copy-start.3 = (bf16[128,2048]{1,0:T(8,128)(2,1)S(1)}, bf16[128,2048]{1,0:T(8,128)(2,1)}, u32[]{:S(2)}) copy-start(bf16[128,2048]{1,0:T(8,128)(2,1)} %get-tuple-element.129.scan_ref) | copy-start | bytes 1572868
  81.9 1.6 %collective-permute-start.12 = (bf16[576,128]{1,0:T(8,128)(2,1)}, bf16[576,128]{1,0:T(8,128)(2,1)S(1)}, u32[]{:S(2)}, u32[]{:S(2)}) collective-permute-start(bf16[576,128]{1,0:T(8,128)(2,1)} %get-tuple-element.125), channel_id=1, source_target_pairs={{0,1},{1,0},{2,3},{3,2},{4,5},{5,4},{6,7},{7,6},{8,9},{9,8},{10,11... | collective-permute-start | bytes 442376 | tf_op jit(solution)/shard_map/ppermute | solution.py:733
  84.5 6.2 %collective-permute-start.13 = (bf16[576,128]{1,0:T(8,128)(2,1)S(1)}, bf16[576,128]{1,0:T(8,128)(2,1)S(1)}, u32[]{:S(2)}, u32[]{:S(2)}) collective-permute-start(bf16[576,128]{1,0:T(8,128)(2,1)S(1)} %add_convert_fusion.3), channel_id=1, source_target_pairs={{0,2},{1,3},{2,0},{3,1},{4,6},{5,7},{6,4},{7,5},{8,10},{9,11},{10,... | collective-permute-start | bytes 442376 | tf_op jit(solution)/shard_map/ppermute | solution.py:733
  86.6 22.2 %collective-permute-start.19 = (bf16[144,1024]{1,0:T(8,128)(2,1)}, bf16[144,1024]{1,0:T(8,128)(2,1)S(1)}, u32[]{:S(2)}, u32[]{:S(2)}) collective-permute-start(bf16[144,1024]{1,0:T(8,128)(2,1)} %get-tuple-element.150.refs_2_), channel_id=1, source_target_pairs={{0,16},{8,24},{16,0},{24,8},{1,17},{9,25},{17,1},{25,9},{2,18},{10... | collective-permute-start | bytes 884744 | tf_op jit(solution)/shard_map/ppermute | solution.py:733
  90.8 18.0 %copy-start.6 = (bf16[144,1024]{1,0:T(8,128)(2,1)S(1)}, bf16[144,1024]{1,0:T(8,128)(2,1)}, u32[]{:S(2)}) copy-start(bf16[144,1024]{1,0:T(8,128)(2,1)} %get-tuple-element.150.refs_2_) | copy-start | bytes 884740
  91.5 17.2 %collective-permute-start.18 = (bf16[144,1024]{1,0:T(8,128)(2,1)S(1)}, bf16[144,1024]{1,0:T(8,128)(2,1)S(1)}, u32[]{:S(2)}, u32[]{:S(2)}) collective-permute-start(bf16[144,1024]{1,0:T(8,128)(2,1)S(1)} %get-tuple-element.143), channel_id=1, source_target_pairs={{0,8},{8,0},{16,24},{24,16},{1,9},{9,1},{17,25},{25,17},{2,10},{10... | collective-permute-start | bytes 884744 | tf_op jit(solution)/shard_map/ppermute | solution.py:733
  93.1 5.1 %collective-permute-start.14 = (bf16[576,128]{1,0:T(8,128)(2,1)S(1)}, bf16[576,128]{1,0:T(8,128)(2,1)S(1)}, u32[]{:S(2)}, u32[]{:S(2)}) collective-permute-start(bf16[576,128]{1,0:T(8,128)(2,1)S(1)} %add_convert_fusion.2.back_a), channel_id=1, source_target_pairs={{0,4},{1,5},{2,6},{3,7},{4,0},{5,1},{6,2},{7,3},{8,12},{9,13},{10,... | collective-permute-start | bytes 442376 | tf_op jit(solution)/shard_map/ppermute | solution.py:733
  98.3 16.2 %copy-start.1 = (bf16[128,2048]{1,0:T(8,128)(2,1)S(1)}, bf16[128,2048]{1,0:T(8,128)(2,1)}, u32[]{:S(2)}) copy-start(bf16[128,2048]{1,0:T(8,128)(2,1)} %get-tuple-element.158.refs_6_.refs_4_) | copy-start | bytes 1572868
  98.3 10.4 %collective-permute-start.15 = (bf16[144,128]{1,0:T(8,128)(2,1)S(1)}, bf16[144,128]{1,0:T(8,128)(2,1)S(1)}, u32[]{:S(2)}, u32[]{:S(2)}) collective-permute-start(bf16[144,128]{1,0:T(8,128)(2,1)S(1)} %get-tuple-element.135), channel_id=1, source_target_pairs={{0,8},{8,0},{16,24},{24,16},{1,9},{9,1},{17,25},{25,17},{2,10},{10... | collective-permute-start | bytes 110600 | tf_op jit(solution)/shard_map/ppermute | solution.py:733
  98.9 9.8 %collective-permute-start.16 = (bf16[144,128]{1,0:T(8,128)(2,1)S(1)}, bf16[144,128]{1,0:T(8,128)(2,1)S(1)}, u32[]{:S(2)}, u32[]{:S(2)}) collective-permute-start(bf16[144,128]{1,0:T(8,128)(2,1)S(1)} %get-tuple-element.136), channel_id=1, source_target_pairs={{0,16},{8,24},{16,0},{24,8},{1,17},{9,25},{17,1},{25,9},{2,18},{10... | collective-permute-start | bytes 110600 | tf_op jit(solution)/shard_map/ppermute | solution.py:733
  100.5 8.2 %collective-permute-start.17 = (bf16[144,128]{1,0:T(8,128)(2,1)S(1)}, bf16[144,128]{1,0:T(8,128)(2,1)S(1)}, u32[]{:S(2)}, u32[]{:S(2)}) collective-permute-start(bf16[144,128]{1,0:T(8,128)(2,1)S(1)} %get-tuple-element.137), channel_id=1, source_target_pairs={{0,24},{8,16},{16,8},{24,0},{1,25},{9,17},{17,9},{25,1},{2,26},{10... | collective-permute-start | bytes 110600 | tf_op jit(solution)/shard_map/ppermute | solution.py:733
  102.8 0.8 copy-start.7
  109.5 8.9 %collective-permute-start.23 = (bf16[144,1024]{1,0:T(8,128)(2,1)S(1)}, bf16[144,1024]{1,0:T(8,128)(2,1)S(1)}, u32[]{:S(2)}, u32[]{:S(2)}) collective-permute-start(bf16[144,1024]{1,0:T(8,128)(2,1)S(1)} %get-tuple-element.153), channel_id=1, source_target_pairs={{0,8},{8,0},{16,24},{24,16},{1,9},{9,1},{17,25},{25,17},{2,10},{10... | collective-permute-start | bytes 884744 | tf_op jit(solution)/shard_map/ppermute | solution.py:733
  109.6 10.1 %collective-permute-start.22 = (bf16[16,2048]{1,0:T(8,128)(2,1)S(1)}, bf16[16,2048]{1,0:T(8,128)(2,1)S(1)}, u32[]{:S(2)}, u32[]{:S(2)}) collective-permute-start(bf16[16,2048]{1,0:T(8,128)(2,1)S(1)} %get-tuple-element.168.refs_3_), channel_id=1, source_target_pairs={{0,24},{8,0},{16,8},{24,16},{1,25},{9,1},{17,9},{25,17},{2,26},{10... | collective-permute-start | bytes 196616 | tf_op jit(solution)/shard_map/ppermute | solution.py:52
  112.0 7.7 %collective-permute-start.21 = (bf16[16,2048]{1,0:T(8,128)(2,1)S(1)}, bf16[16,2048]{1,0:T(8,128)(2,1)S(1)}, u32[]{:S(2)}, u32[]{:S(2)}) collective-permute-start(bf16[16,2048]{1,0:T(8,128)(2,1)S(1)} %get-tuple-element.168.refs_3_), channel_id=1, source_target_pairs={{0,16},{8,24},{16,0},{24,8},{1,17},{9,25},{17,1},{25,9},{2,18},{10... | collective-permute-start | bytes 196616 | tf_op jit(solution)/shard_map/ppermute | solution.py:52
  113.1 8.9 %collective-permute-start.20 = (bf16[16,2048]{1,0:T(8,128)(2,1)S(1)}, bf16[16,2048]{1,0:T(8,128)(2,1)S(1)}, u32[]{:S(2)}, u32[]{:S(2)}) collective-permute-start(bf16[16,2048]{1,0:T(8,128)(2,1)S(1)} %get-tuple-element.168.refs_3_), channel_id=1, source_target_pairs={{0,8},{8,16},{16,24},{24,0},{1,9},{9,17},{17,25},{25,1},{2,10},{10... | collective-permute-start | bytes 196616 | tf_op jit(solution)/shard_map/ppermute | solution.py:52
